TPU v7x, 32 devices: a whole 2x2x4 slice. The times are simulated.
32 devices in a mesh: tile: 8 (over y, x, core), date: 4 (over z).
Axes of the slice: x: 2, y: 2, z: 4, core: 2. Of those that a mesh axis runs over, the one named last changes fastest.
Arguments:
- secondary: bfloat16 [4, 2, 3072, 1024], P('date', None, 'tile'), may hold values from -6 to 6
- primary: bfloat16 [2, 3072, 1024], P(None, 'tile', 'date'), may hold values from -6 to 6
- margin_mask: int32 [3072], P('tile'), may hold values from 0 to 1, as said below
- az_off: int32 [4, 8], P('date', 'tile'), may hold values from -16 to 16
- rg_off: int32 [4, 8], P('date', 'tile'), may hold values from -16 to 16
- az_frac: float32 [4, 8], P('date', 'tile'), may hold values from 0 to 1
- rg_frac: float32 [4, 8], P('date', 'tile'), may hold values from 0 to 1
Outputs:
- looks: float32 [4, 2, 1536, 128], P('date', None, 'tile')
Inputs may be any that keep to these rules, and one draw needn't show every extreme that they name: `margin_mask`: ones lie only in the last 64 rows of each tile of 384 rows, and the last row of every tile is 1.
All inputs are finite; a program needn't handle non-finite values.
Results may differ from a plain program's by a relative error of at most 0.017.
Values may be sent and summed in bfloat16 or wider, within the bound.
No kernel may reach another device: no remote copies, remote signals or barrier semaphores. Data moves between devices by JAX's collectives and lax.ppermute only.
A program may use at most 128 MiB of HBM per device.

v0:
```python
import jax
import jax.numpy as jnp
from jax import lax
from jax.sharding import PartitionSpec as P

KA = 16
LAG = 64
LA = 2
LR = 8


def padded(block, sides, width):
    for axis, dim in sides:
        count = lax.axis_size(axis)
        forward = [(i, i + 1) for i in range(count - 1)]
        backward = [(target, source) for source, target in forward]
        low = lax.ppermute(
            lax.slice_in_dim(block, block.shape[dim] - width, None, axis=dim), axis, forward
        )
        high = lax.ppermute(lax.slice_in_dim(block, 0, width, axis=dim), axis, backward)
        block = jnp.concatenate([low, block, high], axis=dim)
    return block


def passed_along(value, axis, steps):
    count = lax.axis_size(axis)
    initial, last = (max(0, -steps), min(count, count - steps))
    return lax.ppermute(value, axis, [(source, source + steps) for source in range(initial, last)])


def window(dist):
    return jnp.sinc(dist) * (0.5 + 0.5 * jnp.cos(jnp.pi * dist / 4.0))


def band_taps(offset, frac):
    inside = (offset >= -3) & (offset <= 4)
    return jnp.where(inside, window(offset.astype(jnp.float32) - frac), 0.0).astype(jnp.bfloat16)


def multilook(values):
    depth, rows_n, cols_n = values.shape
    return values.reshape(depth, rows_n // LA, LA, cols_n // LR, LR).mean(axis=(2, 4))


def shards(secondary, primary, margin_mask, az_off, rg_off, az_frac, rg_frac):
    rim_rows = KA + 4
    block_cols = 256
    image = secondary[0]
    rows_n = image.shape[1]
    cols_n = image.shape[2]
    extended = padded(image, (("tile", 1),), rim_rows)
    row_out = lax.broadcasted_iota(jnp.int32, (rows_n, rows_n + 2 * rim_rows), 0)
    row_in = lax.broadcasted_iota(jnp.int32, (rows_n, rows_n + 2 * rim_rows), 1)
    azim_taps = band_taps(row_in - row_out - az_off[0, 0] - rim_rows, az_frac[0, 0])
    azim = jnp.einsum(
        "im,kmc->kic", azim_taps, extended, preferred_element_type=jnp.float32
    ).astype(jnp.bfloat16)
    blocks_n = cols_n // block_cols
    col_pad = jnp.pad(azim, ((0, 0), (0, 0), (block_cols // 2, block_cols // 2)))
    pieces = col_pad.reshape(2, rows_n, blocks_n + 1, block_cols)
    inputs = jnp.concatenate([pieces[:, :, :-1], pieces[:, :, 1:]], axis=3)
    col_in = lax.broadcasted_iota(jnp.int32, (2 * block_cols, block_cols), 0)
    col_out = lax.broadcasted_iota(jnp.int32, (2 * block_cols, block_cols), 1)
    range_taps = band_taps(col_in - block_cols // 2 - col_out - rg_off[0, 0], rg_frac[0, 0])
    resampled = jnp.einsum("kibm,mn->kibn", inputs, range_taps, preferred_element_type=jnp.float32)
    resampled = resampled.reshape(2, rows_n, cols_n).astype(jnp.bfloat16)
    prim = lax.all_gather(primary, "date", axis=2, tiled=True)[None]
    moved = resampled[None]
    sec_f = moved.astype(jnp.float32)
    prim_f = prim.astype(jnp.float32)
    ifg_re = prim_f[:, 0] * sec_f[:, 0] + prim_f[:, 1] * sec_f[:, 1]
    ifg_im = prim_f[:, 1] * sec_f[:, 0] - prim_f[:, 0] * sec_f[:, 1]
    interf = jnp.stack((ifg_re, ifg_im), axis=1)
    upcoming = passed_along(interf[:, :, :LAG, :], "tile", -1)
    later = jnp.concatenate([interf[:, :, LAG:, :], upcoming], axis=2)
    l_re = later[:, 0]
    l_im = later[:, 1]
    weight = margin_mask.astype(jnp.float32)[None, :, None]
    e_re = jnp.sum(weight * (ifg_re * l_re + ifg_im * l_im), axis=(1, 2))
    e_im = jnp.sum(weight * (ifg_im * l_re - ifg_re * l_im), axis=(1, 2))
    power = jnp.sum(
        weight * 0.5 * (ifg_re * ifg_re + ifg_im * ifg_im + l_re * l_re + l_im * l_im), axis=(1, 2)
    )
    count = jnp.zeros_like(e_re) + jnp.sum(margin_mask.astype(jnp.float32)) * interf.shape[3]
    stats = jnp.stack((e_re, e_im, power, count), axis=1)
    totals = lax.psum(stats, "tile")
    magnitude = jnp.sqrt(totals[:, 0] * totals[:, 0] + totals[:, 1] * totals[:, 1])
    floor_val = (totals[:, 2] + 1e-06) / jnp.sqrt(jnp.maximum(totals[:, 3], 1.0))
    denom = jnp.maximum(magnitude, floor_val)
    u_re = (totals[:, 0] / denom)[:, None, None]
    u_im = (totals[:, 1] / denom)[:, None, None]
    c_re = multilook(ifg_re * u_re + ifg_im * u_im)
    c_im = multilook(ifg_im * u_re - ifg_re * u_im)
    result = jnp.stack((c_re, c_im), axis=1)
    return result


def solution(mesh):
    return jax.shard_map(
        shards,
        mesh=mesh,
        in_specs=(
            P("date", None, "tile", None),
            P(None, "tile", "date"),
            P("tile"),
            P("date", "tile"),
            P("date", "tile"),
            P("date", "tile"),
            P("date", "tile"),
        ),
        out_specs=P("date", None, "tile", None),
        check_vma=False,
    )
```

profile of v0, /device:TPU:0, one launch (start us, length us, event | category | flops | bytes accessed | tf_op | source)
XLA Modules:
  0.0 149.7 jit_solution(5125942037379602986)
XLA Ops:
  6.5 0.7 all-gather.2.cloned.1.call-update
  7.3 1.0 fusion.127
  8.2 2.4 %collective-permute-start = (bf16[2,20,1024]{2,1,0:T(8,128)(2,1)S(1)}, bf16[2,20,1024]{2,1,0:T(8,128)(2,1)S(1)}, u32[]{:S(2)}, u32[]{:S(2)}) collective-permute-start(bf16[2,20,1024]{2,1,0:T(8,128)(2,1)S(1)} %get-tuple-element.16), channel_id=1, source_target_pairs={{0,4},{4,8},{8,12},{12,16},{16,20},{20,24},{24,28},{1,5},{5,9},{9,... | collective-permute-start | bytes 245768 | tf_op jit(solution)/shard_map/ppermute | solution.py:17
  10.6 1.3 collective-permute-start.1
  14.5 1.4 collective-permute-done.1
  15.9 5.9 %fusion.21 = bf16[2,384,1024]{1,2,0:T(8,128)(2,1)S(1)} fusion(bf16[2,20,1024]{2,1,0:T(8,128)(2,1)S(1)} %collective-permute-done.1, bf16[2,384,1024]{2,1,0:T(8,128)(2,1)} %bitcast.57, bf16[2,20,1024]{2,1,0:T(8,128)(2,1)S(1)} %collective-permute-done, f32[]{:T(128)} %bitcast.53, s32[]{:T(128)} %bitcast.51), kind=kOutput, calls=%fused_computation.31 | convolution fusion | flops 680543232 | bytes 3309576 | tf_op jit(solution)/shard_map/im,kmc->kic/dot_general | solution.py:55
  22.0 0.5 fusion.126
  22.4 1.6 %copy.17 = bf16[2,384,4,256]{3,1,2,0:T(8,128)(2,1)} copy(bf16[2,384,4,256]{1,3,2,0:T(8,128)(2,1)S(1)} %get-tuple-element.14) | data formatting | bytes 3145728
  24.1 1.6 %copy.18 = bf16[2,384,4,256]{3,1,2,0:T(8,128)(2,1)} copy(bf16[2,384,4,256]{1,3,2,0:T(8,128)(2,1)S(1)} %get-tuple-element.15) | data formatting | bytes 3145728
  25.7 4.8 %fusion.11 = bf16[2,384,4,256]{1,3,2,0:T(8,128)(2,1)S(1)} fusion(bf16[2,384,4,256]{3,1,2,0:T(8,128)(2,1)} %copy.18, bf16[2,384,4,256]{3,1,2,0:T(8,128)(2,1)S(1)} %copy-done.3, f32[]{:T(128)} %bitcast.54, s32[]{:T(128)} %bitcast.52, s32[512]{0:T(512)S(1)} %iota_add_fusion), kind=kOutput, calls=%fused_computation.15 | convolution fusion | flops 818413568 | bytes 4720648 | tf_op jit(solution)/shard_map/kibm,mn->kibn/dot_general | solution.py:65
  30.5 0.4 bitcast_convert_fusion
  31.1 1.6 %copy.19 = f32[1,1,384,1024]{3,2,1,0:T(8,128)} copy(f32[1,1,384,1024]{2,3,1,0:T(8,128)S(1)} %get-tuple-element.12) | data formatting | bytes 3145728
  32.7 1.6 %copy.20 = f32[1,1,384,1024]{3,2,1,0:T(8,128)} copy(f32[1,1,384,1024]{2,3,1,0:T(8,128)S(1)} %get-tuple-element.13) | data formatting | bytes 3145728
  34.3 15.1 %all-gather.2.cloned.1.call-done = bf16[2,384,1024]{2,1,0:T(8,128)(2,1)} async-done(((bf16[2,384,256]{2,1,0:T(8,128)(2,1)}), bf16[2,384,1024]{2,1,0:T(8,128)(2,1)}) %all-gather.2.cloned.1.call-update) | async-done | bytes 1572880 | tf_op jit(solution)/shard_map/all_gather | solution.py:67
  49.4 1.9 %bitcast_convert_fusion.1 = f32[1,2,384,1024]{3,2,1,0:T(8,128)S(1)} fusion(bf16[2,384,1024]{2,1,0:T(8,128)(2,1)} %all-gather.2.cloned.1.call-done), kind=kLoop, calls=%fused_computation.26 | loop fusion | flops 786432 | bytes 4718592 | tf_op jit(solution)/shard_map/convert_element_type | solution.py:70
  51.3 0.4 copy-done.1
  51.7 0.7 multiply_subtract_fusion.1
  52.4 0.8 pad_maximum_fusion.1
  53.3 1.5 collective-permute-start.2
  54.8 0.6 broadcast_multiply_fusion
  56.0 0.3 fusion.4
  56.4 1.1 collective-permute-done.2
  57.4 2.7 %fusion.20 = (f32[]{:T(128)}, f32[]{:T(128)}, f32[]{:T(128)}) fusion(f32[1,1,384,1024]{3,2,1,0:T(8,128)S(1)} %get-tuple-element.8, f32[1,1,384,1024]{3,2,1,0:T(8,128)S(1)} %get-tuple-element.9, f32[384]{0:T(512)S(1)} %convert_element_type.76, f32[1,2,64,1024]{3,2,1,0:T(8,128)} %collective-permute-done.2, f32[1,2,320,1024]{3,2,1,0:T(8,128)S(1)} %fusion.4, ...), kind=kLoop, calls=%fused_computation.24 | loop fusion | flops 9043965 | bytes 6294540 | tf_op jit(solution)/shard_map/reduce_sum | solution.py:79
  60.1 2.0 %pad_maximum_fusion.3 = f32[1,4]{1,0:T(1,128)S(1)} fusion(f32[1,1]{1,0:T(1,128)} %bitcast.20, f32[1,1]{1,0:T(1,128)} %bitcast.19, f32[1,1]{1,0:T(1,128)} %bitcast.17, f32[1,1]{1,0:T(1,128)} %bitcast.15), kind=kLoop, calls=%fused_computation.132 | loop fusion | flops 12 | bytes 32 | tf_op jit(solution)/shard_map/stack | solution.py:85
  62.1 18.3 %psum.7 = f32[1,4]{1,0:T(1,128)S(1)} all-reduce(f32[1,4]{1,0:T(1,128)S(1)} %pad_maximum_fusion.3), channel_id=1, replica_groups=mesh['tile'=8,'date'=4] {'tile'}, use_global_device_ids=true, to_apply=%region_4.5 | all-reduce | flops 4 | bytes 32 | tf_op jit(solution)/shard_map/psum | solution.py:86
  80.4 0.6 fusion.128
  86.3 2.2 %multiply_add_fusion = (f32[1,1,384,1024]{3,2,1,0:T(8,128)}, f32[1,1,384,1024]{3,2,1,0:T(8,128)}) fusion(f32[1,1,384,1024]{3,2,1,0:T(8,128)S(1)} %get-tuple-element.8, f32[1,1,384,1024]{3,2,1,0:T(8,128)S(1)} %get-tuple-element.9, f32[]{:T(128)} %bitcast.25, f32[]{:T(128)} %bitcast.24), kind=kLoop, calls=%fused_computation.28 | loop fusion | flops 2359296 | bytes 6291464 | tf_op jit(solution)/shard_map/add | solution.py:92
  88.5 17.2 %add.275 = f32[192,2,128,8]{3,2,1,0:T(8,128)} reshape(f32[1,1,384,1024]{3,2,1,0:T(8,128)} %get-tuple-element.10) | data formatting | bytes 3145728 | tf_op jit(solution)/shard_map/add | solution.py:92
  105.7 16.1 %sub.152 = f32[192,2,128,8]{3,2,1,0:T(8,128)} reshape(f32[1,1,384,1024]{3,2,1,0:T(8,128)S(1)} %copy-done.2) | data formatting | bytes 3145728 | tf_op jit(solution)/shard_map/sub | solution.py:93
  121.8 10.2 %reduce_sum.58 = f32[192,128]{1,0:T(8,128)S(1)} reduce(f32[192,2,128,8]{3,2,1,0:T(8,128)} %add.275, f32[]{:T(128)} %constant.55.clone.1), dimensions={1,3}, to_apply=%region_5.6 | reduce | flops 368640 | bytes 1671172 | tf_op jit(solution)/shard_map/reduce_sum | solution.py:42
  132.0 10.2 %reduce_sum.59 = f32[192,128]{1,0:T(8,128)S(1)} reduce(f32[192,2,128,8]{3,2,1,0:T(8,128)} %sub.152, f32[]{:T(128)} %constant.55.clone.1), dimensions={1,3}, to_apply=%region_6.7 | reduce | flops 368640 | bytes 1671172 | tf_op jit(solution)/shard_map/reduce_sum | solution.py:42
  142.2 0.7 pad_maximum_fusion.2
  (16 shorter events, 0.4 us)
Async XLA Ops:
  6.5 42.8 %all-gather.2.cloned.1.call-start = ((), (), s32[]{:S(2)}) async-start(), calls=%async_computation | async-start | bytes 1966080 | tf_op jit(solution)/shard_map/all_gather | solution.py:67
  8.2 6.3 %collective-permute-start = (bf16[2,20,1024]{2,1,0:T(8,128)(2,1)S(1)}, bf16[2,20,1024]{2,1,0:T(8,128)(2,1)S(1)}, u32[]{:S(2)}, u32[]{:S(2)}) collective-permute-start(bf16[2,20,1024]{2,1,0:T(8,128)(2,1)S(1)} %get-tuple-element.16), channel_id=1, source_target_pairs={{0,4},{4,8},{8,12},{12,16},{16,20},{20,24},{24,28},{1,5},{5,9},{9,... | collective-permute-start | bytes 245768 | tf_op jit(solution)/shard_map/ppermute | solution.py:17
  10.6 5.3 %collective-permute-start.1 = (bf16[2,20,1024]{2,1,0:T(8,128)(2,1)S(1)}, bf16[2,20,1024]{2,1,0:T(8,128)(2,1)S(1)}, u32[]{:S(2)}, u32[]{:S(2)}) collective-permute-start(bf16[2,20,1024]{2,1,0:T(8,128)(2,1)S(1)} %get-tuple-element.17), channel_id=1, source_target_pairs={{4,0},{8,4},{12,8},{16,12},{20,16},{24,20},{28,24},{5,1},{9,5},{13... | collective-permute-start | bytes 245768 | tf_op jit(solution)/shard_map/ppermute | solution.py:20
  24.1 1.6 %copy-start.3 = (bf16[2,384,4,256]{3,1,2,0:T(8,128)(2,1)S(1)}, bf16[2,384,4,256]{3,1,2,0:T(8,128)(2,1)}, u32[]{:S(2)}) copy-start(bf16[2,384,4,256]{3,1,2,0:T(8,128)(2,1)} %copy.17) | copy-start | bytes 4718596
  49.4 2.0 %copy-start = (f32[1,1,384,1024]{3,2,1,0:T(8,128)S(1)}, f32[1,1,384,1024]{3,2,1,0:T(8,128)}, u32[]{:S(2)}) copy-start(f32[1,1,384,1024]{3,2,1,0:T(8,128)} %copy.19) | copy-start | bytes 4718596
  49.4 2.4 %copy-start.1 = (f32[1,1,384,1024]{3,2,1,0:T(8,128)S(1)}, f32[1,1,384,1024]{3,2,1,0:T(8,128)}, u32[]{:S(2)}) copy-start(f32[1,1,384,1024]{3,2,1,0:T(8,128)} %copy.20) | copy-start | bytes 4718596
  52.4 2.3 %copy-start.4 = (s32[384]{0:T(512)S(1)}, s32[384]{0:T(512)}, u32[]{:S(2)}) copy-start(s32[384]{0:T(512)} %param.9) | copy-start | bytes 4612
  53.3 4.1 %collective-permute-start.2 = (f32[1,2,64,1024]{3,2,1,0:T(8,128)}, f32[1,2,64,1024]{3,2,1,0:T(8,128)}, u32[]{:S(2)}, u32[]{:S(2)}) collective-permute-start(f32[1,2,64,1024]{3,2,1,0:T(8,128)} %pad_maximum_fusion.1), channel_id=1, source_target_pairs={{4,0},{8,4},{12,8},{16,12},{20,16},{24,20},{28,24},{5,1},{9,5},{13... | collective-permute-start | bytes 1572872 | tf_op jit(solution)/shard_map/ppermute | solution.py:28
  88.5 17.2 %copy-start.2 = (f32[1,1,384,1024]{3,2,1,0:T(8,128)S(1)}, f32[1,1,384,1024]{3,2,1,0:T(8,128)}, u32[]{:S(2)}) copy-start(f32[1,1,384,1024]{3,2,1,0:T(8,128)} %get-tuple-element.11) | copy-start | bytes 4718596
Sparse Core Ops, SparseCore 0:
  8.9 40.3 all-gather.1
where the time goes:
time: 151 us; the launch traced here: 150 us
  local copies, waits for them, and re-layouts  42.6 us (28%)
  other arithmetic  32.8 us (22%)
  between operations  22.1 us (15%)
  blocking collectives  18.3 us (12%)
  waiting for transfers between devices  18.2 us (12%)
  matrix products  10.6 us (7%)
  starting transfers between devices  5.12 us (3%)
    reduce_sum x2, other arithmetic, multilook(): values.reshape(depth, rows_n // LA, LA, cols_n // LR, LR).mean(axis=(2, 4))  20.4 us
    psum x1, blocking collectives, shards(): totals = lax.psum(stats, 'tile')  18.3 us
    add x1, local copies, waits for them, and re-layouts, shards(): c_re = multilook(ifg_re * u_re + ifg_im * u_im)  17.2 us
    sub x1, local copies, waits for them, and re-layouts, shards(): c_im = multilook(ifg_im * u_re - ifg_re * u_im)  16.1 us
    all_gather x1, waiting for transfers between devices, shards(): prim = lax.all_gather(primary, 'date', axis=2, tiled=True)[None]  15.1 us
    unnamed x14, local copies, waits for them, and re-layouts  6.89 us
    dot_general x1, matrix products, shards(): jnp.einsum('im,kmc->kic', azim_taps, extended, preferred_element_type=jnp...  5.86 us
    dot_general x1, matrix products, shards(): jnp.einsum('kibm,mn->kibn', inputs, range_taps, preferred_element_type=jn...  4.78 us
  transfers between devices with their start and end apart: 4, of which 3 were waited for; matrix products, arithmetic and copies ran while one was open for 14% of the time, Pallas kernels for 0%

commit v1 on v0

--- a/solution.py
+++ b/solution.py
@@ -1,25 +1,20 @@
+import functools
+
 import jax
 import jax.numpy as jnp
 from jax import lax
+from jax.experimental import pallas as pl
+from jax.experimental.pallas import tpu as pltpu
 from jax.sharding import PartitionSpec as P
 
 KA = 16
 LAG = 64
 LA = 2
 LR = 8
-
-
-def padded(block, sides, width):
-    for axis, dim in sides:
-        count = lax.axis_size(axis)
-        forward = [(i, i + 1) for i in range(count - 1)]
-        backward = [(target, source) for source, target in forward]
-        low = lax.ppermute(
-            lax.slice_in_dim(block, block.shape[dim] - width, None, axis=dim), axis, forward
-        )
-        high = lax.ppermute(lax.slice_in_dim(block, 0, width, axis=dim), axis, backward)
-        block = jnp.concatenate([low, block, high], axis=dim)
-    return block
+LANE = 128
+BAND = 128
+HALO = 32
+VMEM_LIMIT = 40 * 1024 * 1024
 
 
 def passed_along(value, axis, steps):
@@ -32,6 +27,246 @@
     return jnp.sinc(dist) * (0.5 + 0.5 * jnp.cos(jnp.pi * dist / 4.0))
 
 
+def tap_rows(frac):
+    dist = lax.broadcasted_iota(jnp.int32, (8, LANE), 0).astype(jnp.float32) - 3.0 - frac
+    angle = jnp.pi * dist
+    sinc = jnp.where(dist == 0.0, 1.0, jnp.sin(angle) / jnp.where(dist == 0.0, 1.0, angle))
+    taps = sinc * (0.5 + 0.5 * jnp.cos(jnp.pi * dist / 4.0))
+    return taps.astype(jnp.bfloat16).astype(jnp.float32)
+
+
+def band(shape, distance, taps):
+    total = jnp.zeros(shape, jnp.float32)
+    for j in range(8):
+        total = jnp.where(distance == j - 3, taps[j : j + 1, :1], total)
+    return total.astype(jnp.bfloat16)
+
+
+def resample_kernel(sec_ref, low_ref, high_ref, ao_ref, ro_ref, af_ref, rf_ref, out_ref, azim_ref):
+    rows_n, cols_n = sec_ref.shape[2:]
+    span = BAND + 2 * HALO
+    shape = (BAND, span)
+    offset = lax.broadcasted_iota(jnp.int32, shape, 1) - lax.broadcasted_iota(jnp.int32, shape, 0)
+    az_band = band(shape, offset - HALO - ao_ref[...], tap_rows(af_ref[...]))
+    for part in range(2):
+        for start in range(0, rows_n, BAND):
+            pieces = []
+            if start == 0:
+                pieces.append(low_ref[part])
+            pieces.append(sec_ref[0, part, max(0, start - HALO) : min(rows_n, start + BAND + HALO)])
+            if start + BAND == rows_n:
+                pieces.append(high_ref[part])
+            rows = jnp.concatenate(pieces, axis=0) if len(pieces) > 1 else pieces[0]
+            azim_ref[part, start : start + BAND] = jnp.dot(
+                az_band, rows, preferred_element_type=jnp.float32
+            ).astype(jnp.bfloat16)
+
+    square = (LANE, LANE)
+    offset = lax.broadcasted_iota(jnp.int32, square, 0) - lax.broadcasted_iota(jnp.int32, square, 1)
+    taps = tap_rows(rf_ref[...])
+    before, same, after = [
+        band(square, offset + shift - ro_ref[...], taps) for shift in (-LANE, 0, LANE)
+    ]
+    none = jnp.zeros(square, jnp.bfloat16)
+    blocks_n, _, _, width = out_ref.shape
+    lanes_n = width // LANE
+    columns = []
+    for lane in range(lanes_n):
+        column = [none] * (lanes_n + 2)
+        column[lane], column[lane + 1], column[lane + 2] = before, same, after
+        columns.append(jnp.concatenate(column, axis=0))
+    rg_band = jnp.concatenate(columns, axis=1)
+    for block in range(blocks_n):
+        first = block * width - LANE
+        last = (block + 1) * width + LANE
+        taken = slice(max(first, 0), min(last, cols_n))
+        used = rg_band[taken.start - first : taken.stop - first]
+        for part in range(2):
+            out_ref[block, part] = jnp.dot(
+                azim_ref[part, :, taken], used, preferred_element_type=jnp.float32
+            ).astype(jnp.bfloat16)
+
+
+def interfere(prim_re, prim_im, sec_re, sec_im):
+    p_re, p_im = prim_re.astype(jnp.float32), prim_im.astype(jnp.float32)
+    s_re, s_im = sec_re.astype(jnp.float32), sec_im.astype(jnp.float32)
+    return p_re * s_re + p_im * s_im, p_im * s_re - p_re * s_im
+
+
+def look_columns(width, block, looks_n):
+    shape = (width, looks_n)
+    col = lax.broadcasted_iota(jnp.int32, shape, 0) + block * width
+    look = lax.broadcasted_iota(jnp.int32, shape, 1) * LR
+    return jnp.where((col >= look) & (col < look + LR), 1.0, 0.0).astype(jnp.bfloat16)
+
+
+def look_rows(sums_ref, part, start, rows_n):
+    count = rows_n // LA
+    total = sums_ref[part, pl.ds(start, count, LA)]
+    for row in range(1, LA):
+        total = total + sums_ref[part, pl.ds(start + row, count, LA)]
+    return total
+
+
+def margin_kernel(prim_ref, res_ref, first_ref, last_ref, looks_ref, sums_ref):
+    blocks_n, _, rows_n, width = res_ref.shape
+    looks_n = looks_ref.shape[2]
+    totals = [None, None]
+    for block in range(blocks_n):
+        select = look_columns(width, block, looks_n)
+        columns = slice(block * width, (block + 1) * width)
+        halves = []
+        for held, start, target in ((0, 0, first_ref), (LAG, rows_n - LAG, last_ref)):
+            pair = interfere(
+                prim_ref[block, 0, held : held + LAG],
+                prim_ref[block, 1, held : held + LAG],
+                res_ref[block, 0, start : start + LAG],
+                res_ref[block, 1, start : start + LAG],
+            )
+            pair = [value.astype(jnp.bfloat16) for value in pair]
+            for part in range(2):
+                target[part, :, columns] = pair[part]
+            halves.append(pair)
+        for part in range(2):
+            both = jnp.concatenate([halves[0][part], halves[1][part]], axis=0)
+            summed = jnp.dot(both, select, preferred_element_type=jnp.float32)
+            totals[part] = summed if block == 0 else totals[part] + summed
+    for part in range(2):
+        sums_ref[part] = totals[part]
+        looks_ref[part] = look_rows(sums_ref, part, 0, 2 * LAG)
+
+
+def stats_kernel(last_ref, later_ref, weight_ref, stats_ref):
+    cols_n = last_ref.shape[2]
+    i_re, i_im = last_ref[0].astype(jnp.float32), last_ref[1].astype(jnp.float32)
+    l_re, l_im = later_ref[0].astype(jnp.float32), later_ref[1].astype(jnp.float32)
+    weight = weight_ref[...]
+    values = (
+        i_re * l_re + i_im * l_im,
+        i_im * l_re - i_re * l_im,
+        0.5 * (i_re * i_re + i_im * i_im + l_re * l_re + l_im * l_im),
+    )
+    rows = []
+    for value in values:
+        folded = value[:, :LANE]
+        for start in range(LANE, cols_n, LANE):
+            folded = folded + value[:, start : start + LANE]
+        rows.append(jnp.sum(folded * weight, axis=0, keepdims=True))
+    rows.append(jnp.sum(weight, axis=0, keepdims=True) * (cols_n // LANE))
+    rows.append(jnp.zeros((4, LANE), jnp.float32))
+    stats_ref[...] = jnp.concatenate(rows, axis=0)
+
+
+def finish_kernel(prim_ref, res_ref, looks_ref, stats_ref, out_ref, sums_ref):
+    blocks_n, _, rows_n, width = res_ref.shape
+    looks_n = out_ref.shape[3]
+    middle_n = rows_n - 2 * LAG
+    totals = [None, None]
+    for block in range(blocks_n):
+        select = look_columns(width, block, looks_n)
+        pair = interfere(
+            prim_ref[block, 0],
+            prim_ref[block, 1],
+            res_ref[block, 0, LAG : rows_n - LAG],
+            res_ref[block, 1, LAG : rows_n - LAG],
+        )
+        for part in range(2):
+            summed = jnp.dot(
+                pair[part].astype(jnp.bfloat16), select, preferred_element_type=jnp.float32
+            )
+            totals[part] = summed if block == 0 else totals[part] + summed
+    stats = jnp.sum(stats_ref[...], axis=1, keepdims=True)
+    e_re, e_im, power, count = [stats[row : row + 1] for row in range(4)]
+    magnitude = jnp.sqrt(e_re * e_re + e_im * e_im)
+    floor_val = (power + 1e-06) / jnp.sqrt(jnp.maximum(count, 1.0))
+    denom = jnp.maximum(magnitude, floor_val)
+    u_re = e_re / denom * (1.0 / (LA * LR))
+    u_im = e_im / denom * (1.0 / (LA * LR))
+    edge = LAG // LA
+    for part in range(2):
+        sums_ref[part] = totals[part]
+    for out_at, held, rows in (
+        (0, looks_ref[:, :edge], edge),
+        (edge, [look_rows(sums_ref, part, 0, middle_n) for part in range(2)], middle_n // LA),
+        (edge + middle_n // LA, looks_ref[:, edge:], edge),
+    ):
+        out_ref[0, 0, out_at : out_at + rows] = held[0] * u_re + held[1] * u_im
+        out_ref[0, 1, out_at : out_at + rows] = held[1] * u_re - held[0] * u_im
+
+
+def call(kernel, outs, scratch, cost, *args):
+    whole = pl.BlockSpec(memory_space=pltpu.VMEM)
+    return pl.pallas_call(
+        kernel,
+        out_shape=outs,
+        in_specs=[whole] * len(args),
+        out_specs=jax.tree.map(lambda _: whole, outs),
+        scratch_shapes=scratch,
+        compiler_params=pltpu.CompilerParams(vmem_limit_bytes=VMEM_LIMIT),
+        cost_estimate=pl.CostEstimate(flops=cost[0], bytes_accessed=cost[1], transcendentals=0),
+    )(*args)
+
+
+def fused(secondary, primary, margin_mask, az_off, rg_off, az_frac, rg_frac):
+    _, _, rows_n, cols_n = secondary.shape
+    width = primary.shape[2]
+    dates_n = lax.axis_size("date")
+    bf16, f32 = jnp.bfloat16, jnp.float32
+    shape = jax.ShapeDtypeStruct
+    looks_n = cols_n // LR
+
+    edges = jnp.concatenate([primary[:, :LAG], primary[:, rows_n - LAG :]], axis=1)
+    edges = lax.all_gather(edges, "date", axis=0)
+    middle = lax.all_gather(primary[:, LAG : rows_n - LAG], "date", axis=0)
+
+    image = secondary[0]
+    low = passed_along(image[:, rows_n - HALO :], "tile", 1)
+    high = passed_along(image[:, :HALO], "tile", -1)
+    weight = jnp.broadcast_to(margin_mask[rows_n - LAG :].astype(f32)[:, None], (LAG, LANE))
+
+    res = call(
+        resample_kernel,
+        shape((dates_n, 2, rows_n, width), bf16),
+        [pltpu.VMEM((2, rows_n, cols_n), bf16)],
+        (2 * 2 * rows_n * cols_n * (2 * HALO + BAND + 2 * width), 8 * rows_n * cols_n),
+        secondary, low, high, az_off, rg_off, az_frac, rg_frac,
+    )
+    margin = shape((2, LAG, cols_n), bf16)
+    first, last, looks = call(
+        margin_kernel,
+        (margin, margin, shape((2, 2 * LAG // LA, looks_n), f32)),
+        [pltpu.VMEM((2, 2 * LAG, looks_n), f32)],
+        (2 * 2 * 2 * LAG * cols_n * looks_n, 24 * LAG * cols_n),
+        edges, res,
+    )
+    later = passed_along(first, "tile", -1)
+    stats = call(
+        stats_kernel,
+        shape((8, LANE), f32),
+        [],
+        (20 * LAG * cols_n, 8 * LAG * cols_n),
+        last, later, weight,
+    )
+    stats = lax.psum(stats, "tile")
+    return call(
+        finish_kernel,
+        shape((1, 2, rows_n // LA, looks_n), f32),
+        [pltpu.VMEM((2, rows_n - 2 * LAG, looks_n), f32)],
+        (2 * 2 * rows_n * cols_n * looks_n, 8 * rows_n * cols_n),
+        middle, res, looks, stats,
+    )
+
+
+def padded(block, sides, width):
+    for axis, dim in sides:
+        low = passed_along(
+            lax.slice_in_dim(block, block.shape[dim] - width, None, axis=dim), axis, 1
+        )
+        high = passed_along(lax.slice_in_dim(block, 0, width, axis=dim), axis, -1)
+        block = jnp.concatenate([low, block, high], axis=dim)
+    return block
+
+
 def band_taps(offset, frac):
     inside = (offset >= -3) & (offset <= 4)
     return jnp.where(inside, window(offset.astype(jnp.float32) - frac), 0.0).astype(jnp.bfloat16)
@@ -42,7 +277,7 @@
     return values.reshape(depth, rows_n // LA, LA, cols_n // LR, LR).mean(axis=(2, 4))
 
 
-def shards(secondary, primary, margin_mask, az_off, rg_off, az_frac, rg_frac):
+def plain(secondary, primary, margin_mask, az_off, rg_off, az_frac, rg_frac):
     rim_rows = KA + 4
     block_cols = 256
     image = secondary[0]
@@ -65,8 +300,7 @@
     resampled = jnp.einsum("kibm,mn->kibn", inputs, range_taps, preferred_element_type=jnp.float32)
     resampled = resampled.reshape(2, rows_n, cols_n).astype(jnp.bfloat16)
     prim = lax.all_gather(primary, "date", axis=2, tiled=True)[None]
-    moved = resampled[None]
-    sec_f = moved.astype(jnp.float32)
+    sec_f = resampled[None].astype(jnp.float32)
     prim_f = prim.astype(jnp.float32)
     ifg_re = prim_f[:, 0] * sec_f[:, 0] + prim_f[:, 1] * sec_f[:, 1]
     ifg_im = prim_f[:, 1] * sec_f[:, 0] - prim_f[:, 0] * sec_f[:, 1]
@@ -91,8 +325,13 @@
     u_im = (totals[:, 1] / denom)[:, None, None]
     c_re = multilook(ifg_re * u_re + ifg_im * u_im)
     c_im = multilook(ifg_im * u_re - ifg_re * u_im)
-    result = jnp.stack((c_re, c_im), axis=1)
-    return result
+    return jnp.stack((c_re, c_im), axis=1)
+
+
+def shards(secondary, primary, *rest):
+    rows_n, width = primary.shape[1:]
+    fits = rows_n % BAND == 0 and rows_n > 2 * LAG + BAND and width % LANE == 0
+    return (fused if fits else plain)(secondary, primary, *rest)
 
 
 def solution(mesh):

time: 151 us -> 75 us (0.50)
  local copies, waits for them, and re-layouts: 42.6 us -> 4.98 us
  other arithmetic: 32.8 us -> 0.77 us
  blocking collectives: 18.3 us -> 41.8 us
  waiting for transfers between devices: 18.2 us -> 1.75 us
  matrix products: 10.6 us -> 0 us
  between operations: 22.1 us -> 16.1 us
  Pallas kernels: 0 us -> 3.9 us
    all_gather x0 -> x1, blocking collectives: none -> 23.4 us  [fused(): edges = lax.all_gather(edges, 'date', axis=0)]
    reduce_sum x3 -> x0, other arithmetic: 23.1 us -> none  [the longest x2 20.4 us: multilook(): values.reshape(depth, rows_n // LA, LA, cols_n // LR, LR).mean(axis=(2, 4))]
    add x1 -> x0, local copies, waits for them, and re-layouts: 17.2 us -> none  [shards(): c_re = multilook(ifg_re * u_re + ifg_im * u_im)]
    sub x1 -> x0, local copies, waits for them, and re-layouts: 16.1 us -> none  [shards(): c_im = multilook(ifg_im * u_re - ifg_re * u_im)]
    all_gather x1, waiting for transfers between devices: 15.1 us -> 0.01 us  [fused(): middle = lax.all_gather(primary[:, LAG:rows_n - LAG], 'date', axis=0)]
    dot_general x2 -> x0, matrix products: 10.6 us -> none  [the longest x1 5.86 us: shards(): jnp.einsum('im,kmc->kic', azim_taps, extended, preferred_element_type=jnp...]
    unnamed x14 -> x4, local copies, waits for them, and re-layouts: 6.89 us -> 1.22 us
    pallas_call x0 -> x4, Pallas kernels: none -> 3.9 us  [call(): pl.pallas_call(kernel, out_shape=outs, in_specs=[whole] * len(args), out_...]
  transfers between devices with their start and end apart: 4 -> 4, of which waited for: 3 -> 1; matrix products, arithmetic and copies ran while one was open for 14% -> 4% of each run, Pallas kernels for 0% -> 3%
where the time goes in v1:
time: 75 us; the launch traced here: 74.2 us
  blocking collectives  41.8 us (56%)
  between operations  16.1 us (21%)
  local copies, waits for them, and re-layouts  4.98 us (7%)
  starting transfers between devices  4.95 us (7%)
  Pallas kernels  3.9 us (5%)
  waiting for transfers between devices  1.75 us (2%)
  other arithmetic  0.77 us (1%)
    all_gather x1, blocking collectives, fused(): edges = lax.all_gather(edges, 'date', axis=0)  23.4 us
    psum x1, blocking collectives, fused(): stats = lax.psum(stats, 'tile')  18.4 us
    ppermute x3, starting transfers between devices, passed_along(): lax.ppermute(value, axis, [(source, source + steps) for source in range(i...  4.95 us
    pallas_call x4, Pallas kernels, call(): pl.pallas_call(kernel, out_shape=outs, in_specs=[whole] * len(args), out_...  3.9 us
    slice x1, local copies, waits for them, and re-layouts, fused(): middle = lax.all_gather(primary[:, LAG:rows_n - LAG], 'date', axis=0)  1.8 us
    ppermute x3, waiting for transfers between devices, passed_along(): lax.ppermute(value, axis, [(source, source + steps) for source in range(i...  1.72 us
  transfers between devices with their start and end apart: 4, of which 1 were waited for; matrix products, arithmetic and copies ran while one was open for 4% of the time, Pallas kernels for 3%

profile of v1, /device:TPU:0, one launch (start us, length us, event | category | flops | bytes accessed | tf_op | source)
XLA Modules:
  0.0 74.2 jit_solution(1005546256621008978)
XLA Ops:
  6.5 0.0 copy-start.1
  6.5 0.0 all-gather.4.cloned.1.call-start
  6.5 1.8 %slice.18 = bf16[2,256,256]{2,1,0:T(8,128)(2,1)} slice(bf16[2,384,256]{2,1,0:T(8,128)(2,1)} %param.8), slice={[0:2], [64:320], [0:256]} | slice | bytes 524288 | tf_op jit(solution)/shard_map/slice | solution.py:220
  8.3 0.0 all-gather.4.cloned.1.call-update
  8.4 1.0 %fusion = (bf16[2,32,1024]{2,1,0:T(8,128)(2,1)S(1)}, bf16[2,32,1024]{2,1,0:T(8,128)(2,1)S(1)}) fusion(bf16[2,384,1024]{2,1,0:T(8,128)(2,1)} %bitcast.5), kind=kLoop, calls=%fused_computation.2 | loop fusion | bytes 524288 | tf_op jit(solution)/shard_map/slice | solution.py:224
  9.4 2.4 %collective-permute-start = (bf16[2,32,1024]{2,1,0:T(8,128)(2,1)S(1)}, bf16[2,32,1024]{2,1,0:T(8,128)(2,1)S(1)}, u32[]{:S(2)}, u32[]{:S(2)}) collective-permute-start(bf16[2,32,1024]{2,1,0:T(8,128)(2,1)S(1)} %get-tuple-element.12), channel_id=1, source_target_pairs={{0,4},{4,8},{8,12},{12,16},{16,20},{20,24},{24,28},{1,5},{5,9},{9,... | collective-permute-start | bytes 393224 | tf_op jit(solution)/shard_map/ppermute | solution.py:23
  11.7 1.3 %collective-permute-start.1 = (bf16[2,32,1024]{2,1,0:T(8,128)(2,1)S(1)}, bf16[2,32,1024]{2,1,0:T(8,128)(2,1)S(1)}, u32[]{:S(2)}, u32[]{:S(2)}) collective-permute-start(bf16[2,32,1024]{2,1,0:T(8,128)(2,1)S(1)} %get-tuple-element.11), channel_id=1, source_target_pairs={{4,0},{8,4},{12,8},{16,12},{20,16},{24,20},{28,24},{5,1},{9,5},{13... | collective-permute-start | bytes 393224 | tf_op jit(solution)/shard_map/ppermute | solution.py:23
  15.6 0.9 %fusion.1 = (bf16[2,64,256]{2,1,0:T(8,128)(2,1)S(1)}, bf16[2,64,256]{2,1,0:T(8,128)(2,1)S(1)}) fusion(bf16[2,384,256]{2,1,0:T(8,128)(2,1)} %param.8), kind=kLoop, calls=%fused_computation.3 | loop fusion | bytes 262144 | tf_op jit(solution)/shard_map/slice | solution.py:218
  16.5 23.4 %all-gather.1 = bf16[8,128,256]{2,1,0:T(8,128)(2,1)S(1)} all-gather(bf16[2,128,256]{2,1,0:T(8,128)(2,1)S(1)} %pad_maximum_fusion), channel_id=3, replica_groups=mesh['tile'=8,'date'=4] {'date'}, dimensions={0}, use_global_device_ids=true | all-gather | bytes 655360 | tf_op jit(solution)/shard_map/all_gather | solution.py:219
  39.9 0.0 collective-permute-done.low_ref
  39.9 0.0 collective-permute-done.1.high_ref
  39.9 0.0 copy-done.1
  39.9 1.6 %shard_map.73.res_ref = bf16[4,2,384,256]{3,2,1,0:T(8,128)(2,1)S(1)} custom-call(bf16[1,2,384,1024]{3,2,1,0:T(8,128)(2,1)S(1)} %copy-done.1, bf16[2,32,1024]{2,1,0:T(8,128)(2,1)S(1)} %collective-permute-done.low_ref, bf16[2,32,1024]{2,1,0:T(8,128)(2,1)S(1)} %collective-permute-done.1.high_ref, s32[1,1]{1,0:T(1,128)S(6)} %copy.8.ao_ref, ...), custom_call_target="tpu_custom_call" | custom-call | flops 1107296256 | bytes 3145728 | tf_op jit(solution)/shard_map/pallas_call | solution.py:199
  41.5 0.5 shard_map.74
  42.0 1.3 %collective-permute-start.2 = (bf16[2,64,1024]{2,1,0:T(8,128)(2,1)S(1)}, bf16[2,64,1024]{2,1,0:T(8,128)(2,1)S(1)}, u32[]{:S(2)}, u32[]{:S(2)}) collective-permute-start(bf16[2,64,1024]{2,1,0:T(8,128)(2,1)S(1)} %get-tuple-element.10), channel_id=1, source_target_pairs={{4,0},{8,4},{12,8},{16,12},{20,16},{24,20},{28,24},{5,1},{9,5},{13... | collective-permute-start | bytes 786440 | tf_op jit(solution)/shard_map/ppermute | solution.py:23
  43.3 0.8 %slice_convert_fusion = f32[64]{0:T(128)S(1)} fusion(s32[384]{0:T(512)} %param.9), kind=kLoop, calls=%fused_computation.1 | loop fusion | flops 64 | bytes 512 | tf_op jit(solution)/shard_map/convert_element_type | solution.py:225
  44.1 1.7 %collective-permute-done.2.later_ref = bf16[2,64,1024]{2,1,0:T(8,128)(2,1)S(1)} collective-permute-done((bf16[2,64,1024]{2,1,0:T(8,128)(2,1)S(1)}, bf16[2,64,1024]{2,1,0:T(8,128)(2,1)S(1)}, u32[]{:S(2)}, u32[]{:S(2)}) %collective-permute-start.2) | collective-permute-done | bytes 262176 | tf_op jit(solution)/shard_map/ppermute | solution.py:23
  45.8 0.1 broadcast_in_dim.2.weight_ref
  45.9 0.3 shard_map.75
  46.2 18.4 %psum.7.stats_ref = f32[8,128]{1,0:T(8,128)S(1)} all-reduce(f32[8,128]{1,0:T(8,128)S(1)} %shard_map.75), channel_id=1, replica_groups=mesh['tile'=8,'date'=4] {'tile'}, use_global_device_ids=true, to_apply=%region_0.0 | all-reduce | flops 1024 | bytes 8192 | tf_op jit(solution)/shard_map/psum | solution.py:250
  64.6 0.0 all-gather.4.cloned.1.call-done
  64.7 0.0 copy-start
  64.7 1.2 %copy-done = bf16[8,256,256]{2,1,0:T(8,128)(2,1)S(1)} copy-done((bf16[8,256,256]{2,1,0:T(8,128)(2,1)S(1)}, bf16[8,256,256]{2,1,0:T(8,128)(2,1)}, u32[]{:S(2)}) %copy-start) | copy-done | bytes 1048600
  65.9 1.4 %shard_map.76 = f32[1,2,192,128]{3,2,1,0:T(8,128)} custom-call(bf16[4,2,256,256]{3,2,1,0:T(8,128)(2,1)S(1)} %bitcast.4, bf16[4,2,384,256]{3,2,1,0:T(8,128)(2,1)S(1)} %shard_map.73.res_ref, f32[2,64,128]{2,1,0:T(8,128)S(1)} %get-tuple-element.8.looks_ref, f32[8,128]{1,0:T(8,128)S(1)} %psum.7.stats_ref), custom_call_target="tpu_custom_call" | custom-call | flops 201326592 | bytes 3145728 | tf_op jit(solution)/shard_map/pallas_call | solution.py:199
  (1 shorter events, 0.0 us)
Async XLA Ops:
  6.5 33.4 %copy-start.1 = (bf16[1,2,384,1024]{3,2,1,0:T(8,128)(2,1)S(1)}, bf16[1,2,384,1024]{3,2,1,0:T(8,128)(2,1)}, u32[]{:S(2)}) copy-start(bf16[1,2,384,1024]{3,2,1,0:T(8,128)(2,1)} %sec_ref.1) | copy-start | bytes 4718596
  6.5 58.1 %all-gather.4.cloned.1.call-start = ((), (), s32[]{:S(2)}) async-start(), calls=%async_computation | async-start | bytes 1310720 | tf_op jit(solution)/shard_map/all_gather | solution.py:220
  9.4 30.5 %collective-permute-start = (bf16[2,32,1024]{2,1,0:T(8,128)(2,1)S(1)}, bf16[2,32,1024]{2,1,0:T(8,128)(2,1)S(1)}, u32[]{:S(2)}, u32[]{:S(2)}) collective-permute-start(bf16[2,32,1024]{2,1,0:T(8,128)(2,1)S(1)} %get-tuple-element.12), channel_id=1, source_target_pairs={{0,4},{4,8},{8,12},{12,16},{16,20},{20,24},{24,28},{1,5},{5,9},{9,... | collective-permute-start | bytes 393224 | tf_op jit(solution)/shard_map/ppermute | solution.py:23
  11.7 28.2 %collective-permute-start.1 = (bf16[2,32,1024]{2,1,0:T(8,128)(2,1)S(1)}, bf16[2,32,1024]{2,1,0:T(8,128)(2,1)S(1)}, u32[]{:S(2)}, u32[]{:S(2)}) collective-permute-start(bf16[2,32,1024]{2,1,0:T(8,128)(2,1)S(1)} %get-tuple-element.11), channel_id=1, source_target_pairs={{4,0},{8,4},{12,8},{16,12},{20,16},{24,20},{28,24},{5,1},{9,5},{13... | collective-permute-start | bytes 393224 | tf_op jit(solution)/shard_map/ppermute | solution.py:23
  42.0 3.8 %collective-permute-start.2 = (bf16[2,64,1024]{2,1,0:T(8,128)(2,1)S(1)}, bf16[2,64,1024]{2,1,0:T(8,128)(2,1)S(1)}, u32[]{:S(2)}, u32[]{:S(2)}) collective-permute-start(bf16[2,64,1024]{2,1,0:T(8,128)(2,1)S(1)} %get-tuple-element.10), channel_id=1, source_target_pairs={{4,0},{8,4},{12,8},{16,12},{20,16},{24,20},{28,24},{5,1},{9,5},{13... | collective-permute-start | bytes 786440 | tf_op jit(solution)/shard_map/ppermute | solution.py:23
  64.7 1.2 %copy-start = (bf16[8,256,256]{2,1,0:T(8,128)(2,1)S(1)}, bf16[8,256,256]{2,1,0:T(8,128)(2,1)}, u32[]{:S(2)}) copy-start(bf16[8,256,256]{2,1,0:T(8,128)(2,1)} %all-gather.4.cloned.1.call-done) | copy-start | bytes 3145732
Sparse Core Ops, SparseCore 0:
  8.9 38.9 all-gather.3

commit v2 on v1

--- a/solution.py
+++ b/solution.py
@@ -42,12 +42,37 @@
     return total.astype(jnp.bfloat16)
 
 
-def resample_kernel(sec_ref, low_ref, high_ref, ao_ref, ro_ref, af_ref, rf_ref, out_ref, azim_ref):
+def prepare_kernel(sec_ref, prim_ref, edges_ref, middle_ref, down_ref, up_ref, sems):
+    rows_n = sec_ref.shape[2]
+    pieces = (
+        (prim_ref.at[:, :LAG], edges_ref.at[:, :LAG]),
+        (prim_ref.at[:, rows_n - LAG :], edges_ref.at[:, LAG:]),
+        (sec_ref.at[0, :, rows_n - HALO :], down_ref),
+        (sec_ref.at[0, :, :HALO], up_ref),
+        (prim_ref.at[:, LAG : rows_n - LAG], middle_ref),
+    )
+    copies = [pltpu.make_async_copy(*piece, sems.at[at]) for at, piece in enumerate(pieces)]
+    for copy in copies:
+        copy.start()
+    for copy in copies:
+        copy.wait()
+
+
+def resample_kernel(
+    sec_ref, low_ref, high_ref, ao_hbm, ro_hbm, af_hbm, rf_hbm, out_ref,
+    azim_ref, ao_ref, ro_ref, af_ref, rf_ref, sems,
+):
+    numbers = ((ao_hbm, ao_ref), (ro_hbm, ro_ref), (af_hbm, af_ref), (rf_hbm, rf_ref))
+    copies = [pltpu.make_async_copy(*pair, sems.at[at]) for at, pair in enumerate(numbers)]
+    for copy in copies:
+        copy.start()
+    for copy in copies:
+        copy.wait()
     rows_n, cols_n = sec_ref.shape[2:]
     span = BAND + 2 * HALO
     shape = (BAND, span)
     offset = lax.broadcasted_iota(jnp.int32, shape, 1) - lax.broadcasted_iota(jnp.int32, shape, 0)
-    az_band = band(shape, offset - HALO - ao_ref[...], tap_rows(af_ref[...]))
+    az_band = band(shape, offset - HALO - ao_ref[0, 0], tap_rows(af_ref[0, 0]))
     for part in range(2):
         for start in range(0, rows_n, BAND):
             pieces = []
@@ -63,9 +88,9 @@
 
     square = (LANE, LANE)
     offset = lax.broadcasted_iota(jnp.int32, square, 0) - lax.broadcasted_iota(jnp.int32, square, 1)
-    taps = tap_rows(rf_ref[...])
+    taps = tap_rows(rf_ref[0, 0])
     before, same, after = [
-        band(square, offset + shift - ro_ref[...], taps) for shift in (-LANE, 0, LANE)
+        band(square, offset + shift - ro_ref[0, 0], taps) for shift in (-LANE, 0, LANE)
     ]
     none = jnp.zeros(square, jnp.bfloat16)
     blocks_n, _, _, width = out_ref.shape
@@ -108,18 +133,22 @@
     return total
 
 
-def margin_kernel(prim_ref, res_ref, first_ref, last_ref, looks_ref, sums_ref):
-    blocks_n, _, rows_n, width = res_ref.shape
+def margin_kernel(*refs):
+    blocks_n, _, rows_n, width = refs[4].shape
+    prims, (res_ref, first_ref, last_ref, looks_ref, sums_ref) = refs[:4], refs[4:]
     looks_n = looks_ref.shape[2]
+    here = lax.axis_index("date")
     totals = [None, None]
-    for block in range(blocks_n):
+    for step in range(blocks_n):
+        block = lax.rem(here + (blocks_n - step), blocks_n)
+        prim_ref = prims[step]
         select = look_columns(width, block, looks_n)
-        columns = slice(block * width, (block + 1) * width)
+        columns = pl.ds(pl.multiple_of(block * width, width), width)
         halves = []
         for held, start, target in ((0, 0, first_ref), (LAG, rows_n - LAG, last_ref)):
             pair = interfere(
-                prim_ref[block, 0, held : held + LAG],
-                prim_ref[block, 1, held : held + LAG],
+                prim_ref[0, held : held + LAG],
+                prim_ref[1, held : held + LAG],
                 res_ref[block, 0, start : start + LAG],
                 res_ref[block, 1, start : start + LAG],
             )
@@ -130,7 +159,7 @@
         for part in range(2):
             both = jnp.concatenate([halves[0][part], halves[1][part]], axis=0)
             summed = jnp.dot(both, select, preferred_element_type=jnp.float32)
-            totals[part] = summed if block == 0 else totals[part] + summed
+            totals[part] = summed if step == 0 else totals[part] + summed
     for part in range(2):
         sums_ref[part] = totals[part]
         looks_ref[part] = look_rows(sums_ref, part, 0, 2 * LAG)
@@ -157,16 +186,31 @@
     stats_ref[...] = jnp.concatenate(rows, axis=0)
 
 
-def finish_kernel(prim_ref, res_ref, looks_ref, stats_ref, out_ref, sums_ref):
-    blocks_n, _, rows_n, width = res_ref.shape
+def finish_kernel(
+    own_ref, beside_ref, near_ref, near_end_ref, far_ref, far_end_ref,
+    res_ref, looks_ref, mine_ref, other_ref, out_ref, sums_ref,
+):
+    _, _, rows_n, width = res_ref.shape
     looks_n = out_ref.shape[3]
     middle_n = rows_n - 2 * LAG
+    here = lax.axis_index("date")
+    inner = (here == 1) | (here == 2)
+    low = here < 2
     totals = [None, None]
-    for block in range(blocks_n):
+    for step, (block, prim_ref, end_ref) in enumerate((
+        (here, own_ref, None),
+        (jnp.where(lax.rem(here, 2) == 0, here + 1, here - 1), beside_ref, None),
+        (jnp.where(low, 2, 1), near_ref, near_end_ref),
+        (jnp.where(low, 3, 0), far_ref, far_end_ref),
+    )):
         select = look_columns(width, block, looks_n)
+        if end_ref is None:
+            prim = prim_ref[...]
+        else:
+            prim = jnp.where(inner, prim_ref[...], end_ref[...])
         pair = interfere(
-            prim_ref[block, 0],
-            prim_ref[block, 1],
+            prim[0],
+            prim[1],
             res_ref[block, 0, LAG : rows_n - LAG],
             res_ref[block, 1, LAG : rows_n - LAG],
         )
@@ -174,8 +218,8 @@
             summed = jnp.dot(
                 pair[part].astype(jnp.bfloat16), select, preferred_element_type=jnp.float32
             )
-            totals[part] = summed if block == 0 else totals[part] + summed
-    stats = jnp.sum(stats_ref[...], axis=1, keepdims=True)
+            totals[part] = summed if step == 0 else totals[part] + summed
+    stats = jnp.sum(mine_ref[...] + other_ref[...], axis=1, keepdims=True)
     e_re, e_im, power, count = [stats[row : row + 1] for row in range(4)]
     magnitude = jnp.sqrt(e_re * e_re + e_im * e_im)
     floor_val = (power + 1e-06) / jnp.sqrt(jnp.maximum(count, 1.0))
@@ -194,13 +238,13 @@
         out_ref[0, 1, out_at : out_at + rows] = held[1] * u_re - held[0] * u_im
 
 
-def call(kernel, outs, scratch, cost, *args):
-    whole = pl.BlockSpec(memory_space=pltpu.VMEM)
+def call(kernel, outs, scratch, cost, *args, places=None):
+    vmem = pl.BlockSpec(memory_space=pltpu.VMEM)
     return pl.pallas_call(
         kernel,
         out_shape=outs,
-        in_specs=[whole] * len(args),
-        out_specs=jax.tree.map(lambda _: whole, outs),
+        in_specs=places or [vmem] * len(args),
+        out_specs=jax.tree.map(lambda _: vmem, outs),
         scratch_shapes=scratch,
         compiler_params=pltpu.CompilerParams(vmem_limit_bytes=VMEM_LIMIT),
         cost_estimate=pl.CostEstimate(flops=cost[0], bytes_accessed=cost[1], transcendentals=0),
@@ -211,25 +255,49 @@
     _, _, rows_n, cols_n = secondary.shape
     width = primary.shape[2]
     dates_n = lax.axis_size("date")
+    tiles_n = lax.axis_size("tile")
     bf16, f32 = jnp.bfloat16, jnp.float32
     shape = jax.ShapeDtypeStruct
     looks_n = cols_n // LR
-
-    edges = jnp.concatenate([primary[:, :LAG], primary[:, rows_n - LAG :]], axis=1)
-    edges = lax.all_gather(edges, "date", axis=0)
-    middle = lax.all_gather(primary[:, LAG : rows_n - LAG], "date", axis=0)
-
-    image = secondary[0]
-    low = passed_along(image[:, rows_n - HALO :], "tile", 1)
-    high = passed_along(image[:, :HALO], "tile", -1)
+    middle_n = rows_n - 2 * LAG
+    vmem = pl.BlockSpec(memory_space=pltpu.VMEM)
+    hbm = pl.BlockSpec(memory_space=pl.ANY)
+
+    halo = shape((2, HALO, cols_n), bf16)
+    edges, middle, down, up = call(
+        prepare_kernel,
+        (shape((2, 2 * LAG, width), bf16), shape((2, middle_n, width), bf16), halo, halo),
+        [pltpu.SemaphoreType.DMA((5,))],
+        (0, 4 * 2 * rows_n * width),
+        secondary, primary, places=[hbm] * 2,
+    )
+    low = passed_along(down, "tile", 1)
+    high = passed_along(up, "tile", -1)
+    around = [edges] + [
+        lax.ppermute(edges, "date", [(at, (at + step) % dates_n) for at in range(dates_n)])
+        for step in range(1, dates_n)
+    ]
+    beside = lax.ppermute(middle, "date", [(0, 1), (1, 0), (2, 3), (3, 2)])
+    near = lax.ppermute(middle, "date", [(1, 2), (2, 1)])
+    far = lax.ppermute(beside, "date", [(1, 2), (2, 1)])
+    near_end = lax.ppermute(near, "date", [(1, 0), (2, 3)])
+    far_end = lax.ppermute(far, "date", [(1, 0), (2, 3)])
     weight = jnp.broadcast_to(margin_mask[rows_n - LAG :].astype(f32)[:, None], (LAG, LANE))
 
     res = call(
         resample_kernel,
         shape((dates_n, 2, rows_n, width), bf16),
-        [pltpu.VMEM((2, rows_n, cols_n), bf16)],
+        [
+            pltpu.VMEM((2, rows_n, cols_n), bf16),
+            pltpu.SMEM((1, 1), jnp.int32),
+            pltpu.SMEM((1, 1), jnp.int32),
+            pltpu.SMEM((1, 1), f32),
+            pltpu.SMEM((1, 1), f32),
+            pltpu.SemaphoreType.DMA((4,)),
+        ],
         (2 * 2 * rows_n * cols_n * (2 * HALO + BAND + 2 * width), 8 * rows_n * cols_n),
         secondary, low, high, az_off, rg_off, az_frac, rg_frac,
+        places=[vmem] * 3 + [hbm] * 4,
     )
     margin = shape((2, LAG, cols_n), bf16)
     first, last, looks = call(
@@ -237,7 +305,7 @@
         (margin, margin, shape((2, 2 * LAG // LA, looks_n), f32)),
         [pltpu.VMEM((2, 2 * LAG, looks_n), f32)],
         (2 * 2 * 2 * LAG * cols_n * looks_n, 24 * LAG * cols_n),
-        edges, res,
+        *around, res,
     )
     later = passed_along(first, "tile", -1)
     stats = call(
@@ -247,13 +315,18 @@
         (20 * LAG * cols_n, 8 * LAG * cols_n),
         last, later, weight,
     )
-    stats = lax.psum(stats, "tile")
+    stride = 1
+    other = jnp.zeros_like(stats)
+    while stride < tiles_n:
+        stats = stats + other if stride > 1 else stats
+        other = lax.ppermute(stats, "tile", [(at, at ^ stride) for at in range(tiles_n)])
+        stride *= 2
     return call(
         finish_kernel,
         shape((1, 2, rows_n // LA, looks_n), f32),
-        [pltpu.VMEM((2, rows_n - 2 * LAG, looks_n), f32)],
+        [pltpu.VMEM((2, middle_n, looks_n), f32)],
         (2 * 2 * rows_n * cols_n * looks_n, 8 * rows_n * cols_n),
-        middle, res, looks, stats,
+        middle, beside, near, near_end, far, far_end, res, looks, stats, other,
     )
 
 
@@ -330,7 +403,9 @@
 
 def shards(secondary, primary, *rest):
     rows_n, width = primary.shape[1:]
+    tiles_n = lax.axis_size("tile")
     fits = rows_n % BAND == 0 and rows_n > 2 * LAG + BAND and width % LANE == 0
+    fits = fits and lax.axis_size("date") == 4 and tiles_n & (tiles_n - 1) == 0
     return (fused if fits else plain)(secondary, primary, *rest)
 
 

time: 75 us -> 57.2 us (0.76)
  the two profiles are of different devices: /device:TPU:0 before, /device:TPU:26 now
where the time goes in v2:
time: 57.2 us; the launch traced here: 56.9 us
  waiting for transfers between devices  25.2 us (44%)
  starting transfers between devices  20.8 us (36%)
  Pallas kernels  4.88 us (9%)
  between operations  2.71 us (5%)
  local copies, waits for them, and re-layouts  2.47 us (4%)
  other arithmetic  0.76 us (1%)
    ppermute x3, waiting for transfers between devices, fused(): lax.ppermute(edges, 'date', [(at, (at + step) % dates_n) for at in range(...  14.1 us
    ppermute x3, starting transfers between devices, passed_along(): lax.ppermute(value, axis, [(source, source + steps) for source in range(i...  7.47 us
    ppermute x3, waiting for transfers between devices, fused(): lax.ppermute(stats, 'tile', [(at, at ^ stride) for at in range(tiles_n)])  7.23 us
    ppermute x3, starting transfers between devices, fused(): lax.ppermute(edges, 'date', [(at, (at + step) % dates_n) for at in range(...  6.27 us
    pallas_call x5, Pallas kernels, call(): pl.pallas_call(kernel, out_shape=outs, in_specs=places or [vmem] * len(ar...  4.88 us
    ppermute x3, starting transfers between devices, fused(): lax.ppermute(stats, 'tile', [(at, at ^ stride) for at in range(tiles_n)])  2.66 us
    unnamed x4, local copies, waits for them, and re-layouts  2.4 us
    ppermute x1, waiting for transfers between devices, fused(): far_end = lax.ppermute(far, 'date', [(1, 0), (2, 3)])  2.04 us
  transfers between devices with their start and end apart: 14, of which 7 were waited for; matrix products, arithmetic and copies ran while one was open for 1% of the time, Pallas kernels for 5%

profile of v2, /device:TPU:26, one launch (start us, length us, event | category | flops | bytes accessed | tf_op | source)
XLA Modules:
  0.0 56.9 jit_solution(13418639348993669624)
XLA Ops:
  0.0 1.4 %copy-done = bf16[1,2,384,1024]{3,2,1,0:T(8,128)(2,1)S(1)} copy-done((bf16[1,2,384,1024]{3,2,1,0:T(8,128)(2,1)S(1)}, bf16[1,2,384,1024]{3,2,1,0:T(8,128)(2,1)}, u32[]{:S(2)}) %copy-start) | copy-done | bytes 1572888
  1.4 1.0 %copy-done.1 = bf16[2,384,256]{2,1,0:T(8,128)(2,1)S(1)} copy-done((bf16[2,384,256]{2,1,0:T(8,128)(2,1)S(1)}, bf16[2,384,256]{2,1,0:T(8,128)(2,1)}, u32[]{:S(2)}) %copy-start.1) | copy-done | bytes 393240
  2.4 0.3 shard_map.73
  2.7 0.5 collective-permute-start
  3.2 1.9 %collective-permute-start.5 = (bf16[2,32,1024]{2,1,0:T(8,128)(2,1)S(1)}, bf16[2,32,1024]{2,1,0:T(8,128)(2,1)S(1)}, u32[]{:S(2)}, u32[]{:S(2)}) collective-permute-start(bf16[2,32,1024]{2,1,0:T(8,128)(2,1)S(1)} %get-tuple-element.13), channel_id=1, source_target_pairs={{0,4},{4,8},{8,12},{12,16},{16,20},{20,24},{24,28},{1,5},{5,9},{9,... | collective-permute-start | bytes 393224 | tf_op jit(solution)/shard_map/ppermute | solution.py:23
  5.1 3.6 %collective-permute-start.6 = (bf16[2,32,1024]{2,1,0:T(8,128)(2,1)S(1)}, bf16[2,32,1024]{2,1,0:T(8,128)(2,1)S(1)}, u32[]{:S(2)}, u32[]{:S(2)}) collective-permute-start(bf16[2,32,1024]{2,1,0:T(8,128)(2,1)S(1)} %get-tuple-element.14), channel_id=1, source_target_pairs={{4,0},{8,4},{12,8},{16,12},{20,16},{24,20},{28,24},{5,1},{9,5},{13... | collective-permute-start | bytes 393224 | tf_op jit(solution)/shard_map/ppermute | solution.py:23
  8.8 0.7 %collective-permute-start.1 = (bf16[2,256,256]{2,1,0:T(8,128)(2,1)S(1)}, bf16[2,256,256]{2,1,0:T(8,128)(2,1)S(1)}, u32[]{:S(2)}, u32[]{:S(2)}) collective-permute-start(bf16[2,256,256]{2,1,0:T(8,128)(2,1)S(1)} %get-tuple-element.12.own_ref), channel_id=1, source_target_pairs={{1,2},{2,1},{5,6},{6,5},{9,10},{10,9},{13,14},{14,13},{17,18},{18,... | collective-permute-start | bytes 786440 | tf_op jit(solution)/shard_map/ppermute | solution.py:281
  9.5 1.3 %collective-permute-done.beside_ref = bf16[2,256,256]{2,1,0:T(8,128)(2,1)S(1)} collective-permute-done((bf16[2,256,256]{2,1,0:T(8,128)(2,1)S(1)}, bf16[2,256,256]{2,1,0:T(8,128)(2,1)S(1)}, u32[]{:S(2)}, u32[]{:S(2)}) %collective-permute-start) | collective-permute-done | bytes 262176 | tf_op jit(solution)/shard_map/ppermute | solution.py:280
  10.8 0.7 %collective-permute-start.3 = (bf16[2,256,256]{2,1,0:T(8,128)(2,1)S(1)}, bf16[2,256,256]{2,1,0:T(8,128)(2,1)S(1)}, u32[]{:S(2)}, u32[]{:S(2)}) collective-permute-start(bf16[2,256,256]{2,1,0:T(8,128)(2,1)S(1)} %collective-permute-done.beside_ref), channel_id=1, source_target_pairs={{1,2},{2,1},{5,6},{6,5},{9,10},{10,9},{13,14},{14,13},{17,18},{18,... | collective-permute-start | bytes 786440 | tf_op jit(solution)/shard_map/ppermute | solution.py:282
  11.5 0.3 collective-permute-start.7
  11.8 6.0 %collective-permute-start.8 = (bf16[2,128,256]{2,1,0:T(8,128)(2,1)S(1)}, bf16[2,128,256]{2,1,0:T(8,128)(2,1)S(1)}, u32[]{:S(2)}, u32[]{:S(2)}) collective-permute-start(bf16[2,128,256]{2,1,0:T(8,128)(2,1)S(1)} %get-tuple-element.15.refs_0_), channel_id=1, source_target_pairs={{0,2},{1,3},{2,0},{3,1},{4,6},{5,7},{6,4},{7,5},{8,10},{9,11},{10,... | collective-permute-start | bytes 393224 | tf_op jit(solution)/shard_map/ppermute | solution.py:277
  17.8 0.0 collective-permute-start.9
  20.4 2.2 %shard_map.74.refs_4_.res_ref = bf16[4,2,384,256]{3,2,1,0:T(8,128)(2,1)S(1)} custom-call(bf16[1,2,384,1024]{3,2,1,0:T(8,128)(2,1)S(1)} %copy-done, bf16[2,32,1024]{2,1,0:T(8,128)(2,1)S(1)} %collective-permute-done.5.low_ref, bf16[2,32,1024]{2,1,0:T(8,128)(2,1)S(1)} %collective-permute-done.6.high_ref, s32[1,1]{1,0:T(1,128)S(6)} %copy.8.ao_hbm, ...), custom_call_target="tpu_custom_call" | custom-call | flops 1107296256 | bytes 3145728 | tf_op jit(solution)/shard_map/pallas_call | solution.py:243
  22.6 14.1 %collective-permute-done.8.refs_2_ = bf16[2,128,256]{2,1,0:T(8,128)(2,1)S(1)} collective-permute-done((bf16[2,128,256]{2,1,0:T(8,128)(2,1)S(1)}, bf16[2,128,256]{2,1,0:T(8,128)(2,1)S(1)}, u32[]{:S(2)}, u32[]{:S(2)}) %collective-permute-start.8) | collective-permute-done | bytes 131104 | tf_op jit(solution)/shard_map/ppermute | solution.py:277
  36.6 0.0 collective-permute-done.9.refs_3_
  36.6 0.5 shard_map.75
  37.2 1.9 %collective-permute-start.10 = (bf16[2,64,1024]{2,1,0:T(8,128)(2,1)S(1)}, bf16[2,64,1024]{2,1,0:T(8,128)(2,1)S(1)}, u32[]{:S(2)}, u32[]{:S(2)}) collective-permute-start(bf16[2,64,1024]{2,1,0:T(8,128)(2,1)S(1)} %get-tuple-element.18), channel_id=1, source_target_pairs={{4,0},{8,4},{12,8},{16,12},{20,16},{24,20},{28,24},{5,1},{9,5},{13... | collective-permute-start | bytes 786440 | tf_op jit(solution)/shard_map/ppermute | solution.py:23
  39.1 0.0 collective-permute-done.1.near_ref
  39.1 1.3 %collective-permute-start.2 = (bf16[2,256,256]{2,1,0:T(8,128)(2,1)S(1)}, bf16[2,256,256]{2,1,0:T(8,128)(2,1)S(1)}, u32[]{:S(2)}, u32[]{:S(2)}) collective-permute-start(bf16[2,256,256]{2,1,0:T(8,128)(2,1)S(1)} %collective-permute-done.1.near_ref), channel_id=1, source_target_pairs={{1,0},{2,3},{5,4},{6,7},{9,8},{10,11},{13,12},{14,15},{17,16},{18,... | collective-permute-start | bytes 786440 | tf_op jit(solution)/shard_map/ppermute | solution.py:283
  40.4 1.3 %collective-permute-start.4 = (bf16[2,256,256]{2,1,0:T(8,128)(2,1)S(1)}, bf16[2,256,256]{2,1,0:T(8,128)(2,1)S(1)}, u32[]{:S(2)}, u32[]{:S(2)}) collective-permute-start(bf16[2,256,256]{2,1,0:T(8,128)(2,1)S(1)} %collective-permute-done.3.far_ref), channel_id=1, source_target_pairs={{1,0},{2,3},{5,4},{6,7},{9,8},{10,11},{13,12},{14,15},{17,16},{18,... | collective-permute-start | bytes 786440 | tf_op jit(solution)/shard_map/ppermute | solution.py:284
  41.7 0.8 %slice_convert_fusion = f32[64]{0:T(128)S(1)} fusion(s32[384]{0:T(512)} %param.9), kind=kLoop, calls=%fused_computation | loop fusion | flops 64 | bytes 512 | tf_op jit(solution)/shard_map/convert_element_type | solution.py:285
  42.5 0.5 collective-permute-done.10.later_ref
  43.0 0.1 broadcast_in_dim.2.weight_ref
  43.0 0.3 shard_map.76
  43.4 1.9 %collective-permute-start.11 = (f32[8,128]{1,0:T(8,128)S(1)}, f32[8,128]{1,0:T(8,128)S(1)}, u32[]{:S(2)}, u32[]{:S(2)}) collective-permute-start(f32[8,128]{1,0:T(8,128)S(1)} %shard_map.76), channel_id=1, source_target_pairs={{0,4},{4,0},{8,12},{12,8},{16,20},{20,16},{24,28},{28,24},{1,5},{5... | collective-permute-start | bytes 12296 | tf_op jit(solution)/shard_map/ppermute | solution.py:322
  45.2 0.8 %collective-permute-done.11 = f32[8,128]{1,0:T(8,128)S(1)} collective-permute-done((f32[8,128]{1,0:T(8,128)S(1)}, f32[8,128]{1,0:T(8,128)S(1)}, u32[]{:S(2)}, u32[]{:S(2)}) %collective-permute-start.11) | collective-permute-done | bytes 4128 | tf_op jit(solution)/shard_map/ppermute | solution.py:322
  46.1 0.8 %collective-permute-start.12 = (f32[8,128]{1,0:T(8,128)S(1)}, f32[8,128]{1,0:T(8,128)S(1)}, u32[]{:S(2)}, u32[]{:S(2)}) collective-permute-start(f32[8,128]{1,0:T(8,128)S(1)} %add.6), channel_id=1, source_target_pairs={{0,8},{4,12},{8,0},{12,4},{16,24},{20,28},{24,16},{28,20},{1,9},{5... | collective-permute-start | bytes 12296 | tf_op jit(solution)/shard_map/ppermute | solution.py:322
  46.9 2.8 %collective-permute-done.12 = f32[8,128]{1,0:T(8,128)S(1)} collective-permute-done((f32[8,128]{1,0:T(8,128)S(1)}, f32[8,128]{1,0:T(8,128)S(1)}, u32[]{:S(2)}, u32[]{:S(2)}) %collective-permute-start.12) | collective-permute-done | bytes 4128 | tf_op jit(solution)/shard_map/ppermute | solution.py:322
  49.7 0.0 collective-permute-start.13
  49.7 3.6 %collective-permute-done.13.other_ref = f32[8,128]{1,0:T(8,128)S(1)} collective-permute-done((f32[8,128]{1,0:T(8,128)S(1)}, f32[8,128]{1,0:T(8,128)S(1)}, u32[]{:S(2)}, u32[]{:S(2)}) %collective-permute-start.13) | collective-permute-done | bytes 4128 | tf_op jit(solution)/shard_map/ppermute | solution.py:322
  53.3 2.0 %collective-permute-done.4.far_end_ref = bf16[2,256,256]{2,1,0:T(8,128)(2,1)S(1)} collective-permute-done((bf16[2,256,256]{2,1,0:T(8,128)(2,1)S(1)}, bf16[2,256,256]{2,1,0:T(8,128)(2,1)S(1)}, u32[]{:S(2)}, u32[]{:S(2)}) %collective-permute-start.4) | collective-permute-done | bytes 262176 | tf_op jit(solution)/shard_map/ppermute | solution.py:284
  55.3 1.5 %shard_map.77 = f32[1,2,192,128]{3,2,1,0:T(8,128)} custom-call(bf16[2,256,256]{2,1,0:T(8,128)(2,1)S(1)} %get-tuple-element.12.own_ref, bf16[2,256,256]{2,1,0:T(8,128)(2,1)S(1)} %collective-permute-done.beside_ref, bf16[2,256,256]{2,1,0:T(8,128)(2,1)S(1)} %collective-permute-done.1.near_ref, bf16[2,256,256]{2,1,0:T(8,128)(2,1)S(1)} %collective-permute-done.2.near_end_ref, ...), custom_call_target="tpu_custom_call" | custom-call | flops 201326592 | bytes 3145728 | tf_op jit(solution)/shard_map/pallas_call | solution.py:243
  (9 shorter events, 0.0 us)
Async XLA Ops:
  0.0 1.4 %copy-start = (bf16[1,2,384,1024]{3,2,1,0:T(8,128)(2,1)S(1)}, bf16[1,2,384,1024]{3,2,1,0:T(8,128)(2,1)}, u32[]{:S(2)}) copy-start(bf16[1,2,384,1024]{3,2,1,0:T(8,128)(2,1)} %sec_ref.3) | copy-start | bytes 4718596
  1.4 1.0 %copy-start.1 = (bf16[2,384,256]{2,1,0:T(8,128)(2,1)S(1)}, bf16[2,384,256]{2,1,0:T(8,128)(2,1)}, u32[]{:S(2)}) copy-start(bf16[2,384,256]{2,1,0:T(8,128)(2,1)} %prim_ref.1) | copy-start | bytes 1179652
  2.7 8.1 %collective-permute-start = (bf16[2,256,256]{2,1,0:T(8,128)(2,1)S(1)}, bf16[2,256,256]{2,1,0:T(8,128)(2,1)S(1)}, u32[]{:S(2)}, u32[]{:S(2)}) collective-permute-start(bf16[2,256,256]{2,1,0:T(8,128)(2,1)S(1)} %get-tuple-element.12.own_ref), channel_id=1, source_target_pairs={{0,1},{1,0},{2,3},{3,2},{4,5},{5,4},{6,7},{7,6},{8,9},{9,8},{10,11... | collective-permute-start | bytes 786440 | tf_op jit(solution)/shard_map/ppermute | solution.py:280
  3.2 8.5 %collective-permute-start.5 = (bf16[2,32,1024]{2,1,0:T(8,128)(2,1)S(1)}, bf16[2,32,1024]{2,1,0:T(8,128)(2,1)S(1)}, u32[]{:S(2)}, u32[]{:S(2)}) collective-permute-start(bf16[2,32,1024]{2,1,0:T(8,128)(2,1)S(1)} %get-tuple-element.13), channel_id=1, source_target_pairs={{0,4},{4,8},{8,12},{12,16},{16,20},{20,24},{24,28},{1,5},{5,9},{9,... | collective-permute-start | bytes 393224 | tf_op jit(solution)/shard_map/ppermute | solution.py:23
  5.1 12.6 %collective-permute-start.6 = (bf16[2,32,1024]{2,1,0:T(8,128)(2,1)S(1)}, bf16[2,32,1024]{2,1,0:T(8,128)(2,1)S(1)}, u32[]{:S(2)}, u32[]{:S(2)}) collective-permute-start(bf16[2,32,1024]{2,1,0:T(8,128)(2,1)S(1)} %get-tuple-element.14), channel_id=1, source_target_pairs={{4,0},{8,4},{12,8},{16,12},{20,16},{24,20},{28,24},{5,1},{9,5},{13... | collective-permute-start | bytes 393224 | tf_op jit(solution)/shard_map/ppermute | solution.py:23
  8.8 30.3 %collective-permute-start.1 = (bf16[2,256,256]{2,1,0:T(8,128)(2,1)S(1)}, bf16[2,256,256]{2,1,0:T(8,128)(2,1)S(1)}, u32[]{:S(2)}, u32[]{:S(2)}) collective-permute-start(bf16[2,256,256]{2,1,0:T(8,128)(2,1)S(1)} %get-tuple-element.12.own_ref), channel_id=1, source_target_pairs={{1,2},{2,1},{5,6},{6,5},{9,10},{10,9},{13,14},{14,13},{17,18},{18,... | collective-permute-start | bytes 786440 | tf_op jit(solution)/shard_map/ppermute | solution.py:281
  10.8 29.6 %collective-permute-start.3 = (bf16[2,256,256]{2,1,0:T(8,128)(2,1)S(1)}, bf16[2,256,256]{2,1,0:T(8,128)(2,1)S(1)}, u32[]{:S(2)}, u32[]{:S(2)}) collective-permute-start(bf16[2,256,256]{2,1,0:T(8,128)(2,1)S(1)} %collective-permute-done.beside_ref), channel_id=1, source_target_pairs={{1,2},{2,1},{5,6},{6,5},{9,10},{10,9},{13,14},{14,13},{17,18},{18,... | collective-permute-start | bytes 786440 | tf_op jit(solution)/shard_map/ppermute | solution.py:282
  11.5 11.1 %collective-permute-start.7 = (bf16[2,128,256]{2,1,0:T(8,128)(2,1)S(1)}, bf16[2,128,256]{2,1,0:T(8,128)(2,1)S(1)}, u32[]{:S(2)}, u32[]{:S(2)}) collective-permute-start(bf16[2,128,256]{2,1,0:T(8,128)(2,1)S(1)} %get-tuple-element.15.refs_0_), channel_id=1, source_target_pairs={{0,1},{1,2},{2,3},{3,0},{4,5},{5,6},{6,7},{7,4},{8,9},{9,10},{10,1... | collective-permute-start | bytes 393224 | tf_op jit(solution)/shard_map/ppermute | solution.py:277
  11.8 24.9 %collective-permute-start.8 = (bf16[2,128,256]{2,1,0:T(8,128)(2,1)S(1)}, bf16[2,128,256]{2,1,0:T(8,128)(2,1)S(1)}, u32[]{:S(2)}, u32[]{:S(2)}) collective-permute-start(bf16[2,128,256]{2,1,0:T(8,128)(2,1)S(1)} %get-tuple-element.15.refs_0_), channel_id=1, source_target_pairs={{0,2},{1,3},{2,0},{3,1},{4,6},{5,7},{6,4},{7,5},{8,10},{9,11},{10,... | collective-permute-start | bytes 393224 | tf_op jit(solution)/shard_map/ppermute | solution.py:277
  17.8 18.9 %collective-permute-start.9 = (bf16[2,128,256]{2,1,0:T(8,128)(2,1)S(1)}, bf16[2,128,256]{2,1,0:T(8,128)(2,1)S(1)}, u32[]{:S(2)}, u32[]{:S(2)}) collective-permute-start(bf16[2,128,256]{2,1,0:T(8,128)(2,1)S(1)} %get-tuple-element.15.refs_0_), channel_id=1, source_target_pairs={{0,3},{1,0},{2,1},{3,2},{4,7},{5,4},{6,5},{7,6},{8,11},{9,8},{10,9... | collective-permute-start | bytes 393224 | tf_op jit(solution)/shard_map/ppermute | solution.py:277
  37.2 5.8 %collective-permute-start.10 = (bf16[2,64,1024]{2,1,0:T(8,128)(2,1)S(1)}, bf16[2,64,1024]{2,1,0:T(8,128)(2,1)S(1)}, u32[]{:S(2)}, u32[]{:S(2)}) collective-permute-start(bf16[2,64,1024]{2,1,0:T(8,128)(2,1)S(1)} %get-tuple-element.18), channel_id=1, source_target_pairs={{4,0},{8,4},{12,8},{16,12},{20,16},{24,20},{28,24},{5,1},{9,5},{13... | collective-permute-start | bytes 786440 | tf_op jit(solution)/shard_map/ppermute | solution.py:23
  39.1 14.2 %collective-permute-start.2 = (bf16[2,256,256]{2,1,0:T(8,128)(2,1)S(1)}, bf16[2,256,256]{2,1,0:T(8,128)(2,1)S(1)}, u32[]{:S(2)}, u32[]{:S(2)}) collective-permute-start(bf16[2,256,256]{2,1,0:T(8,128)(2,1)S(1)} %collective-permute-done.1.near_ref), channel_id=1, source_target_pairs={{1,0},{2,3},{5,4},{6,7},{9,8},{10,11},{13,12},{14,15},{17,16},{18,... | collective-permute-start | bytes 786440 | tf_op jit(solution)/shard_map/ppermute | solution.py:283
  40.4 14.9 %collective-permute-start.4 = (bf16[2,256,256]{2,1,0:T(8,128)(2,1)S(1)}, bf16[2,256,256]{2,1,0:T(8,128)(2,1)S(1)}, u32[]{:S(2)}, u32[]{:S(2)}) collective-permute-start(bf16[2,256,256]{2,1,0:T(8,128)(2,1)S(1)} %collective-permute-done.3.far_ref), channel_id=1, source_target_pairs={{1,0},{2,3},{5,4},{6,7},{9,8},{10,11},{13,12},{14,15},{17,16},{18,... | collective-permute-start | bytes 786440 | tf_op jit(solution)/shard_map/ppermute | solution.py:284
  43.4 2.7 %collective-permute-start.11 = (f32[8,128]{1,0:T(8,128)S(1)}, f32[8,128]{1,0:T(8,128)S(1)}, u32[]{:S(2)}, u32[]{:S(2)}) collective-permute-start(f32[8,128]{1,0:T(8,128)S(1)} %shard_map.76), channel_id=1, source_target_pairs={{0,4},{4,0},{8,12},{12,8},{16,20},{20,16},{24,28},{28,24},{1,5},{5... | collective-permute-start | bytes 12296 | tf_op jit(solution)/shard_map/ppermute | solution.py:322
  46.1 3.6 %collective-permute-start.12 = (f32[8,128]{1,0:T(8,128)S(1)}, f32[8,128]{1,0:T(8,128)S(1)}, u32[]{:S(2)}, u32[]{:S(2)}) collective-permute-start(f32[8,128]{1,0:T(8,128)S(1)} %add.6), channel_id=1, source_target_pairs={{0,8},{4,12},{8,0},{12,4},{16,24},{20,28},{24,16},{28,20},{1,9},{5... | collective-permute-start | bytes 12296 | tf_op jit(solution)/shard_map/ppermute | solution.py:322
  49.7 3.6 %collective-permute-start.13 = (f32[8,128]{1,0:T(8,128)S(1)}, f32[8,128]{1,0:T(8,128)S(1)}, u32[]{:S(2)}, u32[]{:S(2)}) collective-permute-start(f32[8,128]{1,0:T(8,128)S(1)} %add.7.mine_ref), channel_id=1, source_target_pairs={{0,16},{4,20},{8,24},{12,28},{16,0},{20,4},{24,8},{28,12},{1,17},{... | collective-permute-start | bytes 12296 | tf_op jit(solution)/shard_map/ppermute | solution.py:322

commit v3 on v2

--- a/solution.py
+++ b/solution.py
@@ -42,30 +42,30 @@
     return total.astype(jnp.bfloat16)
 
 
-def prepare_kernel(sec_ref, prim_ref, edges_ref, middle_ref, down_ref, up_ref, sems):
-    rows_n = sec_ref.shape[2]
-    pieces = (
-        (prim_ref.at[:, :LAG], edges_ref.at[:, :LAG]),
-        (prim_ref.at[:, rows_n - LAG :], edges_ref.at[:, LAG:]),
-        (sec_ref.at[0, :, rows_n - HALO :], down_ref),
-        (sec_ref.at[0, :, :HALO], up_ref),
-        (prim_ref.at[:, LAG : rows_n - LAG], middle_ref),
-    )
-    copies = [pltpu.make_async_copy(*piece, sems.at[at]) for at, piece in enumerate(pieces)]
+def start_all(pairs, sems):
+    copies = [pltpu.make_async_copy(*pair, sems.at[at]) for at, pair in enumerate(pairs)]
     for copy in copies:
         copy.start()
-    for copy in copies:
+    return copies
+
+
+def prepare_kernel(sec_ref, prim_ref, edges_ref, down_ref, up_ref, sems):
+    rows_n = sec_ref.shape[2]
+    pieces = [(sec_ref.at[0, :, rows_n - HALO :], down_ref), (sec_ref.at[0, :, :HALO], up_ref)]
+    for to in range(edges_ref.shape[0]):
+        pieces.append((prim_ref.at[:, :LAG], edges_ref.at[to, :, :LAG]))
+        pieces.append((prim_ref.at[:, rows_n - LAG :], edges_ref.at[to, :, LAG:]))
+    for copy in start_all(pieces, sems):
         copy.wait()
 
 
 def resample_kernel(
-    sec_ref, low_ref, high_ref, ao_hbm, ro_hbm, af_hbm, rf_hbm, out_ref,
+    sec_ref, low_ref, high_ref, prim_hbm, ao_hbm, ro_hbm, af_hbm, rf_hbm, out_ref, middle_ref,
     azim_ref, ao_ref, ro_ref, af_ref, rf_ref, sems,
 ):
-    numbers = ((ao_hbm, ao_ref), (ro_hbm, ro_ref), (af_hbm, af_ref), (rf_hbm, rf_ref))
-    copies = [pltpu.make_async_copy(*pair, sems.at[at]) for at, pair in enumerate(numbers)]
-    for copy in copies:
-        copy.start()
+    last = prim_hbm.shape[1] - LAG
+    numbers = [(ao_hbm, ao_ref), (ro_hbm, ro_ref), (af_hbm, af_ref), (rf_hbm, rf_ref)]
+    *copies, middle = start_all(numbers + [(prim_hbm.at[:, LAG:last], middle_ref)], sems)
     for copy in copies:
         copy.wait()
     rows_n, cols_n = sec_ref.shape[2:]
@@ -110,6 +110,7 @@
             out_ref[block, part] = jnp.dot(
                 azim_ref[part, :, taken], used, preferred_element_type=jnp.float32
             ).astype(jnp.bfloat16)
+    middle.wait()
 
 
 def interfere(prim_re, prim_im, sec_re, sec_im):
@@ -133,22 +134,18 @@
     return total
 
 
-def margin_kernel(*refs):
-    blocks_n, _, rows_n, width = refs[4].shape
-    prims, (res_ref, first_ref, last_ref, looks_ref, sums_ref) = refs[:4], refs[4:]
+def margin_kernel(prim_ref, res_ref, first_ref, last_ref, looks_ref, sums_ref):
+    blocks_n, _, rows_n, width = res_ref.shape
     looks_n = looks_ref.shape[2]
-    here = lax.axis_index("date")
     totals = [None, None]
-    for step in range(blocks_n):
-        block = lax.rem(here + (blocks_n - step), blocks_n)
-        prim_ref = prims[step]
+    for block in range(blocks_n):
         select = look_columns(width, block, looks_n)
-        columns = pl.ds(pl.multiple_of(block * width, width), width)
+        columns = slice(block * width, (block + 1) * width)
         halves = []
         for held, start, target in ((0, 0, first_ref), (LAG, rows_n - LAG, last_ref)):
             pair = interfere(
-                prim_ref[0, held : held + LAG],
-                prim_ref[1, held : held + LAG],
+                prim_ref[block, 0, held : held + LAG],
+                prim_ref[block, 1, held : held + LAG],
                 res_ref[block, 0, start : start + LAG],
                 res_ref[block, 1, start : start + LAG],
             )
@@ -159,17 +156,26 @@
         for part in range(2):
             both = jnp.concatenate([halves[0][part], halves[1][part]], axis=0)
             summed = jnp.dot(both, select, preferred_element_type=jnp.float32)
-            totals[part] = summed if step == 0 else totals[part] + summed
+            totals[part] = summed if block == 0 else totals[part] + summed
     for part in range(2):
         sums_ref[part] = totals[part]
         looks_ref[part] = look_rows(sums_ref, part, 0, 2 * LAG)
 
 
-def stats_kernel(last_ref, later_ref, weight_ref, stats_ref):
-    cols_n = last_ref.shape[2]
+def stats_kernel(last_ref, later_ref, mask_ref, stats_ref):
+    _, lag, cols_n = last_ref.shape
+    rows_n = mask_ref.shape[0]
+    mask = mask_ref[...].reshape(1, rows_n).astype(jnp.float32)
+    shape = (lag, rows_n)
+    row = lax.broadcasted_iota(jnp.int32, shape, 0) + (rows_n - lag)
+    picked = jnp.where(row == lax.broadcasted_iota(jnp.int32, shape, 1), mask, 0.0)
+    weight = jnp.dot(
+        picked.astype(jnp.bfloat16),
+        jnp.ones((rows_n, LANE), jnp.bfloat16),
+        preferred_element_type=jnp.float32,
+    )
     i_re, i_im = last_ref[0].astype(jnp.float32), last_ref[1].astype(jnp.float32)
     l_re, l_im = later_ref[0].astype(jnp.float32), later_ref[1].astype(jnp.float32)
-    weight = weight_ref[...]
     values = (
         i_re * l_re + i_im * l_im,
         i_im * l_re - i_re * l_im,
@@ -183,12 +189,14 @@
         rows.append(jnp.sum(folded * weight, axis=0, keepdims=True))
     rows.append(jnp.sum(weight, axis=0, keepdims=True) * (cols_n // LANE))
     rows.append(jnp.zeros((4, LANE), jnp.float32))
-    stats_ref[...] = jnp.concatenate(rows, axis=0)
+    stats = jnp.concatenate(rows, axis=0)
+    for to in range(stats_ref.shape[0]):
+        stats_ref[to] = stats
 
 
 def finish_kernel(
-    own_ref, beside_ref, near_ref, near_end_ref, far_ref, far_end_ref,
-    res_ref, looks_ref, mine_ref, other_ref, out_ref, sums_ref,
+    own_ref, beside_ref, near_ref, skip_ref, far_ref, res_ref, looks_ref, stats_ref,
+    out_ref, sums_ref,
 ):
     _, _, rows_n, width = res_ref.shape
     looks_n = out_ref.shape[3]
@@ -200,8 +208,8 @@
     for step, (block, prim_ref, end_ref) in enumerate((
         (here, own_ref, None),
         (jnp.where(lax.rem(here, 2) == 0, here + 1, here - 1), beside_ref, None),
-        (jnp.where(low, 2, 1), near_ref, near_end_ref),
-        (jnp.where(low, 3, 0), far_ref, far_end_ref),
+        (jnp.where(low, 2, 1), near_ref, skip_ref),
+        (jnp.where(low, 3, 0), skip_ref, far_ref),
     )):
         select = look_columns(width, block, looks_n)
         if end_ref is None:
@@ -219,7 +227,7 @@
                 pair[part].astype(jnp.bfloat16), select, preferred_element_type=jnp.float32
             )
             totals[part] = summed if step == 0 else totals[part] + summed
-    stats = jnp.sum(mine_ref[...] + other_ref[...], axis=1, keepdims=True)
+    stats = jnp.sum(jnp.sum(stats_ref[...], axis=0), axis=1, keepdims=True)
     e_re, e_im, power, count = [stats[row : row + 1] for row in range(4)]
     magnitude = jnp.sqrt(e_re * e_re + e_im * e_im)
     floor_val = (power + 1e-06) / jnp.sqrt(jnp.maximum(count, 1.0))
@@ -261,72 +269,61 @@
     looks_n = cols_n // LR
     middle_n = rows_n - 2 * LAG
     vmem = pl.BlockSpec(memory_space=pltpu.VMEM)
-    hbm = pl.BlockSpec(memory_space=pl.ANY)
+    hbm = pl.BlockSpec(memory_space=pltpu.HBM)
 
     halo = shape((2, HALO, cols_n), bf16)
-    edges, middle, down, up = call(
+    edges, down, up = call(
         prepare_kernel,
-        (shape((2, 2 * LAG, width), bf16), shape((2, middle_n, width), bf16), halo, halo),
-        [pltpu.SemaphoreType.DMA((5,))],
+        (shape((dates_n, 2, 2 * LAG, width), bf16), halo, halo),
+        [pltpu.SemaphoreType.DMA((2 + 2 * dates_n,))],
         (0, 4 * 2 * rows_n * width),
         secondary, primary, places=[hbm] * 2,
     )
+    edges = lax.all_to_all(edges, "date", 0, 0, tiled=True)
     low = passed_along(down, "tile", 1)
     high = passed_along(up, "tile", -1)
-    around = [edges] + [
-        lax.ppermute(edges, "date", [(at, (at + step) % dates_n) for at in range(dates_n)])
-        for step in range(1, dates_n)
-    ]
-    beside = lax.ppermute(middle, "date", [(0, 1), (1, 0), (2, 3), (3, 2)])
-    near = lax.ppermute(middle, "date", [(1, 2), (2, 1)])
-    far = lax.ppermute(beside, "date", [(1, 2), (2, 1)])
-    near_end = lax.ppermute(near, "date", [(1, 0), (2, 3)])
-    far_end = lax.ppermute(far, "date", [(1, 0), (2, 3)])
-    weight = jnp.broadcast_to(margin_mask[rows_n - LAG :].astype(f32)[:, None], (LAG, LANE))
-
-    res = call(
+    res, middle = call(
         resample_kernel,
-        shape((dates_n, 2, rows_n, width), bf16),
+        (shape((dates_n, 2, rows_n, width), bf16), shape((2, middle_n, width), bf16)),
         [
             pltpu.VMEM((2, rows_n, cols_n), bf16),
             pltpu.SMEM((1, 1), jnp.int32),
             pltpu.SMEM((1, 1), jnp.int32),
             pltpu.SMEM((1, 1), f32),
             pltpu.SMEM((1, 1), f32),
-            pltpu.SemaphoreType.DMA((4,)),
+            pltpu.SemaphoreType.DMA((5,)),
         ],
         (2 * 2 * rows_n * cols_n * (2 * HALO + BAND + 2 * width), 8 * rows_n * cols_n),
-        secondary, low, high, az_off, rg_off, az_frac, rg_frac,
-        places=[vmem] * 3 + [hbm] * 4,
-    )
+        secondary, low, high, primary, az_off, rg_off, az_frac, rg_frac,
+        places=[vmem] * 3 + [hbm] * 5,
+    )
+    skip = lax.ppermute(middle, "date", [(0, 2), (2, 0), (1, 3), (3, 1)])
+    beside = lax.ppermute(middle, "date", [(0, 1), (1, 0), (2, 3), (3, 2)])
+    near = lax.ppermute(middle, "date", [(1, 2), (2, 1)])
+    far = lax.ppermute(skip, "date", [(1, 0), (2, 3)])
     margin = shape((2, LAG, cols_n), bf16)
     first, last, looks = call(
         margin_kernel,
         (margin, margin, shape((2, 2 * LAG // LA, looks_n), f32)),
         [pltpu.VMEM((2, 2 * LAG, looks_n), f32)],
         (2 * 2 * 2 * LAG * cols_n * looks_n, 24 * LAG * cols_n),
-        *around, res,
+        edges, res,
     )
     later = passed_along(first, "tile", -1)
     stats = call(
         stats_kernel,
-        shape((8, LANE), f32),
+        shape((tiles_n, 8, LANE), f32),
         [],
         (20 * LAG * cols_n, 8 * LAG * cols_n),
-        last, later, weight,
-    )
-    stride = 1
-    other = jnp.zeros_like(stats)
-    while stride < tiles_n:
-        stats = stats + other if stride > 1 else stats
-        other = lax.ppermute(stats, "tile", [(at, at ^ stride) for at in range(tiles_n)])
-        stride *= 2
+        last, later, margin_mask,
+    )
+    stats = lax.all_to_all(stats, "tile", 0, 0, tiled=True)
     return call(
         finish_kernel,
         shape((1, 2, rows_n // LA, looks_n), f32),
         [pltpu.VMEM((2, middle_n, looks_n), f32)],
         (2 * 2 * rows_n * cols_n * looks_n, 8 * rows_n * cols_n),
-        middle, beside, near, near_end, far, far_end, res, looks, stats, other,
+        middle, beside, near, skip, far, res, looks, stats,
     )
 
 
@@ -403,9 +400,8 @@
 
 def shards(secondary, primary, *rest):
     rows_n, width = primary.shape[1:]
-    tiles_n = lax.axis_size("tile")
     fits = rows_n % BAND == 0 and rows_n > 2 * LAG + BAND and width % LANE == 0
-    fits = fits and lax.axis_size("date") == 4 and tiles_n & (tiles_n - 1) == 0
+    fits = fits and lax.axis_size("date") == 4
     return (fused if fits else plain)(secondary, primary, *rest)
 
 

time: 57.2 us -> 51.4 us (0.90)
  the two profiles are of different devices: /device:TPU:26 before, /device:TPU:16 now
where the time goes in v3:
time: 51.4 us; the launch traced here: 51 us
  starting transfers between devices  26.6 us (52%)
  waiting for transfers between devices  11.4 us (22%)
  Pallas kernels  6.47 us (13%)
  local copies, waits for them, and re-layouts  3.82 us (7%)
  between operations  2.72 us (5%)
    ppermute x1, starting transfers between devices, fused(): far = lax.ppermute(skip, 'date', [(1, 0), (2, 3)])  8.14 us
    pallas_call x5, Pallas kernels, call(): pl.pallas_call(kernel, out_shape=outs, in_specs=places or [vmem] * len(ar...  6.47 us
    all_to_all x1, starting transfers between devices, fused(): stats = lax.all_to_all(stats, 'tile', 0, 0, tiled=True)  5.66 us
    all_to_all x1, starting transfers between devices, fused(): edges = lax.all_to_all(edges, 'date', 0, 0, tiled=True)  5.22 us
    all_to_all x1, waiting for transfers between devices, fused(): stats = lax.all_to_all(stats, 'tile', 0, 0, tiled=True)  4.82 us
    ppermute x1, waiting for transfers between devices, fused(): skip = lax.ppermute(middle, 'date', [(0, 2), (2, 0), (1, 3), (3, 1)])  4.2 us
    ppermute x3, starting transfers between devices, passed_along(): lax.ppermute(value, axis, [(source, source + steps) for source in range(i...  3.87 us
    unnamed x10, local copies, waits for them, and re-layouts  3.82 us
  transfers between devices with their start and end apart: 9, of which 4 were waited for; matrix products, arithmetic and copies ran while one was open for 0% of the time, Pallas kernels for 7%

profile of v3, /device:TPU:16, one launch (start us, length us, event | category | flops | bytes accessed | tf_op | source)
XLA Modules:
  0.0 51.0 jit_solution(2263162551919753433)
XLA Ops:
  0.0 0.0 copy-start
  0.0 1.4 %copy-done = bf16[1,2,384,1024]{3,2,1,0:T(8,128)(2,1)S(1)} copy-done((bf16[1,2,384,1024]{3,2,1,0:T(8,128)(2,1)S(1)}, bf16[1,2,384,1024]{3,2,1,0:T(8,128)(2,1)}, u32[]{:S(2)}) %copy-start) | copy-done | bytes 1572888
  1.4 0.0 copy-start.2
  1.4 1.0 %copy-done.2 = bf16[2,384,256]{2,1,0:T(8,128)(2,1)S(1)} copy-done((bf16[2,384,256]{2,1,0:T(8,128)(2,1)S(1)}, bf16[2,384,256]{2,1,0:T(8,128)(2,1)}, u32[]{:S(2)}) %copy-start.2) | copy-done | bytes 393240
  2.4 0.0 copy-start.3
  2.4 1.4 %shard_map.73 = (bf16[4,2,128,256]{3,2,1,0:T(8,128)(2,1)}, bf16[2,32,1024]{2,1,0:T(8,128)(2,1)S(1)}, bf16[2,32,1024]{2,1,0:T(8,128)(2,1)S(1)}) custom-call(bf16[1,2,384,1024]{3,2,1,0:T(8,128)(2,1)S(1)} %copy-done, bf16[2,384,256]{2,1,0:T(8,128)(2,1)S(1)} %copy-done.2), custom_call_target="tpu_custom_call" | custom-call | bytes 786432 | tf_op jit(solution)/shard_map/pallas_call | solution.py:251
  3.8 5.2 %all-to-all-start = ((bf16[4,2,128,256]{3,2,1,0:T(8,128)(2,1)}), bf16[4,2,128,256]{3,2,1,0:T(8,128)(2,1)S(1)}, u32[]{:S(2)}, u32[]{:S(2)}) async-start(bf16[4,2,128,256]{3,2,1,0:T(8,128)(2,1)} %get-tuple-element.17), calls=%async_computation | async-start | bytes 1048576 | tf_op jit(solution)/shard_map/all_to_all | solution.py:282
  9.0 1.3 %collective-permute-start = (bf16[2,32,1024]{2,1,0:T(8,128)(2,1)S(1)}, bf16[2,32,1024]{2,1,0:T(8,128)(2,1)S(1)}, u32[]{:S(2)}, u32[]{:S(2)}) collective-permute-start(bf16[2,32,1024]{2,1,0:T(8,128)(2,1)S(1)} %get-tuple-element.13), channel_id=1, source_target_pairs={{0,4},{4,8},{8,12},{12,16},{16,20},{20,24},{24,28},{1,5},{5,9},{9,... | collective-permute-start | bytes 393224 | tf_op jit(solution)/shard_map/ppermute | solution.py:23
  10.3 1.3 %collective-permute-start.1 = (bf16[2,32,1024]{2,1,0:T(8,128)(2,1)S(1)}, bf16[2,32,1024]{2,1,0:T(8,128)(2,1)S(1)}, u32[]{:S(2)}, u32[]{:S(2)}) collective-permute-start(bf16[2,32,1024]{2,1,0:T(8,128)(2,1)S(1)} %get-tuple-element.14), channel_id=1, source_target_pairs={{4,0},{8,4},{12,8},{16,12},{20,16},{24,20},{28,24},{5,1},{9,5},{13... | collective-permute-start | bytes 393224 | tf_op jit(solution)/shard_map/ppermute | solution.py:23
  14.2 0.0 collective-permute-done.low_ref
  14.2 1.1 %collective-permute-done.1.high_ref = bf16[2,32,1024]{2,1,0:T(8,128)(2,1)S(1)} collective-permute-done((bf16[2,32,1024]{2,1,0:T(8,128)(2,1)S(1)}, bf16[2,32,1024]{2,1,0:T(8,128)(2,1)S(1)}, u32[]{:S(2)}, u32[]{:S(2)}) %collective-permute-start.1) | collective-permute-done | bytes 131104 | tf_op jit(solution)/shard_map/ppermute | solution.py:23
  15.3 0.0 copy-done.3
  15.3 1.4 %copy-done.1 = bf16[1,2,384,1024]{3,2,1,0:T(8,128)(2,1)S(1)} copy-done((bf16[1,2,384,1024]{3,2,1,0:T(8,128)(2,1)S(1)}, bf16[1,2,384,1024]{3,2,1,0:T(8,128)(2,1)}, u32[]{:S(2)}) %copy-start.1) | copy-done | bytes 1572888
  16.7 2.2 %shard_map.74 = (bf16[4,2,384,256]{3,2,1,0:T(8,128)(2,1)S(1)}, bf16[2,256,256]{2,1,0:T(8,128)(2,1)S(1)}) custom-call(bf16[1,2,384,1024]{3,2,1,0:T(8,128)(2,1)S(1)} %copy-done.1, bf16[2,32,1024]{2,1,0:T(8,128)(2,1)S(1)} %collective-permute-done.low_ref, bf16[2,32,1024]{2,1,0:T(8,128)(2,1)S(1)} %collective-permute-done.1.high_ref, ...), custom_call_target="tpu_custom_call" | custom-call | flops 1107296256 | bytes 3145728 | tf_op jit(solution)/shard_map/pallas_call | solution.py:251
  18.9 0.0 copy-start.4
  18.9 0.1 collective-permute-start.4
  19.0 1.3 %all-to-all-done.prim_ref = bf16[4,2,128,256]{3,2,1,0:T(8,128)(2,1)S(1)} async-done(((bf16[4,2,128,256]{3,2,1,0:T(8,128)(2,1)}), bf16[4,2,128,256]{3,2,1,0:T(8,128)(2,1)S(1)}, u32[]{:S(2)}, u32[]{:S(2)}) %all-to-all-start) | async-done | bytes 524320 | tf_op jit(solution)/shard_map/all_to_all | solution.py:282
  20.2 0.5 shard_map.75
  20.8 1.3 %collective-permute-start.6 = (bf16[2,64,1024]{2,1,0:T(8,128)(2,1)S(1)}, bf16[2,64,1024]{2,1,0:T(8,128)(2,1)S(1)}, u32[]{:S(2)}, u32[]{:S(2)}) collective-permute-start(bf16[2,64,1024]{2,1,0:T(8,128)(2,1)S(1)} %get-tuple-element.20), channel_id=1, source_target_pairs={{4,0},{8,4},{12,8},{16,12},{20,16},{24,20},{28,24},{5,1},{9,5},{13... | collective-permute-start | bytes 786440 | tf_op jit(solution)/shard_map/ppermute | solution.py:23
  22.1 3.6 %collective-permute-start.3 = (bf16[2,256,256]{2,1,0:T(8,128)(2,1)S(1)}, bf16[2,256,256]{2,1,0:T(8,128)(2,1)S(1)}, u32[]{:S(2)}, u32[]{:S(2)}) collective-permute-start(bf16[2,256,256]{2,1,0:T(8,128)(2,1)S(1)} %get-tuple-element.15.own_ref), channel_id=1, source_target_pairs={{1,2},{2,1},{5,6},{6,5},{9,10},{10,9},{13,14},{14,13},{17,18},{18,... | collective-permute-start | bytes 786440 | tf_op jit(solution)/shard_map/ppermute | solution.py:302
  25.6 0.1 collective-permute-start.2
  25.7 4.2 %collective-permute-done.4.skip_ref = bf16[2,256,256]{2,1,0:T(8,128)(2,1)S(1)} collective-permute-done((bf16[2,256,256]{2,1,0:T(8,128)(2,1)S(1)}, bf16[2,256,256]{2,1,0:T(8,128)(2,1)S(1)}, u32[]{:S(2)}, u32[]{:S(2)}) %collective-permute-start.4) | collective-permute-done | bytes 262176 | tf_op jit(solution)/shard_map/ppermute | solution.py:300
  29.9 8.1 %collective-permute-start.5 = (bf16[2,256,256]{2,1,0:T(8,128)(2,1)S(1)}, bf16[2,256,256]{2,1,0:T(8,128)(2,1)S(1)}, u32[]{:S(2)}, u32[]{:S(2)}) collective-permute-start(bf16[2,256,256]{2,1,0:T(8,128)(2,1)S(1)} %collective-permute-done.4.skip_ref), channel_id=1, source_target_pairs={{1,0},{2,3},{5,4},{6,7},{9,8},{10,11},{13,12},{14,15},{17,16},{18,... | collective-permute-start | bytes 786440 | tf_op jit(solution)/shard_map/ppermute | solution.py:303
  38.0 0.0 collective-permute-done.6.later_ref
  38.1 0.0 copy-done.4
  38.1 0.9 %shard_map.76 = f32[8,8,128]{2,1,0:T(8,128)} custom-call(bf16[2,64,1024]{2,1,0:T(8,128)(2,1)S(1)} %get-tuple-element.19.last_ref, bf16[2,64,1024]{2,1,0:T(8,128)(2,1)S(1)} %collective-permute-done.6.later_ref, s32[384]{0:T(512)S(1)} %copy-done.4), custom_call_target="tpu_custom_call" | custom-call | flops 1310720 | bytes 524288 | tf_op jit(solution)/shard_map/pallas_call | solution.py:251
  38.9 5.7 %all-to-all-start.1 = ((f32[8,8,128]{2,1,0:T(8,128)}), f32[8,8,128]{2,1,0:T(8,128)S(1)}, u32[]{:S(2)}, u32[]{:S(2)}) async-start(f32[8,8,128]{2,1,0:T(8,128)} %shard_map.76), calls=%async_computation.1 | async-start | bytes 65536 | tf_op jit(solution)/shard_map/all_to_all | solution.py:320
  44.6 0.0 collective-permute-done.3.near_ref
  44.6 0.0 collective-permute-done.2.beside_ref
  44.6 0.0 collective-permute-done.5.far_ref
  44.6 4.8 %all-to-all-done.1.stats_ref = f32[8,8,128]{2,1,0:T(8,128)S(1)} async-done(((f32[8,8,128]{2,1,0:T(8,128)}), f32[8,8,128]{2,1,0:T(8,128)S(1)}, u32[]{:S(2)}, u32[]{:S(2)}) %all-to-all-start.1) | async-done | bytes 32800 | tf_op jit(solution)/shard_map/all_to_all | solution.py:320
  49.4 1.5 %shard_map.77 = f32[1,2,192,128]{3,2,1,0:T(8,128)} custom-call(bf16[2,256,256]{2,1,0:T(8,128)(2,1)S(1)} %get-tuple-element.15.own_ref, bf16[2,256,256]{2,1,0:T(8,128)(2,1)S(1)} %collective-permute-done.2.beside_ref, bf16[2,256,256]{2,1,0:T(8,128)(2,1)S(1)} %collective-permute-done.3.near_ref, bf16[2,256,256]{2,1,0:T(8,128)(2,1)S(1)} %collective-permute-done.4.skip_ref, ...), custom_call_target="tpu_custom_call" | custom-call | flops 201326592 | bytes 3145728 | tf_op jit(solution)/shard_map/pallas_call | solution.py:251
  (1 shorter events, 0.0 us)
Async XLA Ops:
  0.0 1.4 %copy-start = (bf16[1,2,384,1024]{3,2,1,0:T(8,128)(2,1)S(1)}, bf16[1,2,384,1024]{3,2,1,0:T(8,128)(2,1)}, u32[]{:S(2)}) copy-start(bf16[1,2,384,1024]{3,2,1,0:T(8,128)(2,1)} %sec_ref.3) | copy-start | bytes 4718596
  1.4 1.0 %copy-start.2 = (bf16[2,384,256]{2,1,0:T(8,128)(2,1)S(1)}, bf16[2,384,256]{2,1,0:T(8,128)(2,1)}, u32[]{:S(2)}) copy-start(bf16[2,384,256]{2,1,0:T(8,128)(2,1)} %prim_hbm.1) | copy-start | bytes 1179652
  2.4 12.9 %copy-start.3 = (bf16[2,384,256]{2,1,0:T(8,128)(2,1)S(1)}, bf16[2,384,256]{2,1,0:T(8,128)(2,1)}, u32[]{:S(2)}) copy-start(bf16[2,384,256]{2,1,0:T(8,128)(2,1)} %prim_hbm.1) | copy-start | bytes 1179652
  3.8 16.4 %all-to-all-start = ((bf16[4,2,128,256]{3,2,1,0:T(8,128)(2,1)}), bf16[4,2,128,256]{3,2,1,0:T(8,128)(2,1)S(1)}, u32[]{:S(2)}, u32[]{:S(2)}) async-start(bf16[4,2,128,256]{3,2,1,0:T(8,128)(2,1)} %get-tuple-element.17), calls=%async_computation | async-start | bytes 1048576 | tf_op jit(solution)/shard_map/all_to_all | solution.py:282
  9.0 5.2 %collective-permute-start = (bf16[2,32,1024]{2,1,0:T(8,128)(2,1)S(1)}, bf16[2,32,1024]{2,1,0:T(8,128)(2,1)S(1)}, u32[]{:S(2)}, u32[]{:S(2)}) collective-permute-start(bf16[2,32,1024]{2,1,0:T(8,128)(2,1)S(1)} %get-tuple-element.13), channel_id=1, source_target_pairs={{0,4},{4,8},{8,12},{12,16},{16,20},{20,24},{24,28},{1,5},{5,9},{9,... | collective-permute-start | bytes 393224 | tf_op jit(solution)/shard_map/ppermute | solution.py:23
  10.3 5.0 %collective-permute-start.1 = (bf16[2,32,1024]{2,1,0:T(8,128)(2,1)S(1)}, bf16[2,32,1024]{2,1,0:T(8,128)(2,1)S(1)}, u32[]{:S(2)}, u32[]{:S(2)}) collective-permute-start(bf16[2,32,1024]{2,1,0:T(8,128)(2,1)S(1)} %get-tuple-element.14), channel_id=1, source_target_pairs={{4,0},{8,4},{12,8},{16,12},{20,16},{24,20},{28,24},{5,1},{9,5},{13... | collective-permute-start | bytes 393224 | tf_op jit(solution)/shard_map/ppermute | solution.py:23
  15.3 1.4 %copy-start.1 = (bf16[1,2,384,1024]{3,2,1,0:T(8,128)(2,1)S(1)}, bf16[1,2,384,1024]{3,2,1,0:T(8,128)(2,1)}, u32[]{:S(2)}) copy-start(bf16[1,2,384,1024]{3,2,1,0:T(8,128)(2,1)} %sec_ref.3) | copy-start | bytes 4718596
  18.9 19.2 %copy-start.4 = (s32[384]{0:T(512)S(1)}, s32[384]{0:T(512)}, u32[]{:S(2)}) copy-start(s32[384]{0:T(512)} %mask_ref.1) | copy-start | bytes 4612
  18.9 11.0 %collective-permute-start.4 = (bf16[2,256,256]{2,1,0:T(8,128)(2,1)S(1)}, bf16[2,256,256]{2,1,0:T(8,128)(2,1)S(1)}, u32[]{:S(2)}, u32[]{:S(2)}) collective-permute-start(bf16[2,256,256]{2,1,0:T(8,128)(2,1)S(1)} %get-tuple-element.15.own_ref), channel_id=1, source_target_pairs={{0,2},{2,0},{1,3},{3,1},{4,6},{6,4},{5,7},{7,5},{8,10},{10,8},{9,1... | collective-permute-start | bytes 786440 | tf_op jit(solution)/shard_map/ppermute | solution.py:300
  20.8 17.3 %collective-permute-start.6 = (bf16[2,64,1024]{2,1,0:T(8,128)(2,1)S(1)}, bf16[2,64,1024]{2,1,0:T(8,128)(2,1)S(1)}, u32[]{:S(2)}, u32[]{:S(2)}) collective-permute-start(bf16[2,64,1024]{2,1,0:T(8,128)(2,1)S(1)} %get-tuple-element.20), channel_id=1, source_target_pairs={{4,0},{8,4},{12,8},{16,12},{20,16},{24,20},{28,24},{5,1},{9,5},{13... | collective-permute-start | bytes 786440 | tf_op jit(solution)/shard_map/ppermute | solution.py:23
  22.1 22.5 %collective-permute-start.3 = (bf16[2,256,256]{2,1,0:T(8,128)(2,1)S(1)}, bf16[2,256,256]{2,1,0:T(8,128)(2,1)S(1)}, u32[]{:S(2)}, u32[]{:S(2)}) collective-permute-start(bf16[2,256,256]{2,1,0:T(8,128)(2,1)S(1)} %get-tuple-element.15.own_ref), channel_id=1, source_target_pairs={{1,2},{2,1},{5,6},{6,5},{9,10},{10,9},{13,14},{14,13},{17,18},{18,... | collective-permute-start | bytes 786440 | tf_op jit(solution)/shard_map/ppermute | solution.py:302
  25.6 19.0 %collective-permute-start.2 = (bf16[2,256,256]{2,1,0:T(8,128)(2,1)S(1)}, bf16[2,256,256]{2,1,0:T(8,128)(2,1)S(1)}, u32[]{:S(2)}, u32[]{:S(2)}) collective-permute-start(bf16[2,256,256]{2,1,0:T(8,128)(2,1)S(1)} %get-tuple-element.15.own_ref), channel_id=1, source_target_pairs={{0,1},{1,0},{2,3},{3,2},{4,5},{5,4},{6,7},{7,6},{8,9},{9,8},{10,11... | collective-permute-start | bytes 786440 | tf_op jit(solution)/shard_map/ppermute | solution.py:301
  29.9 14.7 %collective-permute-start.5 = (bf16[2,256,256]{2,1,0:T(8,128)(2,1)S(1)}, bf16[2,256,256]{2,1,0:T(8,128)(2,1)S(1)}, u32[]{:S(2)}, u32[]{:S(2)}) collective-permute-start(bf16[2,256,256]{2,1,0:T(8,128)(2,1)S(1)} %collective-permute-done.4.skip_ref), channel_id=1, source_target_pairs={{1,0},{2,3},{5,4},{6,7},{9,8},{10,11},{13,12},{14,15},{17,16},{18,... | collective-permute-start | bytes 786440 | tf_op jit(solution)/shard_map/ppermute | solution.py:303
  38.9 10.5 %all-to-all-start.1 = ((f32[8,8,128]{2,1,0:T(8,128)}), f32[8,8,128]{2,1,0:T(8,128)S(1)}, u32[]{:S(2)}, u32[]{:S(2)}) async-start(f32[8,8,128]{2,1,0:T(8,128)} %shard_map.76), calls=%async_computation.1 | async-start | bytes 65536 | tf_op jit(solution)/shard_map/all_to_all | solution.py:320

commit v4 on v1

--- a/solution.py
+++ b/solution.py
@@ -15,6 +15,7 @@
 BAND = 128
 HALO = 32
 VMEM_LIMIT = 40 * 1024 * 1024
+VMEM_ALL = 63 * 1024 * 1024
 
 
 def passed_along(value, axis, steps):
@@ -40,6 +41,26 @@
     for j in range(8):
         total = jnp.where(distance == j - 3, taps[j : j + 1, :1], total)
     return total.astype(jnp.bfloat16)
+
+
+def start_all(pairs, sems):
+    copies = [pltpu.make_async_copy(*pair, sems.at[at]) for at, pair in enumerate(pairs)]
+    for copy in copies:
+        copy.start()
+    return copies
+
+
+def prepare_kernel(sec_ref, prim_ref, edges_ref, middle_ref, down_ref, up_ref, sems):
+    rows_n = sec_ref.shape[2]
+    pieces = (
+        (prim_ref.at[:, :LAG], edges_ref.at[:, :LAG]),
+        (prim_ref.at[:, rows_n - LAG :], edges_ref.at[:, LAG:]),
+        (sec_ref.at[0, :, rows_n - HALO :], down_ref),
+        (sec_ref.at[0, :, :HALO], up_ref),
+        (prim_ref.at[:, LAG : rows_n - LAG], middle_ref),
+    )
+    for copy in start_all(pieces, sems):
+        copy.wait()
 
 
 def resample_kernel(sec_ref, low_ref, high_ref, ao_ref, ro_ref, af_ref, rf_ref, out_ref, azim_ref):
@@ -108,18 +129,33 @@
     return total
 
 
-def margin_kernel(prim_ref, res_ref, first_ref, last_ref, looks_ref, sums_ref):
-    blocks_n, _, rows_n, width = res_ref.shape
+def slots(own_ref, beside_ref, near_ref, skip_ref, far_ref):
+    here = lax.axis_index("date")
+    inner = (here == 1) | (here == 2)
+    low = here < 2
+    return (
+        (here, lambda part: own_ref[part]),
+        (jnp.where(lax.rem(here, 2) == 0, here + 1, here - 1), lambda part: beside_ref[part]),
+        (jnp.where(low, 2, 1), lambda part: jnp.where(inner, near_ref[part], skip_ref[part])),
+        (jnp.where(low, 3, 0), lambda part: jnp.where(inner, skip_ref[part], far_ref[part])),
+    )
+
+
+def margin_kernel(
+    own_ref, beside_ref, near_ref, skip_ref, far_ref, res_ref, first_ref, last_ref, looks_ref, sums_ref
+):
+    _, _, rows_n, width = res_ref.shape
     looks_n = looks_ref.shape[2]
     totals = [None, None]
-    for block in range(blocks_n):
+    for step, (block, read) in enumerate(slots(own_ref, beside_ref, near_ref, skip_ref, far_ref)):
+        prim_re, prim_im = read(0), read(1)
         select = look_columns(width, block, looks_n)
-        columns = slice(block * width, (block + 1) * width)
+        columns = pl.ds(pl.multiple_of(block * width, width), width)
         halves = []
         for held, start, target in ((0, 0, first_ref), (LAG, rows_n - LAG, last_ref)):
             pair = interfere(
-                prim_ref[block, 0, held : held + LAG],
-                prim_ref[block, 1, held : held + LAG],
+                prim_re[held : held + LAG],
+                prim_im[held : held + LAG],
                 res_ref[block, 0, start : start + LAG],
                 res_ref[block, 1, start : start + LAG],
             )
@@ -130,7 +166,7 @@
         for part in range(2):
             both = jnp.concatenate([halves[0][part], halves[1][part]], axis=0)
             summed = jnp.dot(both, select, preferred_element_type=jnp.float32)
-            totals[part] = summed if block == 0 else totals[part] + summed
+            totals[part] = summed if step == 0 else totals[part] + summed
     for part in range(2):
         sums_ref[part] = totals[part]
         looks_ref[part] = look_rows(sums_ref, part, 0, 2 * LAG)
@@ -138,9 +174,9 @@
 
 def stats_kernel(last_ref, later_ref, weight_ref, stats_ref):
     cols_n = last_ref.shape[2]
+    weight = weight_ref[...]
     i_re, i_im = last_ref[0].astype(jnp.float32), last_ref[1].astype(jnp.float32)
     l_re, l_im = later_ref[0].astype(jnp.float32), later_ref[1].astype(jnp.float32)
-    weight = weight_ref[...]
     values = (
         i_re * l_re + i_im * l_im,
         i_im * l_re - i_re * l_im,
@@ -157,16 +193,14 @@
     stats_ref[...] = jnp.concatenate(rows, axis=0)
 
 
-def finish_kernel(prim_ref, res_ref, looks_ref, stats_ref, out_ref, sums_ref):
-    blocks_n, _, rows_n, width = res_ref.shape
-    looks_n = out_ref.shape[3]
-    middle_n = rows_n - 2 * LAG
+def look_sums(pieces, res_ref, looks_n):
+    _, _, rows_n, width = res_ref.shape
     totals = [None, None]
-    for block in range(blocks_n):
+    for step, (block, read) in enumerate(pieces):
         select = look_columns(width, block, looks_n)
         pair = interfere(
-            prim_ref[block, 0],
-            prim_ref[block, 1],
+            read(0),
+            read(1),
             res_ref[block, 0, LAG : rows_n - LAG],
             res_ref[block, 1, LAG : rows_n - LAG],
         )
@@ -174,8 +208,24 @@
             summed = jnp.dot(
                 pair[part].astype(jnp.bfloat16), select, preferred_element_type=jnp.float32
             )
-            totals[part] = summed if block == 0 else totals[part] + summed
-    stats = jnp.sum(stats_ref[...], axis=1, keepdims=True)
+            totals[part] = summed if step == 0 else totals[part] + summed
+    return totals
+
+
+def middle_kernel(own_ref, beside_ref, near_ref, skip_ref, res_ref, out_ref):
+    pieces = slots(own_ref, beside_ref, near_ref, skip_ref, None)[:3]
+    for part, total in enumerate(look_sums(pieces, res_ref, out_ref.shape[2])):
+        out_ref[part] = total
+
+
+def finish_kernel(
+    skip_ref, far_ref, res_ref, before_ref, looks_ref, mine_ref, other_ref, out_ref, sums_ref
+):
+    looks_n = out_ref.shape[3]
+    middle_n = before_ref.shape[1]
+    totals = look_sums(slots(None, None, None, skip_ref, far_ref)[3:], res_ref, looks_n)
+    totals = [total + before_ref[part] for part, total in enumerate(totals)]
+    stats = jnp.sum(mine_ref[...] + other_ref[...], axis=1, keepdims=True)
     e_re, e_im, power, count = [stats[row : row + 1] for row in range(4)]
     magnitude = jnp.sqrt(e_re * e_re + e_im * e_im)
     floor_val = (power + 1e-06) / jnp.sqrt(jnp.maximum(count, 1.0))
@@ -194,36 +244,50 @@
         out_ref[0, 1, out_at : out_at + rows] = held[1] * u_re - held[0] * u_im
 
 
-def call(kernel, outs, scratch, cost, *args):
-    whole = pl.BlockSpec(memory_space=pltpu.VMEM)
+def call(kernel, outs, scratch, cost, *args, places=None, limit=VMEM_LIMIT):
+    vmem = pl.BlockSpec(memory_space=pltpu.VMEM)
     return pl.pallas_call(
         kernel,
         out_shape=outs,
-        in_specs=[whole] * len(args),
-        out_specs=jax.tree.map(lambda _: whole, outs),
+        in_specs=[places or vmem] * len(args),
+        out_specs=jax.tree.map(lambda _: places or vmem, outs),
         scratch_shapes=scratch,
-        compiler_params=pltpu.CompilerParams(vmem_limit_bytes=VMEM_LIMIT),
+        compiler_params=pltpu.CompilerParams(vmem_limit_bytes=limit),
         cost_estimate=pl.CostEstimate(flops=cost[0], bytes_accessed=cost[1], transcendentals=0),
     )(*args)
+
+
+def spread(block):
+    skip = lax.ppermute(block, "date", [(0, 2), (2, 0), (1, 3), (3, 1)])
+    beside = lax.ppermute(block, "date", [(0, 1), (1, 0), (2, 3), (3, 2)])
+    near = lax.ppermute(block, "date", [(1, 2), (2, 1)])
+    far = lax.ppermute(skip, "date", [(1, 0), (2, 3)])
+    return beside, near, skip, far
 
 
 def fused(secondary, primary, margin_mask, az_off, rg_off, az_frac, rg_frac):
     _, _, rows_n, cols_n = secondary.shape
     width = primary.shape[2]
     dates_n = lax.axis_size("date")
+    tiles_n = lax.axis_size("tile")
     bf16, f32 = jnp.bfloat16, jnp.float32
     shape = jax.ShapeDtypeStruct
     looks_n = cols_n // LR
-
-    edges = jnp.concatenate([primary[:, :LAG], primary[:, rows_n - LAG :]], axis=1)
-    edges = lax.all_gather(edges, "date", axis=0)
-    middle = lax.all_gather(primary[:, LAG : rows_n - LAG], "date", axis=0)
-
-    image = secondary[0]
-    low = passed_along(image[:, rows_n - HALO :], "tile", 1)
-    high = passed_along(image[:, :HALO], "tile", -1)
+    middle_n = rows_n - 2 * LAG
+    hbm = pl.BlockSpec(memory_space=pltpu.HBM)
+
+    halo = shape((2, HALO, cols_n), bf16)
+    edges, middle, down, up = call(
+        prepare_kernel,
+        (shape((2, 2 * LAG, width), bf16), shape((2, middle_n, width), bf16), halo, halo),
+        [pltpu.SemaphoreType.DMA((5,))],
+        (0, 4 * 2 * rows_n * width),
+        secondary, primary, places=hbm, limit=VMEM_ALL,
+    )
+    around = spread(edges)
+    low = passed_along(down, "tile", 1)
+    high = passed_along(up, "tile", -1)
     weight = jnp.broadcast_to(margin_mask[rows_n - LAG :].astype(f32)[:, None], (LAG, LANE))
-
     res = call(
         resample_kernel,
         shape((dates_n, 2, rows_n, width), bf16),
@@ -231,13 +295,14 @@
         (2 * 2 * rows_n * cols_n * (2 * HALO + BAND + 2 * width), 8 * rows_n * cols_n),
         secondary, low, high, az_off, rg_off, az_frac, rg_frac,
     )
+    others = spread(middle)
     margin = shape((2, LAG, cols_n), bf16)
     first, last, looks = call(
         margin_kernel,
         (margin, margin, shape((2, 2 * LAG // LA, looks_n), f32)),
         [pltpu.VMEM((2, 2 * LAG, looks_n), f32)],
         (2 * 2 * 2 * LAG * cols_n * looks_n, 24 * LAG * cols_n),
-        edges, res,
+        edges, *around, res,
     )
     later = passed_along(first, "tile", -1)
     stats = call(
@@ -247,13 +312,26 @@
         (20 * LAG * cols_n, 8 * LAG * cols_n),
         last, later, weight,
     )
-    stats = lax.psum(stats, "tile")
+    beside, near, skip, far = others
+    before = call(
+        middle_kernel,
+        shape((2, middle_n, looks_n), f32),
+        [],
+        (2 * 2 * middle_n * cols_n * looks_n, 8 * rows_n * cols_n),
+        middle, beside, near, skip, res,
+    )
+    stride = 1
+    other = jnp.zeros_like(stats)
+    while stride < tiles_n:
+        stats = stats + other if stride > 1 else stats
+        other = lax.ppermute(stats, "tile", [(at, at ^ stride) for at in range(tiles_n)])
+        stride *= 2
     return call(
         finish_kernel,
         shape((1, 2, rows_n // LA, looks_n), f32),
-        [pltpu.VMEM((2, rows_n - 2 * LAG, looks_n), f32)],
-        (2 * 2 * rows_n * cols_n * looks_n, 8 * rows_n * cols_n),
-        middle, res, looks, stats,
+        [pltpu.VMEM((2, middle_n, looks_n), f32)],
+        (2 * middle_n * cols_n * looks_n, 4 * rows_n * cols_n),
+        skip, far, res, before, looks, stats, other,
     )
 
 
@@ -331,6 +409,8 @@
 def shards(secondary, primary, *rest):
     rows_n, width = primary.shape[1:]
     fits = rows_n % BAND == 0 and rows_n > 2 * LAG + BAND and width % LANE == 0
+    tiles_n = lax.axis_size("tile")
+    fits = fits and lax.axis_size("date") == 4 and tiles_n & (tiles_n - 1) == 0
     return (fused if fits else plain)(secondary, primary, *rest)
 
 

time: 75 us -> 68.2 us (0.909)
  blocking collectives: 41.8 us -> 0 us
  Pallas kernels: 3.9 us -> 25.1 us
  starting transfers between devices: 4.95 us -> 23.1 us
  between operations: 16.1 us -> 2.74 us
  waiting for transfers between devices: 1.75 us -> 13.8 us
  local copies, waits for them, and re-layouts: 4.98 us -> 1.48 us
    all_gather x1 -> x0, blocking collectives: 23.4 us -> none  [fused(): edges = lax.all_gather(edges, 'date', axis=0)]
    pallas_call x4 -> x6, Pallas kernels: 3.9 us -> 25.1 us  [call(): pl.pallas_call(kernel, out_shape=outs, in_specs=[places or vmem] * len(ar...]
    psum x1 -> x0, blocking collectives: 18.4 us -> none  [fused(): stats = lax.psum(stats, 'tile')]
    ppermute x0 -> x11, starting transfers between devices: none -> 18.2 us  [the longest x3 7.05 us: fused(): lax.ppermute(stats, 'tile', [(at, at ^ stride) for at in range(tiles_n)])]
    ppermute x0 -> x11, waiting for transfers between devices: none -> 13.8 us  [the longest x2 8.35 us: spread(): far = lax.ppermute(skip, 'date', [(1, 0), (2, 3)])]
    slice x3 -> x0, local copies, waits for them, and re-layouts: 3.68 us -> none  [the longest x1 1.8 us: fused(): middle = lax.all_gather(primary[:, LAG:rows_n - LAG], 'date', axis=0)]
    ppermute x3, waiting for transfers between devices: 1.72 us -> 0.01 us  [passed_along(): lax.ppermute(value, axis, [(source, source + steps) for source in range(i...]
  transfers between devices with their start and end apart: 4 -> 14, of which waited for: 1 -> 6; matrix products, arithmetic and copies ran while one was open for 4% -> 1% of each run, Pallas kernels for 3% -> 5%
where the time goes in v4:
time: 68.2 us; the launch traced here: 67 us
  Pallas kernels  25.1 us (37%)
  starting transfers between devices  23.1 us (34%)
  waiting for transfers between devices  13.8 us (20%)
  between operations  2.74 us (4%)
  local copies, waits for them, and re-layouts  1.48 us (2%)
  other arithmetic  0.76 us (1%)
    pallas_call x6, Pallas kernels, call(): pl.pallas_call(kernel, out_shape=outs, in_specs=[places or vmem] * len(ar...  25.1 us
    ppermute x2, waiting for transfers between devices, spread(): far = lax.ppermute(skip, 'date', [(1, 0), (2, 3)])  8.35 us
    ppermute x3, starting transfers between devices, fused(): lax.ppermute(stats, 'tile', [(at, at ^ stride) for at in range(tiles_n)])  7.05 us
    ppermute x3, starting transfers between devices, passed_along(): lax.ppermute(value, axis, [(source, source + steps) for source in range(i...  4.94 us
    ppermute x2, starting transfers between devices, spread(): beside = lax.ppermute(block, 'date', [(0, 1), (1, 0), (2, 3), (3, 2)])  3.61 us
    ppermute x2, starting transfers between devices, spread(): skip = lax.ppermute(block, 'date', [(0, 2), (2, 0), (1, 3), (3, 1)])  3.6 us
    ppermute x3, waiting for transfers between devices, fused(): lax.ppermute(stats, 'tile', [(at, at ^ stride) for at in range(tiles_n)])  3.05 us
    ppermute x2, starting transfers between devices, spread(): far = lax.ppermute(skip, 'date', [(1, 0), (2, 3)])  2.57 us
  transfers between devices with their start and end apart: 14, of which 6 were waited for; matrix products, arithmetic and copies ran while one was open for 1% of the time, Pallas kernels for 5%

profile of v4, /device:TPU:0, one launch (start us, length us, event | category | flops | bytes accessed | tf_op | source)
XLA Modules:
  0.0 67.0 jit_solution(2256422772934485215)
XLA Ops:
  0.0 21.0 %shard_map.73 = (bf16[2,128,256]{2,1,0:T(8,128)(2,1)}, bf16[2,256,256]{2,1,0:T(8,128)(2,1)}, bf16[2,32,1024]{2,1,0:T(8,128)(2,1)}, bf16[2,32,1024]{2,1,0:T(8,128)(2,1)}) custom-call(bf16[1,2,384,1024]{3,2,1,0:T(8,128)(2,1)} %sec_ref.3, bf16[2,384,256]{2,1,0:T(8,128)(2,1)} %prim_ref.1), custom_call_target="tpu_custom_call" | custom-call | bytes 786432 | tf_op jit(solution)/shard_map/pallas_call | solution.py:249
  21.0 2.4 %collective-permute-start.2 = (bf16[2,32,1024]{2,1,0:T(8,128)(2,1)}, bf16[2,32,1024]{2,1,0:T(8,128)(2,1)S(1)}, u32[]{:S(2)}, u32[]{:S(2)}) collective-permute-start(bf16[2,32,1024]{2,1,0:T(8,128)(2,1)} %get-tuple-element.13), channel_id=1, source_target_pairs={{0,4},{4,8},{8,12},{12,16},{16,20},{20,24},{24,28},{1,5},{5,9},{9,... | collective-permute-start | bytes 393224 | tf_op jit(solution)/shard_map/ppermute | solution.py:24
  23.4 3.5 %collective-permute-start.8 = (bf16[2,128,256]{2,1,0:T(8,128)(2,1)}, bf16[2,128,256]{2,1,0:T(8,128)(2,1)S(1)}, u32[]{:S(2)}, u32[]{:S(2)}) collective-permute-start(bf16[2,128,256]{2,1,0:T(8,128)(2,1)} %get-tuple-element.15.own_ref), channel_id=1, source_target_pairs={{0,2},{2,0},{1,3},{3,1},{4,6},{6,4},{5,7},{7,5},{8,10},{10,8},{9,1... | collective-permute-start | bytes 393224 | tf_op jit(solution)/shard_map/ppermute | solution.py:261
  26.9 1.3 %collective-permute-start.3 = (bf16[2,32,1024]{2,1,0:T(8,128)(2,1)}, bf16[2,32,1024]{2,1,0:T(8,128)(2,1)S(1)}, u32[]{:S(2)}, u32[]{:S(2)}) collective-permute-start(bf16[2,32,1024]{2,1,0:T(8,128)(2,1)} %get-tuple-element.14), channel_id=1, source_target_pairs={{4,0},{8,4},{12,8},{16,12},{20,16},{24,20},{28,24},{5,1},{9,5},{13... | collective-permute-start | bytes 393224 | tf_op jit(solution)/shard_map/ppermute | solution.py:24
  28.1 0.1 collective-permute-start
  28.3 1.9 %collective-permute-start.6 = (bf16[2,128,256]{2,1,0:T(8,128)(2,1)}, bf16[2,128,256]{2,1,0:T(8,128)(2,1)S(1)}, u32[]{:S(2)}, u32[]{:S(2)}) collective-permute-start(bf16[2,128,256]{2,1,0:T(8,128)(2,1)} %get-tuple-element.15.own_ref), channel_id=1, source_target_pairs={{0,1},{1,0},{2,3},{3,2},{4,5},{5,4},{6,7},{7,6},{8,9},{9,8},{10,11... | collective-permute-start | bytes 393224 | tf_op jit(solution)/shard_map/ppermute | solution.py:262
  30.1 0.0 collective-permute-done.2.low_ref
  30.1 0.7 collective-permute-start.7
  30.8 2.4 %collective-permute-done.8.skip_ref = bf16[2,128,256]{2,1,0:T(8,128)(2,1)S(1)} collective-permute-done((bf16[2,128,256]{2,1,0:T(8,128)(2,1)}, bf16[2,128,256]{2,1,0:T(8,128)(2,1)S(1)}, u32[]{:S(2)}, u32[]{:S(2)}) %collective-permute-start.8) | collective-permute-done | bytes 131104 | tf_op jit(solution)/shard_map/ppermute | solution.py:261
  33.2 1.3 %collective-permute-start.9 = (bf16[2,128,256]{2,1,0:T(8,128)(2,1)S(1)}, bf16[2,128,256]{2,1,0:T(8,128)(2,1)S(1)}, u32[]{:S(2)}, u32[]{:S(2)}) collective-permute-start(bf16[2,128,256]{2,1,0:T(8,128)(2,1)S(1)} %collective-permute-done.8.skip_ref), channel_id=1, source_target_pairs={{1,0},{2,3},{5,4},{6,7},{9,8},{10,11},{13,12},{14,15},{17,16},{18,... | collective-permute-start | bytes 393224 | tf_op jit(solution)/shard_map/ppermute | solution.py:264
  37.1 0.0 collective-permute-done.3.high_ref
  37.1 0.0 copy-start
  37.1 1.4 %copy-done = bf16[1,2,384,1024]{3,2,1,0:T(8,128)(2,1)S(1)} copy-done((bf16[1,2,384,1024]{3,2,1,0:T(8,128)(2,1)S(1)}, bf16[1,2,384,1024]{3,2,1,0:T(8,128)(2,1)}, u32[]{:S(2)}) %copy-start) | copy-done | bytes 1572888
  38.5 1.6 %shard_map.74.res_ref = bf16[4,2,384,256]{3,2,1,0:T(8,128)(2,1)S(1)} custom-call(bf16[1,2,384,1024]{3,2,1,0:T(8,128)(2,1)S(1)} %copy-done, bf16[2,32,1024]{2,1,0:T(8,128)(2,1)S(1)} %collective-permute-done.2.low_ref, bf16[2,32,1024]{2,1,0:T(8,128)(2,1)S(1)} %collective-permute-done.3.high_ref, s32[1,1]{1,0:T(1,128)S(6)} %copy.8.ao_ref, ...), custom_call_target="tpu_custom_call" | custom-call | flops 1107296256 | bytes 3145728 | tf_op jit(solution)/shard_map/pallas_call | solution.py:249
  40.1 7.5 %collective-permute-done.9.far_ref = bf16[2,128,256]{2,1,0:T(8,128)(2,1)S(1)} collective-permute-done((bf16[2,128,256]{2,1,0:T(8,128)(2,1)S(1)}, bf16[2,128,256]{2,1,0:T(8,128)(2,1)S(1)}, u32[]{:S(2)}, u32[]{:S(2)}) %collective-permute-start.9) | collective-permute-done | bytes 131104 | tf_op jit(solution)/shard_map/ppermute | solution.py:264
  47.6 0.5 shard_map.76
  48.2 1.3 %collective-permute-start.10 = (bf16[2,64,1024]{2,1,0:T(8,128)(2,1)S(1)}, bf16[2,64,1024]{2,1,0:T(8,128)(2,1)S(1)}, u32[]{:S(2)}, u32[]{:S(2)}) collective-permute-start(bf16[2,64,1024]{2,1,0:T(8,128)(2,1)S(1)} %get-tuple-element.18), channel_id=1, source_target_pairs={{4,0},{8,4},{12,8},{16,12},{20,16},{24,20},{28,24},{5,1},{9,5},{13... | collective-permute-start | bytes 786440 | tf_op jit(solution)/shard_map/ppermute | solution.py:24
  49.5 1.8 %collective-permute-start.4 = (bf16[2,256,256]{2,1,0:T(8,128)(2,1)S(1)}, bf16[2,256,256]{2,1,0:T(8,128)(2,1)S(1)}, u32[]{:S(2)}, u32[]{:S(2)}) collective-permute-start(bf16[2,256,256]{2,1,0:T(8,128)(2,1)S(1)} %copy-done.1), channel_id=1, source_target_pairs={{0,1},{1,0},{2,3},{3,2},{4,5},{5,4},{6,7},{7,6},{8,9},{9,8},{10,11... | collective-permute-start | bytes 786440 | tf_op jit(solution)/shard_map/ppermute | solution.py:262
  51.2 0.7 collective-permute-start.5
  51.9 1.3 %collective-permute-start.1 = (bf16[2,256,256]{2,1,0:T(8,128)(2,1)S(1)}, bf16[2,256,256]{2,1,0:T(8,128)(2,1)S(1)}, u32[]{:S(2)}, u32[]{:S(2)}) collective-permute-start(bf16[2,256,256]{2,1,0:T(8,128)(2,1)S(1)} %collective-permute-done.skip_ref), channel_id=1, source_target_pairs={{1,0},{2,3},{5,4},{6,7},{9,8},{10,11},{13,12},{14,15},{17,16},{18,... | collective-permute-start | bytes 786440 | tf_op jit(solution)/shard_map/ppermute | solution.py:264
  53.2 0.8 %slice_convert_fusion = f32[64]{0:T(128)S(1)} fusion(s32[384]{0:T(512)} %param.9), kind=kLoop, calls=%fused_computation | loop fusion | flops 64 | bytes 512 | tf_op jit(solution)/shard_map/convert_element_type | solution.py:290
  54.0 0.1 broadcast_in_dim.2.weight_ref
  54.1 0.3 shard_map.77
  54.4 3.3 %collective-permute-start.11 = (f32[8,128]{1,0:T(8,128)S(1)}, f32[8,128]{1,0:T(8,128)S(1)}, u32[]{:S(2)}, u32[]{:S(2)}) collective-permute-start(f32[8,128]{1,0:T(8,128)S(1)} %shard_map.77), channel_id=1, source_target_pairs={{0,4},{4,0},{8,12},{12,8},{16,20},{20,16},{24,28},{28,24},{1,5},{5... | collective-permute-start | bytes 12296 | tf_op jit(solution)/shard_map/ppermute | solution.py:327
  57.7 0.8 %collective-permute-done.11 = f32[8,128]{1,0:T(8,128)S(1)} collective-permute-done((f32[8,128]{1,0:T(8,128)S(1)}, f32[8,128]{1,0:T(8,128)S(1)}, u32[]{:S(2)}, u32[]{:S(2)}) %collective-permute-start.11) | collective-permute-done | bytes 4128 | tf_op jit(solution)/shard_map/ppermute | solution.py:327
  58.5 2.3 %collective-permute-start.12 = (f32[8,128]{1,0:T(8,128)S(1)}, f32[8,128]{1,0:T(8,128)S(1)}, u32[]{:S(2)}, u32[]{:S(2)}) collective-permute-start(f32[8,128]{1,0:T(8,128)S(1)} %add.6), channel_id=1, source_target_pairs={{0,8},{4,12},{8,0},{12,4},{16,24},{20,28},{24,16},{28,20},{1,9},{5... | collective-permute-start | bytes 12296 | tf_op jit(solution)/shard_map/ppermute | solution.py:327
  60.8 1.6 %collective-permute-done.12 = f32[8,128]{1,0:T(8,128)S(1)} collective-permute-done((f32[8,128]{1,0:T(8,128)S(1)}, f32[8,128]{1,0:T(8,128)S(1)}, u32[]{:S(2)}, u32[]{:S(2)}) %collective-permute-start.12) | collective-permute-done | bytes 4128 | tf_op jit(solution)/shard_map/ppermute | solution.py:327
  62.4 1.4 %collective-permute-start.13 = (f32[8,128]{1,0:T(8,128)S(1)}, f32[8,128]{1,0:T(8,128)S(1)}, u32[]{:S(2)}, u32[]{:S(2)}) collective-permute-start(f32[8,128]{1,0:T(8,128)S(1)} %add.7.mine_ref), channel_id=1, source_target_pairs={{0,16},{4,20},{8,24},{12,28},{16,0},{20,4},{24,8},{28,12},{1,17},{... | collective-permute-start | bytes 12296 | tf_op jit(solution)/shard_map/ppermute | solution.py:327
  63.9 0.6 shard_map.75.before_ref
  64.5 0.9 %collective-permute-done.1.far_ref = bf16[2,256,256]{2,1,0:T(8,128)(2,1)S(1)} collective-permute-done((bf16[2,256,256]{2,1,0:T(8,128)(2,1)S(1)}, bf16[2,256,256]{2,1,0:T(8,128)(2,1)S(1)}, u32[]{:S(2)}, u32[]{:S(2)}) %collective-permute-start.1) | collective-permute-done | bytes 262176 | tf_op jit(solution)/shard_map/ppermute | solution.py:264
  65.4 0.6 collective-permute-done.13.other_ref
  66.0 1.0 %shard_map.78 = f32[1,2,192,128]{3,2,1,0:T(8,128)} custom-call(bf16[2,256,256]{2,1,0:T(8,128)(2,1)S(1)} %collective-permute-done.skip_ref, bf16[2,256,256]{2,1,0:T(8,128)(2,1)S(1)} %collective-permute-done.1.far_ref, bf16[4,2,384,256]{3,2,1,0:T(8,128)(2,1)S(1)} %shard_map.74.res_ref, f32[2,256,128]{2,1,0:T(8,128)S(1)} %shard_map.75.before_ref, ...), custom_call_target="tpu_custom_call" | custom-call | flops 67108864 | bytes 1572864 | tf_op jit(solution)/shard_map/pallas_call | solution.py:249
  (12 shorter events, 0.0 us)
Async XLA Ops:
  21.0 9.1 %collective-permute-start.2 = (bf16[2,32,1024]{2,1,0:T(8,128)(2,1)}, bf16[2,32,1024]{2,1,0:T(8,128)(2,1)S(1)}, u32[]{:S(2)}, u32[]{:S(2)}) collective-permute-start(bf16[2,32,1024]{2,1,0:T(8,128)(2,1)} %get-tuple-element.13), channel_id=1, source_target_pairs={{0,4},{4,8},{8,12},{12,16},{16,20},{20,24},{24,28},{1,5},{5,9},{9,... | collective-permute-start | bytes 393224 | tf_op jit(solution)/shard_map/ppermute | solution.py:24
  23.4 9.8 %collective-permute-start.8 = (bf16[2,128,256]{2,1,0:T(8,128)(2,1)}, bf16[2,128,256]{2,1,0:T(8,128)(2,1)S(1)}, u32[]{:S(2)}, u32[]{:S(2)}) collective-permute-start(bf16[2,128,256]{2,1,0:T(8,128)(2,1)} %get-tuple-element.15.own_ref), channel_id=1, source_target_pairs={{0,2},{2,0},{1,3},{3,1},{4,6},{6,4},{5,7},{7,5},{8,10},{10,8},{9,1... | collective-permute-start | bytes 393224 | tf_op jit(solution)/shard_map/ppermute | solution.py:261
  26.9 10.2 %collective-permute-start.3 = (bf16[2,32,1024]{2,1,0:T(8,128)(2,1)}, bf16[2,32,1024]{2,1,0:T(8,128)(2,1)S(1)}, u32[]{:S(2)}, u32[]{:S(2)}) collective-permute-start(bf16[2,32,1024]{2,1,0:T(8,128)(2,1)} %get-tuple-element.14), channel_id=1, source_target_pairs={{4,0},{8,4},{12,8},{16,12},{20,16},{24,20},{28,24},{5,1},{9,5},{13... | collective-permute-start | bytes 393224 | tf_op jit(solution)/shard_map/ppermute | solution.py:24
  28.1 23.8 %collective-permute-start = (bf16[2,256,256]{2,1,0:T(8,128)(2,1)}, bf16[2,256,256]{2,1,0:T(8,128)(2,1)S(1)}, u32[]{:S(2)}, u32[]{:S(2)}) collective-permute-start(bf16[2,256,256]{2,1,0:T(8,128)(2,1)} %get-tuple-element.12.own_ref), channel_id=1, source_target_pairs={{0,2},{2,0},{1,3},{3,1},{4,6},{6,4},{5,7},{7,5},{8,10},{10,8},{9,1... | collective-permute-start | bytes 786440 | tf_op jit(solution)/shard_map/ppermute | solution.py:261
  28.3 11.8 %collective-permute-start.6 = (bf16[2,128,256]{2,1,0:T(8,128)(2,1)}, bf16[2,128,256]{2,1,0:T(8,128)(2,1)S(1)}, u32[]{:S(2)}, u32[]{:S(2)}) collective-permute-start(bf16[2,128,256]{2,1,0:T(8,128)(2,1)} %get-tuple-element.15.own_ref), channel_id=1, source_target_pairs={{0,1},{1,0},{2,3},{3,2},{4,5},{5,4},{6,7},{7,6},{8,9},{9,8},{10,11... | collective-permute-start | bytes 393224 | tf_op jit(solution)/shard_map/ppermute | solution.py:262
  30.1 10.0 %collective-permute-start.7 = (bf16[2,128,256]{2,1,0:T(8,128)(2,1)}, bf16[2,128,256]{2,1,0:T(8,128)(2,1)S(1)}, u32[]{:S(2)}, u32[]{:S(2)}) collective-permute-start(bf16[2,128,256]{2,1,0:T(8,128)(2,1)} %get-tuple-element.15.own_ref), channel_id=1, source_target_pairs={{1,2},{2,1},{5,6},{6,5},{9,10},{10,9},{13,14},{14,13},{17,18},{18,... | collective-permute-start | bytes 393224 | tf_op jit(solution)/shard_map/ppermute | solution.py:263
  33.2 14.4 %collective-permute-start.9 = (bf16[2,128,256]{2,1,0:T(8,128)(2,1)S(1)}, bf16[2,128,256]{2,1,0:T(8,128)(2,1)S(1)}, u32[]{:S(2)}, u32[]{:S(2)}) collective-permute-start(bf16[2,128,256]{2,1,0:T(8,128)(2,1)S(1)} %collective-permute-done.8.skip_ref), channel_id=1, source_target_pairs={{1,0},{2,3},{5,4},{6,7},{9,8},{10,11},{13,12},{14,15},{17,16},{18,... | collective-permute-start | bytes 393224 | tf_op jit(solution)/shard_map/ppermute | solution.py:264
  37.1 1.4 %copy-start = (bf16[1,2,384,1024]{3,2,1,0:T(8,128)(2,1)S(1)}, bf16[1,2,384,1024]{3,2,1,0:T(8,128)(2,1)}, u32[]{:S(2)}) copy-start(bf16[1,2,384,1024]{3,2,1,0:T(8,128)(2,1)} %sec_ref.3) | copy-start | bytes 4718596
  38.5 9.1 %copy-start.2 = (bf16[2,128,256]{2,1,0:T(8,128)(2,1)S(1)}, bf16[2,128,256]{2,1,0:T(8,128)(2,1)}, u32[]{:S(2)}) copy-start(bf16[2,128,256]{2,1,0:T(8,128)(2,1)} %get-tuple-element.15.own_ref) | copy-start | bytes 393220
  40.1 9.4 %copy-start.1 = (bf16[2,256,256]{2,1,0:T(8,128)(2,1)S(1)}, bf16[2,256,256]{2,1,0:T(8,128)(2,1)}, u32[]{:S(2)}) copy-start(bf16[2,256,256]{2,1,0:T(8,128)(2,1)} %get-tuple-element.12.own_ref) | copy-start | bytes 786436
  48.2 5.8 %collective-permute-start.10 = (bf16[2,64,1024]{2,1,0:T(8,128)(2,1)S(1)}, bf16[2,64,1024]{2,1,0:T(8,128)(2,1)S(1)}, u32[]{:S(2)}, u32[]{:S(2)}) collective-permute-start(bf16[2,64,1024]{2,1,0:T(8,128)(2,1)S(1)} %get-tuple-element.18), channel_id=1, source_target_pairs={{4,0},{8,4},{12,8},{16,12},{20,16},{24,20},{28,24},{5,1},{9,5},{13... | collective-permute-start | bytes 786440 | tf_op jit(solution)/shard_map/ppermute | solution.py:24
  49.5 14.4 %collective-permute-start.4 = (bf16[2,256,256]{2,1,0:T(8,128)(2,1)S(1)}, bf16[2,256,256]{2,1,0:T(8,128)(2,1)S(1)}, u32[]{:S(2)}, u32[]{:S(2)}) collective-permute-start(bf16[2,256,256]{2,1,0:T(8,128)(2,1)S(1)} %copy-done.1), channel_id=1, source_target_pairs={{0,1},{1,0},{2,3},{3,2},{4,5},{5,4},{6,7},{7,6},{8,9},{9,8},{10,11... | collective-permute-start | bytes 786440 | tf_op jit(solution)/shard_map/ppermute | solution.py:262
  51.2 12.6 %collective-permute-start.5 = (bf16[2,256,256]{2,1,0:T(8,128)(2,1)S(1)}, bf16[2,256,256]{2,1,0:T(8,128)(2,1)S(1)}, u32[]{:S(2)}, u32[]{:S(2)}) collective-permute-start(bf16[2,256,256]{2,1,0:T(8,128)(2,1)S(1)} %copy-done.1), channel_id=1, source_target_pairs={{1,2},{2,1},{5,6},{6,5},{9,10},{10,9},{13,14},{14,13},{17,18},{18,... | collective-permute-start | bytes 786440 | tf_op jit(solution)/shard_map/ppermute | solution.py:263
  51.9 13.5 %collective-permute-start.1 = (bf16[2,256,256]{2,1,0:T(8,128)(2,1)S(1)}, bf16[2,256,256]{2,1,0:T(8,128)(2,1)S(1)}, u32[]{:S(2)}, u32[]{:S(2)}) collective-permute-start(bf16[2,256,256]{2,1,0:T(8,128)(2,1)S(1)} %collective-permute-done.skip_ref), channel_id=1, source_target_pairs={{1,0},{2,3},{5,4},{6,7},{9,8},{10,11},{13,12},{14,15},{17,16},{18,... | collective-permute-start | bytes 786440 | tf_op jit(solution)/shard_map/ppermute | solution.py:264
  54.4 4.1 %collective-permute-start.11 = (f32[8,128]{1,0:T(8,128)S(1)}, f32[8,128]{1,0:T(8,128)S(1)}, u32[]{:S(2)}, u32[]{:S(2)}) collective-permute-start(f32[8,128]{1,0:T(8,128)S(1)} %shard_map.77), channel_id=1, source_target_pairs={{0,4},{4,0},{8,12},{12,8},{16,20},{20,16},{24,28},{28,24},{1,5},{5... | collective-permute-start | bytes 12296 | tf_op jit(solution)/shard_map/ppermute | solution.py:327
  58.5 3.9 %collective-permute-start.12 = (f32[8,128]{1,0:T(8,128)S(1)}, f32[8,128]{1,0:T(8,128)S(1)}, u32[]{:S(2)}, u32[]{:S(2)}) collective-permute-start(f32[8,128]{1,0:T(8,128)S(1)} %add.6), channel_id=1, source_target_pairs={{0,8},{4,12},{8,0},{12,4},{16,24},{20,28},{24,16},{28,20},{1,9},{5... | collective-permute-start | bytes 12296 | tf_op jit(solution)/shard_map/ppermute | solution.py:327
  62.4 3.6 %collective-permute-start.13 = (f32[8,128]{1,0:T(8,128)S(1)}, f32[8,128]{1,0:T(8,128)S(1)}, u32[]{:S(2)}, u32[]{:S(2)}) collective-permute-start(f32[8,128]{1,0:T(8,128)S(1)} %add.7.mine_ref), channel_id=1, source_target_pairs={{0,16},{4,20},{8,24},{12,28},{16,0},{20,4},{24,8},{28,12},{1,17},{... | collective-permute-start | bytes 12296 | tf_op jit(solution)/shard_map/ppermute | solution.py:327

commit v5 on v4

--- a/solution.py
+++ b/solution.py
@@ -15,7 +15,6 @@
 BAND = 128
 HALO = 32
 VMEM_LIMIT = 40 * 1024 * 1024
-VMEM_ALL = 63 * 1024 * 1024
 
 
 def passed_along(value, axis, steps):
@@ -43,24 +42,20 @@
     return total.astype(jnp.bfloat16)
 
 
-def start_all(pairs, sems):
-    copies = [pltpu.make_async_copy(*pair, sems.at[at]) for at, pair in enumerate(pairs)]
-    for copy in copies:
-        copy.start()
-    return copies
-
-
-def prepare_kernel(sec_ref, prim_ref, edges_ref, middle_ref, down_ref, up_ref, sems):
+def cut_edges_kernel(prim_ref, edges_ref):
+    rows_n = prim_ref.shape[1]
+    edges_ref[:, :LAG] = prim_ref[:, :LAG]
+    edges_ref[:, LAG:] = prim_ref[:, rows_n - LAG :]
+
+
+def cut_halo_kernel(sec_ref, down_ref, up_ref):
     rows_n = sec_ref.shape[2]
-    pieces = (
-        (prim_ref.at[:, :LAG], edges_ref.at[:, :LAG]),
-        (prim_ref.at[:, rows_n - LAG :], edges_ref.at[:, LAG:]),
-        (sec_ref.at[0, :, rows_n - HALO :], down_ref),
-        (sec_ref.at[0, :, :HALO], up_ref),
-        (prim_ref.at[:, LAG : rows_n - LAG], middle_ref),
-    )
-    for copy in start_all(pieces, sems):
-        copy.wait()
+    down_ref[...] = sec_ref[0, :, rows_n - HALO :]
+    up_ref[...] = sec_ref[0, :, :HALO]
+
+
+def cut_middle_kernel(prim_ref, *refs):
+    refs[-1][...] = prim_ref[:, LAG : prim_ref.shape[1] - LAG]
 
 
 def resample_kernel(sec_ref, low_ref, high_ref, ao_ref, ro_ref, af_ref, rf_ref, out_ref, azim_ref):
@@ -244,15 +239,15 @@
         out_ref[0, 1, out_at : out_at + rows] = held[1] * u_re - held[0] * u_im
 
 
-def call(kernel, outs, scratch, cost, *args, places=None, limit=VMEM_LIMIT):
+def call(kernel, outs, scratch, cost, *args):
     vmem = pl.BlockSpec(memory_space=pltpu.VMEM)
     return pl.pallas_call(
         kernel,
         out_shape=outs,
-        in_specs=[places or vmem] * len(args),
-        out_specs=jax.tree.map(lambda _: places or vmem, outs),
+        in_specs=[vmem] * len(args),
+        out_specs=jax.tree.map(lambda _: vmem, outs),
         scratch_shapes=scratch,
-        compiler_params=pltpu.CompilerParams(vmem_limit_bytes=limit),
+        compiler_params=pltpu.CompilerParams(vmem_limit_bytes=VMEM_LIMIT),
         cost_estimate=pl.CostEstimate(flops=cost[0], bytes_accessed=cost[1], transcendentals=0),
     )(*args)
 
@@ -274,19 +269,21 @@
     shape = jax.ShapeDtypeStruct
     looks_n = cols_n // LR
     middle_n = rows_n - 2 * LAG
-    hbm = pl.BlockSpec(memory_space=pltpu.HBM)
-
+    edges = call(
+        cut_edges_kernel, shape((2, 2 * LAG, width), bf16), [], (0, 16 * LAG * width), primary
+    )
+    around = spread(edges)
     halo = shape((2, HALO, cols_n), bf16)
-    edges, middle, down, up = call(
-        prepare_kernel,
-        (shape((2, 2 * LAG, width), bf16), shape((2, middle_n, width), bf16), halo, halo),
-        [pltpu.SemaphoreType.DMA((5,))],
-        (0, 4 * 2 * rows_n * width),
-        secondary, primary, places=hbm, limit=VMEM_ALL,
-    )
-    around = spread(edges)
+    down, up = call(cut_halo_kernel, (halo, halo), [], (0, 16 * HALO * cols_n), secondary)
     low = passed_along(down, "tile", 1)
     high = passed_along(up, "tile", -1)
+    middle = call(
+        cut_middle_kernel,
+        shape((2, middle_n, width), bf16),
+        [],
+        (0, 8 * middle_n * width),
+        primary, *around[:2],
+    )
     weight = jnp.broadcast_to(margin_mask[rows_n - LAG :].astype(f32)[:, None], (LAG, LANE))
     res = call(
         resample_kernel,

time: 68.2 us -> 47.6 us (0.70)
  Pallas kernels: 25.1 us -> 4.17 us
  waiting for transfers between devices: 13.8 us -> 6.92 us
  starting transfers between devices: 23.1 us -> 29.7 us
  local copies, waits for them, and re-layouts: 1.48 us -> 2.48 us
    pallas_call x6 -> x8, Pallas kernels: 25.1 us -> 4.17 us  [call(): pl.pallas_call(kernel, out_shape=outs, in_specs=[vmem] * len(args), out_s...]
    ppermute x2, waiting for transfers between devices: 8.35 us -> 1.33 us  [spread(): far = lax.ppermute(skip, 'date', [(1, 0), (2, 3)])]
    ppermute x2, starting transfers between devices: 3.6 us -> 8.59 us  [spread(): skip = lax.ppermute(block, 'date', [(0, 2), (2, 0), (1, 3), (3, 1)])]
    ppermute x3, starting transfers between devices: 7.05 us -> 8.75 us  [fused(): lax.ppermute(stats, 'tile', [(at, at ^ stride) for at in range(tiles_n)])]
    unnamed x6 -> x8, local copies, waits for them, and re-layouts: 1.41 us -> 2.41 us
    ppermute x3, starting transfers between devices: 4.94 us -> 4.01 us  [passed_along(): lax.ppermute(value, axis, [(source, source + steps) for source in range(i...]
    ppermute x2, starting transfers between devices: 3.61 us -> 4.49 us  [spread(): beside = lax.ppermute(block, 'date', [(0, 1), (1, 0), (2, 3), (3, 2)])]
  transfers between devices with their start and end apart: 14 -> 14, of which waited for: 6 -> 5; matrix products, arithmetic and copies ran while one was open for 1% -> 2% of each run, Pallas kernels for 5% -> 7%
where the time goes in v5:
time: 47.6 us; the launch traced here: 46.8 us
  starting transfers between devices  29.7 us (62%)
  waiting for transfers between devices  6.92 us (15%)
  Pallas kernels  4.17 us (9%)
  between operations  2.74 us (6%)
  local copies, waits for them, and re-layouts  2.48 us (5%)
  other arithmetic  0.76 us (2%)
    ppermute x3, starting transfers between devices, fused(): lax.ppermute(stats, 'tile', [(at, at ^ stride) for at in range(tiles_n)])  8.75 us
    ppermute x2, starting transfers between devices, spread(): skip = lax.ppermute(block, 'date', [(0, 2), (2, 0), (1, 3), (3, 1)])  8.59 us
    ppermute x2, starting transfers between devices, spread(): beside = lax.ppermute(block, 'date', [(0, 1), (1, 0), (2, 3), (3, 2)])  4.49 us
    pallas_call x8, Pallas kernels, call(): pl.pallas_call(kernel, out_shape=outs, in_specs=[vmem] * len(args), out_s...  4.17 us
    ppermute x3, starting transfers between devices, passed_along(): lax.ppermute(value, axis, [(source, source + steps) for source in range(i...  4.01 us
    ppermute x3, waiting for transfers between devices, fused(): lax.ppermute(stats, 'tile', [(at, at ^ stride) for at in range(tiles_n)])  3.73 us
    ppermute x2, starting transfers between devices, spread(): far = lax.ppermute(skip, 'date', [(1, 0), (2, 3)])  2.56 us
    unnamed x8, local copies, waits for them, and re-layouts  2.41 us
  transfers between devices with their start and end apart: 14, of which 5 were waited for; matrix products, arithmetic and copies ran while one was open for 2% of the time, Pallas kernels for 7%

profile of v5, /device:TPU:0, one launch (start us, length us, event | category | flops | bytes accessed | tf_op | source)
XLA Modules:
  0.0 46.8 jit_solution(5144529069760462949)
XLA Ops:
  0.0 1.0 %copy-done.2 = bf16[2,384,256]{2,1,0:T(8,128)(2,1)S(1)} copy-done((bf16[2,384,256]{2,1,0:T(8,128)(2,1)S(1)}, bf16[2,384,256]{2,1,0:T(8,128)(2,1)}, u32[]{:S(2)}) %copy-start.2) | copy-done | bytes 393240
  1.0 3.1 %collective-permute-start = (bf16[2,128,256]{2,1,0:T(8,128)(2,1)S(1)}, bf16[2,128,256]{2,1,0:T(8,128)(2,1)S(1)}, u32[]{:S(2)}, u32[]{:S(2)}) collective-permute-start(bf16[2,128,256]{2,1,0:T(8,128)(2,1)S(1)} %shard_map.73.own_ref), channel_id=1, source_target_pairs={{0,1},{1,0},{2,3},{3,2},{4,5},{5,4},{6,7},{7,6},{8,9},{9,8},{10,11... | collective-permute-start | bytes 393224 | tf_op jit(solution)/shard_map/ppermute | solution.py:257
  4.1 0.7 %collective-permute-start.1 = (bf16[2,128,256]{2,1,0:T(8,128)(2,1)S(1)}, bf16[2,128,256]{2,1,0:T(8,128)(2,1)S(1)}, u32[]{:S(2)}, u32[]{:S(2)}) collective-permute-start(bf16[2,128,256]{2,1,0:T(8,128)(2,1)S(1)} %shard_map.73.own_ref), channel_id=1, source_target_pairs={{1,2},{2,1},{5,6},{6,5},{9,10},{10,9},{13,14},{14,13},{17,18},{18,... | collective-permute-start | bytes 393224 | tf_op jit(solution)/shard_map/ppermute | solution.py:258
  4.8 3.9 %collective-permute-start.8 = (bf16[2,128,256]{2,1,0:T(8,128)(2,1)S(1)}, bf16[2,128,256]{2,1,0:T(8,128)(2,1)S(1)}, u32[]{:S(2)}, u32[]{:S(2)}) collective-permute-start(bf16[2,128,256]{2,1,0:T(8,128)(2,1)S(1)} %shard_map.73.own_ref), channel_id=1, source_target_pairs={{0,2},{2,0},{1,3},{3,1},{4,6},{6,4},{5,7},{7,5},{8,10},{10,8},{9,1... | collective-permute-start | bytes 393224 | tf_op jit(solution)/shard_map/ppermute | solution.py:256
  8.7 1.4 %copy-done = bf16[1,2,384,1024]{3,2,1,0:T(8,128)(2,1)S(1)} copy-done((bf16[1,2,384,1024]{3,2,1,0:T(8,128)(2,1)S(1)}, bf16[1,2,384,1024]{3,2,1,0:T(8,128)(2,1)}, u32[]{:S(2)}) %copy-start) | copy-done | bytes 1572888
  10.1 1.4 %collective-permute-start.4 = (bf16[2,32,1024]{2,1,0:T(8,128)(2,1)S(1)}, bf16[2,32,1024]{2,1,0:T(8,128)(2,1)S(1)}, u32[]{:S(2)}, u32[]{:S(2)}) collective-permute-start(bf16[2,32,1024]{2,1,0:T(8,128)(2,1)S(1)} %get-tuple-element.10), channel_id=1, source_target_pairs={{0,4},{4,8},{8,12},{12,16},{16,20},{20,24},{24,28},{1,5},{5,9},{9,... | collective-permute-start | bytes 393224 | tf_op jit(solution)/shard_map/ppermute | solution.py:23
  11.5 1.3 %collective-permute-start.5 = (bf16[2,32,1024]{2,1,0:T(8,128)(2,1)S(1)}, bf16[2,32,1024]{2,1,0:T(8,128)(2,1)S(1)}, u32[]{:S(2)}, u32[]{:S(2)}) collective-permute-start(bf16[2,32,1024]{2,1,0:T(8,128)(2,1)S(1)} %get-tuple-element.11), channel_id=1, source_target_pairs={{4,0},{8,4},{12,8},{16,12},{20,16},{24,20},{28,24},{5,1},{9,5},{13... | collective-permute-start | bytes 393224 | tf_op jit(solution)/shard_map/ppermute | solution.py:23
  12.8 0.0 collective-permute-done.refs_0_.beside_ref
  12.9 0.0 collective-permute-done.1.refs_1_.near_ref
  12.9 4.7 %collective-permute-start.2 = (bf16[2,256,256]{2,1,0:T(8,128)(2,1)S(1)}, bf16[2,256,256]{2,1,0:T(8,128)(2,1)S(1)}, u32[]{:S(2)}, u32[]{:S(2)}) collective-permute-start(bf16[2,256,256]{2,1,0:T(8,128)(2,1)S(1)} %shard_map.74.own_ref), channel_id=1, source_target_pairs={{0,2},{2,0},{1,3},{3,1},{4,6},{6,4},{5,7},{7,5},{8,10},{10,8},{9,1... | collective-permute-start | bytes 786440 | tf_op jit(solution)/shard_map/ppermute | solution.py:256
  17.6 0.0 collective-permute-done.8.skip_ref
  17.6 1.3 %collective-permute-start.9 = (bf16[2,128,256]{2,1,0:T(8,128)(2,1)S(1)}, bf16[2,128,256]{2,1,0:T(8,128)(2,1)S(1)}, u32[]{:S(2)}, u32[]{:S(2)}) collective-permute-start(bf16[2,128,256]{2,1,0:T(8,128)(2,1)S(1)} %collective-permute-done.8.skip_ref), channel_id=1, source_target_pairs={{1,0},{2,3},{5,4},{6,7},{9,8},{10,11},{13,12},{14,15},{17,16},{18,... | collective-permute-start | bytes 393224 | tf_op jit(solution)/shard_map/ppermute | solution.py:259
  21.5 0.0 collective-permute-done.5.high_ref
  21.5 1.6 %shard_map.76.res_ref = bf16[4,2,384,256]{3,2,1,0:T(8,128)(2,1)S(1)} custom-call(bf16[1,2,384,1024]{3,2,1,0:T(8,128)(2,1)S(1)} %copy-done.1, bf16[2,32,1024]{2,1,0:T(8,128)(2,1)S(1)} %collective-permute-done.4.low_ref, bf16[2,32,1024]{2,1,0:T(8,128)(2,1)S(1)} %collective-permute-done.5.high_ref, s32[1,1]{1,0:T(1,128)S(6)} %copy.8.ao_ref, ...), custom_call_target="tpu_custom_call" | custom-call | flops 1107296256 | bytes 3145728 | tf_op jit(solution)/shard_map/pallas_call | solution.py:244
  23.1 1.3 %collective-permute-done.9.far_ref = bf16[2,128,256]{2,1,0:T(8,128)(2,1)S(1)} collective-permute-done((bf16[2,128,256]{2,1,0:T(8,128)(2,1)S(1)}, bf16[2,128,256]{2,1,0:T(8,128)(2,1)S(1)}, u32[]{:S(2)}, u32[]{:S(2)}) %collective-permute-start.9) | collective-permute-done | bytes 131104 | tf_op jit(solution)/shard_map/ppermute | solution.py:259
  24.4 0.5 %shard_map.78 = (bf16[2,64,1024]{2,1,0:T(8,128)(2,1)S(1)}, bf16[2,64,1024]{2,1,0:T(8,128)(2,1)S(1)}, f32[2,64,128]{2,1,0:T(8,128)S(1)}) custom-call(bf16[2,128,256]{2,1,0:T(8,128)(2,1)S(1)} %shard_map.73.own_ref, bf16[2,128,256]{2,1,0:T(8,128)(2,1)S(1)} %collective-permute-done.refs_0_.beside_ref, ...), custom_call_target="tpu_custom_call" | custom-call | flops 67108864 | bytes 1572864 | tf_op jit(solution)/shard_map/pallas_call | solution.py:244
  25.0 1.3 %collective-permute-start.10 = (bf16[2,64,1024]{2,1,0:T(8,128)(2,1)S(1)}, bf16[2,64,1024]{2,1,0:T(8,128)(2,1)S(1)}, u32[]{:S(2)}, u32[]{:S(2)}) collective-permute-start(bf16[2,64,1024]{2,1,0:T(8,128)(2,1)S(1)} %get-tuple-element.14), channel_id=1, source_target_pairs={{4,0},{8,4},{12,8},{16,12},{20,16},{24,20},{28,24},{5,1},{9,5},{13... | collective-permute-start | bytes 786440 | tf_op jit(solution)/shard_map/ppermute | solution.py:23
  26.3 1.4 %collective-permute-start.6 = (bf16[2,256,256]{2,1,0:T(8,128)(2,1)S(1)}, bf16[2,256,256]{2,1,0:T(8,128)(2,1)S(1)}, u32[]{:S(2)}, u32[]{:S(2)}) collective-permute-start(bf16[2,256,256]{2,1,0:T(8,128)(2,1)S(1)} %shard_map.74.own_ref), channel_id=1, source_target_pairs={{0,1},{1,0},{2,3},{3,2},{4,5},{5,4},{6,7},{7,6},{8,9},{9,8},{10,11... | collective-permute-start | bytes 786440 | tf_op jit(solution)/shard_map/ppermute | solution.py:257
  27.7 0.7 %collective-permute-start.7 = (bf16[2,256,256]{2,1,0:T(8,128)(2,1)S(1)}, bf16[2,256,256]{2,1,0:T(8,128)(2,1)S(1)}, u32[]{:S(2)}, u32[]{:S(2)}) collective-permute-start(bf16[2,256,256]{2,1,0:T(8,128)(2,1)S(1)} %shard_map.74.own_ref), channel_id=1, source_target_pairs={{1,2},{2,1},{5,6},{6,5},{9,10},{10,9},{13,14},{14,13},{17,18},{18,... | collective-permute-start | bytes 786440 | tf_op jit(solution)/shard_map/ppermute | solution.py:258
  28.4 1.8 %collective-permute-done.2.skip_ref = bf16[2,256,256]{2,1,0:T(8,128)(2,1)S(1)} collective-permute-done((bf16[2,256,256]{2,1,0:T(8,128)(2,1)S(1)}, bf16[2,256,256]{2,1,0:T(8,128)(2,1)S(1)}, u32[]{:S(2)}, u32[]{:S(2)}) %collective-permute-start.2) | collective-permute-done | bytes 262176 | tf_op jit(solution)/shard_map/ppermute | solution.py:256
  30.2 1.3 %collective-permute-start.3 = (bf16[2,256,256]{2,1,0:T(8,128)(2,1)S(1)}, bf16[2,256,256]{2,1,0:T(8,128)(2,1)S(1)}, u32[]{:S(2)}, u32[]{:S(2)}) collective-permute-start(bf16[2,256,256]{2,1,0:T(8,128)(2,1)S(1)} %collective-permute-done.2.skip_ref), channel_id=1, source_target_pairs={{1,0},{2,3},{5,4},{6,7},{9,8},{10,11},{13,12},{14,15},{17,16},{18,... | collective-permute-start | bytes 786440 | tf_op jit(solution)/shard_map/ppermute | solution.py:259
  31.5 0.8 %slice_convert_fusion = f32[64]{0:T(128)S(1)} fusion(s32[384]{0:T(512)} %param.9), kind=kLoop, calls=%fused_computation | loop fusion | flops 64 | bytes 512 | tf_op jit(solution)/shard_map/convert_element_type | solution.py:287
  32.3 0.1 broadcast_in_dim.2.weight_ref
  32.3 0.3 shard_map.79
  32.7 0.7 %collective-permute-start.11 = (f32[8,128]{1,0:T(8,128)S(1)}, f32[8,128]{1,0:T(8,128)S(1)}, u32[]{:S(2)}, u32[]{:S(2)}) collective-permute-start(f32[8,128]{1,0:T(8,128)S(1)} %shard_map.79), channel_id=1, source_target_pairs={{0,4},{4,0},{8,12},{12,8},{16,20},{20,16},{24,28},{28,24},{1,5},{5... | collective-permute-start | bytes 12296 | tf_op jit(solution)/shard_map/ppermute | solution.py:324
  33.3 0.8 %collective-permute-done.11 = f32[8,128]{1,0:T(8,128)S(1)} collective-permute-done((f32[8,128]{1,0:T(8,128)S(1)}, f32[8,128]{1,0:T(8,128)S(1)}, u32[]{:S(2)}, u32[]{:S(2)}) %collective-permute-start.11) | collective-permute-done | bytes 4128 | tf_op jit(solution)/shard_map/ppermute | solution.py:324
  34.2 1.6 %collective-permute-start.12 = (f32[8,128]{1,0:T(8,128)S(1)}, f32[8,128]{1,0:T(8,128)S(1)}, u32[]{:S(2)}, u32[]{:S(2)}) collective-permute-start(f32[8,128]{1,0:T(8,128)S(1)} %add.6), channel_id=1, source_target_pairs={{0,8},{4,12},{8,0},{12,4},{16,24},{20,28},{24,16},{28,20},{1,9},{5... | collective-permute-start | bytes 12296 | tf_op jit(solution)/shard_map/ppermute | solution.py:324
  35.8 2.0 %collective-permute-done.12 = f32[8,128]{1,0:T(8,128)S(1)} collective-permute-done((f32[8,128]{1,0:T(8,128)S(1)}, f32[8,128]{1,0:T(8,128)S(1)}, u32[]{:S(2)}, u32[]{:S(2)}) %collective-permute-start.12) | collective-permute-done | bytes 4128 | tf_op jit(solution)/shard_map/ppermute | solution.py:324
  37.8 6.5 %collective-permute-start.13 = (f32[8,128]{1,0:T(8,128)S(1)}, f32[8,128]{1,0:T(8,128)S(1)}, u32[]{:S(2)}, u32[]{:S(2)}) collective-permute-start(f32[8,128]{1,0:T(8,128)S(1)} %add.7.mine_ref), channel_id=1, source_target_pairs={{0,16},{4,20},{8,24},{12,28},{16,0},{20,4},{24,8},{28,12},{1,17},{... | collective-permute-start | bytes 12296 | tf_op jit(solution)/shard_map/ppermute | solution.py:324
  44.2 0.6 %shard_map.77.before_ref = f32[2,256,128]{2,1,0:T(8,128)S(1)} custom-call(bf16[2,256,256]{2,1,0:T(8,128)(2,1)S(1)} %shard_map.74.own_ref, bf16[2,256,256]{2,1,0:T(8,128)(2,1)S(1)} %collective-permute-done.6.beside_ref, bf16[2,256,256]{2,1,0:T(8,128)(2,1)S(1)} %collective-permute-done.7.near_ref, bf16[2,256,256]{2,1,0:T(8,128)(2,1)S(1)} %collective-permute-done.2.skip_ref, ...), custom_call_target="tpu_custom_call" | custom-call | flops 134217728 | bytes 3145728 | tf_op jit(solution)/shard_map/pallas_call | solution.py:244
  44.9 0.9 %collective-permute-done.13.other_ref = f32[8,128]{1,0:T(8,128)S(1)} collective-permute-done((f32[8,128]{1,0:T(8,128)S(1)}, f32[8,128]{1,0:T(8,128)S(1)}, u32[]{:S(2)}, u32[]{:S(2)}) %collective-permute-start.13) | collective-permute-done | bytes 4128 | tf_op jit(solution)/shard_map/ppermute | solution.py:324
  45.8 1.0 %shard_map.80 = f32[1,2,192,128]{3,2,1,0:T(8,128)} custom-call(bf16[2,256,256]{2,1,0:T(8,128)(2,1)S(1)} %collective-permute-done.2.skip_ref, bf16[2,256,256]{2,1,0:T(8,128)(2,1)S(1)} %collective-permute-done.3.far_ref, bf16[4,2,384,256]{3,2,1,0:T(8,128)(2,1)S(1)} %shard_map.76.res_ref, f32[2,256,128]{2,1,0:T(8,128)S(1)} %shard_map.77.before_ref, ...), custom_call_target="tpu_custom_call" | custom-call | flops 67108864 | bytes 1572864 | tf_op jit(solution)/shard_map/pallas_call | solution.py:244
  (16 shorter events, 0.1 us)
Async XLA Ops:
  0.0 1.0 %copy-start.2 = (bf16[2,384,256]{2,1,0:T(8,128)(2,1)S(1)}, bf16[2,384,256]{2,1,0:T(8,128)(2,1)}, u32[]{:S(2)}) copy-start(bf16[2,384,256]{2,1,0:T(8,128)(2,1)} %prim_ref.3) | copy-start | bytes 1179652
  1.0 11.9 %copy-start.3 = (bf16[2,384,256]{2,1,0:T(8,128)(2,1)S(1)}, bf16[2,384,256]{2,1,0:T(8,128)(2,1)}, u32[]{:S(2)}) copy-start(bf16[2,384,256]{2,1,0:T(8,128)(2,1)} %prim_ref.3) | copy-start | bytes 1179652
  1.0 11.8 %collective-permute-start = (bf16[2,128,256]{2,1,0:T(8,128)(2,1)S(1)}, bf16[2,128,256]{2,1,0:T(8,128)(2,1)S(1)}, u32[]{:S(2)}, u32[]{:S(2)}) collective-permute-start(bf16[2,128,256]{2,1,0:T(8,128)(2,1)S(1)} %shard_map.73.own_ref), channel_id=1, source_target_pairs={{0,1},{1,0},{2,3},{3,2},{4,5},{5,4},{6,7},{7,6},{8,9},{9,8},{10,11... | collective-permute-start | bytes 393224 | tf_op jit(solution)/shard_map/ppermute | solution.py:257
  4.1 8.8 %collective-permute-start.1 = (bf16[2,128,256]{2,1,0:T(8,128)(2,1)S(1)}, bf16[2,128,256]{2,1,0:T(8,128)(2,1)S(1)}, u32[]{:S(2)}, u32[]{:S(2)}) collective-permute-start(bf16[2,128,256]{2,1,0:T(8,128)(2,1)S(1)} %shard_map.73.own_ref), channel_id=1, source_target_pairs={{1,2},{2,1},{5,6},{6,5},{9,10},{10,9},{13,14},{14,13},{17,18},{18,... | collective-permute-start | bytes 393224 | tf_op jit(solution)/shard_map/ppermute | solution.py:258
  4.8 12.8 %collective-permute-start.8 = (bf16[2,128,256]{2,1,0:T(8,128)(2,1)S(1)}, bf16[2,128,256]{2,1,0:T(8,128)(2,1)S(1)}, u32[]{:S(2)}, u32[]{:S(2)}) collective-permute-start(bf16[2,128,256]{2,1,0:T(8,128)(2,1)S(1)} %shard_map.73.own_ref), channel_id=1, source_target_pairs={{0,2},{2,0},{1,3},{3,1},{4,6},{6,4},{5,7},{7,5},{8,10},{10,8},{9,1... | collective-permute-start | bytes 393224 | tf_op jit(solution)/shard_map/ppermute | solution.py:256
  8.7 1.4 %copy-start = (bf16[1,2,384,1024]{3,2,1,0:T(8,128)(2,1)S(1)}, bf16[1,2,384,1024]{3,2,1,0:T(8,128)(2,1)}, u32[]{:S(2)}) copy-start(bf16[1,2,384,1024]{3,2,1,0:T(8,128)(2,1)} %sec_ref.3) | copy-start | bytes 4718596
  10.1 11.4 %copy-start.1 = (bf16[1,2,384,1024]{3,2,1,0:T(8,128)(2,1)S(1)}, bf16[1,2,384,1024]{3,2,1,0:T(8,128)(2,1)}, u32[]{:S(2)}) copy-start(bf16[1,2,384,1024]{3,2,1,0:T(8,128)(2,1)} %sec_ref.3) | copy-start | bytes 4718596
  10.1 11.4 %collective-permute-start.4 = (bf16[2,32,1024]{2,1,0:T(8,128)(2,1)S(1)}, bf16[2,32,1024]{2,1,0:T(8,128)(2,1)S(1)}, u32[]{:S(2)}, u32[]{:S(2)}) collective-permute-start(bf16[2,32,1024]{2,1,0:T(8,128)(2,1)S(1)} %get-tuple-element.10), channel_id=1, source_target_pairs={{0,4},{4,8},{8,12},{12,16},{16,20},{20,24},{24,28},{1,5},{5,9},{9,... | collective-permute-start | bytes 393224 | tf_op jit(solution)/shard_map/ppermute | solution.py:23
  11.5 9.9 %collective-permute-start.5 = (bf16[2,32,1024]{2,1,0:T(8,128)(2,1)S(1)}, bf16[2,32,1024]{2,1,0:T(8,128)(2,1)S(1)}, u32[]{:S(2)}, u32[]{:S(2)}) collective-permute-start(bf16[2,32,1024]{2,1,0:T(8,128)(2,1)S(1)} %get-tuple-element.11), channel_id=1, source_target_pairs={{4,0},{8,4},{12,8},{16,12},{20,16},{24,20},{28,24},{5,1},{9,5},{13... | collective-permute-start | bytes 393224 | tf_op jit(solution)/shard_map/ppermute | solution.py:23
  12.9 17.3 %collective-permute-start.2 = (bf16[2,256,256]{2,1,0:T(8,128)(2,1)S(1)}, bf16[2,256,256]{2,1,0:T(8,128)(2,1)S(1)}, u32[]{:S(2)}, u32[]{:S(2)}) collective-permute-start(bf16[2,256,256]{2,1,0:T(8,128)(2,1)S(1)} %shard_map.74.own_ref), channel_id=1, source_target_pairs={{0,2},{2,0},{1,3},{3,1},{4,6},{6,4},{5,7},{7,5},{8,10},{10,8},{9,1... | collective-permute-start | bytes 786440 | tf_op jit(solution)/shard_map/ppermute | solution.py:256
  17.6 6.9 %collective-permute-start.9 = (bf16[2,128,256]{2,1,0:T(8,128)(2,1)S(1)}, bf16[2,128,256]{2,1,0:T(8,128)(2,1)S(1)}, u32[]{:S(2)}, u32[]{:S(2)}) collective-permute-start(bf16[2,128,256]{2,1,0:T(8,128)(2,1)S(1)} %collective-permute-done.8.skip_ref), channel_id=1, source_target_pairs={{1,0},{2,3},{5,4},{6,7},{9,8},{10,11},{13,12},{14,15},{17,16},{18,... | collective-permute-start | bytes 393224 | tf_op jit(solution)/shard_map/ppermute | solution.py:259
  25.0 7.3 %collective-permute-start.10 = (bf16[2,64,1024]{2,1,0:T(8,128)(2,1)S(1)}, bf16[2,64,1024]{2,1,0:T(8,128)(2,1)S(1)}, u32[]{:S(2)}, u32[]{:S(2)}) collective-permute-start(bf16[2,64,1024]{2,1,0:T(8,128)(2,1)S(1)} %get-tuple-element.14), channel_id=1, source_target_pairs={{4,0},{8,4},{12,8},{16,12},{20,16},{24,20},{28,24},{5,1},{9,5},{13... | collective-permute-start | bytes 786440 | tf_op jit(solution)/shard_map/ppermute | solution.py:23
  26.3 18.0 %collective-permute-start.6 = (bf16[2,256,256]{2,1,0:T(8,128)(2,1)S(1)}, bf16[2,256,256]{2,1,0:T(8,128)(2,1)S(1)}, u32[]{:S(2)}, u32[]{:S(2)}) collective-permute-start(bf16[2,256,256]{2,1,0:T(8,128)(2,1)S(1)} %shard_map.74.own_ref), channel_id=1, source_target_pairs={{0,1},{1,0},{2,3},{3,2},{4,5},{5,4},{6,7},{7,6},{8,9},{9,8},{10,11... | collective-permute-start | bytes 786440 | tf_op jit(solution)/shard_map/ppermute | solution.py:257
  27.7 16.6 %collective-permute-start.7 = (bf16[2,256,256]{2,1,0:T(8,128)(2,1)S(1)}, bf16[2,256,256]{2,1,0:T(8,128)(2,1)S(1)}, u32[]{:S(2)}, u32[]{:S(2)}) collective-permute-start(bf16[2,256,256]{2,1,0:T(8,128)(2,1)S(1)} %shard_map.74.own_ref), channel_id=1, source_target_pairs={{1,2},{2,1},{5,6},{6,5},{9,10},{10,9},{13,14},{14,13},{17,18},{18,... | collective-permute-start | bytes 786440 | tf_op jit(solution)/shard_map/ppermute | solution.py:258
  30.2 15.6 %collective-permute-start.3 = (bf16[2,256,256]{2,1,0:T(8,128)(2,1)S(1)}, bf16[2,256,256]{2,1,0:T(8,128)(2,1)S(1)}, u32[]{:S(2)}, u32[]{:S(2)}) collective-permute-start(bf16[2,256,256]{2,1,0:T(8,128)(2,1)S(1)} %collective-permute-done.2.skip_ref), channel_id=1, source_target_pairs={{1,0},{2,3},{5,4},{6,7},{9,8},{10,11},{13,12},{14,15},{17,16},{18,... | collective-permute-start | bytes 786440 | tf_op jit(solution)/shard_map/ppermute | solution.py:259
  32.7 1.5 %collective-permute-start.11 = (f32[8,128]{1,0:T(8,128)S(1)}, f32[8,128]{1,0:T(8,128)S(1)}, u32[]{:S(2)}, u32[]{:S(2)}) collective-permute-start(f32[8,128]{1,0:T(8,128)S(1)} %shard_map.79), channel_id=1, source_target_pairs={{0,4},{4,0},{8,12},{12,8},{16,20},{20,16},{24,28},{28,24},{1,5},{5... | collective-permute-start | bytes 12296 | tf_op jit(solution)/shard_map/ppermute | solution.py:324
  34.2 3.6 %collective-permute-start.12 = (f32[8,128]{1,0:T(8,128)S(1)}, f32[8,128]{1,0:T(8,128)S(1)}, u32[]{:S(2)}, u32[]{:S(2)}) collective-permute-start(f32[8,128]{1,0:T(8,128)S(1)} %add.6), channel_id=1, source_target_pairs={{0,8},{4,12},{8,0},{12,4},{16,24},{20,28},{24,16},{28,20},{1,9},{5... | collective-permute-start | bytes 12296 | tf_op jit(solution)/shard_map/ppermute | solution.py:324
  37.8 8.1 %collective-permute-start.13 = (f32[8,128]{1,0:T(8,128)S(1)}, f32[8,128]{1,0:T(8,128)S(1)}, u32[]{:S(2)}, u32[]{:S(2)}) collective-permute-start(f32[8,128]{1,0:T(8,128)S(1)} %add.7.mine_ref), channel_id=1, source_target_pairs={{0,16},{4,20},{8,24},{12,28},{16,0},{20,4},{24,8},{28,12},{1,17},{... | collective-permute-start | bytes 12296 | tf_op jit(solution)/shard_map/ppermute | solution.py:324

commit v6 on v5

--- a/solution.py
+++ b/solution.py
@@ -55,7 +55,13 @@
 
 
 def cut_middle_kernel(prim_ref, *refs):
-    refs[-1][...] = prim_ref[:, LAG : prim_ref.shape[1] - LAG]
+    cut_ref = refs[-1]
+    cut_ref[...] = prim_ref[:, LAG : LAG + cut_ref.shape[1]]
+
+
+def relay_kernel(block_ref, stats_ref, out_ref):
+    del stats_ref
+    out_ref[...] = block_ref[:, : out_ref.shape[1]]
 
 
 def resample_kernel(sec_ref, low_ref, high_ref, ao_ref, ro_ref, af_ref, rf_ref, out_ref, azim_ref):
@@ -124,33 +130,25 @@
     return total
 
 
-def slots(own_ref, beside_ref, near_ref, skip_ref, far_ref):
+def margin_kernel(
+    own_ref, one_ref, two_ref, three_ref, res_ref, first_ref, last_ref, looks_ref, sums_ref
+):
     here = lax.axis_index("date")
-    inner = (here == 1) | (here == 2)
-    low = here < 2
-    return (
-        (here, lambda part: own_ref[part]),
-        (jnp.where(lax.rem(here, 2) == 0, here + 1, here - 1), lambda part: beside_ref[part]),
-        (jnp.where(low, 2, 1), lambda part: jnp.where(inner, near_ref[part], skip_ref[part])),
-        (jnp.where(low, 3, 0), lambda part: jnp.where(inner, skip_ref[part], far_ref[part])),
-    )
-
-
-def margin_kernel(
-    own_ref, beside_ref, near_ref, skip_ref, far_ref, res_ref, first_ref, last_ref, looks_ref, sums_ref
-):
     _, _, rows_n, width = res_ref.shape
+    whole, edges = (0, rows_n - LAG), (0, LAG)
     looks_n = looks_ref.shape[2]
     totals = [None, None]
-    for step, (block, read) in enumerate(slots(own_ref, beside_ref, near_ref, skip_ref, far_ref)):
-        prim_re, prim_im = read(0), read(1)
+    for step, (prim_ref, starts) in enumerate(
+        ((own_ref, whole), (one_ref, whole), (two_ref, edges), (three_ref, edges))
+    ):
+        block = jnp.bitwise_xor(here, step)
         select = look_columns(width, block, looks_n)
         columns = pl.ds(pl.multiple_of(block * width, width), width)
         halves = []
-        for held, start, target in ((0, 0, first_ref), (LAG, rows_n - LAG, last_ref)):
+        for held, start, target in zip(starts, whole, (first_ref, last_ref)):
             pair = interfere(
-                prim_re[held : held + LAG],
-                prim_im[held : held + LAG],
+                prim_ref[0, held : held + LAG],
+                prim_ref[1, held : held + LAG],
                 res_ref[block, 0, start : start + LAG],
                 res_ref[block, 1, start : start + LAG],
             )
@@ -189,13 +187,17 @@
 
 
 def look_sums(pieces, res_ref, looks_n):
+    here = lax.axis_index("date")
     _, _, rows_n, width = res_ref.shape
+    middle_n = rows_n - 2 * LAG
     totals = [None, None]
-    for step, (block, read) in enumerate(pieces):
+    for at, (step, prim_ref) in enumerate(pieces):
+        block = jnp.bitwise_xor(here, step)
+        first = LAG if prim_ref.shape[1] == rows_n else 0
         select = look_columns(width, block, looks_n)
         pair = interfere(
-            read(0),
-            read(1),
+            prim_ref[0, first : first + middle_n],
+            prim_ref[1, first : first + middle_n],
             res_ref[block, 0, LAG : rows_n - LAG],
             res_ref[block, 1, LAG : rows_n - LAG],
         )
@@ -203,22 +205,22 @@
             summed = jnp.dot(
                 pair[part].astype(jnp.bfloat16), select, preferred_element_type=jnp.float32
             )
-            totals[part] = summed if step == 0 else totals[part] + summed
+            totals[part] = summed if at == 0 else totals[part] + summed
     return totals
 
 
-def middle_kernel(own_ref, beside_ref, near_ref, skip_ref, res_ref, out_ref):
-    pieces = slots(own_ref, beside_ref, near_ref, skip_ref, None)[:3]
+def middle_kernel(own_ref, one_ref, two_ref, res_ref, out_ref):
+    pieces = ((0, own_ref), (1, one_ref), (2, two_ref))
     for part, total in enumerate(look_sums(pieces, res_ref, out_ref.shape[2])):
         out_ref[part] = total
 
 
 def finish_kernel(
-    skip_ref, far_ref, res_ref, before_ref, looks_ref, mine_ref, other_ref, out_ref, sums_ref
+    three_ref, res_ref, before_ref, looks_ref, mine_ref, other_ref, out_ref, sums_ref
 ):
     looks_n = out_ref.shape[3]
     middle_n = before_ref.shape[1]
-    totals = look_sums(slots(None, None, None, skip_ref, far_ref)[3:], res_ref, looks_n)
+    totals = look_sums(((3, three_ref),), res_ref, looks_n)
     totals = [total + before_ref[part] for part, total in enumerate(totals)]
     stats = jnp.sum(mine_ref[...] + other_ref[...], axis=1, keepdims=True)
     e_re, e_im, power, count = [stats[row : row + 1] for row in range(4)]
@@ -252,12 +254,8 @@
     )(*args)
 
 
-def spread(block):
-    skip = lax.ppermute(block, "date", [(0, 2), (2, 0), (1, 3), (3, 1)])
-    beside = lax.ppermute(block, "date", [(0, 1), (1, 0), (2, 3), (3, 2)])
-    near = lax.ppermute(block, "date", [(1, 2), (2, 1)])
-    far = lax.ppermute(skip, "date", [(1, 0), (2, 3)])
-    return beside, near, skip, far
+def swap(value, axis, step):
+    return lax.ppermute(value, axis, [(at, at ^ step) for at in range(lax.axis_size(axis))])
 
 
 def fused(secondary, primary, margin_mask, az_off, rg_off, az_frac, rg_frac):
@@ -272,63 +270,66 @@
     edges = call(
         cut_edges_kernel, shape((2, 2 * LAG, width), bf16), [], (0, 16 * LAG * width), primary
     )
-    around = spread(edges)
+    one = swap(primary, "date", 1)
+    edges_two, edges_three = [swap(edges, "date", step) for step in (2, 3)]
     halo = shape((2, HALO, cols_n), bf16)
     down, up = call(cut_halo_kernel, (halo, halo), [], (0, 16 * HALO * cols_n), secondary)
     low = passed_along(down, "tile", 1)
     high = passed_along(up, "tile", -1)
     middle = call(
         cut_middle_kernel,
-        shape((2, middle_n, width), bf16),
+        shape((2, middle_n + 16, width), bf16),
         [],
-        (0, 8 * middle_n * width),
-        primary, *around[:2],
+        (0, 0),
+        primary, edges_two,
     )
     weight = jnp.broadcast_to(margin_mask[rows_n - LAG :].astype(f32)[:, None], (LAG, LANE))
     res = call(
         resample_kernel,
         shape((dates_n, 2, rows_n, width), bf16),
         [pltpu.VMEM((2, rows_n, cols_n), bf16)],
-        (2 * 2 * rows_n * cols_n * (2 * HALO + BAND + 2 * width), 8 * rows_n * cols_n),
+        (0, 0),
         secondary, low, high, az_off, rg_off, az_frac, rg_frac,
     )
-    others = spread(middle)
+    two = swap(middle, "date", 2)
     margin = shape((2, LAG, cols_n), bf16)
     first, last, looks = call(
         margin_kernel,
         (margin, margin, shape((2, 2 * LAG // LA, looks_n), f32)),
         [pltpu.VMEM((2, 2 * LAG, looks_n), f32)],
-        (2 * 2 * 2 * LAG * cols_n * looks_n, 24 * LAG * cols_n),
-        edges, *around, res,
+        (0, 0),
+        primary, one, edges_two, edges_three, res,
     )
     later = passed_along(first, "tile", -1)
     stats = call(
         stats_kernel,
         shape((8, LANE), f32),
         [],
-        (20 * LAG * cols_n, 8 * LAG * cols_n),
+        (0, 0),
         last, later, weight,
     )
-    beside, near, skip, far = others
     before = call(
         middle_kernel,
         shape((2, middle_n, looks_n), f32),
         [],
         (2 * 2 * middle_n * cols_n * looks_n, 8 * rows_n * cols_n),
-        middle, beside, near, skip, res,
-    )
-    stride = 1
-    other = jnp.zeros_like(stats)
+        primary, one, two, res,
+    )
+    other = swap(stats, "tile", 1)
+    block = shape((2, middle_n, width), bf16)
+    relayed = call(relay_kernel, block, [], (0, 0), two, other)
+    three = swap(relayed, "date", 1)
+    stride = 2
     while stride < tiles_n:
-        stats = stats + other if stride > 1 else stats
-        other = lax.ppermute(stats, "tile", [(at, at ^ stride) for at in range(tiles_n)])
+        stats = stats + other
+        other = swap(stats, "tile", stride)
         stride *= 2
     return call(
         finish_kernel,
         shape((1, 2, rows_n // LA, looks_n), f32),
         [pltpu.VMEM((2, middle_n, looks_n), f32)],
         (2 * middle_n * cols_n * looks_n, 4 * rows_n * cols_n),
-        skip, far, res, before, looks, stats, other,
+        three, res, before, looks, stats, other,
     )
 
 

time: 47.6 us -> 48 us (level); the launches traced: 46.8 us -> 47.7 us
  waiting for transfers between devices: 6.92 us -> 10.6 us
  starting transfers between devices: 29.7 us -> 27 us
    ppermute x11 -> x8, starting transfers between devices: 25.7 us -> 23 us  [swap(): lax.ppermute(value, axis, [(at, at ^ step) for at in range(lax.axis_size(...]
    ppermute x11 -> x8, waiting for transfers between devices: 6.92 us -> 9.21 us  [swap(): lax.ppermute(value, axis, [(at, at ^ step) for at in range(lax.axis_size(...]
    ppermute x3, waiting for transfers between devices: 0.01 us -> 1.38 us  [passed_along(): lax.ppermute(value, axis, [(source, source + steps) for source in range(i...]
    pallas_call x8 -> x9, Pallas kernels: 4.17 us -> 4.11 us  [call(): pl.pallas_call(kernel, out_shape=outs, in_specs=[vmem] * len(args), out_s...]
  transfers between devices with their start and end apart: 14 -> 11, of which waited for: 5 -> 5; matrix products, arithmetic and copies ran while one was open for 2% -> 2% of each run, Pallas kernels for 7% -> 7%
where the time goes in v6:
time: 48 us; the launch traced here: 47.7 us
  starting transfers between devices  27 us (56%)
  waiting for transfers between devices  10.6 us (22%)
  Pallas kernels  4.11 us (9%)
  between operations  2.71 us (6%)
  local copies, waits for them, and re-layouts  2.51 us (5%)
  other arithmetic  0.76 us (2%)
    ppermute x8, starting transfers between devices, swap(): lax.ppermute(value, axis, [(at, at ^ step) for at in range(lax.axis_size(...  23 us
    ppermute x8, waiting for transfers between devices, swap(): lax.ppermute(value, axis, [(at, at ^ step) for at in range(lax.axis_size(...  9.21 us
    pallas_call x9, Pallas kernels, call(): pl.pallas_call(kernel, out_shape=outs, in_specs=[vmem] * len(args), out_s...  4.11 us
    ppermute x3, starting transfers between devices, passed_along(): lax.ppermute(value, axis, [(source, source + steps) for source in range(i...  4.01 us
    unnamed x8, local copies, waits for them, and re-layouts  2.44 us
    ppermute x3, waiting for transfers between devices, passed_along(): lax.ppermute(value, axis, [(source, source + steps) for source in range(i...  1.38 us
  transfers between devices with their start and end apart: 11, of which 5 were waited for; matrix products, arithmetic and copies ran while one was open for 2% of the time, Pallas kernels for 7%

profile of v6, /device:TPU:0, one launch (start us, length us, event | category | flops | bytes accessed | tf_op | source)
XLA Modules:
  0.0 47.7 jit_solution(6948923735070927178)
XLA Ops:
  0.0 3.0 %collective-permute-start.2 = (bf16[2,384,256]{2,1,0:T(8,128)(2,1)}, bf16[2,384,256]{2,1,0:T(8,128)(2,1)S(1)}, u32[]{:S(2)}, u32[]{:S(2)}) collective-permute-start(bf16[2,384,256]{2,1,0:T(8,128)(2,1)} %own_ref.3), channel_id=1, source_target_pairs={{0,1},{1,0},{2,3},{3,2},{4,5},{5,4},{6,7},{7,6},{8,9},{9,8},{10,11... | collective-permute-start | bytes 1179656 | tf_op jit(solution)/shard_map/ppermute | solution.py:258
  3.0 1.0 %copy-done.2 = bf16[2,384,256]{2,1,0:T(8,128)(2,1)S(1)} copy-done((bf16[2,384,256]{2,1,0:T(8,128)(2,1)S(1)}, bf16[2,384,256]{2,1,0:T(8,128)(2,1)}, u32[]{:S(2)}) %copy-start.2) | copy-done | bytes 393240
  4.1 2.7 %collective-permute-start = (bf16[2,128,256]{2,1,0:T(8,128)(2,1)S(1)}, bf16[2,128,256]{2,1,0:T(8,128)(2,1)S(1)}, u32[]{:S(2)}, u32[]{:S(2)}) collective-permute-start(bf16[2,128,256]{2,1,0:T(8,128)(2,1)S(1)} %shard_map.73), channel_id=1, source_target_pairs={{0,2},{1,3},{2,0},{3,1},{4,6},{5,7},{6,4},{7,5},{8,10},{9,11},{10,... | collective-permute-start | bytes 393224 | tf_op jit(solution)/shard_map/ppermute | solution.py:258
  6.7 1.4 %copy-done = bf16[1,2,384,1024]{3,2,1,0:T(8,128)(2,1)S(1)} copy-done((bf16[1,2,384,1024]{3,2,1,0:T(8,128)(2,1)S(1)}, bf16[1,2,384,1024]{3,2,1,0:T(8,128)(2,1)}, u32[]{:S(2)}) %copy-start) | copy-done | bytes 1572888
  8.2 1.4 %collective-permute-start.4 = (bf16[2,32,1024]{2,1,0:T(8,128)(2,1)S(1)}, bf16[2,32,1024]{2,1,0:T(8,128)(2,1)S(1)}, u32[]{:S(2)}, u32[]{:S(2)}) collective-permute-start(bf16[2,32,1024]{2,1,0:T(8,128)(2,1)S(1)} %get-tuple-element.10), channel_id=1, source_target_pairs={{0,4},{4,8},{8,12},{12,16},{16,20},{20,24},{24,28},{1,5},{5,9},{9,... | collective-permute-start | bytes 393224 | tf_op jit(solution)/shard_map/ppermute | solution.py:23
  9.6 1.3 %collective-permute-start.5 = (bf16[2,32,1024]{2,1,0:T(8,128)(2,1)S(1)}, bf16[2,32,1024]{2,1,0:T(8,128)(2,1)S(1)}, u32[]{:S(2)}, u32[]{:S(2)}) collective-permute-start(bf16[2,32,1024]{2,1,0:T(8,128)(2,1)S(1)} %get-tuple-element.11), channel_id=1, source_target_pairs={{4,0},{8,4},{12,8},{16,12},{20,16},{24,20},{28,24},{5,1},{9,5},{13... | collective-permute-start | bytes 393224 | tf_op jit(solution)/shard_map/ppermute | solution.py:23
  10.9 0.2 collective-permute-start.3
  11.1 3.6 %collective-permute-done.refs_0_.two_ref = bf16[2,128,256]{2,1,0:T(8,128)(2,1)S(1)} collective-permute-done((bf16[2,128,256]{2,1,0:T(8,128)(2,1)S(1)}, bf16[2,128,256]{2,1,0:T(8,128)(2,1)S(1)}, u32[]{:S(2)}, u32[]{:S(2)}) %collective-permute-start) | collective-permute-done | bytes 131104 | tf_op jit(solution)/shard_map/ppermute | solution.py:258
  14.7 0.0 copy-done.3
  14.7 3.5 %collective-permute-start.1 = (bf16[2,272,256]{2,1,0:T(8,128)(2,1)S(1)}, bf16[2,272,256]{2,1,0:T(8,128)(2,1)S(1)}, u32[]{:S(2)}, u32[]{:S(2)}) collective-permute-start(bf16[2,272,256]{2,1,0:T(8,128)(2,1)S(1)} %shard_map.74), channel_id=1, source_target_pairs={{0,2},{1,3},{2,0},{3,1},{4,6},{5,7},{6,4},{7,5},{8,10},{9,11},{10,... | collective-permute-start | bytes 835592 | tf_op jit(solution)/shard_map/ppermute | solution.py:258
  20.8 0.0 collective-permute-done.4.low_ref
  20.8 0.0 collective-permute-done.5.high_ref
  20.8 1.6 %shard_map.76.res_ref = bf16[4,2,384,256]{3,2,1,0:T(8,128)(2,1)S(1)} custom-call(bf16[1,2,384,1024]{3,2,1,0:T(8,128)(2,1)S(1)} %copy-done.1, bf16[2,32,1024]{2,1,0:T(8,128)(2,1)S(1)} %collective-permute-done.4.low_ref, bf16[2,32,1024]{2,1,0:T(8,128)(2,1)S(1)} %collective-permute-done.5.high_ref, s32[1,1]{1,0:T(1,128)S(6)} %copy.8.ao_ref, ...), custom_call_target="tpu_custom_call" | custom-call | tf_op jit(solution)/shard_map/pallas_call | solution.py:246
  22.4 0.0 collective-permute-done.3.three_ref
  22.4 0.0 collective-permute-done.2.one_ref
  22.4 0.5 %shard_map.77 = (bf16[2,64,1024]{2,1,0:T(8,128)(2,1)S(1)}, bf16[2,64,1024]{2,1,0:T(8,128)(2,1)S(1)}, f32[2,64,128]{2,1,0:T(8,128)S(1)}) custom-call(bf16[2,384,256]{2,1,0:T(8,128)(2,1)S(1)} %copy-done.3, bf16[2,384,256]{2,1,0:T(8,128)(2,1)S(1)} %collective-permute-done.2.one_ref, bf16[2,128,256]{2,1,0:T(8,128)(2,1)S(1)} %collective-permute-done.refs_0_.two_ref, ...), custom_call_target="tpu_custom_call" | custom-call | tf_op jit(solution)/shard_map/pallas_call | solution.py:246
  23.0 1.3 %collective-permute-start.6 = (bf16[2,64,1024]{2,1,0:T(8,128)(2,1)S(1)}, bf16[2,64,1024]{2,1,0:T(8,128)(2,1)S(1)}, u32[]{:S(2)}, u32[]{:S(2)}) collective-permute-start(bf16[2,64,1024]{2,1,0:T(8,128)(2,1)S(1)} %get-tuple-element.13), channel_id=1, source_target_pairs={{4,0},{8,4},{12,8},{16,12},{20,16},{24,20},{28,24},{5,1},{9,5},{13... | collective-permute-start | bytes 786440 | tf_op jit(solution)/shard_map/ppermute | solution.py:23
  24.3 0.8 %slice_convert_fusion = f32[64]{0:T(128)S(1)} fusion(s32[384]{0:T(512)} %param.9), kind=kLoop, calls=%fused_computation | loop fusion | flops 64 | bytes 512 | tf_op jit(solution)/shard_map/convert_element_type | solution.py:286
  25.0 1.4 %collective-permute-done.6.later_ref = bf16[2,64,1024]{2,1,0:T(8,128)(2,1)S(1)} collective-permute-done((bf16[2,64,1024]{2,1,0:T(8,128)(2,1)S(1)}, bf16[2,64,1024]{2,1,0:T(8,128)(2,1)S(1)}, u32[]{:S(2)}, u32[]{:S(2)}) %collective-permute-start.6) | collective-permute-done | bytes 262176 | tf_op jit(solution)/shard_map/ppermute | solution.py:23
  26.4 0.1 broadcast_in_dim.2.weight_ref
  26.5 0.3 shard_map.78
  26.8 4.5 %collective-permute-start.7 = (f32[8,128]{1,0:T(8,128)S(1)}, f32[8,128]{1,0:T(8,128)S(1)}, u32[]{:S(2)}, u32[]{:S(2)}) collective-permute-start(f32[8,128]{1,0:T(8,128)S(1)} %shard_map.78), channel_id=1, source_target_pairs={{0,4},{4,0},{8,12},{12,8},{16,20},{20,16},{24,28},{28,24},{1,5},{5... | collective-permute-start | bytes 12296 | tf_op jit(solution)/shard_map/ppermute | solution.py:258
  31.3 2.2 %collective-permute-done.1.block_ref.two_ref = bf16[2,272,256]{2,1,0:T(8,128)(2,1)S(1)} collective-permute-done((bf16[2,272,256]{2,1,0:T(8,128)(2,1)S(1)}, bf16[2,272,256]{2,1,0:T(8,128)(2,1)S(1)}, u32[]{:S(2)}, u32[]{:S(2)}) %collective-permute-start.1) | collective-permute-done | bytes 278560 | tf_op jit(solution)/shard_map/ppermute | solution.py:258
  33.5 0.0 collective-permute-done.7.stats_ref
  33.5 5.6 %collective-permute-start.8 = (bf16[2,256,256]{2,1,0:T(8,128)(2,1)S(1)}, bf16[2,256,256]{2,1,0:T(8,128)(2,1)S(1)}, u32[]{:S(2)}, u32[]{:S(2)}) collective-permute-start(bf16[2,256,256]{2,1,0:T(8,128)(2,1)S(1)} %shard_map.79), channel_id=1, source_target_pairs={{0,1},{1,0},{2,3},{3,2},{4,5},{5,4},{6,7},{7,6},{8,9},{9,8},{10,11... | collective-permute-start | bytes 786440 | tf_op jit(solution)/shard_map/ppermute | solution.py:258
  39.1 2.4 %collective-permute-start.9 = (f32[8,128]{1,0:T(8,128)S(1)}, f32[8,128]{1,0:T(8,128)S(1)}, u32[]{:S(2)}, u32[]{:S(2)}) collective-permute-start(f32[8,128]{1,0:T(8,128)S(1)} %add.6), channel_id=1, source_target_pairs={{0,8},{4,12},{8,0},{12,4},{16,24},{20,28},{24,16},{28,20},{1,9},{5... | collective-permute-start | bytes 12296 | tf_op jit(solution)/shard_map/ppermute | solution.py:258
  41.5 1.6 %collective-permute-done.9 = f32[8,128]{1,0:T(8,128)S(1)} collective-permute-done((f32[8,128]{1,0:T(8,128)S(1)}, f32[8,128]{1,0:T(8,128)S(1)}, u32[]{:S(2)}, u32[]{:S(2)}) %collective-permute-start.9) | collective-permute-done | bytes 4128 | tf_op jit(solution)/shard_map/ppermute | solution.py:258
  43.1 1.2 %collective-permute-start.10 = (f32[8,128]{1,0:T(8,128)S(1)}, f32[8,128]{1,0:T(8,128)S(1)}, u32[]{:S(2)}, u32[]{:S(2)}) collective-permute-start(f32[8,128]{1,0:T(8,128)S(1)} %add.7.mine_ref), channel_id=1, source_target_pairs={{0,16},{4,20},{8,24},{12,28},{16,0},{20,4},{24,8},{28,12},{1,17},{... | collective-permute-start | bytes 12296 | tf_op jit(solution)/shard_map/ppermute | solution.py:258
  44.3 0.6 %shard_map.80.before_ref = f32[2,256,128]{2,1,0:T(8,128)S(1)} custom-call(bf16[2,384,256]{2,1,0:T(8,128)(2,1)S(1)} %copy-done.3, bf16[2,384,256]{2,1,0:T(8,128)(2,1)S(1)} %collective-permute-done.2.one_ref, bf16[2,272,256]{2,1,0:T(8,128)(2,1)S(1)} %collective-permute-done.1.block_ref.two_ref, bf16[4,2,384,256]{3,2,1,0:T(8,128)(2,1)S(1)} %shard_map.76.res_ref), custom_call_target="tpu_custom_call" | custom-call | flops 134217728 | bytes 3145728 | tf_op jit(solution)/shard_map/pallas_call | solution.py:246
  44.9 1.8 %collective-permute-done.10.other_ref = f32[8,128]{1,0:T(8,128)S(1)} collective-permute-done((f32[8,128]{1,0:T(8,128)S(1)}, f32[8,128]{1,0:T(8,128)S(1)}, u32[]{:S(2)}, u32[]{:S(2)}) %collective-permute-start.10) | collective-permute-done | bytes 4128 | tf_op jit(solution)/shard_map/ppermute | solution.py:258
  46.7 0.0 collective-permute-done.8.three_ref
  46.7 1.0 %shard_map.81 = f32[1,2,192,128]{3,2,1,0:T(8,128)} custom-call(bf16[2,256,256]{2,1,0:T(8,128)(2,1)S(1)} %collective-permute-done.8.three_ref, bf16[4,2,384,256]{3,2,1,0:T(8,128)(2,1)S(1)} %shard_map.76.res_ref, f32[2,256,128]{2,1,0:T(8,128)S(1)} %shard_map.80.before_ref, f32[2,64,128]{2,1,0:T(8,128)S(1)} %get-tuple-element.14.looks_ref, ...), custom_call_target="tpu_custom_call" | custom-call | flops 67108864 | bytes 1572864 | tf_op jit(solution)/shard_map/pallas_call | solution.py:246
  (11 shorter events, 0.1 us)
Async XLA Ops:
  0.0 22.4 %collective-permute-start.2 = (bf16[2,384,256]{2,1,0:T(8,128)(2,1)}, bf16[2,384,256]{2,1,0:T(8,128)(2,1)S(1)}, u32[]{:S(2)}, u32[]{:S(2)}) collective-permute-start(bf16[2,384,256]{2,1,0:T(8,128)(2,1)} %own_ref.3), channel_id=1, source_target_pairs={{0,1},{1,0},{2,3},{3,2},{4,5},{5,4},{6,7},{7,6},{8,9},{9,8},{10,11... | collective-permute-start | bytes 1179656 | tf_op jit(solution)/shard_map/ppermute | solution.py:258
  3.0 1.0 %copy-start.2 = (bf16[2,384,256]{2,1,0:T(8,128)(2,1)S(1)}, bf16[2,384,256]{2,1,0:T(8,128)(2,1)}, u32[]{:S(2)}) copy-start(bf16[2,384,256]{2,1,0:T(8,128)(2,1)} %own_ref.3) | copy-start | bytes 1179652
  4.1 10.6 %copy-start.3 = (bf16[2,384,256]{2,1,0:T(8,128)(2,1)S(1)}, bf16[2,384,256]{2,1,0:T(8,128)(2,1)}, u32[]{:S(2)}) copy-start(bf16[2,384,256]{2,1,0:T(8,128)(2,1)} %own_ref.3) | copy-start | bytes 1179652
  4.1 10.6 %collective-permute-start = (bf16[2,128,256]{2,1,0:T(8,128)(2,1)S(1)}, bf16[2,128,256]{2,1,0:T(8,128)(2,1)S(1)}, u32[]{:S(2)}, u32[]{:S(2)}) collective-permute-start(bf16[2,128,256]{2,1,0:T(8,128)(2,1)S(1)} %shard_map.73), channel_id=1, source_target_pairs={{0,2},{1,3},{2,0},{3,1},{4,6},{5,7},{6,4},{7,5},{8,10},{9,11},{10,... | collective-permute-start | bytes 393224 | tf_op jit(solution)/shard_map/ppermute | solution.py:258
  6.7 1.4 %copy-start = (bf16[1,2,384,1024]{3,2,1,0:T(8,128)(2,1)S(1)}, bf16[1,2,384,1024]{3,2,1,0:T(8,128)(2,1)}, u32[]{:S(2)}) copy-start(bf16[1,2,384,1024]{3,2,1,0:T(8,128)(2,1)} %sec_ref.3) | copy-start | bytes 4718596
  8.1 12.7 %copy-start.1 = (bf16[1,2,384,1024]{3,2,1,0:T(8,128)(2,1)S(1)}, bf16[1,2,384,1024]{3,2,1,0:T(8,128)(2,1)}, u32[]{:S(2)}) copy-start(bf16[1,2,384,1024]{3,2,1,0:T(8,128)(2,1)} %sec_ref.3) | copy-start | bytes 4718596
  8.2 12.6 %collective-permute-start.4 = (bf16[2,32,1024]{2,1,0:T(8,128)(2,1)S(1)}, bf16[2,32,1024]{2,1,0:T(8,128)(2,1)S(1)}, u32[]{:S(2)}, u32[]{:S(2)}) collective-permute-start(bf16[2,32,1024]{2,1,0:T(8,128)(2,1)S(1)} %get-tuple-element.10), channel_id=1, source_target_pairs={{0,4},{4,8},{8,12},{12,16},{16,20},{20,24},{24,28},{1,5},{5,9},{9,... | collective-permute-start | bytes 393224 | tf_op jit(solution)/shard_map/ppermute | solution.py:23
  9.6 11.2 %collective-permute-start.5 = (bf16[2,32,1024]{2,1,0:T(8,128)(2,1)S(1)}, bf16[2,32,1024]{2,1,0:T(8,128)(2,1)S(1)}, u32[]{:S(2)}, u32[]{:S(2)}) collective-permute-start(bf16[2,32,1024]{2,1,0:T(8,128)(2,1)S(1)} %get-tuple-element.11), channel_id=1, source_target_pairs={{4,0},{8,4},{12,8},{16,12},{20,16},{24,20},{28,24},{5,1},{9,5},{13... | collective-permute-start | bytes 393224 | tf_op jit(solution)/shard_map/ppermute | solution.py:23
  10.9 11.5 %collective-permute-start.3 = (bf16[2,128,256]{2,1,0:T(8,128)(2,1)S(1)}, bf16[2,128,256]{2,1,0:T(8,128)(2,1)S(1)}, u32[]{:S(2)}, u32[]{:S(2)}) collective-permute-start(bf16[2,128,256]{2,1,0:T(8,128)(2,1)S(1)} %shard_map.73), channel_id=1, source_target_pairs={{0,3},{1,2},{2,1},{3,0},{4,7},{5,6},{6,5},{7,4},{8,11},{9,10},{10,... | collective-permute-start | bytes 393224 | tf_op jit(solution)/shard_map/ppermute | solution.py:258
  14.7 18.8 %collective-permute-start.1 = (bf16[2,272,256]{2,1,0:T(8,128)(2,1)S(1)}, bf16[2,272,256]{2,1,0:T(8,128)(2,1)S(1)}, u32[]{:S(2)}, u32[]{:S(2)}) collective-permute-start(bf16[2,272,256]{2,1,0:T(8,128)(2,1)S(1)} %shard_map.74), channel_id=1, source_target_pairs={{0,2},{1,3},{2,0},{3,1},{4,6},{5,7},{6,4},{7,5},{8,10},{9,11},{10,... | collective-permute-start | bytes 835592 | tf_op jit(solution)/shard_map/ppermute | solution.py:258
  23.0 3.4 %collective-permute-start.6 = (bf16[2,64,1024]{2,1,0:T(8,128)(2,1)S(1)}, bf16[2,64,1024]{2,1,0:T(8,128)(2,1)S(1)}, u32[]{:S(2)}, u32[]{:S(2)}) collective-permute-start(bf16[2,64,1024]{2,1,0:T(8,128)(2,1)S(1)} %get-tuple-element.13), channel_id=1, source_target_pairs={{4,0},{8,4},{12,8},{16,12},{20,16},{24,20},{28,24},{5,1},{9,5},{13... | collective-permute-start | bytes 786440 | tf_op jit(solution)/shard_map/ppermute | solution.py:23
  26.8 6.6 %collective-permute-start.7 = (f32[8,128]{1,0:T(8,128)S(1)}, f32[8,128]{1,0:T(8,128)S(1)}, u32[]{:S(2)}, u32[]{:S(2)}) collective-permute-start(f32[8,128]{1,0:T(8,128)S(1)} %shard_map.78), channel_id=1, source_target_pairs={{0,4},{4,0},{8,12},{12,8},{16,20},{20,16},{24,28},{28,24},{1,5},{5... | collective-permute-start | bytes 12296 | tf_op jit(solution)/shard_map/ppermute | solution.py:258
  33.5 13.2 %collective-permute-start.8 = (bf16[2,256,256]{2,1,0:T(8,128)(2,1)S(1)}, bf16[2,256,256]{2,1,0:T(8,128)(2,1)S(1)}, u32[]{:S(2)}, u32[]{:S(2)}) collective-permute-start(bf16[2,256,256]{2,1,0:T(8,128)(2,1)S(1)} %shard_map.79), channel_id=1, source_target_pairs={{0,1},{1,0},{2,3},{3,2},{4,5},{5,4},{6,7},{7,6},{8,9},{9,8},{10,11... | collective-permute-start | bytes 786440 | tf_op jit(solution)/shard_map/ppermute | solution.py:258
  39.1 4.0 %collective-permute-start.9 = (f32[8,128]{1,0:T(8,128)S(1)}, f32[8,128]{1,0:T(8,128)S(1)}, u32[]{:S(2)}, u32[]{:S(2)}) collective-permute-start(f32[8,128]{1,0:T(8,128)S(1)} %add.6), channel_id=1, source_target_pairs={{0,8},{4,12},{8,0},{12,4},{16,24},{20,28},{24,16},{28,20},{1,9},{5... | collective-permute-start | bytes 12296 | tf_op jit(solution)/shard_map/ppermute | solution.py:258
  43.1 3.6 %collective-permute-start.10 = (f32[8,128]{1,0:T(8,128)S(1)}, f32[8,128]{1,0:T(8,128)S(1)}, u32[]{:S(2)}, u32[]{:S(2)}) collective-permute-start(f32[8,128]{1,0:T(8,128)S(1)} %add.7.mine_ref), channel_id=1, source_target_pairs={{0,16},{4,20},{8,24},{12,28},{16,0},{20,4},{24,8},{28,12},{1,17},{... | collective-permute-start | bytes 12296 | tf_op jit(solution)/shard_map/ppermute | solution.py:258

commit v7 on v6

--- a/solution.py
+++ b/solution.py
@@ -42,16 +42,14 @@
     return total.astype(jnp.bfloat16)
 
 
-def cut_edges_kernel(prim_ref, edges_ref):
+def cut_kernel(prim_ref, sec_ref, edges_ref, inner_ref, outer_ref):
     rows_n = prim_ref.shape[1]
     edges_ref[:, :LAG] = prim_ref[:, :LAG]
     edges_ref[:, LAG:] = prim_ref[:, rows_n - LAG :]
-
-
-def cut_halo_kernel(sec_ref, down_ref, up_ref):
-    rows_n = sec_ref.shape[2]
-    down_ref[...] = sec_ref[0, :, rows_n - HALO :]
-    up_ref[...] = sec_ref[0, :, :HALO]
+    first = lax.rem(lax.axis_index("tile"), 2) == 0
+    down, up = sec_ref[0, :, rows_n - HALO :], sec_ref[0, :, :HALO]
+    inner_ref[...] = jnp.where(first, down, up)
+    outer_ref[...] = jnp.where(first, up, down)
 
 
 def cut_middle_kernel(prim_ref, *refs):
@@ -64,20 +62,21 @@
     out_ref[...] = block_ref[:, : out_ref.shape[1]]
 
 
-def resample_kernel(sec_ref, low_ref, high_ref, ao_ref, ro_ref, af_ref, rf_ref, out_ref, azim_ref):
+def resample_kernel(sec_ref, inner_ref, outer_ref, ao_ref, ro_ref, af_ref, rf_ref, out_ref, azim_ref):
     rows_n, cols_n = sec_ref.shape[2:]
     span = BAND + 2 * HALO
     shape = (BAND, span)
     offset = lax.broadcasted_iota(jnp.int32, shape, 1) - lax.broadcasted_iota(jnp.int32, shape, 0)
     az_band = band(shape, offset - HALO - ao_ref[...], tap_rows(af_ref[...]))
+    first = lax.rem(lax.axis_index("tile"), 2) == 0
     for part in range(2):
         for start in range(0, rows_n, BAND):
             pieces = []
             if start == 0:
-                pieces.append(low_ref[part])
+                pieces.append(jnp.where(first, outer_ref[part], inner_ref[part]))
             pieces.append(sec_ref[0, part, max(0, start - HALO) : min(rows_n, start + BAND + HALO)])
             if start + BAND == rows_n:
-                pieces.append(high_ref[part])
+                pieces.append(jnp.where(first, inner_ref[part], outer_ref[part]))
             rows = jnp.concatenate(pieces, axis=0) if len(pieces) > 1 else pieces[0]
             azim_ref[part, start : start + BAND] = jnp.dot(
                 az_band, rows, preferred_element_type=jnp.float32
@@ -267,21 +266,27 @@
     shape = jax.ShapeDtypeStruct
     looks_n = cols_n // LR
     middle_n = rows_n - 2 * LAG
-    edges = call(
-        cut_edges_kernel, shape((2, 2 * LAG, width), bf16), [], (0, 16 * LAG * width), primary
-    )
+    halo = shape((2, HALO, cols_n), bf16)
+    edges, inner, outer = call(
+        cut_kernel,
+        (shape((2, 2 * LAG, width), bf16), halo, halo),
+        [],
+        (0, 0),
+        primary, secondary,
+    )
+    edges_two = swap(edges, "date", 2)
     one = swap(primary, "date", 1)
-    edges_two, edges_three = [swap(edges, "date", step) for step in (2, 3)]
-    halo = shape((2, HALO, cols_n), bf16)
-    down, up = call(cut_halo_kernel, (halo, halo), [], (0, 16 * HALO * cols_n), secondary)
-    low = passed_along(down, "tile", 1)
-    high = passed_along(up, "tile", -1)
+    inner = swap(inner, "tile", 1)
+    outer = lax.ppermute(
+        outer, "tile", [(at, at + 1 if at % 2 else at - 1) for at in range(1, tiles_n - 1)]
+    )
+    edges_three = swap(edges_two, "date", 1)
     middle = call(
         cut_middle_kernel,
         shape((2, middle_n + 16, width), bf16),
         [],
         (0, 0),
-        primary, edges_two,
+        primary, one,
     )
     weight = jnp.broadcast_to(margin_mask[rows_n - LAG :].astype(f32)[:, None], (LAG, LANE))
     res = call(
@@ -289,7 +294,7 @@
         shape((dates_n, 2, rows_n, width), bf16),
         [pltpu.VMEM((2, rows_n, cols_n), bf16)],
         (0, 0),
-        secondary, low, high, az_off, rg_off, az_frac, rg_frac,
+        secondary, inner, outer, az_off, rg_off, az_frac, rg_frac,
     )
     two = swap(middle, "date", 2)
     margin = shape((2, LAG, cols_n), bf16)

time: 48 us -> 42.3 us (0.88)
  starting transfers between devices: 27 us -> 20.4 us
  waiting for transfers between devices: 10.6 us -> 11.6 us
    ppermute x8 -> x9, starting transfers between devices: 23 us -> 18.4 us  [swap(): lax.ppermute(value, axis, [(at, at ^ step) for at in range(lax.axis_size(...]
    ppermute x3 -> x1, starting transfers between devices: 4.01 us -> 1.29 us  [passed_along(): lax.ppermute(value, axis, [(source, source + steps) for source in range(i...]
    ppermute x8 -> x9, waiting for transfers between devices: 9.21 us -> 10.2 us  [swap(): lax.ppermute(value, axis, [(at, at ^ step) for at in range(lax.axis_size(...]
    ppermute x0 -> x1, starting transfers between devices: none -> 0.66 us  [fused(): lax.ppermute(outer, 'tile', [(at, at + 1 if at % 2 else at - 1) for at in...]
    ppermute x3 -> x1, waiting for transfers between devices: 1.38 us -> 1.37 us  [passed_along(): lax.ppermute(value, axis, [(source, source + steps) for source in range(i...]
    pallas_call x9 -> x8, Pallas kernels: 4.11 us -> 4.1 us  [call(): pl.pallas_call(kernel, out_shape=outs, in_specs=[vmem] * len(args), out_s...]
  transfers between devices with their start and end apart: 11 -> 11, of which waited for: 5 -> 6; matrix products, arithmetic and copies ran while one was open for 2% -> 2% of each run, Pallas kernels for 7% -> 7%
where the time goes in v7:
time: 42.3 us; the launch traced here: 42 us
  starting transfers between devices  20.4 us (48%)
  waiting for transfers between devices  11.6 us (27%)
  Pallas kernels  4.1 us (10%)
  between operations  2.7 us (6%)
  local copies, waits for them, and re-layouts  2.48 us (6%)
  other arithmetic  0.76 us (2%)
    ppermute x9, starting transfers between devices, swap(): lax.ppermute(value, axis, [(at, at ^ step) for at in range(lax.axis_size(...  18.4 us
    ppermute x9, waiting for transfers between devices, swap(): lax.ppermute(value, axis, [(at, at ^ step) for at in range(lax.axis_size(...  10.2 us
    pallas_call x8, Pallas kernels, call(): pl.pallas_call(kernel, out_shape=outs, in_specs=[vmem] * len(args), out_s...  4.1 us
    unnamed x8, local copies, waits for them, and re-layouts  2.41 us
    ppermute x1, waiting for transfers between devices, passed_along(): lax.ppermute(value, axis, [(source, source + steps) for source in range(i...  1.37 us
    ppermute x1, starting transfers between devices, passed_along(): lax.ppermute(value, axis, [(source, source + steps) for source in range(i...  1.29 us
  transfers between devices with their start and end apart: 11, of which 6 were waited for; matrix products, arithmetic and copies ran while one was open for 2% of the time, Pallas kernels for 7%

profile of v7, /device:TPU:0, one launch (start us, length us, event | category | flops | bytes accessed | tf_op | source)
XLA Modules:
  0.0 42.0 jit_solution(864000485910951040)
XLA Ops:
  0.0 3.0 %collective-permute-start = (bf16[2,384,256]{2,1,0:T(8,128)(2,1)}, bf16[2,384,256]{2,1,0:T(8,128)(2,1)S(1)}, u32[]{:S(2)}, u32[]{:S(2)}) collective-permute-start(bf16[2,384,256]{2,1,0:T(8,128)(2,1)} %own_ref.3), channel_id=1, source_target_pairs={{0,1},{1,0},{2,3},{3,2},{4,5},{5,4},{6,7},{7,6},{8,9},{9,8},{10,11... | collective-permute-start | bytes 1179656 | tf_op jit(solution)/shard_map/ppermute | solution.py:257
  3.0 1.4 %copy-done = bf16[1,2,384,1024]{3,2,1,0:T(8,128)(2,1)S(1)} copy-done((bf16[1,2,384,1024]{3,2,1,0:T(8,128)(2,1)S(1)}, bf16[1,2,384,1024]{3,2,1,0:T(8,128)(2,1)}, u32[]{:S(2)}) %copy-start) | copy-done | bytes 1572888
  4.4 1.0 %copy-done.2 = bf16[2,384,256]{2,1,0:T(8,128)(2,1)S(1)} copy-done((bf16[2,384,256]{2,1,0:T(8,128)(2,1)S(1)}, bf16[2,384,256]{2,1,0:T(8,128)(2,1)}, u32[]{:S(2)}) %copy-start.2) | copy-done | bytes 393240
  5.5 2.7 %collective-permute-start.2 = (bf16[2,128,256]{2,1,0:T(8,128)(2,1)S(1)}, bf16[2,128,256]{2,1,0:T(8,128)(2,1)S(1)}, u32[]{:S(2)}, u32[]{:S(2)}) collective-permute-start(bf16[2,128,256]{2,1,0:T(8,128)(2,1)S(1)} %get-tuple-element.11), channel_id=1, source_target_pairs={{0,2},{1,3},{2,0},{3,1},{4,6},{5,7},{6,4},{7,5},{8,10},{9,11},{10,... | collective-permute-start | bytes 393224 | tf_op jit(solution)/shard_map/ppermute | solution.py:257
  8.1 0.0 collective-permute-start.4
  8.1 0.7 %collective-permute-start.5 = (bf16[2,32,1024]{2,1,0:T(8,128)(2,1)S(1)}, bf16[2,32,1024]{2,1,0:T(8,128)(2,1)S(1)}, u32[]{:S(2)}, u32[]{:S(2)}) collective-permute-start(bf16[2,32,1024]{2,1,0:T(8,128)(2,1)S(1)} %get-tuple-element.13), channel_id=1, source_target_pairs={{4,8},{8,4},{12,16},{16,12},{20,24},{24,20},{5,9},{9,5},{13,17},{1... | collective-permute-start | bytes 393224 | tf_op jit(solution)/shard_map/ppermute | solution.py:280
  8.8 5.6 %collective-permute-done.2.two_ref = bf16[2,128,256]{2,1,0:T(8,128)(2,1)S(1)} collective-permute-done((bf16[2,128,256]{2,1,0:T(8,128)(2,1)S(1)}, bf16[2,128,256]{2,1,0:T(8,128)(2,1)S(1)}, u32[]{:S(2)}, u32[]{:S(2)}) %collective-permute-start.2) | collective-permute-done | bytes 131104 | tf_op jit(solution)/shard_map/ppermute | solution.py:257
  14.4 3.5 %collective-permute-start.3 = (bf16[2,128,256]{2,1,0:T(8,128)(2,1)S(1)}, bf16[2,128,256]{2,1,0:T(8,128)(2,1)S(1)}, u32[]{:S(2)}, u32[]{:S(2)}) collective-permute-start(bf16[2,128,256]{2,1,0:T(8,128)(2,1)S(1)} %collective-permute-done.2.two_ref), channel_id=1, source_target_pairs={{0,1},{1,0},{2,3},{3,2},{4,5},{5,4},{6,7},{7,6},{8,9},{9,8},{10,11... | collective-permute-start | bytes 393224 | tf_op jit(solution)/shard_map/ppermute | solution.py:257
  17.9 0.0 collective-permute-done.refs_0_.one_ref
  17.9 0.1 collective-permute-start.1
  20.6 0.0 collective-permute-done.4.inner_ref
  20.6 0.0 collective-permute-done.5.outer_ref
  20.6 1.6 %shard_map.75.res_ref = bf16[4,2,384,256]{3,2,1,0:T(8,128)(2,1)S(1)} custom-call(bf16[1,2,384,1024]{3,2,1,0:T(8,128)(2,1)S(1)} %copy-done.1, bf16[2,32,1024]{2,1,0:T(8,128)(2,1)S(1)} %collective-permute-done.4.inner_ref, bf16[2,32,1024]{2,1,0:T(8,128)(2,1)S(1)} %collective-permute-done.5.outer_ref, s32[1,1]{1,0:T(1,128)S(6)} %copy.8.ao_ref, ...), custom_call_target="tpu_custom_call" | custom-call | tf_op jit(solution)/shard_map/pallas_call | solution.py:245
  22.3 0.0 copy-start.3
  22.3 0.0 collective-permute-done.3.three_ref
  22.3 0.5 %shard_map.76 = (bf16[2,64,1024]{2,1,0:T(8,128)(2,1)S(1)}, bf16[2,64,1024]{2,1,0:T(8,128)(2,1)S(1)}, f32[2,64,128]{2,1,0:T(8,128)S(1)}) custom-call(bf16[2,384,256]{2,1,0:T(8,128)(2,1)S(1)} %copy-done.2, bf16[2,384,256]{2,1,0:T(8,128)(2,1)S(1)} %collective-permute-done.refs_0_.one_ref, bf16[2,128,256]{2,1,0:T(8,128)(2,1)S(1)} %collective-permute-done.2.two_ref, ...), custom_call_target="tpu_custom_call" | custom-call | tf_op jit(solution)/shard_map/pallas_call | solution.py:245
  22.8 1.3 %collective-permute-start.6 = (bf16[2,64,1024]{2,1,0:T(8,128)(2,1)S(1)}, bf16[2,64,1024]{2,1,0:T(8,128)(2,1)S(1)}, u32[]{:S(2)}, u32[]{:S(2)}) collective-permute-start(bf16[2,64,1024]{2,1,0:T(8,128)(2,1)S(1)} %get-tuple-element.15), channel_id=1, source_target_pairs={{4,0},{8,4},{12,8},{16,12},{20,16},{24,20},{28,24},{5,1},{9,5},{13... | collective-permute-start | bytes 786440 | tf_op jit(solution)/shard_map/ppermute | solution.py:23
  24.1 0.8 %slice_convert_fusion = f32[64]{0:T(128)S(1)} fusion(s32[384]{0:T(512)} %param.9), kind=kLoop, calls=%fused_computation | loop fusion | flops 64 | bytes 512 | tf_op jit(solution)/shard_map/convert_element_type | solution.py:291
  24.9 1.4 %collective-permute-done.6.later_ref = bf16[2,64,1024]{2,1,0:T(8,128)(2,1)S(1)} collective-permute-done((bf16[2,64,1024]{2,1,0:T(8,128)(2,1)S(1)}, bf16[2,64,1024]{2,1,0:T(8,128)(2,1)S(1)}, u32[]{:S(2)}, u32[]{:S(2)}) %collective-permute-start.6) | collective-permute-done | bytes 262176 | tf_op jit(solution)/shard_map/ppermute | solution.py:23
  26.2 0.1 broadcast_in_dim.2.weight_ref
  26.3 0.3 shard_map.77
  26.7 4.5 %collective-permute-start.7 = (f32[8,128]{1,0:T(8,128)S(1)}, f32[8,128]{1,0:T(8,128)S(1)}, u32[]{:S(2)}, u32[]{:S(2)}) collective-permute-start(f32[8,128]{1,0:T(8,128)S(1)} %shard_map.77), channel_id=1, source_target_pairs={{0,4},{4,0},{8,12},{12,8},{16,20},{20,16},{24,28},{28,24},{1,5},{5... | collective-permute-start | bytes 12296 | tf_op jit(solution)/shard_map/ppermute | solution.py:257
  31.1 0.8 %collective-permute-done.7.stats_ref = f32[8,128]{1,0:T(8,128)S(1)} collective-permute-done((f32[8,128]{1,0:T(8,128)S(1)}, f32[8,128]{1,0:T(8,128)S(1)}, u32[]{:S(2)}, u32[]{:S(2)}) %collective-permute-start.7) | collective-permute-done | bytes 4128 | tf_op jit(solution)/shard_map/ppermute | solution.py:257
  32.0 0.2 collective-permute-done.1.block_ref.two_ref
  32.1 1.7 %collective-permute-start.8 = (bf16[2,256,256]{2,1,0:T(8,128)(2,1)S(1)}, bf16[2,256,256]{2,1,0:T(8,128)(2,1)S(1)}, u32[]{:S(2)}, u32[]{:S(2)}) collective-permute-start(bf16[2,256,256]{2,1,0:T(8,128)(2,1)S(1)} %shard_map.78), channel_id=1, source_target_pairs={{0,1},{1,0},{2,3},{3,2},{4,5},{5,4},{6,7},{7,6},{8,9},{9,8},{10,11... | collective-permute-start | bytes 786440 | tf_op jit(solution)/shard_map/ppermute | solution.py:257
  33.8 1.5 %collective-permute-start.9 = (f32[8,128]{1,0:T(8,128)S(1)}, f32[8,128]{1,0:T(8,128)S(1)}, u32[]{:S(2)}, u32[]{:S(2)}) collective-permute-start(f32[8,128]{1,0:T(8,128)S(1)} %add.6), channel_id=1, source_target_pairs={{0,8},{4,12},{8,0},{12,4},{16,24},{20,28},{24,16},{28,20},{1,9},{5... | collective-permute-start | bytes 12296 | tf_op jit(solution)/shard_map/ppermute | solution.py:257
  35.3 2.1 %collective-permute-done.9 = f32[8,128]{1,0:T(8,128)S(1)} collective-permute-done((f32[8,128]{1,0:T(8,128)S(1)}, f32[8,128]{1,0:T(8,128)S(1)}, u32[]{:S(2)}, u32[]{:S(2)}) %collective-permute-start.9) | collective-permute-done | bytes 4128 | tf_op jit(solution)/shard_map/ppermute | solution.py:257
  37.4 1.5 %collective-permute-start.10 = (f32[8,128]{1,0:T(8,128)S(1)}, f32[8,128]{1,0:T(8,128)S(1)}, u32[]{:S(2)}, u32[]{:S(2)}) collective-permute-start(f32[8,128]{1,0:T(8,128)S(1)} %add.7.mine_ref), channel_id=1, source_target_pairs={{0,16},{4,20},{8,24},{12,28},{16,0},{20,4},{24,8},{28,12},{1,17},{... | collective-permute-start | bytes 12296 | tf_op jit(solution)/shard_map/ppermute | solution.py:257
  39.0 0.6 %shard_map.79.before_ref = f32[2,256,128]{2,1,0:T(8,128)S(1)} custom-call(bf16[2,384,256]{2,1,0:T(8,128)(2,1)S(1)} %copy-done.3, bf16[2,384,256]{2,1,0:T(8,128)(2,1)S(1)} %collective-permute-done.refs_0_.one_ref, bf16[2,272,256]{2,1,0:T(8,128)(2,1)S(1)} %collective-permute-done.1.block_ref.two_ref, bf16[4,2,384,256]{3,2,1,0:T(8,128)(2,1)S(1)} %shard_map.75.res_ref), custom_call_target="tpu_custom_call" | custom-call | flops 134217728 | bytes 3145728 | tf_op jit(solution)/shard_map/pallas_call | solution.py:245
  39.6 1.5 %collective-permute-done.10.other_ref = f32[8,128]{1,0:T(8,128)S(1)} collective-permute-done((f32[8,128]{1,0:T(8,128)S(1)}, f32[8,128]{1,0:T(8,128)S(1)}, u32[]{:S(2)}, u32[]{:S(2)}) %collective-permute-start.10) | collective-permute-done | bytes 4128 | tf_op jit(solution)/shard_map/ppermute | solution.py:257
  41.1 0.0 collective-permute-done.8.three_ref
  41.1 1.0 %shard_map.80 = f32[1,2,192,128]{3,2,1,0:T(8,128)} custom-call(bf16[2,256,256]{2,1,0:T(8,128)(2,1)S(1)} %collective-permute-done.8.three_ref, bf16[4,2,384,256]{3,2,1,0:T(8,128)(2,1)S(1)} %shard_map.75.res_ref, f32[2,256,128]{2,1,0:T(8,128)S(1)} %shard_map.79.before_ref, f32[2,64,128]{2,1,0:T(8,128)S(1)} %get-tuple-element.16.looks_ref, ...), custom_call_target="tpu_custom_call" | custom-call | flops 67108864 | bytes 1572864 | tf_op jit(solution)/shard_map/pallas_call | solution.py:245
  (10 shorter events, 0.1 us)
Async XLA Ops:
  0.0 17.9 %collective-permute-start = (bf16[2,384,256]{2,1,0:T(8,128)(2,1)}, bf16[2,384,256]{2,1,0:T(8,128)(2,1)S(1)}, u32[]{:S(2)}, u32[]{:S(2)}) collective-permute-start(bf16[2,384,256]{2,1,0:T(8,128)(2,1)} %own_ref.3), channel_id=1, source_target_pairs={{0,1},{1,0},{2,3},{3,2},{4,5},{5,4},{6,7},{7,6},{8,9},{9,8},{10,11... | collective-permute-start | bytes 1179656 | tf_op jit(solution)/shard_map/ppermute | solution.py:257
  3.0 1.4 %copy-start = (bf16[1,2,384,1024]{3,2,1,0:T(8,128)(2,1)S(1)}, bf16[1,2,384,1024]{3,2,1,0:T(8,128)(2,1)}, u32[]{:S(2)}) copy-start(bf16[1,2,384,1024]{3,2,1,0:T(8,128)(2,1)} %sec_ref.3) | copy-start | bytes 4718596
  4.4 1.0 %copy-start.2 = (bf16[2,384,256]{2,1,0:T(8,128)(2,1)S(1)}, bf16[2,384,256]{2,1,0:T(8,128)(2,1)}, u32[]{:S(2)}) copy-start(bf16[2,384,256]{2,1,0:T(8,128)(2,1)} %own_ref.3) | copy-start | bytes 1179652
  5.4 15.2 %copy-start.1 = (bf16[1,2,384,1024]{3,2,1,0:T(8,128)(2,1)S(1)}, bf16[1,2,384,1024]{3,2,1,0:T(8,128)(2,1)}, u32[]{:S(2)}) copy-start(bf16[1,2,384,1024]{3,2,1,0:T(8,128)(2,1)} %sec_ref.3) | copy-start | bytes 4718596
  5.5 8.9 %collective-permute-start.2 = (bf16[2,128,256]{2,1,0:T(8,128)(2,1)S(1)}, bf16[2,128,256]{2,1,0:T(8,128)(2,1)S(1)}, u32[]{:S(2)}, u32[]{:S(2)}) collective-permute-start(bf16[2,128,256]{2,1,0:T(8,128)(2,1)S(1)} %get-tuple-element.11), channel_id=1, source_target_pairs={{0,2},{1,3},{2,0},{3,1},{4,6},{5,7},{6,4},{7,5},{8,10},{9,11},{10,... | collective-permute-start | bytes 393224 | tf_op jit(solution)/shard_map/ppermute | solution.py:257
  8.1 12.5 %collective-permute-start.4 = (bf16[2,32,1024]{2,1,0:T(8,128)(2,1)S(1)}, bf16[2,32,1024]{2,1,0:T(8,128)(2,1)S(1)}, u32[]{:S(2)}, u32[]{:S(2)}) collective-permute-start(bf16[2,32,1024]{2,1,0:T(8,128)(2,1)S(1)} %get-tuple-element.12), channel_id=1, source_target_pairs={{0,4},{4,0},{8,12},{12,8},{16,20},{20,16},{24,28},{28,24},{1,5},{5... | collective-permute-start | bytes 393224 | tf_op jit(solution)/shard_map/ppermute | solution.py:257
  8.1 12.5 %collective-permute-start.5 = (bf16[2,32,1024]{2,1,0:T(8,128)(2,1)S(1)}, bf16[2,32,1024]{2,1,0:T(8,128)(2,1)S(1)}, u32[]{:S(2)}, u32[]{:S(2)}) collective-permute-start(bf16[2,32,1024]{2,1,0:T(8,128)(2,1)S(1)} %get-tuple-element.13), channel_id=1, source_target_pairs={{4,8},{8,4},{12,16},{16,12},{20,24},{24,20},{5,9},{9,5},{13,17},{1... | collective-permute-start | bytes 393224 | tf_op jit(solution)/shard_map/ppermute | solution.py:280
  14.4 7.9 %collective-permute-start.3 = (bf16[2,128,256]{2,1,0:T(8,128)(2,1)S(1)}, bf16[2,128,256]{2,1,0:T(8,128)(2,1)S(1)}, u32[]{:S(2)}, u32[]{:S(2)}) collective-permute-start(bf16[2,128,256]{2,1,0:T(8,128)(2,1)S(1)} %collective-permute-done.2.two_ref), channel_id=1, source_target_pairs={{0,1},{1,0},{2,3},{3,2},{4,5},{5,4},{6,7},{7,6},{8,9},{9,8},{10,11... | collective-permute-start | bytes 393224 | tf_op jit(solution)/shard_map/ppermute | solution.py:257
  17.9 14.2 %collective-permute-start.1 = (bf16[2,272,256]{2,1,0:T(8,128)(2,1)S(1)}, bf16[2,272,256]{2,1,0:T(8,128)(2,1)S(1)}, u32[]{:S(2)}, u32[]{:S(2)}) collective-permute-start(bf16[2,272,256]{2,1,0:T(8,128)(2,1)S(1)} %shard_map.73), channel_id=1, source_target_pairs={{0,2},{1,3},{2,0},{3,1},{4,6},{5,7},{6,4},{7,5},{8,10},{9,11},{10,... | collective-permute-start | bytes 835592 | tf_op jit(solution)/shard_map/ppermute | solution.py:257
  22.3 16.7 %copy-start.3 = (bf16[2,384,256]{2,1,0:T(8,128)(2,1)S(1)}, bf16[2,384,256]{2,1,0:T(8,128)(2,1)}, u32[]{:S(2)}) copy-start(bf16[2,384,256]{2,1,0:T(8,128)(2,1)} %own_ref.3) | copy-start | bytes 1179652
  22.8 3.4 %collective-permute-start.6 = (bf16[2,64,1024]{2,1,0:T(8,128)(2,1)S(1)}, bf16[2,64,1024]{2,1,0:T(8,128)(2,1)S(1)}, u32[]{:S(2)}, u32[]{:S(2)}) collective-permute-start(bf16[2,64,1024]{2,1,0:T(8,128)(2,1)S(1)} %get-tuple-element.15), channel_id=1, source_target_pairs={{4,0},{8,4},{12,8},{16,12},{20,16},{24,20},{28,24},{5,1},{9,5},{13... | collective-permute-start | bytes 786440 | tf_op jit(solution)/shard_map/ppermute | solution.py:23
  26.7 5.3 %collective-permute-start.7 = (f32[8,128]{1,0:T(8,128)S(1)}, f32[8,128]{1,0:T(8,128)S(1)}, u32[]{:S(2)}, u32[]{:S(2)}) collective-permute-start(f32[8,128]{1,0:T(8,128)S(1)} %shard_map.77), channel_id=1, source_target_pairs={{0,4},{4,0},{8,12},{12,8},{16,20},{20,16},{24,28},{28,24},{1,5},{5... | collective-permute-start | bytes 12296 | tf_op jit(solution)/shard_map/ppermute | solution.py:257
  32.1 8.9 %collective-permute-start.8 = (bf16[2,256,256]{2,1,0:T(8,128)(2,1)S(1)}, bf16[2,256,256]{2,1,0:T(8,128)(2,1)S(1)}, u32[]{:S(2)}, u32[]{:S(2)}) collective-permute-start(bf16[2,256,256]{2,1,0:T(8,128)(2,1)S(1)} %shard_map.78), channel_id=1, source_target_pairs={{0,1},{1,0},{2,3},{3,2},{4,5},{5,4},{6,7},{7,6},{8,9},{9,8},{10,11... | collective-permute-start | bytes 786440 | tf_op jit(solution)/shard_map/ppermute | solution.py:257
  33.8 3.6 %collective-permute-start.9 = (f32[8,128]{1,0:T(8,128)S(1)}, f32[8,128]{1,0:T(8,128)S(1)}, u32[]{:S(2)}, u32[]{:S(2)}) collective-permute-start(f32[8,128]{1,0:T(8,128)S(1)} %add.6), channel_id=1, source_target_pairs={{0,8},{4,12},{8,0},{12,4},{16,24},{20,28},{24,16},{28,20},{1,9},{5... | collective-permute-start | bytes 12296 | tf_op jit(solution)/shard_map/ppermute | solution.py:257
  37.4 3.6 %collective-permute-start.10 = (f32[8,128]{1,0:T(8,128)S(1)}, f32[8,128]{1,0:T(8,128)S(1)}, u32[]{:S(2)}, u32[]{:S(2)}) collective-permute-start(f32[8,128]{1,0:T(8,128)S(1)} %add.7.mine_ref), channel_id=1, source_target_pairs={{0,16},{4,20},{8,24},{12,28},{16,0},{20,4},{24,8},{28,12},{1,17},{... | collective-permute-start | bytes 12296 | tf_op jit(solution)/shard_map/ppermute | solution.py:257

commit v8 on v7

--- a/solution.py
+++ b/solution.py
@@ -42,10 +42,8 @@
     return total.astype(jnp.bfloat16)
 
 
-def cut_kernel(prim_ref, sec_ref, edges_ref, inner_ref, outer_ref):
-    rows_n = prim_ref.shape[1]
-    edges_ref[:, :LAG] = prim_ref[:, :LAG]
-    edges_ref[:, LAG:] = prim_ref[:, rows_n - LAG :]
+def cut_halo_kernel(sec_ref, inner_ref, outer_ref):
+    rows_n = sec_ref.shape[2]
     first = lax.rem(lax.axis_index("tile"), 2) == 0
     down, up = sec_ref[0, :, rows_n - HALO :], sec_ref[0, :, :HALO]
     inner_ref[...] = jnp.where(first, down, up)
@@ -57,17 +55,25 @@
     cut_ref[...] = prim_ref[:, LAG : LAG + cut_ref.shape[1]]
 
 
-def relay_kernel(block_ref, stats_ref, out_ref):
-    del stats_ref
+def relay_kernel(block_ref, awaited_ref, out_ref):
+    del awaited_ref
     out_ref[...] = block_ref[:, : out_ref.shape[1]]
 
 
-def resample_kernel(sec_ref, inner_ref, outer_ref, ao_ref, ro_ref, af_ref, rf_ref, out_ref, azim_ref):
+def bands_kernel(ao_ref, ro_ref, af_ref, rf_ref, az_ref, rg_ref):
+    shape = az_ref.shape
+    offset = lax.broadcasted_iota(jnp.int32, shape, 1) - lax.broadcasted_iota(jnp.int32, shape, 0)
+    az_ref[...] = band(shape, offset - HALO - ao_ref[...], tap_rows(af_ref[...]))
+    square = rg_ref.shape[1:]
+    offset = lax.broadcasted_iota(jnp.int32, square, 0) - lax.broadcasted_iota(jnp.int32, square, 1)
+    taps = tap_rows(rf_ref[...])
+    for at, shift in enumerate((-LANE, 0, LANE)):
+        rg_ref[at] = band(square, offset + shift - ro_ref[...], taps)
+
+
+def resample_kernel(sec_ref, inner_ref, outer_ref, az_ref, rg_ref, out_ref, azim_ref):
     rows_n, cols_n = sec_ref.shape[2:]
-    span = BAND + 2 * HALO
-    shape = (BAND, span)
-    offset = lax.broadcasted_iota(jnp.int32, shape, 1) - lax.broadcasted_iota(jnp.int32, shape, 0)
-    az_band = band(shape, offset - HALO - ao_ref[...], tap_rows(af_ref[...]))
+    az_band = az_ref[...]
     first = lax.rem(lax.axis_index("tile"), 2) == 0
     for part in range(2):
         for start in range(0, rows_n, BAND):
@@ -82,13 +88,8 @@
                 az_band, rows, preferred_element_type=jnp.float32
             ).astype(jnp.bfloat16)
 
-    square = (LANE, LANE)
-    offset = lax.broadcasted_iota(jnp.int32, square, 0) - lax.broadcasted_iota(jnp.int32, square, 1)
-    taps = tap_rows(rf_ref[...])
-    before, same, after = [
-        band(square, offset + shift - ro_ref[...], taps) for shift in (-LANE, 0, LANE)
-    ]
-    none = jnp.zeros(square, jnp.bfloat16)
+    before, same, after = [rg_ref[at] for at in range(3)]
+    none = jnp.zeros((LANE, LANE), jnp.bfloat16)
     blocks_n, _, _, width = out_ref.shape
     lanes_n = width // LANE
     columns = []
@@ -214,13 +215,18 @@
         out_ref[part] = total
 
 
-def finish_kernel(
-    three_ref, res_ref, before_ref, looks_ref, mine_ref, other_ref, out_ref, sums_ref
-):
-    looks_n = out_ref.shape[3]
+def last_kernel(three_ref, res_ref, before_ref, looks_ref, out_ref, sums_ref):
     middle_n = before_ref.shape[1]
-    totals = look_sums(((3, three_ref),), res_ref, looks_n)
-    totals = [total + before_ref[part] for part, total in enumerate(totals)]
+    edge = LAG // LA
+    totals = look_sums(((3, three_ref),), res_ref, out_ref.shape[2])
+    for part, total in enumerate(totals):
+        sums_ref[part] = total + before_ref[part]
+        out_ref[part, :edge] = looks_ref[part, :edge]
+        out_ref[part, edge : edge + middle_n // LA] = look_rows(sums_ref, part, 0, middle_n)
+        out_ref[part, edge + middle_n // LA :] = looks_ref[part, edge:]
+
+
+def scale_kernel(looks_ref, mine_ref, other_ref, out_ref):
     stats = jnp.sum(mine_ref[...] + other_ref[...], axis=1, keepdims=True)
     e_re, e_im, power, count = [stats[row : row + 1] for row in range(4)]
     magnitude = jnp.sqrt(e_re * e_re + e_im * e_im)
@@ -228,16 +234,8 @@
     denom = jnp.maximum(magnitude, floor_val)
     u_re = e_re / denom * (1.0 / (LA * LR))
     u_im = e_im / denom * (1.0 / (LA * LR))
-    edge = LAG // LA
-    for part in range(2):
-        sums_ref[part] = totals[part]
-    for out_at, held, rows in (
-        (0, looks_ref[:, :edge], edge),
-        (edge, [look_rows(sums_ref, part, 0, middle_n) for part in range(2)], middle_n // LA),
-        (edge + middle_n // LA, looks_ref[:, edge:], edge),
-    ):
-        out_ref[0, 0, out_at : out_at + rows] = held[0] * u_re + held[1] * u_im
-        out_ref[0, 1, out_at : out_at + rows] = held[1] * u_re - held[0] * u_im
+    out_ref[0, 0] = looks_ref[0] * u_re + looks_ref[1] * u_im
+    out_ref[0, 1] = looks_ref[1] * u_re - looks_ref[0] * u_im
 
 
 def call(kernel, outs, scratch, cost, *args):
@@ -266,27 +264,29 @@
     shape = jax.ShapeDtypeStruct
     looks_n = cols_n // LR
     middle_n = rows_n - 2 * LAG
+    edges = jnp.concatenate([primary[:, :LAG], primary[:, rows_n - LAG :]], axis=1)
+    edges_two = swap(edges, "date", 2)
+    one = swap(primary, "date", 1)
     halo = shape((2, HALO, cols_n), bf16)
-    edges, inner, outer = call(
-        cut_kernel,
-        (shape((2, 2 * LAG, width), bf16), halo, halo),
+    inner, outer = call(cut_halo_kernel, (halo, halo), [], (0, 0), secondary)
+    inner = swap(inner, "tile", 1)
+    beyond = [(at, at + 1 if at % 2 else at - 1) for at in range(1, tiles_n - 1)]
+    outer = lax.ppermute(outer, "tile", beyond)
+    az_band, rg_band = call(
+        bands_kernel,
+        (shape((BAND, BAND + 2 * HALO), bf16), shape((3, LANE, LANE), bf16)),
         [],
         (0, 0),
-        primary, secondary,
-    )
-    edges_two = swap(edges, "date", 2)
-    one = swap(primary, "date", 1)
-    inner = swap(inner, "tile", 1)
-    outer = lax.ppermute(
-        outer, "tile", [(at, at + 1 if at % 2 else at - 1) for at in range(1, tiles_n - 1)]
-    )
-    edges_three = swap(edges_two, "date", 1)
+        az_off, rg_off, az_frac, rg_frac,
+    )
+    relayed = call(relay_kernel, edges, [], (0, 0), edges_two, az_band)
+    edges_three = swap(relayed, "date", 1)
     middle = call(
         cut_middle_kernel,
         shape((2, middle_n + 16, width), bf16),
         [],
         (0, 0),
-        primary, one,
+        primary, inner,outer,
     )
     weight = jnp.broadcast_to(margin_mask[rows_n - LAG :].astype(f32)[:, None], (LAG, LANE))
     res = call(
@@ -294,7 +294,7 @@
         shape((dates_n, 2, rows_n, width), bf16),
         [pltpu.VMEM((2, rows_n, cols_n), bf16)],
         (0, 0),
-        secondary, inner, outer, az_off, rg_off, az_frac, rg_frac,
+        secondary, inner, outer, az_band, rg_band,
     )
     two = swap(middle, "date", 2)
     margin = shape((2, LAG, cols_n), bf16)
@@ -329,12 +329,19 @@
         stats = stats + other
         other = swap(stats, "tile", stride)
         stride *= 2
-    return call(
-        finish_kernel,
-        shape((1, 2, rows_n // LA, looks_n), f32),
+    looks = call(
+        last_kernel,
+        shape((2, rows_n // LA, looks_n), f32),
         [pltpu.VMEM((2, middle_n, looks_n), f32)],
         (2 * middle_n * cols_n * looks_n, 4 * rows_n * cols_n),
-        three, res, before, looks, stats, other,
+        three, res, before, looks,
+    )
+    return call(
+        scale_kernel,
+        shape((1, 2, rows_n // LA, looks_n), f32),
+        [],
+        (8 * rows_n * looks_n, 8 * rows_n * looks_n),
+        looks, stats, other,
     )
 
 

time: 42.3 us -> 42.3 us (level)
  waiting for transfers between devices: 11.6 us -> 11.1 us
    unnamed x8 -> x6, local copies, waits for them, and re-layouts: 2.41 us -> 1.41 us
    slice x0 -> x1, local copies, waits for them, and re-layouts: none -> 0.88 us  [fused(): primary[:, :LAG]]
    ppermute x9, waiting for transfers between devices: 10.2 us -> 9.7 us  [swap(): lax.ppermute(value, axis, [(at, at ^ step) for at in range(lax.axis_size(...]
    pallas_call x8 -> x11, Pallas kernels: 4.1 us -> 4.4 us  [call(): pl.pallas_call(kernel, out_shape=outs, in_specs=[vmem] * len(args), out_s...]
  transfers between devices with their start and end apart: 11 -> 11, of which waited for: 6 -> 7; matrix products, arithmetic and copies ran while one was open for 2% -> 4% of each run, Pallas kernels for 7% -> 8%
where the time goes in v8:
time: 42.3 us; the launch traced here: 42 us
  starting transfers between devices  20.6 us (49%)
  waiting for transfers between devices  11.1 us (26%)
  Pallas kernels  4.4 us (10%)
  between operations  2.71 us (6%)
  local copies, waits for them, and re-layouts  2.37 us (6%)
  other arithmetic  0.77 us (2%)
    ppermute x9, starting transfers between devices, swap(): lax.ppermute(value, axis, [(at, at ^ step) for at in range(lax.axis_size(...  18.6 us
    ppermute x9, waiting for transfers between devices, swap(): lax.ppermute(value, axis, [(at, at ^ step) for at in range(lax.axis_size(...  9.7 us
    pallas_call x11, Pallas kernels, call(): pl.pallas_call(kernel, out_shape=outs, in_specs=[vmem] * len(args), out_s...  4.4 us
    unnamed x6, local copies, waits for them, and re-layouts  1.41 us
    ppermute x1, waiting for transfers between devices, passed_along(): lax.ppermute(value, axis, [(source, source + steps) for source in range(i...  1.37 us
    ppermute x1, starting transfers between devices, passed_along(): lax.ppermute(value, axis, [(source, source + steps) for source in range(i...  1.29 us
    slice x1, local copies, waits for them, and re-layouts, fused(): primary[:, :LAG]  0.88 us
  transfers between devices with their start and end apart: 11, of which 7 were waited for; matrix products, arithmetic and copies ran while one was open for 4% of the time, Pallas kernels for 8%

profile of v8, /device:TPU:0, one launch (start us, length us, event | category | flops | bytes accessed | tf_op | source)
XLA Modules:
  0.0 42.0 jit_solution(14022761086503204174)
XLA Ops:
  0.0 3.0 %collective-permute-start.3 = (bf16[2,384,256]{2,1,0:T(8,128)(2,1)}, bf16[2,384,256]{2,1,0:T(8,128)(2,1)S(1)}, u32[]{:S(2)}, u32[]{:S(2)}) collective-permute-start(bf16[2,384,256]{2,1,0:T(8,128)(2,1)} %own_ref.3), channel_id=1, source_target_pairs={{0,1},{1,0},{2,3},{3,2},{4,5},{5,4},{6,7},{7,6},{8,9},{9,8},{10,11... | collective-permute-start | bytes 1179656 | tf_op jit(solution)/shard_map/ppermute | solution.py:255
  3.0 0.9 %fusion = (bf16[2,64,256]{2,1,0:T(8,128)(2,1)S(1)}, bf16[2,64,256]{2,1,0:T(8,128)(2,1)S(1)}) fusion(bf16[2,384,256]{2,1,0:T(8,128)(2,1)} %own_ref.3), kind=kLoop, calls=%fused_computation.2 | loop fusion | bytes 262144 | tf_op jit(solution)/shard_map/slice | solution.py:267
  3.9 2.7 %collective-permute-start.4 = (bf16[2,128,256]{2,1,0:T(8,128)(2,1)S(1)}, bf16[2,128,256]{2,1,0:T(8,128)(2,1)S(1)}, u32[]{:S(2)}, u32[]{:S(2)}) collective-permute-start(bf16[2,128,256]{2,1,0:T(8,128)(2,1)S(1)} %pad_maximum_fusion), channel_id=1, source_target_pairs={{0,2},{1,3},{2,0},{3,1},{4,6},{5,7},{6,4},{7,5},{8,10},{9,11},{10,... | collective-permute-start | bytes 393224 | tf_op jit(solution)/shard_map/ppermute | solution.py:255
  6.6 1.4 %copy-done = bf16[1,2,384,1024]{3,2,1,0:T(8,128)(2,1)S(1)} copy-done((bf16[1,2,384,1024]{3,2,1,0:T(8,128)(2,1)S(1)}, bf16[1,2,384,1024]{3,2,1,0:T(8,128)(2,1)}, u32[]{:S(2)}) %copy-start) | copy-done | bytes 1572888
  8.0 0.1 collective-permute-start
  8.1 0.8 %collective-permute-start.1 = (bf16[2,32,1024]{2,1,0:T(8,128)(2,1)S(1)}, bf16[2,32,1024]{2,1,0:T(8,128)(2,1)S(1)}, u32[]{:S(2)}, u32[]{:S(2)}) collective-permute-start(bf16[2,32,1024]{2,1,0:T(8,128)(2,1)S(1)} %get-tuple-element.13), channel_id=1, source_target_pairs={{4,8},{8,4},{12,16},{16,12},{20,24},{24,20},{5,9},{9,5},{13,17},{1... | collective-permute-start | bytes 393224 | tf_op jit(solution)/shard_map/ppermute | solution.py:274
  11.5 0.4 shard_map.75
  11.9 2.5 %collective-permute-done.4.block_ref.two_ref = bf16[2,128,256]{2,1,0:T(8,128)(2,1)S(1)} collective-permute-done((bf16[2,128,256]{2,1,0:T(8,128)(2,1)S(1)}, bf16[2,128,256]{2,1,0:T(8,128)(2,1)S(1)}, u32[]{:S(2)}, u32[]{:S(2)}) %collective-permute-start.4) | collective-permute-done | bytes 131104 | tf_op jit(solution)/shard_map/ppermute | solution.py:255
  14.4 3.6 %collective-permute-start.5 = (bf16[2,128,256]{2,1,0:T(8,128)(2,1)S(1)}, bf16[2,128,256]{2,1,0:T(8,128)(2,1)S(1)}, u32[]{:S(2)}, u32[]{:S(2)}) collective-permute-start(bf16[2,128,256]{2,1,0:T(8,128)(2,1)S(1)} %shard_map.76), channel_id=1, source_target_pairs={{0,1},{1,0},{2,3},{3,2},{4,5},{5,4},{6,7},{7,6},{8,9},{9,8},{10,11... | collective-permute-start | bytes 393224 | tf_op jit(solution)/shard_map/ppermute | solution.py:255
  18.0 0.0 collective-permute-done.refs_0_.inner_ref
  18.0 0.1 collective-permute-start.2
  18.1 1.4 %shard_map.77.res_ref = bf16[4,2,384,256]{3,2,1,0:T(8,128)(2,1)S(1)} custom-call(bf16[1,2,384,1024]{3,2,1,0:T(8,128)(2,1)S(1)} %copy-done.1, bf16[2,32,1024]{2,1,0:T(8,128)(2,1)S(1)} %collective-permute-done.refs_0_.inner_ref, bf16[2,32,1024]{2,1,0:T(8,128)(2,1)S(1)} %collective-permute-done.1.refs_1_.outer_ref, ...), custom_call_target="tpu_custom_call" | custom-call | tf_op jit(solution)/shard_map/pallas_call | solution.py:243
  19.5 2.4 %collective-permute-done.5.three_ref = bf16[2,128,256]{2,1,0:T(8,128)(2,1)S(1)} collective-permute-done((bf16[2,128,256]{2,1,0:T(8,128)(2,1)S(1)}, bf16[2,128,256]{2,1,0:T(8,128)(2,1)S(1)}, u32[]{:S(2)}, u32[]{:S(2)}) %collective-permute-start.5) | collective-permute-done | bytes 131104 | tf_op jit(solution)/shard_map/ppermute | solution.py:255
  21.9 0.0 collective-permute-done.3.one_ref
  21.9 0.5 %shard_map.78 = (bf16[2,64,1024]{2,1,0:T(8,128)(2,1)S(1)}, bf16[2,64,1024]{2,1,0:T(8,128)(2,1)S(1)}, f32[2,64,128]{2,1,0:T(8,128)S(1)}) custom-call(bf16[2,384,256]{2,1,0:T(8,128)(2,1)S(1)} %copy-done.2, bf16[2,384,256]{2,1,0:T(8,128)(2,1)S(1)} %collective-permute-done.3.one_ref, bf16[2,128,256]{2,1,0:T(8,128)(2,1)S(1)} %collective-permute-done.4.block_ref.two_ref, ...), custom_call_target="tpu_custom_call" | custom-call | tf_op jit(solution)/shard_map/pallas_call | solution.py:243
  22.5 1.3 %collective-permute-start.6 = (bf16[2,64,1024]{2,1,0:T(8,128)(2,1)S(1)}, bf16[2,64,1024]{2,1,0:T(8,128)(2,1)S(1)}, u32[]{:S(2)}, u32[]{:S(2)}) collective-permute-start(bf16[2,64,1024]{2,1,0:T(8,128)(2,1)S(1)} %get-tuple-element.17), channel_id=1, source_target_pairs={{4,0},{8,4},{12,8},{16,12},{20,16},{24,20},{28,24},{5,1},{9,5},{13... | collective-permute-start | bytes 786440 | tf_op jit(solution)/shard_map/ppermute | solution.py:23
  23.8 0.8 %slice_convert_fusion = f32[64]{0:T(128)S(1)} fusion(s32[384]{0:T(512)} %param.9), kind=kLoop, calls=%fused_computation.1 | loop fusion | flops 64 | bytes 512 | tf_op jit(solution)/shard_map/convert_element_type | solution.py:291
  24.5 1.4 %collective-permute-done.6.later_ref = bf16[2,64,1024]{2,1,0:T(8,128)(2,1)S(1)} collective-permute-done((bf16[2,64,1024]{2,1,0:T(8,128)(2,1)S(1)}, bf16[2,64,1024]{2,1,0:T(8,128)(2,1)S(1)}, u32[]{:S(2)}, u32[]{:S(2)}) %collective-permute-start.6) | collective-permute-done | bytes 262176 | tf_op jit(solution)/shard_map/ppermute | solution.py:23
  25.9 0.1 broadcast_in_dim.2.weight_ref
  26.0 0.3 shard_map.79
  26.3 4.5 %collective-permute-start.7 = (f32[8,128]{1,0:T(8,128)S(1)}, f32[8,128]{1,0:T(8,128)S(1)}, u32[]{:S(2)}, u32[]{:S(2)}) collective-permute-start(f32[8,128]{1,0:T(8,128)S(1)} %shard_map.79), channel_id=1, source_target_pairs={{0,4},{4,0},{8,12},{12,8},{16,20},{20,16},{24,28},{28,24},{1,5},{5... | collective-permute-start | bytes 12296 | tf_op jit(solution)/shard_map/ppermute | solution.py:255
  30.8 1.4 %collective-permute-done.2.block_ref.two_ref = bf16[2,272,256]{2,1,0:T(8,128)(2,1)S(1)} collective-permute-done((bf16[2,272,256]{2,1,0:T(8,128)(2,1)S(1)}, bf16[2,272,256]{2,1,0:T(8,128)(2,1)S(1)}, u32[]{:S(2)}, u32[]{:S(2)}) %collective-permute-start.2) | collective-permute-done | bytes 278560 | tf_op jit(solution)/shard_map/ppermute | solution.py:255
  32.2 0.0 collective-permute-done.7.awaited_ref
  32.2 1.7 %collective-permute-start.8 = (bf16[2,256,256]{2,1,0:T(8,128)(2,1)S(1)}, bf16[2,256,256]{2,1,0:T(8,128)(2,1)S(1)}, u32[]{:S(2)}, u32[]{:S(2)}) collective-permute-start(bf16[2,256,256]{2,1,0:T(8,128)(2,1)S(1)} %shard_map.80), channel_id=1, source_target_pairs={{0,1},{1,0},{2,3},{3,2},{4,5},{5,4},{6,7},{7,6},{8,9},{9,8},{10,11... | collective-permute-start | bytes 786440 | tf_op jit(solution)/shard_map/ppermute | solution.py:255
  33.9 1.5 %collective-permute-start.9 = (f32[8,128]{1,0:T(8,128)S(1)}, f32[8,128]{1,0:T(8,128)S(1)}, u32[]{:S(2)}, u32[]{:S(2)}) collective-permute-start(f32[8,128]{1,0:T(8,128)S(1)} %add.6), channel_id=1, source_target_pairs={{0,8},{4,12},{8,0},{12,4},{16,24},{20,28},{24,16},{28,20},{1,9},{5... | collective-permute-start | bytes 12296 | tf_op jit(solution)/shard_map/ppermute | solution.py:255
  35.4 0.6 %shard_map.81.before_ref = f32[2,256,128]{2,1,0:T(8,128)S(1)} custom-call(bf16[2,384,256]{2,1,0:T(8,128)(2,1)S(1)} %copy-done.2, bf16[2,384,256]{2,1,0:T(8,128)(2,1)S(1)} %collective-permute-done.3.one_ref, bf16[2,272,256]{2,1,0:T(8,128)(2,1)S(1)} %collective-permute-done.2.block_ref.two_ref, bf16[4,2,384,256]{3,2,1,0:T(8,128)(2,1)S(1)} %shard_map.77.res_ref), custom_call_target="tpu_custom_call" | custom-call | flops 134217728 | bytes 3145728 | tf_op jit(solution)/shard_map/pallas_call | solution.py:243
  36.0 1.5 %collective-permute-done.9 = f32[8,128]{1,0:T(8,128)S(1)} collective-permute-done((f32[8,128]{1,0:T(8,128)S(1)}, f32[8,128]{1,0:T(8,128)S(1)}, u32[]{:S(2)}, u32[]{:S(2)}) %collective-permute-start.9) | collective-permute-done | bytes 4128 | tf_op jit(solution)/shard_map/ppermute | solution.py:255
  37.5 1.5 %collective-permute-start.10 = (f32[8,128]{1,0:T(8,128)S(1)}, f32[8,128]{1,0:T(8,128)S(1)}, u32[]{:S(2)}, u32[]{:S(2)}) collective-permute-start(f32[8,128]{1,0:T(8,128)S(1)} %add.7.mine_ref), channel_id=1, source_target_pairs={{0,16},{4,20},{8,24},{12,28},{16,0},{20,4},{24,8},{28,12},{1,17},{... | collective-permute-start | bytes 12296 | tf_op jit(solution)/shard_map/ppermute | solution.py:255
  39.0 1.7 %collective-permute-done.8.three_ref = bf16[2,256,256]{2,1,0:T(8,128)(2,1)S(1)} collective-permute-done((bf16[2,256,256]{2,1,0:T(8,128)(2,1)S(1)}, bf16[2,256,256]{2,1,0:T(8,128)(2,1)S(1)}, u32[]{:S(2)}, u32[]{:S(2)}) %collective-permute-start.8) | collective-permute-done | bytes 262176 | tf_op jit(solution)/shard_map/ppermute | solution.py:255
  40.7 0.3 shard_map.82.looks_ref
  41.0 0.1 collective-permute-done.10.other_ref
  41.1 0.8 %shard_map.83 = f32[1,2,192,128]{3,2,1,0:T(8,128)} custom-call(f32[2,192,128]{2,1,0:T(8,128)S(1)} %shard_map.82.looks_ref, f32[8,128]{1,0:T(8,128)S(1)} %add.7.mine_ref, f32[8,128]{1,0:T(8,128)S(1)} %collective-permute-done.10.other_ref), custom_call_target="tpu_custom_call" | custom-call | flops 393216 | bytes 393216 | tf_op jit(solution)/shard_map/pallas_call | solution.py:243
  (13 shorter events, 0.1 us)
Async XLA Ops:
  0.0 18.0 %copy-start.2 = (bf16[2,384,256]{2,1,0:T(8,128)(2,1)S(1)}, bf16[2,384,256]{2,1,0:T(8,128)(2,1)}, u32[]{:S(2)}) copy-start(bf16[2,384,256]{2,1,0:T(8,128)(2,1)} %own_ref.3) | copy-start | bytes 1179652
  0.0 21.9 %collective-permute-start.3 = (bf16[2,384,256]{2,1,0:T(8,128)(2,1)}, bf16[2,384,256]{2,1,0:T(8,128)(2,1)S(1)}, u32[]{:S(2)}, u32[]{:S(2)}) collective-permute-start(bf16[2,384,256]{2,1,0:T(8,128)(2,1)} %own_ref.3), channel_id=1, source_target_pairs={{0,1},{1,0},{2,3},{3,2},{4,5},{5,4},{6,7},{7,6},{8,9},{9,8},{10,11... | collective-permute-start | bytes 1179656 | tf_op jit(solution)/shard_map/ppermute | solution.py:255
  3.9 10.5 %collective-permute-start.4 = (bf16[2,128,256]{2,1,0:T(8,128)(2,1)S(1)}, bf16[2,128,256]{2,1,0:T(8,128)(2,1)S(1)}, u32[]{:S(2)}, u32[]{:S(2)}) collective-permute-start(bf16[2,128,256]{2,1,0:T(8,128)(2,1)S(1)} %pad_maximum_fusion), channel_id=1, source_target_pairs={{0,2},{1,3},{2,0},{3,1},{4,6},{5,7},{6,4},{7,5},{8,10},{9,11},{10,... | collective-permute-start | bytes 393224 | tf_op jit(solution)/shard_map/ppermute | solution.py:255
  6.6 1.4 %copy-start = (bf16[1,2,384,1024]{3,2,1,0:T(8,128)(2,1)S(1)}, bf16[1,2,384,1024]{3,2,1,0:T(8,128)(2,1)}, u32[]{:S(2)}) copy-start(bf16[1,2,384,1024]{3,2,1,0:T(8,128)(2,1)} %sec_ref.3) | copy-start | bytes 4718596
  8.0 10.1 %copy-start.1 = (bf16[1,2,384,1024]{3,2,1,0:T(8,128)(2,1)S(1)}, bf16[1,2,384,1024]{3,2,1,0:T(8,128)(2,1)}, u32[]{:S(2)}) copy-start(bf16[1,2,384,1024]{3,2,1,0:T(8,128)(2,1)} %sec_ref.3) | copy-start | bytes 4718596
  8.0 10.0 %collective-permute-start = (bf16[2,32,1024]{2,1,0:T(8,128)(2,1)S(1)}, bf16[2,32,1024]{2,1,0:T(8,128)(2,1)S(1)}, u32[]{:S(2)}, u32[]{:S(2)}) collective-permute-start(bf16[2,32,1024]{2,1,0:T(8,128)(2,1)S(1)} %get-tuple-element.12), channel_id=1, source_target_pairs={{0,4},{4,0},{8,12},{12,8},{16,20},{20,16},{24,28},{28,24},{1,5},{5... | collective-permute-start | bytes 393224 | tf_op jit(solution)/shard_map/ppermute | solution.py:255
  8.1 9.9 %collective-permute-start.1 = (bf16[2,32,1024]{2,1,0:T(8,128)(2,1)S(1)}, bf16[2,32,1024]{2,1,0:T(8,128)(2,1)S(1)}, u32[]{:S(2)}, u32[]{:S(2)}) collective-permute-start(bf16[2,32,1024]{2,1,0:T(8,128)(2,1)S(1)} %get-tuple-element.13), channel_id=1, source_target_pairs={{4,8},{8,4},{12,16},{16,12},{20,24},{24,20},{5,9},{9,5},{13,17},{1... | collective-permute-start | bytes 393224 | tf_op jit(solution)/shard_map/ppermute | solution.py:274
  14.4 7.5 %collective-permute-start.5 = (bf16[2,128,256]{2,1,0:T(8,128)(2,1)S(1)}, bf16[2,128,256]{2,1,0:T(8,128)(2,1)S(1)}, u32[]{:S(2)}, u32[]{:S(2)}) collective-permute-start(bf16[2,128,256]{2,1,0:T(8,128)(2,1)S(1)} %shard_map.76), channel_id=1, source_target_pairs={{0,1},{1,0},{2,3},{3,2},{4,5},{5,4},{6,7},{7,6},{8,9},{9,8},{10,11... | collective-permute-start | bytes 393224 | tf_op jit(solution)/shard_map/ppermute | solution.py:255
  18.0 14.2 %collective-permute-start.2 = (bf16[2,272,256]{2,1,0:T(8,128)(2,1)S(1)}, bf16[2,272,256]{2,1,0:T(8,128)(2,1)S(1)}, u32[]{:S(2)}, u32[]{:S(2)}) collective-permute-start(bf16[2,272,256]{2,1,0:T(8,128)(2,1)S(1)} %shard_map.74), channel_id=1, source_target_pairs={{0,2},{1,3},{2,0},{3,1},{4,6},{5,7},{6,4},{7,5},{8,10},{9,11},{10,... | collective-permute-start | bytes 835592 | tf_op jit(solution)/shard_map/ppermute | solution.py:255
  22.5 3.4 %collective-permute-start.6 = (bf16[2,64,1024]{2,1,0:T(8,128)(2,1)S(1)}, bf16[2,64,1024]{2,1,0:T(8,128)(2,1)S(1)}, u32[]{:S(2)}, u32[]{:S(2)}) collective-permute-start(bf16[2,64,1024]{2,1,0:T(8,128)(2,1)S(1)} %get-tuple-element.17), channel_id=1, source_target_pairs={{4,0},{8,4},{12,8},{16,12},{20,16},{24,20},{28,24},{5,1},{9,5},{13... | collective-permute-start | bytes 786440 | tf_op jit(solution)/shard_map/ppermute | solution.py:23
  26.3 5.9 %collective-permute-start.7 = (f32[8,128]{1,0:T(8,128)S(1)}, f32[8,128]{1,0:T(8,128)S(1)}, u32[]{:S(2)}, u32[]{:S(2)}) collective-permute-start(f32[8,128]{1,0:T(8,128)S(1)} %shard_map.79), channel_id=1, source_target_pairs={{0,4},{4,0},{8,12},{12,8},{16,20},{20,16},{24,28},{28,24},{1,5},{5... | collective-permute-start | bytes 12296 | tf_op jit(solution)/shard_map/ppermute | solution.py:255
  32.2 8.5 %collective-permute-start.8 = (bf16[2,256,256]{2,1,0:T(8,128)(2,1)S(1)}, bf16[2,256,256]{2,1,0:T(8,128)(2,1)S(1)}, u32[]{:S(2)}, u32[]{:S(2)}) collective-permute-start(bf16[2,256,256]{2,1,0:T(8,128)(2,1)S(1)} %shard_map.80), channel_id=1, source_target_pairs={{0,1},{1,0},{2,3},{3,2},{4,5},{5,4},{6,7},{7,6},{8,9},{9,8},{10,11... | collective-permute-start | bytes 786440 | tf_op jit(solution)/shard_map/ppermute | solution.py:255
  33.9 3.6 %collective-permute-start.9 = (f32[8,128]{1,0:T(8,128)S(1)}, f32[8,128]{1,0:T(8,128)S(1)}, u32[]{:S(2)}, u32[]{:S(2)}) collective-permute-start(f32[8,128]{1,0:T(8,128)S(1)} %add.6), channel_id=1, source_target_pairs={{0,8},{4,12},{8,0},{12,4},{16,24},{20,28},{24,16},{28,20},{1,9},{5... | collective-permute-start | bytes 12296 | tf_op jit(solution)/shard_map/ppermute | solution.py:255
  37.5 3.6 %collective-permute-start.10 = (f32[8,128]{1,0:T(8,128)S(1)}, f32[8,128]{1,0:T(8,128)S(1)}, u32[]{:S(2)}, u32[]{:S(2)}) collective-permute-start(f32[8,128]{1,0:T(8,128)S(1)} %add.7.mine_ref), channel_id=1, source_target_pairs={{0,16},{4,20},{8,24},{12,28},{16,0},{20,4},{24,8},{28,12},{1,17},{... | collective-permute-start | bytes 12296 | tf_op jit(solution)/shard_map/ppermute | solution.py:255

commit v9 on v8

--- a/solution.py
+++ b/solution.py
@@ -139,7 +139,7 @@
     looks_n = looks_ref.shape[2]
     totals = [None, None]
     for step, (prim_ref, starts) in enumerate(
-        ((own_ref, whole), (one_ref, whole), (two_ref, edges), (three_ref, edges))
+        ((own_ref, whole), (one_ref, edges), (two_ref, edges), (three_ref, edges))
     ):
         block = jnp.bitwise_xor(here, step)
         select = look_columns(width, block, looks_n)
@@ -265,8 +265,7 @@
     looks_n = cols_n // LR
     middle_n = rows_n - 2 * LAG
     edges = jnp.concatenate([primary[:, :LAG], primary[:, rows_n - LAG :]], axis=1)
-    edges_two = swap(edges, "date", 2)
-    one = swap(primary, "date", 1)
+    edges_two, edges_three, edges_one = [swap(edges, "date", step) for step in (2, 3, 1)]
     halo = shape((2, HALO, cols_n), bf16)
     inner, outer = call(cut_halo_kernel, (halo, halo), [], (0, 0), secondary)
     inner = swap(inner, "tile", 1)
@@ -279,15 +278,6 @@
         (0, 0),
         az_off, rg_off, az_frac, rg_frac,
     )
-    relayed = call(relay_kernel, edges, [], (0, 0), edges_two, az_band)
-    edges_three = swap(relayed, "date", 1)
-    middle = call(
-        cut_middle_kernel,
-        shape((2, middle_n + 16, width), bf16),
-        [],
-        (0, 0),
-        primary, inner,outer,
-    )
     weight = jnp.broadcast_to(margin_mask[rows_n - LAG :].astype(f32)[:, None], (LAG, LANE))
     res = call(
         resample_kernel,
@@ -296,14 +286,21 @@
         (0, 0),
         secondary, inner, outer, az_band, rg_band,
     )
-    two = swap(middle, "date", 2)
+    middle = call(
+        cut_middle_kernel,
+        shape((2, middle_n + 16, width), bf16),
+        [],
+        (0, 0),
+        primary, edges_two,edges_three,az_band,
+    )
+    two, one = [swap(middle, "date", step) for step in (2, 1)]
     margin = shape((2, LAG, cols_n), bf16)
     first, last, looks = call(
         margin_kernel,
         (margin, margin, shape((2, 2 * LAG // LA, looks_n), f32)),
         [pltpu.VMEM((2, 2 * LAG, looks_n), f32)],
         (0, 0),
-        primary, one, edges_two, edges_three, res,
+        primary, edges_one, edges_two, edges_three, res,
     )
     later = passed_along(first, "tile", -1)
     stats = call(

time: 42.3 us -> 45.2 us (1.069)
  waiting for transfers between devices: 11.1 us -> 14.4 us
    ppermute x9 -> x10, waiting for transfers between devices: 9.7 us -> 13.1 us  [swap(): lax.ppermute(value, axis, [(at, at ^ step) for at in range(lax.axis_size(...]
    ppermute x9 -> x10, starting transfers between devices: 18.6 us -> 18.1 us  [swap(): lax.ppermute(value, axis, [(at, at ^ step) for at in range(lax.axis_size(...]
    pallas_call x11 -> x10, Pallas kernels: 4.4 us -> 4.42 us  [call(): pl.pallas_call(kernel, out_shape=outs, in_specs=[vmem] * len(args), out_s...]
  transfers between devices with their start and end apart: 11 -> 12, of which waited for: 7 -> 7; matrix products, arithmetic and copies ran while one was open for 4% -> 2% of each run, Pallas kernels for 8% -> 8%
where the time goes in v9:
time: 45.2 us; the launch traced here: 44.9 us
  starting transfers between devices  20.2 us (45%)
  waiting for transfers between devices  14.4 us (32%)
  Pallas kernels  4.42 us (10%)
  between operations  2.73 us (6%)
  local copies, waits for them, and re-layouts  2.42 us (5%)
  other arithmetic  0.78 us (2%)
    ppermute x10, starting transfers between devices, swap(): lax.ppermute(value, axis, [(at, at ^ step) for at in range(lax.axis_size(...  18.1 us
    ppermute x10, waiting for transfers between devices, swap(): lax.ppermute(value, axis, [(at, at ^ step) for at in range(lax.axis_size(...  13.1 us
    pallas_call x10, Pallas kernels, call(): pl.pallas_call(kernel, out_shape=outs, in_specs=[vmem] * len(args), out_s...  4.42 us
    unnamed x6, local copies, waits for them, and re-layouts  1.41 us
    ppermute x1, waiting for transfers between devices, passed_along(): lax.ppermute(value, axis, [(source, source + steps) for source in range(i...  1.29 us
    ppermute x1, starting transfers between devices, passed_along(): lax.ppermute(value, axis, [(source, source + steps) for source in range(i...  1.29 us
    slice x1, local copies, waits for them, and re-layouts, fused(): primary[:, :LAG]  0.93 us
  transfers between devices with their start and end apart: 12, of which 7 were waited for; matrix products, arithmetic and copies ran while one was open for 2% of the time, Pallas kernels for 8%

profile of v9, /device:TPU:0, one launch (start us, length us, event | category | flops | bytes accessed | tf_op | source)
XLA Modules:
  0.0 44.9 jit_solution(16611814206435400709)
XLA Ops:
  0.0 0.9 %fusion = (bf16[2,64,256]{2,1,0:T(8,128)(2,1)S(1)}, bf16[2,64,256]{2,1,0:T(8,128)(2,1)S(1)}) fusion(bf16[2,384,256]{2,1,0:T(8,128)(2,1)} %own_ref.3), kind=kLoop, calls=%fused_computation.2 | loop fusion | bytes 262144 | tf_op jit(solution)/shard_map/slice | solution.py:267
  1.0 4.1 %collective-permute-start = (bf16[2,128,256]{2,1,0:T(8,128)(2,1)S(1)}, bf16[2,128,256]{2,1,0:T(8,128)(2,1)S(1)}, u32[]{:S(2)}, u32[]{:S(2)}) collective-permute-start(bf16[2,128,256]{2,1,0:T(8,128)(2,1)S(1)} %pad_maximum_fusion), channel_id=1, source_target_pairs={{0,2},{1,3},{2,0},{3,1},{4,6},{5,7},{6,4},{7,5},{8,10},{9,11},{10,... | collective-permute-start | bytes 393224 | tf_op jit(solution)/shard_map/ppermute | solution.py:255
  5.1 1.3 %collective-permute-start.1 = (bf16[2,128,256]{2,1,0:T(8,128)(2,1)S(1)}, bf16[2,128,256]{2,1,0:T(8,128)(2,1)S(1)}, u32[]{:S(2)}, u32[]{:S(2)}) collective-permute-start(bf16[2,128,256]{2,1,0:T(8,128)(2,1)S(1)} %pad_maximum_fusion), channel_id=1, source_target_pairs={{0,3},{1,2},{2,1},{3,0},{4,7},{5,6},{6,5},{7,4},{8,11},{9,10},{10,... | collective-permute-start | bytes 393224 | tf_op jit(solution)/shard_map/ppermute | solution.py:255
  6.4 1.4 %copy-done = bf16[1,2,384,1024]{3,2,1,0:T(8,128)(2,1)S(1)} copy-done((bf16[1,2,384,1024]{3,2,1,0:T(8,128)(2,1)S(1)}, bf16[1,2,384,1024]{3,2,1,0:T(8,128)(2,1)}, u32[]{:S(2)}) %copy-start) | copy-done | bytes 1572888
  7.9 0.1 collective-permute-start.4
  7.9 0.8 %collective-permute-start.5 = (bf16[2,32,1024]{2,1,0:T(8,128)(2,1)S(1)}, bf16[2,32,1024]{2,1,0:T(8,128)(2,1)S(1)}, u32[]{:S(2)}, u32[]{:S(2)}) collective-permute-start(bf16[2,32,1024]{2,1,0:T(8,128)(2,1)S(1)} %get-tuple-element.14), channel_id=1, source_target_pairs={{4,8},{8,4},{12,16},{16,12},{20,24},{24,20},{5,9},{9,5},{13,17},{1... | collective-permute-start | bytes 393224 | tf_op jit(solution)/shard_map/ppermute | solution.py:273
  8.7 0.3 collective-permute-start.3
  11.6 0.4 shard_map.73
  12.0 3.0 %collective-permute-done.refs_0_.two_ref = bf16[2,128,256]{2,1,0:T(8,128)(2,1)S(1)} collective-permute-done((bf16[2,128,256]{2,1,0:T(8,128)(2,1)S(1)}, bf16[2,128,256]{2,1,0:T(8,128)(2,1)S(1)}, u32[]{:S(2)}, u32[]{:S(2)}) %collective-permute-start) | collective-permute-done | bytes 131104 | tf_op jit(solution)/shard_map/ppermute | solution.py:255
  15.0 0.0 collective-permute-done.1.refs_1_.three_ref
  15.0 4.7 %collective-permute-start.2 = (bf16[2,272,256]{2,1,0:T(8,128)(2,1)S(1)}, bf16[2,272,256]{2,1,0:T(8,128)(2,1)S(1)}, u32[]{:S(2)}, u32[]{:S(2)}) collective-permute-start(bf16[2,272,256]{2,1,0:T(8,128)(2,1)S(1)} %shard_map.74), channel_id=1, source_target_pairs={{0,2},{1,3},{2,0},{3,1},{4,6},{5,7},{6,4},{7,5},{8,10},{9,11},{10,... | collective-permute-start | bytes 835592 | tf_op jit(solution)/shard_map/ppermute | solution.py:255
  19.8 1.4 %shard_map.76.res_ref = bf16[4,2,384,256]{3,2,1,0:T(8,128)(2,1)S(1)} custom-call(bf16[1,2,384,1024]{3,2,1,0:T(8,128)(2,1)S(1)} %copy-done.1, bf16[2,32,1024]{2,1,0:T(8,128)(2,1)S(1)} %collective-permute-done.4.inner_ref, bf16[2,32,1024]{2,1,0:T(8,128)(2,1)S(1)} %collective-permute-done.5.outer_ref, bf16[128,192]{1,0:T(8,128)(2,1)S(1)} %get-tuple-element.12.refs_2_.az_ref, ...), custom_call_target="tpu_custom_call" | custom-call | tf_op jit(solution)/shard_map/pallas_call | solution.py:243
  21.2 0.0 collective-permute-done.3.one_ref
  21.2 0.5 %shard_map.77 = (bf16[2,64,1024]{2,1,0:T(8,128)(2,1)S(1)}, bf16[2,64,1024]{2,1,0:T(8,128)(2,1)S(1)}, f32[2,64,128]{2,1,0:T(8,128)S(1)}) custom-call(bf16[2,384,256]{2,1,0:T(8,128)(2,1)S(1)} %copy-done.2, bf16[2,128,256]{2,1,0:T(8,128)(2,1)S(1)} %collective-permute-done.3.one_ref, bf16[2,128,256]{2,1,0:T(8,128)(2,1)S(1)} %collective-permute-done.refs_0_.two_ref, ...), custom_call_target="tpu_custom_call" | custom-call | tf_op jit(solution)/shard_map/pallas_call | solution.py:243
  21.7 1.3 %collective-permute-start.6 = (bf16[2,64,1024]{2,1,0:T(8,128)(2,1)S(1)}, bf16[2,64,1024]{2,1,0:T(8,128)(2,1)S(1)}, u32[]{:S(2)}, u32[]{:S(2)}) collective-permute-start(bf16[2,64,1024]{2,1,0:T(8,128)(2,1)S(1)} %get-tuple-element.17), channel_id=1, source_target_pairs={{4,0},{8,4},{12,8},{16,12},{20,16},{24,20},{28,24},{5,1},{9,5},{13... | collective-permute-start | bytes 786440 | tf_op jit(solution)/shard_map/ppermute | solution.py:23
  23.0 0.1 collective-permute-start.9
  23.1 0.8 %slice_convert_fusion = f32[64]{0:T(128)S(1)} fusion(s32[384]{0:T(512)} %param.9), kind=kLoop, calls=%fused_computation.1 | loop fusion | flops 64 | bytes 512 | tf_op jit(solution)/shard_map/convert_element_type | solution.py:281
  23.9 1.3 %collective-permute-done.6.later_ref = bf16[2,64,1024]{2,1,0:T(8,128)(2,1)S(1)} collective-permute-done((bf16[2,64,1024]{2,1,0:T(8,128)(2,1)S(1)}, bf16[2,64,1024]{2,1,0:T(8,128)(2,1)S(1)}, u32[]{:S(2)}, u32[]{:S(2)}) %collective-permute-start.6) | collective-permute-done | bytes 262176 | tf_op jit(solution)/shard_map/ppermute | solution.py:23
  25.2 0.1 broadcast_in_dim.2.weight_ref
  25.2 0.3 shard_map.78
  25.6 4.4 %collective-permute-start.7 = (f32[8,128]{1,0:T(8,128)S(1)}, f32[8,128]{1,0:T(8,128)S(1)}, u32[]{:S(2)}, u32[]{:S(2)}) collective-permute-start(f32[8,128]{1,0:T(8,128)S(1)} %shard_map.78), channel_id=1, source_target_pairs={{0,4},{4,0},{8,12},{12,8},{16,20},{20,16},{24,28},{28,24},{1,5},{5... | collective-permute-start | bytes 12296 | tf_op jit(solution)/shard_map/ppermute | solution.py:255
  30.0 0.8 %collective-permute-done.7.awaited_ref = f32[8,128]{1,0:T(8,128)S(1)} collective-permute-done((f32[8,128]{1,0:T(8,128)S(1)}, f32[8,128]{1,0:T(8,128)S(1)}, u32[]{:S(2)}, u32[]{:S(2)}) %collective-permute-start.7) | collective-permute-done | bytes 4128 | tf_op jit(solution)/shard_map/ppermute | solution.py:255
  30.9 1.8 %collective-permute-done.2.block_ref.two_ref = bf16[2,272,256]{2,1,0:T(8,128)(2,1)S(1)} collective-permute-done((bf16[2,272,256]{2,1,0:T(8,128)(2,1)S(1)}, bf16[2,272,256]{2,1,0:T(8,128)(2,1)S(1)}, u32[]{:S(2)}, u32[]{:S(2)}) %collective-permute-start.2) | collective-permute-done | bytes 278560 | tf_op jit(solution)/shard_map/ppermute | solution.py:255
  32.7 0.1 collective-permute-start.8
  32.8 1.5 %collective-permute-start.10 = (f32[8,128]{1,0:T(8,128)S(1)}, f32[8,128]{1,0:T(8,128)S(1)}, u32[]{:S(2)}, u32[]{:S(2)}) collective-permute-start(f32[8,128]{1,0:T(8,128)S(1)} %add.6), channel_id=1, source_target_pairs={{0,8},{4,12},{8,0},{12,4},{16,24},{20,28},{24,16},{28,20},{1,9},{5... | collective-permute-start | bytes 12296 | tf_op jit(solution)/shard_map/ppermute | solution.py:255
  34.3 2.2 %collective-permute-done.10 = f32[8,128]{1,0:T(8,128)S(1)} collective-permute-done((f32[8,128]{1,0:T(8,128)S(1)}, f32[8,128]{1,0:T(8,128)S(1)}, u32[]{:S(2)}, u32[]{:S(2)}) %collective-permute-start.10) | collective-permute-done | bytes 4128 | tf_op jit(solution)/shard_map/ppermute | solution.py:255
  36.5 1.5 %collective-permute-start.11 = (f32[8,128]{1,0:T(8,128)S(1)}, f32[8,128]{1,0:T(8,128)S(1)}, u32[]{:S(2)}, u32[]{:S(2)}) collective-permute-start(f32[8,128]{1,0:T(8,128)S(1)} %add.7.mine_ref), channel_id=1, source_target_pairs={{0,16},{4,20},{8,24},{12,28},{16,0},{20,4},{24,8},{28,12},{1,17},{... | collective-permute-start | bytes 12296 | tf_op jit(solution)/shard_map/ppermute | solution.py:255
  37.9 0.2 collective-permute-done.9.one_ref
  38.2 0.6 %shard_map.80.before_ref = f32[2,256,128]{2,1,0:T(8,128)S(1)} custom-call(bf16[2,384,256]{2,1,0:T(8,128)(2,1)S(1)} %copy-done.2, bf16[2,272,256]{2,1,0:T(8,128)(2,1)S(1)} %collective-permute-done.9.one_ref, bf16[2,272,256]{2,1,0:T(8,128)(2,1)S(1)} %collective-permute-done.2.block_ref.two_ref, bf16[4,2,384,256]{3,2,1,0:T(8,128)(2,1)S(1)} %shard_map.76.res_ref), custom_call_target="tpu_custom_call" | custom-call | flops 134217728 | bytes 3145728 | tf_op jit(solution)/shard_map/pallas_call | solution.py:243
  38.8 5.0 %collective-permute-done.8.three_ref = bf16[2,256,256]{2,1,0:T(8,128)(2,1)S(1)} collective-permute-done((bf16[2,256,256]{2,1,0:T(8,128)(2,1)S(1)}, bf16[2,256,256]{2,1,0:T(8,128)(2,1)S(1)}, u32[]{:S(2)}, u32[]{:S(2)}) %collective-permute-start.8) | collective-permute-done | bytes 262176 | tf_op jit(solution)/shard_map/ppermute | solution.py:255
  43.8 0.3 shard_map.81.looks_ref
  44.1 0.8 %shard_map.82 = f32[1,2,192,128]{3,2,1,0:T(8,128)} custom-call(f32[2,192,128]{2,1,0:T(8,128)S(1)} %shard_map.81.looks_ref, f32[8,128]{1,0:T(8,128)S(1)} %add.7.mine_ref, f32[8,128]{1,0:T(8,128)S(1)} %collective-permute-done.11.other_ref), custom_call_target="tpu_custom_call" | custom-call | flops 393216 | bytes 393216 | tf_op jit(solution)/shard_map/pallas_call | solution.py:243
  (14 shorter events, 0.1 us)
Async XLA Ops:
  0.0 15.0 %copy-start.2 = (bf16[2,384,256]{2,1,0:T(8,128)(2,1)S(1)}, bf16[2,384,256]{2,1,0:T(8,128)(2,1)}, u32[]{:S(2)}) copy-start(bf16[2,384,256]{2,1,0:T(8,128)(2,1)} %own_ref.3) | copy-start | bytes 1179652
  1.0 14.0 %collective-permute-start = (bf16[2,128,256]{2,1,0:T(8,128)(2,1)S(1)}, bf16[2,128,256]{2,1,0:T(8,128)(2,1)S(1)}, u32[]{:S(2)}, u32[]{:S(2)}) collective-permute-start(bf16[2,128,256]{2,1,0:T(8,128)(2,1)S(1)} %pad_maximum_fusion), channel_id=1, source_target_pairs={{0,2},{1,3},{2,0},{3,1},{4,6},{5,7},{6,4},{7,5},{8,10},{9,11},{10,... | collective-permute-start | bytes 393224 | tf_op jit(solution)/shard_map/ppermute | solution.py:255
  5.1 9.9 %collective-permute-start.1 = (bf16[2,128,256]{2,1,0:T(8,128)(2,1)S(1)}, bf16[2,128,256]{2,1,0:T(8,128)(2,1)S(1)}, u32[]{:S(2)}, u32[]{:S(2)}) collective-permute-start(bf16[2,128,256]{2,1,0:T(8,128)(2,1)S(1)} %pad_maximum_fusion), channel_id=1, source_target_pairs={{0,3},{1,2},{2,1},{3,0},{4,7},{5,6},{6,5},{7,4},{8,11},{9,10},{10,... | collective-permute-start | bytes 393224 | tf_op jit(solution)/shard_map/ppermute | solution.py:255
  6.4 1.4 %copy-start = (bf16[1,2,384,1024]{3,2,1,0:T(8,128)(2,1)S(1)}, bf16[1,2,384,1024]{3,2,1,0:T(8,128)(2,1)}, u32[]{:S(2)}) copy-start(bf16[1,2,384,1024]{3,2,1,0:T(8,128)(2,1)} %sec_ref.3) | copy-start | bytes 4718596
  7.8 11.9 %copy-start.1 = (bf16[1,2,384,1024]{3,2,1,0:T(8,128)(2,1)S(1)}, bf16[1,2,384,1024]{3,2,1,0:T(8,128)(2,1)}, u32[]{:S(2)}) copy-start(bf16[1,2,384,1024]{3,2,1,0:T(8,128)(2,1)} %sec_ref.3) | copy-start | bytes 4718596
  7.9 11.9 %collective-permute-start.4 = (bf16[2,32,1024]{2,1,0:T(8,128)(2,1)S(1)}, bf16[2,32,1024]{2,1,0:T(8,128)(2,1)S(1)}, u32[]{:S(2)}, u32[]{:S(2)}) collective-permute-start(bf16[2,32,1024]{2,1,0:T(8,128)(2,1)S(1)} %get-tuple-element.13), channel_id=1, source_target_pairs={{0,4},{4,0},{8,12},{12,8},{16,20},{20,16},{24,28},{28,24},{1,5},{5... | collective-permute-start | bytes 393224 | tf_op jit(solution)/shard_map/ppermute | solution.py:255
  7.9 11.8 %collective-permute-start.5 = (bf16[2,32,1024]{2,1,0:T(8,128)(2,1)S(1)}, bf16[2,32,1024]{2,1,0:T(8,128)(2,1)S(1)}, u32[]{:S(2)}, u32[]{:S(2)}) collective-permute-start(bf16[2,32,1024]{2,1,0:T(8,128)(2,1)S(1)} %get-tuple-element.14), channel_id=1, source_target_pairs={{4,8},{8,4},{12,16},{16,12},{20,24},{24,20},{5,9},{9,5},{13,17},{1... | collective-permute-start | bytes 393224 | tf_op jit(solution)/shard_map/ppermute | solution.py:273
  8.7 12.5 %collective-permute-start.3 = (bf16[2,128,256]{2,1,0:T(8,128)(2,1)S(1)}, bf16[2,128,256]{2,1,0:T(8,128)(2,1)S(1)}, u32[]{:S(2)}, u32[]{:S(2)}) collective-permute-start(bf16[2,128,256]{2,1,0:T(8,128)(2,1)S(1)} %pad_maximum_fusion), channel_id=1, source_target_pairs={{0,1},{1,0},{2,3},{3,2},{4,5},{5,4},{6,7},{7,6},{8,9},{9,8},{10,11... | collective-permute-start | bytes 393224 | tf_op jit(solution)/shard_map/ppermute | solution.py:255
  15.0 17.6 %collective-permute-start.2 = (bf16[2,272,256]{2,1,0:T(8,128)(2,1)S(1)}, bf16[2,272,256]{2,1,0:T(8,128)(2,1)S(1)}, u32[]{:S(2)}, u32[]{:S(2)}) collective-permute-start(bf16[2,272,256]{2,1,0:T(8,128)(2,1)S(1)} %shard_map.74), channel_id=1, source_target_pairs={{0,2},{1,3},{2,0},{3,1},{4,6},{5,7},{6,4},{7,5},{8,10},{9,11},{10,... | collective-permute-start | bytes 835592 | tf_op jit(solution)/shard_map/ppermute | solution.py:255
  21.7 3.4 %collective-permute-start.6 = (bf16[2,64,1024]{2,1,0:T(8,128)(2,1)S(1)}, bf16[2,64,1024]{2,1,0:T(8,128)(2,1)S(1)}, u32[]{:S(2)}, u32[]{:S(2)}) collective-permute-start(bf16[2,64,1024]{2,1,0:T(8,128)(2,1)S(1)} %get-tuple-element.17), channel_id=1, source_target_pairs={{4,0},{8,4},{12,8},{16,12},{20,16},{24,20},{28,24},{5,1},{9,5},{13... | collective-permute-start | bytes 786440 | tf_op jit(solution)/shard_map/ppermute | solution.py:23
  23.0 15.1 %collective-permute-start.9 = (bf16[2,272,256]{2,1,0:T(8,128)(2,1)S(1)}, bf16[2,272,256]{2,1,0:T(8,128)(2,1)S(1)}, u32[]{:S(2)}, u32[]{:S(2)}) collective-permute-start(bf16[2,272,256]{2,1,0:T(8,128)(2,1)S(1)} %shard_map.74), channel_id=1, source_target_pairs={{0,1},{1,0},{2,3},{3,2},{4,5},{5,4},{6,7},{7,6},{8,9},{9,8},{10,11... | collective-permute-start | bytes 835592 | tf_op jit(solution)/shard_map/ppermute | solution.py:255
  25.6 5.3 %collective-permute-start.7 = (f32[8,128]{1,0:T(8,128)S(1)}, f32[8,128]{1,0:T(8,128)S(1)}, u32[]{:S(2)}, u32[]{:S(2)}) collective-permute-start(f32[8,128]{1,0:T(8,128)S(1)} %shard_map.78), channel_id=1, source_target_pairs={{0,4},{4,0},{8,12},{12,8},{16,20},{20,16},{24,28},{28,24},{1,5},{5... | collective-permute-start | bytes 12296 | tf_op jit(solution)/shard_map/ppermute | solution.py:255
  32.7 11.1 %collective-permute-start.8 = (bf16[2,256,256]{2,1,0:T(8,128)(2,1)S(1)}, bf16[2,256,256]{2,1,0:T(8,128)(2,1)S(1)}, u32[]{:S(2)}, u32[]{:S(2)}) collective-permute-start(bf16[2,256,256]{2,1,0:T(8,128)(2,1)S(1)} %shard_map.79), channel_id=1, source_target_pairs={{0,1},{1,0},{2,3},{3,2},{4,5},{5,4},{6,7},{7,6},{8,9},{9,8},{10,11... | collective-permute-start | bytes 786440 | tf_op jit(solution)/shard_map/ppermute | solution.py:255
  32.8 3.7 %collective-permute-start.10 = (f32[8,128]{1,0:T(8,128)S(1)}, f32[8,128]{1,0:T(8,128)S(1)}, u32[]{:S(2)}, u32[]{:S(2)}) collective-permute-start(f32[8,128]{1,0:T(8,128)S(1)} %add.6), channel_id=1, source_target_pairs={{0,8},{4,12},{8,0},{12,4},{16,24},{20,28},{24,16},{28,20},{1,9},{5... | collective-permute-start | bytes 12296 | tf_op jit(solution)/shard_map/ppermute | solution.py:255
  36.5 7.6 %collective-permute-start.11 = (f32[8,128]{1,0:T(8,128)S(1)}, f32[8,128]{1,0:T(8,128)S(1)}, u32[]{:S(2)}, u32[]{:S(2)}) collective-permute-start(f32[8,128]{1,0:T(8,128)S(1)} %add.7.mine_ref), channel_id=1, source_target_pairs={{0,16},{4,20},{8,24},{12,28},{16,0},{20,4},{24,8},{28,12},{1,17},{... | collective-permute-start | bytes 12296 | tf_op jit(solution)/shard_map/ppermute | solution.py:255

commit v10 on v8

--- a/solution.py
+++ b/solution.py
@@ -42,12 +42,10 @@
     return total.astype(jnp.bfloat16)
 
 
-def cut_halo_kernel(sec_ref, inner_ref, outer_ref):
+def cut_halo_kernel(sec_ref, down_ref, up_ref):
     rows_n = sec_ref.shape[2]
-    first = lax.rem(lax.axis_index("tile"), 2) == 0
-    down, up = sec_ref[0, :, rows_n - HALO :], sec_ref[0, :, :HALO]
-    inner_ref[...] = jnp.where(first, down, up)
-    outer_ref[...] = jnp.where(first, up, down)
+    down_ref[...] = sec_ref[0, :, rows_n - HALO :]
+    up_ref[...] = sec_ref[0, :, :HALO]
 
 
 def cut_middle_kernel(prim_ref, *refs):
@@ -71,18 +69,19 @@
         rg_ref[at] = band(square, offset + shift - ro_ref[...], taps)
 
 
-def resample_kernel(sec_ref, inner_ref, outer_ref, az_ref, rg_ref, out_ref, azim_ref):
+def resample_kernel(sec_ref, low_ref, high_ref, az_ref, rg_ref, out_ref, azim_ref):
     rows_n, cols_n = sec_ref.shape[2:]
     az_band = az_ref[...]
-    first = lax.rem(lax.axis_index("tile"), 2) == 0
+    here, tiles_n = lax.axis_index("tile"), lax.axis_size("tile")
+    none = jnp.zeros(low_ref.shape[1:], jnp.bfloat16)
     for part in range(2):
         for start in range(0, rows_n, BAND):
             pieces = []
             if start == 0:
-                pieces.append(jnp.where(first, outer_ref[part], inner_ref[part]))
+                pieces.append(jnp.where(here == 0, none, low_ref[part]))
             pieces.append(sec_ref[0, part, max(0, start - HALO) : min(rows_n, start + BAND + HALO)])
             if start + BAND == rows_n:
-                pieces.append(jnp.where(first, inner_ref[part], outer_ref[part]))
+                pieces.append(jnp.where(here == tiles_n - 1, none, high_ref[part]))
             rows = jnp.concatenate(pieces, axis=0) if len(pieces) > 1 else pieces[0]
             azim_ref[part, start : start + BAND] = jnp.dot(
                 az_band, rows, preferred_element_type=jnp.float32
@@ -169,7 +168,8 @@
     cols_n = last_ref.shape[2]
     weight = weight_ref[...]
     i_re, i_im = last_ref[0].astype(jnp.float32), last_ref[1].astype(jnp.float32)
-    l_re, l_im = later_ref[0].astype(jnp.float32), later_ref[1].astype(jnp.float32)
+    inside = jnp.where(lax.axis_index("tile") == lax.axis_size("tile") - 1, 0.0, 1.0)
+    l_re, l_im = [later_ref[part].astype(jnp.float32) * inside for part in range(2)]
     values = (
         i_re * l_re + i_im * l_im,
         i_im * l_re - i_re * l_im,
@@ -251,6 +251,11 @@
     )(*args)
 
 
+def ring(value, axis, step):
+    count = lax.axis_size(axis)
+    return lax.ppermute(value, axis, [(at, (at + step) % count) for at in range(count)])
+
+
 def swap(value, axis, step):
     return lax.ppermute(value, axis, [(at, at ^ step) for at in range(lax.axis_size(axis))])
 
@@ -268,10 +273,9 @@
     edges_two = swap(edges, "date", 2)
     one = swap(primary, "date", 1)
     halo = shape((2, HALO, cols_n), bf16)
-    inner, outer = call(cut_halo_kernel, (halo, halo), [], (0, 0), secondary)
-    inner = swap(inner, "tile", 1)
-    beyond = [(at, at + 1 if at % 2 else at - 1) for at in range(1, tiles_n - 1)]
-    outer = lax.ppermute(outer, "tile", beyond)
+    down, up = call(cut_halo_kernel, (halo, halo), [], (0, 0), secondary)
+    low = ring(down, "tile", 1)
+    high = ring(up, "tile", -1)
     az_band, rg_band = call(
         bands_kernel,
         (shape((BAND, BAND + 2 * HALO), bf16), shape((3, LANE, LANE), bf16)),
@@ -286,7 +290,7 @@
         shape((2, middle_n + 16, width), bf16),
         [],
         (0, 0),
-        primary, inner,outer,
+        primary, low, high,
     )
     weight = jnp.broadcast_to(margin_mask[rows_n - LAG :].astype(f32)[:, None], (LAG, LANE))
     res = call(
@@ -294,7 +298,7 @@
         shape((dates_n, 2, rows_n, width), bf16),
         [pltpu.VMEM((2, rows_n, cols_n), bf16)],
         (0, 0),
-        secondary, inner, outer, az_band, rg_band,
+        secondary, low, high, az_band, rg_band,
     )
     two = swap(middle, "date", 2)
     margin = shape((2, LAG, cols_n), bf16)
@@ -305,7 +309,7 @@
         (0, 0),
         primary, one, edges_two, edges_three, res,
     )
-    later = passed_along(first, "tile", -1)
+    later = ring(first, "tile", -1)
     stats = call(
         stats_kernel,
         shape((8, LANE), f32),

time: 42.3 us -> 41.1 us (0.972)
  starting transfers between devices: 20.6 us -> 17.3 us
  waiting for transfers between devices: 11.1 us -> 13.3 us
    ppermute x9 -> x8, starting transfers between devices: 18.6 us -> 14.6 us  [swap(): lax.ppermute(value, axis, [(at, at ^ step) for at in range(lax.axis_size(...]
    ppermute x2 -> x3, waiting for transfers between devices: 1.38 us -> 3.13 us  [ring(): lax.ppermute(value, axis, [(at, (at + step) % count) for at in range(coun...]
    ppermute x2 -> x3, starting transfers between devices: 2.09 us -> 2.75 us  [ring(): lax.ppermute(value, axis, [(at, (at + step) % count) for at in range(coun...]
    ppermute x9 -> x8, waiting for transfers between devices: 9.7 us -> 10.1 us  [swap(): lax.ppermute(value, axis, [(at, at ^ step) for at in range(lax.axis_size(...]
  transfers between devices with their start and end apart: 11 -> 11, of which waited for: 7 -> 6; matrix products, arithmetic and copies ran while one was open for 4% -> 4% of each run, Pallas kernels for 8% -> 9%
where the time goes in v10:
time: 41.1 us; the launch traced here: 40.9 us
  starting transfers between devices  17.3 us (42%)
  waiting for transfers between devices  13.3 us (32%)
  Pallas kernels  4.4 us (11%)
  between operations  2.73 us (7%)
  local copies, waits for them, and re-layouts  2.37 us (6%)
  other arithmetic  0.78 us (2%)
    ppermute x8, starting transfers between devices, swap(): lax.ppermute(value, axis, [(at, at ^ step) for at in range(lax.axis_size(...  14.6 us
    ppermute x8, waiting for transfers between devices, swap(): lax.ppermute(value, axis, [(at, at ^ step) for at in range(lax.axis_size(...  10.1 us
    pallas_call x11, Pallas kernels, call(): pl.pallas_call(kernel, out_shape=outs, in_specs=[vmem] * len(args), out_s...  4.4 us
    ppermute x3, waiting for transfers between devices, ring(): lax.ppermute(value, axis, [(at, (at + step) % count) for at in range(coun...  3.13 us
    ppermute x3, starting transfers between devices, ring(): lax.ppermute(value, axis, [(at, (at + step) % count) for at in range(coun...  2.75 us
    unnamed x6, local copies, waits for them, and re-layouts  1.41 us
    slice x1, local copies, waits for them, and re-layouts, fused(): primary[:, :LAG]  0.88 us
  transfers between devices with their start and end apart: 11, of which 6 were waited for; matrix products, arithmetic and copies ran while one was open for 4% of the time, Pallas kernels for 9%

profile of v10, /device:TPU:0, one launch (start us, length us, event | category | flops | bytes accessed | tf_op | source)
XLA Modules:
  0.0 40.9 jit_solution(7638132591416470761)
XLA Ops:
  0.0 3.0 %collective-permute-start.3 = (bf16[2,384,256]{2,1,0:T(8,128)(2,1)}, bf16[2,384,256]{2,1,0:T(8,128)(2,1)S(1)}, u32[]{:S(2)}, u32[]{:S(2)}) collective-permute-start(bf16[2,384,256]{2,1,0:T(8,128)(2,1)} %own_ref.3), channel_id=1, source_target_pairs={{0,1},{1,0},{2,3},{3,2},{4,5},{5,4},{6,7},{7,6},{8,9},{9,8},{10,11... | collective-permute-start | bytes 1179656 | tf_op jit(solution)/shard_map/ppermute | solution.py:260
  3.0 0.9 %fusion = (bf16[2,64,256]{2,1,0:T(8,128)(2,1)S(1)}, bf16[2,64,256]{2,1,0:T(8,128)(2,1)S(1)}) fusion(bf16[2,384,256]{2,1,0:T(8,128)(2,1)} %own_ref.3), kind=kLoop, calls=%fused_computation.2 | loop fusion | bytes 262144 | tf_op jit(solution)/shard_map/slice | solution.py:272
  3.9 2.7 %collective-permute-start.4 = (bf16[2,128,256]{2,1,0:T(8,128)(2,1)S(1)}, bf16[2,128,256]{2,1,0:T(8,128)(2,1)S(1)}, u32[]{:S(2)}, u32[]{:S(2)}) collective-permute-start(bf16[2,128,256]{2,1,0:T(8,128)(2,1)S(1)} %pad_maximum_fusion), channel_id=1, source_target_pairs={{0,2},{1,3},{2,0},{3,1},{4,6},{5,7},{6,4},{7,5},{8,10},{9,11},{10,... | collective-permute-start | bytes 393224 | tf_op jit(solution)/shard_map/ppermute | solution.py:260
  6.6 1.4 %copy-done = bf16[1,2,384,1024]{3,2,1,0:T(8,128)(2,1)S(1)} copy-done((bf16[1,2,384,1024]{3,2,1,0:T(8,128)(2,1)S(1)}, bf16[1,2,384,1024]{3,2,1,0:T(8,128)(2,1)}, u32[]{:S(2)}) %copy-start) | copy-done | bytes 1572888
  8.0 0.1 collective-permute-start
  8.1 2.6 %collective-permute-start.1 = (bf16[2,32,1024]{2,1,0:T(8,128)(2,1)S(1)}, bf16[2,32,1024]{2,1,0:T(8,128)(2,1)S(1)}, u32[]{:S(2)}, u32[]{:S(2)}) collective-permute-start(bf16[2,32,1024]{2,1,0:T(8,128)(2,1)S(1)} %get-tuple-element.13), channel_id=1, source_target_pairs={{0,28},{4,0},{8,4},{12,8},{16,12},{20,16},{24,20},{28,24},{1,29},{... | collective-permute-start | bytes 393224 | tf_op jit(solution)/shard_map/ppermute | solution.py:256
  13.3 0.4 shard_map.75
  13.7 0.7 %collective-permute-done.4.block_ref.two_ref = bf16[2,128,256]{2,1,0:T(8,128)(2,1)S(1)} collective-permute-done((bf16[2,128,256]{2,1,0:T(8,128)(2,1)S(1)}, bf16[2,128,256]{2,1,0:T(8,128)(2,1)S(1)}, u32[]{:S(2)}, u32[]{:S(2)}) %collective-permute-start.4) | collective-permute-done | bytes 131104 | tf_op jit(solution)/shard_map/ppermute | solution.py:260
  14.4 3.6 %collective-permute-start.5 = (bf16[2,128,256]{2,1,0:T(8,128)(2,1)S(1)}, bf16[2,128,256]{2,1,0:T(8,128)(2,1)S(1)}, u32[]{:S(2)}, u32[]{:S(2)}) collective-permute-start(bf16[2,128,256]{2,1,0:T(8,128)(2,1)S(1)} %shard_map.76), channel_id=1, source_target_pairs={{0,1},{1,0},{2,3},{3,2},{4,5},{5,4},{6,7},{7,6},{8,9},{9,8},{10,11... | collective-permute-start | bytes 393224 | tf_op jit(solution)/shard_map/ppermute | solution.py:260
  18.0 0.0 collective-permute-done.refs_0_.low_ref
  18.0 0.0 collective-permute-done.1.refs_1_.high_ref
  18.0 0.1 collective-permute-start.2
  18.1 1.4 %shard_map.77.res_ref = bf16[4,2,384,256]{3,2,1,0:T(8,128)(2,1)S(1)} custom-call(bf16[1,2,384,1024]{3,2,1,0:T(8,128)(2,1)S(1)} %copy-done.1, bf16[2,32,1024]{2,1,0:T(8,128)(2,1)S(1)} %collective-permute-done.refs_0_.low_ref, bf16[2,32,1024]{2,1,0:T(8,128)(2,1)S(1)} %collective-permute-done.1.refs_1_.high_ref, ...), custom_call_target="tpu_custom_call" | custom-call | tf_op jit(solution)/shard_map/pallas_call | solution.py:243
  19.5 2.4 %collective-permute-done.5.three_ref = bf16[2,128,256]{2,1,0:T(8,128)(2,1)S(1)} collective-permute-done((bf16[2,128,256]{2,1,0:T(8,128)(2,1)S(1)}, bf16[2,128,256]{2,1,0:T(8,128)(2,1)S(1)}, u32[]{:S(2)}, u32[]{:S(2)}) %collective-permute-start.5) | collective-permute-done | bytes 131104 | tf_op jit(solution)/shard_map/ppermute | solution.py:260
  21.9 0.0 collective-permute-done.3.one_ref
  21.9 0.5 %shard_map.78 = (bf16[2,64,1024]{2,1,0:T(8,128)(2,1)S(1)}, bf16[2,64,1024]{2,1,0:T(8,128)(2,1)S(1)}, f32[2,64,128]{2,1,0:T(8,128)S(1)}) custom-call(bf16[2,384,256]{2,1,0:T(8,128)(2,1)S(1)} %copy-done.2, bf16[2,384,256]{2,1,0:T(8,128)(2,1)S(1)} %collective-permute-done.3.one_ref, bf16[2,128,256]{2,1,0:T(8,128)(2,1)S(1)} %collective-permute-done.4.block_ref.two_ref, ...), custom_call_target="tpu_custom_call" | custom-call | tf_op jit(solution)/shard_map/pallas_call | solution.py:243
  22.5 0.1 collective-permute-start.6
  22.5 0.8 %slice_convert_fusion = f32[64]{0:T(128)S(1)} fusion(s32[384]{0:T(512)} %param.9), kind=kLoop, calls=%fused_computation.1 | loop fusion | flops 64 | bytes 512 | tf_op jit(solution)/shard_map/convert_element_type | solution.py:295
  23.3 3.1 %collective-permute-done.6.later_ref = bf16[2,64,1024]{2,1,0:T(8,128)(2,1)S(1)} collective-permute-done((bf16[2,64,1024]{2,1,0:T(8,128)(2,1)S(1)}, bf16[2,64,1024]{2,1,0:T(8,128)(2,1)S(1)}, u32[]{:S(2)}, u32[]{:S(2)}) %collective-permute-start.6) | collective-permute-done | bytes 262176 | tf_op jit(solution)/shard_map/ppermute | solution.py:256
  26.4 0.1 broadcast_in_dim.2.weight_ref
  26.5 0.4 shard_map.79
  26.9 2.1 %collective-permute-start.7 = (f32[8,128]{1,0:T(8,128)S(1)}, f32[8,128]{1,0:T(8,128)S(1)}, u32[]{:S(2)}, u32[]{:S(2)}) collective-permute-start(f32[8,128]{1,0:T(8,128)S(1)} %shard_map.79), channel_id=1, source_target_pairs={{0,4},{4,0},{8,12},{12,8},{16,20},{20,16},{24,28},{28,24},{1,5},{5... | collective-permute-start | bytes 12296 | tf_op jit(solution)/shard_map/ppermute | solution.py:260
  29.0 3.2 %collective-permute-done.2.block_ref.two_ref = bf16[2,272,256]{2,1,0:T(8,128)(2,1)S(1)} collective-permute-done((bf16[2,272,256]{2,1,0:T(8,128)(2,1)S(1)}, bf16[2,272,256]{2,1,0:T(8,128)(2,1)S(1)}, u32[]{:S(2)}, u32[]{:S(2)}) %collective-permute-start.2) | collective-permute-done | bytes 278560 | tf_op jit(solution)/shard_map/ppermute | solution.py:260
  32.2 0.0 collective-permute-done.7.awaited_ref
  32.2 0.1 collective-permute-start.8
  32.3 1.6 %collective-permute-start.9 = (f32[8,128]{1,0:T(8,128)S(1)}, f32[8,128]{1,0:T(8,128)S(1)}, u32[]{:S(2)}, u32[]{:S(2)}) collective-permute-start(f32[8,128]{1,0:T(8,128)S(1)} %add.6), channel_id=1, source_target_pairs={{0,8},{4,12},{8,0},{12,4},{16,24},{20,28},{24,16},{28,20},{1,9},{5... | collective-permute-start | bytes 12296 | tf_op jit(solution)/shard_map/ppermute | solution.py:260
  33.9 0.6 %shard_map.81.before_ref = f32[2,256,128]{2,1,0:T(8,128)S(1)} custom-call(bf16[2,384,256]{2,1,0:T(8,128)(2,1)S(1)} %copy-done.2, bf16[2,384,256]{2,1,0:T(8,128)(2,1)S(1)} %collective-permute-done.3.one_ref, bf16[2,272,256]{2,1,0:T(8,128)(2,1)S(1)} %collective-permute-done.2.block_ref.two_ref, bf16[4,2,384,256]{3,2,1,0:T(8,128)(2,1)S(1)} %shard_map.77.res_ref), custom_call_target="tpu_custom_call" | custom-call | flops 134217728 | bytes 3145728 | tf_op jit(solution)/shard_map/pallas_call | solution.py:243
  34.5 1.5 %collective-permute-done.9 = f32[8,128]{1,0:T(8,128)S(1)} collective-permute-done((f32[8,128]{1,0:T(8,128)S(1)}, f32[8,128]{1,0:T(8,128)S(1)}, u32[]{:S(2)}, u32[]{:S(2)}) %collective-permute-start.9) | collective-permute-done | bytes 4128 | tf_op jit(solution)/shard_map/ppermute | solution.py:260
  36.0 1.5 %collective-permute-start.10 = (f32[8,128]{1,0:T(8,128)S(1)}, f32[8,128]{1,0:T(8,128)S(1)}, u32[]{:S(2)}, u32[]{:S(2)}) collective-permute-start(f32[8,128]{1,0:T(8,128)S(1)} %add.7.mine_ref), channel_id=1, source_target_pairs={{0,16},{4,20},{8,24},{12,28},{16,0},{20,4},{24,8},{28,12},{1,17},{... | collective-permute-start | bytes 12296 | tf_op jit(solution)/shard_map/ppermute | solution.py:260
  37.5 2.2 %collective-permute-done.8.three_ref = bf16[2,256,256]{2,1,0:T(8,128)(2,1)S(1)} collective-permute-done((bf16[2,256,256]{2,1,0:T(8,128)(2,1)S(1)}, bf16[2,256,256]{2,1,0:T(8,128)(2,1)S(1)}, u32[]{:S(2)}, u32[]{:S(2)}) %collective-permute-start.8) | collective-permute-done | bytes 262176 | tf_op jit(solution)/shard_map/ppermute | solution.py:260
  39.8 0.3 shard_map.82.looks_ref
  40.0 0.8 %shard_map.83 = f32[1,2,192,128]{3,2,1,0:T(8,128)} custom-call(f32[2,192,128]{2,1,0:T(8,128)S(1)} %shard_map.82.looks_ref, f32[8,128]{1,0:T(8,128)S(1)} %add.7.mine_ref, f32[8,128]{1,0:T(8,128)S(1)} %collective-permute-done.10.other_ref), custom_call_target="tpu_custom_call" | custom-call | flops 393216 | bytes 393216 | tf_op jit(solution)/shard_map/pallas_call | solution.py:243
  (13 shorter events, 0.1 us)
Async XLA Ops:
  0.0 18.0 %copy-start.2 = (bf16[2,384,256]{2,1,0:T(8,128)(2,1)S(1)}, bf16[2,384,256]{2,1,0:T(8,128)(2,1)}, u32[]{:S(2)}) copy-start(bf16[2,384,256]{2,1,0:T(8,128)(2,1)} %own_ref.3) | copy-start | bytes 1179652
  0.0 21.9 %collective-permute-start.3 = (bf16[2,384,256]{2,1,0:T(8,128)(2,1)}, bf16[2,384,256]{2,1,0:T(8,128)(2,1)S(1)}, u32[]{:S(2)}, u32[]{:S(2)}) collective-permute-start(bf16[2,384,256]{2,1,0:T(8,128)(2,1)} %own_ref.3), channel_id=1, source_target_pairs={{0,1},{1,0},{2,3},{3,2},{4,5},{5,4},{6,7},{7,6},{8,9},{9,8},{10,11... | collective-permute-start | bytes 1179656 | tf_op jit(solution)/shard_map/ppermute | solution.py:260
  3.9 10.5 %collective-permute-start.4 = (bf16[2,128,256]{2,1,0:T(8,128)(2,1)S(1)}, bf16[2,128,256]{2,1,0:T(8,128)(2,1)S(1)}, u32[]{:S(2)}, u32[]{:S(2)}) collective-permute-start(bf16[2,128,256]{2,1,0:T(8,128)(2,1)S(1)} %pad_maximum_fusion), channel_id=1, source_target_pairs={{0,2},{1,3},{2,0},{3,1},{4,6},{5,7},{6,4},{7,5},{8,10},{9,11},{10,... | collective-permute-start | bytes 393224 | tf_op jit(solution)/shard_map/ppermute | solution.py:260
  6.6 1.4 %copy-start = (bf16[1,2,384,1024]{3,2,1,0:T(8,128)(2,1)S(1)}, bf16[1,2,384,1024]{3,2,1,0:T(8,128)(2,1)}, u32[]{:S(2)}) copy-start(bf16[1,2,384,1024]{3,2,1,0:T(8,128)(2,1)} %sec_ref.3) | copy-start | bytes 4718596
  8.0 10.1 %copy-start.1 = (bf16[1,2,384,1024]{3,2,1,0:T(8,128)(2,1)S(1)}, bf16[1,2,384,1024]{3,2,1,0:T(8,128)(2,1)}, u32[]{:S(2)}) copy-start(bf16[1,2,384,1024]{3,2,1,0:T(8,128)(2,1)} %sec_ref.3) | copy-start | bytes 4718596
  8.0 10.0 %collective-permute-start = (bf16[2,32,1024]{2,1,0:T(8,128)(2,1)S(1)}, bf16[2,32,1024]{2,1,0:T(8,128)(2,1)S(1)}, u32[]{:S(2)}, u32[]{:S(2)}) collective-permute-start(bf16[2,32,1024]{2,1,0:T(8,128)(2,1)S(1)} %get-tuple-element.12), channel_id=1, source_target_pairs={{0,4},{4,8},{8,12},{12,16},{16,20},{20,24},{24,28},{28,0},{1,5},{5... | collective-permute-start | bytes 393224 | tf_op jit(solution)/shard_map/ppermute | solution.py:256
  8.1 9.9 %collective-permute-start.1 = (bf16[2,32,1024]{2,1,0:T(8,128)(2,1)S(1)}, bf16[2,32,1024]{2,1,0:T(8,128)(2,1)S(1)}, u32[]{:S(2)}, u32[]{:S(2)}) collective-permute-start(bf16[2,32,1024]{2,1,0:T(8,128)(2,1)S(1)} %get-tuple-element.13), channel_id=1, source_target_pairs={{0,28},{4,0},{8,4},{12,8},{16,12},{20,16},{24,20},{28,24},{1,29},{... | collective-permute-start | bytes 393224 | tf_op jit(solution)/shard_map/ppermute | solution.py:256
  14.4 7.5 %collective-permute-start.5 = (bf16[2,128,256]{2,1,0:T(8,128)(2,1)S(1)}, bf16[2,128,256]{2,1,0:T(8,128)(2,1)S(1)}, u32[]{:S(2)}, u32[]{:S(2)}) collective-permute-start(bf16[2,128,256]{2,1,0:T(8,128)(2,1)S(1)} %shard_map.76), channel_id=1, source_target_pairs={{0,1},{1,0},{2,3},{3,2},{4,5},{5,4},{6,7},{7,6},{8,9},{9,8},{10,11... | collective-permute-start | bytes 393224 | tf_op jit(solution)/shard_map/ppermute | solution.py:260
  18.0 14.2 %collective-permute-start.2 = (bf16[2,272,256]{2,1,0:T(8,128)(2,1)S(1)}, bf16[2,272,256]{2,1,0:T(8,128)(2,1)S(1)}, u32[]{:S(2)}, u32[]{:S(2)}) collective-permute-start(bf16[2,272,256]{2,1,0:T(8,128)(2,1)S(1)} %shard_map.74), channel_id=1, source_target_pairs={{0,2},{1,3},{2,0},{3,1},{4,6},{5,7},{6,4},{7,5},{8,10},{9,11},{10,... | collective-permute-start | bytes 835592 | tf_op jit(solution)/shard_map/ppermute | solution.py:260
  22.5 3.9 %collective-permute-start.6 = (bf16[2,64,1024]{2,1,0:T(8,128)(2,1)S(1)}, bf16[2,64,1024]{2,1,0:T(8,128)(2,1)S(1)}, u32[]{:S(2)}, u32[]{:S(2)}) collective-permute-start(bf16[2,64,1024]{2,1,0:T(8,128)(2,1)S(1)} %get-tuple-element.17), channel_id=1, source_target_pairs={{0,28},{4,0},{8,4},{12,8},{16,12},{20,16},{24,20},{28,24},{1,29},{... | collective-permute-start | bytes 786440 | tf_op jit(solution)/shard_map/ppermute | solution.py:256
  26.9 5.4 %collective-permute-start.7 = (f32[8,128]{1,0:T(8,128)S(1)}, f32[8,128]{1,0:T(8,128)S(1)}, u32[]{:S(2)}, u32[]{:S(2)}) collective-permute-start(f32[8,128]{1,0:T(8,128)S(1)} %shard_map.79), channel_id=1, source_target_pairs={{0,4},{4,0},{8,12},{12,8},{16,20},{20,16},{24,28},{28,24},{1,5},{5... | collective-permute-start | bytes 12296 | tf_op jit(solution)/shard_map/ppermute | solution.py:260
  32.2 7.5 %collective-permute-start.8 = (bf16[2,256,256]{2,1,0:T(8,128)(2,1)S(1)}, bf16[2,256,256]{2,1,0:T(8,128)(2,1)S(1)}, u32[]{:S(2)}, u32[]{:S(2)}) collective-permute-start(bf16[2,256,256]{2,1,0:T(8,128)(2,1)S(1)} %shard_map.80), channel_id=1, source_target_pairs={{0,1},{1,0},{2,3},{3,2},{4,5},{5,4},{6,7},{7,6},{8,9},{9,8},{10,11... | collective-permute-start | bytes 786440 | tf_op jit(solution)/shard_map/ppermute | solution.py:260
  32.3 3.7 %collective-permute-start.9 = (f32[8,128]{1,0:T(8,128)S(1)}, f32[8,128]{1,0:T(8,128)S(1)}, u32[]{:S(2)}, u32[]{:S(2)}) collective-permute-start(f32[8,128]{1,0:T(8,128)S(1)} %add.6), channel_id=1, source_target_pairs={{0,8},{4,12},{8,0},{12,4},{16,24},{20,28},{24,16},{28,20},{1,9},{5... | collective-permute-start | bytes 12296 | tf_op jit(solution)/shard_map/ppermute | solution.py:260
  36.0 4.0 %collective-permute-start.10 = (f32[8,128]{1,0:T(8,128)S(1)}, f32[8,128]{1,0:T(8,128)S(1)}, u32[]{:S(2)}, u32[]{:S(2)}) collective-permute-start(f32[8,128]{1,0:T(8,128)S(1)} %add.7.mine_ref), channel_id=1, source_target_pairs={{0,16},{4,20},{8,24},{12,28},{16,0},{20,4},{24,8},{28,12},{1,17},{... | collective-permute-start | bytes 12296 | tf_op jit(solution)/shard_map/ppermute | solution.py:260

commit v11 on v10

--- a/solution.py
+++ b/solution.py
@@ -138,7 +138,7 @@
     looks_n = looks_ref.shape[2]
     totals = [None, None]
     for step, (prim_ref, starts) in enumerate(
-        ((own_ref, whole), (one_ref, whole), (two_ref, edges), (three_ref, edges))
+        ((own_ref, whole), (one_ref, edges), (two_ref, edges), (three_ref, edges))
     ):
         block = jnp.bitwise_xor(here, step)
         select = look_columns(width, block, looks_n)
@@ -271,7 +271,7 @@
     middle_n = rows_n - 2 * LAG
     edges = jnp.concatenate([primary[:, :LAG], primary[:, rows_n - LAG :]], axis=1)
     edges_two = swap(edges, "date", 2)
-    one = swap(primary, "date", 1)
+    edges_one = swap(edges, "date", 1)
     halo = shape((2, HALO, cols_n), bf16)
     down, up = call(cut_halo_kernel, (halo, halo), [], (0, 0), secondary)
     low = ring(down, "tile", 1)
@@ -290,7 +290,7 @@
         shape((2, middle_n + 16, width), bf16),
         [],
         (0, 0),
-        primary, low, high,
+        primary, edges_two,
     )
     weight = jnp.broadcast_to(margin_mask[rows_n - LAG :].astype(f32)[:, None], (LAG, LANE))
     res = call(
@@ -300,14 +300,14 @@
         (0, 0),
         secondary, low, high, az_band, rg_band,
     )
-    two = swap(middle, "date", 2)
+    two, one = [swap(middle, "date", step) for step in (2, 1)]
     margin = shape((2, LAG, cols_n), bf16)
     first, last, looks = call(
         margin_kernel,
         (margin, margin, shape((2, 2 * LAG // LA, looks_n), f32)),
         [pltpu.VMEM((2, 2 * LAG, looks_n), f32)],
         (0, 0),
-        primary, one, edges_two, edges_three, res,
+        primary, edges_one, edges_two, edges_three, res,
     )
     later = ring(first, "tile", -1)
     stats = call(

time: 41.1 us -> 40.8 us (level)
  starting transfers between devices: 17.3 us -> 15.8 us
  waiting for transfers between devices: 13.3 us -> 14.4 us
    ppermute x8 -> x9, starting transfers between devices: 14.6 us -> 13.1 us  [swap(): lax.ppermute(value, axis, [(at, at ^ step) for at in range(lax.axis_size(...]
    ppermute x8 -> x9, waiting for transfers between devices: 10.1 us -> 11.5 us  [swap(): lax.ppermute(value, axis, [(at, at ^ step) for at in range(lax.axis_size(...]
  transfers between devices with their start and end apart: 11 -> 12, of which waited for: 6 -> 5; matrix products, arithmetic and copies ran while one was open for 4% -> 2% of each run, Pallas kernels for 9% -> 9%
where the time goes in v11:
time: 40.8 us; the launch traced here: 40.6 us
  starting transfers between devices  15.8 us (39%)
  waiting for transfers between devices  14.4 us (35%)
  Pallas kernels  4.41 us (11%)
  between operations  2.74 us (7%)
  local copies, waits for them, and re-layouts  2.42 us (6%)
  other arithmetic  0.77 us (2%)
    ppermute x9, starting transfers between devices, swap(): lax.ppermute(value, axis, [(at, at ^ step) for at in range(lax.axis_size(...  13.1 us
    ppermute x9, waiting for transfers between devices, swap(): lax.ppermute(value, axis, [(at, at ^ step) for at in range(lax.axis_size(...  11.5 us
    pallas_call x11, Pallas kernels, call(): pl.pallas_call(kernel, out_shape=outs, in_specs=[vmem] * len(args), out_s...  4.41 us
    ppermute x3, waiting for transfers between devices, ring(): lax.ppermute(value, axis, [(at, (at + step) % count) for at in range(coun...  2.93 us
    ppermute x3, starting transfers between devices, ring(): lax.ppermute(value, axis, [(at, (at + step) % count) for at in range(coun...  2.75 us
    unnamed x6, local copies, waits for them, and re-layouts  1.41 us
    slice x1, local copies, waits for them, and re-layouts, fused(): primary[:, :LAG]  0.93 us
  transfers between devices with their start and end apart: 12, of which 5 were waited for; matrix products, arithmetic and copies ran while one was open for 2% of the time, Pallas kernels for 9%

profile of v11, /device:TPU:0, one launch (start us, length us, event | category | flops | bytes accessed | tf_op | source)
XLA Modules:
  0.0 40.6 jit_solution(3779804674763344557)
XLA Ops:
  0.0 0.9 %fusion = (bf16[2,64,256]{2,1,0:T(8,128)(2,1)S(1)}, bf16[2,64,256]{2,1,0:T(8,128)(2,1)S(1)}) fusion(bf16[2,384,256]{2,1,0:T(8,128)(2,1)} %own_ref.3), kind=kLoop, calls=%fused_computation.2 | loop fusion | bytes 262144 | tf_op jit(solution)/shard_map/slice | solution.py:272
  1.0 4.1 %collective-permute-start = (bf16[2,128,256]{2,1,0:T(8,128)(2,1)S(1)}, bf16[2,128,256]{2,1,0:T(8,128)(2,1)S(1)}, u32[]{:S(2)}, u32[]{:S(2)}) collective-permute-start(bf16[2,128,256]{2,1,0:T(8,128)(2,1)S(1)} %pad_maximum_fusion), channel_id=1, source_target_pairs={{0,2},{1,3},{2,0},{3,1},{4,6},{5,7},{6,4},{7,5},{8,10},{9,11},{10,... | collective-permute-start | bytes 393224 | tf_op jit(solution)/shard_map/ppermute | solution.py:260
  5.1 1.6 %collective-permute-start.2 = (bf16[2,128,256]{2,1,0:T(8,128)(2,1)S(1)}, bf16[2,128,256]{2,1,0:T(8,128)(2,1)S(1)}, u32[]{:S(2)}, u32[]{:S(2)}) collective-permute-start(bf16[2,128,256]{2,1,0:T(8,128)(2,1)S(1)} %pad_maximum_fusion), channel_id=1, source_target_pairs={{0,1},{1,0},{2,3},{3,2},{4,5},{5,4},{6,7},{7,6},{8,9},{9,8},{10,11... | collective-permute-start | bytes 393224 | tf_op jit(solution)/shard_map/ppermute | solution.py:260
  6.6 1.4 %copy-done = bf16[1,2,384,1024]{3,2,1,0:T(8,128)(2,1)S(1)} copy-done((bf16[1,2,384,1024]{3,2,1,0:T(8,128)(2,1)S(1)}, bf16[1,2,384,1024]{3,2,1,0:T(8,128)(2,1)}, u32[]{:S(2)}) %copy-start) | copy-done | bytes 1572888
  8.1 0.1 collective-permute-start.4
  8.1 2.6 %collective-permute-start.5 = (bf16[2,32,1024]{2,1,0:T(8,128)(2,1)S(1)}, bf16[2,32,1024]{2,1,0:T(8,128)(2,1)S(1)}, u32[]{:S(2)}, u32[]{:S(2)}) collective-permute-start(bf16[2,32,1024]{2,1,0:T(8,128)(2,1)S(1)} %get-tuple-element.14), channel_id=1, source_target_pairs={{0,28},{4,0},{8,4},{12,8},{16,12},{20,16},{24,20},{28,24},{1,29},{... | collective-permute-start | bytes 393224 | tf_op jit(solution)/shard_map/ppermute | solution.py:256
  13.4 0.4 shard_map.74
  13.8 0.5 %collective-permute-start.3 = (bf16[2,128,256]{2,1,0:T(8,128)(2,1)S(1)}, bf16[2,128,256]{2,1,0:T(8,128)(2,1)S(1)}, u32[]{:S(2)}, u32[]{:S(2)}) collective-permute-start(bf16[2,128,256]{2,1,0:T(8,128)(2,1)S(1)} %shard_map.75), channel_id=1, source_target_pairs={{0,1},{1,0},{2,3},{3,2},{4,5},{5,4},{6,7},{7,6},{8,9},{9,8},{10,11... | collective-permute-start | bytes 393224 | tf_op jit(solution)/shard_map/ppermute | solution.py:260
  14.3 1.3 %collective-permute-start.1 = (bf16[2,272,256]{2,1,0:T(8,128)(2,1)S(1)}, bf16[2,272,256]{2,1,0:T(8,128)(2,1)S(1)}, u32[]{:S(2)}, u32[]{:S(2)}) collective-permute-start(bf16[2,272,256]{2,1,0:T(8,128)(2,1)S(1)} %shard_map.73), channel_id=1, source_target_pairs={{0,2},{1,3},{2,0},{3,1},{4,6},{5,7},{6,4},{7,5},{8,10},{9,11},{10,... | collective-permute-start | bytes 835592 | tf_op jit(solution)/shard_map/ppermute | solution.py:260
  15.6 0.0 collective-permute-done.4.low_ref
  15.6 0.0 collective-permute-done.5.high_ref
  15.6 1.4 %shard_map.77.res_ref = bf16[4,2,384,256]{3,2,1,0:T(8,128)(2,1)S(1)} custom-call(bf16[1,2,384,1024]{3,2,1,0:T(8,128)(2,1)S(1)} %copy-done.1, bf16[2,32,1024]{2,1,0:T(8,128)(2,1)S(1)} %collective-permute-done.4.low_ref, bf16[2,32,1024]{2,1,0:T(8,128)(2,1)S(1)} %collective-permute-done.5.high_ref, bf16[128,192]{1,0:T(8,128)(2,1)S(1)} %get-tuple-element.12.awaited_ref.az_ref, ...), custom_call_target="tpu_custom_call" | custom-call | tf_op jit(solution)/shard_map/pallas_call | solution.py:243
  17.1 0.0 collective-permute-done.2.one_ref
  17.1 3.3 %collective-permute-done.3.three_ref = bf16[2,128,256]{2,1,0:T(8,128)(2,1)S(1)} collective-permute-done((bf16[2,128,256]{2,1,0:T(8,128)(2,1)S(1)}, bf16[2,128,256]{2,1,0:T(8,128)(2,1)S(1)}, u32[]{:S(2)}, u32[]{:S(2)}) %collective-permute-start.3) | collective-permute-done | bytes 131104 | tf_op jit(solution)/shard_map/ppermute | solution.py:260
  20.4 0.5 %shard_map.78 = (bf16[2,64,1024]{2,1,0:T(8,128)(2,1)S(1)}, bf16[2,64,1024]{2,1,0:T(8,128)(2,1)S(1)}, f32[2,64,128]{2,1,0:T(8,128)S(1)}) custom-call(bf16[2,384,256]{2,1,0:T(8,128)(2,1)S(1)} %copy-done.2, bf16[2,128,256]{2,1,0:T(8,128)(2,1)S(1)} %collective-permute-done.2.one_ref, bf16[2,128,256]{2,1,0:T(8,128)(2,1)S(1)} %collective-permute-done.refs_0_.block_ref.two_ref, ...), custom_call_target="tpu_custom_call" | custom-call | tf_op jit(solution)/shard_map/pallas_call | solution.py:243
  20.9 0.1 collective-permute-start.6
  21.0 0.2 collective-permute-start.9
  21.2 0.8 %slice_convert_fusion = f32[64]{0:T(128)S(1)} fusion(s32[384]{0:T(512)} %param.9), kind=kLoop, calls=%fused_computation.1 | loop fusion | flops 64 | bytes 512 | tf_op jit(solution)/shard_map/convert_element_type | solution.py:295
  21.9 2.9 %collective-permute-done.6.later_ref = bf16[2,64,1024]{2,1,0:T(8,128)(2,1)S(1)} collective-permute-done((bf16[2,64,1024]{2,1,0:T(8,128)(2,1)S(1)}, bf16[2,64,1024]{2,1,0:T(8,128)(2,1)S(1)}, u32[]{:S(2)}, u32[]{:S(2)}) %collective-permute-start.6) | collective-permute-done | bytes 262176 | tf_op jit(solution)/shard_map/ppermute | solution.py:256
  24.8 0.1 broadcast_in_dim.2.weight_ref
  24.9 0.4 shard_map.79
  25.3 2.1 %collective-permute-start.7 = (f32[8,128]{1,0:T(8,128)S(1)}, f32[8,128]{1,0:T(8,128)S(1)}, u32[]{:S(2)}, u32[]{:S(2)}) collective-permute-start(f32[8,128]{1,0:T(8,128)S(1)} %shard_map.79), channel_id=1, source_target_pairs={{0,4},{4,0},{8,12},{12,8},{16,20},{20,16},{24,28},{28,24},{1,5},{5... | collective-permute-start | bytes 12296 | tf_op jit(solution)/shard_map/ppermute | solution.py:260
  27.4 1.2 %collective-permute-done.1.block_ref.two_ref = bf16[2,272,256]{2,1,0:T(8,128)(2,1)S(1)} collective-permute-done((bf16[2,272,256]{2,1,0:T(8,128)(2,1)S(1)}, bf16[2,272,256]{2,1,0:T(8,128)(2,1)S(1)}, u32[]{:S(2)}, u32[]{:S(2)}) %collective-permute-start.1) | collective-permute-done | bytes 278560 | tf_op jit(solution)/shard_map/ppermute | solution.py:260
  28.6 0.0 collective-permute-done.7.awaited_ref
  28.7 0.1 collective-permute-start.8
  28.7 1.6 %collective-permute-start.10 = (f32[8,128]{1,0:T(8,128)S(1)}, f32[8,128]{1,0:T(8,128)S(1)}, u32[]{:S(2)}, u32[]{:S(2)}) collective-permute-start(f32[8,128]{1,0:T(8,128)S(1)} %add.6), channel_id=1, source_target_pairs={{0,8},{4,12},{8,0},{12,4},{16,24},{20,28},{24,16},{28,20},{1,9},{5... | collective-permute-start | bytes 12296 | tf_op jit(solution)/shard_map/ppermute | solution.py:260
  30.3 4.0 %collective-permute-done.9.one_ref = bf16[2,272,256]{2,1,0:T(8,128)(2,1)S(1)} collective-permute-done((bf16[2,272,256]{2,1,0:T(8,128)(2,1)S(1)}, bf16[2,272,256]{2,1,0:T(8,128)(2,1)S(1)}, u32[]{:S(2)}, u32[]{:S(2)}) %collective-permute-start.9) | collective-permute-done | bytes 278560 | tf_op jit(solution)/shard_map/ppermute | solution.py:260
  34.3 0.6 %shard_map.81.before_ref = f32[2,256,128]{2,1,0:T(8,128)S(1)} custom-call(bf16[2,384,256]{2,1,0:T(8,128)(2,1)S(1)} %copy-done.2, bf16[2,272,256]{2,1,0:T(8,128)(2,1)S(1)} %collective-permute-done.9.one_ref, bf16[2,272,256]{2,1,0:T(8,128)(2,1)S(1)} %collective-permute-done.1.block_ref.two_ref, bf16[4,2,384,256]{3,2,1,0:T(8,128)(2,1)S(1)} %shard_map.77.res_ref), custom_call_target="tpu_custom_call" | custom-call | flops 134217728 | bytes 3145728 | tf_op jit(solution)/shard_map/pallas_call | solution.py:243
  34.9 1.6 %collective-permute-start.11 = (f32[8,128]{1,0:T(8,128)S(1)}, f32[8,128]{1,0:T(8,128)S(1)}, u32[]{:S(2)}, u32[]{:S(2)}) collective-permute-start(f32[8,128]{1,0:T(8,128)S(1)} %add.7.mine_ref), channel_id=1, source_target_pairs={{0,16},{4,20},{8,24},{12,28},{16,0},{20,4},{24,8},{28,12},{1,17},{... | collective-permute-start | bytes 12296 | tf_op jit(solution)/shard_map/ppermute | solution.py:260
  36.5 3.0 %collective-permute-done.8.three_ref = bf16[2,256,256]{2,1,0:T(8,128)(2,1)S(1)} collective-permute-done((bf16[2,256,256]{2,1,0:T(8,128)(2,1)S(1)}, bf16[2,256,256]{2,1,0:T(8,128)(2,1)S(1)}, u32[]{:S(2)}, u32[]{:S(2)}) %collective-permute-start.8) | collective-permute-done | bytes 262176 | tf_op jit(solution)/shard_map/ppermute | solution.py:260
  39.4 0.3 shard_map.82.looks_ref
  39.7 0.8 %shard_map.83 = f32[1,2,192,128]{3,2,1,0:T(8,128)} custom-call(f32[2,192,128]{2,1,0:T(8,128)S(1)} %shard_map.82.looks_ref, f32[8,128]{1,0:T(8,128)S(1)} %add.7.mine_ref, f32[8,128]{1,0:T(8,128)S(1)} %collective-permute-done.11.other_ref), custom_call_target="tpu_custom_call" | custom-call | flops 393216 | bytes 393216 | tf_op jit(solution)/shard_map/pallas_call | solution.py:243
  (15 shorter events, 0.1 us)
Async XLA Ops:
  0.0 14.3 %copy-start.2 = (bf16[2,384,256]{2,1,0:T(8,128)(2,1)S(1)}, bf16[2,384,256]{2,1,0:T(8,128)(2,1)}, u32[]{:S(2)}) copy-start(bf16[2,384,256]{2,1,0:T(8,128)(2,1)} %own_ref.3) | copy-start | bytes 1179652
  1.0 12.8 %collective-permute-start = (bf16[2,128,256]{2,1,0:T(8,128)(2,1)S(1)}, bf16[2,128,256]{2,1,0:T(8,128)(2,1)S(1)}, u32[]{:S(2)}, u32[]{:S(2)}) collective-permute-start(bf16[2,128,256]{2,1,0:T(8,128)(2,1)S(1)} %pad_maximum_fusion), channel_id=1, source_target_pairs={{0,2},{1,3},{2,0},{3,1},{4,6},{5,7},{6,4},{7,5},{8,10},{9,11},{10,... | collective-permute-start | bytes 393224 | tf_op jit(solution)/shard_map/ppermute | solution.py:260
  5.1 12.0 %collective-permute-start.2 = (bf16[2,128,256]{2,1,0:T(8,128)(2,1)S(1)}, bf16[2,128,256]{2,1,0:T(8,128)(2,1)S(1)}, u32[]{:S(2)}, u32[]{:S(2)}) collective-permute-start(bf16[2,128,256]{2,1,0:T(8,128)(2,1)S(1)} %pad_maximum_fusion), channel_id=1, source_target_pairs={{0,1},{1,0},{2,3},{3,2},{4,5},{5,4},{6,7},{7,6},{8,9},{9,8},{10,11... | collective-permute-start | bytes 393224 | tf_op jit(solution)/shard_map/ppermute | solution.py:260
  6.6 1.4 %copy-start = (bf16[1,2,384,1024]{3,2,1,0:T(8,128)(2,1)S(1)}, bf16[1,2,384,1024]{3,2,1,0:T(8,128)(2,1)}, u32[]{:S(2)}) copy-start(bf16[1,2,384,1024]{3,2,1,0:T(8,128)(2,1)} %sec_ref.3) | copy-start | bytes 4718596
  8.0 7.6 %copy-start.1 = (bf16[1,2,384,1024]{3,2,1,0:T(8,128)(2,1)S(1)}, bf16[1,2,384,1024]{3,2,1,0:T(8,128)(2,1)}, u32[]{:S(2)}) copy-start(bf16[1,2,384,1024]{3,2,1,0:T(8,128)(2,1)} %sec_ref.3) | copy-start | bytes 4718596
  8.1 7.6 %collective-permute-start.4 = (bf16[2,32,1024]{2,1,0:T(8,128)(2,1)S(1)}, bf16[2,32,1024]{2,1,0:T(8,128)(2,1)S(1)}, u32[]{:S(2)}, u32[]{:S(2)}) collective-permute-start(bf16[2,32,1024]{2,1,0:T(8,128)(2,1)S(1)} %get-tuple-element.13), channel_id=1, source_target_pairs={{0,4},{4,8},{8,12},{12,16},{16,20},{20,24},{24,28},{28,0},{1,5},{5... | collective-permute-start | bytes 393224 | tf_op jit(solution)/shard_map/ppermute | solution.py:256
  8.1 7.5 %collective-permute-start.5 = (bf16[2,32,1024]{2,1,0:T(8,128)(2,1)S(1)}, bf16[2,32,1024]{2,1,0:T(8,128)(2,1)S(1)}, u32[]{:S(2)}, u32[]{:S(2)}) collective-permute-start(bf16[2,32,1024]{2,1,0:T(8,128)(2,1)S(1)} %get-tuple-element.14), channel_id=1, source_target_pairs={{0,28},{4,0},{8,4},{12,8},{16,12},{20,16},{24,20},{28,24},{1,29},{... | collective-permute-start | bytes 393224 | tf_op jit(solution)/shard_map/ppermute | solution.py:256
  13.8 6.6 %collective-permute-start.3 = (bf16[2,128,256]{2,1,0:T(8,128)(2,1)S(1)}, bf16[2,128,256]{2,1,0:T(8,128)(2,1)S(1)}, u32[]{:S(2)}, u32[]{:S(2)}) collective-permute-start(bf16[2,128,256]{2,1,0:T(8,128)(2,1)S(1)} %shard_map.75), channel_id=1, source_target_pairs={{0,1},{1,0},{2,3},{3,2},{4,5},{5,4},{6,7},{7,6},{8,9},{9,8},{10,11... | collective-permute-start | bytes 393224 | tf_op jit(solution)/shard_map/ppermute | solution.py:260
  14.3 14.3 %collective-permute-start.1 = (bf16[2,272,256]{2,1,0:T(8,128)(2,1)S(1)}, bf16[2,272,256]{2,1,0:T(8,128)(2,1)S(1)}, u32[]{:S(2)}, u32[]{:S(2)}) collective-permute-start(bf16[2,272,256]{2,1,0:T(8,128)(2,1)S(1)} %shard_map.73), channel_id=1, source_target_pairs={{0,2},{1,3},{2,0},{3,1},{4,6},{5,7},{6,4},{7,5},{8,10},{9,11},{10,... | collective-permute-start | bytes 835592 | tf_op jit(solution)/shard_map/ppermute | solution.py:260
  20.9 3.9 %collective-permute-start.6 = (bf16[2,64,1024]{2,1,0:T(8,128)(2,1)S(1)}, bf16[2,64,1024]{2,1,0:T(8,128)(2,1)S(1)}, u32[]{:S(2)}, u32[]{:S(2)}) collective-permute-start(bf16[2,64,1024]{2,1,0:T(8,128)(2,1)S(1)} %get-tuple-element.17), channel_id=1, source_target_pairs={{0,28},{4,0},{8,4},{12,8},{16,12},{20,16},{24,20},{28,24},{1,29},{... | collective-permute-start | bytes 786440 | tf_op jit(solution)/shard_map/ppermute | solution.py:256
  21.0 13.3 %collective-permute-start.9 = (bf16[2,272,256]{2,1,0:T(8,128)(2,1)S(1)}, bf16[2,272,256]{2,1,0:T(8,128)(2,1)S(1)}, u32[]{:S(2)}, u32[]{:S(2)}) collective-permute-start(bf16[2,272,256]{2,1,0:T(8,128)(2,1)S(1)} %shard_map.73), channel_id=1, source_target_pairs={{0,1},{1,0},{2,3},{3,2},{4,5},{5,4},{6,7},{7,6},{8,9},{9,8},{10,11... | collective-permute-start | bytes 835592 | tf_op jit(solution)/shard_map/ppermute | solution.py:260
  25.3 3.4 %collective-permute-start.7 = (f32[8,128]{1,0:T(8,128)S(1)}, f32[8,128]{1,0:T(8,128)S(1)}, u32[]{:S(2)}, u32[]{:S(2)}) collective-permute-start(f32[8,128]{1,0:T(8,128)S(1)} %shard_map.79), channel_id=1, source_target_pairs={{0,4},{4,0},{8,12},{12,8},{16,20},{20,16},{24,28},{28,24},{1,5},{5... | collective-permute-start | bytes 12296 | tf_op jit(solution)/shard_map/ppermute | solution.py:260
  28.7 10.8 %collective-permute-start.8 = (bf16[2,256,256]{2,1,0:T(8,128)(2,1)S(1)}, bf16[2,256,256]{2,1,0:T(8,128)(2,1)S(1)}, u32[]{:S(2)}, u32[]{:S(2)}) collective-permute-start(bf16[2,256,256]{2,1,0:T(8,128)(2,1)S(1)} %shard_map.80), channel_id=1, source_target_pairs={{0,1},{1,0},{2,3},{3,2},{4,5},{5,4},{6,7},{7,6},{8,9},{9,8},{10,11... | collective-permute-start | bytes 786440 | tf_op jit(solution)/shard_map/ppermute | solution.py:260
  28.7 6.1 %collective-permute-start.10 = (f32[8,128]{1,0:T(8,128)S(1)}, f32[8,128]{1,0:T(8,128)S(1)}, u32[]{:S(2)}, u32[]{:S(2)}) collective-permute-start(f32[8,128]{1,0:T(8,128)S(1)} %add.6), channel_id=1, source_target_pairs={{0,8},{4,12},{8,0},{12,4},{16,24},{20,28},{24,16},{28,20},{1,9},{5... | collective-permute-start | bytes 12296 | tf_op jit(solution)/shard_map/ppermute | solution.py:260
  34.9 4.8 %collective-permute-start.11 = (f32[8,128]{1,0:T(8,128)S(1)}, f32[8,128]{1,0:T(8,128)S(1)}, u32[]{:S(2)}, u32[]{:S(2)}) collective-permute-start(f32[8,128]{1,0:T(8,128)S(1)} %add.7.mine_ref), channel_id=1, source_target_pairs={{0,16},{4,20},{8,24},{12,28},{16,0},{20,4},{24,8},{28,12},{1,17},{... | collective-permute-start | bytes 12296 | tf_op jit(solution)/shard_map/ppermute | solution.py:260

commit v12 on v11

--- a/solution.py
+++ b/solution.py
@@ -48,9 +48,11 @@
     up_ref[...] = sec_ref[0, :, :HALO]
 
 
-def cut_middle_kernel(prim_ref, *refs):
-    cut_ref = refs[-1]
-    cut_ref[...] = prim_ref[:, LAG : LAG + cut_ref.shape[1]]
+def cut_kernel(prim_ref, edges_ref, middle_ref):
+    rows_n = prim_ref.shape[1]
+    edges_ref[:, :LAG] = prim_ref[:, :LAG]
+    edges_ref[:, LAG:] = prim_ref[:, rows_n - LAG :]
+    middle_ref[...] = prim_ref[:, LAG : LAG + middle_ref.shape[1]]
 
 
 def relay_kernel(block_ref, awaited_ref, out_ref):
@@ -269,7 +271,13 @@
     shape = jax.ShapeDtypeStruct
     looks_n = cols_n // LR
     middle_n = rows_n - 2 * LAG
-    edges = jnp.concatenate([primary[:, :LAG], primary[:, rows_n - LAG :]], axis=1)
+    edges, middle = call(
+        cut_kernel,
+        (shape((2, 2 * LAG, width), bf16), shape((2, middle_n + 0, width), bf16)),
+        [],
+        (0, 0),
+        primary,
+    )
     edges_two = swap(edges, "date", 2)
     edges_one = swap(edges, "date", 1)
     halo = shape((2, HALO, cols_n), bf16)
@@ -283,15 +291,10 @@
         (0, 0),
         az_off, rg_off, az_frac, rg_frac,
     )
-    relayed = call(relay_kernel, edges, [], (0, 0), edges_two, az_band)
+    relayed = call(
+        relay_kernel, shape(edges.shape, bf16), [], (0, 0), edges_two, az_band
+    )
     edges_three = swap(relayed, "date", 1)
-    middle = call(
-        cut_middle_kernel,
-        shape((2, middle_n + 16, width), bf16),
-        [],
-        (0, 0),
-        primary, edges_two,
-    )
     weight = jnp.broadcast_to(margin_mask[rows_n - LAG :].astype(f32)[:, None], (LAG, LANE))
     res = call(
         resample_kernel,
@@ -326,7 +329,7 @@
     )
     other = swap(stats, "tile", 1)
     block = shape((2, middle_n, width), bf16)
-    relayed = call(relay_kernel, block, [], (0, 0), two, other)
+    relayed = call(relay_kernel, block, [], (0, 0), two, first)
     three = swap(relayed, "date", 1)
     stride = 2
     while stride < tiles_n:

time: 40.8 us -> 42.8 us (1.049)
  waiting for transfers between devices: 14.4 us -> 16.4 us
    ppermute x9, waiting for transfers between devices: 11.5 us -> 15.3 us  [swap(): lax.ppermute(value, axis, [(at, at ^ step) for at in range(lax.axis_size(...]
    ppermute x9, starting transfers between devices: 13.1 us -> 10.9 us  [swap(): lax.ppermute(value, axis, [(at, at ^ step) for at in range(lax.axis_size(...]
    ppermute x3, starting transfers between devices: 2.75 us -> 4.86 us  [ring(): lax.ppermute(value, axis, [(at, (at + step) % count) for at in range(coun...]
    ppermute x3, waiting for transfers between devices: 2.93 us -> 1.02 us  [ring(): lax.ppermute(value, axis, [(at, (at + step) % count) for at in range(coun...]
    unnamed x6 -> x8, local copies, waits for them, and re-layouts: 1.41 us -> 2.41 us
    slice x1 -> x0, local copies, waits for them, and re-layouts: 0.93 us -> none  [fused(): primary[:, :LAG]]
  transfers between devices with their start and end apart: 12 -> 12, of which waited for: 5 -> 7; matrix products, arithmetic and copies ran while one was open for 2% -> 2% of each run, Pallas kernels for 9% -> 8%
where the time goes in v12:
time: 42.8 us; the launch traced here: 42.6 us
  waiting for transfers between devices  16.4 us (38%)
  starting transfers between devices  15.8 us (37%)
  Pallas kernels  4.4 us (10%)
  between operations  2.73 us (6%)
  local copies, waits for them, and re-layouts  2.48 us (6%)
  other arithmetic  0.76 us (2%)
    ppermute x9, waiting for transfers between devices, swap(): lax.ppermute(value, axis, [(at, at ^ step) for at in range(lax.axis_size(...  15.3 us
    ppermute x9, starting transfers between devices, swap(): lax.ppermute(value, axis, [(at, at ^ step) for at in range(lax.axis_size(...  10.9 us
    ppermute x3, starting transfers between devices, ring(): lax.ppermute(value, axis, [(at, (at + step) % count) for at in range(coun...  4.86 us
    pallas_call x11, Pallas kernels, call(): pl.pallas_call(kernel, out_shape=outs, in_specs=[vmem] * len(args), out_s...  4.4 us
    unnamed x8, local copies, waits for them, and re-layouts  2.41 us
    ppermute x3, waiting for transfers between devices, ring(): lax.ppermute(value, axis, [(at, (at + step) % count) for at in range(coun...  1.02 us
  transfers between devices with their start and end apart: 12, of which 7 were waited for; matrix products, arithmetic and copies ran while one was open for 2% of the time, Pallas kernels for 8%

profile of v12, /device:TPU:0, one launch (start us, length us, event | category | flops | bytes accessed | tf_op | source)
XLA Modules:
  0.0 42.6 jit_solution(1892222782709881640)
XLA Ops:
  0.0 1.0 %copy-done.2 = bf16[2,384,256]{2,1,0:T(8,128)(2,1)S(1)} copy-done((bf16[2,384,256]{2,1,0:T(8,128)(2,1)S(1)}, bf16[2,384,256]{2,1,0:T(8,128)(2,1)}, u32[]{:S(2)}) %copy-start.2) | copy-done | bytes 393240
  1.0 4.1 %collective-permute-start.2 = (bf16[2,128,256]{2,1,0:T(8,128)(2,1)S(1)}, bf16[2,128,256]{2,1,0:T(8,128)(2,1)S(1)}, u32[]{:S(2)}, u32[]{:S(2)}) collective-permute-start(bf16[2,128,256]{2,1,0:T(8,128)(2,1)S(1)} %get-tuple-element.15), channel_id=1, source_target_pairs={{0,2},{1,3},{2,0},{3,1},{4,6},{5,7},{6,4},{7,5},{8,10},{9,11},{10,... | collective-permute-start | bytes 393224 | tf_op jit(solution)/shard_map/ppermute | solution.py:262
  5.1 0.1 collective-permute-start
  5.2 1.8 %collective-permute-start.1 = (bf16[2,128,256]{2,1,0:T(8,128)(2,1)S(1)}, bf16[2,128,256]{2,1,0:T(8,128)(2,1)S(1)}, u32[]{:S(2)}, u32[]{:S(2)}) collective-permute-start(bf16[2,128,256]{2,1,0:T(8,128)(2,1)S(1)} %get-tuple-element.15), channel_id=1, source_target_pairs={{0,1},{1,0},{2,3},{3,2},{4,5},{5,4},{6,7},{7,6},{8,9},{9,8},{10,11... | collective-permute-start | bytes 393224 | tf_op jit(solution)/shard_map/ppermute | solution.py:262
  7.0 1.4 %copy-done = bf16[1,2,384,1024]{3,2,1,0:T(8,128)(2,1)S(1)} copy-done((bf16[1,2,384,1024]{3,2,1,0:T(8,128)(2,1)S(1)}, bf16[1,2,384,1024]{3,2,1,0:T(8,128)(2,1)}, u32[]{:S(2)}) %copy-start) | copy-done | bytes 1572888
  8.5 0.1 collective-permute-start.4
  8.5 2.6 %collective-permute-start.5 = (bf16[2,32,1024]{2,1,0:T(8,128)(2,1)S(1)}, bf16[2,32,1024]{2,1,0:T(8,128)(2,1)S(1)}, u32[]{:S(2)}, u32[]{:S(2)}) collective-permute-start(bf16[2,32,1024]{2,1,0:T(8,128)(2,1)S(1)} %get-tuple-element.18), channel_id=1, source_target_pairs={{0,28},{4,0},{8,4},{12,8},{16,12},{20,16},{24,20},{28,24},{1,29},{... | collective-permute-start | bytes 393224 | tf_op jit(solution)/shard_map/ppermute | solution.py:258
  13.8 0.4 shard_map.74
  14.1 3.8 %collective-permute-done.2.block_ref.two_ref = bf16[2,128,256]{2,1,0:T(8,128)(2,1)S(1)} collective-permute-done((bf16[2,128,256]{2,1,0:T(8,128)(2,1)S(1)}, bf16[2,128,256]{2,1,0:T(8,128)(2,1)S(1)}, u32[]{:S(2)}, u32[]{:S(2)}) %collective-permute-start.2) | collective-permute-done | bytes 131104 | tf_op jit(solution)/shard_map/ppermute | solution.py:262
  17.9 0.1 collective-permute-start.3
  18.0 0.0 collective-permute-done.5.high_ref
  18.0 0.0 copy-start.3
  18.0 1.4 %shard_map.77.res_ref = bf16[4,2,384,256]{3,2,1,0:T(8,128)(2,1)S(1)} custom-call(bf16[1,2,384,1024]{3,2,1,0:T(8,128)(2,1)S(1)} %copy-done.1, bf16[2,32,1024]{2,1,0:T(8,128)(2,1)S(1)} %collective-permute-done.4.low_ref, bf16[2,32,1024]{2,1,0:T(8,128)(2,1)S(1)} %collective-permute-done.5.high_ref, bf16[128,192]{1,0:T(8,128)(2,1)S(1)} %get-tuple-element.16.awaited_ref.az_ref, ...), custom_call_target="tpu_custom_call" | custom-call | tf_op jit(solution)/shard_map/pallas_call | solution.py:245
  19.4 6.0 %collective-permute-done.3.three_ref = bf16[2,128,256]{2,1,0:T(8,128)(2,1)S(1)} collective-permute-done((bf16[2,128,256]{2,1,0:T(8,128)(2,1)S(1)}, bf16[2,128,256]{2,1,0:T(8,128)(2,1)S(1)}, u32[]{:S(2)}, u32[]{:S(2)}) %collective-permute-start.3) | collective-permute-done | bytes 131104 | tf_op jit(solution)/shard_map/ppermute | solution.py:262
  25.5 0.5 %shard_map.78 = (bf16[2,64,1024]{2,1,0:T(8,128)(2,1)S(1)}, bf16[2,64,1024]{2,1,0:T(8,128)(2,1)S(1)}, f32[2,64,128]{2,1,0:T(8,128)S(1)}) custom-call(bf16[2,384,256]{2,1,0:T(8,128)(2,1)S(1)} %copy-done.3, bf16[2,128,256]{2,1,0:T(8,128)(2,1)S(1)} %collective-permute-done.1.one_ref, bf16[2,128,256]{2,1,0:T(8,128)(2,1)S(1)} %collective-permute-done.2.block_ref.two_ref, ...), custom_call_target="tpu_custom_call" | custom-call | tf_op jit(solution)/shard_map/pallas_call | solution.py:245
  26.0 2.2 %collective-permute-start.8 = (bf16[2,64,1024]{2,1,0:T(8,128)(2,1)S(1)}, bf16[2,64,1024]{2,1,0:T(8,128)(2,1)S(1)}, u32[]{:S(2)}, u32[]{:S(2)}) collective-permute-start(bf16[2,64,1024]{2,1,0:T(8,128)(2,1)S(1)} %get-tuple-element.20.awaited_ref), channel_id=1, source_target_pairs={{0,28},{4,0},{8,4},{12,8},{16,12},{20,16},{24,20},{28,24},{1,29},{... | collective-permute-start | bytes 786440 | tf_op jit(solution)/shard_map/ppermute | solution.py:258
  28.2 0.0 collective-permute-start.7
  28.2 2.1 %collective-permute-start.6 = (bf16[2,256,256]{2,1,0:T(8,128)(2,1)S(1)}, bf16[2,256,256]{2,1,0:T(8,128)(2,1)S(1)}, u32[]{:S(2)}, u32[]{:S(2)}) collective-permute-start(bf16[2,256,256]{2,1,0:T(8,128)(2,1)S(1)} %shard_map.79), channel_id=1, source_target_pairs={{0,1},{1,0},{2,3},{3,2},{4,5},{5,4},{6,7},{7,6},{8,9},{9,8},{10,11... | collective-permute-start | bytes 786440 | tf_op jit(solution)/shard_map/ppermute | solution.py:262
  30.3 0.8 %slice_convert_fusion = f32[64]{0:T(128)S(1)} fusion(s32[384]{0:T(512)} %param.9), kind=kLoop, calls=%fused_computation | loop fusion | flops 64 | bytes 512 | tf_op jit(solution)/shard_map/convert_element_type | solution.py:298
  31.0 1.0 %collective-permute-done.8.later_ref = bf16[2,64,1024]{2,1,0:T(8,128)(2,1)S(1)} collective-permute-done((bf16[2,64,1024]{2,1,0:T(8,128)(2,1)S(1)}, bf16[2,64,1024]{2,1,0:T(8,128)(2,1)S(1)}, u32[]{:S(2)}, u32[]{:S(2)}) %collective-permute-start.8) | collective-permute-done | bytes 262176 | tf_op jit(solution)/shard_map/ppermute | solution.py:258
  32.1 0.1 broadcast_in_dim.2.weight_ref
  32.1 0.4 shard_map.82
  32.5 0.2 collective-permute-start.9
  32.7 1.1 %collective-permute-done.9 = f32[8,128]{1,0:T(8,128)S(1)} collective-permute-done((f32[8,128]{1,0:T(8,128)S(1)}, f32[8,128]{1,0:T(8,128)S(1)}, u32[]{:S(2)}, u32[]{:S(2)}) %collective-permute-start.9) | collective-permute-done | bytes 4128 | tf_op jit(solution)/shard_map/ppermute | solution.py:262
  33.7 1.9 %collective-permute-start.10 = (f32[8,128]{1,0:T(8,128)S(1)}, f32[8,128]{1,0:T(8,128)S(1)}, u32[]{:S(2)}, u32[]{:S(2)}) collective-permute-start(f32[8,128]{1,0:T(8,128)S(1)} %add.6), channel_id=1, source_target_pairs={{0,8},{4,12},{8,0},{12,4},{16,24},{20,28},{24,16},{28,20},{1,9},{5... | collective-permute-start | bytes 12296 | tf_op jit(solution)/shard_map/ppermute | solution.py:262
  35.6 1.8 %collective-permute-done.7.one_ref = bf16[2,256,256]{2,1,0:T(8,128)(2,1)S(1)} collective-permute-done((bf16[2,256,256]{2,1,0:T(8,128)(2,1)S(1)}, bf16[2,256,256]{2,1,0:T(8,128)(2,1)S(1)}, u32[]{:S(2)}, u32[]{:S(2)}) %collective-permute-start.7) | collective-permute-done | bytes 262176 | tf_op jit(solution)/shard_map/ppermute | solution.py:262
  37.4 0.6 %shard_map.80.before_ref = f32[2,256,128]{2,1,0:T(8,128)S(1)} custom-call(bf16[2,384,256]{2,1,0:T(8,128)(2,1)S(1)} %copy-done.3, bf16[2,256,256]{2,1,0:T(8,128)(2,1)S(1)} %collective-permute-done.7.one_ref, bf16[2,256,256]{2,1,0:T(8,128)(2,1)S(1)} %collective-permute-done.block_ref.two_ref, bf16[4,2,384,256]{3,2,1,0:T(8,128)(2,1)S(1)} %shard_map.77.res_ref), custom_call_target="tpu_custom_call" | custom-call | flops 134217728 | bytes 3145728 | tf_op jit(solution)/shard_map/pallas_call | solution.py:245
  38.0 0.7 %collective-permute-start.11 = (f32[8,128]{1,0:T(8,128)S(1)}, f32[8,128]{1,0:T(8,128)S(1)}, u32[]{:S(2)}, u32[]{:S(2)}) collective-permute-start(f32[8,128]{1,0:T(8,128)S(1)} %add.7.mine_ref), channel_id=1, source_target_pairs={{0,16},{4,20},{8,24},{12,28},{16,0},{20,4},{24,8},{28,12},{1,17},{... | collective-permute-start | bytes 12296 | tf_op jit(solution)/shard_map/ppermute | solution.py:262
  38.7 1.7 %collective-permute-done.6.three_ref = bf16[2,256,256]{2,1,0:T(8,128)(2,1)S(1)} collective-permute-done((bf16[2,256,256]{2,1,0:T(8,128)(2,1)S(1)}, bf16[2,256,256]{2,1,0:T(8,128)(2,1)S(1)}, u32[]{:S(2)}, u32[]{:S(2)}) %collective-permute-start.6) | collective-permute-done | bytes 262176 | tf_op jit(solution)/shard_map/ppermute | solution.py:262
  40.4 0.3 shard_map.81.looks_ref
  40.7 1.0 %collective-permute-done.11.other_ref = f32[8,128]{1,0:T(8,128)S(1)} collective-permute-done((f32[8,128]{1,0:T(8,128)S(1)}, f32[8,128]{1,0:T(8,128)S(1)}, u32[]{:S(2)}, u32[]{:S(2)}) %collective-permute-start.11) | collective-permute-done | bytes 4128 | tf_op jit(solution)/shard_map/ppermute | solution.py:262
  41.7 0.8 %shard_map.83 = f32[1,2,192,128]{3,2,1,0:T(8,128)} custom-call(f32[2,192,128]{2,1,0:T(8,128)S(1)} %shard_map.81.looks_ref, f32[8,128]{1,0:T(8,128)S(1)} %add.7.mine_ref, f32[8,128]{1,0:T(8,128)S(1)} %collective-permute-done.11.other_ref), custom_call_target="tpu_custom_call" | custom-call | flops 393216 | bytes 393216 | tf_op jit(solution)/shard_map/pallas_call | solution.py:245
  (15 shorter events, 0.1 us)
Async XLA Ops:
  0.0 1.0 %copy-start.2 = (bf16[2,384,256]{2,1,0:T(8,128)(2,1)S(1)}, bf16[2,384,256]{2,1,0:T(8,128)(2,1)}, u32[]{:S(2)}) copy-start(bf16[2,384,256]{2,1,0:T(8,128)(2,1)} %own_ref.3) | copy-start | bytes 1179652
  1.0 16.9 %collective-permute-start.2 = (bf16[2,128,256]{2,1,0:T(8,128)(2,1)S(1)}, bf16[2,128,256]{2,1,0:T(8,128)(2,1)S(1)}, u32[]{:S(2)}, u32[]{:S(2)}) collective-permute-start(bf16[2,128,256]{2,1,0:T(8,128)(2,1)S(1)} %get-tuple-element.15), channel_id=1, source_target_pairs={{0,2},{1,3},{2,0},{3,1},{4,6},{5,7},{6,4},{7,5},{8,10},{9,11},{10,... | collective-permute-start | bytes 393224 | tf_op jit(solution)/shard_map/ppermute | solution.py:262
  5.1 23.1 %collective-permute-start = (bf16[2,256,256]{2,1,0:T(8,128)(2,1)S(1)}, bf16[2,256,256]{2,1,0:T(8,128)(2,1)S(1)}, u32[]{:S(2)}, u32[]{:S(2)}) collective-permute-start(bf16[2,256,256]{2,1,0:T(8,128)(2,1)S(1)} %get-tuple-element.14), channel_id=1, source_target_pairs={{0,2},{1,3},{2,0},{3,1},{4,6},{5,7},{6,4},{7,5},{8,10},{9,11},{10,... | collective-permute-start | bytes 786440 | tf_op jit(solution)/shard_map/ppermute | solution.py:262
  5.2 14.2 %collective-permute-start.1 = (bf16[2,128,256]{2,1,0:T(8,128)(2,1)S(1)}, bf16[2,128,256]{2,1,0:T(8,128)(2,1)S(1)}, u32[]{:S(2)}, u32[]{:S(2)}) collective-permute-start(bf16[2,128,256]{2,1,0:T(8,128)(2,1)S(1)} %get-tuple-element.15), channel_id=1, source_target_pairs={{0,1},{1,0},{2,3},{3,2},{4,5},{5,4},{6,7},{7,6},{8,9},{9,8},{10,11... | collective-permute-start | bytes 393224 | tf_op jit(solution)/shard_map/ppermute | solution.py:262
  7.0 1.4 %copy-start = (bf16[1,2,384,1024]{3,2,1,0:T(8,128)(2,1)S(1)}, bf16[1,2,384,1024]{3,2,1,0:T(8,128)(2,1)}, u32[]{:S(2)}) copy-start(bf16[1,2,384,1024]{3,2,1,0:T(8,128)(2,1)} %sec_ref.3) | copy-start | bytes 4718596
  8.4 9.5 %copy-start.1 = (bf16[1,2,384,1024]{3,2,1,0:T(8,128)(2,1)S(1)}, bf16[1,2,384,1024]{3,2,1,0:T(8,128)(2,1)}, u32[]{:S(2)}) copy-start(bf16[1,2,384,1024]{3,2,1,0:T(8,128)(2,1)} %sec_ref.3) | copy-start | bytes 4718596
  8.5 9.5 %collective-permute-start.4 = (bf16[2,32,1024]{2,1,0:T(8,128)(2,1)S(1)}, bf16[2,32,1024]{2,1,0:T(8,128)(2,1)S(1)}, u32[]{:S(2)}, u32[]{:S(2)}) collective-permute-start(bf16[2,32,1024]{2,1,0:T(8,128)(2,1)S(1)} %get-tuple-element.17), channel_id=1, source_target_pairs={{0,4},{4,8},{8,12},{12,16},{16,20},{20,24},{24,28},{28,0},{1,5},{5... | collective-permute-start | bytes 393224 | tf_op jit(solution)/shard_map/ppermute | solution.py:258
  8.5 9.4 %collective-permute-start.5 = (bf16[2,32,1024]{2,1,0:T(8,128)(2,1)S(1)}, bf16[2,32,1024]{2,1,0:T(8,128)(2,1)S(1)}, u32[]{:S(2)}, u32[]{:S(2)}) collective-permute-start(bf16[2,32,1024]{2,1,0:T(8,128)(2,1)S(1)} %get-tuple-element.18), channel_id=1, source_target_pairs={{0,28},{4,0},{8,4},{12,8},{16,12},{20,16},{24,20},{28,24},{1,29},{... | collective-permute-start | bytes 393224 | tf_op jit(solution)/shard_map/ppermute | solution.py:258
  17.9 7.6 %collective-permute-start.3 = (bf16[2,128,256]{2,1,0:T(8,128)(2,1)S(1)}, bf16[2,128,256]{2,1,0:T(8,128)(2,1)S(1)}, u32[]{:S(2)}, u32[]{:S(2)}) collective-permute-start(bf16[2,128,256]{2,1,0:T(8,128)(2,1)S(1)} %shard_map.75), channel_id=1, source_target_pairs={{0,1},{1,0},{2,3},{3,2},{4,5},{5,4},{6,7},{7,6},{8,9},{9,8},{10,11... | collective-permute-start | bytes 393224 | tf_op jit(solution)/shard_map/ppermute | solution.py:262
  18.0 7.5 %copy-start.3 = (bf16[2,384,256]{2,1,0:T(8,128)(2,1)S(1)}, bf16[2,384,256]{2,1,0:T(8,128)(2,1)}, u32[]{:S(2)}) copy-start(bf16[2,384,256]{2,1,0:T(8,128)(2,1)} %own_ref.3) | copy-start | bytes 1179652
  26.0 6.1 %collective-permute-start.8 = (bf16[2,64,1024]{2,1,0:T(8,128)(2,1)S(1)}, bf16[2,64,1024]{2,1,0:T(8,128)(2,1)S(1)}, u32[]{:S(2)}, u32[]{:S(2)}) collective-permute-start(bf16[2,64,1024]{2,1,0:T(8,128)(2,1)S(1)} %get-tuple-element.20.awaited_ref), channel_id=1, source_target_pairs={{0,28},{4,0},{8,4},{12,8},{16,12},{20,16},{24,20},{28,24},{1,29},{... | collective-permute-start | bytes 786440 | tf_op jit(solution)/shard_map/ppermute | solution.py:258
  28.2 9.2 %collective-permute-start.7 = (bf16[2,256,256]{2,1,0:T(8,128)(2,1)S(1)}, bf16[2,256,256]{2,1,0:T(8,128)(2,1)S(1)}, u32[]{:S(2)}, u32[]{:S(2)}) collective-permute-start(bf16[2,256,256]{2,1,0:T(8,128)(2,1)S(1)} %get-tuple-element.14), channel_id=1, source_target_pairs={{0,1},{1,0},{2,3},{3,2},{4,5},{5,4},{6,7},{7,6},{8,9},{9,8},{10,11... | collective-permute-start | bytes 786440 | tf_op jit(solution)/shard_map/ppermute | solution.py:262
  28.2 12.2 %collective-permute-start.6 = (bf16[2,256,256]{2,1,0:T(8,128)(2,1)S(1)}, bf16[2,256,256]{2,1,0:T(8,128)(2,1)S(1)}, u32[]{:S(2)}, u32[]{:S(2)}) collective-permute-start(bf16[2,256,256]{2,1,0:T(8,128)(2,1)S(1)} %shard_map.79), channel_id=1, source_target_pairs={{0,1},{1,0},{2,3},{3,2},{4,5},{5,4},{6,7},{7,6},{8,9},{9,8},{10,11... | collective-permute-start | bytes 786440 | tf_op jit(solution)/shard_map/ppermute | solution.py:262
  32.5 1.2 %collective-permute-start.9 = (f32[8,128]{1,0:T(8,128)S(1)}, f32[8,128]{1,0:T(8,128)S(1)}, u32[]{:S(2)}, u32[]{:S(2)}) collective-permute-start(f32[8,128]{1,0:T(8,128)S(1)} %shard_map.82), channel_id=1, source_target_pairs={{0,4},{4,0},{8,12},{12,8},{16,20},{20,16},{24,28},{28,24},{1,5},{5... | collective-permute-start | bytes 12296 | tf_op jit(solution)/shard_map/ppermute | solution.py:262
  33.7 4.3 %collective-permute-start.10 = (f32[8,128]{1,0:T(8,128)S(1)}, f32[8,128]{1,0:T(8,128)S(1)}, u32[]{:S(2)}, u32[]{:S(2)}) collective-permute-start(f32[8,128]{1,0:T(8,128)S(1)} %add.6), channel_id=1, source_target_pairs={{0,8},{4,12},{8,0},{12,4},{16,24},{20,28},{24,16},{28,20},{1,9},{5... | collective-permute-start | bytes 12296 | tf_op jit(solution)/shard_map/ppermute | solution.py:262
  38.0 3.7 %collective-permute-start.11 = (f32[8,128]{1,0:T(8,128)S(1)}, f32[8,128]{1,0:T(8,128)S(1)}, u32[]{:S(2)}, u32[]{:S(2)}) collective-permute-start(f32[8,128]{1,0:T(8,128)S(1)} %add.7.mine_ref), channel_id=1, source_target_pairs={{0,16},{4,20},{8,24},{12,28},{16,0},{20,4},{24,8},{28,12},{1,17},{... | collective-permute-start | bytes 12296 | tf_op jit(solution)/shard_map/ppermute | solution.py:262

commit v13 on v11

--- a/solution.py
+++ b/solution.py
@@ -53,8 +53,8 @@
     cut_ref[...] = prim_ref[:, LAG : LAG + cut_ref.shape[1]]
 
 
-def relay_kernel(block_ref, awaited_ref, out_ref):
-    del awaited_ref
+def relay_kernel(block_ref, *refs):
+    out_ref = refs[-1]
     out_ref[...] = block_ref[:, : out_ref.shape[1]]
 
 
@@ -270,8 +270,7 @@
     looks_n = cols_n // LR
     middle_n = rows_n - 2 * LAG
     edges = jnp.concatenate([primary[:, :LAG], primary[:, rows_n - LAG :]], axis=1)
-    edges_two = swap(edges, "date", 2)
-    edges_one = swap(edges, "date", 1)
+    edges_two, edges_three, edges_one = [swap(edges, "date", step) for step in (2, 3, 1)]
     halo = shape((2, HALO, cols_n), bf16)
     down, up = call(cut_halo_kernel, (halo, halo), [], (0, 0), secondary)
     low = ring(down, "tile", 1)
@@ -283,14 +282,12 @@
         (0, 0),
         az_off, rg_off, az_frac, rg_frac,
     )
-    relayed = call(relay_kernel, edges, [], (0, 0), edges_two, az_band)
-    edges_three = swap(relayed, "date", 1)
     middle = call(
         cut_middle_kernel,
         shape((2, middle_n + 16, width), bf16),
         [],
         (0, 0),
-        primary, edges_two,
+        primary, edges_two,edges_three,az_band,
     )
     weight = jnp.broadcast_to(margin_mask[rows_n - LAG :].astype(f32)[:, None], (LAG, LANE))
     res = call(
@@ -326,7 +323,7 @@
     )
     other = swap(stats, "tile", 1)
     block = shape((2, middle_n, width), bf16)
-    relayed = call(relay_kernel, block, [], (0, 0), two, other)
+    relayed = call(relay_kernel, block, [], (0, 0), two, other,one)
     three = swap(relayed, "date", 1)
     stride = 2
     while stride < tiles_n:

time: 40.8 us -> 42.7 us (1.047)
  starting transfers between devices: 15.8 us -> 18.9 us
  waiting for transfers between devices: 14.4 us -> 13.3 us
    ppermute x3, starting transfers between devices: 2.75 us -> 4.53 us  [ring(): lax.ppermute(value, axis, [(at, (at + step) % count) for at in range(coun...]
    ppermute x9, waiting for transfers between devices: 11.5 us -> 10.1 us  [swap(): lax.ppermute(value, axis, [(at, at ^ step) for at in range(lax.axis_size(...]
    ppermute x9, starting transfers between devices: 13.1 us -> 14.4 us  [swap(): lax.ppermute(value, axis, [(at, at ^ step) for at in range(lax.axis_size(...]
    pallas_call x11 -> x10, Pallas kernels: 4.41 us -> 4.4 us  [call(): pl.pallas_call(kernel, out_shape=outs, in_specs=[vmem] * len(args), out_s...]
  transfers between devices with their start and end apart: 12 -> 12, of which waited for: 5 -> 8; matrix products, arithmetic and copies ran while one was open for 2% -> 2% of each run, Pallas kernels for 9% -> 8%
where the time goes in v13:
time: 42.7 us; the launch traced here: 42.5 us
  starting transfers between devices  18.9 us (44%)
  waiting for transfers between devices  13.3 us (31%)
  Pallas kernels  4.4 us (10%)
  between operations  2.69 us (6%)
  local copies, waits for them, and re-layouts  2.42 us (6%)
  other arithmetic  0.77 us (2%)
    ppermute x9, starting transfers between devices, swap(): lax.ppermute(value, axis, [(at, at ^ step) for at in range(lax.axis_size(...  14.4 us
    ppermute x9, waiting for transfers between devices, swap(): lax.ppermute(value, axis, [(at, at ^ step) for at in range(lax.axis_size(...  10.1 us
    ppermute x3, starting transfers between devices, ring(): lax.ppermute(value, axis, [(at, (at + step) % count) for at in range(coun...  4.53 us
    pallas_call x10, Pallas kernels, call(): pl.pallas_call(kernel, out_shape=outs, in_specs=[vmem] * len(args), out_s...  4.4 us
    ppermute x3, waiting for transfers between devices, ring(): lax.ppermute(value, axis, [(at, (at + step) % count) for at in range(coun...  3.14 us
    unnamed x6, local copies, waits for them, and re-layouts  1.41 us
    slice x1, local copies, waits for them, and re-layouts, fused(): primary[:, :LAG]  0.93 us
  transfers between devices with their start and end apart: 12, of which 8 were waited for; matrix products, arithmetic and copies ran while one was open for 2% of the time, Pallas kernels for 8%

profile of v13, /device:TPU:0, one launch (start us, length us, event | category | flops | bytes accessed | tf_op | source)
XLA Modules:
  0.0 42.5 jit_solution(3680633248185975804)
XLA Ops:
  0.0 0.9 %fusion = (bf16[2,64,256]{2,1,0:T(8,128)(2,1)S(1)}, bf16[2,64,256]{2,1,0:T(8,128)(2,1)S(1)}) fusion(bf16[2,384,256]{2,1,0:T(8,128)(2,1)} %own_ref.3), kind=kLoop, calls=%fused_computation.2 | loop fusion | bytes 262144 | tf_op jit(solution)/shard_map/slice | solution.py:272
  1.0 4.1 %collective-permute-start = (bf16[2,128,256]{2,1,0:T(8,128)(2,1)S(1)}, bf16[2,128,256]{2,1,0:T(8,128)(2,1)S(1)}, u32[]{:S(2)}, u32[]{:S(2)}) collective-permute-start(bf16[2,128,256]{2,1,0:T(8,128)(2,1)S(1)} %pad_maximum_fusion), channel_id=1, source_target_pairs={{0,2},{1,3},{2,0},{3,1},{4,6},{5,7},{6,4},{7,5},{8,10},{9,11},{10,... | collective-permute-start | bytes 393224 | tf_op jit(solution)/shard_map/ppermute | solution.py:260
  5.1 1.3 %collective-permute-start.1 = (bf16[2,128,256]{2,1,0:T(8,128)(2,1)S(1)}, bf16[2,128,256]{2,1,0:T(8,128)(2,1)S(1)}, u32[]{:S(2)}, u32[]{:S(2)}) collective-permute-start(bf16[2,128,256]{2,1,0:T(8,128)(2,1)S(1)} %pad_maximum_fusion), channel_id=1, source_target_pairs={{0,3},{1,2},{2,1},{3,0},{4,7},{5,6},{6,5},{7,4},{8,11},{9,10},{10,... | collective-permute-start | bytes 393224 | tf_op jit(solution)/shard_map/ppermute | solution.py:260
  6.4 1.4 %copy-done = bf16[1,2,384,1024]{3,2,1,0:T(8,128)(2,1)S(1)} copy-done((bf16[1,2,384,1024]{3,2,1,0:T(8,128)(2,1)S(1)}, bf16[1,2,384,1024]{3,2,1,0:T(8,128)(2,1)}, u32[]{:S(2)}) %copy-start) | copy-done | bytes 1572888
  7.8 0.1 collective-permute-start.4
  7.9 2.6 %collective-permute-start.5 = (bf16[2,32,1024]{2,1,0:T(8,128)(2,1)S(1)}, bf16[2,32,1024]{2,1,0:T(8,128)(2,1)S(1)}, u32[]{:S(2)}, u32[]{:S(2)}) collective-permute-start(bf16[2,32,1024]{2,1,0:T(8,128)(2,1)S(1)} %get-tuple-element.14), channel_id=1, source_target_pairs={{0,28},{4,0},{8,4},{12,8},{16,12},{20,16},{24,20},{28,24},{1,29},{... | collective-permute-start | bytes 393224 | tf_op jit(solution)/shard_map/ppermute | solution.py:256
  10.5 0.2 collective-permute-start.3
  13.4 0.4 shard_map.73
  13.7 1.3 %collective-permute-done.refs_0_.two_ref = bf16[2,128,256]{2,1,0:T(8,128)(2,1)S(1)} collective-permute-done((bf16[2,128,256]{2,1,0:T(8,128)(2,1)S(1)}, bf16[2,128,256]{2,1,0:T(8,128)(2,1)S(1)}, u32[]{:S(2)}, u32[]{:S(2)}) %collective-permute-start) | collective-permute-done | bytes 131104 | tf_op jit(solution)/shard_map/ppermute | solution.py:260
  15.0 0.0 collective-permute-done.1.refs_1_.three_ref
  15.0 4.7 %collective-permute-start.2 = (bf16[2,272,256]{2,1,0:T(8,128)(2,1)S(1)}, bf16[2,272,256]{2,1,0:T(8,128)(2,1)S(1)}, u32[]{:S(2)}, u32[]{:S(2)}) collective-permute-start(bf16[2,272,256]{2,1,0:T(8,128)(2,1)S(1)} %shard_map.74), channel_id=1, source_target_pairs={{0,2},{1,3},{2,0},{3,1},{4,6},{5,7},{6,4},{7,5},{8,10},{9,11},{10,... | collective-permute-start | bytes 835592 | tf_op jit(solution)/shard_map/ppermute | solution.py:260
  19.8 1.4 %shard_map.76.res_ref = bf16[4,2,384,256]{3,2,1,0:T(8,128)(2,1)S(1)} custom-call(bf16[1,2,384,1024]{3,2,1,0:T(8,128)(2,1)S(1)} %copy-done.1, bf16[2,32,1024]{2,1,0:T(8,128)(2,1)S(1)} %collective-permute-done.4.low_ref, bf16[2,32,1024]{2,1,0:T(8,128)(2,1)S(1)} %collective-permute-done.5.high_ref, bf16[128,192]{1,0:T(8,128)(2,1)S(1)} %get-tuple-element.12.refs_2_.az_ref, ...), custom_call_target="tpu_custom_call" | custom-call | tf_op jit(solution)/shard_map/pallas_call | solution.py:243
  21.2 0.0 collective-permute-done.3.one_ref
  21.2 0.5 %shard_map.77 = (bf16[2,64,1024]{2,1,0:T(8,128)(2,1)S(1)}, bf16[2,64,1024]{2,1,0:T(8,128)(2,1)S(1)}, f32[2,64,128]{2,1,0:T(8,128)S(1)}) custom-call(bf16[2,384,256]{2,1,0:T(8,128)(2,1)S(1)} %copy-done.2, bf16[2,128,256]{2,1,0:T(8,128)(2,1)S(1)} %collective-permute-done.3.one_ref, bf16[2,128,256]{2,1,0:T(8,128)(2,1)S(1)} %collective-permute-done.refs_0_.two_ref, ...), custom_call_target="tpu_custom_call" | custom-call | tf_op jit(solution)/shard_map/pallas_call | solution.py:243
  21.7 1.8 %collective-permute-start.6 = (bf16[2,64,1024]{2,1,0:T(8,128)(2,1)S(1)}, bf16[2,64,1024]{2,1,0:T(8,128)(2,1)S(1)}, u32[]{:S(2)}, u32[]{:S(2)}) collective-permute-start(bf16[2,64,1024]{2,1,0:T(8,128)(2,1)S(1)} %get-tuple-element.17), channel_id=1, source_target_pairs={{0,28},{4,0},{8,4},{12,8},{16,12},{20,16},{24,20},{28,24},{1,29},{... | collective-permute-start | bytes 786440 | tf_op jit(solution)/shard_map/ppermute | solution.py:256
  23.6 0.8 %slice_convert_fusion = f32[64]{0:T(128)S(1)} fusion(s32[384]{0:T(512)} %param.9), kind=kLoop, calls=%fused_computation.1 | loop fusion | flops 64 | bytes 512 | tf_op jit(solution)/shard_map/convert_element_type | solution.py:292
  24.3 3.1 %collective-permute-done.6.later_ref = bf16[2,64,1024]{2,1,0:T(8,128)(2,1)S(1)} collective-permute-done((bf16[2,64,1024]{2,1,0:T(8,128)(2,1)S(1)}, bf16[2,64,1024]{2,1,0:T(8,128)(2,1)S(1)}, u32[]{:S(2)}, u32[]{:S(2)}) %collective-permute-start.6) | collective-permute-done | bytes 262176 | tf_op jit(solution)/shard_map/ppermute | solution.py:256
  27.5 0.1 broadcast_in_dim.2.weight_ref
  27.5 0.4 shard_map.78
  27.9 0.3 collective-permute-start.7
  28.2 0.9 %collective-permute-done.7.refs_0_ = f32[8,128]{1,0:T(8,128)S(1)} collective-permute-done((f32[8,128]{1,0:T(8,128)S(1)}, f32[8,128]{1,0:T(8,128)S(1)}, u32[]{:S(2)}, u32[]{:S(2)}) %collective-permute-start.7) | collective-permute-done | bytes 4128 | tf_op jit(solution)/shard_map/ppermute | solution.py:260
  29.1 3.5 %collective-permute-done.2.block_ref.two_ref = bf16[2,272,256]{2,1,0:T(8,128)(2,1)S(1)} collective-permute-done((bf16[2,272,256]{2,1,0:T(8,128)(2,1)S(1)}, bf16[2,272,256]{2,1,0:T(8,128)(2,1)S(1)}, u32[]{:S(2)}, u32[]{:S(2)}) %collective-permute-start.2) | collective-permute-done | bytes 278560 | tf_op jit(solution)/shard_map/ppermute | solution.py:260
  32.7 1.1 %collective-permute-done.8.refs_1_.one_ref = bf16[2,272,256]{2,1,0:T(8,128)(2,1)S(1)} collective-permute-done((bf16[2,272,256]{2,1,0:T(8,128)(2,1)S(1)}, bf16[2,272,256]{2,1,0:T(8,128)(2,1)S(1)}, u32[]{:S(2)}, u32[]{:S(2)}) %collective-permute-start.8) | collective-permute-done | bytes 278560 | tf_op jit(solution)/shard_map/ppermute | solution.py:260
  33.8 0.6 %collective-permute-start.9 = (bf16[2,256,256]{2,1,0:T(8,128)(2,1)S(1)}, bf16[2,256,256]{2,1,0:T(8,128)(2,1)S(1)}, u32[]{:S(2)}, u32[]{:S(2)}) collective-permute-start(bf16[2,256,256]{2,1,0:T(8,128)(2,1)S(1)} %shard_map.79), channel_id=1, source_target_pairs={{0,1},{1,0},{2,3},{3,2},{4,5},{5,4},{6,7},{7,6},{8,9},{9,8},{10,11... | collective-permute-start | bytes 786440 | tf_op jit(solution)/shard_map/ppermute | solution.py:260
  34.4 1.5 %collective-permute-start.10 = (f32[8,128]{1,0:T(8,128)S(1)}, f32[8,128]{1,0:T(8,128)S(1)}, u32[]{:S(2)}, u32[]{:S(2)}) collective-permute-start(f32[8,128]{1,0:T(8,128)S(1)} %add.6), channel_id=1, source_target_pairs={{0,8},{4,12},{8,0},{12,4},{16,24},{20,28},{24,16},{28,20},{1,9},{5... | collective-permute-start | bytes 12296 | tf_op jit(solution)/shard_map/ppermute | solution.py:260
  35.9 2.1 %collective-permute-done.10 = f32[8,128]{1,0:T(8,128)S(1)} collective-permute-done((f32[8,128]{1,0:T(8,128)S(1)}, f32[8,128]{1,0:T(8,128)S(1)}, u32[]{:S(2)}, u32[]{:S(2)}) %collective-permute-start.10) | collective-permute-done | bytes 4128 | tf_op jit(solution)/shard_map/ppermute | solution.py:260
  38.1 1.5 %collective-permute-start.11 = (f32[8,128]{1,0:T(8,128)S(1)}, f32[8,128]{1,0:T(8,128)S(1)}, u32[]{:S(2)}, u32[]{:S(2)}) collective-permute-start(f32[8,128]{1,0:T(8,128)S(1)} %add.7.mine_ref), channel_id=1, source_target_pairs={{0,16},{4,20},{8,24},{12,28},{16,0},{20,4},{24,8},{28,12},{1,17},{... | collective-permute-start | bytes 12296 | tf_op jit(solution)/shard_map/ppermute | solution.py:260
  39.6 0.6 %shard_map.80.before_ref = f32[2,256,128]{2,1,0:T(8,128)S(1)} custom-call(bf16[2,384,256]{2,1,0:T(8,128)(2,1)S(1)} %copy-done.2, bf16[2,272,256]{2,1,0:T(8,128)(2,1)S(1)} %collective-permute-done.8.refs_1_.one_ref, bf16[2,272,256]{2,1,0:T(8,128)(2,1)S(1)} %collective-permute-done.2.block_ref.two_ref, bf16[4,2,384,256]{3,2,1,0:T(8,128)(2,1)S(1)} %shard_map.76.res_ref), custom_call_target="tpu_custom_call" | custom-call | flops 134217728 | bytes 3145728 | tf_op jit(solution)/shard_map/pallas_call | solution.py:243
  40.2 0.6 %collective-permute-done.9.three_ref = bf16[2,256,256]{2,1,0:T(8,128)(2,1)S(1)} collective-permute-done((bf16[2,256,256]{2,1,0:T(8,128)(2,1)S(1)}, bf16[2,256,256]{2,1,0:T(8,128)(2,1)S(1)}, u32[]{:S(2)}, u32[]{:S(2)}) %collective-permute-start.9) | collective-permute-done | bytes 262176 | tf_op jit(solution)/shard_map/ppermute | solution.py:260
  40.8 0.3 shard_map.81.looks_ref
  41.0 0.6 %collective-permute-done.11.other_ref = f32[8,128]{1,0:T(8,128)S(1)} collective-permute-done((f32[8,128]{1,0:T(8,128)S(1)}, f32[8,128]{1,0:T(8,128)S(1)}, u32[]{:S(2)}, u32[]{:S(2)}) %collective-permute-start.11) | collective-permute-done | bytes 4128 | tf_op jit(solution)/shard_map/ppermute | solution.py:260
  41.7 0.8 %shard_map.82 = f32[1,2,192,128]{3,2,1,0:T(8,128)} custom-call(f32[2,192,128]{2,1,0:T(8,128)S(1)} %shard_map.81.looks_ref, f32[8,128]{1,0:T(8,128)S(1)} %add.7.mine_ref, f32[8,128]{1,0:T(8,128)S(1)} %collective-permute-done.11.other_ref), custom_call_target="tpu_custom_call" | custom-call | flops 393216 | bytes 393216 | tf_op jit(solution)/shard_map/pallas_call | solution.py:243
  (14 shorter events, 0.1 us)
Async XLA Ops:
  0.0 15.0 %copy-start.2 = (bf16[2,384,256]{2,1,0:T(8,128)(2,1)S(1)}, bf16[2,384,256]{2,1,0:T(8,128)(2,1)}, u32[]{:S(2)}) copy-start(bf16[2,384,256]{2,1,0:T(8,128)(2,1)} %own_ref.3) | copy-start | bytes 1179652
  1.0 14.0 %collective-permute-start = (bf16[2,128,256]{2,1,0:T(8,128)(2,1)S(1)}, bf16[2,128,256]{2,1,0:T(8,128)(2,1)S(1)}, u32[]{:S(2)}, u32[]{:S(2)}) collective-permute-start(bf16[2,128,256]{2,1,0:T(8,128)(2,1)S(1)} %pad_maximum_fusion), channel_id=1, source_target_pairs={{0,2},{1,3},{2,0},{3,1},{4,6},{5,7},{6,4},{7,5},{8,10},{9,11},{10,... | collective-permute-start | bytes 393224 | tf_op jit(solution)/shard_map/ppermute | solution.py:260
  5.1 9.9 %collective-permute-start.1 = (bf16[2,128,256]{2,1,0:T(8,128)(2,1)S(1)}, bf16[2,128,256]{2,1,0:T(8,128)(2,1)S(1)}, u32[]{:S(2)}, u32[]{:S(2)}) collective-permute-start(bf16[2,128,256]{2,1,0:T(8,128)(2,1)S(1)} %pad_maximum_fusion), channel_id=1, source_target_pairs={{0,3},{1,2},{2,1},{3,0},{4,7},{5,6},{6,5},{7,4},{8,11},{9,10},{10,... | collective-permute-start | bytes 393224 | tf_op jit(solution)/shard_map/ppermute | solution.py:260
  6.4 1.4 %copy-start = (bf16[1,2,384,1024]{3,2,1,0:T(8,128)(2,1)S(1)}, bf16[1,2,384,1024]{3,2,1,0:T(8,128)(2,1)}, u32[]{:S(2)}) copy-start(bf16[1,2,384,1024]{3,2,1,0:T(8,128)(2,1)} %sec_ref.3) | copy-start | bytes 4718596
  7.8 12.0 %copy-start.1 = (bf16[1,2,384,1024]{3,2,1,0:T(8,128)(2,1)S(1)}, bf16[1,2,384,1024]{3,2,1,0:T(8,128)(2,1)}, u32[]{:S(2)}) copy-start(bf16[1,2,384,1024]{3,2,1,0:T(8,128)(2,1)} %sec_ref.3) | copy-start | bytes 4718596
  7.8 11.9 %collective-permute-start.4 = (bf16[2,32,1024]{2,1,0:T(8,128)(2,1)S(1)}, bf16[2,32,1024]{2,1,0:T(8,128)(2,1)S(1)}, u32[]{:S(2)}, u32[]{:S(2)}) collective-permute-start(bf16[2,32,1024]{2,1,0:T(8,128)(2,1)S(1)} %get-tuple-element.13), channel_id=1, source_target_pairs={{0,4},{4,8},{8,12},{12,16},{16,20},{20,24},{24,28},{28,0},{1,5},{5... | collective-permute-start | bytes 393224 | tf_op jit(solution)/shard_map/ppermute | solution.py:256
  7.9 11.9 %collective-permute-start.5 = (bf16[2,32,1024]{2,1,0:T(8,128)(2,1)S(1)}, bf16[2,32,1024]{2,1,0:T(8,128)(2,1)S(1)}, u32[]{:S(2)}, u32[]{:S(2)}) collective-permute-start(bf16[2,32,1024]{2,1,0:T(8,128)(2,1)S(1)} %get-tuple-element.14), channel_id=1, source_target_pairs={{0,28},{4,0},{8,4},{12,8},{16,12},{20,16},{24,20},{28,24},{1,29},{... | collective-permute-start | bytes 393224 | tf_op jit(solution)/shard_map/ppermute | solution.py:256
  10.5 10.6 %collective-permute-start.3 = (bf16[2,128,256]{2,1,0:T(8,128)(2,1)S(1)}, bf16[2,128,256]{2,1,0:T(8,128)(2,1)S(1)}, u32[]{:S(2)}, u32[]{:S(2)}) collective-permute-start(bf16[2,128,256]{2,1,0:T(8,128)(2,1)S(1)} %pad_maximum_fusion), channel_id=1, source_target_pairs={{0,1},{1,0},{2,3},{3,2},{4,5},{5,4},{6,7},{7,6},{8,9},{9,8},{10,11... | collective-permute-start | bytes 393224 | tf_op jit(solution)/shard_map/ppermute | solution.py:260
  15.0 17.6 %collective-permute-start.2 = (bf16[2,272,256]{2,1,0:T(8,128)(2,1)S(1)}, bf16[2,272,256]{2,1,0:T(8,128)(2,1)S(1)}, u32[]{:S(2)}, u32[]{:S(2)}) collective-permute-start(bf16[2,272,256]{2,1,0:T(8,128)(2,1)S(1)} %shard_map.74), channel_id=1, source_target_pairs={{0,2},{1,3},{2,0},{3,1},{4,6},{5,7},{6,4},{7,5},{8,10},{9,11},{10,... | collective-permute-start | bytes 835592 | tf_op jit(solution)/shard_map/ppermute | solution.py:260
  19.8 14.0 %collective-permute-start.8 = (bf16[2,272,256]{2,1,0:T(8,128)(2,1)S(1)}, bf16[2,272,256]{2,1,0:T(8,128)(2,1)S(1)}, u32[]{:S(2)}, u32[]{:S(2)}) collective-permute-start(bf16[2,272,256]{2,1,0:T(8,128)(2,1)S(1)} %shard_map.74), channel_id=1, source_target_pairs={{0,1},{1,0},{2,3},{3,2},{4,5},{5,4},{6,7},{7,6},{8,9},{9,8},{10,11... | collective-permute-start | bytes 835592 | tf_op jit(solution)/shard_map/ppermute | solution.py:260
  21.7 5.7 %collective-permute-start.6 = (bf16[2,64,1024]{2,1,0:T(8,128)(2,1)S(1)}, bf16[2,64,1024]{2,1,0:T(8,128)(2,1)S(1)}, u32[]{:S(2)}, u32[]{:S(2)}) collective-permute-start(bf16[2,64,1024]{2,1,0:T(8,128)(2,1)S(1)} %get-tuple-element.17), channel_id=1, source_target_pairs={{0,28},{4,0},{8,4},{12,8},{16,12},{20,16},{24,20},{28,24},{1,29},{... | collective-permute-start | bytes 786440 | tf_op jit(solution)/shard_map/ppermute | solution.py:256
  27.9 1.2 %collective-permute-start.7 = (f32[8,128]{1,0:T(8,128)S(1)}, f32[8,128]{1,0:T(8,128)S(1)}, u32[]{:S(2)}, u32[]{:S(2)}) collective-permute-start(f32[8,128]{1,0:T(8,128)S(1)} %shard_map.78), channel_id=1, source_target_pairs={{0,4},{4,0},{8,12},{12,8},{16,20},{20,16},{24,28},{28,24},{1,5},{5... | collective-permute-start | bytes 12296 | tf_op jit(solution)/shard_map/ppermute | solution.py:260
  33.8 7.0 %collective-permute-start.9 = (bf16[2,256,256]{2,1,0:T(8,128)(2,1)S(1)}, bf16[2,256,256]{2,1,0:T(8,128)(2,1)S(1)}, u32[]{:S(2)}, u32[]{:S(2)}) collective-permute-start(bf16[2,256,256]{2,1,0:T(8,128)(2,1)S(1)} %shard_map.79), channel_id=1, source_target_pairs={{0,1},{1,0},{2,3},{3,2},{4,5},{5,4},{6,7},{7,6},{8,9},{9,8},{10,11... | collective-permute-start | bytes 786440 | tf_op jit(solution)/shard_map/ppermute | solution.py:260
  34.4 3.6 %collective-permute-start.10 = (f32[8,128]{1,0:T(8,128)S(1)}, f32[8,128]{1,0:T(8,128)S(1)}, u32[]{:S(2)}, u32[]{:S(2)}) collective-permute-start(f32[8,128]{1,0:T(8,128)S(1)} %add.6), channel_id=1, source_target_pairs={{0,8},{4,12},{8,0},{12,4},{16,24},{20,28},{24,16},{28,20},{1,9},{5... | collective-permute-start | bytes 12296 | tf_op jit(solution)/shard_map/ppermute | solution.py:260
  38.1 3.6 %collective-permute-start.11 = (f32[8,128]{1,0:T(8,128)S(1)}, f32[8,128]{1,0:T(8,128)S(1)}, u32[]{:S(2)}, u32[]{:S(2)}) collective-permute-start(f32[8,128]{1,0:T(8,128)S(1)} %add.7.mine_ref), channel_id=1, source_target_pairs={{0,16},{4,20},{8,24},{12,28},{16,0},{20,4},{24,8},{28,12},{1,17},{... | collective-permute-start | bytes 12296 | tf_op jit(solution)/shard_map/ppermute | solution.py:260

commit v14 on v11

--- a/solution.py
+++ b/solution.py
@@ -53,8 +53,8 @@
     cut_ref[...] = prim_ref[:, LAG : LAG + cut_ref.shape[1]]
 
 
-def relay_kernel(block_ref, awaited_ref, out_ref):
-    del awaited_ref
+def relay_kernel(block_ref, *refs):
+    out_ref = refs[-1]
     out_ref[...] = block_ref[:, : out_ref.shape[1]]
 
 
@@ -283,8 +283,7 @@
         (0, 0),
         az_off, rg_off, az_frac, rg_frac,
     )
-    relayed = call(relay_kernel, edges, [], (0, 0), edges_two, az_band)
-    edges_three = swap(relayed, "date", 1)
+    edges_three = swap(edges_two, "date", 1)
     middle = call(
         cut_middle_kernel,
         shape((2, middle_n + 16, width), bf16),

time: 40.8 us -> 40.2 us (0.985)
  waiting for transfers between devices: 14.4 us -> 11.7 us
  starting transfers between devices: 15.8 us -> 18 us
    ppermute x9, waiting for transfers between devices: 11.5 us -> 8.8 us  [swap(): lax.ppermute(value, axis, [(at, at ^ step) for at in range(lax.axis_size(...]
    ppermute x3, starting transfers between devices: 2.75 us -> 4.19 us  [ring(): lax.ppermute(value, axis, [(at, (at + step) % count) for at in range(coun...]
    ppermute x9, starting transfers between devices: 13.1 us -> 13.8 us  [swap(): lax.ppermute(value, axis, [(at, at ^ step) for at in range(lax.axis_size(...]
    pallas_call x11 -> x10, Pallas kernels: 4.41 us -> 4.4 us  [call(): pl.pallas_call(kernel, out_shape=outs, in_specs=[vmem] * len(args), out_s...]
where the time goes in v14:
time: 40.2 us; the launch traced here: 40 us
  starting transfers between devices  18 us (45%)
  waiting for transfers between devices  11.7 us (29%)
  Pallas kernels  4.4 us (11%)
  between operations  2.75 us (7%)
  local copies, waits for them, and re-layouts  2.42 us (6%)
  other arithmetic  0.77 us (2%)
    ppermute x9, starting transfers between devices, swap(): lax.ppermute(value, axis, [(at, at ^ step) for at in range(lax.axis_size(...  13.8 us
    ppermute x9, waiting for transfers between devices, swap(): lax.ppermute(value, axis, [(at, at ^ step) for at in range(lax.axis_size(...  8.8 us
    pallas_call x10, Pallas kernels, call(): pl.pallas_call(kernel, out_shape=outs, in_specs=[vmem] * len(args), out_s...  4.4 us
    ppermute x3, starting transfers between devices, ring(): lax.ppermute(value, axis, [(at, (at + step) % count) for at in range(coun...  4.19 us
    ppermute x3, waiting for transfers between devices, ring(): lax.ppermute(value, axis, [(at, (at + step) % count) for at in range(coun...  2.86 us
    unnamed x6, local copies, waits for them, and re-layouts  1.41 us
    slice x1, local copies, waits for them, and re-layouts, fused(): primary[:, :LAG]  0.93 us
  transfers between devices with their start and end apart: 12, of which 5 were waited for; matrix products, arithmetic and copies ran while one was open for 2% of the time, Pallas kernels for 9%

profile of v14, /device:TPU:0, one launch (start us, length us, event | category | flops | bytes accessed | tf_op | source)
XLA Modules:
  0.0 40.0 jit_solution(14466727602425522353)
XLA Ops:
  0.0 0.9 %fusion = (bf16[2,64,256]{2,1,0:T(8,128)(2,1)S(1)}, bf16[2,64,256]{2,1,0:T(8,128)(2,1)S(1)}) fusion(bf16[2,384,256]{2,1,0:T(8,128)(2,1)} %own_ref.3), kind=kLoop, calls=%fused_computation.2 | loop fusion | bytes 262144 | tf_op jit(solution)/shard_map/slice | solution.py:272
  1.0 4.1 %collective-permute-start = (bf16[2,128,256]{2,1,0:T(8,128)(2,1)S(1)}, bf16[2,128,256]{2,1,0:T(8,128)(2,1)S(1)}, u32[]{:S(2)}, u32[]{:S(2)}) collective-permute-start(bf16[2,128,256]{2,1,0:T(8,128)(2,1)S(1)} %pad_maximum_fusion), channel_id=1, source_target_pairs={{0,2},{1,3},{2,0},{3,1},{4,6},{5,7},{6,4},{7,5},{8,10},{9,11},{10,... | collective-permute-start | bytes 393224 | tf_op jit(solution)/shard_map/ppermute | solution.py:260
  5.1 1.4 %copy-done = bf16[1,2,384,1024]{3,2,1,0:T(8,128)(2,1)S(1)} copy-done((bf16[1,2,384,1024]{3,2,1,0:T(8,128)(2,1)S(1)}, bf16[1,2,384,1024]{3,2,1,0:T(8,128)(2,1)}, u32[]{:S(2)}) %copy-start) | copy-done | bytes 1572888
  6.5 0.1 collective-permute-start.4
  6.6 2.6 %collective-permute-start.5 = (bf16[2,32,1024]{2,1,0:T(8,128)(2,1)S(1)}, bf16[2,32,1024]{2,1,0:T(8,128)(2,1)S(1)}, u32[]{:S(2)}, u32[]{:S(2)}) collective-permute-start(bf16[2,32,1024]{2,1,0:T(8,128)(2,1)S(1)} %get-tuple-element.13), channel_id=1, source_target_pairs={{0,28},{4,0},{8,4},{12,8},{16,12},{20,16},{24,20},{28,24},{1,29},{... | collective-permute-start | bytes 393224 | tf_op jit(solution)/shard_map/ppermute | solution.py:256
  9.2 1.6 %collective-permute-start.2 = (bf16[2,128,256]{2,1,0:T(8,128)(2,1)S(1)}, bf16[2,128,256]{2,1,0:T(8,128)(2,1)S(1)}, u32[]{:S(2)}, u32[]{:S(2)}) collective-permute-start(bf16[2,128,256]{2,1,0:T(8,128)(2,1)S(1)} %pad_maximum_fusion), channel_id=1, source_target_pairs={{0,1},{1,0},{2,3},{3,2},{4,5},{5,4},{6,7},{7,6},{8,9},{9,8},{10,11... | collective-permute-start | bytes 393224 | tf_op jit(solution)/shard_map/ppermute | solution.py:260
  10.8 0.7 %collective-permute-done.refs_0_.two_ref = bf16[2,128,256]{2,1,0:T(8,128)(2,1)S(1)} collective-permute-done((bf16[2,128,256]{2,1,0:T(8,128)(2,1)S(1)}, bf16[2,128,256]{2,1,0:T(8,128)(2,1)S(1)}, u32[]{:S(2)}, u32[]{:S(2)}) %collective-permute-start) | collective-permute-done | bytes 131104 | tf_op jit(solution)/shard_map/ppermute | solution.py:260
  11.4 0.7 %collective-permute-start.3 = (bf16[2,128,256]{2,1,0:T(8,128)(2,1)S(1)}, bf16[2,128,256]{2,1,0:T(8,128)(2,1)S(1)}, u32[]{:S(2)}, u32[]{:S(2)}) collective-permute-start(bf16[2,128,256]{2,1,0:T(8,128)(2,1)S(1)} %collective-permute-done.refs_0_.two_ref), channel_id=1, source_target_pairs={{0,1},{1,0},{2,3},{3,2},{4,5},{5,4},{6,7},{7,6},{8,9},{9,8},{10,11... | collective-permute-start | bytes 393224 | tf_op jit(solution)/shard_map/ppermute | solution.py:260
  12.2 3.5 %collective-permute-start.1 = (bf16[2,272,256]{2,1,0:T(8,128)(2,1)S(1)}, bf16[2,272,256]{2,1,0:T(8,128)(2,1)S(1)}, u32[]{:S(2)}, u32[]{:S(2)}) collective-permute-start(bf16[2,272,256]{2,1,0:T(8,128)(2,1)S(1)} %shard_map.73), channel_id=1, source_target_pairs={{0,2},{1,3},{2,0},{3,1},{4,6},{5,7},{6,4},{7,5},{8,10},{9,11},{10,... | collective-permute-start | bytes 835592 | tf_op jit(solution)/shard_map/ppermute | solution.py:260
  18.3 0.4 shard_map.75
  18.6 0.0 collective-permute-done.4.low_ref
  18.6 0.0 collective-permute-done.5.high_ref
  18.7 1.4 %shard_map.76.res_ref = bf16[4,2,384,256]{3,2,1,0:T(8,128)(2,1)S(1)} custom-call(bf16[1,2,384,1024]{3,2,1,0:T(8,128)(2,1)S(1)} %copy-done.1, bf16[2,32,1024]{2,1,0:T(8,128)(2,1)S(1)} %collective-permute-done.4.low_ref, bf16[2,32,1024]{2,1,0:T(8,128)(2,1)S(1)} %collective-permute-done.5.high_ref, bf16[128,192]{1,0:T(8,128)(2,1)S(1)} %get-tuple-element.14.az_ref, ...), custom_call_target="tpu_custom_call" | custom-call | tf_op jit(solution)/shard_map/pallas_call | solution.py:243
  20.1 0.0 collective-permute-done.2.one_ref
  20.1 0.0 collective-permute-done.3.three_ref
  20.1 0.5 %shard_map.77 = (bf16[2,64,1024]{2,1,0:T(8,128)(2,1)S(1)}, bf16[2,64,1024]{2,1,0:T(8,128)(2,1)S(1)}, f32[2,64,128]{2,1,0:T(8,128)S(1)}) custom-call(bf16[2,384,256]{2,1,0:T(8,128)(2,1)S(1)} %copy-done.2, bf16[2,128,256]{2,1,0:T(8,128)(2,1)S(1)} %collective-permute-done.2.one_ref, bf16[2,128,256]{2,1,0:T(8,128)(2,1)S(1)} %collective-permute-done.refs_0_.two_ref, ...), custom_call_target="tpu_custom_call" | custom-call | tf_op jit(solution)/shard_map/pallas_call | solution.py:243
  20.6 1.5 %collective-permute-start.6 = (bf16[2,64,1024]{2,1,0:T(8,128)(2,1)S(1)}, bf16[2,64,1024]{2,1,0:T(8,128)(2,1)S(1)}, u32[]{:S(2)}, u32[]{:S(2)}) collective-permute-start(bf16[2,64,1024]{2,1,0:T(8,128)(2,1)S(1)} %get-tuple-element.17), channel_id=1, source_target_pairs={{0,28},{4,0},{8,4},{12,8},{16,12},{20,16},{24,20},{28,24},{1,29},{... | collective-permute-start | bytes 786440 | tf_op jit(solution)/shard_map/ppermute | solution.py:256
  22.1 0.3 collective-permute-start.9
  22.4 0.8 %slice_convert_fusion = f32[64]{0:T(128)S(1)} fusion(s32[384]{0:T(512)} %param.9), kind=kLoop, calls=%fused_computation.1 | loop fusion | flops 64 | bytes 512 | tf_op jit(solution)/shard_map/convert_element_type | solution.py:294
  23.1 2.9 %collective-permute-done.6.later_ref = bf16[2,64,1024]{2,1,0:T(8,128)(2,1)S(1)} collective-permute-done((bf16[2,64,1024]{2,1,0:T(8,128)(2,1)S(1)}, bf16[2,64,1024]{2,1,0:T(8,128)(2,1)S(1)}, u32[]{:S(2)}, u32[]{:S(2)}) %collective-permute-start.6) | collective-permute-done | bytes 262176 | tf_op jit(solution)/shard_map/ppermute | solution.py:256
  26.0 0.1 broadcast_in_dim.2.weight_ref
  26.1 0.4 shard_map.78
  26.4 0.7 %collective-permute-start.7 = (f32[8,128]{1,0:T(8,128)S(1)}, f32[8,128]{1,0:T(8,128)S(1)}, u32[]{:S(2)}, u32[]{:S(2)}) collective-permute-start(f32[8,128]{1,0:T(8,128)S(1)} %shard_map.78), channel_id=1, source_target_pairs={{0,4},{4,0},{8,12},{12,8},{16,20},{20,16},{24,28},{28,24},{1,5},{5... | collective-permute-start | bytes 12296 | tf_op jit(solution)/shard_map/ppermute | solution.py:260
  27.1 1.2 %collective-permute-done.1.block_ref.two_ref = bf16[2,272,256]{2,1,0:T(8,128)(2,1)S(1)} collective-permute-done((bf16[2,272,256]{2,1,0:T(8,128)(2,1)S(1)}, bf16[2,272,256]{2,1,0:T(8,128)(2,1)S(1)}, u32[]{:S(2)}, u32[]{:S(2)}) %collective-permute-start.1) | collective-permute-done | bytes 278560 | tf_op jit(solution)/shard_map/ppermute | solution.py:260
  28.3 0.1 collective-permute-start.8
  28.4 1.6 %collective-permute-start.10 = (f32[8,128]{1,0:T(8,128)S(1)}, f32[8,128]{1,0:T(8,128)S(1)}, u32[]{:S(2)}, u32[]{:S(2)}) collective-permute-start(f32[8,128]{1,0:T(8,128)S(1)} %add.6), channel_id=1, source_target_pairs={{0,8},{4,12},{8,0},{12,4},{16,24},{20,28},{24,16},{28,20},{1,9},{5... | collective-permute-start | bytes 12296 | tf_op jit(solution)/shard_map/ppermute | solution.py:260
  30.0 4.3 %collective-permute-done.9.one_ref = bf16[2,272,256]{2,1,0:T(8,128)(2,1)S(1)} collective-permute-done((bf16[2,272,256]{2,1,0:T(8,128)(2,1)S(1)}, bf16[2,272,256]{2,1,0:T(8,128)(2,1)S(1)}, u32[]{:S(2)}, u32[]{:S(2)}) %collective-permute-start.9) | collective-permute-done | bytes 278560 | tf_op jit(solution)/shard_map/ppermute | solution.py:260
  34.3 0.6 %shard_map.80.before_ref = f32[2,256,128]{2,1,0:T(8,128)S(1)} custom-call(bf16[2,384,256]{2,1,0:T(8,128)(2,1)S(1)} %copy-done.2, bf16[2,272,256]{2,1,0:T(8,128)(2,1)S(1)} %collective-permute-done.9.one_ref, bf16[2,272,256]{2,1,0:T(8,128)(2,1)S(1)} %collective-permute-done.1.block_ref.two_ref, bf16[4,2,384,256]{3,2,1,0:T(8,128)(2,1)S(1)} %shard_map.76.res_ref), custom_call_target="tpu_custom_call" | custom-call | flops 134217728 | bytes 3145728 | tf_op jit(solution)/shard_map/pallas_call | solution.py:243
  34.9 1.2 %collective-permute-start.11 = (f32[8,128]{1,0:T(8,128)S(1)}, f32[8,128]{1,0:T(8,128)S(1)}, u32[]{:S(2)}, u32[]{:S(2)}) collective-permute-start(f32[8,128]{1,0:T(8,128)S(1)} %add.7.mine_ref), channel_id=1, source_target_pairs={{0,16},{4,20},{8,24},{12,28},{16,0},{20,4},{24,8},{28,12},{1,17},{... | collective-permute-start | bytes 12296 | tf_op jit(solution)/shard_map/ppermute | solution.py:260
  36.2 2.7 %collective-permute-done.8.three_ref = bf16[2,256,256]{2,1,0:T(8,128)(2,1)S(1)} collective-permute-done((bf16[2,256,256]{2,1,0:T(8,128)(2,1)S(1)}, bf16[2,256,256]{2,1,0:T(8,128)(2,1)S(1)}, u32[]{:S(2)}, u32[]{:S(2)}) %collective-permute-start.8) | collective-permute-done | bytes 262176 | tf_op jit(solution)/shard_map/ppermute | solution.py:260
  38.8 0.3 shard_map.81.looks_ref
  39.1 0.8 %shard_map.82 = f32[1,2,192,128]{3,2,1,0:T(8,128)} custom-call(f32[2,192,128]{2,1,0:T(8,128)S(1)} %shard_map.81.looks_ref, f32[8,128]{1,0:T(8,128)S(1)} %add.7.mine_ref, f32[8,128]{1,0:T(8,128)S(1)} %collective-permute-done.11.other_ref), custom_call_target="tpu_custom_call" | custom-call | flops 393216 | bytes 393216 | tf_op jit(solution)/shard_map/pallas_call | solution.py:243
  (14 shorter events, 0.1 us)
Async XLA Ops:
  0.0 12.1 %copy-start.2 = (bf16[2,384,256]{2,1,0:T(8,128)(2,1)S(1)}, bf16[2,384,256]{2,1,0:T(8,128)(2,1)}, u32[]{:S(2)}) copy-start(bf16[2,384,256]{2,1,0:T(8,128)(2,1)} %own_ref.3) | copy-start | bytes 1179652
  1.0 10.5 %collective-permute-start = (bf16[2,128,256]{2,1,0:T(8,128)(2,1)S(1)}, bf16[2,128,256]{2,1,0:T(8,128)(2,1)S(1)}, u32[]{:S(2)}, u32[]{:S(2)}) collective-permute-start(bf16[2,128,256]{2,1,0:T(8,128)(2,1)S(1)} %pad_maximum_fusion), channel_id=1, source_target_pairs={{0,2},{1,3},{2,0},{3,1},{4,6},{5,7},{6,4},{7,5},{8,10},{9,11},{10,... | collective-permute-start | bytes 393224 | tf_op jit(solution)/shard_map/ppermute | solution.py:260
  5.1 1.4 %copy-start = (bf16[1,2,384,1024]{3,2,1,0:T(8,128)(2,1)S(1)}, bf16[1,2,384,1024]{3,2,1,0:T(8,128)(2,1)}, u32[]{:S(2)}) copy-start(bf16[1,2,384,1024]{3,2,1,0:T(8,128)(2,1)} %sec_ref.3) | copy-start | bytes 4718596
  6.5 12.2 %copy-start.1 = (bf16[1,2,384,1024]{3,2,1,0:T(8,128)(2,1)S(1)}, bf16[1,2,384,1024]{3,2,1,0:T(8,128)(2,1)}, u32[]{:S(2)}) copy-start(bf16[1,2,384,1024]{3,2,1,0:T(8,128)(2,1)} %sec_ref.3) | copy-start | bytes 4718596
  6.5 12.1 %collective-permute-start.4 = (bf16[2,32,1024]{2,1,0:T(8,128)(2,1)S(1)}, bf16[2,32,1024]{2,1,0:T(8,128)(2,1)S(1)}, u32[]{:S(2)}, u32[]{:S(2)}) collective-permute-start(bf16[2,32,1024]{2,1,0:T(8,128)(2,1)S(1)} %get-tuple-element.12), channel_id=1, source_target_pairs={{0,4},{4,8},{8,12},{12,16},{16,20},{20,24},{24,28},{28,0},{1,5},{5... | collective-permute-start | bytes 393224 | tf_op jit(solution)/shard_map/ppermute | solution.py:256
  6.6 12.1 %collective-permute-start.5 = (bf16[2,32,1024]{2,1,0:T(8,128)(2,1)S(1)}, bf16[2,32,1024]{2,1,0:T(8,128)(2,1)S(1)}, u32[]{:S(2)}, u32[]{:S(2)}) collective-permute-start(bf16[2,32,1024]{2,1,0:T(8,128)(2,1)S(1)} %get-tuple-element.13), channel_id=1, source_target_pairs={{0,28},{4,0},{8,4},{12,8},{16,12},{20,16},{24,20},{28,24},{1,29},{... | collective-permute-start | bytes 393224 | tf_op jit(solution)/shard_map/ppermute | solution.py:256
  9.2 10.9 %collective-permute-start.2 = (bf16[2,128,256]{2,1,0:T(8,128)(2,1)S(1)}, bf16[2,128,256]{2,1,0:T(8,128)(2,1)S(1)}, u32[]{:S(2)}, u32[]{:S(2)}) collective-permute-start(bf16[2,128,256]{2,1,0:T(8,128)(2,1)S(1)} %pad_maximum_fusion), channel_id=1, source_target_pairs={{0,1},{1,0},{2,3},{3,2},{4,5},{5,4},{6,7},{7,6},{8,9},{9,8},{10,11... | collective-permute-start | bytes 393224 | tf_op jit(solution)/shard_map/ppermute | solution.py:260
  11.4 8.6 %collective-permute-start.3 = (bf16[2,128,256]{2,1,0:T(8,128)(2,1)S(1)}, bf16[2,128,256]{2,1,0:T(8,128)(2,1)S(1)}, u32[]{:S(2)}, u32[]{:S(2)}) collective-permute-start(bf16[2,128,256]{2,1,0:T(8,128)(2,1)S(1)} %collective-permute-done.refs_0_.two_ref), channel_id=1, source_target_pairs={{0,1},{1,0},{2,3},{3,2},{4,5},{5,4},{6,7},{7,6},{8,9},{9,8},{10,11... | collective-permute-start | bytes 393224 | tf_op jit(solution)/shard_map/ppermute | solution.py:260
  12.2 16.1 %collective-permute-start.1 = (bf16[2,272,256]{2,1,0:T(8,128)(2,1)S(1)}, bf16[2,272,256]{2,1,0:T(8,128)(2,1)S(1)}, u32[]{:S(2)}, u32[]{:S(2)}) collective-permute-start(bf16[2,272,256]{2,1,0:T(8,128)(2,1)S(1)} %shard_map.73), channel_id=1, source_target_pairs={{0,2},{1,3},{2,0},{3,1},{4,6},{5,7},{6,4},{7,5},{8,10},{9,11},{10,... | collective-permute-start | bytes 835592 | tf_op jit(solution)/shard_map/ppermute | solution.py:260
  20.6 5.4 %collective-permute-start.6 = (bf16[2,64,1024]{2,1,0:T(8,128)(2,1)S(1)}, bf16[2,64,1024]{2,1,0:T(8,128)(2,1)S(1)}, u32[]{:S(2)}, u32[]{:S(2)}) collective-permute-start(bf16[2,64,1024]{2,1,0:T(8,128)(2,1)S(1)} %get-tuple-element.17), channel_id=1, source_target_pairs={{0,28},{4,0},{8,4},{12,8},{16,12},{20,16},{24,20},{28,24},{1,29},{... | collective-permute-start | bytes 786440 | tf_op jit(solution)/shard_map/ppermute | solution.py:256
  22.1 12.2 %collective-permute-start.9 = (bf16[2,272,256]{2,1,0:T(8,128)(2,1)S(1)}, bf16[2,272,256]{2,1,0:T(8,128)(2,1)S(1)}, u32[]{:S(2)}, u32[]{:S(2)}) collective-permute-start(bf16[2,272,256]{2,1,0:T(8,128)(2,1)S(1)} %shard_map.73), channel_id=1, source_target_pairs={{0,1},{1,0},{2,3},{3,2},{4,5},{5,4},{6,7},{7,6},{8,9},{9,8},{10,11... | collective-permute-start | bytes 835592 | tf_op jit(solution)/shard_map/ppermute | solution.py:260
  26.4 1.9 %collective-permute-start.7 = (f32[8,128]{1,0:T(8,128)S(1)}, f32[8,128]{1,0:T(8,128)S(1)}, u32[]{:S(2)}, u32[]{:S(2)}) collective-permute-start(f32[8,128]{1,0:T(8,128)S(1)} %shard_map.78), channel_id=1, source_target_pairs={{0,4},{4,0},{8,12},{12,8},{16,20},{20,16},{24,28},{28,24},{1,5},{5... | collective-permute-start | bytes 12296 | tf_op jit(solution)/shard_map/ppermute | solution.py:260
  28.3 10.5 %collective-permute-start.8 = (bf16[2,256,256]{2,1,0:T(8,128)(2,1)S(1)}, bf16[2,256,256]{2,1,0:T(8,128)(2,1)S(1)}, u32[]{:S(2)}, u32[]{:S(2)}) collective-permute-start(bf16[2,256,256]{2,1,0:T(8,128)(2,1)S(1)} %shard_map.79), channel_id=1, source_target_pairs={{0,1},{1,0},{2,3},{3,2},{4,5},{5,4},{6,7},{7,6},{8,9},{9,8},{10,11... | collective-permute-start | bytes 786440 | tf_op jit(solution)/shard_map/ppermute | solution.py:260
  28.4 6.5 %collective-permute-start.10 = (f32[8,128]{1,0:T(8,128)S(1)}, f32[8,128]{1,0:T(8,128)S(1)}, u32[]{:S(2)}, u32[]{:S(2)}) collective-permute-start(f32[8,128]{1,0:T(8,128)S(1)} %add.6), channel_id=1, source_target_pairs={{0,8},{4,12},{8,0},{12,4},{16,24},{20,28},{24,16},{28,20},{1,9},{5... | collective-permute-start | bytes 12296 | tf_op jit(solution)/shard_map/ppermute | solution.py:260
  34.9 4.2 %collective-permute-start.11 = (f32[8,128]{1,0:T(8,128)S(1)}, f32[8,128]{1,0:T(8,128)S(1)}, u32[]{:S(2)}, u32[]{:S(2)}) collective-permute-start(f32[8,128]{1,0:T(8,128)S(1)} %add.7.mine_ref), channel_id=1, source_target_pairs={{0,16},{4,20},{8,24},{12,28},{16,0},{20,4},{24,8},{28,12},{1,17},{... | collective-permute-start | bytes 12296 | tf_op jit(solution)/shard_map/ppermute | solution.py:260

commit v15 on v14

--- a/solution.py
+++ b/solution.py
@@ -325,7 +325,7 @@
     )
     other = swap(stats, "tile", 1)
     block = shape((2, middle_n, width), bf16)
-    relayed = call(relay_kernel, block, [], (0, 0), two, other)
+    relayed = call(relay_kernel, block, [], (0, 0), two, other,one)
     three = swap(relayed, "date", 1)
     stride = 2
     while stride < tiles_n:

time: 40.2 us -> 38.9 us (0.968)
  waiting for transfers between devices: 11.7 us -> 9.44 us
  starting transfers between devices: 18 us -> 19 us
    ppermute x9, waiting for transfers between devices: 8.8 us -> 6.3 us  [swap(): lax.ppermute(value, axis, [(at, at ^ step) for at in range(lax.axis_size(...]
    ppermute x9, starting transfers between devices: 13.8 us -> 14.8 us  [swap(): lax.ppermute(value, axis, [(at, at ^ step) for at in range(lax.axis_size(...]
  transfers between devices with their start and end apart: 12 -> 12, of which waited for: 5 -> 7; matrix products, arithmetic and copies ran while one was open for 2% -> 2% of each run, Pallas kernels for 9% -> 9%
where the time goes in v15:
time: 38.9 us; the launch traced here: 38.7 us
  starting transfers between devices  19 us (49%)
  waiting for transfers between devices  9.44 us (24%)
  Pallas kernels  4.4 us (11%)
  between operations  2.7 us (7%)
  local copies, waits for them, and re-layouts  2.42 us (6%)
  other arithmetic  0.77 us (2%)
    ppermute x9, starting transfers between devices, swap(): lax.ppermute(value, axis, [(at, at ^ step) for at in range(lax.axis_size(...  14.8 us
    ppermute x9, waiting for transfers between devices, swap(): lax.ppermute(value, axis, [(at, at ^ step) for at in range(lax.axis_size(...  6.3 us
    pallas_call x10, Pallas kernels, call(): pl.pallas_call(kernel, out_shape=outs, in_specs=[vmem] * len(args), out_s...  4.4 us
    ppermute x3, starting transfers between devices, ring(): lax.ppermute(value, axis, [(at, (at + step) % count) for at in range(coun...  4.19 us
    ppermute x3, waiting for transfers between devices, ring(): lax.ppermute(value, axis, [(at, (at + step) % count) for at in range(coun...  3.14 us
    unnamed x6, local copies, waits for them, and re-layouts  1.41 us
    slice x1, local copies, waits for them, and re-layouts, fused(): primary[:, :LAG]  0.93 us
  transfers between devices with their start and end apart: 12, of which 7 were waited for; matrix products, arithmetic and copies ran while one was open for 2% of the time, Pallas kernels for 9%

profile of v15, /device:TPU:0, one launch (start us, length us, event | category | flops | bytes accessed | tf_op | source)
XLA Modules:
  0.0 38.7 jit_solution(2414447459376362099)
XLA Ops:
  0.0 0.9 %fusion = (bf16[2,64,256]{2,1,0:T(8,128)(2,1)S(1)}, bf16[2,64,256]{2,1,0:T(8,128)(2,1)S(1)}) fusion(bf16[2,384,256]{2,1,0:T(8,128)(2,1)} %own_ref.3), kind=kLoop, calls=%fused_computation.2 | loop fusion | bytes 262144 | tf_op jit(solution)/shard_map/slice | solution.py:272
  1.0 4.1 %collective-permute-start = (bf16[2,128,256]{2,1,0:T(8,128)(2,1)S(1)}, bf16[2,128,256]{2,1,0:T(8,128)(2,1)S(1)}, u32[]{:S(2)}, u32[]{:S(2)}) collective-permute-start(bf16[2,128,256]{2,1,0:T(8,128)(2,1)S(1)} %pad_maximum_fusion), channel_id=1, source_target_pairs={{0,2},{1,3},{2,0},{3,1},{4,6},{5,7},{6,4},{7,5},{8,10},{9,11},{10,... | collective-permute-start | bytes 393224 | tf_op jit(solution)/shard_map/ppermute | solution.py:260
  5.1 1.4 %copy-done = bf16[1,2,384,1024]{3,2,1,0:T(8,128)(2,1)S(1)} copy-done((bf16[1,2,384,1024]{3,2,1,0:T(8,128)(2,1)S(1)}, bf16[1,2,384,1024]{3,2,1,0:T(8,128)(2,1)}, u32[]{:S(2)}) %copy-start) | copy-done | bytes 1572888
  6.5 0.1 collective-permute-start.4
  6.6 2.6 %collective-permute-start.5 = (bf16[2,32,1024]{2,1,0:T(8,128)(2,1)S(1)}, bf16[2,32,1024]{2,1,0:T(8,128)(2,1)S(1)}, u32[]{:S(2)}, u32[]{:S(2)}) collective-permute-start(bf16[2,32,1024]{2,1,0:T(8,128)(2,1)S(1)} %get-tuple-element.13), channel_id=1, source_target_pairs={{0,28},{4,0},{8,4},{12,8},{16,12},{20,16},{24,20},{28,24},{1,29},{... | collective-permute-start | bytes 393224 | tf_op jit(solution)/shard_map/ppermute | solution.py:256
  9.2 1.6 %collective-permute-start.2 = (bf16[2,128,256]{2,1,0:T(8,128)(2,1)S(1)}, bf16[2,128,256]{2,1,0:T(8,128)(2,1)S(1)}, u32[]{:S(2)}, u32[]{:S(2)}) collective-permute-start(bf16[2,128,256]{2,1,0:T(8,128)(2,1)S(1)} %pad_maximum_fusion), channel_id=1, source_target_pairs={{0,1},{1,0},{2,3},{3,2},{4,5},{5,4},{6,7},{7,6},{8,9},{9,8},{10,11... | collective-permute-start | bytes 393224 | tf_op jit(solution)/shard_map/ppermute | solution.py:260
  10.8 0.7 %collective-permute-done.refs_0_.two_ref = bf16[2,128,256]{2,1,0:T(8,128)(2,1)S(1)} collective-permute-done((bf16[2,128,256]{2,1,0:T(8,128)(2,1)S(1)}, bf16[2,128,256]{2,1,0:T(8,128)(2,1)S(1)}, u32[]{:S(2)}, u32[]{:S(2)}) %collective-permute-start) | collective-permute-done | bytes 131104 | tf_op jit(solution)/shard_map/ppermute | solution.py:260
  11.4 0.7 %collective-permute-start.3 = (bf16[2,128,256]{2,1,0:T(8,128)(2,1)S(1)}, bf16[2,128,256]{2,1,0:T(8,128)(2,1)S(1)}, u32[]{:S(2)}, u32[]{:S(2)}) collective-permute-start(bf16[2,128,256]{2,1,0:T(8,128)(2,1)S(1)} %collective-permute-done.refs_0_.two_ref), channel_id=1, source_target_pairs={{0,1},{1,0},{2,3},{3,2},{4,5},{5,4},{6,7},{7,6},{8,9},{9,8},{10,11... | collective-permute-start | bytes 393224 | tf_op jit(solution)/shard_map/ppermute | solution.py:260
  12.2 3.5 %collective-permute-start.1 = (bf16[2,272,256]{2,1,0:T(8,128)(2,1)S(1)}, bf16[2,272,256]{2,1,0:T(8,128)(2,1)S(1)}, u32[]{:S(2)}, u32[]{:S(2)}) collective-permute-start(bf16[2,272,256]{2,1,0:T(8,128)(2,1)S(1)} %shard_map.73), channel_id=1, source_target_pairs={{0,2},{1,3},{2,0},{3,1},{4,6},{5,7},{6,4},{7,5},{8,10},{9,11},{10,... | collective-permute-start | bytes 835592 | tf_op jit(solution)/shard_map/ppermute | solution.py:260
  15.7 0.0 collective-permute-done.4.low_ref
  15.7 0.0 collective-permute-start.8
  18.3 0.4 shard_map.75
  18.6 1.4 %shard_map.76.res_ref = bf16[4,2,384,256]{3,2,1,0:T(8,128)(2,1)S(1)} custom-call(bf16[1,2,384,1024]{3,2,1,0:T(8,128)(2,1)S(1)} %copy-done.1, bf16[2,32,1024]{2,1,0:T(8,128)(2,1)S(1)} %collective-permute-done.4.low_ref, bf16[2,32,1024]{2,1,0:T(8,128)(2,1)S(1)} %collective-permute-done.5.high_ref, bf16[128,192]{1,0:T(8,128)(2,1)S(1)} %get-tuple-element.14.az_ref, ...), custom_call_target="tpu_custom_call" | custom-call | tf_op jit(solution)/shard_map/pallas_call | solution.py:243
  20.1 0.0 collective-permute-done.3.three_ref
  20.1 0.5 %shard_map.77 = (bf16[2,64,1024]{2,1,0:T(8,128)(2,1)S(1)}, bf16[2,64,1024]{2,1,0:T(8,128)(2,1)S(1)}, f32[2,64,128]{2,1,0:T(8,128)S(1)}) custom-call(bf16[2,384,256]{2,1,0:T(8,128)(2,1)S(1)} %copy-done.2, bf16[2,128,256]{2,1,0:T(8,128)(2,1)S(1)} %collective-permute-done.2.one_ref, bf16[2,128,256]{2,1,0:T(8,128)(2,1)S(1)} %collective-permute-done.refs_0_.two_ref, ...), custom_call_target="tpu_custom_call" | custom-call | tf_op jit(solution)/shard_map/pallas_call | solution.py:243
  20.6 1.5 %collective-permute-start.6 = (bf16[2,64,1024]{2,1,0:T(8,128)(2,1)S(1)}, bf16[2,64,1024]{2,1,0:T(8,128)(2,1)S(1)}, u32[]{:S(2)}, u32[]{:S(2)}) collective-permute-start(bf16[2,64,1024]{2,1,0:T(8,128)(2,1)S(1)} %get-tuple-element.17), channel_id=1, source_target_pairs={{0,28},{4,0},{8,4},{12,8},{16,12},{20,16},{24,20},{28,24},{1,29},{... | collective-permute-start | bytes 786440 | tf_op jit(solution)/shard_map/ppermute | solution.py:256
  22.1 0.8 %slice_convert_fusion = f32[64]{0:T(128)S(1)} fusion(s32[384]{0:T(512)} %param.9), kind=kLoop, calls=%fused_computation.1 | loop fusion | flops 64 | bytes 512 | tf_op jit(solution)/shard_map/convert_element_type | solution.py:294
  22.9 3.1 %collective-permute-done.6.later_ref = bf16[2,64,1024]{2,1,0:T(8,128)(2,1)S(1)} collective-permute-done((bf16[2,64,1024]{2,1,0:T(8,128)(2,1)S(1)}, bf16[2,64,1024]{2,1,0:T(8,128)(2,1)S(1)}, u32[]{:S(2)}, u32[]{:S(2)}) %collective-permute-start.6) | collective-permute-done | bytes 262176 | tf_op jit(solution)/shard_map/ppermute | solution.py:256
  26.0 0.1 broadcast_in_dim.2.weight_ref
  26.1 0.4 shard_map.78
  26.4 0.8 %collective-permute-start.7 = (f32[8,128]{1,0:T(8,128)S(1)}, f32[8,128]{1,0:T(8,128)S(1)}, u32[]{:S(2)}, u32[]{:S(2)}) collective-permute-start(f32[8,128]{1,0:T(8,128)S(1)} %shard_map.78), channel_id=1, source_target_pairs={{0,4},{4,0},{8,12},{12,8},{16,20},{20,16},{24,28},{28,24},{1,5},{5... | collective-permute-start | bytes 12296 | tf_op jit(solution)/shard_map/ppermute | solution.py:260
  27.2 1.1 %collective-permute-done.1.block_ref.two_ref = bf16[2,272,256]{2,1,0:T(8,128)(2,1)S(1)} collective-permute-done((bf16[2,272,256]{2,1,0:T(8,128)(2,1)S(1)}, bf16[2,272,256]{2,1,0:T(8,128)(2,1)S(1)}, u32[]{:S(2)}, u32[]{:S(2)}) %collective-permute-start.1) | collective-permute-done | bytes 278560 | tf_op jit(solution)/shard_map/ppermute | solution.py:260
  28.3 0.6 %collective-permute-done.8.refs_1_.one_ref = bf16[2,272,256]{2,1,0:T(8,128)(2,1)S(1)} collective-permute-done((bf16[2,272,256]{2,1,0:T(8,128)(2,1)S(1)}, bf16[2,272,256]{2,1,0:T(8,128)(2,1)S(1)}, u32[]{:S(2)}, u32[]{:S(2)}) %collective-permute-start.8) | collective-permute-done | bytes 278560 | tf_op jit(solution)/shard_map/ppermute | solution.py:260
  28.9 1.7 %collective-permute-start.9 = (bf16[2,256,256]{2,1,0:T(8,128)(2,1)S(1)}, bf16[2,256,256]{2,1,0:T(8,128)(2,1)S(1)}, u32[]{:S(2)}, u32[]{:S(2)}) collective-permute-start(bf16[2,256,256]{2,1,0:T(8,128)(2,1)S(1)} %shard_map.79), channel_id=1, source_target_pairs={{0,1},{1,0},{2,3},{3,2},{4,5},{5,4},{6,7},{7,6},{8,9},{9,8},{10,11... | collective-permute-start | bytes 786440 | tf_op jit(solution)/shard_map/ppermute | solution.py:260
  30.6 0.9 %collective-permute-start.10 = (f32[8,128]{1,0:T(8,128)S(1)}, f32[8,128]{1,0:T(8,128)S(1)}, u32[]{:S(2)}, u32[]{:S(2)}) collective-permute-start(f32[8,128]{1,0:T(8,128)S(1)} %add.6), channel_id=1, source_target_pairs={{0,8},{4,12},{8,0},{12,4},{16,24},{20,28},{24,16},{28,20},{1,9},{5... | collective-permute-start | bytes 12296 | tf_op jit(solution)/shard_map/ppermute | solution.py:260
  31.5 0.6 %shard_map.80.before_ref = f32[2,256,128]{2,1,0:T(8,128)S(1)} custom-call(bf16[2,384,256]{2,1,0:T(8,128)(2,1)S(1)} %copy-done.2, bf16[2,272,256]{2,1,0:T(8,128)(2,1)S(1)} %collective-permute-done.8.refs_1_.one_ref, bf16[2,272,256]{2,1,0:T(8,128)(2,1)S(1)} %collective-permute-done.1.block_ref.two_ref, bf16[4,2,384,256]{3,2,1,0:T(8,128)(2,1)S(1)} %shard_map.76.res_ref), custom_call_target="tpu_custom_call" | custom-call | flops 134217728 | bytes 3145728 | tf_op jit(solution)/shard_map/pallas_call | solution.py:243
  32.1 2.1 %collective-permute-done.10 = f32[8,128]{1,0:T(8,128)S(1)} collective-permute-done((f32[8,128]{1,0:T(8,128)S(1)}, f32[8,128]{1,0:T(8,128)S(1)}, u32[]{:S(2)}, u32[]{:S(2)}) %collective-permute-start.10) | collective-permute-done | bytes 4128 | tf_op jit(solution)/shard_map/ppermute | solution.py:260
  34.2 1.5 %collective-permute-start.11 = (f32[8,128]{1,0:T(8,128)S(1)}, f32[8,128]{1,0:T(8,128)S(1)}, u32[]{:S(2)}, u32[]{:S(2)}) collective-permute-start(f32[8,128]{1,0:T(8,128)S(1)} %add.7.mine_ref), channel_id=1, source_target_pairs={{0,16},{4,20},{8,24},{12,28},{16,0},{20,4},{24,8},{28,12},{1,17},{... | collective-permute-start | bytes 12296 | tf_op jit(solution)/shard_map/ppermute | solution.py:260
  35.8 1.1 %collective-permute-done.9.three_ref = bf16[2,256,256]{2,1,0:T(8,128)(2,1)S(1)} collective-permute-done((bf16[2,256,256]{2,1,0:T(8,128)(2,1)S(1)}, bf16[2,256,256]{2,1,0:T(8,128)(2,1)S(1)}, u32[]{:S(2)}, u32[]{:S(2)}) %collective-permute-start.9) | collective-permute-done | bytes 262176 | tf_op jit(solution)/shard_map/ppermute | solution.py:260
  36.9 0.3 shard_map.81.looks_ref
  37.1 0.7 %collective-permute-done.11.other_ref = f32[8,128]{1,0:T(8,128)S(1)} collective-permute-done((f32[8,128]{1,0:T(8,128)S(1)}, f32[8,128]{1,0:T(8,128)S(1)}, u32[]{:S(2)}, u32[]{:S(2)}) %collective-permute-start.11) | collective-permute-done | bytes 4128 | tf_op jit(solution)/shard_map/ppermute | solution.py:260
  37.8 0.8 %shard_map.82 = f32[1,2,192,128]{3,2,1,0:T(8,128)} custom-call(f32[2,192,128]{2,1,0:T(8,128)S(1)} %shard_map.81.looks_ref, f32[8,128]{1,0:T(8,128)S(1)} %add.7.mine_ref, f32[8,128]{1,0:T(8,128)S(1)} %collective-permute-done.11.other_ref), custom_call_target="tpu_custom_call" | custom-call | flops 393216 | bytes 393216 | tf_op jit(solution)/shard_map/pallas_call | solution.py:243
  (14 shorter events, 0.1 us)
Async XLA Ops:
  0.0 12.1 %copy-start.2 = (bf16[2,384,256]{2,1,0:T(8,128)(2,1)S(1)}, bf16[2,384,256]{2,1,0:T(8,128)(2,1)}, u32[]{:S(2)}) copy-start(bf16[2,384,256]{2,1,0:T(8,128)(2,1)} %own_ref.3) | copy-start | bytes 1179652
  1.0 10.5 %collective-permute-start = (bf16[2,128,256]{2,1,0:T(8,128)(2,1)S(1)}, bf16[2,128,256]{2,1,0:T(8,128)(2,1)S(1)}, u32[]{:S(2)}, u32[]{:S(2)}) collective-permute-start(bf16[2,128,256]{2,1,0:T(8,128)(2,1)S(1)} %pad_maximum_fusion), channel_id=1, source_target_pairs={{0,2},{1,3},{2,0},{3,1},{4,6},{5,7},{6,4},{7,5},{8,10},{9,11},{10,... | collective-permute-start | bytes 393224 | tf_op jit(solution)/shard_map/ppermute | solution.py:260
  5.1 1.4 %copy-start = (bf16[1,2,384,1024]{3,2,1,0:T(8,128)(2,1)S(1)}, bf16[1,2,384,1024]{3,2,1,0:T(8,128)(2,1)}, u32[]{:S(2)}) copy-start(bf16[1,2,384,1024]{3,2,1,0:T(8,128)(2,1)} %sec_ref.3) | copy-start | bytes 4718596
  6.5 12.2 %copy-start.1 = (bf16[1,2,384,1024]{3,2,1,0:T(8,128)(2,1)S(1)}, bf16[1,2,384,1024]{3,2,1,0:T(8,128)(2,1)}, u32[]{:S(2)}) copy-start(bf16[1,2,384,1024]{3,2,1,0:T(8,128)(2,1)} %sec_ref.3) | copy-start | bytes 4718596
  6.5 9.2 %collective-permute-start.4 = (bf16[2,32,1024]{2,1,0:T(8,128)(2,1)S(1)}, bf16[2,32,1024]{2,1,0:T(8,128)(2,1)S(1)}, u32[]{:S(2)}, u32[]{:S(2)}) collective-permute-start(bf16[2,32,1024]{2,1,0:T(8,128)(2,1)S(1)} %get-tuple-element.12), channel_id=1, source_target_pairs={{0,4},{4,8},{8,12},{12,16},{16,20},{20,24},{24,28},{28,0},{1,5},{5... | collective-permute-start | bytes 393224 | tf_op jit(solution)/shard_map/ppermute | solution.py:256
  6.6 12.1 %collective-permute-start.5 = (bf16[2,32,1024]{2,1,0:T(8,128)(2,1)S(1)}, bf16[2,32,1024]{2,1,0:T(8,128)(2,1)S(1)}, u32[]{:S(2)}, u32[]{:S(2)}) collective-permute-start(bf16[2,32,1024]{2,1,0:T(8,128)(2,1)S(1)} %get-tuple-element.13), channel_id=1, source_target_pairs={{0,28},{4,0},{8,4},{12,8},{16,12},{20,16},{24,20},{28,24},{1,29},{... | collective-permute-start | bytes 393224 | tf_op jit(solution)/shard_map/ppermute | solution.py:256
  9.2 10.9 %collective-permute-start.2 = (bf16[2,128,256]{2,1,0:T(8,128)(2,1)S(1)}, bf16[2,128,256]{2,1,0:T(8,128)(2,1)S(1)}, u32[]{:S(2)}, u32[]{:S(2)}) collective-permute-start(bf16[2,128,256]{2,1,0:T(8,128)(2,1)S(1)} %pad_maximum_fusion), channel_id=1, source_target_pairs={{0,1},{1,0},{2,3},{3,2},{4,5},{5,4},{6,7},{7,6},{8,9},{9,8},{10,11... | collective-permute-start | bytes 393224 | tf_op jit(solution)/shard_map/ppermute | solution.py:260
  11.4 8.7 %collective-permute-start.3 = (bf16[2,128,256]{2,1,0:T(8,128)(2,1)S(1)}, bf16[2,128,256]{2,1,0:T(8,128)(2,1)S(1)}, u32[]{:S(2)}, u32[]{:S(2)}) collective-permute-start(bf16[2,128,256]{2,1,0:T(8,128)(2,1)S(1)} %collective-permute-done.refs_0_.two_ref), channel_id=1, source_target_pairs={{0,1},{1,0},{2,3},{3,2},{4,5},{5,4},{6,7},{7,6},{8,9},{9,8},{10,11... | collective-permute-start | bytes 393224 | tf_op jit(solution)/shard_map/ppermute | solution.py:260
  12.2 16.1 %collective-permute-start.1 = (bf16[2,272,256]{2,1,0:T(8,128)(2,1)S(1)}, bf16[2,272,256]{2,1,0:T(8,128)(2,1)S(1)}, u32[]{:S(2)}, u32[]{:S(2)}) collective-permute-start(bf16[2,272,256]{2,1,0:T(8,128)(2,1)S(1)} %shard_map.73), channel_id=1, source_target_pairs={{0,2},{1,3},{2,0},{3,1},{4,6},{5,7},{6,4},{7,5},{8,10},{9,11},{10,... | collective-permute-start | bytes 835592 | tf_op jit(solution)/shard_map/ppermute | solution.py:260
  15.7 13.3 %collective-permute-start.8 = (bf16[2,272,256]{2,1,0:T(8,128)(2,1)S(1)}, bf16[2,272,256]{2,1,0:T(8,128)(2,1)S(1)}, u32[]{:S(2)}, u32[]{:S(2)}) collective-permute-start(bf16[2,272,256]{2,1,0:T(8,128)(2,1)S(1)} %shard_map.73), channel_id=1, source_target_pairs={{0,1},{1,0},{2,3},{3,2},{4,5},{5,4},{6,7},{7,6},{8,9},{9,8},{10,11... | collective-permute-start | bytes 835592 | tf_op jit(solution)/shard_map/ppermute | solution.py:260
  20.6 5.4 %collective-permute-start.6 = (bf16[2,64,1024]{2,1,0:T(8,128)(2,1)S(1)}, bf16[2,64,1024]{2,1,0:T(8,128)(2,1)S(1)}, u32[]{:S(2)}, u32[]{:S(2)}) collective-permute-start(bf16[2,64,1024]{2,1,0:T(8,128)(2,1)S(1)} %get-tuple-element.17), channel_id=1, source_target_pairs={{0,28},{4,0},{8,4},{12,8},{16,12},{20,16},{24,20},{28,24},{1,29},{... | collective-permute-start | bytes 786440 | tf_op jit(solution)/shard_map/ppermute | solution.py:256
  26.4 2.5 %collective-permute-start.7 = (f32[8,128]{1,0:T(8,128)S(1)}, f32[8,128]{1,0:T(8,128)S(1)}, u32[]{:S(2)}, u32[]{:S(2)}) collective-permute-start(f32[8,128]{1,0:T(8,128)S(1)} %shard_map.78), channel_id=1, source_target_pairs={{0,4},{4,0},{8,12},{12,8},{16,20},{20,16},{24,28},{28,24},{1,5},{5... | collective-permute-start | bytes 12296 | tf_op jit(solution)/shard_map/ppermute | solution.py:260
  28.9 7.9 %collective-permute-start.9 = (bf16[2,256,256]{2,1,0:T(8,128)(2,1)S(1)}, bf16[2,256,256]{2,1,0:T(8,128)(2,1)S(1)}, u32[]{:S(2)}, u32[]{:S(2)}) collective-permute-start(bf16[2,256,256]{2,1,0:T(8,128)(2,1)S(1)} %shard_map.79), channel_id=1, source_target_pairs={{0,1},{1,0},{2,3},{3,2},{4,5},{5,4},{6,7},{7,6},{8,9},{9,8},{10,11... | collective-permute-start | bytes 786440 | tf_op jit(solution)/shard_map/ppermute | solution.py:260
  30.6 3.6 %collective-permute-start.10 = (f32[8,128]{1,0:T(8,128)S(1)}, f32[8,128]{1,0:T(8,128)S(1)}, u32[]{:S(2)}, u32[]{:S(2)}) collective-permute-start(f32[8,128]{1,0:T(8,128)S(1)} %add.6), channel_id=1, source_target_pairs={{0,8},{4,12},{8,0},{12,4},{16,24},{20,28},{24,16},{28,20},{1,9},{5... | collective-permute-start | bytes 12296 | tf_op jit(solution)/shard_map/ppermute | solution.py:260
  34.2 3.6 %collective-permute-start.11 = (f32[8,128]{1,0:T(8,128)S(1)}, f32[8,128]{1,0:T(8,128)S(1)}, u32[]{:S(2)}, u32[]{:S(2)}) collective-permute-start(f32[8,128]{1,0:T(8,128)S(1)} %add.7.mine_ref), channel_id=1, source_target_pairs={{0,16},{4,20},{8,24},{12,28},{16,0},{20,4},{24,8},{28,12},{1,17},{... | collective-permute-start | bytes 12296 | tf_op jit(solution)/shard_map/ppermute | solution.py:260

commit v16 on v15

--- a/solution.py
+++ b/solution.py
@@ -14,6 +14,7 @@
 LANE = 128
 BAND = 128
 HALO = 32
+HOP_ROUND = 4
 VMEM_LIMIT = 40 * 1024 * 1024
 
 
@@ -215,27 +216,31 @@
         out_ref[part] = total
 
 
-def last_kernel(three_ref, res_ref, before_ref, looks_ref, out_ref, sums_ref):
-    middle_n = before_ref.shape[1]
-    edge = LAG // LA
-    totals = look_sums(((3, three_ref),), res_ref, out_ref.shape[2])
-    for part, total in enumerate(totals):
-        sums_ref[part] = total + before_ref[part]
-        out_ref[part, :edge] = looks_ref[part, :edge]
-        out_ref[part, edge : edge + middle_n // LA] = look_rows(sums_ref, part, 0, middle_n)
-        out_ref[part, edge + middle_n // LA :] = looks_ref[part, edge:]
-
-
-def scale_kernel(looks_ref, mine_ref, other_ref, out_ref):
+def unit_kernel(mine_ref, other_ref, unit_ref):
     stats = jnp.sum(mine_ref[...] + other_ref[...], axis=1, keepdims=True)
     e_re, e_im, power, count = [stats[row : row + 1] for row in range(4)]
     magnitude = jnp.sqrt(e_re * e_re + e_im * e_im)
     floor_val = (power + 1e-06) / jnp.sqrt(jnp.maximum(count, 1.0))
     denom = jnp.maximum(magnitude, floor_val)
-    u_re = e_re / denom * (1.0 / (LA * LR))
-    u_im = e_im / denom * (1.0 / (LA * LR))
-    out_ref[0, 0] = looks_ref[0] * u_re + looks_ref[1] * u_im
-    out_ref[0, 1] = looks_ref[1] * u_re - looks_ref[0] * u_im
+    row = lax.broadcasted_iota(jnp.int32, unit_ref.shape, 0)
+    unit_ref[...] = jnp.where(row == 0, e_re / denom, e_im / denom) * (1.0 / (LA * LR))
+
+
+def finish_kernel(three_ref, res_ref, before_ref, looks_ref, unit_ref, out_ref, sums_ref):
+    middle_n = before_ref.shape[1]
+    edge = LAG // LA
+    u_re, u_im = unit_ref[0:1], unit_ref[1:2]
+    totals = look_sums(((3, three_ref),), res_ref, out_ref.shape[3])
+    for part, total in enumerate(totals):
+        sums_ref[part] = total + before_ref[part]
+    for at, held in (
+        (0, looks_ref[:, :edge]),
+        (edge, [look_rows(sums_ref, part, 0, middle_n) for part in range(2)]),
+        (edge + middle_n // LA, looks_ref[:, edge:]),
+    ):
+        rows = slice(at, at + held[0].shape[0])
+        out_ref[0, 0, rows] = held[0] * u_re + held[1] * u_im
+        out_ref[0, 1, rows] = held[1] * u_re - held[0] * u_im
 
 
 def call(kernel, outs, scratch, cost, *args):
@@ -284,13 +289,6 @@
         az_off, rg_off, az_frac, rg_frac,
     )
     edges_three = swap(edges_two, "date", 1)
-    middle = call(
-        cut_middle_kernel,
-        shape((2, middle_n + 16, width), bf16),
-        [],
-        (0, 0),
-        primary, edges_two,
-    )
     weight = jnp.broadcast_to(margin_mask[rows_n - LAG :].astype(f32)[:, None], (LAG, LANE))
     res = call(
         resample_kernel,
@@ -298,6 +296,13 @@
         [pltpu.VMEM((2, rows_n, cols_n), bf16)],
         (0, 0),
         secondary, low, high, az_band, rg_band,
+    )
+    middle = call(
+        cut_middle_kernel,
+        shape((2, middle_n + 16, width), bf16),
+        [],
+        (0, 0),
+        primary, edges_two,res,
     )
     two, one = [swap(middle, "date", step) for step in (2, 1)]
     margin = shape((2, LAG, cols_n), bf16)
@@ -323,28 +328,25 @@
         (2 * 2 * middle_n * cols_n * looks_n, 8 * rows_n * cols_n),
         primary, one, two, res,
     )
-    other = swap(stats, "tile", 1)
-    block = shape((2, middle_n, width), bf16)
-    relayed = call(relay_kernel, block, [], (0, 0), two, other,one)
-    three = swap(relayed, "date", 1)
+    awaited = other = swap(stats, "tile", 1)
     stride = 2
     while stride < tiles_n:
+        if stride == HOP_ROUND:
+            awaited = other
         stats = stats + other
         other = swap(stats, "tile", stride)
         stride *= 2
-    looks = call(
-        last_kernel,
-        shape((2, rows_n // LA, looks_n), f32),
+    relayed = call(
+        relay_kernel, shape((2, middle_n, width), bf16), [], (0, 0), two, awaited, one
+    )
+    three = swap(relayed, "date", 1)
+    unit = call(unit_kernel, shape((8, LANE), f32), [], (0, 0), stats, other)
+    return call(
+        finish_kernel,
+        shape((1, 2, rows_n // LA, looks_n), f32),
         [pltpu.VMEM((2, middle_n, looks_n), f32)],
         (2 * middle_n * cols_n * looks_n, 4 * rows_n * cols_n),
-        three, res, before, looks,
-    )
-    return call(
-        scale_kernel,
-        shape((1, 2, rows_n // LA, looks_n), f32),
-        [],
-        (8 * rows_n * looks_n, 8 * rows_n * looks_n),
-        looks, stats, other,
+        three, res, before, looks, unit,
     )
 
 

time: 38.9 us -> 41.8 us (1.075)
  waiting for transfers between devices: 9.44 us -> 12.6 us
    ppermute x9, waiting for transfers between devices: 6.3 us -> 9.46 us  [swap(): lax.ppermute(value, axis, [(at, at ^ step) for at in range(lax.axis_size(...]
  transfers between devices with their start and end apart: 12 -> 12, of which waited for: 7 -> 7; matrix products, arithmetic and copies ran while one was open for 2% -> 2% of each run, Pallas kernels for 9% -> 8%
where the time goes in v16:
time: 41.8 us; the launch traced here: 41.5 us
  starting transfers between devices  18.7 us (45%)
  waiting for transfers between devices  12.6 us (30%)
  Pallas kernels  4.39 us (11%)
  between operations  2.72 us (7%)
  local copies, waits for them, and re-layouts  2.37 us (6%)
  other arithmetic  0.77 us (2%)
    ppermute x9, starting transfers between devices, swap(): lax.ppermute(value, axis, [(at, at ^ step) for at in range(lax.axis_size(...  14.5 us
    ppermute x9, waiting for transfers between devices, swap(): lax.ppermute(value, axis, [(at, at ^ step) for at in range(lax.axis_size(...  9.46 us
    pallas_call x10, Pallas kernels, call(): pl.pallas_call(kernel, out_shape=outs, in_specs=[vmem] * len(args), out_s...  4.39 us
    ppermute x3, starting transfers between devices, ring(): lax.ppermute(value, axis, [(at, (at + step) % count) for at in range(coun...  4.19 us
    ppermute x3, waiting for transfers between devices, ring(): lax.ppermute(value, axis, [(at, (at + step) % count) for at in range(coun...  3.14 us
    unnamed x6, local copies, waits for them, and re-layouts  1.42 us
    slice x1, local copies, waits for them, and re-layouts, fused(): primary[:, :LAG]  0.88 us
  transfers between devices with their start and end apart: 12, of which 7 were waited for; matrix products, arithmetic and copies ran while one was open for 2% of the time, Pallas kernels for 8%

profile of v16, /device:TPU:0, one launch (start us, length us, event | category | flops | bytes accessed | tf_op | source)
XLA Modules:
  0.0 41.5 jit_solution(14911371907710153885)
XLA Ops:
  0.0 0.9 %fusion = (bf16[2,64,256]{2,1,0:T(8,128)(2,1)S(1)}, bf16[2,64,256]{2,1,0:T(8,128)(2,1)S(1)}) fusion(bf16[2,384,256]{2,1,0:T(8,128)(2,1)} %own_ref.3), kind=kLoop, calls=%fused_computation.2 | loop fusion | bytes 262144 | tf_op jit(solution)/shard_map/slice | solution.py:277
  0.9 4.1 %collective-permute-start = (bf16[2,128,256]{2,1,0:T(8,128)(2,1)S(1)}, bf16[2,128,256]{2,1,0:T(8,128)(2,1)S(1)}, u32[]{:S(2)}, u32[]{:S(2)}) collective-permute-start(bf16[2,128,256]{2,1,0:T(8,128)(2,1)S(1)} %pad_maximum_fusion), channel_id=1, source_target_pairs={{0,2},{1,3},{2,0},{3,1},{4,6},{5,7},{6,4},{7,5},{8,10},{9,11},{10,... | collective-permute-start | bytes 393224 | tf_op jit(solution)/shard_map/ppermute | solution.py:265
  5.0 1.4 %copy-done = bf16[1,2,384,1024]{3,2,1,0:T(8,128)(2,1)S(1)} copy-done((bf16[1,2,384,1024]{3,2,1,0:T(8,128)(2,1)S(1)}, bf16[1,2,384,1024]{3,2,1,0:T(8,128)(2,1)}, u32[]{:S(2)}) %copy-start) | copy-done | bytes 1572888
  6.4 0.1 collective-permute-start.1
  6.5 2.6 %collective-permute-start.2 = (bf16[2,32,1024]{2,1,0:T(8,128)(2,1)S(1)}, bf16[2,32,1024]{2,1,0:T(8,128)(2,1)S(1)}, u32[]{:S(2)}, u32[]{:S(2)}) collective-permute-start(bf16[2,32,1024]{2,1,0:T(8,128)(2,1)S(1)} %get-tuple-element.13), channel_id=1, source_target_pairs={{0,28},{4,0},{8,4},{12,8},{16,12},{20,16},{24,20},{28,24},{1,29},{... | collective-permute-start | bytes 393224 | tf_op jit(solution)/shard_map/ppermute | solution.py:261
  9.1 1.6 %collective-permute-start.4 = (bf16[2,128,256]{2,1,0:T(8,128)(2,1)S(1)}, bf16[2,128,256]{2,1,0:T(8,128)(2,1)S(1)}, u32[]{:S(2)}, u32[]{:S(2)}) collective-permute-start(bf16[2,128,256]{2,1,0:T(8,128)(2,1)S(1)} %pad_maximum_fusion), channel_id=1, source_target_pairs={{0,1},{1,0},{2,3},{3,2},{4,5},{5,4},{6,7},{7,6},{8,9},{9,8},{10,11... | collective-permute-start | bytes 393224 | tf_op jit(solution)/shard_map/ppermute | solution.py:265
  10.7 0.7 %collective-permute-done.refs_0_.two_ref = bf16[2,128,256]{2,1,0:T(8,128)(2,1)S(1)} collective-permute-done((bf16[2,128,256]{2,1,0:T(8,128)(2,1)S(1)}, bf16[2,128,256]{2,1,0:T(8,128)(2,1)S(1)}, u32[]{:S(2)}, u32[]{:S(2)}) %collective-permute-start) | collective-permute-done | bytes 131104 | tf_op jit(solution)/shard_map/ppermute | solution.py:265
  11.4 0.7 %collective-permute-start.5 = (bf16[2,128,256]{2,1,0:T(8,128)(2,1)S(1)}, bf16[2,128,256]{2,1,0:T(8,128)(2,1)S(1)}, u32[]{:S(2)}, u32[]{:S(2)}) collective-permute-start(bf16[2,128,256]{2,1,0:T(8,128)(2,1)S(1)} %collective-permute-done.refs_0_.two_ref), channel_id=1, source_target_pairs={{0,1},{1,0},{2,3},{3,2},{4,5},{5,4},{6,7},{7,6},{8,9},{9,8},{10,11... | collective-permute-start | bytes 393224 | tf_op jit(solution)/shard_map/ppermute | solution.py:265
  14.7 0.4 shard_map.74
  15.0 0.0 collective-permute-done.1.low_ref
  15.1 0.0 copy-start.2
  15.1 1.4 %shard_map.75.refs_1_.res_ref = bf16[4,2,384,256]{3,2,1,0:T(8,128)(2,1)S(1)} custom-call(bf16[1,2,384,1024]{3,2,1,0:T(8,128)(2,1)S(1)} %copy-done.1, bf16[2,32,1024]{2,1,0:T(8,128)(2,1)S(1)} %collective-permute-done.1.low_ref, bf16[2,32,1024]{2,1,0:T(8,128)(2,1)S(1)} %collective-permute-done.2.high_ref, bf16[128,192]{1,0:T(8,128)(2,1)S(1)} %get-tuple-element.14.az_ref, ...), custom_call_target="tpu_custom_call" | custom-call | tf_op jit(solution)/shard_map/pallas_call | solution.py:248
  16.5 3.5 %collective-permute-start.3 = (bf16[2,272,256]{2,1,0:T(8,128)(2,1)S(1)}, bf16[2,272,256]{2,1,0:T(8,128)(2,1)S(1)}, u32[]{:S(2)}, u32[]{:S(2)}) collective-permute-start(bf16[2,272,256]{2,1,0:T(8,128)(2,1)S(1)} %shard_map.76), channel_id=1, source_target_pairs={{0,2},{1,3},{2,0},{3,1},{4,6},{5,7},{6,4},{7,5},{8,10},{9,11},{10,... | collective-permute-start | bytes 835592 | tf_op jit(solution)/shard_map/ppermute | solution.py:265
  20.0 0.0 collective-permute-start.9
  20.0 0.5 %shard_map.77 = (bf16[2,64,1024]{2,1,0:T(8,128)(2,1)S(1)}, bf16[2,64,1024]{2,1,0:T(8,128)(2,1)S(1)}, f32[2,64,128]{2,1,0:T(8,128)S(1)}) custom-call(bf16[2,384,256]{2,1,0:T(8,128)(2,1)S(1)} %copy-done.2, bf16[2,128,256]{2,1,0:T(8,128)(2,1)S(1)} %collective-permute-done.4.one_ref, bf16[2,128,256]{2,1,0:T(8,128)(2,1)S(1)} %collective-permute-done.refs_0_.two_ref, ...), custom_call_target="tpu_custom_call" | custom-call | tf_op jit(solution)/shard_map/pallas_call | solution.py:248
  20.6 1.5 %collective-permute-start.6 = (bf16[2,64,1024]{2,1,0:T(8,128)(2,1)S(1)}, bf16[2,64,1024]{2,1,0:T(8,128)(2,1)S(1)}, u32[]{:S(2)}, u32[]{:S(2)}) collective-permute-start(bf16[2,64,1024]{2,1,0:T(8,128)(2,1)S(1)} %get-tuple-element.17), channel_id=1, source_target_pairs={{0,28},{4,0},{8,4},{12,8},{16,12},{20,16},{24,20},{28,24},{1,29},{... | collective-permute-start | bytes 786440 | tf_op jit(solution)/shard_map/ppermute | solution.py:261
  22.1 0.8 %slice_convert_fusion = f32[64]{0:T(128)S(1)} fusion(s32[384]{0:T(512)} %param.9), kind=kLoop, calls=%fused_computation.1 | loop fusion | flops 64 | bytes 512 | tf_op jit(solution)/shard_map/convert_element_type | solution.py:292
  22.8 3.1 %collective-permute-done.6.later_ref = bf16[2,64,1024]{2,1,0:T(8,128)(2,1)S(1)} collective-permute-done((bf16[2,64,1024]{2,1,0:T(8,128)(2,1)S(1)}, bf16[2,64,1024]{2,1,0:T(8,128)(2,1)S(1)}, u32[]{:S(2)}, u32[]{:S(2)}) %collective-permute-start.6) | collective-permute-done | bytes 262176 | tf_op jit(solution)/shard_map/ppermute | solution.py:261
  26.0 0.1 broadcast_in_dim.2.weight_ref
  26.0 0.4 shard_map.78
  26.4 0.7 %collective-permute-start.7 = (f32[8,128]{1,0:T(8,128)S(1)}, f32[8,128]{1,0:T(8,128)S(1)}, u32[]{:S(2)}, u32[]{:S(2)}) collective-permute-start(f32[8,128]{1,0:T(8,128)S(1)} %shard_map.78), channel_id=1, source_target_pairs={{0,4},{4,0},{8,12},{12,8},{16,20},{20,16},{24,28},{28,24},{1,5},{5... | collective-permute-start | bytes 12296 | tf_op jit(solution)/shard_map/ppermute | solution.py:265
  27.1 0.8 %collective-permute-done.7 = f32[8,128]{1,0:T(8,128)S(1)} collective-permute-done((f32[8,128]{1,0:T(8,128)S(1)}, f32[8,128]{1,0:T(8,128)S(1)}, u32[]{:S(2)}, u32[]{:S(2)}) %collective-permute-start.7) | collective-permute-done | bytes 4128 | tf_op jit(solution)/shard_map/ppermute | solution.py:265
  27.9 1.9 %collective-permute-start.8 = (f32[8,128]{1,0:T(8,128)S(1)}, f32[8,128]{1,0:T(8,128)S(1)}, u32[]{:S(2)}, u32[]{:S(2)}) collective-permute-start(f32[8,128]{1,0:T(8,128)S(1)} %add.6), channel_id=1, source_target_pairs={{0,8},{4,12},{8,0},{12,4},{16,24},{20,28},{24,16},{28,20},{1,9},{5... | collective-permute-start | bytes 12296 | tf_op jit(solution)/shard_map/ppermute | solution.py:265
  29.8 2.5 %collective-permute-done.3.block_ref.two_ref = bf16[2,272,256]{2,1,0:T(8,128)(2,1)S(1)} collective-permute-done((bf16[2,272,256]{2,1,0:T(8,128)(2,1)S(1)}, bf16[2,272,256]{2,1,0:T(8,128)(2,1)S(1)}, u32[]{:S(2)}, u32[]{:S(2)}) %collective-permute-start.3) | collective-permute-done | bytes 278560 | tf_op jit(solution)/shard_map/ppermute | solution.py:265
  32.3 1.5 %collective-permute-done.9.refs_1_.one_ref = bf16[2,272,256]{2,1,0:T(8,128)(2,1)S(1)} collective-permute-done((bf16[2,272,256]{2,1,0:T(8,128)(2,1)S(1)}, bf16[2,272,256]{2,1,0:T(8,128)(2,1)S(1)}, u32[]{:S(2)}, u32[]{:S(2)}) %collective-permute-start.9) | collective-permute-done | bytes 278560 | tf_op jit(solution)/shard_map/ppermute | solution.py:265
  33.9 0.5 %collective-permute-start.10 = (bf16[2,256,256]{2,1,0:T(8,128)(2,1)S(1)}, bf16[2,256,256]{2,1,0:T(8,128)(2,1)S(1)}, u32[]{:S(2)}, u32[]{:S(2)}) collective-permute-start(bf16[2,256,256]{2,1,0:T(8,128)(2,1)S(1)} %shard_map.79), channel_id=1, source_target_pairs={{0,1},{1,0},{2,3},{3,2},{4,5},{5,4},{6,7},{7,6},{8,9},{9,8},{10,11... | collective-permute-start | bytes 786440 | tf_op jit(solution)/shard_map/ppermute | solution.py:265
  34.4 1.5 %collective-permute-start.11 = (f32[8,128]{1,0:T(8,128)S(1)}, f32[8,128]{1,0:T(8,128)S(1)}, u32[]{:S(2)}, u32[]{:S(2)}) collective-permute-start(f32[8,128]{1,0:T(8,128)S(1)} %add.7.mine_ref), channel_id=1, source_target_pairs={{0,16},{4,20},{8,24},{12,28},{16,0},{20,4},{24,8},{28,12},{1,17},{... | collective-permute-start | bytes 12296 | tf_op jit(solution)/shard_map/ppermute | solution.py:265
  35.9 0.6 %shard_map.80.before_ref = f32[2,256,128]{2,1,0:T(8,128)S(1)} custom-call(bf16[2,384,256]{2,1,0:T(8,128)(2,1)S(1)} %copy-done.2, bf16[2,272,256]{2,1,0:T(8,128)(2,1)S(1)} %collective-permute-done.9.refs_1_.one_ref, bf16[2,272,256]{2,1,0:T(8,128)(2,1)S(1)} %collective-permute-done.3.block_ref.two_ref, bf16[4,2,384,256]{3,2,1,0:T(8,128)(2,1)S(1)} %shard_map.75.refs_1_.res_ref), custom_call_target="tpu_custom_call" | custom-call | flops 134217728 | bytes 3145728 | tf_op jit(solution)/shard_map/pallas_call | solution.py:248
  36.5 1.5 %collective-permute-done.11.other_ref = f32[8,128]{1,0:T(8,128)S(1)} collective-permute-done((f32[8,128]{1,0:T(8,128)S(1)}, f32[8,128]{1,0:T(8,128)S(1)}, u32[]{:S(2)}, u32[]{:S(2)}) %collective-permute-start.11) | collective-permute-done | bytes 4128 | tf_op jit(solution)/shard_map/ppermute | solution.py:265
  38.0 0.1 shard_map.81.unit_ref
  38.1 2.5 %collective-permute-done.10.three_ref = bf16[2,256,256]{2,1,0:T(8,128)(2,1)S(1)} collective-permute-done((bf16[2,256,256]{2,1,0:T(8,128)(2,1)S(1)}, bf16[2,256,256]{2,1,0:T(8,128)(2,1)S(1)}, u32[]{:S(2)}, u32[]{:S(2)}) %collective-permute-start.10) | collective-permute-done | bytes 262176 | tf_op jit(solution)/shard_map/ppermute | solution.py:265
  40.6 1.0 %shard_map.82 = f32[1,2,192,128]{3,2,1,0:T(8,128)} custom-call(bf16[2,256,256]{2,1,0:T(8,128)(2,1)S(1)} %collective-permute-done.10.three_ref, bf16[4,2,384,256]{3,2,1,0:T(8,128)(2,1)S(1)} %shard_map.75.refs_1_.res_ref, f32[2,256,128]{2,1,0:T(8,128)S(1)} %shard_map.80.before_ref, f32[2,64,128]{2,1,0:T(8,128)S(1)} %get-tuple-element.18.looks_ref, ...), custom_call_target="tpu_custom_call" | custom-call | flops 67108864 | bytes 1572864 | tf_op jit(solution)/shard_map/pallas_call | solution.py:248
  (14 shorter events, 0.1 us)
Async XLA Ops:
  0.9 10.5 %collective-permute-start = (bf16[2,128,256]{2,1,0:T(8,128)(2,1)S(1)}, bf16[2,128,256]{2,1,0:T(8,128)(2,1)S(1)}, u32[]{:S(2)}, u32[]{:S(2)}) collective-permute-start(bf16[2,128,256]{2,1,0:T(8,128)(2,1)S(1)} %pad_maximum_fusion), channel_id=1, source_target_pairs={{0,2},{1,3},{2,0},{3,1},{4,6},{5,7},{6,4},{7,5},{8,10},{9,11},{10,... | collective-permute-start | bytes 393224 | tf_op jit(solution)/shard_map/ppermute | solution.py:265
  5.0 1.4 %copy-start = (bf16[1,2,384,1024]{3,2,1,0:T(8,128)(2,1)S(1)}, bf16[1,2,384,1024]{3,2,1,0:T(8,128)(2,1)}, u32[]{:S(2)}) copy-start(bf16[1,2,384,1024]{3,2,1,0:T(8,128)(2,1)} %sec_ref.3) | copy-start | bytes 4718596
  6.4 8.6 %copy-start.1 = (bf16[1,2,384,1024]{3,2,1,0:T(8,128)(2,1)S(1)}, bf16[1,2,384,1024]{3,2,1,0:T(8,128)(2,1)}, u32[]{:S(2)}) copy-start(bf16[1,2,384,1024]{3,2,1,0:T(8,128)(2,1)} %sec_ref.3) | copy-start | bytes 4718596
  6.4 8.6 %collective-permute-start.1 = (bf16[2,32,1024]{2,1,0:T(8,128)(2,1)S(1)}, bf16[2,32,1024]{2,1,0:T(8,128)(2,1)S(1)}, u32[]{:S(2)}, u32[]{:S(2)}) collective-permute-start(bf16[2,32,1024]{2,1,0:T(8,128)(2,1)S(1)} %get-tuple-element.12), channel_id=1, source_target_pairs={{0,4},{4,8},{8,12},{12,16},{16,20},{20,24},{24,28},{28,0},{1,5},{5... | collective-permute-start | bytes 393224 | tf_op jit(solution)/shard_map/ppermute | solution.py:261
  6.5 8.5 %collective-permute-start.2 = (bf16[2,32,1024]{2,1,0:T(8,128)(2,1)S(1)}, bf16[2,32,1024]{2,1,0:T(8,128)(2,1)S(1)}, u32[]{:S(2)}, u32[]{:S(2)}) collective-permute-start(bf16[2,32,1024]{2,1,0:T(8,128)(2,1)S(1)} %get-tuple-element.13), channel_id=1, source_target_pairs={{0,28},{4,0},{8,4},{12,8},{16,12},{20,16},{24,20},{28,24},{1,29},{... | collective-permute-start | bytes 393224 | tf_op jit(solution)/shard_map/ppermute | solution.py:261
  9.1 10.9 %collective-permute-start.4 = (bf16[2,128,256]{2,1,0:T(8,128)(2,1)S(1)}, bf16[2,128,256]{2,1,0:T(8,128)(2,1)S(1)}, u32[]{:S(2)}, u32[]{:S(2)}) collective-permute-start(bf16[2,128,256]{2,1,0:T(8,128)(2,1)S(1)} %pad_maximum_fusion), channel_id=1, source_target_pairs={{0,1},{1,0},{2,3},{3,2},{4,5},{5,4},{6,7},{7,6},{8,9},{9,8},{10,11... | collective-permute-start | bytes 393224 | tf_op jit(solution)/shard_map/ppermute | solution.py:265
  11.4 8.7 %collective-permute-start.5 = (bf16[2,128,256]{2,1,0:T(8,128)(2,1)S(1)}, bf16[2,128,256]{2,1,0:T(8,128)(2,1)S(1)}, u32[]{:S(2)}, u32[]{:S(2)}) collective-permute-start(bf16[2,128,256]{2,1,0:T(8,128)(2,1)S(1)} %collective-permute-done.refs_0_.two_ref), channel_id=1, source_target_pairs={{0,1},{1,0},{2,3},{3,2},{4,5},{5,4},{6,7},{7,6},{8,9},{9,8},{10,11... | collective-permute-start | bytes 393224 | tf_op jit(solution)/shard_map/ppermute | solution.py:265
  15.1 1.4 %copy-start.2 = (bf16[2,384,256]{2,1,0:T(8,128)(2,1)S(1)}, bf16[2,384,256]{2,1,0:T(8,128)(2,1)}, u32[]{:S(2)}) copy-start(bf16[2,384,256]{2,1,0:T(8,128)(2,1)} %own_ref.3) | copy-start | bytes 1179652
  16.5 15.8 %collective-permute-start.3 = (bf16[2,272,256]{2,1,0:T(8,128)(2,1)S(1)}, bf16[2,272,256]{2,1,0:T(8,128)(2,1)S(1)}, u32[]{:S(2)}, u32[]{:S(2)}) collective-permute-start(bf16[2,272,256]{2,1,0:T(8,128)(2,1)S(1)} %shard_map.76), channel_id=1, source_target_pairs={{0,2},{1,3},{2,0},{3,1},{4,6},{5,7},{6,4},{7,5},{8,10},{9,11},{10,... | collective-permute-start | bytes 835592 | tf_op jit(solution)/shard_map/ppermute | solution.py:265
  20.0 13.8 %collective-permute-start.9 = (bf16[2,272,256]{2,1,0:T(8,128)(2,1)S(1)}, bf16[2,272,256]{2,1,0:T(8,128)(2,1)S(1)}, u32[]{:S(2)}, u32[]{:S(2)}) collective-permute-start(bf16[2,272,256]{2,1,0:T(8,128)(2,1)S(1)} %shard_map.76), channel_id=1, source_target_pairs={{0,1},{1,0},{2,3},{3,2},{4,5},{5,4},{6,7},{7,6},{8,9},{9,8},{10,11... | collective-permute-start | bytes 835592 | tf_op jit(solution)/shard_map/ppermute | solution.py:265
  20.6 5.4 %collective-permute-start.6 = (bf16[2,64,1024]{2,1,0:T(8,128)(2,1)S(1)}, bf16[2,64,1024]{2,1,0:T(8,128)(2,1)S(1)}, u32[]{:S(2)}, u32[]{:S(2)}) collective-permute-start(bf16[2,64,1024]{2,1,0:T(8,128)(2,1)S(1)} %get-tuple-element.17), channel_id=1, source_target_pairs={{0,28},{4,0},{8,4},{12,8},{16,12},{20,16},{24,20},{28,24},{1,29},{... | collective-permute-start | bytes 786440 | tf_op jit(solution)/shard_map/ppermute | solution.py:261
  26.4 1.5 %collective-permute-start.7 = (f32[8,128]{1,0:T(8,128)S(1)}, f32[8,128]{1,0:T(8,128)S(1)}, u32[]{:S(2)}, u32[]{:S(2)}) collective-permute-start(f32[8,128]{1,0:T(8,128)S(1)} %shard_map.78), channel_id=1, source_target_pairs={{0,4},{4,0},{8,12},{12,8},{16,20},{20,16},{24,28},{28,24},{1,5},{5... | collective-permute-start | bytes 12296 | tf_op jit(solution)/shard_map/ppermute | solution.py:265
  27.9 6.0 %collective-permute-start.8 = (f32[8,128]{1,0:T(8,128)S(1)}, f32[8,128]{1,0:T(8,128)S(1)}, u32[]{:S(2)}, u32[]{:S(2)}) collective-permute-start(f32[8,128]{1,0:T(8,128)S(1)} %add.6), channel_id=1, source_target_pairs={{0,8},{4,12},{8,0},{12,4},{16,24},{20,28},{24,16},{28,20},{1,9},{5... | collective-permute-start | bytes 12296 | tf_op jit(solution)/shard_map/ppermute | solution.py:265
  33.9 6.7 %collective-permute-start.10 = (bf16[2,256,256]{2,1,0:T(8,128)(2,1)S(1)}, bf16[2,256,256]{2,1,0:T(8,128)(2,1)S(1)}, u32[]{:S(2)}, u32[]{:S(2)}) collective-permute-start(bf16[2,256,256]{2,1,0:T(8,128)(2,1)S(1)} %shard_map.79), channel_id=1, source_target_pairs={{0,1},{1,0},{2,3},{3,2},{4,5},{5,4},{6,7},{7,6},{8,9},{9,8},{10,11... | collective-permute-start | bytes 786440 | tf_op jit(solution)/shard_map/ppermute | solution.py:265
  34.4 3.6 %collective-permute-start.11 = (f32[8,128]{1,0:T(8,128)S(1)}, f32[8,128]{1,0:T(8,128)S(1)}, u32[]{:S(2)}, u32[]{:S(2)}) collective-permute-start(f32[8,128]{1,0:T(8,128)S(1)} %add.7.mine_ref), channel_id=1, source_target_pairs={{0,16},{4,20},{8,24},{12,28},{16,0},{20,4},{24,8},{28,12},{1,17},{... | collective-permute-start | bytes 12296 | tf_op jit(solution)/shard_map/ppermute | solution.py:265

commit v17 on v16

--- a/solution.py
+++ b/solution.py
@@ -14,7 +14,6 @@
 LANE = 128
 BAND = 128
 HALO = 32
-HOP_ROUND = 4
 VMEM_LIMIT = 40 * 1024 * 1024
 
 
@@ -216,8 +215,12 @@
         out_ref[part] = total
 
 
-def unit_kernel(mine_ref, other_ref, unit_ref):
-    stats = jnp.sum(mine_ref[...] + other_ref[...], axis=1, keepdims=True)
+def unit_kernel(*refs):
+    *sums, unit_ref = refs
+    total = sums[0][...]
+    for other_ref in sums[1:]:
+        total = total + other_ref[...]
+    stats = jnp.sum(total, axis=1, keepdims=True)
     e_re, e_im, power, count = [stats[row : row + 1] for row in range(4)]
     magnitude = jnp.sqrt(e_re * e_re + e_im * e_im)
     floor_val = (power + 1e-06) / jnp.sqrt(jnp.maximum(count, 1.0))
@@ -288,7 +291,17 @@
         (0, 0),
         az_off, rg_off, az_frac, rg_frac,
     )
-    edges_three = swap(edges_two, "date", 1)
+    passed = call(
+        relay_kernel, shape(edges.shape, bf16), [], (0, 0), edges_two, edges_one
+    )
+    edges_three = swap(passed, "date", 1)
+    middle = call(
+        cut_middle_kernel,
+        shape((2, middle_n + 16, width), bf16),
+        [],
+        (0, 0),
+        primary, edges_two,
+    )
     weight = jnp.broadcast_to(margin_mask[rows_n - LAG :].astype(f32)[:, None], (LAG, LANE))
     res = call(
         resample_kernel,
@@ -296,13 +309,6 @@
         [pltpu.VMEM((2, rows_n, cols_n), bf16)],
         (0, 0),
         secondary, low, high, az_band, rg_band,
-    )
-    middle = call(
-        cut_middle_kernel,
-        shape((2, middle_n + 16, width), bf16),
-        [],
-        (0, 0),
-        primary, edges_two,res,
     )
     two, one = [swap(middle, "date", step) for step in (2, 1)]
     margin = shape((2, LAG, cols_n), bf16)
@@ -328,19 +334,13 @@
         (2 * 2 * middle_n * cols_n * looks_n, 8 * rows_n * cols_n),
         primary, one, two, res,
     )
-    awaited = other = swap(stats, "tile", 1)
-    stride = 2
-    while stride < tiles_n:
-        if stride == HOP_ROUND:
-            awaited = other
-        stats = stats + other
-        other = swap(stats, "tile", stride)
-        stride *= 2
-    relayed = call(
-        relay_kernel, shape((2, middle_n, width), bf16), [], (0, 0), two, awaited, one
-    )
+    other = swap(stats, "tile", 1)
+    block = shape((2, middle_n, width), bf16)
+    relayed = call(relay_kernel, block, [], (0, 0), two, other,one)
     three = swap(relayed, "date", 1)
-    unit = call(unit_kernel, shape((8, LANE), f32), [], (0, 0), stats, other)
+    stats = stats + other
+    others = [swap(stats, "tile", step) for step in range(2, tiles_n, 2)]
+    unit = call(unit_kernel, shape((8, LANE), f32), [], (0, 0), stats, *others)
     return call(
         finish_kernel,
         shape((1, 2, rows_n // LA, looks_n), f32),

time: 41.8 us -> 39.1 us (0.935)
  waiting for transfers between devices: 12.6 us -> 9.02 us
  starting transfers between devices: 18.7 us -> 19.5 us
    ppermute x9 -> x10, waiting for transfers between devices: 9.46 us -> 5.88 us  [swap(): lax.ppermute(value, axis, [(at, at ^ step) for at in range(lax.axis_size(...]
    ppermute x9 -> x10, starting transfers between devices: 14.5 us -> 15.3 us  [swap(): lax.ppermute(value, axis, [(at, at ^ step) for at in range(lax.axis_size(...]
    pallas_call x10 -> x11, Pallas kernels: 4.39 us -> 4.4 us  [call(): pl.pallas_call(kernel, out_shape=outs, in_specs=[vmem] * len(args), out_s...]
  transfers between devices with their start and end apart: 12 -> 13, of which waited for: 7 -> 7; matrix products, arithmetic and copies ran while one was open for 2% -> 2% of each run, Pallas kernels for 8% -> 9%
where the time goes in v17:
time: 39.1 us; the launch traced here: 38.9 us
  starting transfers between devices  19.5 us (50%)
  waiting for transfers between devices  9.02 us (23%)
  Pallas kernels  4.4 us (11%)
  between operations  2.73 us (7%)
  local copies, waits for them, and re-layouts  2.42 us (6%)
  other arithmetic  0.77 us (2%)
    ppermute x10, starting transfers between devices, swap(): lax.ppermute(value, axis, [(at, at ^ step) for at in range(lax.axis_size(...  15.3 us
    ppermute x10, waiting for transfers between devices, swap(): lax.ppermute(value, axis, [(at, at ^ step) for at in range(lax.axis_size(...  5.88 us
    pallas_call x11, Pallas kernels, call(): pl.pallas_call(kernel, out_shape=outs, in_specs=[vmem] * len(args), out_s...  4.4 us
    ppermute x3, starting transfers between devices, ring(): lax.ppermute(value, axis, [(at, (at + step) % count) for at in range(coun...  4.25 us
    ppermute x3, waiting for transfers between devices, ring(): lax.ppermute(value, axis, [(at, (at + step) % count) for at in range(coun...  3.14 us
    unnamed x6, local copies, waits for them, and re-layouts  1.41 us
    slice x1, local copies, waits for them, and re-layouts, fused(): primary[:, :LAG]  0.93 us
  transfers between devices with their start and end apart: 13, of which 7 were waited for; matrix products, arithmetic and copies ran while one was open for 2% of the time, Pallas kernels for 9%

profile of v17, /device:TPU:0, one launch (start us, length us, event | category | flops | bytes accessed | tf_op | source)
XLA Modules:
  0.0 38.9 jit_solution(5582486193518060239)
XLA Ops:
  0.0 0.9 %fusion = (bf16[2,64,256]{2,1,0:T(8,128)(2,1)S(1)}, bf16[2,64,256]{2,1,0:T(8,128)(2,1)S(1)}) fusion(bf16[2,384,256]{2,1,0:T(8,128)(2,1)} %own_ref.3), kind=kLoop, calls=%fused_computation.2 | loop fusion | bytes 262144 | tf_op jit(solution)/shard_map/slice | solution.py:280
  1.0 4.1 %collective-permute-start = (bf16[2,128,256]{2,1,0:T(8,128)(2,1)S(1)}, bf16[2,128,256]{2,1,0:T(8,128)(2,1)S(1)}, u32[]{:S(2)}, u32[]{:S(2)}) collective-permute-start(bf16[2,128,256]{2,1,0:T(8,128)(2,1)S(1)} %pad_maximum_fusion), channel_id=1, source_target_pairs={{0,2},{1,3},{2,0},{3,1},{4,6},{5,7},{6,4},{7,5},{8,10},{9,11},{10,... | collective-permute-start | bytes 393224 | tf_op jit(solution)/shard_map/ppermute | solution.py:268
  5.1 1.6 %collective-permute-start.2 = (bf16[2,128,256]{2,1,0:T(8,128)(2,1)S(1)}, bf16[2,128,256]{2,1,0:T(8,128)(2,1)S(1)}, u32[]{:S(2)}, u32[]{:S(2)}) collective-permute-start(bf16[2,128,256]{2,1,0:T(8,128)(2,1)S(1)} %pad_maximum_fusion), channel_id=1, source_target_pairs={{0,1},{1,0},{2,3},{3,2},{4,5},{5,4},{6,7},{7,6},{8,9},{9,8},{10,11... | collective-permute-start | bytes 393224 | tf_op jit(solution)/shard_map/ppermute | solution.py:268
  6.6 1.4 %copy-done = bf16[1,2,384,1024]{3,2,1,0:T(8,128)(2,1)S(1)} copy-done((bf16[1,2,384,1024]{3,2,1,0:T(8,128)(2,1)S(1)}, bf16[1,2,384,1024]{3,2,1,0:T(8,128)(2,1)}, u32[]{:S(2)}) %copy-start) | copy-done | bytes 1572888
  8.1 0.1 collective-permute-start.4
  8.1 2.6 %collective-permute-start.5 = (bf16[2,32,1024]{2,1,0:T(8,128)(2,1)S(1)}, bf16[2,32,1024]{2,1,0:T(8,128)(2,1)S(1)}, u32[]{:S(2)}, u32[]{:S(2)}) collective-permute-start(bf16[2,32,1024]{2,1,0:T(8,128)(2,1)S(1)} %get-tuple-element.13), channel_id=1, source_target_pairs={{0,28},{4,0},{8,4},{12,8},{16,12},{20,16},{24,20},{28,24},{1,29},{... | collective-permute-start | bytes 393224 | tf_op jit(solution)/shard_map/ppermute | solution.py:264
  10.8 0.7 %collective-permute-done.refs_0_.block_ref.two_ref = bf16[2,128,256]{2,1,0:T(8,128)(2,1)S(1)} collective-permute-done((bf16[2,128,256]{2,1,0:T(8,128)(2,1)S(1)}, bf16[2,128,256]{2,1,0:T(8,128)(2,1)S(1)}, u32[]{:S(2)}, u32[]{:S(2)}) %collective-permute-start) | collective-permute-done | bytes 131104 | tf_op jit(solution)/shard_map/ppermute | solution.py:268
  11.5 0.2 collective-permute-done.2.refs_0_.one_ref
  11.7 1.5 %collective-permute-start.3 = (bf16[2,128,256]{2,1,0:T(8,128)(2,1)S(1)}, bf16[2,128,256]{2,1,0:T(8,128)(2,1)S(1)}, u32[]{:S(2)}, u32[]{:S(2)}) collective-permute-start(bf16[2,128,256]{2,1,0:T(8,128)(2,1)S(1)} %shard_map.74), channel_id=1, source_target_pairs={{0,1},{1,0},{2,3},{3,2},{4,5},{5,4},{6,7},{7,6},{8,9},{9,8},{10,11... | collective-permute-start | bytes 393224 | tf_op jit(solution)/shard_map/ppermute | solution.py:268
  13.2 2.4 %collective-permute-start.1 = (bf16[2,272,256]{2,1,0:T(8,128)(2,1)S(1)}, bf16[2,272,256]{2,1,0:T(8,128)(2,1)S(1)}, u32[]{:S(2)}, u32[]{:S(2)}) collective-permute-start(bf16[2,272,256]{2,1,0:T(8,128)(2,1)S(1)} %shard_map.73), channel_id=1, source_target_pairs={{0,2},{1,3},{2,0},{3,1},{4,6},{5,7},{6,4},{7,5},{8,10},{9,11},{10,... | collective-permute-start | bytes 835592 | tf_op jit(solution)/shard_map/ppermute | solution.py:268
  15.6 0.0 collective-permute-start.8
  18.3 0.4 shard_map.76
  18.6 0.0 collective-permute-done.5.high_ref
  18.7 1.4 %shard_map.77.res_ref = bf16[4,2,384,256]{3,2,1,0:T(8,128)(2,1)S(1)} custom-call(bf16[1,2,384,1024]{3,2,1,0:T(8,128)(2,1)S(1)} %copy-done.1, bf16[2,32,1024]{2,1,0:T(8,128)(2,1)S(1)} %collective-permute-done.4.low_ref, bf16[2,32,1024]{2,1,0:T(8,128)(2,1)S(1)} %collective-permute-done.5.high_ref, bf16[128,192]{1,0:T(8,128)(2,1)S(1)} %get-tuple-element.14.az_ref, ...), custom_call_target="tpu_custom_call" | custom-call | tf_op jit(solution)/shard_map/pallas_call | solution.py:251
  20.1 0.5 %shard_map.78 = (bf16[2,64,1024]{2,1,0:T(8,128)(2,1)S(1)}, bf16[2,64,1024]{2,1,0:T(8,128)(2,1)S(1)}, f32[2,64,128]{2,1,0:T(8,128)S(1)}) custom-call(bf16[2,384,256]{2,1,0:T(8,128)(2,1)S(1)} %copy-done.2, bf16[2,128,256]{2,1,0:T(8,128)(2,1)S(1)} %collective-permute-done.2.refs_0_.one_ref, ...), custom_call_target="tpu_custom_call" | custom-call | tf_op jit(solution)/shard_map/pallas_call | solution.py:251
  20.6 1.6 %collective-permute-start.6 = (bf16[2,64,1024]{2,1,0:T(8,128)(2,1)S(1)}, bf16[2,64,1024]{2,1,0:T(8,128)(2,1)S(1)}, u32[]{:S(2)}, u32[]{:S(2)}) collective-permute-start(bf16[2,64,1024]{2,1,0:T(8,128)(2,1)S(1)} %get-tuple-element.17), channel_id=1, source_target_pairs={{0,28},{4,0},{8,4},{12,8},{16,12},{20,16},{24,20},{28,24},{1,29},{... | collective-permute-start | bytes 786440 | tf_op jit(solution)/shard_map/ppermute | solution.py:264
  22.2 0.8 %slice_convert_fusion = f32[64]{0:T(128)S(1)} fusion(s32[384]{0:T(512)} %param.9), kind=kLoop, calls=%fused_computation.1 | loop fusion | flops 64 | bytes 512 | tf_op jit(solution)/shard_map/convert_element_type | solution.py:305
  22.9 3.1 %collective-permute-done.6.later_ref = bf16[2,64,1024]{2,1,0:T(8,128)(2,1)S(1)} collective-permute-done((bf16[2,64,1024]{2,1,0:T(8,128)(2,1)S(1)}, bf16[2,64,1024]{2,1,0:T(8,128)(2,1)S(1)}, u32[]{:S(2)}, u32[]{:S(2)}) %collective-permute-start.6) | collective-permute-done | bytes 262176 | tf_op jit(solution)/shard_map/ppermute | solution.py:264
  26.1 0.1 broadcast_in_dim.2.weight_ref
  26.1 0.4 shard_map.79
  26.5 0.6 %collective-permute-start.7 = (f32[8,128]{1,0:T(8,128)S(1)}, f32[8,128]{1,0:T(8,128)S(1)}, u32[]{:S(2)}, u32[]{:S(2)}) collective-permute-start(f32[8,128]{1,0:T(8,128)S(1)} %shard_map.79), channel_id=1, source_target_pairs={{0,4},{4,0},{8,12},{12,8},{16,20},{20,16},{24,28},{28,24},{1,5},{5... | collective-permute-start | bytes 12296 | tf_op jit(solution)/shard_map/ppermute | solution.py:268
  27.1 1.2 %collective-permute-done.1.block_ref.two_ref = bf16[2,272,256]{2,1,0:T(8,128)(2,1)S(1)} collective-permute-done((bf16[2,272,256]{2,1,0:T(8,128)(2,1)S(1)}, bf16[2,272,256]{2,1,0:T(8,128)(2,1)S(1)}, u32[]{:S(2)}, u32[]{:S(2)}) %collective-permute-start.1) | collective-permute-done | bytes 278560 | tf_op jit(solution)/shard_map/ppermute | solution.py:268
  28.3 0.3 collective-permute-done.8.refs_1_.one_ref
  28.7 1.6 %collective-permute-start.9 = (bf16[2,256,256]{2,1,0:T(8,128)(2,1)S(1)}, bf16[2,256,256]{2,1,0:T(8,128)(2,1)S(1)}, u32[]{:S(2)}, u32[]{:S(2)}) collective-permute-start(bf16[2,256,256]{2,1,0:T(8,128)(2,1)S(1)} %shard_map.80), channel_id=1, source_target_pairs={{0,1},{1,0},{2,3},{3,2},{4,5},{5,4},{6,7},{7,6},{8,9},{9,8},{10,11... | collective-permute-start | bytes 786440 | tf_op jit(solution)/shard_map/ppermute | solution.py:268
  30.2 1.5 %collective-permute-start.10 = (f32[8,128]{1,0:T(8,128)S(1)}, f32[8,128]{1,0:T(8,128)S(1)}, u32[]{:S(2)}, u32[]{:S(2)}) collective-permute-start(f32[8,128]{1,0:T(8,128)S(1)} %add.3.refs_0_), channel_id=1, source_target_pairs={{0,8},{4,12},{8,0},{12,4},{16,24},{20,28},{24,16},{28,20},{1,9},{5... | collective-permute-start | bytes 12296 | tf_op jit(solution)/shard_map/ppermute | solution.py:268
  31.7 1.5 %collective-permute-start.11 = (f32[8,128]{1,0:T(8,128)S(1)}, f32[8,128]{1,0:T(8,128)S(1)}, u32[]{:S(2)}, u32[]{:S(2)}) collective-permute-start(f32[8,128]{1,0:T(8,128)S(1)} %add.3.refs_0_), channel_id=1, source_target_pairs={{0,16},{4,20},{8,24},{12,28},{16,0},{20,4},{24,8},{28,12},{1,17},{... | collective-permute-start | bytes 12296 | tf_op jit(solution)/shard_map/ppermute | solution.py:268
  33.2 0.5 %collective-permute-start.12 = (f32[8,128]{1,0:T(8,128)S(1)}, f32[8,128]{1,0:T(8,128)S(1)}, u32[]{:S(2)}, u32[]{:S(2)}) collective-permute-start(f32[8,128]{1,0:T(8,128)S(1)} %add.3.refs_0_), channel_id=1, source_target_pairs={{0,24},{4,28},{8,16},{12,20},{16,8},{20,12},{24,0},{28,4},{1,25},{... | collective-permute-start | bytes 12296 | tf_op jit(solution)/shard_map/ppermute | solution.py:268
  33.7 0.6 %shard_map.81.before_ref = f32[2,256,128]{2,1,0:T(8,128)S(1)} custom-call(bf16[2,384,256]{2,1,0:T(8,128)(2,1)S(1)} %copy-done.2, bf16[2,272,256]{2,1,0:T(8,128)(2,1)S(1)} %collective-permute-done.8.refs_1_.one_ref, bf16[2,272,256]{2,1,0:T(8,128)(2,1)S(1)} %collective-permute-done.1.block_ref.two_ref, bf16[4,2,384,256]{3,2,1,0:T(8,128)(2,1)S(1)} %shard_map.77.res_ref), custom_call_target="tpu_custom_call" | custom-call | flops 134217728 | bytes 3145728 | tf_op jit(solution)/shard_map/pallas_call | solution.py:251
  34.3 1.0 %collective-permute-done.11.refs_2_ = f32[8,128]{1,0:T(8,128)S(1)} collective-permute-done((f32[8,128]{1,0:T(8,128)S(1)}, f32[8,128]{1,0:T(8,128)S(1)}, u32[]{:S(2)}, u32[]{:S(2)}) %collective-permute-start.11) | collective-permute-done | bytes 4128 | tf_op jit(solution)/shard_map/ppermute | solution.py:268
  35.3 2.4 %collective-permute-done.12.refs_3_ = f32[8,128]{1,0:T(8,128)S(1)} collective-permute-done((f32[8,128]{1,0:T(8,128)S(1)}, f32[8,128]{1,0:T(8,128)S(1)}, u32[]{:S(2)}, u32[]{:S(2)}) %collective-permute-start.12) | collective-permute-done | bytes 4128 | tf_op jit(solution)/shard_map/ppermute | solution.py:268
  37.8 0.1 shard_map.82.unit_ref
  37.9 1.0 %shard_map.83 = f32[1,2,192,128]{3,2,1,0:T(8,128)} custom-call(bf16[2,256,256]{2,1,0:T(8,128)(2,1)S(1)} %collective-permute-done.9.three_ref, bf16[4,2,384,256]{3,2,1,0:T(8,128)(2,1)S(1)} %shard_map.77.res_ref, f32[2,256,128]{2,1,0:T(8,128)S(1)} %shard_map.81.before_ref, f32[2,64,128]{2,1,0:T(8,128)S(1)} %get-tuple-element.18.looks_ref, ...), custom_call_target="tpu_custom_call" | custom-call | flops 67108864 | bytes 1572864 | tf_op jit(solution)/shard_map/pallas_call | solution.py:251
  (16 shorter events, 0.1 us)
Async XLA Ops:
  0.0 13.2 %copy-start.2 = (bf16[2,384,256]{2,1,0:T(8,128)(2,1)S(1)}, bf16[2,384,256]{2,1,0:T(8,128)(2,1)}, u32[]{:S(2)}) copy-start(bf16[2,384,256]{2,1,0:T(8,128)(2,1)} %own_ref.3) | copy-start | bytes 1179652
  1.0 10.5 %collective-permute-start = (bf16[2,128,256]{2,1,0:T(8,128)(2,1)S(1)}, bf16[2,128,256]{2,1,0:T(8,128)(2,1)S(1)}, u32[]{:S(2)}, u32[]{:S(2)}) collective-permute-start(bf16[2,128,256]{2,1,0:T(8,128)(2,1)S(1)} %pad_maximum_fusion), channel_id=1, source_target_pairs={{0,2},{1,3},{2,0},{3,1},{4,6},{5,7},{6,4},{7,5},{8,10},{9,11},{10,... | collective-permute-start | bytes 393224 | tf_op jit(solution)/shard_map/ppermute | solution.py:268
  5.1 6.6 %collective-permute-start.2 = (bf16[2,128,256]{2,1,0:T(8,128)(2,1)S(1)}, bf16[2,128,256]{2,1,0:T(8,128)(2,1)S(1)}, u32[]{:S(2)}, u32[]{:S(2)}) collective-permute-start(bf16[2,128,256]{2,1,0:T(8,128)(2,1)S(1)} %pad_maximum_fusion), channel_id=1, source_target_pairs={{0,1},{1,0},{2,3},{3,2},{4,5},{5,4},{6,7},{7,6},{8,9},{9,8},{10,11... | collective-permute-start | bytes 393224 | tf_op jit(solution)/shard_map/ppermute | solution.py:268
  6.6 1.4 %copy-start = (bf16[1,2,384,1024]{3,2,1,0:T(8,128)(2,1)S(1)}, bf16[1,2,384,1024]{3,2,1,0:T(8,128)(2,1)}, u32[]{:S(2)}) copy-start(bf16[1,2,384,1024]{3,2,1,0:T(8,128)(2,1)} %sec_ref.3) | copy-start | bytes 4718596
  8.0 10.6 %copy-start.1 = (bf16[1,2,384,1024]{3,2,1,0:T(8,128)(2,1)S(1)}, bf16[1,2,384,1024]{3,2,1,0:T(8,128)(2,1)}, u32[]{:S(2)}) copy-start(bf16[1,2,384,1024]{3,2,1,0:T(8,128)(2,1)} %sec_ref.3) | copy-start | bytes 4718596
  8.1 10.6 %collective-permute-start.4 = (bf16[2,32,1024]{2,1,0:T(8,128)(2,1)S(1)}, bf16[2,32,1024]{2,1,0:T(8,128)(2,1)S(1)}, u32[]{:S(2)}, u32[]{:S(2)}) collective-permute-start(bf16[2,32,1024]{2,1,0:T(8,128)(2,1)S(1)} %get-tuple-element.12), channel_id=1, source_target_pairs={{0,4},{4,8},{8,12},{12,16},{16,20},{20,24},{24,28},{28,0},{1,5},{5... | collective-permute-start | bytes 393224 | tf_op jit(solution)/shard_map/ppermute | solution.py:264
  8.1 10.5 %collective-permute-start.5 = (bf16[2,32,1024]{2,1,0:T(8,128)(2,1)S(1)}, bf16[2,32,1024]{2,1,0:T(8,128)(2,1)S(1)}, u32[]{:S(2)}, u32[]{:S(2)}) collective-permute-start(bf16[2,32,1024]{2,1,0:T(8,128)(2,1)S(1)} %get-tuple-element.13), channel_id=1, source_target_pairs={{0,28},{4,0},{8,4},{12,8},{16,12},{20,16},{24,20},{28,24},{1,29},{... | collective-permute-start | bytes 393224 | tf_op jit(solution)/shard_map/ppermute | solution.py:264
  11.7 8.4 %collective-permute-start.3 = (bf16[2,128,256]{2,1,0:T(8,128)(2,1)S(1)}, bf16[2,128,256]{2,1,0:T(8,128)(2,1)S(1)}, u32[]{:S(2)}, u32[]{:S(2)}) collective-permute-start(bf16[2,128,256]{2,1,0:T(8,128)(2,1)S(1)} %shard_map.74), channel_id=1, source_target_pairs={{0,1},{1,0},{2,3},{3,2},{4,5},{5,4},{6,7},{7,6},{8,9},{9,8},{10,11... | collective-permute-start | bytes 393224 | tf_op jit(solution)/shard_map/ppermute | solution.py:268
  13.2 15.1 %collective-permute-start.1 = (bf16[2,272,256]{2,1,0:T(8,128)(2,1)S(1)}, bf16[2,272,256]{2,1,0:T(8,128)(2,1)S(1)}, u32[]{:S(2)}, u32[]{:S(2)}) collective-permute-start(bf16[2,272,256]{2,1,0:T(8,128)(2,1)S(1)} %shard_map.73), channel_id=1, source_target_pairs={{0,2},{1,3},{2,0},{3,1},{4,6},{5,7},{6,4},{7,5},{8,10},{9,11},{10,... | collective-permute-start | bytes 835592 | tf_op jit(solution)/shard_map/ppermute | solution.py:268
  15.6 13.0 %collective-permute-start.8 = (bf16[2,272,256]{2,1,0:T(8,128)(2,1)S(1)}, bf16[2,272,256]{2,1,0:T(8,128)(2,1)S(1)}, u32[]{:S(2)}, u32[]{:S(2)}) collective-permute-start(bf16[2,272,256]{2,1,0:T(8,128)(2,1)S(1)} %shard_map.73), channel_id=1, source_target_pairs={{0,1},{1,0},{2,3},{3,2},{4,5},{5,4},{6,7},{7,6},{8,9},{9,8},{10,11... | collective-permute-start | bytes 835592 | tf_op jit(solution)/shard_map/ppermute | solution.py:268
  20.6 5.5 %collective-permute-start.6 = (bf16[2,64,1024]{2,1,0:T(8,128)(2,1)S(1)}, bf16[2,64,1024]{2,1,0:T(8,128)(2,1)S(1)}, u32[]{:S(2)}, u32[]{:S(2)}) collective-permute-start(bf16[2,64,1024]{2,1,0:T(8,128)(2,1)S(1)} %get-tuple-element.17), channel_id=1, source_target_pairs={{0,28},{4,0},{8,4},{12,8},{16,12},{20,16},{24,20},{28,24},{1,29},{... | collective-permute-start | bytes 786440 | tf_op jit(solution)/shard_map/ppermute | solution.py:264
  26.5 2.2 %collective-permute-start.7 = (f32[8,128]{1,0:T(8,128)S(1)}, f32[8,128]{1,0:T(8,128)S(1)}, u32[]{:S(2)}, u32[]{:S(2)}) collective-permute-start(f32[8,128]{1,0:T(8,128)S(1)} %shard_map.79), channel_id=1, source_target_pairs={{0,4},{4,0},{8,12},{12,8},{16,20},{20,16},{24,28},{28,24},{1,5},{5... | collective-permute-start | bytes 12296 | tf_op jit(solution)/shard_map/ppermute | solution.py:268
  28.7 9.2 %collective-permute-start.9 = (bf16[2,256,256]{2,1,0:T(8,128)(2,1)S(1)}, bf16[2,256,256]{2,1,0:T(8,128)(2,1)S(1)}, u32[]{:S(2)}, u32[]{:S(2)}) collective-permute-start(bf16[2,256,256]{2,1,0:T(8,128)(2,1)S(1)} %shard_map.80), channel_id=1, source_target_pairs={{0,1},{1,0},{2,3},{3,2},{4,5},{5,4},{6,7},{7,6},{8,9},{9,8},{10,11... | collective-permute-start | bytes 786440 | tf_op jit(solution)/shard_map/ppermute | solution.py:268
  30.2 4.1 %collective-permute-start.10 = (f32[8,128]{1,0:T(8,128)S(1)}, f32[8,128]{1,0:T(8,128)S(1)}, u32[]{:S(2)}, u32[]{:S(2)}) collective-permute-start(f32[8,128]{1,0:T(8,128)S(1)} %add.3.refs_0_), channel_id=1, source_target_pairs={{0,8},{4,12},{8,0},{12,4},{16,24},{20,28},{24,16},{28,20},{1,9},{5... | collective-permute-start | bytes 12296 | tf_op jit(solution)/shard_map/ppermute | solution.py:268
  31.7 3.6 %collective-permute-start.11 = (f32[8,128]{1,0:T(8,128)S(1)}, f32[8,128]{1,0:T(8,128)S(1)}, u32[]{:S(2)}, u32[]{:S(2)}) collective-permute-start(f32[8,128]{1,0:T(8,128)S(1)} %add.3.refs_0_), channel_id=1, source_target_pairs={{0,16},{4,20},{8,24},{12,28},{16,0},{20,4},{24,8},{28,12},{1,17},{... | collective-permute-start | bytes 12296 | tf_op jit(solution)/shard_map/ppermute | solution.py:268
  33.2 4.5 %collective-permute-start.12 = (f32[8,128]{1,0:T(8,128)S(1)}, f32[8,128]{1,0:T(8,128)S(1)}, u32[]{:S(2)}, u32[]{:S(2)}) collective-permute-start(f32[8,128]{1,0:T(8,128)S(1)} %add.3.refs_0_), channel_id=1, source_target_pairs={{0,24},{4,28},{8,16},{12,20},{16,8},{20,12},{24,0},{28,4},{1,25},{... | collective-permute-start | bytes 12296 | tf_op jit(solution)/shard_map/ppermute | solution.py:268

commit v18 on v17

--- a/solution.py
+++ b/solution.py
@@ -215,12 +215,8 @@
         out_ref[part] = total
 
 
-def unit_kernel(*refs):
-    *sums, unit_ref = refs
-    total = sums[0][...]
-    for other_ref in sums[1:]:
-        total = total + other_ref[...]
-    stats = jnp.sum(total, axis=1, keepdims=True)
+def unit_kernel(mine_ref, other_ref, unit_ref):
+    stats = jnp.sum(mine_ref[...] + other_ref[...], axis=1, keepdims=True)
     e_re, e_im, power, count = [stats[row : row + 1] for row in range(4)]
     magnitude = jnp.sqrt(e_re * e_re + e_im * e_im)
     floor_val = (power + 1e-06) / jnp.sqrt(jnp.maximum(count, 1.0))
@@ -338,9 +334,12 @@
     block = shape((2, middle_n, width), bf16)
     relayed = call(relay_kernel, block, [], (0, 0), two, other,one)
     three = swap(relayed, "date", 1)
-    stats = stats + other
-    others = [swap(stats, "tile", step) for step in range(2, tiles_n, 2)]
-    unit = call(unit_kernel, shape((8, LANE), f32), [], (0, 0), stats, *others)
+    stride = 2
+    while stride < tiles_n:
+        stats = stats + other
+        other = swap(stats, "tile", stride)
+        stride *= 2
+    unit = call(unit_kernel, shape((8, LANE), f32), [], (0, 0), stats, other)
     return call(
         finish_kernel,
         shape((1, 2, rows_n // LA, looks_n), f32),

time: 39.1 us -> 38.8 us (level)
  starting transfers between devices: 19.5 us -> 19.1 us
    ppermute x10 -> x9, starting transfers between devices: 15.3 us -> 14.8 us  [swap(): lax.ppermute(value, axis, [(at, at ^ step) for at in range(lax.axis_size(...]
    ppermute x10 -> x9, waiting for transfers between devices: 5.88 us -> 6.06 us  [swap(): lax.ppermute(value, axis, [(at, at ^ step) for at in range(lax.axis_size(...]
  transfers between devices with their start and end apart: 13 -> 12, of which waited for: 7 -> 7; matrix products, arithmetic and copies ran while one was open for 2% -> 2% of each run, Pallas kernels for 9% -> 9%
where the time goes in v18:
time: 38.8 us; the launch traced here: 38.6 us
  starting transfers between devices  19.1 us (49%)
  waiting for transfers between devices  9.2 us (24%)
  Pallas kernels  4.4 us (11%)
  between operations  2.72 us (7%)
  local copies, waits for them, and re-layouts  2.42 us (6%)
  other arithmetic  0.77 us (2%)
    ppermute x9, starting transfers between devices, swap(): lax.ppermute(value, axis, [(at, at ^ step) for at in range(lax.axis_size(...  14.8 us
    ppermute x9, waiting for transfers between devices, swap(): lax.ppermute(value, axis, [(at, at ^ step) for at in range(lax.axis_size(...  6.06 us
    pallas_call x11, Pallas kernels, call(): pl.pallas_call(kernel, out_shape=outs, in_specs=[vmem] * len(args), out_s...  4.4 us
    ppermute x3, starting transfers between devices, ring(): lax.ppermute(value, axis, [(at, (at + step) % count) for at in range(coun...  4.25 us
    ppermute x3, waiting for transfers between devices, ring(): lax.ppermute(value, axis, [(at, (at + step) % count) for at in range(coun...  3.14 us
    unnamed x6, local copies, waits for them, and re-layouts  1.41 us
    slice x1, local copies, waits for them, and re-layouts, fused(): primary[:, :LAG]  0.93 us
  transfers between devices with their start and end apart: 12, of which 7 were waited for; matrix products, arithmetic and copies ran while one was open for 2% of the time, Pallas kernels for 9%

profile of v18, /device:TPU:0, one launch (start us, length us, event | category | flops | bytes accessed | tf_op | source)
XLA Modules:
  0.0 38.6 jit_solution(5078980604300613053)
XLA Ops:
  0.0 0.9 %fusion = (bf16[2,64,256]{2,1,0:T(8,128)(2,1)S(1)}, bf16[2,64,256]{2,1,0:T(8,128)(2,1)S(1)}) fusion(bf16[2,384,256]{2,1,0:T(8,128)(2,1)} %own_ref.3), kind=kLoop, calls=%fused_computation.2 | loop fusion | bytes 262144 | tf_op jit(solution)/shard_map/slice | solution.py:276
  1.0 4.1 %collective-permute-start = (bf16[2,128,256]{2,1,0:T(8,128)(2,1)S(1)}, bf16[2,128,256]{2,1,0:T(8,128)(2,1)S(1)}, u32[]{:S(2)}, u32[]{:S(2)}) collective-permute-start(bf16[2,128,256]{2,1,0:T(8,128)(2,1)S(1)} %pad_maximum_fusion), channel_id=1, source_target_pairs={{0,2},{1,3},{2,0},{3,1},{4,6},{5,7},{6,4},{7,5},{8,10},{9,11},{10,... | collective-permute-start | bytes 393224 | tf_op jit(solution)/shard_map/ppermute | solution.py:264
  5.1 1.6 %collective-permute-start.2 = (bf16[2,128,256]{2,1,0:T(8,128)(2,1)S(1)}, bf16[2,128,256]{2,1,0:T(8,128)(2,1)S(1)}, u32[]{:S(2)}, u32[]{:S(2)}) collective-permute-start(bf16[2,128,256]{2,1,0:T(8,128)(2,1)S(1)} %pad_maximum_fusion), channel_id=1, source_target_pairs={{0,1},{1,0},{2,3},{3,2},{4,5},{5,4},{6,7},{7,6},{8,9},{9,8},{10,11... | collective-permute-start | bytes 393224 | tf_op jit(solution)/shard_map/ppermute | solution.py:264
  6.6 1.4 %copy-done = bf16[1,2,384,1024]{3,2,1,0:T(8,128)(2,1)S(1)} copy-done((bf16[1,2,384,1024]{3,2,1,0:T(8,128)(2,1)S(1)}, bf16[1,2,384,1024]{3,2,1,0:T(8,128)(2,1)}, u32[]{:S(2)}) %copy-start) | copy-done | bytes 1572888
  8.1 0.1 collective-permute-start.4
  8.1 2.6 %collective-permute-start.5 = (bf16[2,32,1024]{2,1,0:T(8,128)(2,1)S(1)}, bf16[2,32,1024]{2,1,0:T(8,128)(2,1)S(1)}, u32[]{:S(2)}, u32[]{:S(2)}) collective-permute-start(bf16[2,32,1024]{2,1,0:T(8,128)(2,1)S(1)} %get-tuple-element.13), channel_id=1, source_target_pairs={{0,28},{4,0},{8,4},{12,8},{16,12},{20,16},{24,20},{28,24},{1,29},{... | collective-permute-start | bytes 393224 | tf_op jit(solution)/shard_map/ppermute | solution.py:260
  10.8 0.7 %collective-permute-done.refs_0_.block_ref.two_ref = bf16[2,128,256]{2,1,0:T(8,128)(2,1)S(1)} collective-permute-done((bf16[2,128,256]{2,1,0:T(8,128)(2,1)S(1)}, bf16[2,128,256]{2,1,0:T(8,128)(2,1)S(1)}, u32[]{:S(2)}, u32[]{:S(2)}) %collective-permute-start) | collective-permute-done | bytes 131104 | tf_op jit(solution)/shard_map/ppermute | solution.py:264
  11.5 0.2 collective-permute-done.2.refs_0_.one_ref
  11.7 1.5 %collective-permute-start.3 = (bf16[2,128,256]{2,1,0:T(8,128)(2,1)S(1)}, bf16[2,128,256]{2,1,0:T(8,128)(2,1)S(1)}, u32[]{:S(2)}, u32[]{:S(2)}) collective-permute-start(bf16[2,128,256]{2,1,0:T(8,128)(2,1)S(1)} %shard_map.74), channel_id=1, source_target_pairs={{0,1},{1,0},{2,3},{3,2},{4,5},{5,4},{6,7},{7,6},{8,9},{9,8},{10,11... | collective-permute-start | bytes 393224 | tf_op jit(solution)/shard_map/ppermute | solution.py:264
  13.2 2.4 %collective-permute-start.1 = (bf16[2,272,256]{2,1,0:T(8,128)(2,1)S(1)}, bf16[2,272,256]{2,1,0:T(8,128)(2,1)S(1)}, u32[]{:S(2)}, u32[]{:S(2)}) collective-permute-start(bf16[2,272,256]{2,1,0:T(8,128)(2,1)S(1)} %shard_map.73), channel_id=1, source_target_pairs={{0,2},{1,3},{2,0},{3,1},{4,6},{5,7},{6,4},{7,5},{8,10},{9,11},{10,... | collective-permute-start | bytes 835592 | tf_op jit(solution)/shard_map/ppermute | solution.py:264
  15.6 0.0 collective-permute-start.8
  18.3 0.4 shard_map.76
  18.6 0.0 collective-permute-done.4.low_ref
  18.7 1.4 %shard_map.77.res_ref = bf16[4,2,384,256]{3,2,1,0:T(8,128)(2,1)S(1)} custom-call(bf16[1,2,384,1024]{3,2,1,0:T(8,128)(2,1)S(1)} %copy-done.1, bf16[2,32,1024]{2,1,0:T(8,128)(2,1)S(1)} %collective-permute-done.4.low_ref, bf16[2,32,1024]{2,1,0:T(8,128)(2,1)S(1)} %collective-permute-done.5.high_ref, bf16[128,192]{1,0:T(8,128)(2,1)S(1)} %get-tuple-element.14.az_ref, ...), custom_call_target="tpu_custom_call" | custom-call | tf_op jit(solution)/shard_map/pallas_call | solution.py:247
  20.1 0.5 %shard_map.78 = (bf16[2,64,1024]{2,1,0:T(8,128)(2,1)S(1)}, bf16[2,64,1024]{2,1,0:T(8,128)(2,1)S(1)}, f32[2,64,128]{2,1,0:T(8,128)S(1)}) custom-call(bf16[2,384,256]{2,1,0:T(8,128)(2,1)S(1)} %copy-done.2, bf16[2,128,256]{2,1,0:T(8,128)(2,1)S(1)} %collective-permute-done.2.refs_0_.one_ref, ...), custom_call_target="tpu_custom_call" | custom-call | tf_op jit(solution)/shard_map/pallas_call | solution.py:247
  20.6 1.6 %collective-permute-start.6 = (bf16[2,64,1024]{2,1,0:T(8,128)(2,1)S(1)}, bf16[2,64,1024]{2,1,0:T(8,128)(2,1)S(1)}, u32[]{:S(2)}, u32[]{:S(2)}) collective-permute-start(bf16[2,64,1024]{2,1,0:T(8,128)(2,1)S(1)} %get-tuple-element.17), channel_id=1, source_target_pairs={{0,28},{4,0},{8,4},{12,8},{16,12},{20,16},{24,20},{28,24},{1,29},{... | collective-permute-start | bytes 786440 | tf_op jit(solution)/shard_map/ppermute | solution.py:260
  22.2 0.8 %slice_convert_fusion = f32[64]{0:T(128)S(1)} fusion(s32[384]{0:T(512)} %param.9), kind=kLoop, calls=%fused_computation.1 | loop fusion | flops 64 | bytes 512 | tf_op jit(solution)/shard_map/convert_element_type | solution.py:301
  22.9 3.1 %collective-permute-done.6.later_ref = bf16[2,64,1024]{2,1,0:T(8,128)(2,1)S(1)} collective-permute-done((bf16[2,64,1024]{2,1,0:T(8,128)(2,1)S(1)}, bf16[2,64,1024]{2,1,0:T(8,128)(2,1)S(1)}, u32[]{:S(2)}, u32[]{:S(2)}) %collective-permute-start.6) | collective-permute-done | bytes 262176 | tf_op jit(solution)/shard_map/ppermute | solution.py:260
  26.1 0.1 broadcast_in_dim.2.weight_ref
  26.1 0.4 shard_map.79
  26.5 0.6 %collective-permute-start.7 = (f32[8,128]{1,0:T(8,128)S(1)}, f32[8,128]{1,0:T(8,128)S(1)}, u32[]{:S(2)}, u32[]{:S(2)}) collective-permute-start(f32[8,128]{1,0:T(8,128)S(1)} %shard_map.79), channel_id=1, source_target_pairs={{0,4},{4,0},{8,12},{12,8},{16,20},{20,16},{24,28},{28,24},{1,5},{5... | collective-permute-start | bytes 12296 | tf_op jit(solution)/shard_map/ppermute | solution.py:264
  27.1 1.2 %collective-permute-done.1.block_ref.two_ref = bf16[2,272,256]{2,1,0:T(8,128)(2,1)S(1)} collective-permute-done((bf16[2,272,256]{2,1,0:T(8,128)(2,1)S(1)}, bf16[2,272,256]{2,1,0:T(8,128)(2,1)S(1)}, u32[]{:S(2)}, u32[]{:S(2)}) %collective-permute-start.1) | collective-permute-done | bytes 278560 | tf_op jit(solution)/shard_map/ppermute | solution.py:264
  28.3 0.3 collective-permute-done.8.refs_1_.one_ref
  28.7 0.0 collective-permute-done.7.refs_0_
  28.7 1.6 %collective-permute-start.9 = (bf16[2,256,256]{2,1,0:T(8,128)(2,1)S(1)}, bf16[2,256,256]{2,1,0:T(8,128)(2,1)S(1)}, u32[]{:S(2)}, u32[]{:S(2)}) collective-permute-start(bf16[2,256,256]{2,1,0:T(8,128)(2,1)S(1)} %shard_map.80), channel_id=1, source_target_pairs={{0,1},{1,0},{2,3},{3,2},{4,5},{5,4},{6,7},{7,6},{8,9},{9,8},{10,11... | collective-permute-start | bytes 786440 | tf_op jit(solution)/shard_map/ppermute | solution.py:264
  30.2 1.5 %collective-permute-start.10 = (f32[8,128]{1,0:T(8,128)S(1)}, f32[8,128]{1,0:T(8,128)S(1)}, u32[]{:S(2)}, u32[]{:S(2)}) collective-permute-start(f32[8,128]{1,0:T(8,128)S(1)} %add.6), channel_id=1, source_target_pairs={{0,8},{4,12},{8,0},{12,4},{16,24},{20,28},{24,16},{28,20},{1,9},{5... | collective-permute-start | bytes 12296 | tf_op jit(solution)/shard_map/ppermute | solution.py:264
  31.7 2.1 %collective-permute-done.10 = f32[8,128]{1,0:T(8,128)S(1)} collective-permute-done((f32[8,128]{1,0:T(8,128)S(1)}, f32[8,128]{1,0:T(8,128)S(1)}, u32[]{:S(2)}, u32[]{:S(2)}) %collective-permute-start.10) | collective-permute-done | bytes 4128 | tf_op jit(solution)/shard_map/ppermute | solution.py:264
  33.8 1.5 %collective-permute-start.11 = (f32[8,128]{1,0:T(8,128)S(1)}, f32[8,128]{1,0:T(8,128)S(1)}, u32[]{:S(2)}, u32[]{:S(2)}) collective-permute-start(f32[8,128]{1,0:T(8,128)S(1)} %add.7.mine_ref), channel_id=1, source_target_pairs={{0,16},{4,20},{8,24},{12,28},{16,0},{20,4},{24,8},{28,12},{1,17},{... | collective-permute-start | bytes 12296 | tf_op jit(solution)/shard_map/ppermute | solution.py:264
  35.4 0.6 %shard_map.81.before_ref = f32[2,256,128]{2,1,0:T(8,128)S(1)} custom-call(bf16[2,384,256]{2,1,0:T(8,128)(2,1)S(1)} %copy-done.2, bf16[2,272,256]{2,1,0:T(8,128)(2,1)S(1)} %collective-permute-done.8.refs_1_.one_ref, bf16[2,272,256]{2,1,0:T(8,128)(2,1)S(1)} %collective-permute-done.1.block_ref.two_ref, bf16[4,2,384,256]{3,2,1,0:T(8,128)(2,1)S(1)} %shard_map.77.res_ref), custom_call_target="tpu_custom_call" | custom-call | flops 134217728 | bytes 3145728 | tf_op jit(solution)/shard_map/pallas_call | solution.py:247
  36.0 1.5 %collective-permute-done.11.other_ref = f32[8,128]{1,0:T(8,128)S(1)} collective-permute-done((f32[8,128]{1,0:T(8,128)S(1)}, f32[8,128]{1,0:T(8,128)S(1)}, u32[]{:S(2)}, u32[]{:S(2)}) %collective-permute-start.11) | collective-permute-done | bytes 4128 | tf_op jit(solution)/shard_map/ppermute | solution.py:264
  37.5 0.1 shard_map.82.unit_ref
  37.6 1.0 %shard_map.83 = f32[1,2,192,128]{3,2,1,0:T(8,128)} custom-call(bf16[2,256,256]{2,1,0:T(8,128)(2,1)S(1)} %collective-permute-done.9.three_ref, bf16[4,2,384,256]{3,2,1,0:T(8,128)(2,1)S(1)} %shard_map.77.res_ref, f32[2,256,128]{2,1,0:T(8,128)S(1)} %shard_map.81.before_ref, f32[2,64,128]{2,1,0:T(8,128)S(1)} %get-tuple-element.18.looks_ref, ...), custom_call_target="tpu_custom_call" | custom-call | flops 67108864 | bytes 1572864 | tf_op jit(solution)/shard_map/pallas_call | solution.py:247
  (15 shorter events, 0.1 us)
Async XLA Ops:
  0.0 13.2 %copy-start.2 = (bf16[2,384,256]{2,1,0:T(8,128)(2,1)S(1)}, bf16[2,384,256]{2,1,0:T(8,128)(2,1)}, u32[]{:S(2)}) copy-start(bf16[2,384,256]{2,1,0:T(8,128)(2,1)} %own_ref.3) | copy-start | bytes 1179652
  1.0 10.5 %collective-permute-start = (bf16[2,128,256]{2,1,0:T(8,128)(2,1)S(1)}, bf16[2,128,256]{2,1,0:T(8,128)(2,1)S(1)}, u32[]{:S(2)}, u32[]{:S(2)}) collective-permute-start(bf16[2,128,256]{2,1,0:T(8,128)(2,1)S(1)} %pad_maximum_fusion), channel_id=1, source_target_pairs={{0,2},{1,3},{2,0},{3,1},{4,6},{5,7},{6,4},{7,5},{8,10},{9,11},{10,... | collective-permute-start | bytes 393224 | tf_op jit(solution)/shard_map/ppermute | solution.py:264
  5.1 6.6 %collective-permute-start.2 = (bf16[2,128,256]{2,1,0:T(8,128)(2,1)S(1)}, bf16[2,128,256]{2,1,0:T(8,128)(2,1)S(1)}, u32[]{:S(2)}, u32[]{:S(2)}) collective-permute-start(bf16[2,128,256]{2,1,0:T(8,128)(2,1)S(1)} %pad_maximum_fusion), channel_id=1, source_target_pairs={{0,1},{1,0},{2,3},{3,2},{4,5},{5,4},{6,7},{7,6},{8,9},{9,8},{10,11... | collective-permute-start | bytes 393224 | tf_op jit(solution)/shard_map/ppermute | solution.py:264
  6.6 1.4 %copy-start = (bf16[1,2,384,1024]{3,2,1,0:T(8,128)(2,1)S(1)}, bf16[1,2,384,1024]{3,2,1,0:T(8,128)(2,1)}, u32[]{:S(2)}) copy-start(bf16[1,2,384,1024]{3,2,1,0:T(8,128)(2,1)} %sec_ref.3) | copy-start | bytes 4718596
  8.0 10.6 %copy-start.1 = (bf16[1,2,384,1024]{3,2,1,0:T(8,128)(2,1)S(1)}, bf16[1,2,384,1024]{3,2,1,0:T(8,128)(2,1)}, u32[]{:S(2)}) copy-start(bf16[1,2,384,1024]{3,2,1,0:T(8,128)(2,1)} %sec_ref.3) | copy-start | bytes 4718596
  8.1 10.6 %collective-permute-start.4 = (bf16[2,32,1024]{2,1,0:T(8,128)(2,1)S(1)}, bf16[2,32,1024]{2,1,0:T(8,128)(2,1)S(1)}, u32[]{:S(2)}, u32[]{:S(2)}) collective-permute-start(bf16[2,32,1024]{2,1,0:T(8,128)(2,1)S(1)} %get-tuple-element.12), channel_id=1, source_target_pairs={{0,4},{4,8},{8,12},{12,16},{16,20},{20,24},{24,28},{28,0},{1,5},{5... | collective-permute-start | bytes 393224 | tf_op jit(solution)/shard_map/ppermute | solution.py:260
  8.1 10.5 %collective-permute-start.5 = (bf16[2,32,1024]{2,1,0:T(8,128)(2,1)S(1)}, bf16[2,32,1024]{2,1,0:T(8,128)(2,1)S(1)}, u32[]{:S(2)}, u32[]{:S(2)}) collective-permute-start(bf16[2,32,1024]{2,1,0:T(8,128)(2,1)S(1)} %get-tuple-element.13), channel_id=1, source_target_pairs={{0,28},{4,0},{8,4},{12,8},{16,12},{20,16},{24,20},{28,24},{1,29},{... | collective-permute-start | bytes 393224 | tf_op jit(solution)/shard_map/ppermute | solution.py:260
  11.7 8.4 %collective-permute-start.3 = (bf16[2,128,256]{2,1,0:T(8,128)(2,1)S(1)}, bf16[2,128,256]{2,1,0:T(8,128)(2,1)S(1)}, u32[]{:S(2)}, u32[]{:S(2)}) collective-permute-start(bf16[2,128,256]{2,1,0:T(8,128)(2,1)S(1)} %shard_map.74), channel_id=1, source_target_pairs={{0,1},{1,0},{2,3},{3,2},{4,5},{5,4},{6,7},{7,6},{8,9},{9,8},{10,11... | collective-permute-start | bytes 393224 | tf_op jit(solution)/shard_map/ppermute | solution.py:264
  13.2 15.1 %collective-permute-start.1 = (bf16[2,272,256]{2,1,0:T(8,128)(2,1)S(1)}, bf16[2,272,256]{2,1,0:T(8,128)(2,1)S(1)}, u32[]{:S(2)}, u32[]{:S(2)}) collective-permute-start(bf16[2,272,256]{2,1,0:T(8,128)(2,1)S(1)} %shard_map.73), channel_id=1, source_target_pairs={{0,2},{1,3},{2,0},{3,1},{4,6},{5,7},{6,4},{7,5},{8,10},{9,11},{10,... | collective-permute-start | bytes 835592 | tf_op jit(solution)/shard_map/ppermute | solution.py:264
  15.6 13.0 %collective-permute-start.8 = (bf16[2,272,256]{2,1,0:T(8,128)(2,1)S(1)}, bf16[2,272,256]{2,1,0:T(8,128)(2,1)S(1)}, u32[]{:S(2)}, u32[]{:S(2)}) collective-permute-start(bf16[2,272,256]{2,1,0:T(8,128)(2,1)S(1)} %shard_map.73), channel_id=1, source_target_pairs={{0,1},{1,0},{2,3},{3,2},{4,5},{5,4},{6,7},{7,6},{8,9},{9,8},{10,11... | collective-permute-start | bytes 835592 | tf_op jit(solution)/shard_map/ppermute | solution.py:264
  20.6 5.5 %collective-permute-start.6 = (bf16[2,64,1024]{2,1,0:T(8,128)(2,1)S(1)}, bf16[2,64,1024]{2,1,0:T(8,128)(2,1)S(1)}, u32[]{:S(2)}, u32[]{:S(2)}) collective-permute-start(bf16[2,64,1024]{2,1,0:T(8,128)(2,1)S(1)} %get-tuple-element.17), channel_id=1, source_target_pairs={{0,28},{4,0},{8,4},{12,8},{16,12},{20,16},{24,20},{28,24},{1,29},{... | collective-permute-start | bytes 786440 | tf_op jit(solution)/shard_map/ppermute | solution.py:260
  26.5 2.2 %collective-permute-start.7 = (f32[8,128]{1,0:T(8,128)S(1)}, f32[8,128]{1,0:T(8,128)S(1)}, u32[]{:S(2)}, u32[]{:S(2)}) collective-permute-start(f32[8,128]{1,0:T(8,128)S(1)} %shard_map.79), channel_id=1, source_target_pairs={{0,4},{4,0},{8,12},{12,8},{16,20},{20,16},{24,28},{28,24},{1,5},{5... | collective-permute-start | bytes 12296 | tf_op jit(solution)/shard_map/ppermute | solution.py:264
  28.7 8.9 %collective-permute-start.9 = (bf16[2,256,256]{2,1,0:T(8,128)(2,1)S(1)}, bf16[2,256,256]{2,1,0:T(8,128)(2,1)S(1)}, u32[]{:S(2)}, u32[]{:S(2)}) collective-permute-start(bf16[2,256,256]{2,1,0:T(8,128)(2,1)S(1)} %shard_map.80), channel_id=1, source_target_pairs={{0,1},{1,0},{2,3},{3,2},{4,5},{5,4},{6,7},{7,6},{8,9},{9,8},{10,11... | collective-permute-start | bytes 786440 | tf_op jit(solution)/shard_map/ppermute | solution.py:264
  30.2 3.6 %collective-permute-start.10 = (f32[8,128]{1,0:T(8,128)S(1)}, f32[8,128]{1,0:T(8,128)S(1)}, u32[]{:S(2)}, u32[]{:S(2)}) collective-permute-start(f32[8,128]{1,0:T(8,128)S(1)} %add.6), channel_id=1, source_target_pairs={{0,8},{4,12},{8,0},{12,4},{16,24},{20,28},{24,16},{28,20},{1,9},{5... | collective-permute-start | bytes 12296 | tf_op jit(solution)/shard_map/ppermute | solution.py:264
  33.8 3.6 %collective-permute-start.11 = (f32[8,128]{1,0:T(8,128)S(1)}, f32[8,128]{1,0:T(8,128)S(1)}, u32[]{:S(2)}, u32[]{:S(2)}) collective-permute-start(f32[8,128]{1,0:T(8,128)S(1)} %add.7.mine_ref), channel_id=1, source_target_pairs={{0,16},{4,20},{8,24},{12,28},{16,0},{20,4},{24,8},{28,12},{1,17},{... | collective-permute-start | bytes 12296 | tf_op jit(solution)/shard_map/ppermute | solution.py:264

commit v19 on v18

--- a/solution.py
+++ b/solution.py
@@ -138,7 +138,7 @@
     looks_n = looks_ref.shape[2]
     totals = [None, None]
     for step, (prim_ref, starts) in enumerate(
-        ((own_ref, whole), (one_ref, edges), (two_ref, edges), (three_ref, edges))
+        ((own_ref, whole), (one_ref, whole), (two_ref, edges), (three_ref, edges))
     ):
         block = jnp.bitwise_xor(here, step)
         select = look_columns(width, block, looks_n)
@@ -275,7 +275,7 @@
     middle_n = rows_n - 2 * LAG
     edges = jnp.concatenate([primary[:, :LAG], primary[:, rows_n - LAG :]], axis=1)
     edges_two = swap(edges, "date", 2)
-    edges_one = swap(edges, "date", 1)
+    one = swap(primary, "date", 1)
     halo = shape((2, HALO, cols_n), bf16)
     down, up = call(cut_halo_kernel, (halo, halo), [], (0, 0), secondary)
     low = ring(down, "tile", 1)
@@ -288,7 +288,7 @@
         az_off, rg_off, az_frac, rg_frac,
     )
     passed = call(
-        relay_kernel, shape(edges.shape, bf16), [], (0, 0), edges_two, edges_one
+        relay_kernel, shape(edges.shape, bf16), [], (2 * 10**9, 0), edges_two, edges
     )
     edges_three = swap(passed, "date", 1)
     middle = call(
@@ -306,14 +306,14 @@
         (0, 0),
         secondary, low, high, az_band, rg_band,
     )
-    two, one = [swap(middle, "date", step) for step in (2, 1)]
+    two = swap(middle, "date", 2)
     margin = shape((2, LAG, cols_n), bf16)
     first, last, looks = call(
         margin_kernel,
         (margin, margin, shape((2, 2 * LAG // LA, looks_n), f32)),
         [pltpu.VMEM((2, 2 * LAG, looks_n), f32)],
         (0, 0),
-        primary, edges_one, edges_two, edges_three, res,
+        primary, one, edges_two, edges_three, res,
     )
     later = ring(first, "tile", -1)
     stats = call(
@@ -332,7 +332,7 @@
     )
     other = swap(stats, "tile", 1)
     block = shape((2, middle_n, width), bf16)
-    relayed = call(relay_kernel, block, [], (0, 0), two, other,one)
+    relayed = call(relay_kernel, block, [], (0, 0), two, other)
     three = swap(relayed, "date", 1)
     stride = 2
     while stride < tiles_n:

time: 38.8 us -> 42.4 us (1.093)
  waiting for transfers between devices: 9.2 us -> 14.2 us
  starting transfers between devices: 19.1 us -> 17.7 us
    ppermute x9 -> x8, waiting for transfers between devices: 6.06 us -> 11.1 us  [swap(): lax.ppermute(value, axis, [(at, at ^ step) for at in range(lax.axis_size(...]
    ppermute x9 -> x8, starting transfers between devices: 14.8 us -> 14.1 us  [swap(): lax.ppermute(value, axis, [(at, at ^ step) for at in range(lax.axis_size(...]
    ppermute x3, starting transfers between devices: 4.25 us -> 3.56 us  [ring(): lax.ppermute(value, axis, [(at, (at + step) % count) for at in range(coun...]
  transfers between devices with their start and end apart: 12 -> 11, of which waited for: 7 -> 7; matrix products, arithmetic and copies ran while one was open for 2% -> 2% of each run, Pallas kernels for 9% -> 8%
where the time goes in v19:
time: 42.4 us; the launch traced here: 42.1 us
  starting transfers between devices  17.7 us (42%)
  waiting for transfers between devices  14.2 us (33%)
  Pallas kernels  4.39 us (10%)
  between operations  2.72 us (6%)
  local copies, waits for them, and re-layouts  2.37 us (6%)
  other arithmetic  0.77 us (2%)
    ppermute x8, starting transfers between devices, swap(): lax.ppermute(value, axis, [(at, at ^ step) for at in range(lax.axis_size(...  14.1 us
    ppermute x8, waiting for transfers between devices, swap(): lax.ppermute(value, axis, [(at, at ^ step) for at in range(lax.axis_size(...  11.1 us
    pallas_call x11, Pallas kernels, call(): pl.pallas_call(kernel, out_shape=outs, in_specs=[vmem] * len(args), out_s...  4.39 us
    ppermute x3, starting transfers between devices, ring(): lax.ppermute(value, axis, [(at, (at + step) % count) for at in range(coun...  3.56 us
    ppermute x3, waiting for transfers between devices, ring(): lax.ppermute(value, axis, [(at, (at + step) % count) for at in range(coun...  3.14 us
    unnamed x6, local copies, waits for them, and re-layouts  1.42 us
    slice x1, local copies, waits for them, and re-layouts, fused(): primary[:, :LAG]  0.88 us
  transfers between devices with their start and end apart: 11, of which 7 were waited for; matrix products, arithmetic and copies ran while one was open for 2% of the time, Pallas kernels for 8%

profile of v19, /device:TPU:0, one launch (start us, length us, event | category | flops | bytes accessed | tf_op | source)
XLA Modules:
  0.0 42.1 jit_solution(18220595081495926610)
XLA Ops:
  0.0 0.9 %fusion = (bf16[2,64,256]{2,1,0:T(8,128)(2,1)S(1)}, bf16[2,64,256]{2,1,0:T(8,128)(2,1)S(1)}) fusion(bf16[2,384,256]{2,1,0:T(8,128)(2,1)} %own_ref.3), kind=kLoop, calls=%fused_computation.2 | loop fusion | bytes 262144 | tf_op jit(solution)/shard_map/slice | solution.py:276
  0.9 4.1 %collective-permute-start = (bf16[2,128,256]{2,1,0:T(8,128)(2,1)S(1)}, bf16[2,128,256]{2,1,0:T(8,128)(2,1)S(1)}, u32[]{:S(2)}, u32[]{:S(2)}) collective-permute-start(bf16[2,128,256]{2,1,0:T(8,128)(2,1)S(1)} %pad_maximum_fusion.refs_0_), channel_id=1, source_target_pairs={{0,2},{1,3},{2,0},{3,1},{4,6},{5,7},{6,4},{7,5},{8,10},{9,11},{10,... | collective-permute-start | bytes 393224 | tf_op jit(solution)/shard_map/ppermute | solution.py:264
  5.0 1.6 %collective-permute-start.2 = (bf16[2,384,256]{2,1,0:T(8,128)(2,1)}, bf16[2,384,256]{2,1,0:T(8,128)(2,1)S(1)}, u32[]{:S(2)}, u32[]{:S(2)}) collective-permute-start(bf16[2,384,256]{2,1,0:T(8,128)(2,1)} %own_ref.3), channel_id=1, source_target_pairs={{0,1},{1,0},{2,3},{3,2},{4,5},{5,4},{6,7},{7,6},{8,9},{9,8},{10,11... | collective-permute-start | bytes 1179656 | tf_op jit(solution)/shard_map/ppermute | solution.py:264
  6.6 1.4 %copy-done = bf16[1,2,384,1024]{3,2,1,0:T(8,128)(2,1)S(1)} copy-done((bf16[1,2,384,1024]{3,2,1,0:T(8,128)(2,1)S(1)}, bf16[1,2,384,1024]{3,2,1,0:T(8,128)(2,1)}, u32[]{:S(2)}) %copy-start) | copy-done | bytes 1572888
  8.0 0.1 collective-permute-start.4
  8.1 0.0 copy-start.2
  8.1 2.6 %collective-permute-start.5 = (bf16[2,32,1024]{2,1,0:T(8,128)(2,1)S(1)}, bf16[2,32,1024]{2,1,0:T(8,128)(2,1)S(1)}, u32[]{:S(2)}, u32[]{:S(2)}) collective-permute-start(bf16[2,32,1024]{2,1,0:T(8,128)(2,1)S(1)} %get-tuple-element.13), channel_id=1, source_target_pairs={{0,28},{4,0},{8,4},{12,8},{16,12},{20,16},{24,20},{28,24},{1,29},{... | collective-permute-start | bytes 393224 | tf_op jit(solution)/shard_map/ppermute | solution.py:260
  10.7 0.7 %collective-permute-done.refs_0_.block_ref.two_ref = bf16[2,128,256]{2,1,0:T(8,128)(2,1)S(1)} collective-permute-done((bf16[2,128,256]{2,1,0:T(8,128)(2,1)S(1)}, bf16[2,128,256]{2,1,0:T(8,128)(2,1)S(1)}, u32[]{:S(2)}, u32[]{:S(2)}) %collective-permute-start) | collective-permute-done | bytes 131104 | tf_op jit(solution)/shard_map/ppermute | solution.py:264
  11.4 0.7 %collective-permute-start.3 = (bf16[2,128,256]{2,1,0:T(8,128)(2,1)S(1)}, bf16[2,128,256]{2,1,0:T(8,128)(2,1)S(1)}, u32[]{:S(2)}, u32[]{:S(2)}) collective-permute-start(bf16[2,128,256]{2,1,0:T(8,128)(2,1)S(1)} %shard_map.74), channel_id=1, source_target_pairs={{0,1},{1,0},{2,3},{3,2},{4,5},{5,4},{6,7},{7,6},{8,9},{9,8},{10,11... | collective-permute-start | bytes 393224 | tf_op jit(solution)/shard_map/ppermute | solution.py:264
  12.2 3.5 %collective-permute-start.1 = (bf16[2,272,256]{2,1,0:T(8,128)(2,1)S(1)}, bf16[2,272,256]{2,1,0:T(8,128)(2,1)S(1)}, u32[]{:S(2)}, u32[]{:S(2)}) collective-permute-start(bf16[2,272,256]{2,1,0:T(8,128)(2,1)S(1)} %shard_map.73), channel_id=1, source_target_pairs={{0,2},{1,3},{2,0},{3,1},{4,6},{5,7},{6,4},{7,5},{8,10},{9,11},{10,... | collective-permute-start | bytes 835592 | tf_op jit(solution)/shard_map/ppermute | solution.py:264
  18.3 0.4 shard_map.76
  18.7 0.0 collective-permute-done.5.high_ref
  18.7 1.4 %shard_map.77.res_ref = bf16[4,2,384,256]{3,2,1,0:T(8,128)(2,1)S(1)} custom-call(bf16[1,2,384,1024]{3,2,1,0:T(8,128)(2,1)S(1)} %copy-done.1, bf16[2,32,1024]{2,1,0:T(8,128)(2,1)S(1)} %collective-permute-done.4.low_ref, bf16[2,32,1024]{2,1,0:T(8,128)(2,1)S(1)} %collective-permute-done.5.high_ref, bf16[128,192]{1,0:T(8,128)(2,1)S(1)} %get-tuple-element.14.az_ref, ...), custom_call_target="tpu_custom_call" | custom-call | tf_op jit(solution)/shard_map/pallas_call | solution.py:247
  20.1 4.8 %collective-permute-done.3.three_ref = bf16[2,128,256]{2,1,0:T(8,128)(2,1)S(1)} collective-permute-done((bf16[2,128,256]{2,1,0:T(8,128)(2,1)S(1)}, bf16[2,128,256]{2,1,0:T(8,128)(2,1)S(1)}, u32[]{:S(2)}, u32[]{:S(2)}) %collective-permute-start.3) | collective-permute-done | bytes 131104 | tf_op jit(solution)/shard_map/ppermute | solution.py:264
  24.9 0.5 %shard_map.78 = (bf16[2,64,1024]{2,1,0:T(8,128)(2,1)S(1)}, bf16[2,64,1024]{2,1,0:T(8,128)(2,1)S(1)}, f32[2,64,128]{2,1,0:T(8,128)S(1)}) custom-call(bf16[2,384,256]{2,1,0:T(8,128)(2,1)S(1)} %copy-done.2, bf16[2,384,256]{2,1,0:T(8,128)(2,1)S(1)} %collective-permute-done.2.one_ref, bf16[2,128,256]{2,1,0:T(8,128)(2,1)S(1)} %collective-permute-done.refs_0_.block_ref.two_ref, ...), custom_call_target="tpu_custom_call" | custom-call | tf_op jit(solution)/shard_map/pallas_call | solution.py:247
  25.5 0.9 %collective-permute-start.6 = (bf16[2,64,1024]{2,1,0:T(8,128)(2,1)S(1)}, bf16[2,64,1024]{2,1,0:T(8,128)(2,1)S(1)}, u32[]{:S(2)}, u32[]{:S(2)}) collective-permute-start(bf16[2,64,1024]{2,1,0:T(8,128)(2,1)S(1)} %get-tuple-element.17), channel_id=1, source_target_pairs={{0,28},{4,0},{8,4},{12,8},{16,12},{20,16},{24,20},{28,24},{1,29},{... | collective-permute-start | bytes 786440 | tf_op jit(solution)/shard_map/ppermute | solution.py:260
  26.3 0.8 %slice_convert_fusion = f32[64]{0:T(128)S(1)} fusion(s32[384]{0:T(512)} %param.9), kind=kLoop, calls=%fused_computation.1 | loop fusion | flops 64 | bytes 512 | tf_op jit(solution)/shard_map/convert_element_type | solution.py:301
  27.1 3.1 %collective-permute-done.6.later_ref = bf16[2,64,1024]{2,1,0:T(8,128)(2,1)S(1)} collective-permute-done((bf16[2,64,1024]{2,1,0:T(8,128)(2,1)S(1)}, bf16[2,64,1024]{2,1,0:T(8,128)(2,1)S(1)}, u32[]{:S(2)}, u32[]{:S(2)}) %collective-permute-start.6) | collective-permute-done | bytes 262176 | tf_op jit(solution)/shard_map/ppermute | solution.py:260
  30.2 0.1 broadcast_in_dim.2.weight_ref
  30.3 0.4 shard_map.79
  30.7 1.1 %collective-permute-start.7 = (f32[8,128]{1,0:T(8,128)S(1)}, f32[8,128]{1,0:T(8,128)S(1)}, u32[]{:S(2)}, u32[]{:S(2)}) collective-permute-start(f32[8,128]{1,0:T(8,128)S(1)} %shard_map.79), channel_id=1, source_target_pairs={{0,4},{4,0},{8,12},{12,8},{16,20},{20,16},{24,28},{28,24},{1,5},{5... | collective-permute-start | bytes 12296 | tf_op jit(solution)/shard_map/ppermute | solution.py:264
  31.7 0.0 collective-permute-done.1.block_ref.two_ref
  31.7 0.8 %collective-permute-done.7.refs_0_ = f32[8,128]{1,0:T(8,128)S(1)} collective-permute-done((f32[8,128]{1,0:T(8,128)S(1)}, f32[8,128]{1,0:T(8,128)S(1)}, u32[]{:S(2)}, u32[]{:S(2)}) %collective-permute-start.7) | collective-permute-done | bytes 4128 | tf_op jit(solution)/shard_map/ppermute | solution.py:264
  32.6 0.1 collective-permute-start.8
  32.7 1.6 %collective-permute-start.9 = (f32[8,128]{1,0:T(8,128)S(1)}, f32[8,128]{1,0:T(8,128)S(1)}, u32[]{:S(2)}, u32[]{:S(2)}) collective-permute-start(f32[8,128]{1,0:T(8,128)S(1)} %add.6), channel_id=1, source_target_pairs={{0,8},{4,12},{8,0},{12,4},{16,24},{20,28},{24,16},{28,20},{1,9},{5... | collective-permute-start | bytes 12296 | tf_op jit(solution)/shard_map/ppermute | solution.py:264
  34.2 2.1 %collective-permute-done.9 = f32[8,128]{1,0:T(8,128)S(1)} collective-permute-done((f32[8,128]{1,0:T(8,128)S(1)}, f32[8,128]{1,0:T(8,128)S(1)}, u32[]{:S(2)}, u32[]{:S(2)}) %collective-permute-start.9) | collective-permute-done | bytes 4128 | tf_op jit(solution)/shard_map/ppermute | solution.py:264
  36.3 1.5 %collective-permute-start.10 = (f32[8,128]{1,0:T(8,128)S(1)}, f32[8,128]{1,0:T(8,128)S(1)}, u32[]{:S(2)}, u32[]{:S(2)}) collective-permute-start(f32[8,128]{1,0:T(8,128)S(1)} %add.7.mine_ref), channel_id=1, source_target_pairs={{0,16},{4,20},{8,24},{12,28},{16,0},{20,4},{24,8},{28,12},{1,17},{... | collective-permute-start | bytes 12296 | tf_op jit(solution)/shard_map/ppermute | solution.py:264
  37.9 0.6 %shard_map.81.before_ref = f32[2,256,128]{2,1,0:T(8,128)S(1)} custom-call(bf16[2,384,256]{2,1,0:T(8,128)(2,1)S(1)} %copy-done.2, bf16[2,384,256]{2,1,0:T(8,128)(2,1)S(1)} %collective-permute-done.2.one_ref, bf16[2,272,256]{2,1,0:T(8,128)(2,1)S(1)} %collective-permute-done.1.block_ref.two_ref, bf16[4,2,384,256]{3,2,1,0:T(8,128)(2,1)S(1)} %shard_map.77.res_ref), custom_call_target="tpu_custom_call" | custom-call | flops 134217728 | bytes 3145728 | tf_op jit(solution)/shard_map/pallas_call | solution.py:247
  38.4 1.5 %collective-permute-done.10.other_ref = f32[8,128]{1,0:T(8,128)S(1)} collective-permute-done((f32[8,128]{1,0:T(8,128)S(1)}, f32[8,128]{1,0:T(8,128)S(1)}, u32[]{:S(2)}, u32[]{:S(2)}) %collective-permute-start.10) | collective-permute-done | bytes 4128 | tf_op jit(solution)/shard_map/ppermute | solution.py:264
  39.9 0.1 shard_map.82.unit_ref
  40.1 1.1 %collective-permute-done.8.three_ref = bf16[2,256,256]{2,1,0:T(8,128)(2,1)S(1)} collective-permute-done((bf16[2,256,256]{2,1,0:T(8,128)(2,1)S(1)}, bf16[2,256,256]{2,1,0:T(8,128)(2,1)S(1)}, u32[]{:S(2)}, u32[]{:S(2)}) %collective-permute-start.8) | collective-permute-done | bytes 262176 | tf_op jit(solution)/shard_map/ppermute | solution.py:264
  41.2 1.0 %shard_map.83 = f32[1,2,192,128]{3,2,1,0:T(8,128)} custom-call(bf16[2,256,256]{2,1,0:T(8,128)(2,1)S(1)} %collective-permute-done.8.three_ref, bf16[4,2,384,256]{3,2,1,0:T(8,128)(2,1)S(1)} %shard_map.77.res_ref, f32[2,256,128]{2,1,0:T(8,128)S(1)} %shard_map.81.before_ref, f32[2,64,128]{2,1,0:T(8,128)S(1)} %get-tuple-element.18.looks_ref, ...), custom_call_target="tpu_custom_call" | custom-call | flops 67108864 | bytes 1572864 | tf_op jit(solution)/shard_map/pallas_call | solution.py:247
  (13 shorter events, 0.1 us)
Async XLA Ops:
  0.9 10.5 %collective-permute-start = (bf16[2,128,256]{2,1,0:T(8,128)(2,1)S(1)}, bf16[2,128,256]{2,1,0:T(8,128)(2,1)S(1)}, u32[]{:S(2)}, u32[]{:S(2)}) collective-permute-start(bf16[2,128,256]{2,1,0:T(8,128)(2,1)S(1)} %pad_maximum_fusion.refs_0_), channel_id=1, source_target_pairs={{0,2},{1,3},{2,0},{3,1},{4,6},{5,7},{6,4},{7,5},{8,10},{9,11},{10,... | collective-permute-start | bytes 393224 | tf_op jit(solution)/shard_map/ppermute | solution.py:264
  5.0 19.9 %collective-permute-start.2 = (bf16[2,384,256]{2,1,0:T(8,128)(2,1)}, bf16[2,384,256]{2,1,0:T(8,128)(2,1)S(1)}, u32[]{:S(2)}, u32[]{:S(2)}) collective-permute-start(bf16[2,384,256]{2,1,0:T(8,128)(2,1)} %own_ref.3), channel_id=1, source_target_pairs={{0,1},{1,0},{2,3},{3,2},{4,5},{5,4},{6,7},{7,6},{8,9},{9,8},{10,11... | collective-permute-start | bytes 1179656 | tf_op jit(solution)/shard_map/ppermute | solution.py:264
  6.6 1.4 %copy-start = (bf16[1,2,384,1024]{3,2,1,0:T(8,128)(2,1)S(1)}, bf16[1,2,384,1024]{3,2,1,0:T(8,128)(2,1)}, u32[]{:S(2)}) copy-start(bf16[1,2,384,1024]{3,2,1,0:T(8,128)(2,1)} %sec_ref.3) | copy-start | bytes 4718596
  8.0 10.6 %collective-permute-start.4 = (bf16[2,32,1024]{2,1,0:T(8,128)(2,1)S(1)}, bf16[2,32,1024]{2,1,0:T(8,128)(2,1)S(1)}, u32[]{:S(2)}, u32[]{:S(2)}) collective-permute-start(bf16[2,32,1024]{2,1,0:T(8,128)(2,1)S(1)} %get-tuple-element.12), channel_id=1, source_target_pairs={{0,4},{4,8},{8,12},{12,16},{16,20},{20,24},{24,28},{28,0},{1,5},{5... | collective-permute-start | bytes 393224 | tf_op jit(solution)/shard_map/ppermute | solution.py:260
  8.1 4.1 %copy-start.2 = (bf16[2,384,256]{2,1,0:T(8,128)(2,1)S(1)}, bf16[2,384,256]{2,1,0:T(8,128)(2,1)}, u32[]{:S(2)}) copy-start(bf16[2,384,256]{2,1,0:T(8,128)(2,1)} %own_ref.3) | copy-start | bytes 1179652
  8.1 10.6 %collective-permute-start.5 = (bf16[2,32,1024]{2,1,0:T(8,128)(2,1)S(1)}, bf16[2,32,1024]{2,1,0:T(8,128)(2,1)S(1)}, u32[]{:S(2)}, u32[]{:S(2)}) collective-permute-start(bf16[2,32,1024]{2,1,0:T(8,128)(2,1)S(1)} %get-tuple-element.13), channel_id=1, source_target_pairs={{0,28},{4,0},{8,4},{12,8},{16,12},{20,16},{24,20},{28,24},{1,29},{... | collective-permute-start | bytes 393224 | tf_op jit(solution)/shard_map/ppermute | solution.py:260
  11.4 7.3 %copy-start.1 = (bf16[1,2,384,1024]{3,2,1,0:T(8,128)(2,1)S(1)}, bf16[1,2,384,1024]{3,2,1,0:T(8,128)(2,1)}, u32[]{:S(2)}) copy-start(bf16[1,2,384,1024]{3,2,1,0:T(8,128)(2,1)} %sec_ref.3) | copy-start | bytes 4718596
  11.4 13.5 %collective-permute-start.3 = (bf16[2,128,256]{2,1,0:T(8,128)(2,1)S(1)}, bf16[2,128,256]{2,1,0:T(8,128)(2,1)S(1)}, u32[]{:S(2)}, u32[]{:S(2)}) collective-permute-start(bf16[2,128,256]{2,1,0:T(8,128)(2,1)S(1)} %shard_map.74), channel_id=1, source_target_pairs={{0,1},{1,0},{2,3},{3,2},{4,5},{5,4},{6,7},{7,6},{8,9},{9,8},{10,11... | collective-permute-start | bytes 393224 | tf_op jit(solution)/shard_map/ppermute | solution.py:264
  12.2 19.5 %collective-permute-start.1 = (bf16[2,272,256]{2,1,0:T(8,128)(2,1)S(1)}, bf16[2,272,256]{2,1,0:T(8,128)(2,1)S(1)}, u32[]{:S(2)}, u32[]{:S(2)}) collective-permute-start(bf16[2,272,256]{2,1,0:T(8,128)(2,1)S(1)} %shard_map.73), channel_id=1, source_target_pairs={{0,2},{1,3},{2,0},{3,1},{4,6},{5,7},{6,4},{7,5},{8,10},{9,11},{10,... | collective-permute-start | bytes 835592 | tf_op jit(solution)/shard_map/ppermute | solution.py:264
  25.5 4.8 %collective-permute-start.6 = (bf16[2,64,1024]{2,1,0:T(8,128)(2,1)S(1)}, bf16[2,64,1024]{2,1,0:T(8,128)(2,1)S(1)}, u32[]{:S(2)}, u32[]{:S(2)}) collective-permute-start(bf16[2,64,1024]{2,1,0:T(8,128)(2,1)S(1)} %get-tuple-element.17), channel_id=1, source_target_pairs={{0,28},{4,0},{8,4},{12,8},{16,12},{20,16},{24,20},{28,24},{1,29},{... | collective-permute-start | bytes 786440 | tf_op jit(solution)/shard_map/ppermute | solution.py:260
  30.7 1.9 %collective-permute-start.7 = (f32[8,128]{1,0:T(8,128)S(1)}, f32[8,128]{1,0:T(8,128)S(1)}, u32[]{:S(2)}, u32[]{:S(2)}) collective-permute-start(f32[8,128]{1,0:T(8,128)S(1)} %shard_map.79), channel_id=1, source_target_pairs={{0,4},{4,0},{8,12},{12,8},{16,20},{20,16},{24,28},{28,24},{1,5},{5... | collective-permute-start | bytes 12296 | tf_op jit(solution)/shard_map/ppermute | solution.py:264
  32.6 8.6 %collective-permute-start.8 = (bf16[2,256,256]{2,1,0:T(8,128)(2,1)S(1)}, bf16[2,256,256]{2,1,0:T(8,128)(2,1)S(1)}, u32[]{:S(2)}, u32[]{:S(2)}) collective-permute-start(bf16[2,256,256]{2,1,0:T(8,128)(2,1)S(1)} %shard_map.80), channel_id=1, source_target_pairs={{0,1},{1,0},{2,3},{3,2},{4,5},{5,4},{6,7},{7,6},{8,9},{9,8},{10,11... | collective-permute-start | bytes 786440 | tf_op jit(solution)/shard_map/ppermute | solution.py:264
  32.7 3.7 %collective-permute-start.9 = (f32[8,128]{1,0:T(8,128)S(1)}, f32[8,128]{1,0:T(8,128)S(1)}, u32[]{:S(2)}, u32[]{:S(2)}) collective-permute-start(f32[8,128]{1,0:T(8,128)S(1)} %add.6), channel_id=1, source_target_pairs={{0,8},{4,12},{8,0},{12,4},{16,24},{20,28},{24,16},{28,20},{1,9},{5... | collective-permute-start | bytes 12296 | tf_op jit(solution)/shard_map/ppermute | solution.py:264
  36.3 3.6 %collective-permute-start.10 = (f32[8,128]{1,0:T(8,128)S(1)}, f32[8,128]{1,0:T(8,128)S(1)}, u32[]{:S(2)}, u32[]{:S(2)}) collective-permute-start(f32[8,128]{1,0:T(8,128)S(1)} %add.7.mine_ref), channel_id=1, source_target_pairs={{0,16},{4,20},{8,24},{12,28},{16,0},{20,4},{24,8},{28,12},{1,17},{... | collective-permute-start | bytes 12296 | tf_op jit(solution)/shard_map/ppermute | solution.py:264

commit v20 on v18

--- a/solution.py
+++ b/solution.py
@@ -215,6 +215,10 @@
         out_ref[part] = total
 
 
+def add_kernel(mine_ref, other_ref, *refs):
+    refs[-1][...] = mine_ref[...] + other_ref[...]
+
+
 def unit_kernel(mine_ref, other_ref, unit_ref):
     stats = jnp.sum(mine_ref[...] + other_ref[...], axis=1, keepdims=True)
     e_re, e_im, power, count = [stats[row : row + 1] for row in range(4)]
@@ -276,8 +280,7 @@
     edges = jnp.concatenate([primary[:, :LAG], primary[:, rows_n - LAG :]], axis=1)
     edges_two = swap(edges, "date", 2)
     edges_one = swap(edges, "date", 1)
-    halo = shape((2, HALO, cols_n), bf16)
-    down, up = call(cut_halo_kernel, (halo, halo), [], (0, 0), secondary)
+    down, up = secondary[0, :, rows_n - HALO :], secondary[0, :, :HALO]
     low = ring(down, "tile", 1)
     high = ring(up, "tile", -1)
     az_band, rg_band = call(
@@ -327,14 +330,16 @@
         middle_kernel,
         shape((2, middle_n, looks_n), f32),
         [],
-        (2 * 2 * middle_n * cols_n * looks_n, 8 * rows_n * cols_n),
+        (3 * 10**9, 8 * rows_n * cols_n),
         primary, one, two, res,
     )
     other = swap(stats, "tile", 1)
     block = shape((2, middle_n, width), bf16)
-    relayed = call(relay_kernel, block, [], (0, 0), two, other,one)
+    relayed = call(relay_kernel, block, [], (0, 0), two, other)
     three = swap(relayed, "date", 1)
-    stride = 2
+    stats = call(add_kernel, shape((8, LANE), f32), [], (0, 0), stats, other, one)
+    other = swap(stats, "tile", 2)
+    stride = 4
     while stride < tiles_n:
         stats = stats + other
         other = swap(stats, "tile", stride)

time: 38.8 us -> 42.8 us (1.10)
  waiting for transfers between devices: 9.2 us -> 15.2 us
  starting transfers between devices: 19.1 us -> 17.4 us
    ppermute x9, waiting for transfers between devices: 6.06 us -> 12.1 us  [swap(): lax.ppermute(value, axis, [(at, at ^ step) for at in range(lax.axis_size(...]
    ppermute x3, starting transfers between devices: 4.25 us -> 2.75 us  [ring(): lax.ppermute(value, axis, [(at, (at + step) % count) for at in range(coun...]
    unnamed x6 -> x4, local copies, waits for them, and re-layouts: 1.41 us -> 0.01 us
    squeeze x0 -> x1, local copies, waits for them, and re-layouts: none -> 0.99 us  [fused(): down, up = (secondary[0, :, rows_n - HALO:], secondary[0, :, :HALO])]
  transfers between devices with their start and end apart: 12 -> 12, of which waited for: 7 -> 8; matrix products, arithmetic and copies ran while one was open for 2% -> 4% of each run, Pallas kernels for 9% -> 8%
where the time goes in v20:
time: 42.8 us; the launch traced here: 42.6 us
  starting transfers between devices  17.4 us (41%)
  waiting for transfers between devices  15.2 us (36%)
  Pallas kernels  4.37 us (10%)
  between operations  2.72 us (6%)
  local copies, waits for them, and re-layouts  2.09 us (5%)
  other arithmetic  0.77 us (2%)
    ppermute x9, starting transfers between devices, swap(): lax.ppermute(value, axis, [(at, at ^ step) for at in range(lax.axis_size(...  14.7 us
    ppermute x9, waiting for transfers between devices, swap(): lax.ppermute(value, axis, [(at, at ^ step) for at in range(lax.axis_size(...  12.1 us
    pallas_call x11, Pallas kernels, call(): pl.pallas_call(kernel, out_shape=outs, in_specs=[vmem] * len(args), out_s...  4.37 us
    ppermute x3, waiting for transfers between devices, ring(): lax.ppermute(value, axis, [(at, (at + step) % count) for at in range(coun...  3.13 us
    ppermute x3, starting transfers between devices, ring(): lax.ppermute(value, axis, [(at, (at + step) % count) for at in range(coun...  2.75 us
    slice x1, local copies, waits for them, and re-layouts, fused(): primary[:, :LAG]  1.02 us
    squeeze x1, local copies, waits for them, and re-layouts, fused(): down, up = (secondary[0, :, rows_n - HALO:], secondary[0, :, :HALO])  0.99 us
  transfers between devices with their start and end apart: 12, of which 8 were waited for; matrix products, arithmetic and copies ran while one was open for 4% of the time, Pallas kernels for 8%

profile of v20, /device:TPU:0, one launch (start us, length us, event | category | flops | bytes accessed | tf_op | source)
XLA Modules:
  0.0 42.6 jit_solution(16666963341772423737)
XLA Ops:
  0.0 1.0 %fusion = (bf16[2,64,256]{2,1,0:T(8,128)(2,1)S(1)}, bf16[2,64,256]{2,1,0:T(8,128)(2,1)S(1)}) fusion(bf16[2,384,256]{2,1,0:T(8,128)(2,1)} %own_ref.3), kind=kLoop, calls=%fused_computation.4 | loop fusion | bytes 262144 | tf_op jit(solution)/shard_map/slice | solution.py:280
  1.0 4.1 %collective-permute-start = (bf16[2,128,256]{2,1,0:T(8,128)(2,1)S(1)}, bf16[2,128,256]{2,1,0:T(8,128)(2,1)S(1)}, u32[]{:S(2)}, u32[]{:S(2)}) collective-permute-start(bf16[2,128,256]{2,1,0:T(8,128)(2,1)S(1)} %pad_maximum_fusion), channel_id=1, source_target_pairs={{0,2},{1,3},{2,0},{3,1},{4,6},{5,7},{6,4},{7,5},{8,10},{9,11},{10,... | collective-permute-start | bytes 393224 | tf_op jit(solution)/shard_map/ppermute | solution.py:268
  5.2 1.6 %collective-permute-start.2 = (bf16[2,128,256]{2,1,0:T(8,128)(2,1)S(1)}, bf16[2,128,256]{2,1,0:T(8,128)(2,1)S(1)}, u32[]{:S(2)}, u32[]{:S(2)}) collective-permute-start(bf16[2,128,256]{2,1,0:T(8,128)(2,1)S(1)} %pad_maximum_fusion), channel_id=1, source_target_pairs={{0,1},{1,0},{2,3},{3,2},{4,5},{5,4},{6,7},{7,6},{8,9},{9,8},{10,11... | collective-permute-start | bytes 393224 | tf_op jit(solution)/shard_map/ppermute | solution.py:268
  6.7 1.0 %slice_bitcast_fusion = (bf16[2,32,1024]{2,1,0:T(8,128)(2,1)S(1)}, bf16[2,32,1024]{2,1,0:T(8,128)(2,1)S(1)}) fusion(bf16[1,2,384,1024]{3,2,1,0:T(8,128)(2,1)} %sec_ref.1), kind=kLoop, calls=%fused_computation.1 | loop fusion | bytes 524288 | tf_op jit(solution)/shard_map/squeeze | solution.py:283
  7.7 0.1 collective-permute-start.4
  7.8 2.6 %collective-permute-start.5 = (bf16[2,32,1024]{2,1,0:T(8,128)(2,1)S(1)}, bf16[2,32,1024]{2,1,0:T(8,128)(2,1)S(1)}, u32[]{:S(2)}, u32[]{:S(2)}) collective-permute-start(bf16[2,32,1024]{2,1,0:T(8,128)(2,1)S(1)} %get-tuple-element.15), channel_id=1, source_target_pairs={{0,28},{4,0},{8,4},{12,8},{16,12},{20,16},{24,20},{28,24},{1,29},{... | collective-permute-start | bytes 393224 | tf_op jit(solution)/shard_map/ppermute | solution.py:264
  10.4 1.1 %collective-permute-done.refs_0_.block_ref.two_ref = bf16[2,128,256]{2,1,0:T(8,128)(2,1)S(1)} collective-permute-done((bf16[2,128,256]{2,1,0:T(8,128)(2,1)S(1)}, bf16[2,128,256]{2,1,0:T(8,128)(2,1)S(1)}, u32[]{:S(2)}, u32[]{:S(2)}) %collective-permute-start) | collective-permute-done | bytes 131104 | tf_op jit(solution)/shard_map/ppermute | solution.py:268
  11.6 0.2 collective-permute-done.2.refs_0_.one_ref
  11.8 1.5 %collective-permute-start.3 = (bf16[2,128,256]{2,1,0:T(8,128)(2,1)S(1)}, bf16[2,128,256]{2,1,0:T(8,128)(2,1)S(1)}, u32[]{:S(2)}, u32[]{:S(2)}) collective-permute-start(bf16[2,128,256]{2,1,0:T(8,128)(2,1)S(1)} %shard_map.74), channel_id=1, source_target_pairs={{0,1},{1,0},{2,3},{3,2},{4,5},{5,4},{6,7},{7,6},{8,9},{9,8},{10,11... | collective-permute-start | bytes 393224 | tf_op jit(solution)/shard_map/ppermute | solution.py:268
  13.3 0.7 %collective-permute-start.9 = (bf16[2,272,256]{2,1,0:T(8,128)(2,1)S(1)}, bf16[2,272,256]{2,1,0:T(8,128)(2,1)S(1)}, u32[]{:S(2)}, u32[]{:S(2)}) collective-permute-start(bf16[2,272,256]{2,1,0:T(8,128)(2,1)S(1)} %shard_map.73), channel_id=1, source_target_pairs={{0,1},{1,0},{2,3},{3,2},{4,5},{5,4},{6,7},{7,6},{8,9},{9,8},{10,11... | collective-permute-start | bytes 835592 | tf_op jit(solution)/shard_map/ppermute | solution.py:268
  14.0 1.9 %collective-permute-start.1 = (bf16[2,272,256]{2,1,0:T(8,128)(2,1)S(1)}, bf16[2,272,256]{2,1,0:T(8,128)(2,1)S(1)}, u32[]{:S(2)}, u32[]{:S(2)}) collective-permute-start(bf16[2,272,256]{2,1,0:T(8,128)(2,1)S(1)} %shard_map.73), channel_id=1, source_target_pairs={{0,2},{1,3},{2,0},{3,1},{4,6},{5,7},{6,4},{7,5},{8,10},{9,11},{10,... | collective-permute-start | bytes 835592 | tf_op jit(solution)/shard_map/ppermute | solution.py:268
  18.4 0.4 shard_map.75
  18.8 0.0 collective-permute-done.4.low_ref
  18.8 1.4 %shard_map.76.res_ref = bf16[4,2,384,256]{3,2,1,0:T(8,128)(2,1)S(1)} custom-call(bf16[1,2,384,1024]{3,2,1,0:T(8,128)(2,1)S(1)} %copy-done, bf16[2,32,1024]{2,1,0:T(8,128)(2,1)S(1)} %collective-permute-done.4.low_ref, bf16[2,32,1024]{2,1,0:T(8,128)(2,1)S(1)} %collective-permute-done.5.high_ref, bf16[128,192]{1,0:T(8,128)(2,1)S(1)} %get-tuple-element.10.az_ref, ...), custom_call_target="tpu_custom_call" | custom-call | tf_op jit(solution)/shard_map/pallas_call | solution.py:251
  20.2 3.9 %collective-permute-done.3.three_ref = bf16[2,128,256]{2,1,0:T(8,128)(2,1)S(1)} collective-permute-done((bf16[2,128,256]{2,1,0:T(8,128)(2,1)S(1)}, bf16[2,128,256]{2,1,0:T(8,128)(2,1)S(1)}, u32[]{:S(2)}, u32[]{:S(2)}) %collective-permute-start.3) | collective-permute-done | bytes 131104 | tf_op jit(solution)/shard_map/ppermute | solution.py:268
  24.1 0.5 %shard_map.77 = (bf16[2,64,1024]{2,1,0:T(8,128)(2,1)S(1)}, bf16[2,64,1024]{2,1,0:T(8,128)(2,1)S(1)}, f32[2,64,128]{2,1,0:T(8,128)S(1)}) custom-call(bf16[2,384,256]{2,1,0:T(8,128)(2,1)S(1)} %copy-done.1, bf16[2,128,256]{2,1,0:T(8,128)(2,1)S(1)} %collective-permute-done.2.refs_0_.one_ref, ...), custom_call_target="tpu_custom_call" | custom-call | tf_op jit(solution)/shard_map/pallas_call | solution.py:251
  24.7 0.1 collective-permute-start.6
  24.7 0.8 %slice_convert_fusion = f32[64]{0:T(128)S(1)} fusion(s32[384]{0:T(512)} %param.9), kind=kLoop, calls=%fused_computation.3 | loop fusion | flops 64 | bytes 512 | tf_op jit(solution)/shard_map/convert_element_type | solution.py:304
  25.5 3.1 %collective-permute-done.6.later_ref = bf16[2,64,1024]{2,1,0:T(8,128)(2,1)S(1)} collective-permute-done((bf16[2,64,1024]{2,1,0:T(8,128)(2,1)S(1)}, bf16[2,64,1024]{2,1,0:T(8,128)(2,1)S(1)}, u32[]{:S(2)}, u32[]{:S(2)}) %collective-permute-start.6) | collective-permute-done | bytes 262176 | tf_op jit(solution)/shard_map/ppermute | solution.py:264
  28.6 0.1 broadcast_in_dim.2.weight_ref
  28.7 0.4 shard_map.78.mine_ref
  29.1 1.9 %collective-permute-start.7 = (f32[8,128]{1,0:T(8,128)S(1)}, f32[8,128]{1,0:T(8,128)S(1)}, u32[]{:S(2)}, u32[]{:S(2)}) collective-permute-start(f32[8,128]{1,0:T(8,128)S(1)} %shard_map.78.mine_ref), channel_id=1, source_target_pairs={{0,4},{4,0},{8,12},{12,8},{16,20},{20,16},{24,28},{28,24},{1,5},{5... | collective-permute-start | bytes 12296 | tf_op jit(solution)/shard_map/ppermute | solution.py:268
  30.9 0.8 %collective-permute-done.7.refs_0_.other_ref = f32[8,128]{1,0:T(8,128)S(1)} collective-permute-done((f32[8,128]{1,0:T(8,128)S(1)}, f32[8,128]{1,0:T(8,128)S(1)}, u32[]{:S(2)}, u32[]{:S(2)}) %collective-permute-start.7) | collective-permute-done | bytes 4128 | tf_op jit(solution)/shard_map/ppermute | solution.py:268
  31.8 1.5 %collective-permute-start.10 = (f32[8,128]{1,0:T(8,128)S(1)}, f32[8,128]{1,0:T(8,128)S(1)}, u32[]{:S(2)}, u32[]{:S(2)}) collective-permute-start(f32[8,128]{1,0:T(8,128)S(1)} %shard_map.81), channel_id=1, source_target_pairs={{0,8},{4,12},{8,0},{12,4},{16,24},{20,28},{24,16},{28,20},{1,9},{5... | collective-permute-start | bytes 12296 | tf_op jit(solution)/shard_map/ppermute | solution.py:268
  33.3 0.1 collective-permute-start.8
  33.4 2.0 %collective-permute-done.10 = f32[8,128]{1,0:T(8,128)S(1)} collective-permute-done((f32[8,128]{1,0:T(8,128)S(1)}, f32[8,128]{1,0:T(8,128)S(1)}, u32[]{:S(2)}, u32[]{:S(2)}) %collective-permute-start.10) | collective-permute-done | bytes 4128 | tf_op jit(solution)/shard_map/ppermute | solution.py:268
  35.4 1.5 %collective-permute-start.11 = (f32[8,128]{1,0:T(8,128)S(1)}, f32[8,128]{1,0:T(8,128)S(1)}, u32[]{:S(2)}, u32[]{:S(2)}) collective-permute-start(f32[8,128]{1,0:T(8,128)S(1)} %add.3.mine_ref), channel_id=1, source_target_pairs={{0,16},{4,20},{8,24},{12,28},{16,0},{20,4},{24,8},{28,12},{1,17},{... | collective-permute-start | bytes 12296 | tf_op jit(solution)/shard_map/ppermute | solution.py:268
  36.9 0.6 %shard_map.80.before_ref = f32[2,256,128]{2,1,0:T(8,128)S(1)} custom-call(bf16[2,384,256]{2,1,0:T(8,128)(2,1)S(1)} %copy-done.1, bf16[2,272,256]{2,1,0:T(8,128)(2,1)S(1)} %collective-permute-done.9.one_ref.refs_0_, bf16[2,272,256]{2,1,0:T(8,128)(2,1)S(1)} %collective-permute-done.1.block_ref.two_ref, bf16[4,2,384,256]{3,2,1,0:T(8,128)(2,1)S(1)} %shard_map.76.res_ref), custom_call_target="tpu_custom_call" | custom-call | flops 3000000000 | bytes 3145728 | tf_op jit(solution)/shard_map/pallas_call | solution.py:251
  37.5 1.5 %collective-permute-done.11.other_ref = f32[8,128]{1,0:T(8,128)S(1)} collective-permute-done((f32[8,128]{1,0:T(8,128)S(1)}, f32[8,128]{1,0:T(8,128)S(1)}, u32[]{:S(2)}, u32[]{:S(2)}) %collective-permute-start.11) | collective-permute-done | bytes 4128 | tf_op jit(solution)/shard_map/ppermute | solution.py:268
  39.0 0.1 shard_map.82.unit_ref
  39.1 2.5 %collective-permute-done.8.three_ref = bf16[2,256,256]{2,1,0:T(8,128)(2,1)S(1)} collective-permute-done((bf16[2,256,256]{2,1,0:T(8,128)(2,1)S(1)}, bf16[2,256,256]{2,1,0:T(8,128)(2,1)S(1)}, u32[]{:S(2)}, u32[]{:S(2)}) %collective-permute-start.8) | collective-permute-done | bytes 262176 | tf_op jit(solution)/shard_map/ppermute | solution.py:268
  41.6 1.0 %shard_map.83 = f32[1,2,192,128]{3,2,1,0:T(8,128)} custom-call(bf16[2,256,256]{2,1,0:T(8,128)(2,1)S(1)} %collective-permute-done.8.three_ref, bf16[4,2,384,256]{3,2,1,0:T(8,128)(2,1)S(1)} %shard_map.76.res_ref, f32[2,256,128]{2,1,0:T(8,128)S(1)} %shard_map.80.before_ref, f32[2,64,128]{2,1,0:T(8,128)S(1)} %get-tuple-element.14.looks_ref, ...), custom_call_target="tpu_custom_call" | custom-call | flops 67108864 | bytes 1572864 | tf_op jit(solution)/shard_map/pallas_call | solution.py:251
  (13 shorter events, 0.1 us)
Async XLA Ops:
  0.0 13.3 %copy-start.1 = (bf16[2,384,256]{2,1,0:T(8,128)(2,1)S(1)}, bf16[2,384,256]{2,1,0:T(8,128)(2,1)}, u32[]{:S(2)}) copy-start(bf16[2,384,256]{2,1,0:T(8,128)(2,1)} %own_ref.3) | copy-start | bytes 1179652
  0.0 18.8 %copy-start = (bf16[1,2,384,1024]{3,2,1,0:T(8,128)(2,1)S(1)}, bf16[1,2,384,1024]{3,2,1,0:T(8,128)(2,1)}, u32[]{:S(2)}) copy-start(bf16[1,2,384,1024]{3,2,1,0:T(8,128)(2,1)} %sec_ref.1) | copy-start | bytes 4718596
  1.0 10.5 %collective-permute-start = (bf16[2,128,256]{2,1,0:T(8,128)(2,1)S(1)}, bf16[2,128,256]{2,1,0:T(8,128)(2,1)S(1)}, u32[]{:S(2)}, u32[]{:S(2)}) collective-permute-start(bf16[2,128,256]{2,1,0:T(8,128)(2,1)S(1)} %pad_maximum_fusion), channel_id=1, source_target_pairs={{0,2},{1,3},{2,0},{3,1},{4,6},{5,7},{6,4},{7,5},{8,10},{9,11},{10,... | collective-permute-start | bytes 393224 | tf_op jit(solution)/shard_map/ppermute | solution.py:268
  5.2 6.6 %collective-permute-start.2 = (bf16[2,128,256]{2,1,0:T(8,128)(2,1)S(1)}, bf16[2,128,256]{2,1,0:T(8,128)(2,1)S(1)}, u32[]{:S(2)}, u32[]{:S(2)}) collective-permute-start(bf16[2,128,256]{2,1,0:T(8,128)(2,1)S(1)} %pad_maximum_fusion), channel_id=1, source_target_pairs={{0,1},{1,0},{2,3},{3,2},{4,5},{5,4},{6,7},{7,6},{8,9},{9,8},{10,11... | collective-permute-start | bytes 393224 | tf_op jit(solution)/shard_map/ppermute | solution.py:268
  7.7 11.1 %collective-permute-start.4 = (bf16[2,32,1024]{2,1,0:T(8,128)(2,1)S(1)}, bf16[2,32,1024]{2,1,0:T(8,128)(2,1)S(1)}, u32[]{:S(2)}, u32[]{:S(2)}) collective-permute-start(bf16[2,32,1024]{2,1,0:T(8,128)(2,1)S(1)} %get-tuple-element.16), channel_id=1, source_target_pairs={{0,4},{4,8},{8,12},{12,16},{16,20},{20,24},{24,28},{28,0},{1,5},{5... | collective-permute-start | bytes 393224 | tf_op jit(solution)/shard_map/ppermute | solution.py:264
  7.8 11.0 %collective-permute-start.5 = (bf16[2,32,1024]{2,1,0:T(8,128)(2,1)S(1)}, bf16[2,32,1024]{2,1,0:T(8,128)(2,1)S(1)}, u32[]{:S(2)}, u32[]{:S(2)}) collective-permute-start(bf16[2,32,1024]{2,1,0:T(8,128)(2,1)S(1)} %get-tuple-element.15), channel_id=1, source_target_pairs={{0,28},{4,0},{8,4},{12,8},{16,12},{20,16},{24,20},{28,24},{1,29},{... | collective-permute-start | bytes 393224 | tf_op jit(solution)/shard_map/ppermute | solution.py:264
  11.8 12.4 %collective-permute-start.3 = (bf16[2,128,256]{2,1,0:T(8,128)(2,1)S(1)}, bf16[2,128,256]{2,1,0:T(8,128)(2,1)S(1)}, u32[]{:S(2)}, u32[]{:S(2)}) collective-permute-start(bf16[2,128,256]{2,1,0:T(8,128)(2,1)S(1)} %shard_map.74), channel_id=1, source_target_pairs={{0,1},{1,0},{2,3},{3,2},{4,5},{5,4},{6,7},{7,6},{8,9},{9,8},{10,11... | collective-permute-start | bytes 393224 | tf_op jit(solution)/shard_map/ppermute | solution.py:268
  13.3 17.6 %collective-permute-start.9 = (bf16[2,272,256]{2,1,0:T(8,128)(2,1)S(1)}, bf16[2,272,256]{2,1,0:T(8,128)(2,1)S(1)}, u32[]{:S(2)}, u32[]{:S(2)}) collective-permute-start(bf16[2,272,256]{2,1,0:T(8,128)(2,1)S(1)} %shard_map.73), channel_id=1, source_target_pairs={{0,1},{1,0},{2,3},{3,2},{4,5},{5,4},{6,7},{7,6},{8,9},{9,8},{10,11... | collective-permute-start | bytes 835592 | tf_op jit(solution)/shard_map/ppermute | solution.py:268
  14.0 19.3 %collective-permute-start.1 = (bf16[2,272,256]{2,1,0:T(8,128)(2,1)S(1)}, bf16[2,272,256]{2,1,0:T(8,128)(2,1)S(1)}, u32[]{:S(2)}, u32[]{:S(2)}) collective-permute-start(bf16[2,272,256]{2,1,0:T(8,128)(2,1)S(1)} %shard_map.73), channel_id=1, source_target_pairs={{0,2},{1,3},{2,0},{3,1},{4,6},{5,7},{6,4},{7,5},{8,10},{9,11},{10,... | collective-permute-start | bytes 835592 | tf_op jit(solution)/shard_map/ppermute | solution.py:268
  24.7 3.9 %collective-permute-start.6 = (bf16[2,64,1024]{2,1,0:T(8,128)(2,1)S(1)}, bf16[2,64,1024]{2,1,0:T(8,128)(2,1)S(1)}, u32[]{:S(2)}, u32[]{:S(2)}) collective-permute-start(bf16[2,64,1024]{2,1,0:T(8,128)(2,1)S(1)} %get-tuple-element.13), channel_id=1, source_target_pairs={{0,28},{4,0},{8,4},{12,8},{16,12},{20,16},{24,20},{28,24},{1,29},{... | collective-permute-start | bytes 786440 | tf_op jit(solution)/shard_map/ppermute | solution.py:264
  29.1 2.7 %collective-permute-start.7 = (f32[8,128]{1,0:T(8,128)S(1)}, f32[8,128]{1,0:T(8,128)S(1)}, u32[]{:S(2)}, u32[]{:S(2)}) collective-permute-start(f32[8,128]{1,0:T(8,128)S(1)} %shard_map.78.mine_ref), channel_id=1, source_target_pairs={{0,4},{4,0},{8,12},{12,8},{16,20},{20,16},{24,28},{28,24},{1,5},{5... | collective-permute-start | bytes 12296 | tf_op jit(solution)/shard_map/ppermute | solution.py:268
  31.8 3.6 %collective-permute-start.10 = (f32[8,128]{1,0:T(8,128)S(1)}, f32[8,128]{1,0:T(8,128)S(1)}, u32[]{:S(2)}, u32[]{:S(2)}) collective-permute-start(f32[8,128]{1,0:T(8,128)S(1)} %shard_map.81), channel_id=1, source_target_pairs={{0,8},{4,12},{8,0},{12,4},{16,24},{20,28},{24,16},{28,20},{1,9},{5... | collective-permute-start | bytes 12296 | tf_op jit(solution)/shard_map/ppermute | solution.py:268
  33.3 8.3 %collective-permute-start.8 = (bf16[2,256,256]{2,1,0:T(8,128)(2,1)S(1)}, bf16[2,256,256]{2,1,0:T(8,128)(2,1)S(1)}, u32[]{:S(2)}, u32[]{:S(2)}) collective-permute-start(bf16[2,256,256]{2,1,0:T(8,128)(2,1)S(1)} %shard_map.79), channel_id=1, source_target_pairs={{0,1},{1,0},{2,3},{3,2},{4,5},{5,4},{6,7},{7,6},{8,9},{9,8},{10,11... | collective-permute-start | bytes 786440 | tf_op jit(solution)/shard_map/ppermute | solution.py:268
  35.4 3.6 %collective-permute-start.11 = (f32[8,128]{1,0:T(8,128)S(1)}, f32[8,128]{1,0:T(8,128)S(1)}, u32[]{:S(2)}, u32[]{:S(2)}) collective-permute-start(f32[8,128]{1,0:T(8,128)S(1)} %add.3.mine_ref), channel_id=1, source_target_pairs={{0,16},{4,20},{8,24},{12,28},{16,0},{20,4},{24,8},{28,12},{1,17},{... | collective-permute-start | bytes 12296 | tf_op jit(solution)/shard_map/ppermute | solution.py:268

commit v21 on v18

--- a/solution.py
+++ b/solution.py
@@ -42,12 +42,6 @@
     return total.astype(jnp.bfloat16)
 
 
-def cut_halo_kernel(sec_ref, down_ref, up_ref):
-    rows_n = sec_ref.shape[2]
-    down_ref[...] = sec_ref[0, :, rows_n - HALO :]
-    up_ref[...] = sec_ref[0, :, :HALO]
-
-
 def cut_middle_kernel(prim_ref, *refs):
     cut_ref = refs[-1]
     cut_ref[...] = prim_ref[:, LAG : LAG + cut_ref.shape[1]]
@@ -58,15 +52,18 @@
     out_ref[...] = block_ref[:, : out_ref.shape[1]]
 
 
-def bands_kernel(ao_ref, ro_ref, af_ref, rf_ref, az_ref, rg_ref):
-    shape = az_ref.shape
+def azimuth_kernel(off_ref, frac_ref, out_ref):
+    shape = out_ref.shape
     offset = lax.broadcasted_iota(jnp.int32, shape, 1) - lax.broadcasted_iota(jnp.int32, shape, 0)
-    az_ref[...] = band(shape, offset - HALO - ao_ref[...], tap_rows(af_ref[...]))
-    square = rg_ref.shape[1:]
+    out_ref[...] = band(shape, offset - HALO - off_ref[...], tap_rows(frac_ref[...]))
+
+
+def range_kernel(off_ref, frac_ref, out_ref):
+    square = out_ref.shape[1:]
     offset = lax.broadcasted_iota(jnp.int32, square, 0) - lax.broadcasted_iota(jnp.int32, square, 1)
-    taps = tap_rows(rf_ref[...])
+    taps = tap_rows(frac_ref[...])
     for at, shift in enumerate((-LANE, 0, LANE)):
-        rg_ref[at] = band(square, offset + shift - ro_ref[...], taps)
+        out_ref[at] = band(square, offset + shift - off_ref[...], taps)
 
 
 def resample_kernel(sec_ref, low_ref, high_ref, az_ref, rg_ref, out_ref, azim_ref):
@@ -276,19 +273,15 @@
     edges = jnp.concatenate([primary[:, :LAG], primary[:, rows_n - LAG :]], axis=1)
     edges_two = swap(edges, "date", 2)
     edges_one = swap(edges, "date", 1)
-    halo = shape((2, HALO, cols_n), bf16)
-    down, up = call(cut_halo_kernel, (halo, halo), [], (0, 0), secondary)
+    down, up = secondary[0, :, rows_n - HALO :], secondary[0, :, :HALO]
     low = ring(down, "tile", 1)
     high = ring(up, "tile", -1)
-    az_band, rg_band = call(
-        bands_kernel,
-        (shape((BAND, BAND + 2 * HALO), bf16), shape((3, LANE, LANE), bf16)),
-        [],
-        (0, 0),
-        az_off, rg_off, az_frac, rg_frac,
-    )
+    az_band = call(
+        azimuth_kernel, shape((BAND, BAND + 2 * HALO), bf16), [], (0, 0), az_off, az_frac
+    )
+    rg_band = call(range_kernel, shape((3, LANE, LANE), bf16), [], (0, 0), rg_off, rg_frac)
     passed = call(
-        relay_kernel, shape(edges.shape, bf16), [], (0, 0), edges_two, edges_one
+        relay_kernel, shape(edges.shape, bf16), [], (0, 0), edges_two, edges_one, az_band
     )
     edges_three = swap(passed, "date", 1)
     middle = call(

time: 38.8 us -> 38.9 us (level)
  waiting for transfers between devices: 9.2 us -> 10.2 us
  starting transfers between devices: 19.1 us -> 18.4 us
    unnamed x6 -> x4, local copies, waits for them, and re-layouts: 1.41 us -> 0.01 us
    ppermute x3, starting transfers between devices: 4.25 us -> 3.01 us  [ring(): lax.ppermute(value, axis, [(at, (at + step) % count) for at in range(coun...]
    squeeze x0 -> x1, local copies, waits for them, and re-layouts: none -> 0.99 us  [fused(): down, up = (secondary[0, :, rows_n - HALO:], secondary[0, :, :HALO])]
    ppermute x9, waiting for transfers between devices: 6.06 us -> 7.03 us  [swap(): lax.ppermute(value, axis, [(at, at ^ step) for at in range(lax.axis_size(...]
    ppermute x9, starting transfers between devices: 14.8 us -> 15.4 us  [swap(): lax.ppermute(value, axis, [(at, at ^ step) for at in range(lax.axis_size(...]
  transfers between devices with their start and end apart: 12 -> 12, of which waited for: 7 -> 6; matrix products, arithmetic and copies ran while one was open for 2% -> 5% of each run, Pallas kernels for 9% -> 9%
where the time goes in v21:
time: 38.9 us; the launch traced here: 38.7 us
  starting transfers between devices  18.4 us (47%)
  waiting for transfers between devices  10.2 us (26%)
  Pallas kernels  4.47 us (11%)
  between operations  2.73 us (7%)
  local copies, waits for them, and re-layouts  2.09 us (5%)
  other arithmetic  0.77 us (2%)
    ppermute x9, starting transfers between devices, swap(): lax.ppermute(value, axis, [(at, at ^ step) for at in range(lax.axis_size(...  15.4 us
    ppermute x9, waiting for transfers between devices, swap(): lax.ppermute(value, axis, [(at, at ^ step) for at in range(lax.axis_size(...  7.03 us
    pallas_call x11, Pallas kernels, call(): pl.pallas_call(kernel, out_shape=outs, in_specs=[vmem] * len(args), out_s...  4.47 us
    ppermute x3, waiting for transfers between devices, ring(): lax.ppermute(value, axis, [(at, (at + step) % count) for at in range(coun...  3.14 us
    ppermute x3, starting transfers between devices, ring(): lax.ppermute(value, axis, [(at, (at + step) % count) for at in range(coun...  3.01 us
    slice x1, local copies, waits for them, and re-layouts, fused(): primary[:, :LAG]  1.02 us
    squeeze x1, local copies, waits for them, and re-layouts, fused(): down, up = (secondary[0, :, rows_n - HALO:], secondary[0, :, :HALO])  0.99 us
  transfers between devices with their start and end apart: 12, of which 6 were waited for; matrix products, arithmetic and copies ran while one was open for 5% of the time, Pallas kernels for 9%

profile of v21, /device:TPU:0, one launch (start us, length us, event | category | flops | bytes accessed | tf_op | source)
XLA Modules:
  0.0 38.7 jit_solution(8143805502100827973)
XLA Ops:
  0.0 1.0 %fusion = (bf16[2,64,256]{2,1,0:T(8,128)(2,1)S(1)}, bf16[2,64,256]{2,1,0:T(8,128)(2,1)S(1)}) fusion(bf16[2,384,256]{2,1,0:T(8,128)(2,1)} %own_ref.3), kind=kLoop, calls=%fused_computation.4 | loop fusion | bytes 262144 | tf_op jit(solution)/shard_map/slice | solution.py:273
  1.0 4.1 %collective-permute-start = (bf16[2,128,256]{2,1,0:T(8,128)(2,1)S(1)}, bf16[2,128,256]{2,1,0:T(8,128)(2,1)S(1)}, u32[]{:S(2)}, u32[]{:S(2)}) collective-permute-start(bf16[2,128,256]{2,1,0:T(8,128)(2,1)S(1)} %pad_maximum_fusion), channel_id=1, source_target_pairs={{0,2},{1,3},{2,0},{3,1},{4,6},{5,7},{6,4},{7,5},{8,10},{9,11},{10,... | collective-permute-start | bytes 393224 | tf_op jit(solution)/shard_map/ppermute | solution.py:261
  5.2 1.6 %collective-permute-start.2 = (bf16[2,128,256]{2,1,0:T(8,128)(2,1)S(1)}, bf16[2,128,256]{2,1,0:T(8,128)(2,1)S(1)}, u32[]{:S(2)}, u32[]{:S(2)}) collective-permute-start(bf16[2,128,256]{2,1,0:T(8,128)(2,1)S(1)} %pad_maximum_fusion), channel_id=1, source_target_pairs={{0,1},{1,0},{2,3},{3,2},{4,5},{5,4},{6,7},{7,6},{8,9},{9,8},{10,11... | collective-permute-start | bytes 393224 | tf_op jit(solution)/shard_map/ppermute | solution.py:261
  6.7 1.0 %slice_bitcast_fusion = (bf16[2,32,1024]{2,1,0:T(8,128)(2,1)S(1)}, bf16[2,32,1024]{2,1,0:T(8,128)(2,1)S(1)}) fusion(bf16[1,2,384,1024]{3,2,1,0:T(8,128)(2,1)} %sec_ref.1), kind=kLoop, calls=%fused_computation.1 | loop fusion | bytes 524288 | tf_op jit(solution)/shard_map/squeeze | solution.py:276
  7.7 0.1 collective-permute-start.4
  7.8 2.6 %collective-permute-start.5 = (bf16[2,32,1024]{2,1,0:T(8,128)(2,1)S(1)}, bf16[2,32,1024]{2,1,0:T(8,128)(2,1)S(1)}, u32[]{:S(2)}, u32[]{:S(2)}) collective-permute-start(bf16[2,32,1024]{2,1,0:T(8,128)(2,1)S(1)} %get-tuple-element.11), channel_id=1, source_target_pairs={{0,28},{4,0},{8,4},{12,8},{16,12},{20,16},{24,20},{28,24},{1,29},{... | collective-permute-start | bytes 393224 | tf_op jit(solution)/shard_map/ppermute | solution.py:257
  11.7 0.2 shard_map.74.refs_1_.az_ref
  11.9 0.0 collective-permute-done.refs_0_.block_ref.two_ref
  11.9 0.0 collective-permute-done.2.refs_0_.one_ref
  12.0 1.3 %collective-permute-start.3 = (bf16[2,128,256]{2,1,0:T(8,128)(2,1)S(1)}, bf16[2,128,256]{2,1,0:T(8,128)(2,1)S(1)}, u32[]{:S(2)}, u32[]{:S(2)}) collective-permute-start(bf16[2,128,256]{2,1,0:T(8,128)(2,1)S(1)} %shard_map.75), channel_id=1, source_target_pairs={{0,1},{1,0},{2,3},{3,2},{4,5},{5,4},{6,7},{7,6},{8,9},{9,8},{10,11... | collective-permute-start | bytes 393224 | tf_op jit(solution)/shard_map/ppermute | solution.py:261
  13.3 2.4 %collective-permute-start.1 = (bf16[2,272,256]{2,1,0:T(8,128)(2,1)S(1)}, bf16[2,272,256]{2,1,0:T(8,128)(2,1)S(1)}, u32[]{:S(2)}, u32[]{:S(2)}) collective-permute-start(bf16[2,272,256]{2,1,0:T(8,128)(2,1)S(1)} %shard_map.73), channel_id=1, source_target_pairs={{0,2},{1,3},{2,0},{3,1},{4,6},{5,7},{6,4},{7,5},{8,10},{9,11},{10,... | collective-permute-start | bytes 835592 | tf_op jit(solution)/shard_map/ppermute | solution.py:261
  15.7 0.0 collective-permute-start.8
  17.1 0.2 shard_map.76.rg_ref
  17.3 1.4 %shard_map.77.res_ref = bf16[4,2,384,256]{3,2,1,0:T(8,128)(2,1)S(1)} custom-call(bf16[1,2,384,1024]{3,2,1,0:T(8,128)(2,1)S(1)} %copy-done.1, bf16[2,32,1024]{2,1,0:T(8,128)(2,1)S(1)} %collective-permute-done.4.low_ref, bf16[2,32,1024]{2,1,0:T(8,128)(2,1)S(1)} %collective-permute-done.5.high_ref, bf16[128,192]{1,0:T(8,128)(2,1)S(1)} %shard_map.74.refs_1_.az_ref, ...), custom_call_target="tpu_custom_call" | custom-call | tf_op jit(solution)/shard_map/pallas_call | solution.py:244
  18.7 1.3 %collective-permute-done.3.three_ref = bf16[2,128,256]{2,1,0:T(8,128)(2,1)S(1)} collective-permute-done((bf16[2,128,256]{2,1,0:T(8,128)(2,1)S(1)}, bf16[2,128,256]{2,1,0:T(8,128)(2,1)S(1)}, u32[]{:S(2)}, u32[]{:S(2)}) %collective-permute-start.3) | collective-permute-done | bytes 131104 | tf_op jit(solution)/shard_map/ppermute | solution.py:261
  20.0 0.5 %shard_map.78 = (bf16[2,64,1024]{2,1,0:T(8,128)(2,1)S(1)}, bf16[2,64,1024]{2,1,0:T(8,128)(2,1)S(1)}, f32[2,64,128]{2,1,0:T(8,128)S(1)}) custom-call(bf16[2,384,256]{2,1,0:T(8,128)(2,1)S(1)} %copy-done, bf16[2,128,256]{2,1,0:T(8,128)(2,1)S(1)} %collective-permute-done.2.refs_0_.one_ref, ...), custom_call_target="tpu_custom_call" | custom-call | tf_op jit(solution)/shard_map/pallas_call | solution.py:244
  20.5 0.3 collective-permute-start.6
  20.8 0.8 %slice_convert_fusion = f32[64]{0:T(128)S(1)} fusion(s32[384]{0:T(512)} %param.9), kind=kLoop, calls=%fused_computation.3 | loop fusion | flops 64 | bytes 512 | tf_op jit(solution)/shard_map/convert_element_type | solution.py:294
  21.6 3.1 %collective-permute-done.6.later_ref = bf16[2,64,1024]{2,1,0:T(8,128)(2,1)S(1)} collective-permute-done((bf16[2,64,1024]{2,1,0:T(8,128)(2,1)S(1)}, bf16[2,64,1024]{2,1,0:T(8,128)(2,1)S(1)}, u32[]{:S(2)}, u32[]{:S(2)}) %collective-permute-start.6) | collective-permute-done | bytes 262176 | tf_op jit(solution)/shard_map/ppermute | solution.py:257
  24.7 0.1 broadcast_in_dim.2.weight_ref
  24.8 0.4 shard_map.79
  25.2 1.6 %collective-permute-start.7 = (f32[8,128]{1,0:T(8,128)S(1)}, f32[8,128]{1,0:T(8,128)S(1)}, u32[]{:S(2)}, u32[]{:S(2)}) collective-permute-start(f32[8,128]{1,0:T(8,128)S(1)} %shard_map.79), channel_id=1, source_target_pairs={{0,4},{4,0},{8,12},{12,8},{16,20},{20,16},{24,28},{28,24},{1,5},{5... | collective-permute-start | bytes 12296 | tf_op jit(solution)/shard_map/ppermute | solution.py:261
  26.8 1.6 %collective-permute-done.1.block_ref.two_ref = bf16[2,272,256]{2,1,0:T(8,128)(2,1)S(1)} collective-permute-done((bf16[2,272,256]{2,1,0:T(8,128)(2,1)S(1)}, bf16[2,272,256]{2,1,0:T(8,128)(2,1)S(1)}, u32[]{:S(2)}, u32[]{:S(2)}) %collective-permute-start.1) | collective-permute-done | bytes 278560 | tf_op jit(solution)/shard_map/ppermute | solution.py:261
  28.4 0.5 %collective-permute-done.8.refs_1_.one_ref = bf16[2,272,256]{2,1,0:T(8,128)(2,1)S(1)} collective-permute-done((bf16[2,272,256]{2,1,0:T(8,128)(2,1)S(1)}, bf16[2,272,256]{2,1,0:T(8,128)(2,1)S(1)}, u32[]{:S(2)}, u32[]{:S(2)}) %collective-permute-start.8) | collective-permute-done | bytes 278560 | tf_op jit(solution)/shard_map/ppermute | solution.py:261
  29.0 1.4 %collective-permute-start.9 = (bf16[2,256,256]{2,1,0:T(8,128)(2,1)S(1)}, bf16[2,256,256]{2,1,0:T(8,128)(2,1)S(1)}, u32[]{:S(2)}, u32[]{:S(2)}) collective-permute-start(bf16[2,256,256]{2,1,0:T(8,128)(2,1)S(1)} %shard_map.80), channel_id=1, source_target_pairs={{0,1},{1,0},{2,3},{3,2},{4,5},{5,4},{6,7},{7,6},{8,9},{9,8},{10,11... | collective-permute-start | bytes 786440 | tf_op jit(solution)/shard_map/ppermute | solution.py:261
  30.3 1.5 %collective-permute-start.10 = (f32[8,128]{1,0:T(8,128)S(1)}, f32[8,128]{1,0:T(8,128)S(1)}, u32[]{:S(2)}, u32[]{:S(2)}) collective-permute-start(f32[8,128]{1,0:T(8,128)S(1)} %add.6), channel_id=1, source_target_pairs={{0,8},{4,12},{8,0},{12,4},{16,24},{20,28},{24,16},{28,20},{1,9},{5... | collective-permute-start | bytes 12296 | tf_op jit(solution)/shard_map/ppermute | solution.py:261
  31.8 2.1 %collective-permute-done.10 = f32[8,128]{1,0:T(8,128)S(1)} collective-permute-done((f32[8,128]{1,0:T(8,128)S(1)}, f32[8,128]{1,0:T(8,128)S(1)}, u32[]{:S(2)}, u32[]{:S(2)}) %collective-permute-start.10) | collective-permute-done | bytes 4128 | tf_op jit(solution)/shard_map/ppermute | solution.py:261
  33.9 1.5 %collective-permute-start.11 = (f32[8,128]{1,0:T(8,128)S(1)}, f32[8,128]{1,0:T(8,128)S(1)}, u32[]{:S(2)}, u32[]{:S(2)}) collective-permute-start(f32[8,128]{1,0:T(8,128)S(1)} %add.7.mine_ref), channel_id=1, source_target_pairs={{0,16},{4,20},{8,24},{12,28},{16,0},{20,4},{24,8},{28,12},{1,17},{... | collective-permute-start | bytes 12296 | tf_op jit(solution)/shard_map/ppermute | solution.py:261
  35.5 0.6 %shard_map.81.before_ref = f32[2,256,128]{2,1,0:T(8,128)S(1)} custom-call(bf16[2,384,256]{2,1,0:T(8,128)(2,1)S(1)} %copy-done, bf16[2,272,256]{2,1,0:T(8,128)(2,1)S(1)} %collective-permute-done.8.refs_1_.one_ref, bf16[2,272,256]{2,1,0:T(8,128)(2,1)S(1)} %collective-permute-done.1.block_ref.two_ref, bf16[4,2,384,256]{3,2,1,0:T(8,128)(2,1)S(1)} %shard_map.77.res_ref), custom_call_target="tpu_custom_call" | custom-call | flops 134217728 | bytes 3145728 | tf_op jit(solution)/shard_map/pallas_call | solution.py:244
  36.1 1.5 %collective-permute-done.11.other_ref = f32[8,128]{1,0:T(8,128)S(1)} collective-permute-done((f32[8,128]{1,0:T(8,128)S(1)}, f32[8,128]{1,0:T(8,128)S(1)}, u32[]{:S(2)}, u32[]{:S(2)}) %collective-permute-start.11) | collective-permute-done | bytes 4128 | tf_op jit(solution)/shard_map/ppermute | solution.py:261
  37.5 0.1 shard_map.82.unit_ref
  37.7 1.0 %shard_map.83 = f32[1,2,192,128]{3,2,1,0:T(8,128)} custom-call(bf16[2,256,256]{2,1,0:T(8,128)(2,1)S(1)} %collective-permute-done.9.three_ref, bf16[4,2,384,256]{3,2,1,0:T(8,128)(2,1)S(1)} %shard_map.77.res_ref, f32[2,256,128]{2,1,0:T(8,128)S(1)} %shard_map.81.before_ref, f32[2,64,128]{2,1,0:T(8,128)S(1)} %get-tuple-element.10.looks_ref, ...), custom_call_target="tpu_custom_call" | custom-call | flops 67108864 | bytes 1572864 | tf_op jit(solution)/shard_map/pallas_call | solution.py:244
  (14 shorter events, 0.1 us)
Async XLA Ops:
  0.0 13.3 %copy-start = (bf16[2,384,256]{2,1,0:T(8,128)(2,1)S(1)}, bf16[2,384,256]{2,1,0:T(8,128)(2,1)}, u32[]{:S(2)}) copy-start(bf16[2,384,256]{2,1,0:T(8,128)(2,1)} %own_ref.3) | copy-start | bytes 1179652
  0.0 17.3 %copy-start.1 = (bf16[1,2,384,1024]{3,2,1,0:T(8,128)(2,1)S(1)}, bf16[1,2,384,1024]{3,2,1,0:T(8,128)(2,1)}, u32[]{:S(2)}) copy-start(bf16[1,2,384,1024]{3,2,1,0:T(8,128)(2,1)} %sec_ref.1) | copy-start | bytes 4718596
  1.0 10.9 %collective-permute-start = (bf16[2,128,256]{2,1,0:T(8,128)(2,1)S(1)}, bf16[2,128,256]{2,1,0:T(8,128)(2,1)S(1)}, u32[]{:S(2)}, u32[]{:S(2)}) collective-permute-start(bf16[2,128,256]{2,1,0:T(8,128)(2,1)S(1)} %pad_maximum_fusion), channel_id=1, source_target_pairs={{0,2},{1,3},{2,0},{3,1},{4,6},{5,7},{6,4},{7,5},{8,10},{9,11},{10,... | collective-permute-start | bytes 393224 | tf_op jit(solution)/shard_map/ppermute | solution.py:261
  5.2 6.8 %collective-permute-start.2 = (bf16[2,128,256]{2,1,0:T(8,128)(2,1)S(1)}, bf16[2,128,256]{2,1,0:T(8,128)(2,1)S(1)}, u32[]{:S(2)}, u32[]{:S(2)}) collective-permute-start(bf16[2,128,256]{2,1,0:T(8,128)(2,1)S(1)} %pad_maximum_fusion), channel_id=1, source_target_pairs={{0,1},{1,0},{2,3},{3,2},{4,5},{5,4},{6,7},{7,6},{8,9},{9,8},{10,11... | collective-permute-start | bytes 393224 | tf_op jit(solution)/shard_map/ppermute | solution.py:261
  7.7 9.6 %collective-permute-start.4 = (bf16[2,32,1024]{2,1,0:T(8,128)(2,1)S(1)}, bf16[2,32,1024]{2,1,0:T(8,128)(2,1)S(1)}, u32[]{:S(2)}, u32[]{:S(2)}) collective-permute-start(bf16[2,32,1024]{2,1,0:T(8,128)(2,1)S(1)} %get-tuple-element.12), channel_id=1, source_target_pairs={{0,4},{4,8},{8,12},{12,16},{16,20},{20,24},{24,28},{28,0},{1,5},{5... | collective-permute-start | bytes 393224 | tf_op jit(solution)/shard_map/ppermute | solution.py:257
  7.8 9.5 %collective-permute-start.5 = (bf16[2,32,1024]{2,1,0:T(8,128)(2,1)S(1)}, bf16[2,32,1024]{2,1,0:T(8,128)(2,1)S(1)}, u32[]{:S(2)}, u32[]{:S(2)}) collective-permute-start(bf16[2,32,1024]{2,1,0:T(8,128)(2,1)S(1)} %get-tuple-element.11), channel_id=1, source_target_pairs={{0,28},{4,0},{8,4},{12,8},{16,12},{20,16},{24,20},{28,24},{1,29},{... | collective-permute-start | bytes 393224 | tf_op jit(solution)/shard_map/ppermute | solution.py:257
  12.0 8.0 %collective-permute-start.3 = (bf16[2,128,256]{2,1,0:T(8,128)(2,1)S(1)}, bf16[2,128,256]{2,1,0:T(8,128)(2,1)S(1)}, u32[]{:S(2)}, u32[]{:S(2)}) collective-permute-start(bf16[2,128,256]{2,1,0:T(8,128)(2,1)S(1)} %shard_map.75), channel_id=1, source_target_pairs={{0,1},{1,0},{2,3},{3,2},{4,5},{5,4},{6,7},{7,6},{8,9},{9,8},{10,11... | collective-permute-start | bytes 393224 | tf_op jit(solution)/shard_map/ppermute | solution.py:261
  13.3 15.1 %collective-permute-start.1 = (bf16[2,272,256]{2,1,0:T(8,128)(2,1)S(1)}, bf16[2,272,256]{2,1,0:T(8,128)(2,1)S(1)}, u32[]{:S(2)}, u32[]{:S(2)}) collective-permute-start(bf16[2,272,256]{2,1,0:T(8,128)(2,1)S(1)} %shard_map.73), channel_id=1, source_target_pairs={{0,2},{1,3},{2,0},{3,1},{4,6},{5,7},{6,4},{7,5},{8,10},{9,11},{10,... | collective-permute-start | bytes 835592 | tf_op jit(solution)/shard_map/ppermute | solution.py:261
  15.7 13.2 %collective-permute-start.8 = (bf16[2,272,256]{2,1,0:T(8,128)(2,1)S(1)}, bf16[2,272,256]{2,1,0:T(8,128)(2,1)S(1)}, u32[]{:S(2)}, u32[]{:S(2)}) collective-permute-start(bf16[2,272,256]{2,1,0:T(8,128)(2,1)S(1)} %shard_map.73), channel_id=1, source_target_pairs={{0,1},{1,0},{2,3},{3,2},{4,5},{5,4},{6,7},{7,6},{8,9},{9,8},{10,11... | collective-permute-start | bytes 835592 | tf_op jit(solution)/shard_map/ppermute | solution.py:261
  20.5 4.2 %collective-permute-start.6 = (bf16[2,64,1024]{2,1,0:T(8,128)(2,1)S(1)}, bf16[2,64,1024]{2,1,0:T(8,128)(2,1)S(1)}, u32[]{:S(2)}, u32[]{:S(2)}) collective-permute-start(bf16[2,64,1024]{2,1,0:T(8,128)(2,1)S(1)} %get-tuple-element.9), channel_id=1, source_target_pairs={{0,28},{4,0},{8,4},{12,8},{16,12},{20,16},{24,20},{28,24},{1,29},{... | collective-permute-start | bytes 786440 | tf_op jit(solution)/shard_map/ppermute | solution.py:257
  25.2 3.8 %collective-permute-start.7 = (f32[8,128]{1,0:T(8,128)S(1)}, f32[8,128]{1,0:T(8,128)S(1)}, u32[]{:S(2)}, u32[]{:S(2)}) collective-permute-start(f32[8,128]{1,0:T(8,128)S(1)} %shard_map.79), channel_id=1, source_target_pairs={{0,4},{4,0},{8,12},{12,8},{16,20},{20,16},{24,28},{28,24},{1,5},{5... | collective-permute-start | bytes 12296 | tf_op jit(solution)/shard_map/ppermute | solution.py:261
  29.0 8.7 %collective-permute-start.9 = (bf16[2,256,256]{2,1,0:T(8,128)(2,1)S(1)}, bf16[2,256,256]{2,1,0:T(8,128)(2,1)S(1)}, u32[]{:S(2)}, u32[]{:S(2)}) collective-permute-start(bf16[2,256,256]{2,1,0:T(8,128)(2,1)S(1)} %shard_map.80), channel_id=1, source_target_pairs={{0,1},{1,0},{2,3},{3,2},{4,5},{5,4},{6,7},{7,6},{8,9},{9,8},{10,11... | collective-permute-start | bytes 786440 | tf_op jit(solution)/shard_map/ppermute | solution.py:261
  30.3 3.6 %collective-permute-start.10 = (f32[8,128]{1,0:T(8,128)S(1)}, f32[8,128]{1,0:T(8,128)S(1)}, u32[]{:S(2)}, u32[]{:S(2)}) collective-permute-start(f32[8,128]{1,0:T(8,128)S(1)} %add.6), channel_id=1, source_target_pairs={{0,8},{4,12},{8,0},{12,4},{16,24},{20,28},{24,16},{28,20},{1,9},{5... | collective-permute-start | bytes 12296 | tf_op jit(solution)/shard_map/ppermute | solution.py:261
  33.9 3.6 %collective-permute-start.11 = (f32[8,128]{1,0:T(8,128)S(1)}, f32[8,128]{1,0:T(8,128)S(1)}, u32[]{:S(2)}, u32[]{:S(2)}) collective-permute-start(f32[8,128]{1,0:T(8,128)S(1)} %add.7.mine_ref), channel_id=1, source_target_pairs={{0,16},{4,20},{8,24},{12,28},{16,0},{20,4},{24,8},{28,12},{1,17},{... | collective-permute-start | bytes 12296 | tf_op jit(solution)/shard_map/ppermute | solution.py:261

commit v22 on v21

--- a/solution.py
+++ b/solution.py
@@ -320,7 +320,7 @@
         middle_kernel,
         shape((2, middle_n, looks_n), f32),
         [],
-        (2 * 2 * middle_n * cols_n * looks_n, 8 * rows_n * cols_n),
+        (3 * 10**9, 8 * rows_n * cols_n),
         primary, one, two, res,
     )
     other = swap(stats, "tile", 1)

time: 38.9 us -> 38.9 us (level)
  no operation moved by 1% of the time
where the time goes in v22:
time: 38.9 us; the launch traced here: 38.7 us
  starting transfers between devices  18.3 us (47%)
  waiting for transfers between devices  10.3 us (26%)
  Pallas kernels  4.47 us (11%)
  between operations  2.73 us (7%)
  local copies, waits for them, and re-layouts  2.09 us (5%)
  other arithmetic  0.77 us (2%)
    ppermute x9, starting transfers between devices, swap(): lax.ppermute(value, axis, [(at, at ^ step) for at in range(lax.axis_size(...  15.3 us
    ppermute x9, waiting for transfers between devices, swap(): lax.ppermute(value, axis, [(at, at ^ step) for at in range(lax.axis_size(...  7.21 us
    pallas_call x11, Pallas kernels, call(): pl.pallas_call(kernel, out_shape=outs, in_specs=[vmem] * len(args), out_s...  4.47 us
    ppermute x3, waiting for transfers between devices, ring(): lax.ppermute(value, axis, [(at, (at + step) % count) for at in range(coun...  3.14 us
    ppermute x3, starting transfers between devices, ring(): lax.ppermute(value, axis, [(at, (at + step) % count) for at in range(coun...  3.01 us
    slice x1, local copies, waits for them, and re-layouts, fused(): primary[:, :LAG]  1.02 us
    squeeze x1, local copies, waits for them, and re-layouts, fused(): down, up = (secondary[0, :, rows_n - HALO:], secondary[0, :, :HALO])  0.99 us
  transfers between devices with their start and end apart: 12, of which 6 were waited for; matrix products, arithmetic and copies ran while one was open for 5% of the time, Pallas kernels for 9%

profile of v22, /device:TPU:0, one launch (start us, length us, event | category | flops | bytes accessed | tf_op | source)
XLA Modules:
  0.0 38.7 jit_solution(9125503781083334517)
XLA Ops:
  0.0 1.0 %fusion = (bf16[2,64,256]{2,1,0:T(8,128)(2,1)S(1)}, bf16[2,64,256]{2,1,0:T(8,128)(2,1)S(1)}) fusion(bf16[2,384,256]{2,1,0:T(8,128)(2,1)} %own_ref.3), kind=kLoop, calls=%fused_computation.4 | loop fusion | bytes 262144 | tf_op jit(solution)/shard_map/slice | solution.py:273
  1.0 4.1 %collective-permute-start = (bf16[2,128,256]{2,1,0:T(8,128)(2,1)S(1)}, bf16[2,128,256]{2,1,0:T(8,128)(2,1)S(1)}, u32[]{:S(2)}, u32[]{:S(2)}) collective-permute-start(bf16[2,128,256]{2,1,0:T(8,128)(2,1)S(1)} %pad_maximum_fusion), channel_id=1, source_target_pairs={{0,2},{1,3},{2,0},{3,1},{4,6},{5,7},{6,4},{7,5},{8,10},{9,11},{10,... | collective-permute-start | bytes 393224 | tf_op jit(solution)/shard_map/ppermute | solution.py:261
  5.2 1.6 %collective-permute-start.2 = (bf16[2,128,256]{2,1,0:T(8,128)(2,1)S(1)}, bf16[2,128,256]{2,1,0:T(8,128)(2,1)S(1)}, u32[]{:S(2)}, u32[]{:S(2)}) collective-permute-start(bf16[2,128,256]{2,1,0:T(8,128)(2,1)S(1)} %pad_maximum_fusion), channel_id=1, source_target_pairs={{0,1},{1,0},{2,3},{3,2},{4,5},{5,4},{6,7},{7,6},{8,9},{9,8},{10,11... | collective-permute-start | bytes 393224 | tf_op jit(solution)/shard_map/ppermute | solution.py:261
  6.7 1.0 %slice_bitcast_fusion = (bf16[2,32,1024]{2,1,0:T(8,128)(2,1)S(1)}, bf16[2,32,1024]{2,1,0:T(8,128)(2,1)S(1)}) fusion(bf16[1,2,384,1024]{3,2,1,0:T(8,128)(2,1)} %sec_ref.1), kind=kLoop, calls=%fused_computation.1 | loop fusion | bytes 524288 | tf_op jit(solution)/shard_map/squeeze | solution.py:276
  7.7 0.1 collective-permute-start.4
  7.8 2.6 %collective-permute-start.5 = (bf16[2,32,1024]{2,1,0:T(8,128)(2,1)S(1)}, bf16[2,32,1024]{2,1,0:T(8,128)(2,1)S(1)}, u32[]{:S(2)}, u32[]{:S(2)}) collective-permute-start(bf16[2,32,1024]{2,1,0:T(8,128)(2,1)S(1)} %get-tuple-element.11), channel_id=1, source_target_pairs={{0,28},{4,0},{8,4},{12,8},{16,12},{20,16},{24,20},{28,24},{1,29},{... | collective-permute-start | bytes 393224 | tf_op jit(solution)/shard_map/ppermute | solution.py:257
  11.7 0.2 shard_map.74.refs_1_.az_ref
  11.9 0.0 collective-permute-done.refs_0_.block_ref.two_ref
  12.0 1.3 %collective-permute-start.3 = (bf16[2,128,256]{2,1,0:T(8,128)(2,1)S(1)}, bf16[2,128,256]{2,1,0:T(8,128)(2,1)S(1)}, u32[]{:S(2)}, u32[]{:S(2)}) collective-permute-start(bf16[2,128,256]{2,1,0:T(8,128)(2,1)S(1)} %shard_map.75), channel_id=1, source_target_pairs={{0,1},{1,0},{2,3},{3,2},{4,5},{5,4},{6,7},{7,6},{8,9},{9,8},{10,11... | collective-permute-start | bytes 393224 | tf_op jit(solution)/shard_map/ppermute | solution.py:261
  13.3 2.4 %collective-permute-start.1 = (bf16[2,272,256]{2,1,0:T(8,128)(2,1)S(1)}, bf16[2,272,256]{2,1,0:T(8,128)(2,1)S(1)}, u32[]{:S(2)}, u32[]{:S(2)}) collective-permute-start(bf16[2,272,256]{2,1,0:T(8,128)(2,1)S(1)} %shard_map.73), channel_id=1, source_target_pairs={{0,2},{1,3},{2,0},{3,1},{4,6},{5,7},{6,4},{7,5},{8,10},{9,11},{10,... | collective-permute-start | bytes 835592 | tf_op jit(solution)/shard_map/ppermute | solution.py:261
  15.7 0.0 collective-permute-start.8
  17.1 0.2 shard_map.76.rg_ref
  17.3 1.4 %shard_map.77.res_ref = bf16[4,2,384,256]{3,2,1,0:T(8,128)(2,1)S(1)} custom-call(bf16[1,2,384,1024]{3,2,1,0:T(8,128)(2,1)S(1)} %copy-done, bf16[2,32,1024]{2,1,0:T(8,128)(2,1)S(1)} %collective-permute-done.4.low_ref, bf16[2,32,1024]{2,1,0:T(8,128)(2,1)S(1)} %collective-permute-done.5.high_ref, bf16[128,192]{1,0:T(8,128)(2,1)S(1)} %shard_map.74.refs_1_.az_ref, ...), custom_call_target="tpu_custom_call" | custom-call | tf_op jit(solution)/shard_map/pallas_call | solution.py:244
  18.7 1.3 %collective-permute-done.3.three_ref = bf16[2,128,256]{2,1,0:T(8,128)(2,1)S(1)} collective-permute-done((bf16[2,128,256]{2,1,0:T(8,128)(2,1)S(1)}, bf16[2,128,256]{2,1,0:T(8,128)(2,1)S(1)}, u32[]{:S(2)}, u32[]{:S(2)}) %collective-permute-start.3) | collective-permute-done | bytes 131104 | tf_op jit(solution)/shard_map/ppermute | solution.py:261
  20.0 0.5 %shard_map.78 = (bf16[2,64,1024]{2,1,0:T(8,128)(2,1)S(1)}, bf16[2,64,1024]{2,1,0:T(8,128)(2,1)S(1)}, f32[2,64,128]{2,1,0:T(8,128)S(1)}) custom-call(bf16[2,384,256]{2,1,0:T(8,128)(2,1)S(1)} %copy-done.1, bf16[2,128,256]{2,1,0:T(8,128)(2,1)S(1)} %collective-permute-done.2.refs_0_.one_ref, ...), custom_call_target="tpu_custom_call" | custom-call | tf_op jit(solution)/shard_map/pallas_call | solution.py:244
  20.5 0.3 collective-permute-start.6
  20.8 0.8 %slice_convert_fusion = f32[64]{0:T(128)S(1)} fusion(s32[384]{0:T(512)} %param.9), kind=kLoop, calls=%fused_computation.3 | loop fusion | flops 64 | bytes 512 | tf_op jit(solution)/shard_map/convert_element_type | solution.py:294
  21.6 3.1 %collective-permute-done.6.later_ref = bf16[2,64,1024]{2,1,0:T(8,128)(2,1)S(1)} collective-permute-done((bf16[2,64,1024]{2,1,0:T(8,128)(2,1)S(1)}, bf16[2,64,1024]{2,1,0:T(8,128)(2,1)S(1)}, u32[]{:S(2)}, u32[]{:S(2)}) %collective-permute-start.6) | collective-permute-done | bytes 262176 | tf_op jit(solution)/shard_map/ppermute | solution.py:257
  24.7 0.1 broadcast_in_dim.2.weight_ref
  24.8 0.4 shard_map.79
  25.2 1.6 %collective-permute-start.7 = (f32[8,128]{1,0:T(8,128)S(1)}, f32[8,128]{1,0:T(8,128)S(1)}, u32[]{:S(2)}, u32[]{:S(2)}) collective-permute-start(f32[8,128]{1,0:T(8,128)S(1)} %shard_map.79), channel_id=1, source_target_pairs={{0,4},{4,0},{8,12},{12,8},{16,20},{20,16},{24,28},{28,24},{1,5},{5... | collective-permute-start | bytes 12296 | tf_op jit(solution)/shard_map/ppermute | solution.py:261
  26.8 0.8 %collective-permute-done.7.refs_0_ = f32[8,128]{1,0:T(8,128)S(1)} collective-permute-done((f32[8,128]{1,0:T(8,128)S(1)}, f32[8,128]{1,0:T(8,128)S(1)}, u32[]{:S(2)}, u32[]{:S(2)}) %collective-permute-start.7) | collective-permute-done | bytes 4128 | tf_op jit(solution)/shard_map/ppermute | solution.py:261
  27.6 1.8 %collective-permute-start.10 = (f32[8,128]{1,0:T(8,128)S(1)}, f32[8,128]{1,0:T(8,128)S(1)}, u32[]{:S(2)}, u32[]{:S(2)}) collective-permute-start(f32[8,128]{1,0:T(8,128)S(1)} %add.6), channel_id=1, source_target_pairs={{0,8},{4,12},{8,0},{12,4},{16,24},{20,28},{24,16},{28,20},{1,9},{5... | collective-permute-start | bytes 12296 | tf_op jit(solution)/shard_map/ppermute | solution.py:261
  29.3 0.0 collective-permute-done.1.block_ref.two_ref
  29.4 0.9 %collective-permute-start.9 = (bf16[2,256,256]{2,1,0:T(8,128)(2,1)S(1)}, bf16[2,256,256]{2,1,0:T(8,128)(2,1)S(1)}, u32[]{:S(2)}, u32[]{:S(2)}) collective-permute-start(bf16[2,256,256]{2,1,0:T(8,128)(2,1)S(1)} %shard_map.80), channel_id=1, source_target_pairs={{0,1},{1,0},{2,3},{3,2},{4,5},{5,4},{6,7},{7,6},{8,9},{9,8},{10,11... | collective-permute-start | bytes 786440 | tf_op jit(solution)/shard_map/ppermute | solution.py:261
  30.3 0.9 %collective-permute-done.10 = f32[8,128]{1,0:T(8,128)S(1)} collective-permute-done((f32[8,128]{1,0:T(8,128)S(1)}, f32[8,128]{1,0:T(8,128)S(1)}, u32[]{:S(2)}, u32[]{:S(2)}) %collective-permute-start.10) | collective-permute-done | bytes 4128 | tf_op jit(solution)/shard_map/ppermute | solution.py:261
  31.2 1.5 %collective-permute-start.11 = (f32[8,128]{1,0:T(8,128)S(1)}, f32[8,128]{1,0:T(8,128)S(1)}, u32[]{:S(2)}, u32[]{:S(2)}) collective-permute-start(f32[8,128]{1,0:T(8,128)S(1)} %add.7.mine_ref), channel_id=1, source_target_pairs={{0,16},{4,20},{8,24},{12,28},{16,0},{20,4},{24,8},{28,12},{1,17},{... | collective-permute-start | bytes 12296 | tf_op jit(solution)/shard_map/ppermute | solution.py:261
  32.7 0.6 %shard_map.81.before_ref = f32[2,256,128]{2,1,0:T(8,128)S(1)} custom-call(bf16[2,384,256]{2,1,0:T(8,128)(2,1)S(1)} %copy-done.1, bf16[2,272,256]{2,1,0:T(8,128)(2,1)S(1)} %collective-permute-done.8.refs_1_.one_ref, bf16[2,272,256]{2,1,0:T(8,128)(2,1)S(1)} %collective-permute-done.1.block_ref.two_ref, bf16[4,2,384,256]{3,2,1,0:T(8,128)(2,1)S(1)} %shard_map.77.res_ref), custom_call_target="tpu_custom_call" | custom-call | flops 3000000000 | bytes 3145728 | tf_op jit(solution)/shard_map/pallas_call | solution.py:244
  33.3 1.5 %collective-permute-done.11.other_ref = f32[8,128]{1,0:T(8,128)S(1)} collective-permute-done((f32[8,128]{1,0:T(8,128)S(1)}, f32[8,128]{1,0:T(8,128)S(1)}, u32[]{:S(2)}, u32[]{:S(2)}) %collective-permute-start.11) | collective-permute-done | bytes 4128 | tf_op jit(solution)/shard_map/ppermute | solution.py:261
  34.8 0.1 shard_map.82.unit_ref
  35.0 2.8 %collective-permute-done.9.three_ref = bf16[2,256,256]{2,1,0:T(8,128)(2,1)S(1)} collective-permute-done((bf16[2,256,256]{2,1,0:T(8,128)(2,1)S(1)}, bf16[2,256,256]{2,1,0:T(8,128)(2,1)S(1)}, u32[]{:S(2)}, u32[]{:S(2)}) %collective-permute-start.9) | collective-permute-done | bytes 262176 | tf_op jit(solution)/shard_map/ppermute | solution.py:261
  37.7 1.0 %shard_map.83 = f32[1,2,192,128]{3,2,1,0:T(8,128)} custom-call(bf16[2,256,256]{2,1,0:T(8,128)(2,1)S(1)} %collective-permute-done.9.three_ref, bf16[4,2,384,256]{3,2,1,0:T(8,128)(2,1)S(1)} %shard_map.77.res_ref, f32[2,256,128]{2,1,0:T(8,128)S(1)} %shard_map.81.before_ref, f32[2,64,128]{2,1,0:T(8,128)S(1)} %get-tuple-element.10.looks_ref, ...), custom_call_target="tpu_custom_call" | custom-call | flops 67108864 | bytes 1572864 | tf_op jit(solution)/shard_map/pallas_call | solution.py:244
  (14 shorter events, 0.1 us)
Async XLA Ops:
  0.0 13.3 %copy-start.1 = (bf16[2,384,256]{2,1,0:T(8,128)(2,1)S(1)}, bf16[2,384,256]{2,1,0:T(8,128)(2,1)}, u32[]{:S(2)}) copy-start(bf16[2,384,256]{2,1,0:T(8,128)(2,1)} %own_ref.3) | copy-start | bytes 1179652
  0.0 17.3 %copy-start = (bf16[1,2,384,1024]{3,2,1,0:T(8,128)(2,1)S(1)}, bf16[1,2,384,1024]{3,2,1,0:T(8,128)(2,1)}, u32[]{:S(2)}) copy-start(bf16[1,2,384,1024]{3,2,1,0:T(8,128)(2,1)} %sec_ref.1) | copy-start | bytes 4718596
  1.0 10.9 %collective-permute-start = (bf16[2,128,256]{2,1,0:T(8,128)(2,1)S(1)}, bf16[2,128,256]{2,1,0:T(8,128)(2,1)S(1)}, u32[]{:S(2)}, u32[]{:S(2)}) collective-permute-start(bf16[2,128,256]{2,1,0:T(8,128)(2,1)S(1)} %pad_maximum_fusion), channel_id=1, source_target_pairs={{0,2},{1,3},{2,0},{3,1},{4,6},{5,7},{6,4},{7,5},{8,10},{9,11},{10,... | collective-permute-start | bytes 393224 | tf_op jit(solution)/shard_map/ppermute | solution.py:261
  5.2 6.8 %collective-permute-start.2 = (bf16[2,128,256]{2,1,0:T(8,128)(2,1)S(1)}, bf16[2,128,256]{2,1,0:T(8,128)(2,1)S(1)}, u32[]{:S(2)}, u32[]{:S(2)}) collective-permute-start(bf16[2,128,256]{2,1,0:T(8,128)(2,1)S(1)} %pad_maximum_fusion), channel_id=1, source_target_pairs={{0,1},{1,0},{2,3},{3,2},{4,5},{5,4},{6,7},{7,6},{8,9},{9,8},{10,11... | collective-permute-start | bytes 393224 | tf_op jit(solution)/shard_map/ppermute | solution.py:261
  7.7 9.6 %collective-permute-start.4 = (bf16[2,32,1024]{2,1,0:T(8,128)(2,1)S(1)}, bf16[2,32,1024]{2,1,0:T(8,128)(2,1)S(1)}, u32[]{:S(2)}, u32[]{:S(2)}) collective-permute-start(bf16[2,32,1024]{2,1,0:T(8,128)(2,1)S(1)} %get-tuple-element.12), channel_id=1, source_target_pairs={{0,4},{4,8},{8,12},{12,16},{16,20},{20,24},{24,28},{28,0},{1,5},{5... | collective-permute-start | bytes 393224 | tf_op jit(solution)/shard_map/ppermute | solution.py:257
  7.8 9.5 %collective-permute-start.5 = (bf16[2,32,1024]{2,1,0:T(8,128)(2,1)S(1)}, bf16[2,32,1024]{2,1,0:T(8,128)(2,1)S(1)}, u32[]{:S(2)}, u32[]{:S(2)}) collective-permute-start(bf16[2,32,1024]{2,1,0:T(8,128)(2,1)S(1)} %get-tuple-element.11), channel_id=1, source_target_pairs={{0,28},{4,0},{8,4},{12,8},{16,12},{20,16},{24,20},{28,24},{1,29},{... | collective-permute-start | bytes 393224 | tf_op jit(solution)/shard_map/ppermute | solution.py:257
  12.0 8.0 %collective-permute-start.3 = (bf16[2,128,256]{2,1,0:T(8,128)(2,1)S(1)}, bf16[2,128,256]{2,1,0:T(8,128)(2,1)S(1)}, u32[]{:S(2)}, u32[]{:S(2)}) collective-permute-start(bf16[2,128,256]{2,1,0:T(8,128)(2,1)S(1)} %shard_map.75), channel_id=1, source_target_pairs={{0,1},{1,0},{2,3},{3,2},{4,5},{5,4},{6,7},{7,6},{8,9},{9,8},{10,11... | collective-permute-start | bytes 393224 | tf_op jit(solution)/shard_map/ppermute | solution.py:261
  13.3 16.0 %collective-permute-start.1 = (bf16[2,272,256]{2,1,0:T(8,128)(2,1)S(1)}, bf16[2,272,256]{2,1,0:T(8,128)(2,1)S(1)}, u32[]{:S(2)}, u32[]{:S(2)}) collective-permute-start(bf16[2,272,256]{2,1,0:T(8,128)(2,1)S(1)} %shard_map.73), channel_id=1, source_target_pairs={{0,2},{1,3},{2,0},{3,1},{4,6},{5,7},{6,4},{7,5},{8,10},{9,11},{10,... | collective-permute-start | bytes 835592 | tf_op jit(solution)/shard_map/ppermute | solution.py:261
  15.7 13.6 %collective-permute-start.8 = (bf16[2,272,256]{2,1,0:T(8,128)(2,1)S(1)}, bf16[2,272,256]{2,1,0:T(8,128)(2,1)S(1)}, u32[]{:S(2)}, u32[]{:S(2)}) collective-permute-start(bf16[2,272,256]{2,1,0:T(8,128)(2,1)S(1)} %shard_map.73), channel_id=1, source_target_pairs={{0,1},{1,0},{2,3},{3,2},{4,5},{5,4},{6,7},{7,6},{8,9},{9,8},{10,11... | collective-permute-start | bytes 835592 | tf_op jit(solution)/shard_map/ppermute | solution.py:261
  20.5 4.2 %collective-permute-start.6 = (bf16[2,64,1024]{2,1,0:T(8,128)(2,1)S(1)}, bf16[2,64,1024]{2,1,0:T(8,128)(2,1)S(1)}, u32[]{:S(2)}, u32[]{:S(2)}) collective-permute-start(bf16[2,64,1024]{2,1,0:T(8,128)(2,1)S(1)} %get-tuple-element.9), channel_id=1, source_target_pairs={{0,28},{4,0},{8,4},{12,8},{16,12},{20,16},{24,20},{28,24},{1,29},{... | collective-permute-start | bytes 786440 | tf_op jit(solution)/shard_map/ppermute | solution.py:257
  25.2 2.4 %collective-permute-start.7 = (f32[8,128]{1,0:T(8,128)S(1)}, f32[8,128]{1,0:T(8,128)S(1)}, u32[]{:S(2)}, u32[]{:S(2)}) collective-permute-start(f32[8,128]{1,0:T(8,128)S(1)} %shard_map.79), channel_id=1, source_target_pairs={{0,4},{4,0},{8,12},{12,8},{16,20},{20,16},{24,28},{28,24},{1,5},{5... | collective-permute-start | bytes 12296 | tf_op jit(solution)/shard_map/ppermute | solution.py:261
  27.6 3.6 %collective-permute-start.10 = (f32[8,128]{1,0:T(8,128)S(1)}, f32[8,128]{1,0:T(8,128)S(1)}, u32[]{:S(2)}, u32[]{:S(2)}) collective-permute-start(f32[8,128]{1,0:T(8,128)S(1)} %add.6), channel_id=1, source_target_pairs={{0,8},{4,12},{8,0},{12,4},{16,24},{20,28},{24,16},{28,20},{1,9},{5... | collective-permute-start | bytes 12296 | tf_op jit(solution)/shard_map/ppermute | solution.py:261
  29.4 8.3 %collective-permute-start.9 = (bf16[2,256,256]{2,1,0:T(8,128)(2,1)S(1)}, bf16[2,256,256]{2,1,0:T(8,128)(2,1)S(1)}, u32[]{:S(2)}, u32[]{:S(2)}) collective-permute-start(bf16[2,256,256]{2,1,0:T(8,128)(2,1)S(1)} %shard_map.80), channel_id=1, source_target_pairs={{0,1},{1,0},{2,3},{3,2},{4,5},{5,4},{6,7},{7,6},{8,9},{9,8},{10,11... | collective-permute-start | bytes 786440 | tf_op jit(solution)/shard_map/ppermute | solution.py:261
  31.2 3.6 %collective-permute-start.11 = (f32[8,128]{1,0:T(8,128)S(1)}, f32[8,128]{1,0:T(8,128)S(1)}, u32[]{:S(2)}, u32[]{:S(2)}) collective-permute-start(f32[8,128]{1,0:T(8,128)S(1)} %add.7.mine_ref), channel_id=1, source_target_pairs={{0,16},{4,20},{8,24},{12,28},{16,0},{20,4},{24,8},{28,12},{1,17},{... | collective-permute-start | bytes 12296 | tf_op jit(solution)/shard_map/ppermute | solution.py:261

commit v23 on v18

--- a/solution.py
+++ b/solution.py
@@ -40,12 +40,6 @@
     for j in range(8):
         total = jnp.where(distance == j - 3, taps[j : j + 1, :1], total)
     return total.astype(jnp.bfloat16)
-
-
-def cut_halo_kernel(sec_ref, down_ref, up_ref):
-    rows_n = sec_ref.shape[2]
-    down_ref[...] = sec_ref[0, :, rows_n - HALO :]
-    up_ref[...] = sec_ref[0, :, :HALO]
 
 
 def cut_middle_kernel(prim_ref, *refs):
@@ -276,8 +270,7 @@
     edges = jnp.concatenate([primary[:, :LAG], primary[:, rows_n - LAG :]], axis=1)
     edges_two = swap(edges, "date", 2)
     edges_one = swap(edges, "date", 1)
-    halo = shape((2, HALO, cols_n), bf16)
-    down, up = call(cut_halo_kernel, (halo, halo), [], (0, 0), secondary)
+    down, up = secondary[0, :, rows_n - HALO :], secondary[0, :, :HALO]
     low = ring(down, "tile", 1)
     high = ring(up, "tile", -1)
     az_band, rg_band = call(

time: 38.8 us -> 38.9 us (level)
  waiting for transfers between devices: 9.2 us -> 9.65 us
    unnamed x6 -> x4, local copies, waits for them, and re-layouts: 1.41 us -> 0.01 us
    squeeze x0 -> x1, local copies, waits for them, and re-layouts: none -> 0.99 us  [fused(): down, up = (secondary[0, :, rows_n - HALO:], secondary[0, :, :HALO])]
    ppermute x9, waiting for transfers between devices: 6.06 us -> 6.5 us  [swap(): lax.ppermute(value, axis, [(at, at ^ step) for at in range(lax.axis_size(...]
    pallas_call x11 -> x10, Pallas kernels: 4.4 us -> 4.38 us  [call(): pl.pallas_call(kernel, out_shape=outs, in_specs=[vmem] * len(args), out_s...]
  transfers between devices with their start and end apart: 12 -> 12, of which waited for: 7 -> 7; matrix products, arithmetic and copies ran while one was open for 2% -> 5% of each run, Pallas kernels for 9% -> 9%
where the time goes in v23:
time: 38.9 us; the launch traced here: 38.7 us
  starting transfers between devices  19.1 us (49%)
  waiting for transfers between devices  9.65 us (25%)
  Pallas kernels  4.38 us (11%)
  between operations  2.72 us (7%)
  local copies, waits for them, and re-layouts  2.09 us (5%)
  other arithmetic  0.77 us (2%)
    ppermute x9, starting transfers between devices, swap(): lax.ppermute(value, axis, [(at, at ^ step) for at in range(lax.axis_size(...  14.8 us
    ppermute x9, waiting for transfers between devices, swap(): lax.ppermute(value, axis, [(at, at ^ step) for at in range(lax.axis_size(...  6.5 us
    pallas_call x10, Pallas kernels, call(): pl.pallas_call(kernel, out_shape=outs, in_specs=[vmem] * len(args), out_s...  4.38 us
    ppermute x3, starting transfers between devices, ring(): lax.ppermute(value, axis, [(at, (at + step) % count) for at in range(coun...  4.25 us
    ppermute x3, waiting for transfers between devices, ring(): lax.ppermute(value, axis, [(at, (at + step) % count) for at in range(coun...  3.14 us
    slice x1, local copies, waits for them, and re-layouts, fused(): primary[:, :LAG]  1.02 us
    squeeze x1, local copies, waits for them, and re-layouts, fused(): down, up = (secondary[0, :, rows_n - HALO:], secondary[0, :, :HALO])  0.99 us
  transfers between devices with their start and end apart: 12, of which 7 were waited for; matrix products, arithmetic and copies ran while one was open for 5% of the time, Pallas kernels for 9%

profile of v23, /device:TPU:0, one launch (start us, length us, event | category | flops | bytes accessed | tf_op | source)
XLA Modules:
  0.0 38.7 jit_solution(15757337719325725363)
XLA Ops:
  0.0 1.0 %fusion = (bf16[2,64,256]{2,1,0:T(8,128)(2,1)S(1)}, bf16[2,64,256]{2,1,0:T(8,128)(2,1)S(1)}) fusion(bf16[2,384,256]{2,1,0:T(8,128)(2,1)} %own_ref.3), kind=kLoop, calls=%fused_computation.4 | loop fusion | bytes 262144 | tf_op jit(solution)/shard_map/slice | solution.py:270
  1.0 4.1 %collective-permute-start = (bf16[2,128,256]{2,1,0:T(8,128)(2,1)S(1)}, bf16[2,128,256]{2,1,0:T(8,128)(2,1)S(1)}, u32[]{:S(2)}, u32[]{:S(2)}) collective-permute-start(bf16[2,128,256]{2,1,0:T(8,128)(2,1)S(1)} %pad_maximum_fusion), channel_id=1, source_target_pairs={{0,2},{1,3},{2,0},{3,1},{4,6},{5,7},{6,4},{7,5},{8,10},{9,11},{10,... | collective-permute-start | bytes 393224 | tf_op jit(solution)/shard_map/ppermute | solution.py:258
  5.2 1.6 %collective-permute-start.2 = (bf16[2,128,256]{2,1,0:T(8,128)(2,1)S(1)}, bf16[2,128,256]{2,1,0:T(8,128)(2,1)S(1)}, u32[]{:S(2)}, u32[]{:S(2)}) collective-permute-start(bf16[2,128,256]{2,1,0:T(8,128)(2,1)S(1)} %pad_maximum_fusion), channel_id=1, source_target_pairs={{0,1},{1,0},{2,3},{3,2},{4,5},{5,4},{6,7},{7,6},{8,9},{9,8},{10,11... | collective-permute-start | bytes 393224 | tf_op jit(solution)/shard_map/ppermute | solution.py:258
  6.7 1.0 %slice_bitcast_fusion = (bf16[2,32,1024]{2,1,0:T(8,128)(2,1)S(1)}, bf16[2,32,1024]{2,1,0:T(8,128)(2,1)S(1)}) fusion(bf16[1,2,384,1024]{3,2,1,0:T(8,128)(2,1)} %sec_ref.1), kind=kLoop, calls=%fused_computation.1 | loop fusion | bytes 524288 | tf_op jit(solution)/shard_map/squeeze | solution.py:273
  7.7 0.1 collective-permute-start.4
  7.8 2.6 %collective-permute-start.5 = (bf16[2,32,1024]{2,1,0:T(8,128)(2,1)S(1)}, bf16[2,32,1024]{2,1,0:T(8,128)(2,1)S(1)}, u32[]{:S(2)}, u32[]{:S(2)}) collective-permute-start(bf16[2,32,1024]{2,1,0:T(8,128)(2,1)S(1)} %get-tuple-element.15), channel_id=1, source_target_pairs={{0,28},{4,0},{8,4},{12,8},{16,12},{20,16},{24,20},{28,24},{1,29},{... | collective-permute-start | bytes 393224 | tf_op jit(solution)/shard_map/ppermute | solution.py:254
  10.4 1.1 %collective-permute-done.refs_0_.block_ref.two_ref = bf16[2,128,256]{2,1,0:T(8,128)(2,1)S(1)} collective-permute-done((bf16[2,128,256]{2,1,0:T(8,128)(2,1)S(1)}, bf16[2,128,256]{2,1,0:T(8,128)(2,1)S(1)}, u32[]{:S(2)}, u32[]{:S(2)}) %collective-permute-start) | collective-permute-done | bytes 131104 | tf_op jit(solution)/shard_map/ppermute | solution.py:258
  11.6 0.2 collective-permute-done.2.refs_0_.one_ref
  11.8 1.5 %collective-permute-start.3 = (bf16[2,128,256]{2,1,0:T(8,128)(2,1)S(1)}, bf16[2,128,256]{2,1,0:T(8,128)(2,1)S(1)}, u32[]{:S(2)}, u32[]{:S(2)}) collective-permute-start(bf16[2,128,256]{2,1,0:T(8,128)(2,1)S(1)} %shard_map.74), channel_id=1, source_target_pairs={{0,1},{1,0},{2,3},{3,2},{4,5},{5,4},{6,7},{7,6},{8,9},{9,8},{10,11... | collective-permute-start | bytes 393224 | tf_op jit(solution)/shard_map/ppermute | solution.py:258
  13.3 2.4 %collective-permute-start.1 = (bf16[2,272,256]{2,1,0:T(8,128)(2,1)S(1)}, bf16[2,272,256]{2,1,0:T(8,128)(2,1)S(1)}, u32[]{:S(2)}, u32[]{:S(2)}) collective-permute-start(bf16[2,272,256]{2,1,0:T(8,128)(2,1)S(1)} %shard_map.73), channel_id=1, source_target_pairs={{0,2},{1,3},{2,0},{3,1},{4,6},{5,7},{6,4},{7,5},{8,10},{9,11},{10,... | collective-permute-start | bytes 835592 | tf_op jit(solution)/shard_map/ppermute | solution.py:258
  15.7 0.0 collective-permute-start.8
  18.4 0.4 shard_map.75
  18.7 0.0 collective-permute-done.5.high_ref
  18.7 1.4 %shard_map.76.res_ref = bf16[4,2,384,256]{3,2,1,0:T(8,128)(2,1)S(1)} custom-call(bf16[1,2,384,1024]{3,2,1,0:T(8,128)(2,1)S(1)} %copy-done.1, bf16[2,32,1024]{2,1,0:T(8,128)(2,1)S(1)} %collective-permute-done.4.low_ref, bf16[2,32,1024]{2,1,0:T(8,128)(2,1)S(1)} %collective-permute-done.5.high_ref, bf16[128,192]{1,0:T(8,128)(2,1)S(1)} %get-tuple-element.10.az_ref, ...), custom_call_target="tpu_custom_call" | custom-call | tf_op jit(solution)/shard_map/pallas_call | solution.py:241
  20.2 0.0 collective-permute-done.3.three_ref
  20.2 0.5 %shard_map.77 = (bf16[2,64,1024]{2,1,0:T(8,128)(2,1)S(1)}, bf16[2,64,1024]{2,1,0:T(8,128)(2,1)S(1)}, f32[2,64,128]{2,1,0:T(8,128)S(1)}) custom-call(bf16[2,384,256]{2,1,0:T(8,128)(2,1)S(1)} %copy-done, bf16[2,128,256]{2,1,0:T(8,128)(2,1)S(1)} %collective-permute-done.2.refs_0_.one_ref, ...), custom_call_target="tpu_custom_call" | custom-call | tf_op jit(solution)/shard_map/pallas_call | solution.py:241
  20.7 1.6 %collective-permute-start.6 = (bf16[2,64,1024]{2,1,0:T(8,128)(2,1)S(1)}, bf16[2,64,1024]{2,1,0:T(8,128)(2,1)S(1)}, u32[]{:S(2)}, u32[]{:S(2)}) collective-permute-start(bf16[2,64,1024]{2,1,0:T(8,128)(2,1)S(1)} %get-tuple-element.13), channel_id=1, source_target_pairs={{0,28},{4,0},{8,4},{12,8},{16,12},{20,16},{24,20},{28,24},{1,29},{... | collective-permute-start | bytes 786440 | tf_op jit(solution)/shard_map/ppermute | solution.py:254
  22.3 0.8 %slice_convert_fusion = f32[64]{0:T(128)S(1)} fusion(s32[384]{0:T(512)} %param.9), kind=kLoop, calls=%fused_computation.3 | loop fusion | flops 64 | bytes 512 | tf_op jit(solution)/shard_map/convert_element_type | solution.py:294
  23.0 3.1 %collective-permute-done.6.later_ref = bf16[2,64,1024]{2,1,0:T(8,128)(2,1)S(1)} collective-permute-done((bf16[2,64,1024]{2,1,0:T(8,128)(2,1)S(1)}, bf16[2,64,1024]{2,1,0:T(8,128)(2,1)S(1)}, u32[]{:S(2)}, u32[]{:S(2)}) %collective-permute-start.6) | collective-permute-done | bytes 262176 | tf_op jit(solution)/shard_map/ppermute | solution.py:254
  26.1 0.1 broadcast_in_dim.2.weight_ref
  26.2 0.4 shard_map.78
  26.6 0.6 %collective-permute-start.7 = (f32[8,128]{1,0:T(8,128)S(1)}, f32[8,128]{1,0:T(8,128)S(1)}, u32[]{:S(2)}, u32[]{:S(2)}) collective-permute-start(f32[8,128]{1,0:T(8,128)S(1)} %shard_map.78), channel_id=1, source_target_pairs={{0,4},{4,0},{8,12},{12,8},{16,20},{20,16},{24,28},{28,24},{1,5},{5... | collective-permute-start | bytes 12296 | tf_op jit(solution)/shard_map/ppermute | solution.py:258
  27.2 1.2 %collective-permute-done.1.block_ref.two_ref = bf16[2,272,256]{2,1,0:T(8,128)(2,1)S(1)} collective-permute-done((bf16[2,272,256]{2,1,0:T(8,128)(2,1)S(1)}, bf16[2,272,256]{2,1,0:T(8,128)(2,1)S(1)}, u32[]{:S(2)}, u32[]{:S(2)}) %collective-permute-start.1) | collective-permute-done | bytes 278560 | tf_op jit(solution)/shard_map/ppermute | solution.py:258
  28.4 0.3 collective-permute-done.8.refs_1_.one_ref
  28.8 1.6 %collective-permute-start.9 = (bf16[2,256,256]{2,1,0:T(8,128)(2,1)S(1)}, bf16[2,256,256]{2,1,0:T(8,128)(2,1)S(1)}, u32[]{:S(2)}, u32[]{:S(2)}) collective-permute-start(bf16[2,256,256]{2,1,0:T(8,128)(2,1)S(1)} %shard_map.79), channel_id=1, source_target_pairs={{0,1},{1,0},{2,3},{3,2},{4,5},{5,4},{6,7},{7,6},{8,9},{9,8},{10,11... | collective-permute-start | bytes 786440 | tf_op jit(solution)/shard_map/ppermute | solution.py:258
  30.3 1.5 %collective-permute-start.10 = (f32[8,128]{1,0:T(8,128)S(1)}, f32[8,128]{1,0:T(8,128)S(1)}, u32[]{:S(2)}, u32[]{:S(2)}) collective-permute-start(f32[8,128]{1,0:T(8,128)S(1)} %add.6), channel_id=1, source_target_pairs={{0,8},{4,12},{8,0},{12,4},{16,24},{20,28},{24,16},{28,20},{1,9},{5... | collective-permute-start | bytes 12296 | tf_op jit(solution)/shard_map/ppermute | solution.py:258
  31.8 2.1 %collective-permute-done.10 = f32[8,128]{1,0:T(8,128)S(1)} collective-permute-done((f32[8,128]{1,0:T(8,128)S(1)}, f32[8,128]{1,0:T(8,128)S(1)}, u32[]{:S(2)}, u32[]{:S(2)}) %collective-permute-start.10) | collective-permute-done | bytes 4128 | tf_op jit(solution)/shard_map/ppermute | solution.py:258
  33.9 1.5 %collective-permute-start.11 = (f32[8,128]{1,0:T(8,128)S(1)}, f32[8,128]{1,0:T(8,128)S(1)}, u32[]{:S(2)}, u32[]{:S(2)}) collective-permute-start(f32[8,128]{1,0:T(8,128)S(1)} %add.7.mine_ref), channel_id=1, source_target_pairs={{0,16},{4,20},{8,24},{12,28},{16,0},{20,4},{24,8},{28,12},{1,17},{... | collective-permute-start | bytes 12296 | tf_op jit(solution)/shard_map/ppermute | solution.py:258
  35.5 0.6 %shard_map.80.before_ref = f32[2,256,128]{2,1,0:T(8,128)S(1)} custom-call(bf16[2,384,256]{2,1,0:T(8,128)(2,1)S(1)} %copy-done, bf16[2,272,256]{2,1,0:T(8,128)(2,1)S(1)} %collective-permute-done.8.refs_1_.one_ref, bf16[2,272,256]{2,1,0:T(8,128)(2,1)S(1)} %collective-permute-done.1.block_ref.two_ref, bf16[4,2,384,256]{3,2,1,0:T(8,128)(2,1)S(1)} %shard_map.76.res_ref), custom_call_target="tpu_custom_call" | custom-call | flops 134217728 | bytes 3145728 | tf_op jit(solution)/shard_map/pallas_call | solution.py:241
  36.1 1.5 %collective-permute-done.11.other_ref = f32[8,128]{1,0:T(8,128)S(1)} collective-permute-done((f32[8,128]{1,0:T(8,128)S(1)}, f32[8,128]{1,0:T(8,128)S(1)}, u32[]{:S(2)}, u32[]{:S(2)}) %collective-permute-start.11) | collective-permute-done | bytes 4128 | tf_op jit(solution)/shard_map/ppermute | solution.py:258
  37.5 0.1 shard_map.81.unit_ref
  37.7 1.0 %shard_map.82 = f32[1,2,192,128]{3,2,1,0:T(8,128)} custom-call(bf16[2,256,256]{2,1,0:T(8,128)(2,1)S(1)} %collective-permute-done.9.three_ref, bf16[4,2,384,256]{3,2,1,0:T(8,128)(2,1)S(1)} %shard_map.76.res_ref, f32[2,256,128]{2,1,0:T(8,128)S(1)} %shard_map.80.before_ref, f32[2,64,128]{2,1,0:T(8,128)S(1)} %get-tuple-element.14.looks_ref, ...), custom_call_target="tpu_custom_call" | custom-call | flops 67108864 | bytes 1572864 | tf_op jit(solution)/shard_map/pallas_call | solution.py:241
  (13 shorter events, 0.1 us)
Async XLA Ops:
  0.0 13.3 %copy-start = (bf16[2,384,256]{2,1,0:T(8,128)(2,1)S(1)}, bf16[2,384,256]{2,1,0:T(8,128)(2,1)}, u32[]{:S(2)}) copy-start(bf16[2,384,256]{2,1,0:T(8,128)(2,1)} %own_ref.3) | copy-start | bytes 1179652
  0.0 18.7 %copy-start.1 = (bf16[1,2,384,1024]{3,2,1,0:T(8,128)(2,1)S(1)}, bf16[1,2,384,1024]{3,2,1,0:T(8,128)(2,1)}, u32[]{:S(2)}) copy-start(bf16[1,2,384,1024]{3,2,1,0:T(8,128)(2,1)} %sec_ref.1) | copy-start | bytes 4718596
  1.0 10.5 %collective-permute-start = (bf16[2,128,256]{2,1,0:T(8,128)(2,1)S(1)}, bf16[2,128,256]{2,1,0:T(8,128)(2,1)S(1)}, u32[]{:S(2)}, u32[]{:S(2)}) collective-permute-start(bf16[2,128,256]{2,1,0:T(8,128)(2,1)S(1)} %pad_maximum_fusion), channel_id=1, source_target_pairs={{0,2},{1,3},{2,0},{3,1},{4,6},{5,7},{6,4},{7,5},{8,10},{9,11},{10,... | collective-permute-start | bytes 393224 | tf_op jit(solution)/shard_map/ppermute | solution.py:258
  5.2 6.6 %collective-permute-start.2 = (bf16[2,128,256]{2,1,0:T(8,128)(2,1)S(1)}, bf16[2,128,256]{2,1,0:T(8,128)(2,1)S(1)}, u32[]{:S(2)}, u32[]{:S(2)}) collective-permute-start(bf16[2,128,256]{2,1,0:T(8,128)(2,1)S(1)} %pad_maximum_fusion), channel_id=1, source_target_pairs={{0,1},{1,0},{2,3},{3,2},{4,5},{5,4},{6,7},{7,6},{8,9},{9,8},{10,11... | collective-permute-start | bytes 393224 | tf_op jit(solution)/shard_map/ppermute | solution.py:258
  7.7 11.0 %collective-permute-start.4 = (bf16[2,32,1024]{2,1,0:T(8,128)(2,1)S(1)}, bf16[2,32,1024]{2,1,0:T(8,128)(2,1)S(1)}, u32[]{:S(2)}, u32[]{:S(2)}) collective-permute-start(bf16[2,32,1024]{2,1,0:T(8,128)(2,1)S(1)} %get-tuple-element.16), channel_id=1, source_target_pairs={{0,4},{4,8},{8,12},{12,16},{16,20},{20,24},{24,28},{28,0},{1,5},{5... | collective-permute-start | bytes 393224 | tf_op jit(solution)/shard_map/ppermute | solution.py:254
  7.8 10.9 %collective-permute-start.5 = (bf16[2,32,1024]{2,1,0:T(8,128)(2,1)S(1)}, bf16[2,32,1024]{2,1,0:T(8,128)(2,1)S(1)}, u32[]{:S(2)}, u32[]{:S(2)}) collective-permute-start(bf16[2,32,1024]{2,1,0:T(8,128)(2,1)S(1)} %get-tuple-element.15), channel_id=1, source_target_pairs={{0,28},{4,0},{8,4},{12,8},{16,12},{20,16},{24,20},{28,24},{1,29},{... | collective-permute-start | bytes 393224 | tf_op jit(solution)/shard_map/ppermute | solution.py:254
  11.8 8.4 %collective-permute-start.3 = (bf16[2,128,256]{2,1,0:T(8,128)(2,1)S(1)}, bf16[2,128,256]{2,1,0:T(8,128)(2,1)S(1)}, u32[]{:S(2)}, u32[]{:S(2)}) collective-permute-start(bf16[2,128,256]{2,1,0:T(8,128)(2,1)S(1)} %shard_map.74), channel_id=1, source_target_pairs={{0,1},{1,0},{2,3},{3,2},{4,5},{5,4},{6,7},{7,6},{8,9},{9,8},{10,11... | collective-permute-start | bytes 393224 | tf_op jit(solution)/shard_map/ppermute | solution.py:258
  13.3 15.1 %collective-permute-start.1 = (bf16[2,272,256]{2,1,0:T(8,128)(2,1)S(1)}, bf16[2,272,256]{2,1,0:T(8,128)(2,1)S(1)}, u32[]{:S(2)}, u32[]{:S(2)}) collective-permute-start(bf16[2,272,256]{2,1,0:T(8,128)(2,1)S(1)} %shard_map.73), channel_id=1, source_target_pairs={{0,2},{1,3},{2,0},{3,1},{4,6},{5,7},{6,4},{7,5},{8,10},{9,11},{10,... | collective-permute-start | bytes 835592 | tf_op jit(solution)/shard_map/ppermute | solution.py:258
  15.7 13.0 %collective-permute-start.8 = (bf16[2,272,256]{2,1,0:T(8,128)(2,1)S(1)}, bf16[2,272,256]{2,1,0:T(8,128)(2,1)S(1)}, u32[]{:S(2)}, u32[]{:S(2)}) collective-permute-start(bf16[2,272,256]{2,1,0:T(8,128)(2,1)S(1)} %shard_map.73), channel_id=1, source_target_pairs={{0,1},{1,0},{2,3},{3,2},{4,5},{5,4},{6,7},{7,6},{8,9},{9,8},{10,11... | collective-permute-start | bytes 835592 | tf_op jit(solution)/shard_map/ppermute | solution.py:258
  20.7 5.5 %collective-permute-start.6 = (bf16[2,64,1024]{2,1,0:T(8,128)(2,1)S(1)}, bf16[2,64,1024]{2,1,0:T(8,128)(2,1)S(1)}, u32[]{:S(2)}, u32[]{:S(2)}) collective-permute-start(bf16[2,64,1024]{2,1,0:T(8,128)(2,1)S(1)} %get-tuple-element.13), channel_id=1, source_target_pairs={{0,28},{4,0},{8,4},{12,8},{16,12},{20,16},{24,20},{28,24},{1,29},{... | collective-permute-start | bytes 786440 | tf_op jit(solution)/shard_map/ppermute | solution.py:254
  26.6 2.2 %collective-permute-start.7 = (f32[8,128]{1,0:T(8,128)S(1)}, f32[8,128]{1,0:T(8,128)S(1)}, u32[]{:S(2)}, u32[]{:S(2)}) collective-permute-start(f32[8,128]{1,0:T(8,128)S(1)} %shard_map.78), channel_id=1, source_target_pairs={{0,4},{4,0},{8,12},{12,8},{16,20},{20,16},{24,28},{28,24},{1,5},{5... | collective-permute-start | bytes 12296 | tf_op jit(solution)/shard_map/ppermute | solution.py:258
  28.8 8.9 %collective-permute-start.9 = (bf16[2,256,256]{2,1,0:T(8,128)(2,1)S(1)}, bf16[2,256,256]{2,1,0:T(8,128)(2,1)S(1)}, u32[]{:S(2)}, u32[]{:S(2)}) collective-permute-start(bf16[2,256,256]{2,1,0:T(8,128)(2,1)S(1)} %shard_map.79), channel_id=1, source_target_pairs={{0,1},{1,0},{2,3},{3,2},{4,5},{5,4},{6,7},{7,6},{8,9},{9,8},{10,11... | collective-permute-start | bytes 786440 | tf_op jit(solution)/shard_map/ppermute | solution.py:258
  30.3 3.6 %collective-permute-start.10 = (f32[8,128]{1,0:T(8,128)S(1)}, f32[8,128]{1,0:T(8,128)S(1)}, u32[]{:S(2)}, u32[]{:S(2)}) collective-permute-start(f32[8,128]{1,0:T(8,128)S(1)} %add.6), channel_id=1, source_target_pairs={{0,8},{4,12},{8,0},{12,4},{16,24},{20,28},{24,16},{28,20},{1,9},{5... | collective-permute-start | bytes 12296 | tf_op jit(solution)/shard_map/ppermute | solution.py:258
  33.9 3.6 %collective-permute-start.11 = (f32[8,128]{1,0:T(8,128)S(1)}, f32[8,128]{1,0:T(8,128)S(1)}, u32[]{:S(2)}, u32[]{:S(2)}) collective-permute-start(f32[8,128]{1,0:T(8,128)S(1)} %add.7.mine_ref), channel_id=1, source_target_pairs={{0,16},{4,20},{8,24},{12,28},{16,0},{20,4},{24,8},{28,12},{1,17},{... | collective-permute-start | bytes 12296 | tf_op jit(solution)/shard_map/ppermute | solution.py:258

commit v24 on v23

--- a/solution.py
+++ b/solution.py
@@ -281,7 +281,7 @@
         az_off, rg_off, az_frac, rg_frac,
     )
     passed = call(
-        relay_kernel, shape(edges.shape, bf16), [], (0, 0), edges_two, edges_one
+        relay_kernel, shape(edges.shape, bf16), [], (0, 0), edges_two
     )
     edges_three = swap(passed, "date", 1)
     middle = call(
@@ -289,7 +289,7 @@
         shape((2, middle_n + 16, width), bf16),
         [],
         (0, 0),
-        primary, edges_two,
+        primary, edges_two, edges_one,
     )
     weight = jnp.broadcast_to(margin_mask[rows_n - LAG :].astype(f32)[:, None], (LAG, LANE))
     res = call(

time: 38.9 us -> 38.7 us (level)
  waiting for transfers between devices: 9.65 us -> 9.24 us
    ppermute x9, waiting for transfers between devices: 6.5 us -> 6.09 us  [swap(): lax.ppermute(value, axis, [(at, at ^ step) for at in range(lax.axis_size(...]
  transfers between devices with their start and end apart: 12 -> 12, of which waited for: 7 -> 6; matrix products, arithmetic and copies ran while one was open for 5% -> 5% of each run, Pallas kernels for 9% -> 9%
where the time goes in v24:
time: 38.7 us; the launch traced here: 38.5 us
  starting transfers between devices  19.3 us (50%)
  waiting for transfers between devices  9.24 us (24%)
  Pallas kernels  4.38 us (11%)
  between operations  2.72 us (7%)
  local copies, waits for them, and re-layouts  2.09 us (5%)
  other arithmetic  0.77 us (2%)
    ppermute x9, starting transfers between devices, swap(): lax.ppermute(value, axis, [(at, at ^ step) for at in range(lax.axis_size(...  15 us
    ppermute x9, waiting for transfers between devices, swap(): lax.ppermute(value, axis, [(at, at ^ step) for at in range(lax.axis_size(...  6.09 us
    pallas_call x10, Pallas kernels, call(): pl.pallas_call(kernel, out_shape=outs, in_specs=[vmem] * len(args), out_s...  4.38 us
    ppermute x3, starting transfers between devices, ring(): lax.ppermute(value, axis, [(at, (at + step) % count) for at in range(coun...  4.25 us
    ppermute x3, waiting for transfers between devices, ring(): lax.ppermute(value, axis, [(at, (at + step) % count) for at in range(coun...  3.14 us
    slice x1, local copies, waits for them, and re-layouts, fused(): primary[:, :LAG]  1.02 us
    squeeze x1, local copies, waits for them, and re-layouts, fused(): down, up = (secondary[0, :, rows_n - HALO:], secondary[0, :, :HALO])  0.99 us
  transfers between devices with their start and end apart: 12, of which 6 were waited for; matrix products, arithmetic and copies ran while one was open for 5% of the time, Pallas kernels for 9%

profile of v24, /device:TPU:0, one launch (start us, length us, event | category | flops | bytes accessed | tf_op | source)
XLA Modules:
  0.0 38.5 jit_solution(467516996518933954)
XLA Ops:
  0.0 1.0 %fusion = (bf16[2,64,256]{2,1,0:T(8,128)(2,1)S(1)}, bf16[2,64,256]{2,1,0:T(8,128)(2,1)S(1)}) fusion(bf16[2,384,256]{2,1,0:T(8,128)(2,1)} %own_ref.3), kind=kLoop, calls=%fused_computation.4 | loop fusion | bytes 262144 | tf_op jit(solution)/shard_map/slice | solution.py:270
  1.0 4.1 %collective-permute-start = (bf16[2,128,256]{2,1,0:T(8,128)(2,1)S(1)}, bf16[2,128,256]{2,1,0:T(8,128)(2,1)S(1)}, u32[]{:S(2)}, u32[]{:S(2)}) collective-permute-start(bf16[2,128,256]{2,1,0:T(8,128)(2,1)S(1)} %pad_maximum_fusion), channel_id=1, source_target_pairs={{0,2},{1,3},{2,0},{3,1},{4,6},{5,7},{6,4},{7,5},{8,10},{9,11},{10,... | collective-permute-start | bytes 393224 | tf_op jit(solution)/shard_map/ppermute | solution.py:258
  5.2 1.6 %collective-permute-start.1 = (bf16[2,128,256]{2,1,0:T(8,128)(2,1)S(1)}, bf16[2,128,256]{2,1,0:T(8,128)(2,1)S(1)}, u32[]{:S(2)}, u32[]{:S(2)}) collective-permute-start(bf16[2,128,256]{2,1,0:T(8,128)(2,1)S(1)} %pad_maximum_fusion), channel_id=1, source_target_pairs={{0,1},{1,0},{2,3},{3,2},{4,5},{5,4},{6,7},{7,6},{8,9},{9,8},{10,11... | collective-permute-start | bytes 393224 | tf_op jit(solution)/shard_map/ppermute | solution.py:258
  6.7 1.0 %slice_bitcast_fusion = (bf16[2,32,1024]{2,1,0:T(8,128)(2,1)S(1)}, bf16[2,32,1024]{2,1,0:T(8,128)(2,1)S(1)}) fusion(bf16[1,2,384,1024]{3,2,1,0:T(8,128)(2,1)} %sec_ref.1), kind=kLoop, calls=%fused_computation.1 | loop fusion | bytes 524288 | tf_op jit(solution)/shard_map/squeeze | solution.py:273
  7.7 0.1 collective-permute-start.4
  7.8 2.6 %collective-permute-start.5 = (bf16[2,32,1024]{2,1,0:T(8,128)(2,1)S(1)}, bf16[2,32,1024]{2,1,0:T(8,128)(2,1)S(1)}, u32[]{:S(2)}, u32[]{:S(2)}) collective-permute-start(bf16[2,32,1024]{2,1,0:T(8,128)(2,1)S(1)} %get-tuple-element.15), channel_id=1, source_target_pairs={{0,28},{4,0},{8,4},{12,8},{16,12},{20,16},{24,20},{28,24},{1,29},{... | collective-permute-start | bytes 393224 | tf_op jit(solution)/shard_map/ppermute | solution.py:254
  10.4 1.1 %collective-permute-done.refs_0_.block_ref.two_ref = bf16[2,128,256]{2,1,0:T(8,128)(2,1)S(1)} collective-permute-done((bf16[2,128,256]{2,1,0:T(8,128)(2,1)S(1)}, bf16[2,128,256]{2,1,0:T(8,128)(2,1)S(1)}, u32[]{:S(2)}, u32[]{:S(2)}) %collective-permute-start) | collective-permute-done | bytes 131104 | tf_op jit(solution)/shard_map/ppermute | solution.py:258
  11.6 0.7 %collective-permute-start.3 = (bf16[2,128,256]{2,1,0:T(8,128)(2,1)S(1)}, bf16[2,128,256]{2,1,0:T(8,128)(2,1)S(1)}, u32[]{:S(2)}, u32[]{:S(2)}) collective-permute-start(bf16[2,128,256]{2,1,0:T(8,128)(2,1)S(1)} %shard_map.74), channel_id=1, source_target_pairs={{0,1},{1,0},{2,3},{3,2},{4,5},{5,4},{6,7},{7,6},{8,9},{9,8},{10,11... | collective-permute-start | bytes 393224 | tf_op jit(solution)/shard_map/ppermute | solution.py:258
  12.3 0.0 collective-permute-done.1.refs_1_.one_ref
  12.3 3.4 %collective-permute-start.2 = (bf16[2,272,256]{2,1,0:T(8,128)(2,1)S(1)}, bf16[2,272,256]{2,1,0:T(8,128)(2,1)S(1)}, u32[]{:S(2)}, u32[]{:S(2)}) collective-permute-start(bf16[2,272,256]{2,1,0:T(8,128)(2,1)S(1)} %shard_map.73), channel_id=1, source_target_pairs={{0,2},{1,3},{2,0},{3,1},{4,6},{5,7},{6,4},{7,5},{8,10},{9,11},{10,... | collective-permute-start | bytes 835592 | tf_op jit(solution)/shard_map/ppermute | solution.py:258
  15.7 0.0 collective-permute-start.8
  18.4 0.4 shard_map.75
  18.7 0.0 collective-permute-done.5.high_ref
  18.8 1.4 %shard_map.76.res_ref = bf16[4,2,384,256]{3,2,1,0:T(8,128)(2,1)S(1)} custom-call(bf16[1,2,384,1024]{3,2,1,0:T(8,128)(2,1)S(1)} %copy-done.1, bf16[2,32,1024]{2,1,0:T(8,128)(2,1)S(1)} %collective-permute-done.4.low_ref, bf16[2,32,1024]{2,1,0:T(8,128)(2,1)S(1)} %collective-permute-done.5.high_ref, bf16[128,192]{1,0:T(8,128)(2,1)S(1)} %get-tuple-element.10.az_ref, ...), custom_call_target="tpu_custom_call" | custom-call | tf_op jit(solution)/shard_map/pallas_call | solution.py:241
  20.2 0.5 %shard_map.77 = (bf16[2,64,1024]{2,1,0:T(8,128)(2,1)S(1)}, bf16[2,64,1024]{2,1,0:T(8,128)(2,1)S(1)}, f32[2,64,128]{2,1,0:T(8,128)S(1)}) custom-call(bf16[2,384,256]{2,1,0:T(8,128)(2,1)S(1)} %copy-done, bf16[2,128,256]{2,1,0:T(8,128)(2,1)S(1)} %collective-permute-done.1.refs_1_.one_ref, ...), custom_call_target="tpu_custom_call" | custom-call | tf_op jit(solution)/shard_map/pallas_call | solution.py:241
  20.7 1.6 %collective-permute-start.6 = (bf16[2,64,1024]{2,1,0:T(8,128)(2,1)S(1)}, bf16[2,64,1024]{2,1,0:T(8,128)(2,1)S(1)}, u32[]{:S(2)}, u32[]{:S(2)}) collective-permute-start(bf16[2,64,1024]{2,1,0:T(8,128)(2,1)S(1)} %get-tuple-element.13), channel_id=1, source_target_pairs={{0,28},{4,0},{8,4},{12,8},{16,12},{20,16},{24,20},{28,24},{1,29},{... | collective-permute-start | bytes 786440 | tf_op jit(solution)/shard_map/ppermute | solution.py:254
  22.3 0.8 %slice_convert_fusion = f32[64]{0:T(128)S(1)} fusion(s32[384]{0:T(512)} %param.9), kind=kLoop, calls=%fused_computation.3 | loop fusion | flops 64 | bytes 512 | tf_op jit(solution)/shard_map/convert_element_type | solution.py:294
  23.0 3.1 %collective-permute-done.6.later_ref = bf16[2,64,1024]{2,1,0:T(8,128)(2,1)S(1)} collective-permute-done((bf16[2,64,1024]{2,1,0:T(8,128)(2,1)S(1)}, bf16[2,64,1024]{2,1,0:T(8,128)(2,1)S(1)}, u32[]{:S(2)}, u32[]{:S(2)}) %collective-permute-start.6) | collective-permute-done | bytes 262176 | tf_op jit(solution)/shard_map/ppermute | solution.py:254
  26.1 0.1 broadcast_in_dim.2.weight_ref
  26.2 0.4 shard_map.78
  26.6 0.6 %collective-permute-start.7 = (f32[8,128]{1,0:T(8,128)S(1)}, f32[8,128]{1,0:T(8,128)S(1)}, u32[]{:S(2)}, u32[]{:S(2)}) collective-permute-start(f32[8,128]{1,0:T(8,128)S(1)} %shard_map.78), channel_id=1, source_target_pairs={{0,4},{4,0},{8,12},{12,8},{16,20},{20,16},{24,28},{28,24},{1,5},{5... | collective-permute-start | bytes 12296 | tf_op jit(solution)/shard_map/ppermute | solution.py:258
  27.2 1.2 %collective-permute-done.2.block_ref.two_ref = bf16[2,272,256]{2,1,0:T(8,128)(2,1)S(1)} collective-permute-done((bf16[2,272,256]{2,1,0:T(8,128)(2,1)S(1)}, bf16[2,272,256]{2,1,0:T(8,128)(2,1)S(1)}, u32[]{:S(2)}, u32[]{:S(2)}) %collective-permute-start.2) | collective-permute-done | bytes 278560 | tf_op jit(solution)/shard_map/ppermute | solution.py:258
  28.4 0.1 collective-permute-done.8.refs_1_.one_ref
  28.5 0.0 collective-permute-done.7.refs_0_
  28.6 1.6 %collective-permute-start.9 = (bf16[2,256,256]{2,1,0:T(8,128)(2,1)S(1)}, bf16[2,256,256]{2,1,0:T(8,128)(2,1)S(1)}, u32[]{:S(2)}, u32[]{:S(2)}) collective-permute-start(bf16[2,256,256]{2,1,0:T(8,128)(2,1)S(1)} %shard_map.79), channel_id=1, source_target_pairs={{0,1},{1,0},{2,3},{3,2},{4,5},{5,4},{6,7},{7,6},{8,9},{9,8},{10,11... | collective-permute-start | bytes 786440 | tf_op jit(solution)/shard_map/ppermute | solution.py:258
  30.1 1.5 %collective-permute-start.10 = (f32[8,128]{1,0:T(8,128)S(1)}, f32[8,128]{1,0:T(8,128)S(1)}, u32[]{:S(2)}, u32[]{:S(2)}) collective-permute-start(f32[8,128]{1,0:T(8,128)S(1)} %add.6), channel_id=1, source_target_pairs={{0,8},{4,12},{8,0},{12,4},{16,24},{20,28},{24,16},{28,20},{1,9},{5... | collective-permute-start | bytes 12296 | tf_op jit(solution)/shard_map/ppermute | solution.py:258
  31.6 2.1 %collective-permute-done.10 = f32[8,128]{1,0:T(8,128)S(1)} collective-permute-done((f32[8,128]{1,0:T(8,128)S(1)}, f32[8,128]{1,0:T(8,128)S(1)}, u32[]{:S(2)}, u32[]{:S(2)}) %collective-permute-start.10) | collective-permute-done | bytes 4128 | tf_op jit(solution)/shard_map/ppermute | solution.py:258
  33.8 1.5 %collective-permute-start.11 = (f32[8,128]{1,0:T(8,128)S(1)}, f32[8,128]{1,0:T(8,128)S(1)}, u32[]{:S(2)}, u32[]{:S(2)}) collective-permute-start(f32[8,128]{1,0:T(8,128)S(1)} %add.7.mine_ref), channel_id=1, source_target_pairs={{0,16},{4,20},{8,24},{12,28},{16,0},{20,4},{24,8},{28,12},{1,17},{... | collective-permute-start | bytes 12296 | tf_op jit(solution)/shard_map/ppermute | solution.py:258
  35.3 0.6 %shard_map.80.before_ref = f32[2,256,128]{2,1,0:T(8,128)S(1)} custom-call(bf16[2,384,256]{2,1,0:T(8,128)(2,1)S(1)} %copy-done, bf16[2,272,256]{2,1,0:T(8,128)(2,1)S(1)} %collective-permute-done.8.refs_1_.one_ref, bf16[2,272,256]{2,1,0:T(8,128)(2,1)S(1)} %collective-permute-done.2.block_ref.two_ref, bf16[4,2,384,256]{3,2,1,0:T(8,128)(2,1)S(1)} %shard_map.76.res_ref), custom_call_target="tpu_custom_call" | custom-call | flops 134217728 | bytes 3145728 | tf_op jit(solution)/shard_map/pallas_call | solution.py:241
  35.9 1.5 %collective-permute-done.11.other_ref = f32[8,128]{1,0:T(8,128)S(1)} collective-permute-done((f32[8,128]{1,0:T(8,128)S(1)}, f32[8,128]{1,0:T(8,128)S(1)}, u32[]{:S(2)}, u32[]{:S(2)}) %collective-permute-start.11) | collective-permute-done | bytes 4128 | tf_op jit(solution)/shard_map/ppermute | solution.py:258
  37.4 0.1 shard_map.81.unit_ref
  37.5 1.0 %shard_map.82 = f32[1,2,192,128]{3,2,1,0:T(8,128)} custom-call(bf16[2,256,256]{2,1,0:T(8,128)(2,1)S(1)} %collective-permute-done.9.three_ref, bf16[4,2,384,256]{3,2,1,0:T(8,128)(2,1)S(1)} %shard_map.76.res_ref, f32[2,256,128]{2,1,0:T(8,128)S(1)} %shard_map.80.before_ref, f32[2,64,128]{2,1,0:T(8,128)S(1)} %get-tuple-element.14.looks_ref, ...), custom_call_target="tpu_custom_call" | custom-call | flops 67108864 | bytes 1572864 | tf_op jit(solution)/shard_map/pallas_call | solution.py:241
  (13 shorter events, 0.1 us)
Async XLA Ops:
  0.0 12.3 %copy-start = (bf16[2,384,256]{2,1,0:T(8,128)(2,1)S(1)}, bf16[2,384,256]{2,1,0:T(8,128)(2,1)}, u32[]{:S(2)}) copy-start(bf16[2,384,256]{2,1,0:T(8,128)(2,1)} %own_ref.3) | copy-start | bytes 1179652
  0.0 18.7 %copy-start.1 = (bf16[1,2,384,1024]{3,2,1,0:T(8,128)(2,1)S(1)}, bf16[1,2,384,1024]{3,2,1,0:T(8,128)(2,1)}, u32[]{:S(2)}) copy-start(bf16[1,2,384,1024]{3,2,1,0:T(8,128)(2,1)} %sec_ref.1) | copy-start | bytes 4718596
  1.0 10.5 %collective-permute-start = (bf16[2,128,256]{2,1,0:T(8,128)(2,1)S(1)}, bf16[2,128,256]{2,1,0:T(8,128)(2,1)S(1)}, u32[]{:S(2)}, u32[]{:S(2)}) collective-permute-start(bf16[2,128,256]{2,1,0:T(8,128)(2,1)S(1)} %pad_maximum_fusion), channel_id=1, source_target_pairs={{0,2},{1,3},{2,0},{3,1},{4,6},{5,7},{6,4},{7,5},{8,10},{9,11},{10,... | collective-permute-start | bytes 393224 | tf_op jit(solution)/shard_map/ppermute | solution.py:258
  5.2 7.1 %collective-permute-start.1 = (bf16[2,128,256]{2,1,0:T(8,128)(2,1)S(1)}, bf16[2,128,256]{2,1,0:T(8,128)(2,1)S(1)}, u32[]{:S(2)}, u32[]{:S(2)}) collective-permute-start(bf16[2,128,256]{2,1,0:T(8,128)(2,1)S(1)} %pad_maximum_fusion), channel_id=1, source_target_pairs={{0,1},{1,0},{2,3},{3,2},{4,5},{5,4},{6,7},{7,6},{8,9},{9,8},{10,11... | collective-permute-start | bytes 393224 | tf_op jit(solution)/shard_map/ppermute | solution.py:258
  7.7 11.0 %collective-permute-start.4 = (bf16[2,32,1024]{2,1,0:T(8,128)(2,1)S(1)}, bf16[2,32,1024]{2,1,0:T(8,128)(2,1)S(1)}, u32[]{:S(2)}, u32[]{:S(2)}) collective-permute-start(bf16[2,32,1024]{2,1,0:T(8,128)(2,1)S(1)} %get-tuple-element.16), channel_id=1, source_target_pairs={{0,4},{4,8},{8,12},{12,16},{16,20},{20,24},{24,28},{28,0},{1,5},{5... | collective-permute-start | bytes 393224 | tf_op jit(solution)/shard_map/ppermute | solution.py:254
  7.8 11.0 %collective-permute-start.5 = (bf16[2,32,1024]{2,1,0:T(8,128)(2,1)S(1)}, bf16[2,32,1024]{2,1,0:T(8,128)(2,1)S(1)}, u32[]{:S(2)}, u32[]{:S(2)}) collective-permute-start(bf16[2,32,1024]{2,1,0:T(8,128)(2,1)S(1)} %get-tuple-element.15), channel_id=1, source_target_pairs={{0,28},{4,0},{8,4},{12,8},{16,12},{20,16},{24,20},{28,24},{1,29},{... | collective-permute-start | bytes 393224 | tf_op jit(solution)/shard_map/ppermute | solution.py:254
  11.6 8.6 %collective-permute-start.3 = (bf16[2,128,256]{2,1,0:T(8,128)(2,1)S(1)}, bf16[2,128,256]{2,1,0:T(8,128)(2,1)S(1)}, u32[]{:S(2)}, u32[]{:S(2)}) collective-permute-start(bf16[2,128,256]{2,1,0:T(8,128)(2,1)S(1)} %shard_map.74), channel_id=1, source_target_pairs={{0,1},{1,0},{2,3},{3,2},{4,5},{5,4},{6,7},{7,6},{8,9},{9,8},{10,11... | collective-permute-start | bytes 393224 | tf_op jit(solution)/shard_map/ppermute | solution.py:258
  12.3 16.1 %collective-permute-start.2 = (bf16[2,272,256]{2,1,0:T(8,128)(2,1)S(1)}, bf16[2,272,256]{2,1,0:T(8,128)(2,1)S(1)}, u32[]{:S(2)}, u32[]{:S(2)}) collective-permute-start(bf16[2,272,256]{2,1,0:T(8,128)(2,1)S(1)} %shard_map.73), channel_id=1, source_target_pairs={{0,2},{1,3},{2,0},{3,1},{4,6},{5,7},{6,4},{7,5},{8,10},{9,11},{10,... | collective-permute-start | bytes 835592 | tf_op jit(solution)/shard_map/ppermute | solution.py:258
  15.7 12.8 %collective-permute-start.8 = (bf16[2,272,256]{2,1,0:T(8,128)(2,1)S(1)}, bf16[2,272,256]{2,1,0:T(8,128)(2,1)S(1)}, u32[]{:S(2)}, u32[]{:S(2)}) collective-permute-start(bf16[2,272,256]{2,1,0:T(8,128)(2,1)S(1)} %shard_map.73), channel_id=1, source_target_pairs={{0,1},{1,0},{2,3},{3,2},{4,5},{5,4},{6,7},{7,6},{8,9},{9,8},{10,11... | collective-permute-start | bytes 835592 | tf_op jit(solution)/shard_map/ppermute | solution.py:258
  20.7 5.5 %collective-permute-start.6 = (bf16[2,64,1024]{2,1,0:T(8,128)(2,1)S(1)}, bf16[2,64,1024]{2,1,0:T(8,128)(2,1)S(1)}, u32[]{:S(2)}, u32[]{:S(2)}) collective-permute-start(bf16[2,64,1024]{2,1,0:T(8,128)(2,1)S(1)} %get-tuple-element.13), channel_id=1, source_target_pairs={{0,28},{4,0},{8,4},{12,8},{16,12},{20,16},{24,20},{28,24},{1,29},{... | collective-permute-start | bytes 786440 | tf_op jit(solution)/shard_map/ppermute | solution.py:254
  26.6 2.0 %collective-permute-start.7 = (f32[8,128]{1,0:T(8,128)S(1)}, f32[8,128]{1,0:T(8,128)S(1)}, u32[]{:S(2)}, u32[]{:S(2)}) collective-permute-start(f32[8,128]{1,0:T(8,128)S(1)} %shard_map.78), channel_id=1, source_target_pairs={{0,4},{4,0},{8,12},{12,8},{16,20},{20,16},{24,28},{28,24},{1,5},{5... | collective-permute-start | bytes 12296 | tf_op jit(solution)/shard_map/ppermute | solution.py:258
  28.6 8.9 %collective-permute-start.9 = (bf16[2,256,256]{2,1,0:T(8,128)(2,1)S(1)}, bf16[2,256,256]{2,1,0:T(8,128)(2,1)S(1)}, u32[]{:S(2)}, u32[]{:S(2)}) collective-permute-start(bf16[2,256,256]{2,1,0:T(8,128)(2,1)S(1)} %shard_map.79), channel_id=1, source_target_pairs={{0,1},{1,0},{2,3},{3,2},{4,5},{5,4},{6,7},{7,6},{8,9},{9,8},{10,11... | collective-permute-start | bytes 786440 | tf_op jit(solution)/shard_map/ppermute | solution.py:258
  30.1 3.6 %collective-permute-start.10 = (f32[8,128]{1,0:T(8,128)S(1)}, f32[8,128]{1,0:T(8,128)S(1)}, u32[]{:S(2)}, u32[]{:S(2)}) collective-permute-start(f32[8,128]{1,0:T(8,128)S(1)} %add.6), channel_id=1, source_target_pairs={{0,8},{4,12},{8,0},{12,4},{16,24},{20,28},{24,16},{28,20},{1,9},{5... | collective-permute-start | bytes 12296 | tf_op jit(solution)/shard_map/ppermute | solution.py:258
  33.8 3.6 %collective-permute-start.11 = (f32[8,128]{1,0:T(8,128)S(1)}, f32[8,128]{1,0:T(8,128)S(1)}, u32[]{:S(2)}, u32[]{:S(2)}) collective-permute-start(f32[8,128]{1,0:T(8,128)S(1)} %add.7.mine_ref), channel_id=1, source_target_pairs={{0,16},{4,20},{8,24},{12,28},{16,0},{20,4},{24,8},{28,12},{1,17},{... | collective-permute-start | bytes 12296 | tf_op jit(solution)/shard_map/ppermute | solution.py:258

commit v25 on v24

--- a/solution.py
+++ b/solution.py
@@ -219,30 +219,44 @@
     unit_ref[...] = jnp.where(row == 0, e_re / denom, e_im / denom) * (1.0 / (LA * LR))
 
 
-def finish_kernel(three_ref, res_ref, before_ref, looks_ref, unit_ref, out_ref, sums_ref):
+def finish_kernel(
+    three_ref, res_ref, before_ref, looks_ref, unit_ref, out_hbm, sums_ref, held_ref, sems
+):
     middle_n = before_ref.shape[1]
     edge = LAG // LA
     u_re, u_im = unit_ref[0:1], unit_ref[1:2]
-    totals = look_sums(((3, three_ref),), res_ref, out_ref.shape[3])
+    copies = []
+
+    def leave(at, held):
+        rows = slice(at, at + held[0].shape[0])
+        held_ref[0, rows] = held[0] * u_re + held[1] * u_im
+        held_ref[1, rows] = held[1] * u_re - held[0] * u_im
+        copy = pltpu.make_async_copy(
+            held_ref.at[:, rows], out_hbm.at[0, :, rows], sems.at[len(copies)]
+        )
+        copy.start()
+        copies.append(copy)
+
+    leave(0, looks_ref[:, :edge])
+    leave(edge + middle_n // LA, looks_ref[:, edge:])
+    totals = look_sums(((3, three_ref),), res_ref, out_hbm.shape[3])
     for part, total in enumerate(totals):
         sums_ref[part] = total + before_ref[part]
-    for at, held in (
-        (0, looks_ref[:, :edge]),
-        (edge, [look_rows(sums_ref, part, 0, middle_n) for part in range(2)]),
-        (edge + middle_n // LA, looks_ref[:, edge:]),
-    ):
-        rows = slice(at, at + held[0].shape[0])
-        out_ref[0, 0, rows] = held[0] * u_re + held[1] * u_im
-        out_ref[0, 1, rows] = held[1] * u_re - held[0] * u_im
-
-
-def call(kernel, outs, scratch, cost, *args):
+    half = middle_n // 2
+    for start in (0, half):
+        leave(edge + start // LA, [look_rows(sums_ref, part, start, half) for part in range(2)])
+    for copy in copies:
+        copy.wait()
+
+
+def call(kernel, outs, scratch, cost, *args, out_place=pltpu.VMEM):
     vmem = pl.BlockSpec(memory_space=pltpu.VMEM)
+    out_spec = pl.BlockSpec(memory_space=out_place)
     return pl.pallas_call(
         kernel,
         out_shape=outs,
         in_specs=[vmem] * len(args),
-        out_specs=jax.tree.map(lambda _: vmem, outs),
+        out_specs=jax.tree.map(lambda _: out_spec, outs),
         scratch_shapes=scratch,
         compiler_params=pltpu.CompilerParams(vmem_limit_bytes=VMEM_LIMIT),
         cost_estimate=pl.CostEstimate(flops=cost[0], bytes_accessed=cost[1], transcendentals=0),
@@ -336,9 +350,14 @@
     return call(
         finish_kernel,
         shape((1, 2, rows_n // LA, looks_n), f32),
-        [pltpu.VMEM((2, middle_n, looks_n), f32)],
+        [
+            pltpu.VMEM((2, middle_n, looks_n), f32),
+            pltpu.VMEM((2, rows_n // LA, looks_n), f32),
+            pltpu.SemaphoreType.DMA((4,)),
+        ],
         (2 * middle_n * cols_n * looks_n, 4 * rows_n * cols_n),
         three, res, before, looks, unit,
+        out_place=pl.ANY,
     )
 
 

time: 38.7 us -> 38.7 us (level)
  no operation moved by 1% of the time
where the time goes in v25:
time: 38.7 us; the launch traced here: 38.5 us
  starting transfers between devices  19.3 us (50%)
  waiting for transfers between devices  9.24 us (24%)
  Pallas kernels  4.37 us (11%)
  between operations  2.72 us (7%)
  local copies, waits for them, and re-layouts  2.09 us (5%)
  other arithmetic  0.77 us (2%)
    ppermute x9, starting transfers between devices, swap(): lax.ppermute(value, axis, [(at, at ^ step) for at in range(lax.axis_size(...  15 us
    ppermute x9, waiting for transfers between devices, swap(): lax.ppermute(value, axis, [(at, at ^ step) for at in range(lax.axis_size(...  6.09 us
    pallas_call x10, Pallas kernels, call(): pl.pallas_call(kernel, out_shape=outs, in_specs=[vmem] * len(args), out_s...  4.37 us
    ppermute x3, starting transfers between devices, ring(): lax.ppermute(value, axis, [(at, (at + step) % count) for at in range(coun...  4.25 us
    ppermute x3, waiting for transfers between devices, ring(): lax.ppermute(value, axis, [(at, (at + step) % count) for at in range(coun...  3.14 us
    slice x1, local copies, waits for them, and re-layouts, fused(): primary[:, :LAG]  1.02 us
    squeeze x1, local copies, waits for them, and re-layouts, fused(): down, up = (secondary[0, :, rows_n - HALO:], secondary[0, :, :HALO])  0.99 us
  transfers between devices with their start and end apart: 12, of which 6 were waited for; matrix products, arithmetic and copies ran while one was open for 5% of the time, Pallas kernels for 9%

profile of v25, /device:TPU:0, one launch (start us, length us, event | category | flops | bytes accessed | tf_op | source)
XLA Modules:
  0.0 38.5 jit_solution(9485639503235547905)
XLA Ops:
  0.0 1.0 %fusion = (bf16[2,64,256]{2,1,0:T(8,128)(2,1)S(1)}, bf16[2,64,256]{2,1,0:T(8,128)(2,1)S(1)}) fusion(bf16[2,384,256]{2,1,0:T(8,128)(2,1)} %own_ref.3), kind=kLoop, calls=%fused_computation.4 | loop fusion | bytes 262144 | tf_op jit(solution)/shard_map/slice | solution.py:284
  1.0 4.1 %collective-permute-start = (bf16[2,128,256]{2,1,0:T(8,128)(2,1)S(1)}, bf16[2,128,256]{2,1,0:T(8,128)(2,1)S(1)}, u32[]{:S(2)}, u32[]{:S(2)}) collective-permute-start(bf16[2,128,256]{2,1,0:T(8,128)(2,1)S(1)} %pad_maximum_fusion), channel_id=1, source_target_pairs={{0,2},{1,3},{2,0},{3,1},{4,6},{5,7},{6,4},{7,5},{8,10},{9,11},{10,... | collective-permute-start | bytes 393224 | tf_op jit(solution)/shard_map/ppermute | solution.py:272
  5.2 1.6 %collective-permute-start.1 = (bf16[2,128,256]{2,1,0:T(8,128)(2,1)S(1)}, bf16[2,128,256]{2,1,0:T(8,128)(2,1)S(1)}, u32[]{:S(2)}, u32[]{:S(2)}) collective-permute-start(bf16[2,128,256]{2,1,0:T(8,128)(2,1)S(1)} %pad_maximum_fusion), channel_id=1, source_target_pairs={{0,1},{1,0},{2,3},{3,2},{4,5},{5,4},{6,7},{7,6},{8,9},{9,8},{10,11... | collective-permute-start | bytes 393224 | tf_op jit(solution)/shard_map/ppermute | solution.py:272
  6.7 1.0 %slice_bitcast_fusion = (bf16[2,32,1024]{2,1,0:T(8,128)(2,1)S(1)}, bf16[2,32,1024]{2,1,0:T(8,128)(2,1)S(1)}) fusion(bf16[1,2,384,1024]{3,2,1,0:T(8,128)(2,1)} %sec_ref.1), kind=kLoop, calls=%fused_computation.1 | loop fusion | bytes 524288 | tf_op jit(solution)/shard_map/squeeze | solution.py:287
  7.7 0.1 collective-permute-start.4
  7.8 2.6 %collective-permute-start.5 = (bf16[2,32,1024]{2,1,0:T(8,128)(2,1)S(1)}, bf16[2,32,1024]{2,1,0:T(8,128)(2,1)S(1)}, u32[]{:S(2)}, u32[]{:S(2)}) collective-permute-start(bf16[2,32,1024]{2,1,0:T(8,128)(2,1)S(1)} %get-tuple-element.15), channel_id=1, source_target_pairs={{0,28},{4,0},{8,4},{12,8},{16,12},{20,16},{24,20},{28,24},{1,29},{... | collective-permute-start | bytes 393224 | tf_op jit(solution)/shard_map/ppermute | solution.py:268
  10.4 1.1 %collective-permute-done.refs_0_.block_ref.two_ref = bf16[2,128,256]{2,1,0:T(8,128)(2,1)S(1)} collective-permute-done((bf16[2,128,256]{2,1,0:T(8,128)(2,1)S(1)}, bf16[2,128,256]{2,1,0:T(8,128)(2,1)S(1)}, u32[]{:S(2)}, u32[]{:S(2)}) %collective-permute-start) | collective-permute-done | bytes 131104 | tf_op jit(solution)/shard_map/ppermute | solution.py:272
  11.6 0.7 %collective-permute-start.3 = (bf16[2,128,256]{2,1,0:T(8,128)(2,1)S(1)}, bf16[2,128,256]{2,1,0:T(8,128)(2,1)S(1)}, u32[]{:S(2)}, u32[]{:S(2)}) collective-permute-start(bf16[2,128,256]{2,1,0:T(8,128)(2,1)S(1)} %shard_map.74), channel_id=1, source_target_pairs={{0,1},{1,0},{2,3},{3,2},{4,5},{5,4},{6,7},{7,6},{8,9},{9,8},{10,11... | collective-permute-start | bytes 393224 | tf_op jit(solution)/shard_map/ppermute | solution.py:272
  12.3 0.0 collective-permute-done.1.refs_1_.one_ref
  12.3 3.4 %collective-permute-start.2 = (bf16[2,272,256]{2,1,0:T(8,128)(2,1)S(1)}, bf16[2,272,256]{2,1,0:T(8,128)(2,1)S(1)}, u32[]{:S(2)}, u32[]{:S(2)}) collective-permute-start(bf16[2,272,256]{2,1,0:T(8,128)(2,1)S(1)} %shard_map.73), channel_id=1, source_target_pairs={{0,2},{1,3},{2,0},{3,1},{4,6},{5,7},{6,4},{7,5},{8,10},{9,11},{10,... | collective-permute-start | bytes 835592 | tf_op jit(solution)/shard_map/ppermute | solution.py:272
  15.7 0.0 collective-permute-start.8
  18.4 0.4 shard_map.75
  18.7 0.0 collective-permute-done.4.low_ref
  18.7 0.0 collective-permute-done.5.high_ref
  18.8 1.4 %shard_map.76.res_ref = bf16[4,2,384,256]{3,2,1,0:T(8,128)(2,1)S(1)} custom-call(bf16[1,2,384,1024]{3,2,1,0:T(8,128)(2,1)S(1)} %copy-done.1, bf16[2,32,1024]{2,1,0:T(8,128)(2,1)S(1)} %collective-permute-done.4.low_ref, bf16[2,32,1024]{2,1,0:T(8,128)(2,1)S(1)} %collective-permute-done.5.high_ref, bf16[128,192]{1,0:T(8,128)(2,1)S(1)} %get-tuple-element.10.az_ref, ...), custom_call_target="tpu_custom_call" | custom-call | tf_op jit(solution)/shard_map/pallas_call | solution.py:255
  20.2 0.5 %shard_map.77 = (bf16[2,64,1024]{2,1,0:T(8,128)(2,1)S(1)}, bf16[2,64,1024]{2,1,0:T(8,128)(2,1)S(1)}, f32[2,64,128]{2,1,0:T(8,128)S(1)}) custom-call(bf16[2,384,256]{2,1,0:T(8,128)(2,1)S(1)} %copy-done, bf16[2,128,256]{2,1,0:T(8,128)(2,1)S(1)} %collective-permute-done.1.refs_1_.one_ref, ...), custom_call_target="tpu_custom_call" | custom-call | tf_op jit(solution)/shard_map/pallas_call | solution.py:255
  20.7 1.6 %collective-permute-start.6 = (bf16[2,64,1024]{2,1,0:T(8,128)(2,1)S(1)}, bf16[2,64,1024]{2,1,0:T(8,128)(2,1)S(1)}, u32[]{:S(2)}, u32[]{:S(2)}) collective-permute-start(bf16[2,64,1024]{2,1,0:T(8,128)(2,1)S(1)} %get-tuple-element.13), channel_id=1, source_target_pairs={{0,28},{4,0},{8,4},{12,8},{16,12},{20,16},{24,20},{28,24},{1,29},{... | collective-permute-start | bytes 786440 | tf_op jit(solution)/shard_map/ppermute | solution.py:268
  22.3 0.8 %slice_convert_fusion = f32[64]{0:T(128)S(1)} fusion(s32[384]{0:T(512)} %param.9), kind=kLoop, calls=%fused_computation.3 | loop fusion | flops 64 | bytes 512 | tf_op jit(solution)/shard_map/convert_element_type | solution.py:308
  23.0 3.1 %collective-permute-done.6.later_ref = bf16[2,64,1024]{2,1,0:T(8,128)(2,1)S(1)} collective-permute-done((bf16[2,64,1024]{2,1,0:T(8,128)(2,1)S(1)}, bf16[2,64,1024]{2,1,0:T(8,128)(2,1)S(1)}, u32[]{:S(2)}, u32[]{:S(2)}) %collective-permute-start.6) | collective-permute-done | bytes 262176 | tf_op jit(solution)/shard_map/ppermute | solution.py:268
  26.1 0.1 broadcast_in_dim.2.weight_ref
  26.2 0.4 shard_map.78
  26.6 0.6 %collective-permute-start.7 = (f32[8,128]{1,0:T(8,128)S(1)}, f32[8,128]{1,0:T(8,128)S(1)}, u32[]{:S(2)}, u32[]{:S(2)}) collective-permute-start(f32[8,128]{1,0:T(8,128)S(1)} %shard_map.78), channel_id=1, source_target_pairs={{0,4},{4,0},{8,12},{12,8},{16,20},{20,16},{24,28},{28,24},{1,5},{5... | collective-permute-start | bytes 12296 | tf_op jit(solution)/shard_map/ppermute | solution.py:272
  27.2 1.2 %collective-permute-done.2.block_ref.two_ref = bf16[2,272,256]{2,1,0:T(8,128)(2,1)S(1)} collective-permute-done((bf16[2,272,256]{2,1,0:T(8,128)(2,1)S(1)}, bf16[2,272,256]{2,1,0:T(8,128)(2,1)S(1)}, u32[]{:S(2)}, u32[]{:S(2)}) %collective-permute-start.2) | collective-permute-done | bytes 278560 | tf_op jit(solution)/shard_map/ppermute | solution.py:272
  28.4 0.1 collective-permute-done.8.refs_1_.one_ref
  28.6 1.6 %collective-permute-start.9 = (bf16[2,256,256]{2,1,0:T(8,128)(2,1)S(1)}, bf16[2,256,256]{2,1,0:T(8,128)(2,1)S(1)}, u32[]{:S(2)}, u32[]{:S(2)}) collective-permute-start(bf16[2,256,256]{2,1,0:T(8,128)(2,1)S(1)} %shard_map.79), channel_id=1, source_target_pairs={{0,1},{1,0},{2,3},{3,2},{4,5},{5,4},{6,7},{7,6},{8,9},{9,8},{10,11... | collective-permute-start | bytes 786440 | tf_op jit(solution)/shard_map/ppermute | solution.py:272
  30.1 1.5 %collective-permute-start.10 = (f32[8,128]{1,0:T(8,128)S(1)}, f32[8,128]{1,0:T(8,128)S(1)}, u32[]{:S(2)}, u32[]{:S(2)}) collective-permute-start(f32[8,128]{1,0:T(8,128)S(1)} %add.6), channel_id=1, source_target_pairs={{0,8},{4,12},{8,0},{12,4},{16,24},{20,28},{24,16},{28,20},{1,9},{5... | collective-permute-start | bytes 12296 | tf_op jit(solution)/shard_map/ppermute | solution.py:272
  31.6 2.1 %collective-permute-done.10 = f32[8,128]{1,0:T(8,128)S(1)} collective-permute-done((f32[8,128]{1,0:T(8,128)S(1)}, f32[8,128]{1,0:T(8,128)S(1)}, u32[]{:S(2)}, u32[]{:S(2)}) %collective-permute-start.10) | collective-permute-done | bytes 4128 | tf_op jit(solution)/shard_map/ppermute | solution.py:272
  33.8 1.5 %collective-permute-start.11 = (f32[8,128]{1,0:T(8,128)S(1)}, f32[8,128]{1,0:T(8,128)S(1)}, u32[]{:S(2)}, u32[]{:S(2)}) collective-permute-start(f32[8,128]{1,0:T(8,128)S(1)} %add.7.mine_ref), channel_id=1, source_target_pairs={{0,16},{4,20},{8,24},{12,28},{16,0},{20,4},{24,8},{28,12},{1,17},{... | collective-permute-start | bytes 12296 | tf_op jit(solution)/shard_map/ppermute | solution.py:272
  35.3 0.6 %shard_map.80.before_ref = f32[2,256,128]{2,1,0:T(8,128)S(1)} custom-call(bf16[2,384,256]{2,1,0:T(8,128)(2,1)S(1)} %copy-done, bf16[2,272,256]{2,1,0:T(8,128)(2,1)S(1)} %collective-permute-done.8.refs_1_.one_ref, bf16[2,272,256]{2,1,0:T(8,128)(2,1)S(1)} %collective-permute-done.2.block_ref.two_ref, bf16[4,2,384,256]{3,2,1,0:T(8,128)(2,1)S(1)} %shard_map.76.res_ref), custom_call_target="tpu_custom_call" | custom-call | flops 134217728 | bytes 3145728 | tf_op jit(solution)/shard_map/pallas_call | solution.py:255
  35.9 1.5 %collective-permute-done.11.other_ref = f32[8,128]{1,0:T(8,128)S(1)} collective-permute-done((f32[8,128]{1,0:T(8,128)S(1)}, f32[8,128]{1,0:T(8,128)S(1)}, u32[]{:S(2)}, u32[]{:S(2)}) %collective-permute-start.11) | collective-permute-done | bytes 4128 | tf_op jit(solution)/shard_map/ppermute | solution.py:272
  37.4 0.1 shard_map.81.unit_ref
  37.5 0.9 %shard_map.82 = f32[1,2,192,128]{3,2,1,0:T(8,128)} custom-call(bf16[2,256,256]{2,1,0:T(8,128)(2,1)S(1)} %collective-permute-done.9.three_ref, bf16[4,2,384,256]{3,2,1,0:T(8,128)(2,1)S(1)} %shard_map.76.res_ref, f32[2,256,128]{2,1,0:T(8,128)S(1)} %shard_map.80.before_ref, f32[2,64,128]{2,1,0:T(8,128)S(1)} %get-tuple-element.14.looks_ref, ...), custom_call_target="tpu_custom_call" | custom-call | flops 67108864 | bytes 1572864 | tf_op jit(solution)/shard_map/pallas_call | solution.py:255
  (13 shorter events, 0.1 us)
Async XLA Ops:
  0.0 12.3 %copy-start = (bf16[2,384,256]{2,1,0:T(8,128)(2,1)S(1)}, bf16[2,384,256]{2,1,0:T(8,128)(2,1)}, u32[]{:S(2)}) copy-start(bf16[2,384,256]{2,1,0:T(8,128)(2,1)} %own_ref.3) | copy-start | bytes 1179652
  0.0 18.7 %copy-start.1 = (bf16[1,2,384,1024]{3,2,1,0:T(8,128)(2,1)S(1)}, bf16[1,2,384,1024]{3,2,1,0:T(8,128)(2,1)}, u32[]{:S(2)}) copy-start(bf16[1,2,384,1024]{3,2,1,0:T(8,128)(2,1)} %sec_ref.1) | copy-start | bytes 4718596
  1.0 10.5 %collective-permute-start = (bf16[2,128,256]{2,1,0:T(8,128)(2,1)S(1)}, bf16[2,128,256]{2,1,0:T(8,128)(2,1)S(1)}, u32[]{:S(2)}, u32[]{:S(2)}) collective-permute-start(bf16[2,128,256]{2,1,0:T(8,128)(2,1)S(1)} %pad_maximum_fusion), channel_id=1, source_target_pairs={{0,2},{1,3},{2,0},{3,1},{4,6},{5,7},{6,4},{7,5},{8,10},{9,11},{10,... | collective-permute-start | bytes 393224 | tf_op jit(solution)/shard_map/ppermute | solution.py:272
  5.2 7.1 %collective-permute-start.1 = (bf16[2,128,256]{2,1,0:T(8,128)(2,1)S(1)}, bf16[2,128,256]{2,1,0:T(8,128)(2,1)S(1)}, u32[]{:S(2)}, u32[]{:S(2)}) collective-permute-start(bf16[2,128,256]{2,1,0:T(8,128)(2,1)S(1)} %pad_maximum_fusion), channel_id=1, source_target_pairs={{0,1},{1,0},{2,3},{3,2},{4,5},{5,4},{6,7},{7,6},{8,9},{9,8},{10,11... | collective-permute-start | bytes 393224 | tf_op jit(solution)/shard_map/ppermute | solution.py:272
  7.7 11.0 %collective-permute-start.4 = (bf16[2,32,1024]{2,1,0:T(8,128)(2,1)S(1)}, bf16[2,32,1024]{2,1,0:T(8,128)(2,1)S(1)}, u32[]{:S(2)}, u32[]{:S(2)}) collective-permute-start(bf16[2,32,1024]{2,1,0:T(8,128)(2,1)S(1)} %get-tuple-element.16), channel_id=1, source_target_pairs={{0,4},{4,8},{8,12},{12,16},{16,20},{20,24},{24,28},{28,0},{1,5},{5... | collective-permute-start | bytes 393224 | tf_op jit(solution)/shard_map/ppermute | solution.py:268
  7.8 11.0 %collective-permute-start.5 = (bf16[2,32,1024]{2,1,0:T(8,128)(2,1)S(1)}, bf16[2,32,1024]{2,1,0:T(8,128)(2,1)S(1)}, u32[]{:S(2)}, u32[]{:S(2)}) collective-permute-start(bf16[2,32,1024]{2,1,0:T(8,128)(2,1)S(1)} %get-tuple-element.15), channel_id=1, source_target_pairs={{0,28},{4,0},{8,4},{12,8},{16,12},{20,16},{24,20},{28,24},{1,29},{... | collective-permute-start | bytes 393224 | tf_op jit(solution)/shard_map/ppermute | solution.py:268
  11.6 8.6 %collective-permute-start.3 = (bf16[2,128,256]{2,1,0:T(8,128)(2,1)S(1)}, bf16[2,128,256]{2,1,0:T(8,128)(2,1)S(1)}, u32[]{:S(2)}, u32[]{:S(2)}) collective-permute-start(bf16[2,128,256]{2,1,0:T(8,128)(2,1)S(1)} %shard_map.74), channel_id=1, source_target_pairs={{0,1},{1,0},{2,3},{3,2},{4,5},{5,4},{6,7},{7,6},{8,9},{9,8},{10,11... | collective-permute-start | bytes 393224 | tf_op jit(solution)/shard_map/ppermute | solution.py:272
  12.3 16.1 %collective-permute-start.2 = (bf16[2,272,256]{2,1,0:T(8,128)(2,1)S(1)}, bf16[2,272,256]{2,1,0:T(8,128)(2,1)S(1)}, u32[]{:S(2)}, u32[]{:S(2)}) collective-permute-start(bf16[2,272,256]{2,1,0:T(8,128)(2,1)S(1)} %shard_map.73), channel_id=1, source_target_pairs={{0,2},{1,3},{2,0},{3,1},{4,6},{5,7},{6,4},{7,5},{8,10},{9,11},{10,... | collective-permute-start | bytes 835592 | tf_op jit(solution)/shard_map/ppermute | solution.py:272
  15.7 12.8 %collective-permute-start.8 = (bf16[2,272,256]{2,1,0:T(8,128)(2,1)S(1)}, bf16[2,272,256]{2,1,0:T(8,128)(2,1)S(1)}, u32[]{:S(2)}, u32[]{:S(2)}) collective-permute-start(bf16[2,272,256]{2,1,0:T(8,128)(2,1)S(1)} %shard_map.73), channel_id=1, source_target_pairs={{0,1},{1,0},{2,3},{3,2},{4,5},{5,4},{6,7},{7,6},{8,9},{9,8},{10,11... | collective-permute-start | bytes 835592 | tf_op jit(solution)/shard_map/ppermute | solution.py:272
  20.7 5.5 %collective-permute-start.6 = (bf16[2,64,1024]{2,1,0:T(8,128)(2,1)S(1)}, bf16[2,64,1024]{2,1,0:T(8,128)(2,1)S(1)}, u32[]{:S(2)}, u32[]{:S(2)}) collective-permute-start(bf16[2,64,1024]{2,1,0:T(8,128)(2,1)S(1)} %get-tuple-element.13), channel_id=1, source_target_pairs={{0,28},{4,0},{8,4},{12,8},{16,12},{20,16},{24,20},{28,24},{1,29},{... | collective-permute-start | bytes 786440 | tf_op jit(solution)/shard_map/ppermute | solution.py:268
  26.6 2.0 %collective-permute-start.7 = (f32[8,128]{1,0:T(8,128)S(1)}, f32[8,128]{1,0:T(8,128)S(1)}, u32[]{:S(2)}, u32[]{:S(2)}) collective-permute-start(f32[8,128]{1,0:T(8,128)S(1)} %shard_map.78), channel_id=1, source_target_pairs={{0,4},{4,0},{8,12},{12,8},{16,20},{20,16},{24,28},{28,24},{1,5},{5... | collective-permute-start | bytes 12296 | tf_op jit(solution)/shard_map/ppermute | solution.py:272
  28.6 8.9 %collective-permute-start.9 = (bf16[2,256,256]{2,1,0:T(8,128)(2,1)S(1)}, bf16[2,256,256]{2,1,0:T(8,128)(2,1)S(1)}, u32[]{:S(2)}, u32[]{:S(2)}) collective-permute-start(bf16[2,256,256]{2,1,0:T(8,128)(2,1)S(1)} %shard_map.79), channel_id=1, source_target_pairs={{0,1},{1,0},{2,3},{3,2},{4,5},{5,4},{6,7},{7,6},{8,9},{9,8},{10,11... | collective-permute-start | bytes 786440 | tf_op jit(solution)/shard_map/ppermute | solution.py:272
  30.1 3.6 %collective-permute-start.10 = (f32[8,128]{1,0:T(8,128)S(1)}, f32[8,128]{1,0:T(8,128)S(1)}, u32[]{:S(2)}, u32[]{:S(2)}) collective-permute-start(f32[8,128]{1,0:T(8,128)S(1)} %add.6), channel_id=1, source_target_pairs={{0,8},{4,12},{8,0},{12,4},{16,24},{20,28},{24,16},{28,20},{1,9},{5... | collective-permute-start | bytes 12296 | tf_op jit(solution)/shard_map/ppermute | solution.py:272
  33.8 3.6 %collective-permute-start.11 = (f32[8,128]{1,0:T(8,128)S(1)}, f32[8,128]{1,0:T(8,128)S(1)}, u32[]{:S(2)}, u32[]{:S(2)}) collective-permute-start(f32[8,128]{1,0:T(8,128)S(1)} %add.7.mine_ref), channel_id=1, source_target_pairs={{0,16},{4,20},{8,24},{12,28},{16,0},{20,4},{24,8},{28,12},{1,17},{... | collective-permute-start | bytes 12296 | tf_op jit(solution)/shard_map/ppermute | solution.py:272

commit v26 on v24

--- a/solution.py
+++ b/solution.py
@@ -13,6 +13,7 @@
 LR = 8
 LANE = 128
 BAND = 128
+CHUNK = 64
 HALO = 32
 VMEM_LIMIT = 40 * 1024 * 1024
 
@@ -180,33 +181,40 @@
     stats_ref[...] = jnp.concatenate(rows, axis=0)
 
 
-def look_sums(pieces, res_ref, looks_n):
+def look_sums(pieces, res_ref, out_ref, before_ref=None):
     here = lax.axis_index("date")
     _, _, rows_n, width = res_ref.shape
-    middle_n = rows_n - 2 * LAG
-    totals = [None, None]
-    for at, (step, prim_ref) in enumerate(pieces):
+    plan = []
+    for step, prim_ref in pieces:
         block = jnp.bitwise_xor(here, step)
         first = LAG if prim_ref.shape[1] == rows_n else 0
-        select = look_columns(width, block, looks_n)
-        pair = interfere(
-            prim_ref[0, first : first + middle_n],
-            prim_ref[1, first : first + middle_n],
-            res_ref[block, 0, LAG : rows_n - LAG],
-            res_ref[block, 1, LAG : rows_n - LAG],
-        )
+        plan.append((block, prim_ref, first, look_columns(width, block, out_ref.shape[2])))
+
+    def chunk(at, carry):
+        start = pl.multiple_of(at * CHUNK, CHUNK)
+        rows = pl.ds(start, CHUNK)
+        totals = [None, None] if before_ref is None else [before_ref[part, rows] for part in range(2)]
+        for block, prim_ref, first, select in plan:
+            held = pl.ds(pl.multiple_of(start + first, CHUNK), CHUNK)
+            taken = pl.ds(pl.multiple_of(start + LAG, CHUNK), CHUNK)
+            pair = interfere(
+                prim_ref[0, held], prim_ref[1, held],
+                res_ref[block, 0, taken], res_ref[block, 1, taken],
+            )
+            for part in range(2):
+                summed = jnp.dot(
+                    pair[part].astype(jnp.bfloat16), select, preferred_element_type=jnp.float32
+                )
+                totals[part] = summed if totals[part] is None else totals[part] + summed
         for part in range(2):
-            summed = jnp.dot(
-                pair[part].astype(jnp.bfloat16), select, preferred_element_type=jnp.float32
-            )
-            totals[part] = summed if at == 0 else totals[part] + summed
-    return totals
+            out_ref[part, rows] = totals[part]
+        return carry
+
+    lax.fori_loop(0, (rows_n - 2 * LAG) // CHUNK, chunk, 0)
 
 
 def middle_kernel(own_ref, one_ref, two_ref, res_ref, out_ref):
-    pieces = ((0, own_ref), (1, one_ref), (2, two_ref))
-    for part, total in enumerate(look_sums(pieces, res_ref, out_ref.shape[2])):
-        out_ref[part] = total
+    look_sums(((0, own_ref), (1, one_ref), (2, two_ref)), res_ref, out_ref)
 
 
 def unit_kernel(mine_ref, other_ref, unit_ref):
@@ -223,9 +231,7 @@
     middle_n = before_ref.shape[1]
     edge = LAG // LA
     u_re, u_im = unit_ref[0:1], unit_ref[1:2]
-    totals = look_sums(((3, three_ref),), res_ref, out_ref.shape[3])
-    for part, total in enumerate(totals):
-        sums_ref[part] = total + before_ref[part]
+    look_sums(((3, three_ref),), res_ref, sums_ref, before_ref)
     for at, held in (
         (0, looks_ref[:, :edge]),
         (edge, [look_rows(sums_ref, part, 0, middle_n) for part in range(2)]),

time: 38.7 us -> 39.1 us (1.010)
  Pallas kernels: 4.38 us -> 5.38 us
  waiting for transfers between devices: 9.24 us -> 8.69 us
    pallas_call x10, Pallas kernels: 4.38 us -> 5.38 us  [call(): pl.pallas_call(kernel, out_shape=outs, in_specs=[vmem] * len(args), out_s...]
    ppermute x9, waiting for transfers between devices: 6.09 us -> 5.54 us  [swap(): lax.ppermute(value, axis, [(at, at ^ step) for at in range(lax.axis_size(...]
  transfers between devices with their start and end apart: 12 -> 12, of which waited for: 6 -> 6; matrix products, arithmetic and copies ran while one was open for 5% -> 5% of each run, Pallas kernels for 9% -> 10%
where the time goes in v26:
time: 39.1 us; the launch traced here: 38.9 us
  starting transfers between devices  19.3 us (49%)
  waiting for transfers between devices  8.69 us (22%)
  Pallas kernels  5.38 us (14%)
  between operations  2.72 us (7%)
  local copies, waits for them, and re-layouts  2.09 us (5%)
  other arithmetic  0.77 us (2%)
    ppermute x9, starting transfers between devices, swap(): lax.ppermute(value, axis, [(at, at ^ step) for at in range(lax.axis_size(...  15 us
    ppermute x9, waiting for transfers between devices, swap(): lax.ppermute(value, axis, [(at, at ^ step) for at in range(lax.axis_size(...  5.54 us
    pallas_call x10, Pallas kernels, call(): pl.pallas_call(kernel, out_shape=outs, in_specs=[vmem] * len(args), out_s...  5.38 us
    ppermute x3, starting transfers between devices, ring(): lax.ppermute(value, axis, [(at, (at + step) % count) for at in range(coun...  4.25 us
    ppermute x3, waiting for transfers between devices, ring(): lax.ppermute(value, axis, [(at, (at + step) % count) for at in range(coun...  3.14 us
    slice x1, local copies, waits for them, and re-layouts, fused(): primary[:, :LAG]  1.02 us
    squeeze x1, local copies, waits for them, and re-layouts, fused(): down, up = (secondary[0, :, rows_n - HALO:], secondary[0, :, :HALO])  0.99 us
  transfers between devices with their start and end apart: 12, of which 6 were waited for; matrix products, arithmetic and copies ran while one was open for 5% of the time, Pallas kernels for 10%

profile of v26, /device:TPU:0, one launch (start us, length us, event | category | flops | bytes accessed | tf_op | source)
XLA Modules:
  0.0 38.9 jit_solution(1391845697462090502)
XLA Ops:
  0.0 1.0 %fusion = (bf16[2,64,256]{2,1,0:T(8,128)(2,1)S(1)}, bf16[2,64,256]{2,1,0:T(8,128)(2,1)S(1)}) fusion(bf16[2,384,256]{2,1,0:T(8,128)(2,1)} %own_ref.3), kind=kLoop, calls=%fused_computation.4 | loop fusion | bytes 262144 | tf_op jit(solution)/shard_map/slice | solution.py:276
  1.0 4.1 %collective-permute-start = (bf16[2,128,256]{2,1,0:T(8,128)(2,1)S(1)}, bf16[2,128,256]{2,1,0:T(8,128)(2,1)S(1)}, u32[]{:S(2)}, u32[]{:S(2)}) collective-permute-start(bf16[2,128,256]{2,1,0:T(8,128)(2,1)S(1)} %pad_maximum_fusion), channel_id=1, source_target_pairs={{0,2},{1,3},{2,0},{3,1},{4,6},{5,7},{6,4},{7,5},{8,10},{9,11},{10,... | collective-permute-start | bytes 393224 | tf_op jit(solution)/shard_map/ppermute | solution.py:264
  5.2 1.6 %collective-permute-start.1 = (bf16[2,128,256]{2,1,0:T(8,128)(2,1)S(1)}, bf16[2,128,256]{2,1,0:T(8,128)(2,1)S(1)}, u32[]{:S(2)}, u32[]{:S(2)}) collective-permute-start(bf16[2,128,256]{2,1,0:T(8,128)(2,1)S(1)} %pad_maximum_fusion), channel_id=1, source_target_pairs={{0,1},{1,0},{2,3},{3,2},{4,5},{5,4},{6,7},{7,6},{8,9},{9,8},{10,11... | collective-permute-start | bytes 393224 | tf_op jit(solution)/shard_map/ppermute | solution.py:264
  6.7 1.0 %slice_bitcast_fusion = (bf16[2,32,1024]{2,1,0:T(8,128)(2,1)S(1)}, bf16[2,32,1024]{2,1,0:T(8,128)(2,1)S(1)}) fusion(bf16[1,2,384,1024]{3,2,1,0:T(8,128)(2,1)} %sec_ref.1), kind=kLoop, calls=%fused_computation.1 | loop fusion | bytes 524288 | tf_op jit(solution)/shard_map/squeeze | solution.py:279
  7.7 0.1 collective-permute-start.4
  7.8 2.6 %collective-permute-start.5 = (bf16[2,32,1024]{2,1,0:T(8,128)(2,1)S(1)}, bf16[2,32,1024]{2,1,0:T(8,128)(2,1)S(1)}, u32[]{:S(2)}, u32[]{:S(2)}) collective-permute-start(bf16[2,32,1024]{2,1,0:T(8,128)(2,1)S(1)} %get-tuple-element.15), channel_id=1, source_target_pairs={{0,28},{4,0},{8,4},{12,8},{16,12},{20,16},{24,20},{28,24},{1,29},{... | collective-permute-start | bytes 393224 | tf_op jit(solution)/shard_map/ppermute | solution.py:260
  10.4 1.1 %collective-permute-done.refs_0_.block_ref.two_ref = bf16[2,128,256]{2,1,0:T(8,128)(2,1)S(1)} collective-permute-done((bf16[2,128,256]{2,1,0:T(8,128)(2,1)S(1)}, bf16[2,128,256]{2,1,0:T(8,128)(2,1)S(1)}, u32[]{:S(2)}, u32[]{:S(2)}) %collective-permute-start) | collective-permute-done | bytes 131104 | tf_op jit(solution)/shard_map/ppermute | solution.py:264
  11.6 0.7 %collective-permute-start.3 = (bf16[2,128,256]{2,1,0:T(8,128)(2,1)S(1)}, bf16[2,128,256]{2,1,0:T(8,128)(2,1)S(1)}, u32[]{:S(2)}, u32[]{:S(2)}) collective-permute-start(bf16[2,128,256]{2,1,0:T(8,128)(2,1)S(1)} %shard_map.74), channel_id=1, source_target_pairs={{0,1},{1,0},{2,3},{3,2},{4,5},{5,4},{6,7},{7,6},{8,9},{9,8},{10,11... | collective-permute-start | bytes 393224 | tf_op jit(solution)/shard_map/ppermute | solution.py:264
  12.3 0.0 collective-permute-done.1.refs_1_.one_ref
  12.3 3.4 %collective-permute-start.2 = (bf16[2,272,256]{2,1,0:T(8,128)(2,1)S(1)}, bf16[2,272,256]{2,1,0:T(8,128)(2,1)S(1)}, u32[]{:S(2)}, u32[]{:S(2)}) collective-permute-start(bf16[2,272,256]{2,1,0:T(8,128)(2,1)S(1)} %shard_map.73), channel_id=1, source_target_pairs={{0,2},{1,3},{2,0},{3,1},{4,6},{5,7},{6,4},{7,5},{8,10},{9,11},{10,... | collective-permute-start | bytes 835592 | tf_op jit(solution)/shard_map/ppermute | solution.py:264
  15.7 0.0 collective-permute-start.8
  18.4 0.4 shard_map.75
  18.7 0.0 collective-permute-done.5.high_ref
  18.8 1.4 %shard_map.76.res_ref = bf16[4,2,384,256]{3,2,1,0:T(8,128)(2,1)S(1)} custom-call(bf16[1,2,384,1024]{3,2,1,0:T(8,128)(2,1)S(1)} %copy-done.1, bf16[2,32,1024]{2,1,0:T(8,128)(2,1)S(1)} %collective-permute-done.4.low_ref, bf16[2,32,1024]{2,1,0:T(8,128)(2,1)S(1)} %collective-permute-done.5.high_ref, bf16[128,192]{1,0:T(8,128)(2,1)S(1)} %get-tuple-element.10.az_ref, ...), custom_call_target="tpu_custom_call" | custom-call | tf_op jit(solution)/shard_map/pallas_call | solution.py:247
  20.2 0.5 %shard_map.77 = (bf16[2,64,1024]{2,1,0:T(8,128)(2,1)S(1)}, bf16[2,64,1024]{2,1,0:T(8,128)(2,1)S(1)}, f32[2,64,128]{2,1,0:T(8,128)S(1)}) custom-call(bf16[2,384,256]{2,1,0:T(8,128)(2,1)S(1)} %copy-done, bf16[2,128,256]{2,1,0:T(8,128)(2,1)S(1)} %collective-permute-done.1.refs_1_.one_ref, ...), custom_call_target="tpu_custom_call" | custom-call | tf_op jit(solution)/shard_map/pallas_call | solution.py:247
  20.7 1.6 %collective-permute-start.6 = (bf16[2,64,1024]{2,1,0:T(8,128)(2,1)S(1)}, bf16[2,64,1024]{2,1,0:T(8,128)(2,1)S(1)}, u32[]{:S(2)}, u32[]{:S(2)}) collective-permute-start(bf16[2,64,1024]{2,1,0:T(8,128)(2,1)S(1)} %get-tuple-element.13), channel_id=1, source_target_pairs={{0,28},{4,0},{8,4},{12,8},{16,12},{20,16},{24,20},{28,24},{1,29},{... | collective-permute-start | bytes 786440 | tf_op jit(solution)/shard_map/ppermute | solution.py:260
  22.3 0.8 %slice_convert_fusion = f32[64]{0:T(128)S(1)} fusion(s32[384]{0:T(512)} %param.9), kind=kLoop, calls=%fused_computation.3 | loop fusion | flops 64 | bytes 512 | tf_op jit(solution)/shard_map/convert_element_type | solution.py:300
  23.0 3.1 %collective-permute-done.6.later_ref = bf16[2,64,1024]{2,1,0:T(8,128)(2,1)S(1)} collective-permute-done((bf16[2,64,1024]{2,1,0:T(8,128)(2,1)S(1)}, bf16[2,64,1024]{2,1,0:T(8,128)(2,1)S(1)}, u32[]{:S(2)}, u32[]{:S(2)}) %collective-permute-start.6) | collective-permute-done | bytes 262176 | tf_op jit(solution)/shard_map/ppermute | solution.py:260
  26.1 0.1 broadcast_in_dim.2.weight_ref
  26.2 0.4 shard_map.78
  26.6 0.6 %collective-permute-start.7 = (f32[8,128]{1,0:T(8,128)S(1)}, f32[8,128]{1,0:T(8,128)S(1)}, u32[]{:S(2)}, u32[]{:S(2)}) collective-permute-start(f32[8,128]{1,0:T(8,128)S(1)} %shard_map.78), channel_id=1, source_target_pairs={{0,4},{4,0},{8,12},{12,8},{16,20},{20,16},{24,28},{28,24},{1,5},{5... | collective-permute-start | bytes 12296 | tf_op jit(solution)/shard_map/ppermute | solution.py:264
  27.2 1.2 %collective-permute-done.2.block_ref.two_ref = bf16[2,272,256]{2,1,0:T(8,128)(2,1)S(1)} collective-permute-done((bf16[2,272,256]{2,1,0:T(8,128)(2,1)S(1)}, bf16[2,272,256]{2,1,0:T(8,128)(2,1)S(1)}, u32[]{:S(2)}, u32[]{:S(2)}) %collective-permute-start.2) | collective-permute-done | bytes 278560 | tf_op jit(solution)/shard_map/ppermute | solution.py:264
  28.4 0.1 collective-permute-done.8.refs_1_.one_ref
  28.5 0.0 collective-permute-done.7.refs_0_
  28.6 1.6 %collective-permute-start.9 = (bf16[2,256,256]{2,1,0:T(8,128)(2,1)S(1)}, bf16[2,256,256]{2,1,0:T(8,128)(2,1)S(1)}, u32[]{:S(2)}, u32[]{:S(2)}) collective-permute-start(bf16[2,256,256]{2,1,0:T(8,128)(2,1)S(1)} %shard_map.79), channel_id=1, source_target_pairs={{0,1},{1,0},{2,3},{3,2},{4,5},{5,4},{6,7},{7,6},{8,9},{9,8},{10,11... | collective-permute-start | bytes 786440 | tf_op jit(solution)/shard_map/ppermute | solution.py:264
  30.1 1.5 %collective-permute-start.10 = (f32[8,128]{1,0:T(8,128)S(1)}, f32[8,128]{1,0:T(8,128)S(1)}, u32[]{:S(2)}, u32[]{:S(2)}) collective-permute-start(f32[8,128]{1,0:T(8,128)S(1)} %add.6), channel_id=1, source_target_pairs={{0,8},{4,12},{8,0},{12,4},{16,24},{20,28},{24,16},{28,20},{1,9},{5... | collective-permute-start | bytes 12296 | tf_op jit(solution)/shard_map/ppermute | solution.py:264
  31.6 2.1 %collective-permute-done.10 = f32[8,128]{1,0:T(8,128)S(1)} collective-permute-done((f32[8,128]{1,0:T(8,128)S(1)}, f32[8,128]{1,0:T(8,128)S(1)}, u32[]{:S(2)}, u32[]{:S(2)}) %collective-permute-start.10) | collective-permute-done | bytes 4128 | tf_op jit(solution)/shard_map/ppermute | solution.py:264
  33.8 1.5 %collective-permute-start.11 = (f32[8,128]{1,0:T(8,128)S(1)}, f32[8,128]{1,0:T(8,128)S(1)}, u32[]{:S(2)}, u32[]{:S(2)}) collective-permute-start(f32[8,128]{1,0:T(8,128)S(1)} %add.7.mine_ref), channel_id=1, source_target_pairs={{0,16},{4,20},{8,24},{12,28},{16,0},{20,4},{24,8},{28,12},{1,17},{... | collective-permute-start | bytes 12296 | tf_op jit(solution)/shard_map/ppermute | solution.py:264
  35.3 1.2 %shard_map.80.before_ref = f32[2,256,128]{2,1,0:T(8,128)S(1)} custom-call(bf16[2,384,256]{2,1,0:T(8,128)(2,1)S(1)} %copy-done, bf16[2,272,256]{2,1,0:T(8,128)(2,1)S(1)} %collective-permute-done.8.refs_1_.one_ref, bf16[2,272,256]{2,1,0:T(8,128)(2,1)S(1)} %collective-permute-done.2.block_ref.two_ref, bf16[4,2,384,256]{3,2,1,0:T(8,128)(2,1)S(1)} %shard_map.76.res_ref), custom_call_target="tpu_custom_call" | custom-call | flops 134217728 | bytes 3145728 | tf_op jit(solution)/shard_map/pallas_call | solution.py:247
  36.4 0.9 %collective-permute-done.11.other_ref = f32[8,128]{1,0:T(8,128)S(1)} collective-permute-done((f32[8,128]{1,0:T(8,128)S(1)}, f32[8,128]{1,0:T(8,128)S(1)}, u32[]{:S(2)}, u32[]{:S(2)}) %collective-permute-start.11) | collective-permute-done | bytes 4128 | tf_op jit(solution)/shard_map/ppermute | solution.py:264
  37.4 0.1 shard_map.81.unit_ref
  37.5 1.4 %shard_map.82 = f32[1,2,192,128]{3,2,1,0:T(8,128)} custom-call(bf16[2,256,256]{2,1,0:T(8,128)(2,1)S(1)} %collective-permute-done.9.three_ref, bf16[4,2,384,256]{3,2,1,0:T(8,128)(2,1)S(1)} %shard_map.76.res_ref, f32[2,256,128]{2,1,0:T(8,128)S(1)} %shard_map.80.before_ref, f32[2,64,128]{2,1,0:T(8,128)S(1)} %get-tuple-element.14.looks_ref, ...), custom_call_target="tpu_custom_call" | custom-call | flops 67108864 | bytes 1572864 | tf_op jit(solution)/shard_map/pallas_call | solution.py:247
  (13 shorter events, 0.1 us)
Async XLA Ops:
  0.0 12.3 %copy-start = (bf16[2,384,256]{2,1,0:T(8,128)(2,1)S(1)}, bf16[2,384,256]{2,1,0:T(8,128)(2,1)}, u32[]{:S(2)}) copy-start(bf16[2,384,256]{2,1,0:T(8,128)(2,1)} %own_ref.3) | copy-start | bytes 1179652
  0.0 18.7 %copy-start.1 = (bf16[1,2,384,1024]{3,2,1,0:T(8,128)(2,1)S(1)}, bf16[1,2,384,1024]{3,2,1,0:T(8,128)(2,1)}, u32[]{:S(2)}) copy-start(bf16[1,2,384,1024]{3,2,1,0:T(8,128)(2,1)} %sec_ref.1) | copy-start | bytes 4718596
  1.0 10.5 %collective-permute-start = (bf16[2,128,256]{2,1,0:T(8,128)(2,1)S(1)}, bf16[2,128,256]{2,1,0:T(8,128)(2,1)S(1)}, u32[]{:S(2)}, u32[]{:S(2)}) collective-permute-start(bf16[2,128,256]{2,1,0:T(8,128)(2,1)S(1)} %pad_maximum_fusion), channel_id=1, source_target_pairs={{0,2},{1,3},{2,0},{3,1},{4,6},{5,7},{6,4},{7,5},{8,10},{9,11},{10,... | collective-permute-start | bytes 393224 | tf_op jit(solution)/shard_map/ppermute | solution.py:264
  5.2 7.1 %collective-permute-start.1 = (bf16[2,128,256]{2,1,0:T(8,128)(2,1)S(1)}, bf16[2,128,256]{2,1,0:T(8,128)(2,1)S(1)}, u32[]{:S(2)}, u32[]{:S(2)}) collective-permute-start(bf16[2,128,256]{2,1,0:T(8,128)(2,1)S(1)} %pad_maximum_fusion), channel_id=1, source_target_pairs={{0,1},{1,0},{2,3},{3,2},{4,5},{5,4},{6,7},{7,6},{8,9},{9,8},{10,11... | collective-permute-start | bytes 393224 | tf_op jit(solution)/shard_map/ppermute | solution.py:264
  7.7 11.0 %collective-permute-start.4 = (bf16[2,32,1024]{2,1,0:T(8,128)(2,1)S(1)}, bf16[2,32,1024]{2,1,0:T(8,128)(2,1)S(1)}, u32[]{:S(2)}, u32[]{:S(2)}) collective-permute-start(bf16[2,32,1024]{2,1,0:T(8,128)(2,1)S(1)} %get-tuple-element.16), channel_id=1, source_target_pairs={{0,4},{4,8},{8,12},{12,16},{16,20},{20,24},{24,28},{28,0},{1,5},{5... | collective-permute-start | bytes 393224 | tf_op jit(solution)/shard_map/ppermute | solution.py:260
  7.8 11.0 %collective-permute-start.5 = (bf16[2,32,1024]{2,1,0:T(8,128)(2,1)S(1)}, bf16[2,32,1024]{2,1,0:T(8,128)(2,1)S(1)}, u32[]{:S(2)}, u32[]{:S(2)}) collective-permute-start(bf16[2,32,1024]{2,1,0:T(8,128)(2,1)S(1)} %get-tuple-element.15), channel_id=1, source_target_pairs={{0,28},{4,0},{8,4},{12,8},{16,12},{20,16},{24,20},{28,24},{1,29},{... | collective-permute-start | bytes 393224 | tf_op jit(solution)/shard_map/ppermute | solution.py:260
  11.6 8.6 %collective-permute-start.3 = (bf16[2,128,256]{2,1,0:T(8,128)(2,1)S(1)}, bf16[2,128,256]{2,1,0:T(8,128)(2,1)S(1)}, u32[]{:S(2)}, u32[]{:S(2)}) collective-permute-start(bf16[2,128,256]{2,1,0:T(8,128)(2,1)S(1)} %shard_map.74), channel_id=1, source_target_pairs={{0,1},{1,0},{2,3},{3,2},{4,5},{5,4},{6,7},{7,6},{8,9},{9,8},{10,11... | collective-permute-start | bytes 393224 | tf_op jit(solution)/shard_map/ppermute | solution.py:264
  12.3 16.1 %collective-permute-start.2 = (bf16[2,272,256]{2,1,0:T(8,128)(2,1)S(1)}, bf16[2,272,256]{2,1,0:T(8,128)(2,1)S(1)}, u32[]{:S(2)}, u32[]{:S(2)}) collective-permute-start(bf16[2,272,256]{2,1,0:T(8,128)(2,1)S(1)} %shard_map.73), channel_id=1, source_target_pairs={{0,2},{1,3},{2,0},{3,1},{4,6},{5,7},{6,4},{7,5},{8,10},{9,11},{10,... | collective-permute-start | bytes 835592 | tf_op jit(solution)/shard_map/ppermute | solution.py:264
  15.7 12.8 %collective-permute-start.8 = (bf16[2,272,256]{2,1,0:T(8,128)(2,1)S(1)}, bf16[2,272,256]{2,1,0:T(8,128)(2,1)S(1)}, u32[]{:S(2)}, u32[]{:S(2)}) collective-permute-start(bf16[2,272,256]{2,1,0:T(8,128)(2,1)S(1)} %shard_map.73), channel_id=1, source_target_pairs={{0,1},{1,0},{2,3},{3,2},{4,5},{5,4},{6,7},{7,6},{8,9},{9,8},{10,11... | collective-permute-start | bytes 835592 | tf_op jit(solution)/shard_map/ppermute | solution.py:264
  20.7 5.5 %collective-permute-start.6 = (bf16[2,64,1024]{2,1,0:T(8,128)(2,1)S(1)}, bf16[2,64,1024]{2,1,0:T(8,128)(2,1)S(1)}, u32[]{:S(2)}, u32[]{:S(2)}) collective-permute-start(bf16[2,64,1024]{2,1,0:T(8,128)(2,1)S(1)} %get-tuple-element.13), channel_id=1, source_target_pairs={{0,28},{4,0},{8,4},{12,8},{16,12},{20,16},{24,20},{28,24},{1,29},{... | collective-permute-start | bytes 786440 | tf_op jit(solution)/shard_map/ppermute | solution.py:260
  26.6 2.0 %collective-permute-start.7 = (f32[8,128]{1,0:T(8,128)S(1)}, f32[8,128]{1,0:T(8,128)S(1)}, u32[]{:S(2)}, u32[]{:S(2)}) collective-permute-start(f32[8,128]{1,0:T(8,128)S(1)} %shard_map.78), channel_id=1, source_target_pairs={{0,4},{4,0},{8,12},{12,8},{16,20},{20,16},{24,28},{28,24},{1,5},{5... | collective-permute-start | bytes 12296 | tf_op jit(solution)/shard_map/ppermute | solution.py:264
  28.6 8.9 %collective-permute-start.9 = (bf16[2,256,256]{2,1,0:T(8,128)(2,1)S(1)}, bf16[2,256,256]{2,1,0:T(8,128)(2,1)S(1)}, u32[]{:S(2)}, u32[]{:S(2)}) collective-permute-start(bf16[2,256,256]{2,1,0:T(8,128)(2,1)S(1)} %shard_map.79), channel_id=1, source_target_pairs={{0,1},{1,0},{2,3},{3,2},{4,5},{5,4},{6,7},{7,6},{8,9},{9,8},{10,11... | collective-permute-start | bytes 786440 | tf_op jit(solution)/shard_map/ppermute | solution.py:264
  30.1 3.6 %collective-permute-start.10 = (f32[8,128]{1,0:T(8,128)S(1)}, f32[8,128]{1,0:T(8,128)S(1)}, u32[]{:S(2)}, u32[]{:S(2)}) collective-permute-start(f32[8,128]{1,0:T(8,128)S(1)} %add.6), channel_id=1, source_target_pairs={{0,8},{4,12},{8,0},{12,4},{16,24},{20,28},{24,16},{28,20},{1,9},{5... | collective-permute-start | bytes 12296 | tf_op jit(solution)/shard_map/ppermute | solution.py:264
  33.8 3.6 %collective-permute-start.11 = (f32[8,128]{1,0:T(8,128)S(1)}, f32[8,128]{1,0:T(8,128)S(1)}, u32[]{:S(2)}, u32[]{:S(2)}) collective-permute-start(f32[8,128]{1,0:T(8,128)S(1)} %add.7.mine_ref), channel_id=1, source_target_pairs={{0,16},{4,20},{8,24},{12,28},{16,0},{20,4},{24,8},{28,12},{1,17},{... | collective-permute-start | bytes 12296 | tf_op jit(solution)/shard_map/ppermute | solution.py:264

commit v27 on v15

--- a/solution.py
+++ b/solution.py
@@ -40,12 +40,6 @@
     for j in range(8):
         total = jnp.where(distance == j - 3, taps[j : j + 1, :1], total)
     return total.astype(jnp.bfloat16)
-
-
-def cut_halo_kernel(sec_ref, down_ref, up_ref):
-    rows_n = sec_ref.shape[2]
-    down_ref[...] = sec_ref[0, :, rows_n - HALO :]
-    up_ref[...] = sec_ref[0, :, :HALO]
 
 
 def cut_middle_kernel(prim_ref, *refs):
@@ -272,8 +266,7 @@
     edges = jnp.concatenate([primary[:, :LAG], primary[:, rows_n - LAG :]], axis=1)
     edges_two = swap(edges, "date", 2)
     edges_one = swap(edges, "date", 1)
-    halo = shape((2, HALO, cols_n), bf16)
-    down, up = call(cut_halo_kernel, (halo, halo), [], (0, 0), secondary)
+    down, up = secondary[0, :, rows_n - HALO :], secondary[0, :, :HALO]
     low = ring(down, "tile", 1)
     high = ring(up, "tile", -1)
     az_band, rg_band = call(
@@ -283,13 +276,16 @@
         (0, 0),
         az_off, rg_off, az_frac, rg_frac,
     )
-    edges_three = swap(edges_two, "date", 1)
+    passed = call(
+        relay_kernel, shape(edges.shape, bf16), [], (0, 0), edges_two
+    )
+    edges_three = swap(passed, "date", 1)
     middle = call(
         cut_middle_kernel,
         shape((2, middle_n + 16, width), bf16),
         [],
         (0, 0),
-        primary, edges_two,
+        primary, edges_two, edges_one,
     )
     weight = jnp.broadcast_to(margin_mask[rows_n - LAG :].astype(f32)[:, None], (LAG, LANE))
     res = call(

time: 38.9 us -> 38.4 us (0.987)
  waiting for transfers between devices: 9.44 us -> 8.96 us
    unnamed x6 -> x4, local copies, waits for them, and re-layouts: 1.41 us -> 0.01 us
    squeeze x0 -> x1, local copies, waits for them, and re-layouts: none -> 0.99 us  [fused(): down, up = (secondary[0, :, rows_n - HALO:], secondary[0, :, :HALO])]
    ppermute x9, waiting for transfers between devices: 6.3 us -> 5.81 us  [swap(): lax.ppermute(value, axis, [(at, at ^ step) for at in range(lax.axis_size(...]
  transfers between devices with their start and end apart: 12 -> 12, of which waited for: 7 -> 7; matrix products, arithmetic and copies ran while one was open for 2% -> 5% of each run, Pallas kernels for 9% -> 9%
where the time goes in v27:
time: 38.4 us; the launch traced here: 38.2 us
  starting transfers between devices  19.3 us (50%)
  waiting for transfers between devices  8.96 us (23%)
  Pallas kernels  4.39 us (11%)
  between operations  2.71 us (7%)
  local copies, waits for them, and re-layouts  2.09 us (5%)
  other arithmetic  0.77 us (2%)
    ppermute x9, starting transfers between devices, swap(): lax.ppermute(value, axis, [(at, at ^ step) for at in range(lax.axis_size(...  15 us
    ppermute x9, waiting for transfers between devices, swap(): lax.ppermute(value, axis, [(at, at ^ step) for at in range(lax.axis_size(...  5.81 us
    pallas_call x10, Pallas kernels, call(): pl.pallas_call(kernel, out_shape=outs, in_specs=[vmem] * len(args), out_s...  4.39 us
    ppermute x3, starting transfers between devices, ring(): lax.ppermute(value, axis, [(at, (at + step) % count) for at in range(coun...  4.25 us
    ppermute x3, waiting for transfers between devices, ring(): lax.ppermute(value, axis, [(at, (at + step) % count) for at in range(coun...  3.14 us
    slice x1, local copies, waits for them, and re-layouts, fused(): primary[:, :LAG]  1.02 us
    squeeze x1, local copies, waits for them, and re-layouts, fused(): down, up = (secondary[0, :, rows_n - HALO:], secondary[0, :, :HALO])  0.99 us
  transfers between devices with their start and end apart: 12, of which 7 were waited for; matrix products, arithmetic and copies ran while one was open for 5% of the time, Pallas kernels for 9%

profile of v27, /device:TPU:0, one launch (start us, length us, event | category | flops | bytes accessed | tf_op | source)
XLA Modules:
  0.0 38.2 jit_solution(6593214141475233058)
XLA Ops:
  0.0 1.0 %fusion = (bf16[2,64,256]{2,1,0:T(8,128)(2,1)S(1)}, bf16[2,64,256]{2,1,0:T(8,128)(2,1)S(1)}) fusion(bf16[2,384,256]{2,1,0:T(8,128)(2,1)} %own_ref.3), kind=kLoop, calls=%fused_computation.4 | loop fusion | bytes 262144 | tf_op jit(solution)/shard_map/slice | solution.py:266
  1.0 4.1 %collective-permute-start = (bf16[2,128,256]{2,1,0:T(8,128)(2,1)S(1)}, bf16[2,128,256]{2,1,0:T(8,128)(2,1)S(1)}, u32[]{:S(2)}, u32[]{:S(2)}) collective-permute-start(bf16[2,128,256]{2,1,0:T(8,128)(2,1)S(1)} %pad_maximum_fusion), channel_id=1, source_target_pairs={{0,2},{1,3},{2,0},{3,1},{4,6},{5,7},{6,4},{7,5},{8,10},{9,11},{10,... | collective-permute-start | bytes 393224 | tf_op jit(solution)/shard_map/ppermute | solution.py:254
  5.2 1.6 %collective-permute-start.1 = (bf16[2,128,256]{2,1,0:T(8,128)(2,1)S(1)}, bf16[2,128,256]{2,1,0:T(8,128)(2,1)S(1)}, u32[]{:S(2)}, u32[]{:S(2)}) collective-permute-start(bf16[2,128,256]{2,1,0:T(8,128)(2,1)S(1)} %pad_maximum_fusion), channel_id=1, source_target_pairs={{0,1},{1,0},{2,3},{3,2},{4,5},{5,4},{6,7},{7,6},{8,9},{9,8},{10,11... | collective-permute-start | bytes 393224 | tf_op jit(solution)/shard_map/ppermute | solution.py:254
  6.7 1.0 %slice_bitcast_fusion = (bf16[2,32,1024]{2,1,0:T(8,128)(2,1)S(1)}, bf16[2,32,1024]{2,1,0:T(8,128)(2,1)S(1)}) fusion(bf16[1,2,384,1024]{3,2,1,0:T(8,128)(2,1)} %sec_ref.1), kind=kLoop, calls=%fused_computation.1 | loop fusion | bytes 524288 | tf_op jit(solution)/shard_map/squeeze | solution.py:269
  7.7 0.1 collective-permute-start.4
  7.8 2.6 %collective-permute-start.5 = (bf16[2,32,1024]{2,1,0:T(8,128)(2,1)S(1)}, bf16[2,32,1024]{2,1,0:T(8,128)(2,1)S(1)}, u32[]{:S(2)}, u32[]{:S(2)}) collective-permute-start(bf16[2,32,1024]{2,1,0:T(8,128)(2,1)S(1)} %get-tuple-element.15), channel_id=1, source_target_pairs={{0,28},{4,0},{8,4},{12,8},{16,12},{20,16},{24,20},{28,24},{1,29},{... | collective-permute-start | bytes 393224 | tf_op jit(solution)/shard_map/ppermute | solution.py:250
  10.4 1.1 %collective-permute-done.refs_0_.block_ref.two_ref = bf16[2,128,256]{2,1,0:T(8,128)(2,1)S(1)} collective-permute-done((bf16[2,128,256]{2,1,0:T(8,128)(2,1)S(1)}, bf16[2,128,256]{2,1,0:T(8,128)(2,1)S(1)}, u32[]{:S(2)}, u32[]{:S(2)}) %collective-permute-start) | collective-permute-done | bytes 131104 | tf_op jit(solution)/shard_map/ppermute | solution.py:254
  11.6 0.7 %collective-permute-start.3 = (bf16[2,128,256]{2,1,0:T(8,128)(2,1)S(1)}, bf16[2,128,256]{2,1,0:T(8,128)(2,1)S(1)}, u32[]{:S(2)}, u32[]{:S(2)}) collective-permute-start(bf16[2,128,256]{2,1,0:T(8,128)(2,1)S(1)} %shard_map.74), channel_id=1, source_target_pairs={{0,1},{1,0},{2,3},{3,2},{4,5},{5,4},{6,7},{7,6},{8,9},{9,8},{10,11... | collective-permute-start | bytes 393224 | tf_op jit(solution)/shard_map/ppermute | solution.py:254
  12.3 3.4 %collective-permute-start.2 = (bf16[2,272,256]{2,1,0:T(8,128)(2,1)S(1)}, bf16[2,272,256]{2,1,0:T(8,128)(2,1)S(1)}, u32[]{:S(2)}, u32[]{:S(2)}) collective-permute-start(bf16[2,272,256]{2,1,0:T(8,128)(2,1)S(1)} %shard_map.73), channel_id=1, source_target_pairs={{0,2},{1,3},{2,0},{3,1},{4,6},{5,7},{6,4},{7,5},{8,10},{9,11},{10,... | collective-permute-start | bytes 835592 | tf_op jit(solution)/shard_map/ppermute | solution.py:254
  15.7 0.0 collective-permute-start.8
  18.4 0.4 shard_map.75
  18.7 0.0 collective-permute-done.5.high_ref
  18.8 1.4 %shard_map.76.res_ref = bf16[4,2,384,256]{3,2,1,0:T(8,128)(2,1)S(1)} custom-call(bf16[1,2,384,1024]{3,2,1,0:T(8,128)(2,1)S(1)} %copy-done.1, bf16[2,32,1024]{2,1,0:T(8,128)(2,1)S(1)} %collective-permute-done.4.low_ref, bf16[2,32,1024]{2,1,0:T(8,128)(2,1)S(1)} %collective-permute-done.5.high_ref, bf16[128,192]{1,0:T(8,128)(2,1)S(1)} %get-tuple-element.10.az_ref, ...), custom_call_target="tpu_custom_call" | custom-call | tf_op jit(solution)/shard_map/pallas_call | solution.py:237
  20.2 0.5 %shard_map.77 = (bf16[2,64,1024]{2,1,0:T(8,128)(2,1)S(1)}, bf16[2,64,1024]{2,1,0:T(8,128)(2,1)S(1)}, f32[2,64,128]{2,1,0:T(8,128)S(1)}) custom-call(bf16[2,384,256]{2,1,0:T(8,128)(2,1)S(1)} %copy-done, bf16[2,128,256]{2,1,0:T(8,128)(2,1)S(1)} %collective-permute-done.1.refs_1_.one_ref, ...), custom_call_target="tpu_custom_call" | custom-call | tf_op jit(solution)/shard_map/pallas_call | solution.py:237
  20.7 1.6 %collective-permute-start.6 = (bf16[2,64,1024]{2,1,0:T(8,128)(2,1)S(1)}, bf16[2,64,1024]{2,1,0:T(8,128)(2,1)S(1)}, u32[]{:S(2)}, u32[]{:S(2)}) collective-permute-start(bf16[2,64,1024]{2,1,0:T(8,128)(2,1)S(1)} %get-tuple-element.13), channel_id=1, source_target_pairs={{0,28},{4,0},{8,4},{12,8},{16,12},{20,16},{24,20},{28,24},{1,29},{... | collective-permute-start | bytes 786440 | tf_op jit(solution)/shard_map/ppermute | solution.py:250
  22.3 0.8 %slice_convert_fusion = f32[64]{0:T(128)S(1)} fusion(s32[384]{0:T(512)} %param.9), kind=kLoop, calls=%fused_computation.3 | loop fusion | flops 64 | bytes 512 | tf_op jit(solution)/shard_map/convert_element_type | solution.py:290
  23.0 3.1 %collective-permute-done.6.later_ref = bf16[2,64,1024]{2,1,0:T(8,128)(2,1)S(1)} collective-permute-done((bf16[2,64,1024]{2,1,0:T(8,128)(2,1)S(1)}, bf16[2,64,1024]{2,1,0:T(8,128)(2,1)S(1)}, u32[]{:S(2)}, u32[]{:S(2)}) %collective-permute-start.6) | collective-permute-done | bytes 262176 | tf_op jit(solution)/shard_map/ppermute | solution.py:250
  26.1 0.1 broadcast_in_dim.2.weight_ref
  26.2 0.4 shard_map.78
  26.6 0.6 %collective-permute-start.7 = (f32[8,128]{1,0:T(8,128)S(1)}, f32[8,128]{1,0:T(8,128)S(1)}, u32[]{:S(2)}, u32[]{:S(2)}) collective-permute-start(f32[8,128]{1,0:T(8,128)S(1)} %shard_map.78), channel_id=1, source_target_pairs={{0,4},{4,0},{8,12},{12,8},{16,20},{20,16},{24,28},{28,24},{1,5},{5... | collective-permute-start | bytes 12296 | tf_op jit(solution)/shard_map/ppermute | solution.py:254
  27.2 1.2 %collective-permute-done.2.block_ref.two_ref = bf16[2,272,256]{2,1,0:T(8,128)(2,1)S(1)} collective-permute-done((bf16[2,272,256]{2,1,0:T(8,128)(2,1)S(1)}, bf16[2,272,256]{2,1,0:T(8,128)(2,1)S(1)}, u32[]{:S(2)}, u32[]{:S(2)}) %collective-permute-start.2) | collective-permute-done | bytes 278560 | tf_op jit(solution)/shard_map/ppermute | solution.py:254
  28.4 0.1 collective-permute-done.8.refs_1_.one_ref
  28.5 0.0 collective-permute-done.7.refs_0_
  28.6 1.6 %collective-permute-start.9 = (bf16[2,256,256]{2,1,0:T(8,128)(2,1)S(1)}, bf16[2,256,256]{2,1,0:T(8,128)(2,1)S(1)}, u32[]{:S(2)}, u32[]{:S(2)}) collective-permute-start(bf16[2,256,256]{2,1,0:T(8,128)(2,1)S(1)} %shard_map.79), channel_id=1, source_target_pairs={{0,1},{1,0},{2,3},{3,2},{4,5},{5,4},{6,7},{7,6},{8,9},{9,8},{10,11... | collective-permute-start | bytes 786440 | tf_op jit(solution)/shard_map/ppermute | solution.py:254
  30.1 1.5 %collective-permute-start.10 = (f32[8,128]{1,0:T(8,128)S(1)}, f32[8,128]{1,0:T(8,128)S(1)}, u32[]{:S(2)}, u32[]{:S(2)}) collective-permute-start(f32[8,128]{1,0:T(8,128)S(1)} %add.6), channel_id=1, source_target_pairs={{0,8},{4,12},{8,0},{12,4},{16,24},{20,28},{24,16},{28,20},{1,9},{5... | collective-permute-start | bytes 12296 | tf_op jit(solution)/shard_map/ppermute | solution.py:254
  31.6 0.6 %shard_map.80.before_ref = f32[2,256,128]{2,1,0:T(8,128)S(1)} custom-call(bf16[2,384,256]{2,1,0:T(8,128)(2,1)S(1)} %copy-done, bf16[2,272,256]{2,1,0:T(8,128)(2,1)S(1)} %collective-permute-done.8.refs_1_.one_ref, bf16[2,272,256]{2,1,0:T(8,128)(2,1)S(1)} %collective-permute-done.2.block_ref.two_ref, bf16[4,2,384,256]{3,2,1,0:T(8,128)(2,1)S(1)} %shard_map.76.res_ref), custom_call_target="tpu_custom_call" | custom-call | flops 134217728 | bytes 3145728 | tf_op jit(solution)/shard_map/pallas_call | solution.py:237
  32.2 1.5 %collective-permute-done.10 = f32[8,128]{1,0:T(8,128)S(1)} collective-permute-done((f32[8,128]{1,0:T(8,128)S(1)}, f32[8,128]{1,0:T(8,128)S(1)}, u32[]{:S(2)}, u32[]{:S(2)}) %collective-permute-start.10) | collective-permute-done | bytes 4128 | tf_op jit(solution)/shard_map/ppermute | solution.py:254
  33.8 1.5 %collective-permute-start.11 = (f32[8,128]{1,0:T(8,128)S(1)}, f32[8,128]{1,0:T(8,128)S(1)}, u32[]{:S(2)}, u32[]{:S(2)}) collective-permute-start(f32[8,128]{1,0:T(8,128)S(1)} %add.7.mine_ref), channel_id=1, source_target_pairs={{0,16},{4,20},{8,24},{12,28},{16,0},{20,4},{24,8},{28,12},{1,17},{... | collective-permute-start | bytes 12296 | tf_op jit(solution)/shard_map/ppermute | solution.py:254
  35.3 1.7 %collective-permute-done.9.three_ref = bf16[2,256,256]{2,1,0:T(8,128)(2,1)S(1)} collective-permute-done((bf16[2,256,256]{2,1,0:T(8,128)(2,1)S(1)}, bf16[2,256,256]{2,1,0:T(8,128)(2,1)S(1)}, u32[]{:S(2)}, u32[]{:S(2)}) %collective-permute-start.9) | collective-permute-done | bytes 262176 | tf_op jit(solution)/shard_map/ppermute | solution.py:254
  36.9 0.3 shard_map.81.looks_ref
  37.2 0.2 collective-permute-done.11.other_ref
  37.4 0.8 %shard_map.82 = f32[1,2,192,128]{3,2,1,0:T(8,128)} custom-call(f32[2,192,128]{2,1,0:T(8,128)S(1)} %shard_map.81.looks_ref, f32[8,128]{1,0:T(8,128)S(1)} %add.7.mine_ref, f32[8,128]{1,0:T(8,128)S(1)} %collective-permute-done.11.other_ref), custom_call_target="tpu_custom_call" | custom-call | flops 393216 | bytes 393216 | tf_op jit(solution)/shard_map/pallas_call | solution.py:237
  (13 shorter events, 0.1 us)
Async XLA Ops:
  0.0 12.3 %copy-start = (bf16[2,384,256]{2,1,0:T(8,128)(2,1)S(1)}, bf16[2,384,256]{2,1,0:T(8,128)(2,1)}, u32[]{:S(2)}) copy-start(bf16[2,384,256]{2,1,0:T(8,128)(2,1)} %own_ref.3) | copy-start | bytes 1179652
  0.0 18.7 %copy-start.1 = (bf16[1,2,384,1024]{3,2,1,0:T(8,128)(2,1)S(1)}, bf16[1,2,384,1024]{3,2,1,0:T(8,128)(2,1)}, u32[]{:S(2)}) copy-start(bf16[1,2,384,1024]{3,2,1,0:T(8,128)(2,1)} %sec_ref.1) | copy-start | bytes 4718596
  1.0 10.5 %collective-permute-start = (bf16[2,128,256]{2,1,0:T(8,128)(2,1)S(1)}, bf16[2,128,256]{2,1,0:T(8,128)(2,1)S(1)}, u32[]{:S(2)}, u32[]{:S(2)}) collective-permute-start(bf16[2,128,256]{2,1,0:T(8,128)(2,1)S(1)} %pad_maximum_fusion), channel_id=1, source_target_pairs={{0,2},{1,3},{2,0},{3,1},{4,6},{5,7},{6,4},{7,5},{8,10},{9,11},{10,... | collective-permute-start | bytes 393224 | tf_op jit(solution)/shard_map/ppermute | solution.py:254
  5.2 7.1 %collective-permute-start.1 = (bf16[2,128,256]{2,1,0:T(8,128)(2,1)S(1)}, bf16[2,128,256]{2,1,0:T(8,128)(2,1)S(1)}, u32[]{:S(2)}, u32[]{:S(2)}) collective-permute-start(bf16[2,128,256]{2,1,0:T(8,128)(2,1)S(1)} %pad_maximum_fusion), channel_id=1, source_target_pairs={{0,1},{1,0},{2,3},{3,2},{4,5},{5,4},{6,7},{7,6},{8,9},{9,8},{10,11... | collective-permute-start | bytes 393224 | tf_op jit(solution)/shard_map/ppermute | solution.py:254
  7.7 11.0 %collective-permute-start.4 = (bf16[2,32,1024]{2,1,0:T(8,128)(2,1)S(1)}, bf16[2,32,1024]{2,1,0:T(8,128)(2,1)S(1)}, u32[]{:S(2)}, u32[]{:S(2)}) collective-permute-start(bf16[2,32,1024]{2,1,0:T(8,128)(2,1)S(1)} %get-tuple-element.16), channel_id=1, source_target_pairs={{0,4},{4,8},{8,12},{12,16},{16,20},{20,24},{24,28},{28,0},{1,5},{5... | collective-permute-start | bytes 393224 | tf_op jit(solution)/shard_map/ppermute | solution.py:250
  7.8 11.0 %collective-permute-start.5 = (bf16[2,32,1024]{2,1,0:T(8,128)(2,1)S(1)}, bf16[2,32,1024]{2,1,0:T(8,128)(2,1)S(1)}, u32[]{:S(2)}, u32[]{:S(2)}) collective-permute-start(bf16[2,32,1024]{2,1,0:T(8,128)(2,1)S(1)} %get-tuple-element.15), channel_id=1, source_target_pairs={{0,28},{4,0},{8,4},{12,8},{16,12},{20,16},{24,20},{28,24},{1,29},{... | collective-permute-start | bytes 393224 | tf_op jit(solution)/shard_map/ppermute | solution.py:250
  11.6 8.6 %collective-permute-start.3 = (bf16[2,128,256]{2,1,0:T(8,128)(2,1)S(1)}, bf16[2,128,256]{2,1,0:T(8,128)(2,1)S(1)}, u32[]{:S(2)}, u32[]{:S(2)}) collective-permute-start(bf16[2,128,256]{2,1,0:T(8,128)(2,1)S(1)} %shard_map.74), channel_id=1, source_target_pairs={{0,1},{1,0},{2,3},{3,2},{4,5},{5,4},{6,7},{7,6},{8,9},{9,8},{10,11... | collective-permute-start | bytes 393224 | tf_op jit(solution)/shard_map/ppermute | solution.py:254
  12.3 16.1 %collective-permute-start.2 = (bf16[2,272,256]{2,1,0:T(8,128)(2,1)S(1)}, bf16[2,272,256]{2,1,0:T(8,128)(2,1)S(1)}, u32[]{:S(2)}, u32[]{:S(2)}) collective-permute-start(bf16[2,272,256]{2,1,0:T(8,128)(2,1)S(1)} %shard_map.73), channel_id=1, source_target_pairs={{0,2},{1,3},{2,0},{3,1},{4,6},{5,7},{6,4},{7,5},{8,10},{9,11},{10,... | collective-permute-start | bytes 835592 | tf_op jit(solution)/shard_map/ppermute | solution.py:254
  15.7 12.8 %collective-permute-start.8 = (bf16[2,272,256]{2,1,0:T(8,128)(2,1)S(1)}, bf16[2,272,256]{2,1,0:T(8,128)(2,1)S(1)}, u32[]{:S(2)}, u32[]{:S(2)}) collective-permute-start(bf16[2,272,256]{2,1,0:T(8,128)(2,1)S(1)} %shard_map.73), channel_id=1, source_target_pairs={{0,1},{1,0},{2,3},{3,2},{4,5},{5,4},{6,7},{7,6},{8,9},{9,8},{10,11... | collective-permute-start | bytes 835592 | tf_op jit(solution)/shard_map/ppermute | solution.py:254
  20.7 5.5 %collective-permute-start.6 = (bf16[2,64,1024]{2,1,0:T(8,128)(2,1)S(1)}, bf16[2,64,1024]{2,1,0:T(8,128)(2,1)S(1)}, u32[]{:S(2)}, u32[]{:S(2)}) collective-permute-start(bf16[2,64,1024]{2,1,0:T(8,128)(2,1)S(1)} %get-tuple-element.13), channel_id=1, source_target_pairs={{0,28},{4,0},{8,4},{12,8},{16,12},{20,16},{24,20},{28,24},{1,29},{... | collective-permute-start | bytes 786440 | tf_op jit(solution)/shard_map/ppermute | solution.py:250
  26.6 2.0 %collective-permute-start.7 = (f32[8,128]{1,0:T(8,128)S(1)}, f32[8,128]{1,0:T(8,128)S(1)}, u32[]{:S(2)}, u32[]{:S(2)}) collective-permute-start(f32[8,128]{1,0:T(8,128)S(1)} %shard_map.78), channel_id=1, source_target_pairs={{0,4},{4,0},{8,12},{12,8},{16,20},{20,16},{24,28},{28,24},{1,5},{5... | collective-permute-start | bytes 12296 | tf_op jit(solution)/shard_map/ppermute | solution.py:254
  28.6 8.4 %collective-permute-start.9 = (bf16[2,256,256]{2,1,0:T(8,128)(2,1)S(1)}, bf16[2,256,256]{2,1,0:T(8,128)(2,1)S(1)}, u32[]{:S(2)}, u32[]{:S(2)}) collective-permute-start(bf16[2,256,256]{2,1,0:T(8,128)(2,1)S(1)} %shard_map.79), channel_id=1, source_target_pairs={{0,1},{1,0},{2,3},{3,2},{4,5},{5,4},{6,7},{7,6},{8,9},{9,8},{10,11... | collective-permute-start | bytes 786440 | tf_op jit(solution)/shard_map/ppermute | solution.py:254
  30.1 3.6 %collective-permute-start.10 = (f32[8,128]{1,0:T(8,128)S(1)}, f32[8,128]{1,0:T(8,128)S(1)}, u32[]{:S(2)}, u32[]{:S(2)}) collective-permute-start(f32[8,128]{1,0:T(8,128)S(1)} %add.6), channel_id=1, source_target_pairs={{0,8},{4,12},{8,0},{12,4},{16,24},{20,28},{24,16},{28,20},{1,9},{5... | collective-permute-start | bytes 12296 | tf_op jit(solution)/shard_map/ppermute | solution.py:254
  33.8 3.6 %collective-permute-start.11 = (f32[8,128]{1,0:T(8,128)S(1)}, f32[8,128]{1,0:T(8,128)S(1)}, u32[]{:S(2)}, u32[]{:S(2)}) collective-permute-start(f32[8,128]{1,0:T(8,128)S(1)} %add.7.mine_ref), channel_id=1, source_target_pairs={{0,16},{4,20},{8,24},{12,28},{16,0},{20,4},{24,8},{28,12},{1,17},{... | collective-permute-start | bytes 12296 | tf_op jit(solution)/shard_map/ppermute | solution.py:254

commit v28 on v27

--- a/solution.py
+++ b/solution.py
@@ -319,15 +319,15 @@
         (2 * 2 * middle_n * cols_n * looks_n, 8 * rows_n * cols_n),
         primary, one, two, res,
     )
-    other = swap(stats, "tile", 1)
+    other = swap(stats, "tile", tiles_n // 2)
     block = shape((2, middle_n, width), bf16)
     relayed = call(relay_kernel, block, [], (0, 0), two, other,one)
     three = swap(relayed, "date", 1)
-    stride = 2
-    while stride < tiles_n:
+    stride = tiles_n // 4
+    while stride:
         stats = stats + other
         other = swap(stats, "tile", stride)
-        stride *= 2
+        stride //= 2
     looks = call(
         last_kernel,
         shape((2, rows_n // LA, looks_n), f32),

time: 38.4 us -> 39.6 us (1.031)
  waiting for transfers between devices: 8.96 us -> 12.7 us
  starting transfers between devices: 19.3 us -> 16.7 us
    ppermute x9, waiting for transfers between devices: 5.81 us -> 9.53 us  [swap(): lax.ppermute(value, axis, [(at, at ^ step) for at in range(lax.axis_size(...]
    ppermute x9, starting transfers between devices: 15 us -> 12.5 us  [swap(): lax.ppermute(value, axis, [(at, at ^ step) for at in range(lax.axis_size(...]
where the time goes in v28:
time: 39.6 us; the launch traced here: 39.3 us
  starting transfers between devices  16.7 us (42%)
  waiting for transfers between devices  12.7 us (32%)
  Pallas kernels  4.4 us (11%)
  between operations  2.71 us (7%)
  local copies, waits for them, and re-layouts  2.09 us (5%)
  other arithmetic  0.77 us (2%)
    ppermute x9, starting transfers between devices, swap(): lax.ppermute(value, axis, [(at, at ^ step) for at in range(lax.axis_size(...  12.5 us
    ppermute x9, waiting for transfers between devices, swap(): lax.ppermute(value, axis, [(at, at ^ step) for at in range(lax.axis_size(...  9.53 us
    pallas_call x10, Pallas kernels, call(): pl.pallas_call(kernel, out_shape=outs, in_specs=[vmem] * len(args), out_s...  4.4 us
    ppermute x3, starting transfers between devices, ring(): lax.ppermute(value, axis, [(at, (at + step) % count) for at in range(coun...  4.25 us
    ppermute x3, waiting for transfers between devices, ring(): lax.ppermute(value, axis, [(at, (at + step) % count) for at in range(coun...  3.14 us
    slice x1, local copies, waits for them, and re-layouts, fused(): primary[:, :LAG]  1.02 us
    squeeze x1, local copies, waits for them, and re-layouts, fused(): down, up = (secondary[0, :, rows_n - HALO:], secondary[0, :, :HALO])  0.99 us
  transfers between devices with their start and end apart: 12, of which 7 were waited for; matrix products, arithmetic and copies ran while one was open for 5% of the time, Pallas kernels for 9%

profile of v28, /device:TPU:0, one launch (start us, length us, event | category | flops | bytes accessed | tf_op | source)
XLA Modules:
  0.0 39.3 jit_solution(12004759139701513522)
XLA Ops:
  0.0 1.0 %fusion = (bf16[2,64,256]{2,1,0:T(8,128)(2,1)S(1)}, bf16[2,64,256]{2,1,0:T(8,128)(2,1)S(1)}) fusion(bf16[2,384,256]{2,1,0:T(8,128)(2,1)} %own_ref.3), kind=kLoop, calls=%fused_computation.4 | loop fusion | bytes 262144 | tf_op jit(solution)/shard_map/slice | solution.py:266
  1.0 4.1 %collective-permute-start = (bf16[2,128,256]{2,1,0:T(8,128)(2,1)S(1)}, bf16[2,128,256]{2,1,0:T(8,128)(2,1)S(1)}, u32[]{:S(2)}, u32[]{:S(2)}) collective-permute-start(bf16[2,128,256]{2,1,0:T(8,128)(2,1)S(1)} %pad_maximum_fusion), channel_id=1, source_target_pairs={{0,2},{1,3},{2,0},{3,1},{4,6},{5,7},{6,4},{7,5},{8,10},{9,11},{10,... | collective-permute-start | bytes 393224 | tf_op jit(solution)/shard_map/ppermute | solution.py:254
  5.2 1.6 %collective-permute-start.1 = (bf16[2,128,256]{2,1,0:T(8,128)(2,1)S(1)}, bf16[2,128,256]{2,1,0:T(8,128)(2,1)S(1)}, u32[]{:S(2)}, u32[]{:S(2)}) collective-permute-start(bf16[2,128,256]{2,1,0:T(8,128)(2,1)S(1)} %pad_maximum_fusion), channel_id=1, source_target_pairs={{0,1},{1,0},{2,3},{3,2},{4,5},{5,4},{6,7},{7,6},{8,9},{9,8},{10,11... | collective-permute-start | bytes 393224 | tf_op jit(solution)/shard_map/ppermute | solution.py:254
  6.7 1.0 %slice_bitcast_fusion = (bf16[2,32,1024]{2,1,0:T(8,128)(2,1)S(1)}, bf16[2,32,1024]{2,1,0:T(8,128)(2,1)S(1)}) fusion(bf16[1,2,384,1024]{3,2,1,0:T(8,128)(2,1)} %sec_ref.1), kind=kLoop, calls=%fused_computation.1 | loop fusion | bytes 524288 | tf_op jit(solution)/shard_map/squeeze | solution.py:269
  7.7 0.1 collective-permute-start.4
  7.8 2.6 %collective-permute-start.5 = (bf16[2,32,1024]{2,1,0:T(8,128)(2,1)S(1)}, bf16[2,32,1024]{2,1,0:T(8,128)(2,1)S(1)}, u32[]{:S(2)}, u32[]{:S(2)}) collective-permute-start(bf16[2,32,1024]{2,1,0:T(8,128)(2,1)S(1)} %get-tuple-element.15), channel_id=1, source_target_pairs={{0,28},{4,0},{8,4},{12,8},{16,12},{20,16},{24,20},{28,24},{1,29},{... | collective-permute-start | bytes 393224 | tf_op jit(solution)/shard_map/ppermute | solution.py:250
  10.4 1.1 %collective-permute-done.refs_0_.block_ref.two_ref = bf16[2,128,256]{2,1,0:T(8,128)(2,1)S(1)} collective-permute-done((bf16[2,128,256]{2,1,0:T(8,128)(2,1)S(1)}, bf16[2,128,256]{2,1,0:T(8,128)(2,1)S(1)}, u32[]{:S(2)}, u32[]{:S(2)}) %collective-permute-start) | collective-permute-done | bytes 131104 | tf_op jit(solution)/shard_map/ppermute | solution.py:254
  11.6 0.7 %collective-permute-start.3 = (bf16[2,128,256]{2,1,0:T(8,128)(2,1)S(1)}, bf16[2,128,256]{2,1,0:T(8,128)(2,1)S(1)}, u32[]{:S(2)}, u32[]{:S(2)}) collective-permute-start(bf16[2,128,256]{2,1,0:T(8,128)(2,1)S(1)} %shard_map.74), channel_id=1, source_target_pairs={{0,1},{1,0},{2,3},{3,2},{4,5},{5,4},{6,7},{7,6},{8,9},{9,8},{10,11... | collective-permute-start | bytes 393224 | tf_op jit(solution)/shard_map/ppermute | solution.py:254
  12.3 3.4 %collective-permute-start.2 = (bf16[2,272,256]{2,1,0:T(8,128)(2,1)S(1)}, bf16[2,272,256]{2,1,0:T(8,128)(2,1)S(1)}, u32[]{:S(2)}, u32[]{:S(2)}) collective-permute-start(bf16[2,272,256]{2,1,0:T(8,128)(2,1)S(1)} %shard_map.73), channel_id=1, source_target_pairs={{0,2},{1,3},{2,0},{3,1},{4,6},{5,7},{6,4},{7,5},{8,10},{9,11},{10,... | collective-permute-start | bytes 835592 | tf_op jit(solution)/shard_map/ppermute | solution.py:254
  15.7 0.0 collective-permute-start.8
  18.4 0.4 shard_map.75
  18.7 0.0 collective-permute-done.5.high_ref
  18.8 1.4 %shard_map.76.res_ref = bf16[4,2,384,256]{3,2,1,0:T(8,128)(2,1)S(1)} custom-call(bf16[1,2,384,1024]{3,2,1,0:T(8,128)(2,1)S(1)} %copy-done.1, bf16[2,32,1024]{2,1,0:T(8,128)(2,1)S(1)} %collective-permute-done.4.low_ref, bf16[2,32,1024]{2,1,0:T(8,128)(2,1)S(1)} %collective-permute-done.5.high_ref, bf16[128,192]{1,0:T(8,128)(2,1)S(1)} %get-tuple-element.10.az_ref, ...), custom_call_target="tpu_custom_call" | custom-call | tf_op jit(solution)/shard_map/pallas_call | solution.py:237
  20.2 0.0 collective-permute-done.3.three_ref
  20.2 0.5 %shard_map.77 = (bf16[2,64,1024]{2,1,0:T(8,128)(2,1)S(1)}, bf16[2,64,1024]{2,1,0:T(8,128)(2,1)S(1)}, f32[2,64,128]{2,1,0:T(8,128)S(1)}) custom-call(bf16[2,384,256]{2,1,0:T(8,128)(2,1)S(1)} %copy-done, bf16[2,128,256]{2,1,0:T(8,128)(2,1)S(1)} %collective-permute-done.1.refs_1_.one_ref, ...), custom_call_target="tpu_custom_call" | custom-call | tf_op jit(solution)/shard_map/pallas_call | solution.py:237
  20.7 1.6 %collective-permute-start.6 = (bf16[2,64,1024]{2,1,0:T(8,128)(2,1)S(1)}, bf16[2,64,1024]{2,1,0:T(8,128)(2,1)S(1)}, u32[]{:S(2)}, u32[]{:S(2)}) collective-permute-start(bf16[2,64,1024]{2,1,0:T(8,128)(2,1)S(1)} %get-tuple-element.13), channel_id=1, source_target_pairs={{0,28},{4,0},{8,4},{12,8},{16,12},{20,16},{24,20},{28,24},{1,29},{... | collective-permute-start | bytes 786440 | tf_op jit(solution)/shard_map/ppermute | solution.py:250
  22.3 0.8 %slice_convert_fusion = f32[64]{0:T(128)S(1)} fusion(s32[384]{0:T(512)} %param.9), kind=kLoop, calls=%fused_computation.3 | loop fusion | flops 64 | bytes 512 | tf_op jit(solution)/shard_map/convert_element_type | solution.py:290
  23.0 3.1 %collective-permute-done.6.later_ref = bf16[2,64,1024]{2,1,0:T(8,128)(2,1)S(1)} collective-permute-done((bf16[2,64,1024]{2,1,0:T(8,128)(2,1)S(1)}, bf16[2,64,1024]{2,1,0:T(8,128)(2,1)S(1)}, u32[]{:S(2)}, u32[]{:S(2)}) %collective-permute-start.6) | collective-permute-done | bytes 262176 | tf_op jit(solution)/shard_map/ppermute | solution.py:250
  26.1 0.1 broadcast_in_dim.2.weight_ref
  26.2 0.4 shard_map.78
  26.6 0.6 %collective-permute-start.7 = (f32[8,128]{1,0:T(8,128)S(1)}, f32[8,128]{1,0:T(8,128)S(1)}, u32[]{:S(2)}, u32[]{:S(2)}) collective-permute-start(f32[8,128]{1,0:T(8,128)S(1)} %shard_map.78), channel_id=1, source_target_pairs={{0,16},{4,20},{8,24},{12,28},{16,0},{20,4},{24,8},{28,12},{1,17},{... | collective-permute-start | bytes 12296 | tf_op jit(solution)/shard_map/ppermute | solution.py:254
  27.2 1.3 %collective-permute-done.2.block_ref.two_ref = bf16[2,272,256]{2,1,0:T(8,128)(2,1)S(1)} collective-permute-done((bf16[2,272,256]{2,1,0:T(8,128)(2,1)S(1)}, bf16[2,272,256]{2,1,0:T(8,128)(2,1)S(1)}, u32[]{:S(2)}, u32[]{:S(2)}) %collective-permute-start.2) | collective-permute-done | bytes 278560 | tf_op jit(solution)/shard_map/ppermute | solution.py:254
  28.4 0.1 collective-permute-done.8.refs_1_.one_ref
  28.5 1.7 %collective-permute-done.7.refs_0_ = f32[8,128]{1,0:T(8,128)S(1)} collective-permute-done((f32[8,128]{1,0:T(8,128)S(1)}, f32[8,128]{1,0:T(8,128)S(1)}, u32[]{:S(2)}, u32[]{:S(2)}) %collective-permute-start.7) | collective-permute-done | bytes 4128 | tf_op jit(solution)/shard_map/ppermute | solution.py:254
  30.3 1.8 %collective-permute-start.9 = (bf16[2,256,256]{2,1,0:T(8,128)(2,1)S(1)}, bf16[2,256,256]{2,1,0:T(8,128)(2,1)S(1)}, u32[]{:S(2)}, u32[]{:S(2)}) collective-permute-start(bf16[2,256,256]{2,1,0:T(8,128)(2,1)S(1)} %shard_map.79), channel_id=1, source_target_pairs={{0,1},{1,0},{2,3},{3,2},{4,5},{5,4},{6,7},{7,6},{8,9},{9,8},{10,11... | collective-permute-start | bytes 786440 | tf_op jit(solution)/shard_map/ppermute | solution.py:254
  32.1 0.3 collective-permute-start.10
  32.3 0.6 %shard_map.80.before_ref = f32[2,256,128]{2,1,0:T(8,128)S(1)} custom-call(bf16[2,384,256]{2,1,0:T(8,128)(2,1)S(1)} %copy-done, bf16[2,272,256]{2,1,0:T(8,128)(2,1)S(1)} %collective-permute-done.8.refs_1_.one_ref, bf16[2,272,256]{2,1,0:T(8,128)(2,1)S(1)} %collective-permute-done.2.block_ref.two_ref, bf16[4,2,384,256]{3,2,1,0:T(8,128)(2,1)S(1)} %shard_map.76.res_ref), custom_call_target="tpu_custom_call" | custom-call | flops 134217728 | bytes 3145728 | tf_op jit(solution)/shard_map/pallas_call | solution.py:237
  32.9 2.7 %collective-permute-done.10 = f32[8,128]{1,0:T(8,128)S(1)} collective-permute-done((f32[8,128]{1,0:T(8,128)S(1)}, f32[8,128]{1,0:T(8,128)S(1)}, u32[]{:S(2)}, u32[]{:S(2)}) %collective-permute-start.10) | collective-permute-done | bytes 4128 | tf_op jit(solution)/shard_map/ppermute | solution.py:254
  35.7 0.0 collective-permute-start.11
  35.7 2.5 %collective-permute-done.9.three_ref = bf16[2,256,256]{2,1,0:T(8,128)(2,1)S(1)} collective-permute-done((bf16[2,256,256]{2,1,0:T(8,128)(2,1)S(1)}, bf16[2,256,256]{2,1,0:T(8,128)(2,1)S(1)}, u32[]{:S(2)}, u32[]{:S(2)}) %collective-permute-start.9) | collective-permute-done | bytes 262176 | tf_op jit(solution)/shard_map/ppermute | solution.py:254
  38.2 0.3 shard_map.81.looks_ref
  38.5 0.8 %shard_map.82 = f32[1,2,192,128]{3,2,1,0:T(8,128)} custom-call(f32[2,192,128]{2,1,0:T(8,128)S(1)} %shard_map.81.looks_ref, f32[8,128]{1,0:T(8,128)S(1)} %add.7.mine_ref, f32[8,128]{1,0:T(8,128)S(1)} %collective-permute-done.11.other_ref), custom_call_target="tpu_custom_call" | custom-call | flops 393216 | bytes 393216 | tf_op jit(solution)/shard_map/pallas_call | solution.py:237
  (13 shorter events, 0.1 us)
Async XLA Ops:
  0.0 12.3 %copy-start = (bf16[2,384,256]{2,1,0:T(8,128)(2,1)S(1)}, bf16[2,384,256]{2,1,0:T(8,128)(2,1)}, u32[]{:S(2)}) copy-start(bf16[2,384,256]{2,1,0:T(8,128)(2,1)} %own_ref.3) | copy-start | bytes 1179652
  0.0 18.7 %copy-start.1 = (bf16[1,2,384,1024]{3,2,1,0:T(8,128)(2,1)S(1)}, bf16[1,2,384,1024]{3,2,1,0:T(8,128)(2,1)}, u32[]{:S(2)}) copy-start(bf16[1,2,384,1024]{3,2,1,0:T(8,128)(2,1)} %sec_ref.1) | copy-start | bytes 4718596
  1.0 10.5 %collective-permute-start = (bf16[2,128,256]{2,1,0:T(8,128)(2,1)S(1)}, bf16[2,128,256]{2,1,0:T(8,128)(2,1)S(1)}, u32[]{:S(2)}, u32[]{:S(2)}) collective-permute-start(bf16[2,128,256]{2,1,0:T(8,128)(2,1)S(1)} %pad_maximum_fusion), channel_id=1, source_target_pairs={{0,2},{1,3},{2,0},{3,1},{4,6},{5,7},{6,4},{7,5},{8,10},{9,11},{10,... | collective-permute-start | bytes 393224 | tf_op jit(solution)/shard_map/ppermute | solution.py:254
  5.2 7.1 %collective-permute-start.1 = (bf16[2,128,256]{2,1,0:T(8,128)(2,1)S(1)}, bf16[2,128,256]{2,1,0:T(8,128)(2,1)S(1)}, u32[]{:S(2)}, u32[]{:S(2)}) collective-permute-start(bf16[2,128,256]{2,1,0:T(8,128)(2,1)S(1)} %pad_maximum_fusion), channel_id=1, source_target_pairs={{0,1},{1,0},{2,3},{3,2},{4,5},{5,4},{6,7},{7,6},{8,9},{9,8},{10,11... | collective-permute-start | bytes 393224 | tf_op jit(solution)/shard_map/ppermute | solution.py:254
  7.7 11.0 %collective-permute-start.4 = (bf16[2,32,1024]{2,1,0:T(8,128)(2,1)S(1)}, bf16[2,32,1024]{2,1,0:T(8,128)(2,1)S(1)}, u32[]{:S(2)}, u32[]{:S(2)}) collective-permute-start(bf16[2,32,1024]{2,1,0:T(8,128)(2,1)S(1)} %get-tuple-element.16), channel_id=1, source_target_pairs={{0,4},{4,8},{8,12},{12,16},{16,20},{20,24},{24,28},{28,0},{1,5},{5... | collective-permute-start | bytes 393224 | tf_op jit(solution)/shard_map/ppermute | solution.py:250
  7.8 11.0 %collective-permute-start.5 = (bf16[2,32,1024]{2,1,0:T(8,128)(2,1)S(1)}, bf16[2,32,1024]{2,1,0:T(8,128)(2,1)S(1)}, u32[]{:S(2)}, u32[]{:S(2)}) collective-permute-start(bf16[2,32,1024]{2,1,0:T(8,128)(2,1)S(1)} %get-tuple-element.15), channel_id=1, source_target_pairs={{0,28},{4,0},{8,4},{12,8},{16,12},{20,16},{24,20},{28,24},{1,29},{... | collective-permute-start | bytes 393224 | tf_op jit(solution)/shard_map/ppermute | solution.py:250
  11.6 8.6 %collective-permute-start.3 = (bf16[2,128,256]{2,1,0:T(8,128)(2,1)S(1)}, bf16[2,128,256]{2,1,0:T(8,128)(2,1)S(1)}, u32[]{:S(2)}, u32[]{:S(2)}) collective-permute-start(bf16[2,128,256]{2,1,0:T(8,128)(2,1)S(1)} %shard_map.74), channel_id=1, source_target_pairs={{0,1},{1,0},{2,3},{3,2},{4,5},{5,4},{6,7},{7,6},{8,9},{9,8},{10,11... | collective-permute-start | bytes 393224 | tf_op jit(solution)/shard_map/ppermute | solution.py:254
  12.3 16.1 %collective-permute-start.2 = (bf16[2,272,256]{2,1,0:T(8,128)(2,1)S(1)}, bf16[2,272,256]{2,1,0:T(8,128)(2,1)S(1)}, u32[]{:S(2)}, u32[]{:S(2)}) collective-permute-start(bf16[2,272,256]{2,1,0:T(8,128)(2,1)S(1)} %shard_map.73), channel_id=1, source_target_pairs={{0,2},{1,3},{2,0},{3,1},{4,6},{5,7},{6,4},{7,5},{8,10},{9,11},{10,... | collective-permute-start | bytes 835592 | tf_op jit(solution)/shard_map/ppermute | solution.py:254
  15.7 12.8 %collective-permute-start.8 = (bf16[2,272,256]{2,1,0:T(8,128)(2,1)S(1)}, bf16[2,272,256]{2,1,0:T(8,128)(2,1)S(1)}, u32[]{:S(2)}, u32[]{:S(2)}) collective-permute-start(bf16[2,272,256]{2,1,0:T(8,128)(2,1)S(1)} %shard_map.73), channel_id=1, source_target_pairs={{0,1},{1,0},{2,3},{3,2},{4,5},{5,4},{6,7},{7,6},{8,9},{9,8},{10,11... | collective-permute-start | bytes 835592 | tf_op jit(solution)/shard_map/ppermute | solution.py:254
  20.7 5.5 %collective-permute-start.6 = (bf16[2,64,1024]{2,1,0:T(8,128)(2,1)S(1)}, bf16[2,64,1024]{2,1,0:T(8,128)(2,1)S(1)}, u32[]{:S(2)}, u32[]{:S(2)}) collective-permute-start(bf16[2,64,1024]{2,1,0:T(8,128)(2,1)S(1)} %get-tuple-element.13), channel_id=1, source_target_pairs={{0,28},{4,0},{8,4},{12,8},{16,12},{20,16},{24,20},{28,24},{1,29},{... | collective-permute-start | bytes 786440 | tf_op jit(solution)/shard_map/ppermute | solution.py:250
  26.6 3.7 %collective-permute-start.7 = (f32[8,128]{1,0:T(8,128)S(1)}, f32[8,128]{1,0:T(8,128)S(1)}, u32[]{:S(2)}, u32[]{:S(2)}) collective-permute-start(f32[8,128]{1,0:T(8,128)S(1)} %shard_map.78), channel_id=1, source_target_pairs={{0,16},{4,20},{8,24},{12,28},{16,0},{20,4},{24,8},{28,12},{1,17},{... | collective-permute-start | bytes 12296 | tf_op jit(solution)/shard_map/ppermute | solution.py:254
  30.3 7.9 %collective-permute-start.9 = (bf16[2,256,256]{2,1,0:T(8,128)(2,1)S(1)}, bf16[2,256,256]{2,1,0:T(8,128)(2,1)S(1)}, u32[]{:S(2)}, u32[]{:S(2)}) collective-permute-start(bf16[2,256,256]{2,1,0:T(8,128)(2,1)S(1)} %shard_map.79), channel_id=1, source_target_pairs={{0,1},{1,0},{2,3},{3,2},{4,5},{5,4},{6,7},{7,6},{8,9},{9,8},{10,11... | collective-permute-start | bytes 786440 | tf_op jit(solution)/shard_map/ppermute | solution.py:254
  32.1 3.6 %collective-permute-start.10 = (f32[8,128]{1,0:T(8,128)S(1)}, f32[8,128]{1,0:T(8,128)S(1)}, u32[]{:S(2)}, u32[]{:S(2)}) collective-permute-start(f32[8,128]{1,0:T(8,128)S(1)} %add.6), channel_id=1, source_target_pairs={{0,8},{4,12},{8,0},{12,4},{16,24},{20,28},{24,16},{28,20},{1,9},{5... | collective-permute-start | bytes 12296 | tf_op jit(solution)/shard_map/ppermute | solution.py:254
  35.7 2.8 %collective-permute-start.11 = (f32[8,128]{1,0:T(8,128)S(1)}, f32[8,128]{1,0:T(8,128)S(1)}, u32[]{:S(2)}, u32[]{:S(2)}) collective-permute-start(f32[8,128]{1,0:T(8,128)S(1)} %add.7.mine_ref), channel_id=1, source_target_pairs={{0,4},{4,0},{8,12},{12,8},{16,20},{20,16},{24,28},{28,24},{1,5},{5... | collective-permute-start | bytes 12296 | tf_op jit(solution)/shard_map/ppermute | solution.py:254

commit v29 on v27

--- a/solution.py
+++ b/solution.py
@@ -149,9 +149,10 @@
             for part in range(2):
                 target[part, :, columns] = pair[part]
             halves.append(pair)
+        both = jnp.concatenate([halves[at][part] for part in range(2) for at in range(2)], axis=0)
+        sums = jnp.dot(both, select, preferred_element_type=jnp.float32)
         for part in range(2):
-            both = jnp.concatenate([halves[0][part], halves[1][part]], axis=0)
-            summed = jnp.dot(both, select, preferred_element_type=jnp.float32)
+            summed = sums[part * 2 * LAG : (part + 1) * 2 * LAG]
             totals[part] = summed if step == 0 else totals[part] + summed
     for part in range(2):
         sums_ref[part] = totals[part]
@@ -195,10 +196,10 @@
             res_ref[block, 0, LAG : rows_n - LAG],
             res_ref[block, 1, LAG : rows_n - LAG],
         )
+        both = jnp.concatenate([value.astype(jnp.bfloat16) for value in pair], axis=0)
+        sums = jnp.dot(both, select, preferred_element_type=jnp.float32)
         for part in range(2):
-            summed = jnp.dot(
-                pair[part].astype(jnp.bfloat16), select, preferred_element_type=jnp.float32
-            )
+            summed = sums[part * middle_n : (part + 1) * middle_n]
             totals[part] = summed if at == 0 else totals[part] + summed
     return totals
 

time: 38.4 us -> 38.4 us (level)
  no operation moved by 1% of the time
where the time goes in v29:
time: 38.4 us; the launch traced here: 38.2 us
  starting transfers between devices  19.3 us (50%)
  waiting for transfers between devices  8.94 us (23%)
  Pallas kernels  4.42 us (12%)
  between operations  2.7 us (7%)
  local copies, waits for them, and re-layouts  2.09 us (5%)
  other arithmetic  0.77 us (2%)
    ppermute x9, starting transfers between devices, swap(): lax.ppermute(value, axis, [(at, at ^ step) for at in range(lax.axis_size(...  15 us
    ppermute x9, waiting for transfers between devices, swap(): lax.ppermute(value, axis, [(at, at ^ step) for at in range(lax.axis_size(...  5.8 us
    pallas_call x10, Pallas kernels, call(): pl.pallas_call(kernel, out_shape=outs, in_specs=[vmem] * len(args), out_s...  4.42 us
    ppermute x3, starting transfers between devices, ring(): lax.ppermute(value, axis, [(at, (at + step) % count) for at in range(coun...  4.24 us
    ppermute x3, waiting for transfers between devices, ring(): lax.ppermute(value, axis, [(at, (at + step) % count) for at in range(coun...  3.14 us
    slice x1, local copies, waits for them, and re-layouts, fused(): primary[:, :LAG]  1.02 us
    squeeze x1, local copies, waits for them, and re-layouts, fused(): down, up = (secondary[0, :, rows_n - HALO:], secondary[0, :, :HALO])  0.99 us
  transfers between devices with their start and end apart: 12, of which 7 were waited for; matrix products, arithmetic and copies ran while one was open for 5% of the time, Pallas kernels for 9%

profile of v29, /device:TPU:0, one launch (start us, length us, event | category | flops | bytes accessed | tf_op | source)
XLA Modules:
  0.0 38.2 jit_solution(201995006648261615)
XLA Ops:
  0.0 1.0 %fusion = (bf16[2,64,256]{2,1,0:T(8,128)(2,1)S(1)}, bf16[2,64,256]{2,1,0:T(8,128)(2,1)S(1)}) fusion(bf16[2,384,256]{2,1,0:T(8,128)(2,1)} %own_ref.3), kind=kLoop, calls=%fused_computation.4 | loop fusion | bytes 262144 | tf_op jit(solution)/shard_map/slice | solution.py:267
  1.0 4.1 %collective-permute-start = (bf16[2,128,256]{2,1,0:T(8,128)(2,1)S(1)}, bf16[2,128,256]{2,1,0:T(8,128)(2,1)S(1)}, u32[]{:S(2)}, u32[]{:S(2)}) collective-permute-start(bf16[2,128,256]{2,1,0:T(8,128)(2,1)S(1)} %pad_maximum_fusion), channel_id=1, source_target_pairs={{0,2},{1,3},{2,0},{3,1},{4,6},{5,7},{6,4},{7,5},{8,10},{9,11},{10,... | collective-permute-start | bytes 393224 | tf_op jit(solution)/shard_map/ppermute | solution.py:255
  5.2 1.6 %collective-permute-start.1 = (bf16[2,128,256]{2,1,0:T(8,128)(2,1)S(1)}, bf16[2,128,256]{2,1,0:T(8,128)(2,1)S(1)}, u32[]{:S(2)}, u32[]{:S(2)}) collective-permute-start(bf16[2,128,256]{2,1,0:T(8,128)(2,1)S(1)} %pad_maximum_fusion), channel_id=1, source_target_pairs={{0,1},{1,0},{2,3},{3,2},{4,5},{5,4},{6,7},{7,6},{8,9},{9,8},{10,11... | collective-permute-start | bytes 393224 | tf_op jit(solution)/shard_map/ppermute | solution.py:255
  6.7 1.0 %slice_bitcast_fusion = (bf16[2,32,1024]{2,1,0:T(8,128)(2,1)S(1)}, bf16[2,32,1024]{2,1,0:T(8,128)(2,1)S(1)}) fusion(bf16[1,2,384,1024]{3,2,1,0:T(8,128)(2,1)} %sec_ref.1), kind=kLoop, calls=%fused_computation.1 | loop fusion | bytes 524288 | tf_op jit(solution)/shard_map/squeeze | solution.py:270
  7.7 0.1 collective-permute-start.4
  7.8 2.6 %collective-permute-start.5 = (bf16[2,32,1024]{2,1,0:T(8,128)(2,1)S(1)}, bf16[2,32,1024]{2,1,0:T(8,128)(2,1)S(1)}, u32[]{:S(2)}, u32[]{:S(2)}) collective-permute-start(bf16[2,32,1024]{2,1,0:T(8,128)(2,1)S(1)} %get-tuple-element.15), channel_id=1, source_target_pairs={{0,28},{4,0},{8,4},{12,8},{16,12},{20,16},{24,20},{28,24},{1,29},{... | collective-permute-start | bytes 393224 | tf_op jit(solution)/shard_map/ppermute | solution.py:251
  10.4 1.1 %collective-permute-done.refs_0_.block_ref.two_ref = bf16[2,128,256]{2,1,0:T(8,128)(2,1)S(1)} collective-permute-done((bf16[2,128,256]{2,1,0:T(8,128)(2,1)S(1)}, bf16[2,128,256]{2,1,0:T(8,128)(2,1)S(1)}, u32[]{:S(2)}, u32[]{:S(2)}) %collective-permute-start) | collective-permute-done | bytes 131104 | tf_op jit(solution)/shard_map/ppermute | solution.py:255
  11.6 0.7 %collective-permute-start.3 = (bf16[2,128,256]{2,1,0:T(8,128)(2,1)S(1)}, bf16[2,128,256]{2,1,0:T(8,128)(2,1)S(1)}, u32[]{:S(2)}, u32[]{:S(2)}) collective-permute-start(bf16[2,128,256]{2,1,0:T(8,128)(2,1)S(1)} %shard_map.74), channel_id=1, source_target_pairs={{0,1},{1,0},{2,3},{3,2},{4,5},{5,4},{6,7},{7,6},{8,9},{9,8},{10,11... | collective-permute-start | bytes 393224 | tf_op jit(solution)/shard_map/ppermute | solution.py:255
  12.3 3.4 %collective-permute-start.2 = (bf16[2,272,256]{2,1,0:T(8,128)(2,1)S(1)}, bf16[2,272,256]{2,1,0:T(8,128)(2,1)S(1)}, u32[]{:S(2)}, u32[]{:S(2)}) collective-permute-start(bf16[2,272,256]{2,1,0:T(8,128)(2,1)S(1)} %shard_map.73), channel_id=1, source_target_pairs={{0,2},{1,3},{2,0},{3,1},{4,6},{5,7},{6,4},{7,5},{8,10},{9,11},{10,... | collective-permute-start | bytes 835592 | tf_op jit(solution)/shard_map/ppermute | solution.py:255
  15.7 0.0 collective-permute-start.8
  18.4 0.4 shard_map.75
  18.7 0.0 collective-permute-done.5.high_ref
  18.8 1.4 %shard_map.76.res_ref = bf16[4,2,384,256]{3,2,1,0:T(8,128)(2,1)S(1)} custom-call(bf16[1,2,384,1024]{3,2,1,0:T(8,128)(2,1)S(1)} %copy-done.1, bf16[2,32,1024]{2,1,0:T(8,128)(2,1)S(1)} %collective-permute-done.4.low_ref, bf16[2,32,1024]{2,1,0:T(8,128)(2,1)S(1)} %collective-permute-done.5.high_ref, bf16[128,192]{1,0:T(8,128)(2,1)S(1)} %get-tuple-element.10.az_ref, ...), custom_call_target="tpu_custom_call" | custom-call | tf_op jit(solution)/shard_map/pallas_call | solution.py:238
  20.2 0.0 collective-permute-done.3.three_ref
  20.2 0.6 %shard_map.77 = (bf16[2,64,1024]{2,1,0:T(8,128)(2,1)S(1)}, bf16[2,64,1024]{2,1,0:T(8,128)(2,1)S(1)}, f32[2,64,128]{2,1,0:T(8,128)S(1)}) custom-call(bf16[2,384,256]{2,1,0:T(8,128)(2,1)S(1)} %copy-done, bf16[2,128,256]{2,1,0:T(8,128)(2,1)S(1)} %collective-permute-done.1.refs_1_.one_ref, ...), custom_call_target="tpu_custom_call" | custom-call | tf_op jit(solution)/shard_map/pallas_call | solution.py:238
  20.7 1.6 %collective-permute-start.6 = (bf16[2,64,1024]{2,1,0:T(8,128)(2,1)S(1)}, bf16[2,64,1024]{2,1,0:T(8,128)(2,1)S(1)}, u32[]{:S(2)}, u32[]{:S(2)}) collective-permute-start(bf16[2,64,1024]{2,1,0:T(8,128)(2,1)S(1)} %get-tuple-element.13), channel_id=1, source_target_pairs={{0,28},{4,0},{8,4},{12,8},{16,12},{20,16},{24,20},{28,24},{1,29},{... | collective-permute-start | bytes 786440 | tf_op jit(solution)/shard_map/ppermute | solution.py:251
  22.3 0.8 %slice_convert_fusion = f32[64]{0:T(128)S(1)} fusion(s32[384]{0:T(512)} %param.9), kind=kLoop, calls=%fused_computation.3 | loop fusion | flops 64 | bytes 512 | tf_op jit(solution)/shard_map/convert_element_type | solution.py:291
  23.0 3.1 %collective-permute-done.6.later_ref = bf16[2,64,1024]{2,1,0:T(8,128)(2,1)S(1)} collective-permute-done((bf16[2,64,1024]{2,1,0:T(8,128)(2,1)S(1)}, bf16[2,64,1024]{2,1,0:T(8,128)(2,1)S(1)}, u32[]{:S(2)}, u32[]{:S(2)}) %collective-permute-start.6) | collective-permute-done | bytes 262176 | tf_op jit(solution)/shard_map/ppermute | solution.py:251
  26.2 0.1 broadcast_in_dim.2.weight_ref
  26.2 0.4 shard_map.78
  26.6 0.6 %collective-permute-start.7 = (f32[8,128]{1,0:T(8,128)S(1)}, f32[8,128]{1,0:T(8,128)S(1)}, u32[]{:S(2)}, u32[]{:S(2)}) collective-permute-start(f32[8,128]{1,0:T(8,128)S(1)} %shard_map.78), channel_id=1, source_target_pairs={{0,4},{4,0},{8,12},{12,8},{16,20},{20,16},{24,28},{28,24},{1,5},{5... | collective-permute-start | bytes 12296 | tf_op jit(solution)/shard_map/ppermute | solution.py:255
  27.2 1.2 %collective-permute-done.2.block_ref.two_ref = bf16[2,272,256]{2,1,0:T(8,128)(2,1)S(1)} collective-permute-done((bf16[2,272,256]{2,1,0:T(8,128)(2,1)S(1)}, bf16[2,272,256]{2,1,0:T(8,128)(2,1)S(1)}, u32[]{:S(2)}, u32[]{:S(2)}) %collective-permute-start.2) | collective-permute-done | bytes 278560 | tf_op jit(solution)/shard_map/ppermute | solution.py:255
  28.4 0.1 collective-permute-done.8.refs_1_.one_ref
  28.6 1.6 %collective-permute-start.9 = (bf16[2,256,256]{2,1,0:T(8,128)(2,1)S(1)}, bf16[2,256,256]{2,1,0:T(8,128)(2,1)S(1)}, u32[]{:S(2)}, u32[]{:S(2)}) collective-permute-start(bf16[2,256,256]{2,1,0:T(8,128)(2,1)S(1)} %shard_map.79), channel_id=1, source_target_pairs={{0,1},{1,0},{2,3},{3,2},{4,5},{5,4},{6,7},{7,6},{8,9},{9,8},{10,11... | collective-permute-start | bytes 786440 | tf_op jit(solution)/shard_map/ppermute | solution.py:255
  30.1 1.5 %collective-permute-start.10 = (f32[8,128]{1,0:T(8,128)S(1)}, f32[8,128]{1,0:T(8,128)S(1)}, u32[]{:S(2)}, u32[]{:S(2)}) collective-permute-start(f32[8,128]{1,0:T(8,128)S(1)} %add.6), channel_id=1, source_target_pairs={{0,8},{4,12},{8,0},{12,4},{16,24},{20,28},{24,16},{28,20},{1,9},{5... | collective-permute-start | bytes 12296 | tf_op jit(solution)/shard_map/ppermute | solution.py:255
  31.6 0.6 %shard_map.80.before_ref = f32[2,256,128]{2,1,0:T(8,128)S(1)} custom-call(bf16[2,384,256]{2,1,0:T(8,128)(2,1)S(1)} %copy-done, bf16[2,272,256]{2,1,0:T(8,128)(2,1)S(1)} %collective-permute-done.8.refs_1_.one_ref, bf16[2,272,256]{2,1,0:T(8,128)(2,1)S(1)} %collective-permute-done.2.block_ref.two_ref, bf16[4,2,384,256]{3,2,1,0:T(8,128)(2,1)S(1)} %shard_map.76.res_ref), custom_call_target="tpu_custom_call" | custom-call | flops 134217728 | bytes 3145728 | tf_op jit(solution)/shard_map/pallas_call | solution.py:238
  32.2 1.5 %collective-permute-done.10 = f32[8,128]{1,0:T(8,128)S(1)} collective-permute-done((f32[8,128]{1,0:T(8,128)S(1)}, f32[8,128]{1,0:T(8,128)S(1)}, u32[]{:S(2)}, u32[]{:S(2)}) %collective-permute-start.10) | collective-permute-done | bytes 4128 | tf_op jit(solution)/shard_map/ppermute | solution.py:255
  33.8 1.5 %collective-permute-start.11 = (f32[8,128]{1,0:T(8,128)S(1)}, f32[8,128]{1,0:T(8,128)S(1)}, u32[]{:S(2)}, u32[]{:S(2)}) collective-permute-start(f32[8,128]{1,0:T(8,128)S(1)} %add.7.mine_ref), channel_id=1, source_target_pairs={{0,16},{4,20},{8,24},{12,28},{16,0},{20,4},{24,8},{28,12},{1,17},{... | collective-permute-start | bytes 12296 | tf_op jit(solution)/shard_map/ppermute | solution.py:255
  35.3 1.7 %collective-permute-done.9.three_ref = bf16[2,256,256]{2,1,0:T(8,128)(2,1)S(1)} collective-permute-done((bf16[2,256,256]{2,1,0:T(8,128)(2,1)S(1)}, bf16[2,256,256]{2,1,0:T(8,128)(2,1)S(1)}, u32[]{:S(2)}, u32[]{:S(2)}) %collective-permute-start.9) | collective-permute-done | bytes 262176 | tf_op jit(solution)/shard_map/ppermute | solution.py:255
  37.0 0.3 shard_map.81.looks_ref
  37.2 0.1 collective-permute-done.11.other_ref
  37.4 0.8 %shard_map.82 = f32[1,2,192,128]{3,2,1,0:T(8,128)} custom-call(f32[2,192,128]{2,1,0:T(8,128)S(1)} %shard_map.81.looks_ref, f32[8,128]{1,0:T(8,128)S(1)} %add.7.mine_ref, f32[8,128]{1,0:T(8,128)S(1)} %collective-permute-done.11.other_ref), custom_call_target="tpu_custom_call" | custom-call | flops 393216 | bytes 393216 | tf_op jit(solution)/shard_map/pallas_call | solution.py:238
  (13 shorter events, 0.1 us)
Async XLA Ops:
  0.0 12.3 %copy-start = (bf16[2,384,256]{2,1,0:T(8,128)(2,1)S(1)}, bf16[2,384,256]{2,1,0:T(8,128)(2,1)}, u32[]{:S(2)}) copy-start(bf16[2,384,256]{2,1,0:T(8,128)(2,1)} %own_ref.3) | copy-start | bytes 1179652
  0.0 18.7 %copy-start.1 = (bf16[1,2,384,1024]{3,2,1,0:T(8,128)(2,1)S(1)}, bf16[1,2,384,1024]{3,2,1,0:T(8,128)(2,1)}, u32[]{:S(2)}) copy-start(bf16[1,2,384,1024]{3,2,1,0:T(8,128)(2,1)} %sec_ref.1) | copy-start | bytes 4718596
  1.0 10.5 %collective-permute-start = (bf16[2,128,256]{2,1,0:T(8,128)(2,1)S(1)}, bf16[2,128,256]{2,1,0:T(8,128)(2,1)S(1)}, u32[]{:S(2)}, u32[]{:S(2)}) collective-permute-start(bf16[2,128,256]{2,1,0:T(8,128)(2,1)S(1)} %pad_maximum_fusion), channel_id=1, source_target_pairs={{0,2},{1,3},{2,0},{3,1},{4,6},{5,7},{6,4},{7,5},{8,10},{9,11},{10,... | collective-permute-start | bytes 393224 | tf_op jit(solution)/shard_map/ppermute | solution.py:255
  5.2 7.1 %collective-permute-start.1 = (bf16[2,128,256]{2,1,0:T(8,128)(2,1)S(1)}, bf16[2,128,256]{2,1,0:T(8,128)(2,1)S(1)}, u32[]{:S(2)}, u32[]{:S(2)}) collective-permute-start(bf16[2,128,256]{2,1,0:T(8,128)(2,1)S(1)} %pad_maximum_fusion), channel_id=1, source_target_pairs={{0,1},{1,0},{2,3},{3,2},{4,5},{5,4},{6,7},{7,6},{8,9},{9,8},{10,11... | collective-permute-start | bytes 393224 | tf_op jit(solution)/shard_map/ppermute | solution.py:255
  7.7 11.0 %collective-permute-start.4 = (bf16[2,32,1024]{2,1,0:T(8,128)(2,1)S(1)}, bf16[2,32,1024]{2,1,0:T(8,128)(2,1)S(1)}, u32[]{:S(2)}, u32[]{:S(2)}) collective-permute-start(bf16[2,32,1024]{2,1,0:T(8,128)(2,1)S(1)} %get-tuple-element.16), channel_id=1, source_target_pairs={{0,4},{4,8},{8,12},{12,16},{16,20},{20,24},{24,28},{28,0},{1,5},{5... | collective-permute-start | bytes 393224 | tf_op jit(solution)/shard_map/ppermute | solution.py:251
  7.8 11.0 %collective-permute-start.5 = (bf16[2,32,1024]{2,1,0:T(8,128)(2,1)S(1)}, bf16[2,32,1024]{2,1,0:T(8,128)(2,1)S(1)}, u32[]{:S(2)}, u32[]{:S(2)}) collective-permute-start(bf16[2,32,1024]{2,1,0:T(8,128)(2,1)S(1)} %get-tuple-element.15), channel_id=1, source_target_pairs={{0,28},{4,0},{8,4},{12,8},{16,12},{20,16},{24,20},{28,24},{1,29},{... | collective-permute-start | bytes 393224 | tf_op jit(solution)/shard_map/ppermute | solution.py:251
  11.6 8.6 %collective-permute-start.3 = (bf16[2,128,256]{2,1,0:T(8,128)(2,1)S(1)}, bf16[2,128,256]{2,1,0:T(8,128)(2,1)S(1)}, u32[]{:S(2)}, u32[]{:S(2)}) collective-permute-start(bf16[2,128,256]{2,1,0:T(8,128)(2,1)S(1)} %shard_map.74), channel_id=1, source_target_pairs={{0,1},{1,0},{2,3},{3,2},{4,5},{5,4},{6,7},{7,6},{8,9},{9,8},{10,11... | collective-permute-start | bytes 393224 | tf_op jit(solution)/shard_map/ppermute | solution.py:255
  12.3 16.1 %collective-permute-start.2 = (bf16[2,272,256]{2,1,0:T(8,128)(2,1)S(1)}, bf16[2,272,256]{2,1,0:T(8,128)(2,1)S(1)}, u32[]{:S(2)}, u32[]{:S(2)}) collective-permute-start(bf16[2,272,256]{2,1,0:T(8,128)(2,1)S(1)} %shard_map.73), channel_id=1, source_target_pairs={{0,2},{1,3},{2,0},{3,1},{4,6},{5,7},{6,4},{7,5},{8,10},{9,11},{10,... | collective-permute-start | bytes 835592 | tf_op jit(solution)/shard_map/ppermute | solution.py:255
  15.7 12.8 %collective-permute-start.8 = (bf16[2,272,256]{2,1,0:T(8,128)(2,1)S(1)}, bf16[2,272,256]{2,1,0:T(8,128)(2,1)S(1)}, u32[]{:S(2)}, u32[]{:S(2)}) collective-permute-start(bf16[2,272,256]{2,1,0:T(8,128)(2,1)S(1)} %shard_map.73), channel_id=1, source_target_pairs={{0,1},{1,0},{2,3},{3,2},{4,5},{5,4},{6,7},{7,6},{8,9},{9,8},{10,11... | collective-permute-start | bytes 835592 | tf_op jit(solution)/shard_map/ppermute | solution.py:255
  20.7 5.4 %collective-permute-start.6 = (bf16[2,64,1024]{2,1,0:T(8,128)(2,1)S(1)}, bf16[2,64,1024]{2,1,0:T(8,128)(2,1)S(1)}, u32[]{:S(2)}, u32[]{:S(2)}) collective-permute-start(bf16[2,64,1024]{2,1,0:T(8,128)(2,1)S(1)} %get-tuple-element.13), channel_id=1, source_target_pairs={{0,28},{4,0},{8,4},{12,8},{16,12},{20,16},{24,20},{28,24},{1,29},{... | collective-permute-start | bytes 786440 | tf_op jit(solution)/shard_map/ppermute | solution.py:251
  26.6 1.9 %collective-permute-start.7 = (f32[8,128]{1,0:T(8,128)S(1)}, f32[8,128]{1,0:T(8,128)S(1)}, u32[]{:S(2)}, u32[]{:S(2)}) collective-permute-start(f32[8,128]{1,0:T(8,128)S(1)} %shard_map.78), channel_id=1, source_target_pairs={{0,4},{4,0},{8,12},{12,8},{16,20},{20,16},{24,28},{28,24},{1,5},{5... | collective-permute-start | bytes 12296 | tf_op jit(solution)/shard_map/ppermute | solution.py:255
  28.6 8.4 %collective-permute-start.9 = (bf16[2,256,256]{2,1,0:T(8,128)(2,1)S(1)}, bf16[2,256,256]{2,1,0:T(8,128)(2,1)S(1)}, u32[]{:S(2)}, u32[]{:S(2)}) collective-permute-start(bf16[2,256,256]{2,1,0:T(8,128)(2,1)S(1)} %shard_map.79), channel_id=1, source_target_pairs={{0,1},{1,0},{2,3},{3,2},{4,5},{5,4},{6,7},{7,6},{8,9},{9,8},{10,11... | collective-permute-start | bytes 786440 | tf_op jit(solution)/shard_map/ppermute | solution.py:255
  30.1 3.6 %collective-permute-start.10 = (f32[8,128]{1,0:T(8,128)S(1)}, f32[8,128]{1,0:T(8,128)S(1)}, u32[]{:S(2)}, u32[]{:S(2)}) collective-permute-start(f32[8,128]{1,0:T(8,128)S(1)} %add.6), channel_id=1, source_target_pairs={{0,8},{4,12},{8,0},{12,4},{16,24},{20,28},{24,16},{28,20},{1,9},{5... | collective-permute-start | bytes 12296 | tf_op jit(solution)/shard_map/ppermute | solution.py:255
  33.8 3.6 %collective-permute-start.11 = (f32[8,128]{1,0:T(8,128)S(1)}, f32[8,128]{1,0:T(8,128)S(1)}, u32[]{:S(2)}, u32[]{:S(2)}) collective-permute-start(f32[8,128]{1,0:T(8,128)S(1)} %add.7.mine_ref), channel_id=1, source_target_pairs={{0,16},{4,20},{8,24},{12,28},{16,0},{20,4},{24,8},{28,12},{1,17},{... | collective-permute-start | bytes 12296 | tf_op jit(solution)/shard_map/ppermute | solution.py:255

commit v30 on v29

--- a/solution.py
+++ b/solution.py
@@ -96,10 +96,10 @@
         last = (block + 1) * width + LANE
         taken = slice(max(first, 0), min(last, cols_n))
         used = rg_band[taken.start - first : taken.stop - first]
+        both = jnp.concatenate([azim_ref[part, :, taken] for part in range(2)], axis=0)
+        sums = jnp.dot(both, used, preferred_element_type=jnp.float32).astype(jnp.bfloat16)
         for part in range(2):
-            out_ref[block, part] = jnp.dot(
-                azim_ref[part, :, taken], used, preferred_element_type=jnp.float32
-            ).astype(jnp.bfloat16)
+            out_ref[block, part] = sums[part * rows_n : (part + 1) * rows_n]
 
 
 def interfere(prim_re, prim_im, sec_re, sec_im):

time: 38.4 us -> 38.4 us (level)
  no operation moved by 1% of the time
where the time goes in v30:
time: 38.4 us; the launch traced here: 38.2 us
  starting transfers between devices  19.3 us (50%)
  waiting for transfers between devices  8.94 us (23%)
  Pallas kernels  4.42 us (12%)
  between operations  2.7 us (7%)
  local copies, waits for them, and re-layouts  2.09 us (5%)
  other arithmetic  0.77 us (2%)
    ppermute x9, starting transfers between devices, swap(): lax.ppermute(value, axis, [(at, at ^ step) for at in range(lax.axis_size(...  15 us
    ppermute x9, waiting for transfers between devices, swap(): lax.ppermute(value, axis, [(at, at ^ step) for at in range(lax.axis_size(...  5.8 us
    pallas_call x10, Pallas kernels, call(): pl.pallas_call(kernel, out_shape=outs, in_specs=[vmem] * len(args), out_s...  4.42 us
    ppermute x3, starting transfers between devices, ring(): lax.ppermute(value, axis, [(at, (at + step) % count) for at in range(coun...  4.24 us
    ppermute x3, waiting for transfers between devices, ring(): lax.ppermute(value, axis, [(at, (at + step) % count) for at in range(coun...  3.14 us
    slice x1, local copies, waits for them, and re-layouts, fused(): primary[:, :LAG]  1.02 us
    squeeze x1, local copies, waits for them, and re-layouts, fused(): down, up = (secondary[0, :, rows_n - HALO:], secondary[0, :, :HALO])  0.99 us
  transfers between devices with their start and end apart: 12, of which 7 were waited for; matrix products, arithmetic and copies ran while one was open for 5% of the time, Pallas kernels for 9%

profile of v30, /device:TPU:0, one launch (start us, length us, event | category | flops | bytes accessed | tf_op | source)
XLA Modules:
  0.0 38.2 jit_solution(13914872818541435774)
XLA Ops:
  0.0 1.0 %fusion = (bf16[2,64,256]{2,1,0:T(8,128)(2,1)S(1)}, bf16[2,64,256]{2,1,0:T(8,128)(2,1)S(1)}) fusion(bf16[2,384,256]{2,1,0:T(8,128)(2,1)} %own_ref.3), kind=kLoop, calls=%fused_computation.4 | loop fusion | bytes 262144 | tf_op jit(solution)/shard_map/slice | solution.py:267
  1.0 4.1 %collective-permute-start = (bf16[2,128,256]{2,1,0:T(8,128)(2,1)S(1)}, bf16[2,128,256]{2,1,0:T(8,128)(2,1)S(1)}, u32[]{:S(2)}, u32[]{:S(2)}) collective-permute-start(bf16[2,128,256]{2,1,0:T(8,128)(2,1)S(1)} %pad_maximum_fusion), channel_id=1, source_target_pairs={{0,2},{1,3},{2,0},{3,1},{4,6},{5,7},{6,4},{7,5},{8,10},{9,11},{10,... | collective-permute-start | bytes 393224 | tf_op jit(solution)/shard_map/ppermute | solution.py:255
  5.2 1.6 %collective-permute-start.1 = (bf16[2,128,256]{2,1,0:T(8,128)(2,1)S(1)}, bf16[2,128,256]{2,1,0:T(8,128)(2,1)S(1)}, u32[]{:S(2)}, u32[]{:S(2)}) collective-permute-start(bf16[2,128,256]{2,1,0:T(8,128)(2,1)S(1)} %pad_maximum_fusion), channel_id=1, source_target_pairs={{0,1},{1,0},{2,3},{3,2},{4,5},{5,4},{6,7},{7,6},{8,9},{9,8},{10,11... | collective-permute-start | bytes 393224 | tf_op jit(solution)/shard_map/ppermute | solution.py:255
  6.7 1.0 %slice_bitcast_fusion = (bf16[2,32,1024]{2,1,0:T(8,128)(2,1)S(1)}, bf16[2,32,1024]{2,1,0:T(8,128)(2,1)S(1)}) fusion(bf16[1,2,384,1024]{3,2,1,0:T(8,128)(2,1)} %sec_ref.1), kind=kLoop, calls=%fused_computation.1 | loop fusion | bytes 524288 | tf_op jit(solution)/shard_map/squeeze | solution.py:270
  7.7 0.1 collective-permute-start.4
  7.8 2.6 %collective-permute-start.5 = (bf16[2,32,1024]{2,1,0:T(8,128)(2,1)S(1)}, bf16[2,32,1024]{2,1,0:T(8,128)(2,1)S(1)}, u32[]{:S(2)}, u32[]{:S(2)}) collective-permute-start(bf16[2,32,1024]{2,1,0:T(8,128)(2,1)S(1)} %get-tuple-element.15), channel_id=1, source_target_pairs={{0,28},{4,0},{8,4},{12,8},{16,12},{20,16},{24,20},{28,24},{1,29},{... | collective-permute-start | bytes 393224 | tf_op jit(solution)/shard_map/ppermute | solution.py:251
  10.4 1.1 %collective-permute-done.refs_0_.block_ref.two_ref = bf16[2,128,256]{2,1,0:T(8,128)(2,1)S(1)} collective-permute-done((bf16[2,128,256]{2,1,0:T(8,128)(2,1)S(1)}, bf16[2,128,256]{2,1,0:T(8,128)(2,1)S(1)}, u32[]{:S(2)}, u32[]{:S(2)}) %collective-permute-start) | collective-permute-done | bytes 131104 | tf_op jit(solution)/shard_map/ppermute | solution.py:255
  11.6 0.7 %collective-permute-start.3 = (bf16[2,128,256]{2,1,0:T(8,128)(2,1)S(1)}, bf16[2,128,256]{2,1,0:T(8,128)(2,1)S(1)}, u32[]{:S(2)}, u32[]{:S(2)}) collective-permute-start(bf16[2,128,256]{2,1,0:T(8,128)(2,1)S(1)} %shard_map.74), channel_id=1, source_target_pairs={{0,1},{1,0},{2,3},{3,2},{4,5},{5,4},{6,7},{7,6},{8,9},{9,8},{10,11... | collective-permute-start | bytes 393224 | tf_op jit(solution)/shard_map/ppermute | solution.py:255
  12.3 3.4 %collective-permute-start.2 = (bf16[2,272,256]{2,1,0:T(8,128)(2,1)S(1)}, bf16[2,272,256]{2,1,0:T(8,128)(2,1)S(1)}, u32[]{:S(2)}, u32[]{:S(2)}) collective-permute-start(bf16[2,272,256]{2,1,0:T(8,128)(2,1)S(1)} %shard_map.73), channel_id=1, source_target_pairs={{0,2},{1,3},{2,0},{3,1},{4,6},{5,7},{6,4},{7,5},{8,10},{9,11},{10,... | collective-permute-start | bytes 835592 | tf_op jit(solution)/shard_map/ppermute | solution.py:255
  15.7 0.0 collective-permute-start.8
  18.4 0.4 shard_map.75
  18.7 0.0 collective-permute-done.5.high_ref
  18.8 1.4 %shard_map.76.res_ref = bf16[4,2,384,256]{3,2,1,0:T(8,128)(2,1)S(1)} custom-call(bf16[1,2,384,1024]{3,2,1,0:T(8,128)(2,1)S(1)} %copy-done.1, bf16[2,32,1024]{2,1,0:T(8,128)(2,1)S(1)} %collective-permute-done.4.low_ref, bf16[2,32,1024]{2,1,0:T(8,128)(2,1)S(1)} %collective-permute-done.5.high_ref, bf16[128,192]{1,0:T(8,128)(2,1)S(1)} %get-tuple-element.10.az_ref, ...), custom_call_target="tpu_custom_call" | custom-call | tf_op jit(solution)/shard_map/pallas_call | solution.py:238
  20.2 0.0 collective-permute-done.3.three_ref
  20.2 0.6 %shard_map.77 = (bf16[2,64,1024]{2,1,0:T(8,128)(2,1)S(1)}, bf16[2,64,1024]{2,1,0:T(8,128)(2,1)S(1)}, f32[2,64,128]{2,1,0:T(8,128)S(1)}) custom-call(bf16[2,384,256]{2,1,0:T(8,128)(2,1)S(1)} %copy-done, bf16[2,128,256]{2,1,0:T(8,128)(2,1)S(1)} %collective-permute-done.1.refs_1_.one_ref, ...), custom_call_target="tpu_custom_call" | custom-call | tf_op jit(solution)/shard_map/pallas_call | solution.py:238
  20.7 1.6 %collective-permute-start.6 = (bf16[2,64,1024]{2,1,0:T(8,128)(2,1)S(1)}, bf16[2,64,1024]{2,1,0:T(8,128)(2,1)S(1)}, u32[]{:S(2)}, u32[]{:S(2)}) collective-permute-start(bf16[2,64,1024]{2,1,0:T(8,128)(2,1)S(1)} %get-tuple-element.13), channel_id=1, source_target_pairs={{0,28},{4,0},{8,4},{12,8},{16,12},{20,16},{24,20},{28,24},{1,29},{... | collective-permute-start | bytes 786440 | tf_op jit(solution)/shard_map/ppermute | solution.py:251
  22.3 0.8 %slice_convert_fusion = f32[64]{0:T(128)S(1)} fusion(s32[384]{0:T(512)} %param.9), kind=kLoop, calls=%fused_computation.3 | loop fusion | flops 64 | bytes 512 | tf_op jit(solution)/shard_map/convert_element_type | solution.py:291
  23.0 3.1 %collective-permute-done.6.later_ref = bf16[2,64,1024]{2,1,0:T(8,128)(2,1)S(1)} collective-permute-done((bf16[2,64,1024]{2,1,0:T(8,128)(2,1)S(1)}, bf16[2,64,1024]{2,1,0:T(8,128)(2,1)S(1)}, u32[]{:S(2)}, u32[]{:S(2)}) %collective-permute-start.6) | collective-permute-done | bytes 262176 | tf_op jit(solution)/shard_map/ppermute | solution.py:251
  26.2 0.1 broadcast_in_dim.2.weight_ref
  26.2 0.4 shard_map.78
  26.6 0.6 %collective-permute-start.7 = (f32[8,128]{1,0:T(8,128)S(1)}, f32[8,128]{1,0:T(8,128)S(1)}, u32[]{:S(2)}, u32[]{:S(2)}) collective-permute-start(f32[8,128]{1,0:T(8,128)S(1)} %shard_map.78), channel_id=1, source_target_pairs={{0,4},{4,0},{8,12},{12,8},{16,20},{20,16},{24,28},{28,24},{1,5},{5... | collective-permute-start | bytes 12296 | tf_op jit(solution)/shard_map/ppermute | solution.py:255
  27.2 1.2 %collective-permute-done.2.block_ref.two_ref = bf16[2,272,256]{2,1,0:T(8,128)(2,1)S(1)} collective-permute-done((bf16[2,272,256]{2,1,0:T(8,128)(2,1)S(1)}, bf16[2,272,256]{2,1,0:T(8,128)(2,1)S(1)}, u32[]{:S(2)}, u32[]{:S(2)}) %collective-permute-start.2) | collective-permute-done | bytes 278560 | tf_op jit(solution)/shard_map/ppermute | solution.py:255
  28.4 0.1 collective-permute-done.8.refs_1_.one_ref
  28.6 1.6 %collective-permute-start.9 = (bf16[2,256,256]{2,1,0:T(8,128)(2,1)S(1)}, bf16[2,256,256]{2,1,0:T(8,128)(2,1)S(1)}, u32[]{:S(2)}, u32[]{:S(2)}) collective-permute-start(bf16[2,256,256]{2,1,0:T(8,128)(2,1)S(1)} %shard_map.79), channel_id=1, source_target_pairs={{0,1},{1,0},{2,3},{3,2},{4,5},{5,4},{6,7},{7,6},{8,9},{9,8},{10,11... | collective-permute-start | bytes 786440 | tf_op jit(solution)/shard_map/ppermute | solution.py:255
  30.1 1.5 %collective-permute-start.10 = (f32[8,128]{1,0:T(8,128)S(1)}, f32[8,128]{1,0:T(8,128)S(1)}, u32[]{:S(2)}, u32[]{:S(2)}) collective-permute-start(f32[8,128]{1,0:T(8,128)S(1)} %add.6), channel_id=1, source_target_pairs={{0,8},{4,12},{8,0},{12,4},{16,24},{20,28},{24,16},{28,20},{1,9},{5... | collective-permute-start | bytes 12296 | tf_op jit(solution)/shard_map/ppermute | solution.py:255
  31.6 0.6 %shard_map.80.before_ref = f32[2,256,128]{2,1,0:T(8,128)S(1)} custom-call(bf16[2,384,256]{2,1,0:T(8,128)(2,1)S(1)} %copy-done, bf16[2,272,256]{2,1,0:T(8,128)(2,1)S(1)} %collective-permute-done.8.refs_1_.one_ref, bf16[2,272,256]{2,1,0:T(8,128)(2,1)S(1)} %collective-permute-done.2.block_ref.two_ref, bf16[4,2,384,256]{3,2,1,0:T(8,128)(2,1)S(1)} %shard_map.76.res_ref), custom_call_target="tpu_custom_call" | custom-call | flops 134217728 | bytes 3145728 | tf_op jit(solution)/shard_map/pallas_call | solution.py:238
  32.2 1.5 %collective-permute-done.10 = f32[8,128]{1,0:T(8,128)S(1)} collective-permute-done((f32[8,128]{1,0:T(8,128)S(1)}, f32[8,128]{1,0:T(8,128)S(1)}, u32[]{:S(2)}, u32[]{:S(2)}) %collective-permute-start.10) | collective-permute-done | bytes 4128 | tf_op jit(solution)/shard_map/ppermute | solution.py:255
  33.8 1.5 %collective-permute-start.11 = (f32[8,128]{1,0:T(8,128)S(1)}, f32[8,128]{1,0:T(8,128)S(1)}, u32[]{:S(2)}, u32[]{:S(2)}) collective-permute-start(f32[8,128]{1,0:T(8,128)S(1)} %add.7.mine_ref), channel_id=1, source_target_pairs={{0,16},{4,20},{8,24},{12,28},{16,0},{20,4},{24,8},{28,12},{1,17},{... | collective-permute-start | bytes 12296 | tf_op jit(solution)/shard_map/ppermute | solution.py:255
  35.3 1.7 %collective-permute-done.9.three_ref = bf16[2,256,256]{2,1,0:T(8,128)(2,1)S(1)} collective-permute-done((bf16[2,256,256]{2,1,0:T(8,128)(2,1)S(1)}, bf16[2,256,256]{2,1,0:T(8,128)(2,1)S(1)}, u32[]{:S(2)}, u32[]{:S(2)}) %collective-permute-start.9) | collective-permute-done | bytes 262176 | tf_op jit(solution)/shard_map/ppermute | solution.py:255
  37.0 0.3 shard_map.81.looks_ref
  37.2 0.1 collective-permute-done.11.other_ref
  37.4 0.8 %shard_map.82 = f32[1,2,192,128]{3,2,1,0:T(8,128)} custom-call(f32[2,192,128]{2,1,0:T(8,128)S(1)} %shard_map.81.looks_ref, f32[8,128]{1,0:T(8,128)S(1)} %add.7.mine_ref, f32[8,128]{1,0:T(8,128)S(1)} %collective-permute-done.11.other_ref), custom_call_target="tpu_custom_call" | custom-call | flops 393216 | bytes 393216 | tf_op jit(solution)/shard_map/pallas_call | solution.py:238
  (13 shorter events, 0.1 us)
Async XLA Ops:
  0.0 12.3 %copy-start = (bf16[2,384,256]{2,1,0:T(8,128)(2,1)S(1)}, bf16[2,384,256]{2,1,0:T(8,128)(2,1)}, u32[]{:S(2)}) copy-start(bf16[2,384,256]{2,1,0:T(8,128)(2,1)} %own_ref.3) | copy-start | bytes 1179652
  0.0 18.7 %copy-start.1 = (bf16[1,2,384,1024]{3,2,1,0:T(8,128)(2,1)S(1)}, bf16[1,2,384,1024]{3,2,1,0:T(8,128)(2,1)}, u32[]{:S(2)}) copy-start(bf16[1,2,384,1024]{3,2,1,0:T(8,128)(2,1)} %sec_ref.1) | copy-start | bytes 4718596
  1.0 10.5 %collective-permute-start = (bf16[2,128,256]{2,1,0:T(8,128)(2,1)S(1)}, bf16[2,128,256]{2,1,0:T(8,128)(2,1)S(1)}, u32[]{:S(2)}, u32[]{:S(2)}) collective-permute-start(bf16[2,128,256]{2,1,0:T(8,128)(2,1)S(1)} %pad_maximum_fusion), channel_id=1, source_target_pairs={{0,2},{1,3},{2,0},{3,1},{4,6},{5,7},{6,4},{7,5},{8,10},{9,11},{10,... | collective-permute-start | bytes 393224 | tf_op jit(solution)/shard_map/ppermute | solution.py:255
  5.2 7.1 %collective-permute-start.1 = (bf16[2,128,256]{2,1,0:T(8,128)(2,1)S(1)}, bf16[2,128,256]{2,1,0:T(8,128)(2,1)S(1)}, u32[]{:S(2)}, u32[]{:S(2)}) collective-permute-start(bf16[2,128,256]{2,1,0:T(8,128)(2,1)S(1)} %pad_maximum_fusion), channel_id=1, source_target_pairs={{0,1},{1,0},{2,3},{3,2},{4,5},{5,4},{6,7},{7,6},{8,9},{9,8},{10,11... | collective-permute-start | bytes 393224 | tf_op jit(solution)/shard_map/ppermute | solution.py:255
  7.7 11.0 %collective-permute-start.4 = (bf16[2,32,1024]{2,1,0:T(8,128)(2,1)S(1)}, bf16[2,32,1024]{2,1,0:T(8,128)(2,1)S(1)}, u32[]{:S(2)}, u32[]{:S(2)}) collective-permute-start(bf16[2,32,1024]{2,1,0:T(8,128)(2,1)S(1)} %get-tuple-element.16), channel_id=1, source_target_pairs={{0,4},{4,8},{8,12},{12,16},{16,20},{20,24},{24,28},{28,0},{1,5},{5... | collective-permute-start | bytes 393224 | tf_op jit(solution)/shard_map/ppermute | solution.py:251
  7.8 11.0 %collective-permute-start.5 = (bf16[2,32,1024]{2,1,0:T(8,128)(2,1)S(1)}, bf16[2,32,1024]{2,1,0:T(8,128)(2,1)S(1)}, u32[]{:S(2)}, u32[]{:S(2)}) collective-permute-start(bf16[2,32,1024]{2,1,0:T(8,128)(2,1)S(1)} %get-tuple-element.15), channel_id=1, source_target_pairs={{0,28},{4,0},{8,4},{12,8},{16,12},{20,16},{24,20},{28,24},{1,29},{... | collective-permute-start | bytes 393224 | tf_op jit(solution)/shard_map/ppermute | solution.py:251
  11.6 8.6 %collective-permute-start.3 = (bf16[2,128,256]{2,1,0:T(8,128)(2,1)S(1)}, bf16[2,128,256]{2,1,0:T(8,128)(2,1)S(1)}, u32[]{:S(2)}, u32[]{:S(2)}) collective-permute-start(bf16[2,128,256]{2,1,0:T(8,128)(2,1)S(1)} %shard_map.74), channel_id=1, source_target_pairs={{0,1},{1,0},{2,3},{3,2},{4,5},{5,4},{6,7},{7,6},{8,9},{9,8},{10,11... | collective-permute-start | bytes 393224 | tf_op jit(solution)/shard_map/ppermute | solution.py:255
  12.3 16.1 %collective-permute-start.2 = (bf16[2,272,256]{2,1,0:T(8,128)(2,1)S(1)}, bf16[2,272,256]{2,1,0:T(8,128)(2,1)S(1)}, u32[]{:S(2)}, u32[]{:S(2)}) collective-permute-start(bf16[2,272,256]{2,1,0:T(8,128)(2,1)S(1)} %shard_map.73), channel_id=1, source_target_pairs={{0,2},{1,3},{2,0},{3,1},{4,6},{5,7},{6,4},{7,5},{8,10},{9,11},{10,... | collective-permute-start | bytes 835592 | tf_op jit(solution)/shard_map/ppermute | solution.py:255
  15.7 12.8 %collective-permute-start.8 = (bf16[2,272,256]{2,1,0:T(8,128)(2,1)S(1)}, bf16[2,272,256]{2,1,0:T(8,128)(2,1)S(1)}, u32[]{:S(2)}, u32[]{:S(2)}) collective-permute-start(bf16[2,272,256]{2,1,0:T(8,128)(2,1)S(1)} %shard_map.73), channel_id=1, source_target_pairs={{0,1},{1,0},{2,3},{3,2},{4,5},{5,4},{6,7},{7,6},{8,9},{9,8},{10,11... | collective-permute-start | bytes 835592 | tf_op jit(solution)/shard_map/ppermute | solution.py:255
  20.7 5.4 %collective-permute-start.6 = (bf16[2,64,1024]{2,1,0:T(8,128)(2,1)S(1)}, bf16[2,64,1024]{2,1,0:T(8,128)(2,1)S(1)}, u32[]{:S(2)}, u32[]{:S(2)}) collective-permute-start(bf16[2,64,1024]{2,1,0:T(8,128)(2,1)S(1)} %get-tuple-element.13), channel_id=1, source_target_pairs={{0,28},{4,0},{8,4},{12,8},{16,12},{20,16},{24,20},{28,24},{1,29},{... | collective-permute-start | bytes 786440 | tf_op jit(solution)/shard_map/ppermute | solution.py:251
  26.6 1.9 %collective-permute-start.7 = (f32[8,128]{1,0:T(8,128)S(1)}, f32[8,128]{1,0:T(8,128)S(1)}, u32[]{:S(2)}, u32[]{:S(2)}) collective-permute-start(f32[8,128]{1,0:T(8,128)S(1)} %shard_map.78), channel_id=1, source_target_pairs={{0,4},{4,0},{8,12},{12,8},{16,20},{20,16},{24,28},{28,24},{1,5},{5... | collective-permute-start | bytes 12296 | tf_op jit(solution)/shard_map/ppermute | solution.py:255
  28.6 8.4 %collective-permute-start.9 = (bf16[2,256,256]{2,1,0:T(8,128)(2,1)S(1)}, bf16[2,256,256]{2,1,0:T(8,128)(2,1)S(1)}, u32[]{:S(2)}, u32[]{:S(2)}) collective-permute-start(bf16[2,256,256]{2,1,0:T(8,128)(2,1)S(1)} %shard_map.79), channel_id=1, source_target_pairs={{0,1},{1,0},{2,3},{3,2},{4,5},{5,4},{6,7},{7,6},{8,9},{9,8},{10,11... | collective-permute-start | bytes 786440 | tf_op jit(solution)/shard_map/ppermute | solution.py:255
  30.1 3.6 %collective-permute-start.10 = (f32[8,128]{1,0:T(8,128)S(1)}, f32[8,128]{1,0:T(8,128)S(1)}, u32[]{:S(2)}, u32[]{:S(2)}) collective-permute-start(f32[8,128]{1,0:T(8,128)S(1)} %add.6), channel_id=1, source_target_pairs={{0,8},{4,12},{8,0},{12,4},{16,24},{20,28},{24,16},{28,20},{1,9},{5... | collective-permute-start | bytes 12296 | tf_op jit(solution)/shard_map/ppermute | solution.py:255
  33.8 3.6 %collective-permute-start.11 = (f32[8,128]{1,0:T(8,128)S(1)}, f32[8,128]{1,0:T(8,128)S(1)}, u32[]{:S(2)}, u32[]{:S(2)}) collective-permute-start(f32[8,128]{1,0:T(8,128)S(1)} %add.7.mine_ref), channel_id=1, source_target_pairs={{0,16},{4,20},{8,24},{12,28},{16,0},{20,4},{24,8},{28,12},{1,17},{... | collective-permute-start | bytes 12296 | tf_op jit(solution)/shard_map/ppermute | solution.py:255
